TPU v7x, 32 devices: a whole 2x2x4 slice. The times are simulated.
32 devices in a mesh: groups: 2 (over x), tensor: 16 (over z, y, core).
Axes of the slice: x: 2, y: 2, z: 4, core: 2. Of those that a mesh axis runs over, the one named last changes fastest.
Arguments:
- hidden_in: bfloat16 [2, 192, 16384], P(None, 'groups', 'tensor'), parts along dimension 1, may hold values from -6 to 6
- norm_gain: bfloat16 [16384], P('tensor'), may hold values from 0.099609375 to 1.8984375
- qkv_weight: bfloat16 [16384, 18432], P('tensor'), may hold values from -0.046875 to 0.046875
- out_weight: bfloat16 [16384, 16384], P(None, 'tensor'), may hold values from -0.046875 to 0.046875
- cache_pool: bfloat16 [768, 8, 16, 256], P(('groups', 'tensor')), parts along dimension 0, may hold values from -6 to 6
- cache_scale: bfloat16 [768, 8, 2], P(('groups', 'tensor')), parts along dimension 0, may hold values from 0.3 to 120
- request_length: int32 [32], P('groups'), parts along dimension 0, may hold values from 1 to 2304, as said below
- block_table: int32 [32, 16], P('groups'), parts along dimension 0, may hold values from 0 to 23, as said below
Outputs:
- hidden_out: bfloat16 [2, 192, 16384], P(None, 'groups', 'tensor'), parts along dimension 1
There are 2 independent parts, one for each index of `groups`. A program takes and returns all parts, laid end to end along the dimension named above; an argument that names none is the same for every part. Nothing has to cross between parts.
Inputs may be any that keep to these rules, and one draw needn't show every extreme that they name: `request_length`: a request spans ceil(length / 256) stripes; the stripes of the requests of one owner (requests with equal index mod 2) number at most 16 in all and exactly 16 for some owner; the stripes of all requests number exactly 24; some request reaches the largest length. `block_table`: row r lists, for the stripes of request r in order, the pool slot that every device uses for its block of that stripe; over all requests each slot appears once; entries past a request's stripes are zero.
All inputs are finite; a program needn't handle non-finite values.
Results may differ from a plain program's by a relative error of at most 0.005.
The roundings to bfloat16 on the way count: a program that leaves them out, or rounds other values in their place, can miss the bound.
Values may be sent and summed in bfloat16 or wider, within the bound.
No kernel may reach another device: no remote copies, remote signals or barrier semaphores. Data moves between devices by JAX's collectives and lax.ppermute only.
A program may use at most 192 MiB of HBM per device.

v0:
```python
import jax
import jax.numpy as jnp
from jax import lax
from jax.sharding import PartitionSpec as P

D = 16384
QH = 128
KVH = 8
HD = 128
QR = 6
STEPS = 2
BLK = 16
GQ = 16
GW = 2304


EPSILON = 1e-05
ROPE_BASE = 500000.0
NEG_FILL = -1e30


def rotate(values, positions):
    half = values.shape[-1] // 2
    freqs = ROPE_BASE ** (-(jnp.arange(half, dtype=jnp.float32) * 2.0 / values.shape[-1]))
    angles = positions.astype(jnp.float32)[..., None] * freqs
    cosine = jnp.cos(angles)
    sine = jnp.sin(angles)
    first = values[..., :half]
    second = values[..., half:]
    return jnp.concatenate([first * cosine - second * sine, second * cosine + first * sine], -1)


def request_layout(request_owner, request_length, block_table, owners, stripe):
    requests = request_owner.shape[0]
    most = block_table.shape[1]
    order = jnp.arange(requests, dtype=jnp.int32)
    stripes = (request_length + stripe - 1) // stripe
    before = (
        (request_owner[None, :] == request_owner[:, None]) & (order[None, :] < order[:, None])
    ).astype(jnp.int32)
    rank = jnp.sum(before, 1)
    offset = jnp.sum(before * stripes[None, :], 1)
    owner_ids = jnp.arange(owners, dtype=jnp.int32)
    mine = request_owner[None, :] == owner_ids[:, None]
    member = mine[:, :, None] & (
        rank[None, :, None] == jnp.arange(requests // owners, dtype=jnp.int32)[None, None, :]
    )
    owner_requests = jnp.sum(member.astype(jnp.int32) * order[None, :, None], 1)
    columns = jnp.arange(most, dtype=jnp.int32)
    within = columns[None, None, :] - offset[None, :, None]
    hit = (mine[:, :, None] & (within >= 0) & (within < stripes[None, :, None])).astype(jnp.int32)
    stripe_request = jnp.sum(hit * order[None, :, None], 1) - (1 - jnp.sum(hit, 1))
    stripe_rank = jnp.sum(hit * within, 1)
    pick = (within[..., None] == columns[None, None, None, :]).astype(jnp.int32)
    slots = jnp.sum(hit[..., None] * pick * block_table[None, :, None, :], (1, 3))
    return (owner_requests, stripe_request, stripe_rank, slots, rank, stripes)


def cache_partial(queries, keys, values, key_scale, value_scale, mask):
    scores = jnp.einsum("srgd,td->srgt", queries, keys, preferred_element_type=jnp.float32)
    scores = jnp.where(mask, scores * key_scale * HD ** (-0.5), NEG_FILL)
    best = jnp.max(scores, -1)
    expo = jnp.where(mask, jnp.exp(scores - best[..., None]), 0.0)
    total = jnp.sum(expo, -1)
    weights = (expo * value_scale).astype(jnp.bfloat16)
    summed = jnp.einsum("srgt,td->srgd", weights, values, preferred_element_type=jnp.float32)
    return (best, total, summed)


def local(
    hidden_in,
    norm_gain,
    qkv_weight,
    out_weight,
    cache_pool,
    cache_scale,
    request_length,
    block_table,
):
    devices = lax.axis_size("tensor")
    device = lax.axis_index("tensor")
    owners = devices // KVH
    stripe = devices * BLK
    requests = request_length.shape[0]
    request_owner = jnp.arange(requests, dtype=jnp.int32) % owners
    unit_rows = requests // owners * QR
    most = block_table.shape[1]
    local_width = hidden_in.shape[2]
    my_owner = device // KVH
    owner_requests, stripe_request, stripe_rank, slots, rank, stripes = request_layout(
        request_owner, request_length, block_table, owners, stripe
    )
    step_rows = jnp.arange(QR, dtype=jnp.int32)
    row_order = (owner_requests[:, :, None] * QR + step_rows[None, None, :]).reshape(
        owners * unit_rows
    )
    inverse = ((request_owner * unit_rows + rank * QR)[:, None] + step_rows[None, :]).reshape(
        requests * QR
    )
    row_request = jnp.repeat(owner_requests[my_owner], QR)
    row_length = request_length[row_request]
    row_step = jnp.arange(unit_rows, dtype=jnp.int32) % QR
    same_request = row_request[:, None] == row_request[None, :]
    gain = norm_gain.astype(jnp.float32)
    weight_grouped = qkv_weight.reshape(local_width, KVH, GW)
    sent = cache_pool[jnp.transpose(slots)].reshape(most, devices, BLK, 2 * HD)
    sent_scale = cache_scale[jnp.transpose(slots)].reshape(most, devices, 2)
    landed, landed_scale = (
        lax.all_to_all(sent, "tensor", split_axis=1, concat_axis=1, tiled=True),
        lax.all_to_all(sent_scale, "tensor", split_axis=1, concat_axis=1, tiled=True),
    )
    cache_data = landed.reshape(most * stripe, 2 * HD)
    token_scale = jnp.broadcast_to(
        landed_scale.astype(jnp.float32)[:, :, None, :], (most, devices, BLK, 2)
    ).reshape(most * stripe, 2)
    token = jnp.arange(most * stripe, dtype=jnp.int32)
    token_stripe = token // stripe
    token_request = stripe_request[my_owner][token_stripe]
    token_position = stripe_rank[my_owner][token_stripe] * stripe + token % stripe
    token_length = jnp.where(token_request >= 0, request_length[jnp.maximum(token_request, 0)], 0)
    cache_mask = (
        (token_request[None, :] == row_request[:, None]) & (token_position < token_length)[None, :]
    )[None, :, None, :]
    outputs = []
    keys_seen = []
    values_seen = []
    for step in range(STEPS):
        block = hidden_in[step : step + 1]
        project_count = block.shape[0]
        values = block.astype(jnp.float32)
        sums = lax.psum(jnp.sum(values * values, -1), "tensor")
        normed = (values * lax.rsqrt(sums[..., None] / D + EPSILON) * gain).astype(jnp.bfloat16)
        ordered = jnp.take(normed, row_order, axis=1).reshape(
            project_count, owners, unit_rows, local_width
        )
        term = jnp.einsum(
            "sojd,dhg->ohsjg", ordered, weight_grouped, preferred_element_type=jnp.float32
        )
        term = term.reshape(owners * KVH * project_count * unit_rows, GW)
        mine = lax.psum_scatter(term, "tensor", scatter_dimension=0, tiled=True)
        joined_block = mine.astype(jnp.bfloat16).reshape(project_count, unit_rows, GW)
        prepare_count = joined_block.shape[0]
        steps_here = step + jnp.arange(prepare_count, dtype=jnp.int32)
        position = row_length[None, :] + QR * steps_here[:, None] + row_step[None, :]
        prepare_queries = rotate(
            joined_block[..., : GQ * HD]
            .reshape(prepare_count, unit_rows, GQ, HD)
            .astype(jnp.float32),
            position[:, :, None],
        ).astype(jnp.bfloat16)
        keys = rotate(
            joined_block[..., GQ * HD : GQ * HD + HD].astype(jnp.float32), position
        ).astype(jnp.bfloat16)
        queries, keys, values = (prepare_queries, keys, joined_block[..., GQ * HD + HD :])
        keys_seen.append(keys)
        values_seen.append(values)
        keys_all = jnp.concatenate(keys_seen, 0)
        attend_count = queries.shape[0]
        cache_best, cache_total, cache_summed = cache_partial(
            queries,
            cache_data[:, :HD],
            cache_data[:, HD:],
            token_scale[:, 0],
            token_scale[:, 1],
            cache_mask,
        )
        news = jnp.einsum(
            "srgd,pjd->srgpj", queries, keys_all, preferred_element_type=jnp.float32
        ) * HD ** (-0.5)
        query_step = step + jnp.arange(attend_count, dtype=jnp.int32)[:, None, None, None]
        key_step = jnp.arange(keys_all.shape[0], dtype=jnp.int32)[None, None, :, None]
        allowed = (key_step < query_step) | (key_step == query_step) & (
            row_step[None, None, None, :] <= row_step[None, :, None, None]
        )
        allowed = (allowed & same_request[None, :, None, :])[:, :, None, :, :]
        news = jnp.where(allowed, news, NEG_FILL)
        best = jnp.maximum(cache_best, jnp.max(news, (3, 4)))
        factor = jnp.exp(cache_best - best)
        expo = jnp.where(allowed, jnp.exp(news - best[..., None, None]), 0.0)
        total = cache_total * factor + jnp.sum(expo, (3, 4))
        summed = cache_summed * factor[..., None] + jnp.einsum(
            "srgpj,pjd->srgd",
            expo.astype(jnp.bfloat16),
            jnp.concatenate(values_seen, 0),
            preferred_element_type=jnp.float32,
        )
        attention = (
            (summed / total[..., None])
            .astype(jnp.bfloat16)
            .reshape(attend_count, unit_rows, GQ * HD)
        )
        count = attention.shape[0]
        gathered = lax.all_gather(attention, "tensor", axis=2, tiled=True).reshape(
            count, unit_rows, owners, QH * HD
        )
        mixed = jnp.einsum(
            "sjof,fd->sojd", gathered, out_weight, preferred_element_type=jnp.float32
        )
        mixed = jnp.take(mixed.reshape(count, owners * unit_rows, local_width), inverse, axis=1)
        outputs.append(
            (hidden_in[step : step + count].astype(jnp.float32) + mixed).astype(jnp.bfloat16)
        )
    return jnp.concatenate(outputs, 0)


def solution(mesh):
    return jax.shard_map(
        local,
        mesh=mesh,
        in_specs=(
            P(None, "groups", "tensor"),
            P("tensor"),
            P("tensor", None),
            P(None, "tensor"),
            P(("groups", "tensor"), None, None, None),
            P(("groups", "tensor"), None, None),
            P("groups"),
            P("groups", None),
        ),
        out_specs=P(None, "groups", "tensor"),
        check_vma=False,
    )
```

profile of v0, /device:TPU:0, one launch (start us, length us, event | category | flops | bytes accessed | tf_op | source)
XLA Modules:
  0.0 421.6 jit_solution(12418147861268964060)
XLA Ops:
  6.5 0.8 and_select_fusion.2
  7.3 0.2 select_reduce_fusion.3
  7.5 0.7 convert_element_type.173
  8.2 1.2 fusion.31
  9.4 0.2 select_reduce_fusion.2
  10.0 34.9 %all-reduce = (f32[1,96]{1,0:T(1,128)S(1)}, f32[1,96]{1,0:T(1,128)S(1)}) all-reduce(f32[1,96]{1,0:T(1,128)S(1)} %bitcast.235, f32[1,96]{1,0:T(1,128)S(1)} %bitcast.234), channel_id=1, replica_groups=mesh['groups'=2,'tensor'=16] {'tensor'}, use_global_device_ids=true, to_apply=%region_15.18 | all-reduce | flops 192 | bytes 1536 | tf_op jit(solution)/shard_map/psum | solution.py:131
  44.9 1.2 fusion.51
  46.1 0.8 gather_fusion.3
  46.9 0.8 gather_fusion.5
  47.8 17.1 %fusion.1 = f32[2,48,8,2304]{3,1,2,0:T(8,128)} fusion(bf16[2,48,1024,1]{2,1,3,0:T(8,128)(2,1)S(1)} %bitcast.222, bf16[128,8,8,2304]{3,2,1,0:T(8,128)(2,1)} %bitcast.236), kind=kOutput, calls=%fused_computation.9 | convolution fusion | flops 3623878656 | bytes 45023232 | tf_op jit(solution)/shard_map/sojd,dhg->ohsjg/dot_general | solution.py:136
  65.0 19.4 %fusion = f32[2,48,8,2304]{3,1,2,0:T(8,128)} fusion(bf16[2,48,1024,1]{2,1,3,0:T(8,128)(2,1)S(1)} %bitcast.221, bf16[128,8,8,2304]{3,2,1,0:T(8,128)(2,1)} %bitcast.237), kind=kOutput, calls=%fused_computation.8 | convolution fusion | flops 3623878656 | bytes 45023232 | tf_op jit(solution)/shard_map/sojd,dhg->ohsjg/dot_general | solution.py:136
  84.9 0.2 multiply_reduce_fusion
  85.4 0.6 gather_fusion.2
  86.1 0.7 copy.53
  86.7 3.5 all-to-all-start.1
  91.0 0.7 fusion.116
  91.9 2.0 gather_fusion.1
  93.9 3.2 copy.49
  97.1 0.8 gather_fusion
  97.9 6.0 %all-to-all-start = ((bf16[16,16,16,256]{3,2,0,1:T(8,128)(2,1)}), bf16[16,16,16,256]{3,2,0,1:T(8,128)(2,1)}, u32[]{:S(2)}, u32[]{:S(2)}) async-start(bf16[16,16,16,256]{3,2,0,1:T(8,128)(2,1)} %copy.49), calls=%async_computation.1 | async-start | bytes 4194304 | tf_op jit(solution)/shard_map/all_to_all | solution.py:109
  103.9 0.2 all-gather.3.cloned.1.call-start
  104.1 0.7 fusion.115
  104.9 0.7 fusion.114
  105.7 4.4 %compare_select_fusion.2 = s32[4096,1]{0,1:T(1,128)S(1)} fusion(s32[]{:T(128)} %bitcast.27, s32[]{:T(128)} %bitcast.28, s32[]{:T(128)} %bitcast.29, s32[]{:T(128)} %bitcast.30, s32[]{:T(128)} %bitcast.31, s32[]{:T(128)} %bitcast.33, s32[]{:T(128)} %bitcast.32), kind=kLoop, calls=%fused_computation.122 | loop fusion | flops 94208 | bytes 16412 | tf_op jit(solution)/shard_map/gather | solution.py:119
  110.1 4.4 %compare_select_fusion.1 = s32[4096,1]{0,1:T(1,128)S(1)} fusion(s32[]{:T(128)} %bitcast.9, s32[]{:T(128)} %bitcast.10, s32[]{:T(128)} %bitcast.11, s32[]{:T(128)} %bitcast.12, s32[]{:T(128)} %bitcast.13, s32[]{:T(128)} %bitcast.15, s32[]{:T(128)} %bitcast.14), kind=kLoop, calls=%fused_computation.121 | loop fusion | flops 94208 | bytes 16412 | tf_op jit(solution)/shard_map/gather | solution.py:118
  114.5 21.3 %fusion.82 = (pred[4096]{0:T(1024)(128)(4,1)S(1)}, s32[4096]{0:T(1024)S(1)}) fusion(pred[4096]{0:T(1024)(128)(4,1)S(1)} %compare_reduce_fusion, pred[4096]{0:T(1024)(128)(4,1)S(1)} %compare_reduce_fusion.1, pred[4096]{0:T(1024)(128)(4,1)S(1)} %compare_reduce_fusion.2, pred[4096]{0:T(1024)(128)(4,1)S(1)} %compare_reduce_fusion.3, ...), kind=kLoop, calls=%fused_computation.168 | loop fusion | flops 245760 | bytes 90248 | tf_op jit(solution)/shard_map/lt | solution.py:122
  135.8 0.3 multiply_cosine_fusion.3
  136.0 0.2 compare_and_fusion
  136.3 0.1 broadcast_in_dim.87
  136.5 0.2 reshape.1351
  136.7 25.2 %all-to-all-done = bf16[16,16,16,256]{3,2,0,1:T(8,128)(2,1)} async-done(((bf16[16,16,16,256]{3,2,0,1:T(8,128)(2,1)}), bf16[16,16,16,256]{3,2,0,1:T(8,128)(2,1)}, u32[]{:S(2)}, u32[]{:S(2)}) %all-to-all-start) | async-done | bytes 2097184 | tf_op jit(solution)/shard_map/all_to_all | solution.py:109
  161.9 3.1 copy.50
  165.0 19.5 %reduce-scatter.3.cloned.1.call-done = f32[48,2304]{1,0:T(8,128)} async-done(((f32[768,2304]{1,0:T(8,128)}), f32[48,2304]{1,0:T(8,128)}) %reduce-scatter.3.cloned.1.call-update) | async-done | bytes 442384 | tf_op jit(solution)/shard_map/reduce_scatter | solution.py:140
  184.5 1.0 convert_bitcast_fusion.3
  185.6 92.5 %reduce-scatter.5.cloned.1.call-done = f32[48,2304]{1,0:T(8,128)} async-done(((f32[768,2304]{1,0:T(8,128)}), f32[48,2304]{1,0:T(8,128)}) %reduce-scatter.5.cloned.1.call-update) | async-done | bytes 442384 | tf_op jit(solution)/shard_map/reduce_scatter | solution.py:140
  278.1 1.2 convert_bitcast_fusion.2
  279.5 0.3 fusion.70
  279.8 0.2 fusion.46
  280.0 4.4 %fusion.8 = (f32[48,16]{1,0:T(8,128)S(1)}, f32[48,16,4096]{2,1,0:T(8,128)S(1)}) fusion(f32[4096]{0:T(1024)S(1)} %bitcast.225, pred[48,4096]{1,0:T(8,128)(4,1)S(1)} %compare_and_fusion, bf16[4096,256]{1,0:T(8,128)(2,1)} %bitcast.217, bf16[48,16,64]{2,1,0:T(8,128)(2,1)S(1)} %get-tuple-element.25, bf16[48,16,64]{2,1,0:T(8,128)(2,1)S(1)} %get-tuple-element.24), kind=kOutput, calls=%fused_computation.22 | convolution fusion | flops 818281728 | bytes 14044160 | tf_op jit(solution)/shard_map/srgd,td->srgt/dot_general | solution.py:60
  284.4 0.4 fusion.117
  284.8 0.3 fusion.43
  285.2 0.2 fusion.48
  285.4 9.9 %fusion.10 = (f32[48,16]{1,0:T(8,128)S(1)}, f32[48,16]{1,0:T(8,128)S(1)}, f32[48,16,4096]{2,1,0:T(8,128)}) fusion(f32[48,16,4096]{2,1,0:T(8,128)S(1)} %get-tuple-element.108, f32[48,16]{1,0:T(8,128)S(1)} %get-tuple-element.107, f32[4096]{0:T(1024)S(1)} %bitcast.226, pred[48,4096]{1,0:T(8,128)(4,1)S(1)} %compare_and_fusion, ...), kind=kOutput, calls=%fused_computation.24 | convolution fusion | flops 837155328 | bytes 26851328 | tf_op jit(solution)/shard_map/srgd,td->srgt/dot_general | solution.py:60
  295.3 4.2 fusion.23
  299.5 0.3 fusion.24
  299.8 0.8 reshape.1353
  300.6 0.3 all-gather.5.cloned.1.call-start
  300.9 0.1 or_and_fusion
  301.0 0.5 fusion.118
  301.5 0.3 fusion.29
  301.8 0.4 convolution_bitcast_fusion
  302.2 7.5 %fusion.11 = f32[48,16]{1,0:T(8,128)S(1)} fusion(f32[48,16,4096]{2,1,0:T(8,128)} %get-tuple-element.111, f32[48,16]{1,0:T(8,128)S(1)} %get-tuple-element.10, f32[4096]{0:T(1024)S(1)} %bitcast.228, pred[48,4096]{1,0:T(8,128)(4,1)S(1)} %compare_and_fusion), kind=kLoop, calls=%fused_computation.25 | loop fusion | flops 18873600 | bytes 12802048 | tf_op jit(solution)/shard_map/reduce_sum | solution.py:64
  309.7 7.4 %fusion.26 = bf16[48,16,128]{2,1,0:T(8,128)(2,1)S(1)} fusion(f32[48,16,128]{2,1,0:T(8,128)S(1)} %convolution_bitcast_fusion, f32[48,16,4096]{2,1,0:T(8,128)} %get-tuple-element.111, f32[48,16]{1,0:T(8,128)S(1)} %get-tuple-element.10, f32[4096]{0:T(1024)S(1)} %bitcast.233, f32[4096]{0:T(1024)S(1)} %bitcast.229, pred[48,4096]{1,0:T(8,128)(4,1)S(1)} %compare_and_fusion, ...), kind=kOutput, calls=%fused_computation.46 | convolution fusion | flops 827719680 | bytes 14459904 | tf_op jit(solution)/shard_map/srgt,td->srgd/dot_general | solution.py:66
  317.1 0.8 reshape.1359
  318.0 27.5 %all-gather.3.cloned.1.call-done = bf16[1,48,32768]{2,1,0:T(8,128)(2,1)} async-done(((bf16[1,48,2048]{2,1,0:T(8,128)(2,1)}), bf16[1,48,32768]{2,1,0:T(8,128)(2,1)}) %all-gather.3.cloned.1.call-update) | async-done | bytes 3145744 | tf_op jit(solution)/shard_map/all_gather | solution.py:193
  345.5 6.2 %reshape.1354 = bf16[48,2,16384]{2,1,0:T(2,128)(2,1)} reshape(bf16[1,48,32768]{2,1,0:T(8,128)(2,1)} %all-gather.3.cloned.1.call-done) | data formatting | bytes 6291456 | tf_op jit(solution)/shard_map/reshape.65
  351.6 15.0 %fusion.4 = f32[48,2,1024]{2,0,1:T(8,128)S(1)} fusion(bf16[16384,1024]{1,0:T(8,128)(2,1)} %param.15, bf16[48,2,16384]{2,1,0:T(2,128)(2,1)} %reshape.1354), kind=kOutput, calls=%fused_computation.12 | convolution fusion | flops 3221225472 | bytes 37093376 | tf_op jit(solution)/shard_map/sjof,fd->sojd/dot_general | solution.py:196
  366.6 25.0 %all-gather.5.cloned.1.call-done = bf16[1,48,32768]{2,1,0:T(8,128)(2,1)} async-done(((bf16[1,48,2048]{2,1,0:T(8,128)(2,1)}), bf16[1,48,32768]{2,1,0:T(8,128)(2,1)}) %all-gather.5.cloned.1.call-update) | async-done | bytes 3145744 | tf_op jit(solution)/shard_map/all_gather | solution.py:193
  391.6 6.2 %reshape.1360 = bf16[48,2,16384]{2,1,0:T(2,128)(2,1)} reshape(bf16[1,48,32768]{2,1,0:T(8,128)(2,1)} %all-gather.5.cloned.1.call-done) | data formatting | bytes 6291456 | tf_op jit(solution)/shard_map/reshape.99
  397.7 14.9 %fusion.2 = f32[48,2,1024]{2,0,1:T(8,128)S(1)} fusion(bf16[16384,1024]{1,0:T(8,128)(2,1)} %param.15, bf16[48,2,16384]{2,1,0:T(2,128)(2,1)} %reshape.1360), kind=kOutput, calls=%fused_computation.10 | convolution fusion | flops 3221225472 | bytes 37093376 | tf_op jit(solution)/shard_map/sjof,fd->sojd/dot_general | solution.py:196
  412.6 0.7 gather_fusion.4
  413.4 0.7 gather_fusion.6
  414.1 0.2 fusion.34
  414.3 0.7 copy-done.7
  (85 shorter events, 2.7 us)
Async XLA Ops:
  6.5 85.4 %copy-start = (bf16[24,8,16,256]{3,2,1,0:T(8,128)(2,1)S(1)}, bf16[24,8,16,256]{3,2,1,0:T(8,128)(2,1)}, u32[]{:S(2)}) copy-start(bf16[24,8,16,256]{3,2,1,0:T(8,128)(2,1)} %param.16) | copy-start | bytes 4718596
  6.5 178.0 %reduce-scatter.3.cloned.1.call-start = ((), (), s32[]{:S(2)}) async-start(), calls=%async_computation.4 | async-start | bytes 7520256 | tf_op jit(solution)/shard_map/reduce_scatter | solution.py:140
  64.9 213.2 %reduce-scatter.5.cloned.1.call-start = ((), (), s32[]{:S(2)}) async-start(), calls=%async_computation.6 | async-start | bytes 7520256 | tf_op jit(solution)/shard_map/reduce_scatter | solution.py:140
  65.0 19.5 %copy-start.6 = (bf16[24,8,2]{0,2,1:T(2,128)(2,1)S(1)}, bf16[24,8,2]{0,2,1:T(2,128)(2,1)}, u32[]{:S(2)}) copy-start(bf16[24,8,2]{0,2,1:T(2,128)(2,1)} %param.17) | copy-start | bytes 2308
  65.0 19.9 %copy-start.5 = (s32[16,16]{1,0:T(8,128)S(1)}, s32[16,16]{1,0:T(8,128)}, u32[]{:S(2)}) copy-start(s32[16,16]{1,0:T(8,128)} %param.19) | copy-start | bytes 3076
  65.0 26.1 %copy-start.2 = (s32[16]{0:T(128)S(1)}, s32[16]{0:T(128)}, u32[]{:S(2)}) copy-start(s32[16]{0:T(128)} %param.18) | copy-start | bytes 196
  86.7 11.1 %all-to-all-start.1 = ((bf16[16,16,2]{0,2,1:T(2,128)(2,1)}), bf16[16,16,2]{0,2,1:T(2,128)(2,1)S(1)}, u32[]{:S(2)}, u32[]{:S(2)}) async-start(bf16[16,16,2]{0,2,1:T(2,128)(2,1)} %copy.53), calls=%async_computation.2 | async-start | bytes 16384 | tf_op jit(solution)/shard_map/all_to_all | solution.py:110
  97.9 64.1 %all-to-all-start = ((bf16[16,16,16,256]{3,2,0,1:T(8,128)(2,1)}), bf16[16,16,16,256]{3,2,0,1:T(8,128)(2,1)}, u32[]{:S(2)}, u32[]{:S(2)}) async-start(bf16[16,16,16,256]{3,2,0,1:T(8,128)(2,1)} %copy.49), calls=%async_computation.1 | async-start | bytes 4194304 | tf_op jit(solution)/shard_map/all_to_all | solution.py:109
  103.9 241.6 %all-gather.3.cloned.1.call-start = ((), (), s32[]{:S(2)}) async-start(), calls=%async_computation.5 | async-start | bytes 3342336 | tf_op jit(solution)/shard_map/all_gather | solution.py:193
  278.1 7.2 %copy-start.4 = (bf16[16,16,16,256]{3,2,1,0:T(8,128)(2,1)S(1)}, bf16[16,16,16,256]{3,2,1,0:T(8,128)(2,1)}, u32[]{:S(2)}) copy-start(bf16[16,16,16,256]{3,2,1,0:T(8,128)(2,1)} %copy.50) | copy-start | bytes 6291460
  300.6 91.0 %all-gather.5.cloned.1.call-start = ((), (), s32[]{:S(2)}) async-start(), calls=%async_computation.7 | async-start | bytes 3342336 | tf_op jit(solution)/shard_map/all_gather | solution.py:193
  397.7 16.4 %copy-start.3 = (bf16[2,96,1024]{2,1,0:T(8,128)(2,1)S(1)}, bf16[2,96,1024]{2,1,0:T(8,128)(2,1)}, u32[]{:S(2)}) copy-start(bf16[2,96,1024]{2,1,0:T(8,128)(2,1)} %param.12) | copy-start | bytes 1179652
  397.7 17.3 %copy-start.1 = (bf16[24,8,16,256]{3,2,1,0:T(8,128)(2,1)S(1)}, bf16[24,8,16,256]{3,2,1,0:T(8,128)(2,1)}, u32[]{:S(2)}) copy-start(bf16[24,8,16,256]{3,2,1,0:T(8,128)(2,1)} %param.16) | copy-start | bytes 4718596
  414.3 0.7 copy-start.7
Sparse Core Ops, SparseCore 0:
  65.0 119.4 reduce-scatter.2
  189.1 88.9 reduce-scatter.4
  300.7 44.7 all-gather.2
  347.5 44.0 all-gather.4
where the time goes:
time: 423 us; the launch traced here: 422 us
  waiting for transfers between devices  190 us (45%)
  matrix products  93.9 us (22%)
  other arithmetic  47.7 us (11%)
  blocking collectives  34.9 us (8%)
  local copies, waits for them, and re-layouts  31.5 us (7%)
  between operations  13.7 us (3%)
  starting transfers between devices  10 us (2%)
    reduce_scatter x2, waiting for transfers between devices, local(): mine = lax.psum_scatter(term, 'tensor', scatter_dimension=0, tiled=True)  112 us
    all_gather x2, waiting for transfers between devices, local(): lax.all_gather(attention, 'tensor', axis=2, tiled=True)  52.5 us
    dot_general x2, matrix products, local(): jnp.einsum('sojd,dhg->ohsjg', ordered, weight_grouped, preferred_element_...  36.6 us
    psum x1, blocking collectives, local(): sums = lax.psum(jnp.sum(values * values, -1), 'tensor')  34.9 us
    dot_general x2, matrix products, local(): jnp.einsum('sjof,fd->sojd', gathered, out_weight, preferred_element_type=...  29.8 us
    all_to_all x1, waiting for transfers between devices, local(): lax.all_to_all(sent, 'tensor', split_axis=1, concat_axis=1, tiled=True)  25.2 us
    lt x1, other arithmetic, local(): token_position < token_length  21.3 us
    dot_general x2, matrix products, cache_partial(): jnp.einsum('srgd,td->srgt', queries, keys, preferred_element_type=jnp.flo...  14.3 us
  transfers between devices with their start and end apart: 6, of which 5 were waited for; matrix products, arithmetic and copies ran while one was open for 25% of the time, Pallas kernels for 0%

commit v1 on v0

--- a/solution.py
+++ b/solution.py
@@ -1,6 +1,8 @@
 import jax
 import jax.numpy as jnp
 from jax import lax
+from jax.experimental import pallas as pl
+from jax.experimental.pallas import tpu as pltpu
 from jax.sharding import PartitionSpec as P
 
 D = 16384
@@ -67,7 +69,7 @@
     return (best, total, summed)
 
 
-def local(
+def local_general(
     hidden_in,
     norm_gain,
     qkv_weight,
@@ -203,9 +205,419 @@
     return jnp.concatenate(outputs, 0)
 
 
+VMEM_LIMIT = 48 * 1024 * 1024
+LEVELS = 32000.0
+TILE = 16
+MESH_BITS = (1, 2, 4, 8)
+
+
+def swap(value, bit):
+    devices = lax.axis_size("tensor")
+    return lax.ppermute(value, "tensor", [(i, i ^ bit) for i in range(devices)])
+
+
+def encode(block):
+    top = jnp.max(jnp.abs(block), 0, keepdims=True)
+    power = jnp.ceil(jnp.log2(jnp.maximum(top, 1e-30)))
+    codes = jnp.round(block * (jnp.exp2(-power) * LEVELS))
+    return codes.astype(jnp.int32).astype(jnp.int16), power
+
+
+def decode(codes, power):
+    return codes.astype(jnp.int32).astype(jnp.float32) * (jnp.exp2(power) * (1.0 / LEVELS))
+
+
+def pick_row(rows, index):
+    ids = lax.broadcasted_iota(jnp.int32, rows.shape, 0)
+    return jnp.sum(jnp.where(ids == index, rows, 0.0), 0, keepdims=True)
+
+
+def store_codes(sent, powers, block, index, steps):
+    rows = block.shape[0]
+    codes, power = encode(block)
+    sent[pl.ds(pl.multiple_of(index * rows, TILE), rows), :] = codes
+
+    @pl.when(index == 0)
+    def _():
+        powers[...] = jnp.zeros_like(powers)
+
+    powers[pl.ds(index, 1), :] = power
+
+    @pl.when(index == steps - 1)
+    def _():
+        sent[pl.ds(steps * rows, TILE), :] = powers[...].astype(jnp.int32).astype(jnp.int16)
+
+
+def project_kernel(core, normed, *refs):
+    weights = refs[:-3]
+    kept, sent, powers = refs[-3:]
+    half = len(weights) // 2
+    index = pl.program_id(0)
+
+    def product(blocks):
+        terms = [
+            jnp.dot(normed[...], w[...], preferred_element_type=jnp.float32) for w in blocks
+        ]
+        return terms[0] if len(terms) == 1 else jnp.concatenate(terms, 1)
+
+    store_codes(sent, powers, product(weights[half:]), index, KVH)
+    kept[0] = product(weights[:half])
+
+
+def project(core, normed, qkv_weight, chunk, with_pair):
+    rows, width = normed.shape
+    columns = 2 * HD + (HD if with_pair else 0)
+    per_group = GW // (2 * HD)
+
+    def wide(other):
+        def place(t, c):
+            mine = c[0] if not other else 1 - c[0]
+            return (0, t * per_group + mine * (GQ // 4) + chunk)
+
+        return pl.BlockSpec((width, 2 * HD), place)
+
+    def narrow(other):
+        def place(t, c):
+            mine = c[0] if not other else 1 - c[0]
+            return (0, t * (GW // HD) + GQ + mine)
+
+        return pl.BlockSpec((width, HD), place)
+
+    specs = []
+    for other in (False, True):
+        specs.append(wide(other))
+        if with_pair:
+            specs.append(narrow(other))
+    return pl.pallas_call(
+        project_kernel,
+        grid_spec=pltpu.PrefetchScalarGridSpec(
+            num_scalar_prefetch=1,
+            grid=(KVH,),
+            in_specs=[pl.BlockSpec((rows, width), lambda t, c: (0, 0))] + specs,
+            out_specs=[
+                pl.BlockSpec((1, rows, columns), lambda t, c: (t, 0, 0)),
+                pl.BlockSpec((KVH * rows + TILE, columns), lambda t, c: (0, 0)),
+            ],
+            scratch_shapes=[pltpu.VMEM((TILE, columns), jnp.float32)],
+        ),
+        out_shape=[
+            jax.ShapeDtypeStruct((KVH, rows, columns), jnp.float32),
+            jax.ShapeDtypeStruct((KVH * rows + TILE, columns), jnp.int16),
+        ],
+        compiler_params=pltpu.CompilerParams(vmem_limit_bytes=VMEM_LIMIT),
+        cost_estimate=pl.CostEstimate(
+            flops=2 * rows * width * columns * 2 * KVH,
+            bytes_accessed=width * columns * 4 * KVH + rows * columns * 6 * KVH,
+            transcendentals=0,
+        ),
+        name="project",
+    )(core, normed, *([qkv_weight] * len(specs)))
+
+
+def fold_kernel(steps, bit, held, landed, landed_powers, kept, sent, powers):
+    index = pl.program_id(0)
+    rows = held.shape[1]
+    rows_of_powers = landed_powers[...].astype(jnp.int32).astype(jnp.float32)
+
+    def total(side):
+        place = pl.multiple_of(side * rows, TILE)
+        codes = landed[pl.ds(place, rows), :]
+        return held[side] + decode(codes, pick_row(rows_of_powers, 2 * index + side))
+
+    mine = bit[0]
+    store_codes(sent, powers, total(1 - mine), index, steps)
+    kept[0] = total(mine)
+
+
+def fold(bit, held, landed):
+    blocks, rows, columns = held.shape
+    steps = blocks // 2
+    return pl.pallas_call(
+        lambda *refs: fold_kernel(steps, *refs),
+        grid_spec=pltpu.PrefetchScalarGridSpec(
+            num_scalar_prefetch=1,
+            grid=(steps,),
+            in_specs=[
+                pl.BlockSpec((2, rows, columns), lambda i, b: (i, 0, 0)),
+                pl.BlockSpec((2 * rows, columns), lambda i, b: (i, 0)),
+                pl.BlockSpec((TILE, columns), lambda i, b: (blocks * rows // TILE, 0)),
+            ],
+            out_specs=[
+                pl.BlockSpec((1, rows, columns), lambda i, b: (i, 0, 0)),
+                pl.BlockSpec((steps * rows + TILE, columns), lambda i, b: (0, 0)),
+            ],
+            scratch_shapes=[pltpu.VMEM((TILE, columns), jnp.float32)],
+        ),
+        out_shape=[
+            jax.ShapeDtypeStruct((steps, rows, columns), jnp.float32),
+            jax.ShapeDtypeStruct((steps * rows + TILE, columns), jnp.int16),
+        ],
+        compiler_params=pltpu.CompilerParams(vmem_limit_bytes=VMEM_LIMIT),
+        cost_estimate=pl.CostEstimate(
+            flops=20 * blocks * rows * columns,
+            bytes_accessed=blocks * rows * columns * 9,
+            transcendentals=0,
+        ),
+        name="fold",
+    )(bit, held, landed, landed)
+
+
+def finish_kernel(held, landed, joined):
+    rows = held.shape[1]
+    power = landed[pl.ds(rows, TILE), :].astype(jnp.int32).astype(jnp.float32)[0:1]
+    joined[...] = (held[0] + decode(landed[pl.ds(0, rows), :], power)).astype(jnp.bfloat16)
+
+
+def finish(held, landed):
+    _, rows, columns = held.shape
+    return pl.pallas_call(
+        finish_kernel,
+        out_shape=jax.ShapeDtypeStruct((rows, columns), jnp.bfloat16),
+        compiler_params=pltpu.CompilerParams(vmem_limit_bytes=VMEM_LIMIT),
+        name="finish",
+    )(held, landed)
+
+
+def attend_kernel(
+    slot_request,
+    queries,
+    new_keys,
+    new_values,
+    own,
+    other,
+    key_scale,
+    value_scale,
+    cache_bias,
+    new_bias,
+    attention,
+    slot_best,
+    slot_total,
+    slot_sum,
+    best,
+    total,
+    summed,
+):
+    slots = slot_best.shape[0]
+    requests, count, _ = queries.shape
+    transposed = (((1,), (1,)), ((), ()))
+    for request in range(requests):
+        scores = (
+            lax.dot_general(
+                queries[request],
+                new_keys[request],
+                transposed,
+                preferred_element_type=jnp.float32,
+            )
+            * HD ** (-0.5)
+            + new_bias[...]
+        )
+        top = jnp.max(scores, -1, keepdims=True)
+        expo = jnp.exp(scores - top)
+        best[request] = jnp.broadcast_to(top, (count, HD))
+        total[request] = jnp.broadcast_to(jnp.sum(expo, -1, keepdims=True), (count, HD))
+        summed[request] = jnp.dot(
+            expo.astype(jnp.bfloat16), new_values[request], preferred_element_type=jnp.float32
+        )
+    for slot in range(slots):
+        request = slot_request[slot]
+        query = queries[request]
+        raw = [
+            part[:, slot * BLK : (slot + 1) * BLK, :].reshape(KVH * BLK, 2 * HD)
+            for part in (own, other)
+        ]
+        scores = jnp.concatenate(
+            [
+                lax.dot_general(
+                    query, kv[:, :HD], transposed, preferred_element_type=jnp.float32
+                )
+                for kv in raw
+            ],
+            1,
+        )
+        scores = scores * key_scale[slot : slot + 1, :] + cache_bias[slot : slot + 1, :]
+        top = jnp.max(scores, -1, keepdims=True)
+        expo = jnp.exp(scores - top)
+        weights = (expo * value_scale[slot : slot + 1, :]).astype(jnp.bfloat16)
+        slot_best[slot] = jnp.broadcast_to(top, (count, HD))
+        slot_total[slot] = jnp.broadcast_to(jnp.sum(expo, -1, keepdims=True), (count, HD))
+        values = jnp.concatenate([kv[:, HD:] for kv in raw], 0)
+        slot_sum[slot] = jnp.dot(weights, values, preferred_element_type=jnp.float32)
+    for slot in range(slots):
+        request = slot_request[slot]
+        before = best[request]
+        here = slot_best[slot]
+        top = jnp.maximum(before, here)
+        keep = jnp.exp(before - top)
+        add = jnp.exp(here - top)
+        best[request] = top
+        total[request] = total[request] * keep + slot_total[slot] * add
+        summed[request] = summed[request] * keep + slot_sum[slot] * add
+    for request in range(requests):
+        attention[request] = (summed[request] / total[request]).astype(jnp.bfloat16)
+
+
+def attend(slot_request, *arrays):
+    queries = arrays[0]
+    slots = arrays[5].shape[0]
+    requests, count, _ = queries.shape
+    whole = pl.BlockSpec(memory_space=pltpu.VMEM)
+    return pl.pallas_call(
+        attend_kernel,
+        in_specs=[pl.BlockSpec(memory_space=pltpu.SMEM)] + [whole] * len(arrays),
+        out_specs=whole,
+        out_shape=jax.ShapeDtypeStruct((requests, count, HD), jnp.bfloat16),
+        scratch_shapes=[pltpu.VMEM((slots, count, HD), jnp.float32)] * 3
+        + [pltpu.VMEM((requests, count, HD), jnp.float32)] * 3,
+        compiler_params=pltpu.CompilerParams(vmem_limit_bytes=VMEM_LIMIT),
+        cost_estimate=pl.CostEstimate(
+            flops=4 * slots * count * 2 * KVH * BLK * HD,
+            bytes_accessed=2 * slots * 2 * KVH * BLK * 2 * HD,
+            transcendentals=slots * count * 2 * KVH * BLK,
+        ),
+        name="attend",
+    )(slot_request, *arrays)
+
+
+def slot_layout(request_length, block_table, slots, stripe):
+    requests, most = block_table.shape
+    stripes = (request_length + stripe - 1) // stripe
+    columns = jnp.arange(most, dtype=jnp.int32)
+    held = columns[None, :] < stripes[:, None]
+    hit = held[:, :, None] & (
+        block_table[:, :, None] == jnp.arange(slots, dtype=jnp.int32)[None, None, :]
+    )
+    hit = hit.astype(jnp.int32)
+    order = jnp.arange(requests, dtype=jnp.int32)
+    request = jnp.sum(hit * order[:, None, None], (0, 1))
+    rank = jnp.sum(hit * columns[None, :, None], (0, 1))
+    length = jnp.sum(hit * request_length[:, None, None], (0, 1))
+    return request, rank, length
+
+
+def handover(cache_pool, cache_scale, chip):
+    slots = cache_pool.shape[0]
+    scales = jnp.pad(
+        jnp.transpose(cache_scale, (1, 2, 0)).reshape(KVH, 1, 2 * slots),
+        ((0, 0), (0, TILE - 1), (0, 2 * HD - 2 * slots)),
+    )
+    landed = []
+    for k in range(KVH):
+        head = chip ^ k
+        blocks = lax.dynamic_index_in_dim(cache_pool, head, 1, keepdims=False)
+        rows = jnp.concatenate(
+            [
+                blocks.reshape(slots * BLK, 2 * HD),
+                lax.dynamic_index_in_dim(scales, head, 0, keepdims=False),
+            ],
+            0,
+        )
+        landed.append(swap(rows, 2 * k) if k else rows)
+    own = jnp.stack(landed)
+    return own, swap(own, 1)
+
+
+def local_pairs(
+    hidden_in,
+    norm_gain,
+    qkv_weight,
+    out_weight,
+    cache_pool,
+    cache_scale,
+    request_length,
+    block_table,
+):
+    devices = lax.axis_size("tensor")
+    device = lax.axis_index("tensor")
+    core = device % 2
+    chip = device // 2
+    stripe = devices * BLK
+    slots = cache_pool.shape[0]
+    requests = request_length.shape[0]
+    rows = STEPS * requests * QR
+    width = hidden_in.shape[2]
+    heads = GQ // 2
+
+    hidden = hidden_in.astype(jnp.float32)
+    sums = jnp.sum(hidden * hidden, -1)
+    for bit in MESH_BITS:
+        sums = sums + swap(sums, bit)
+    normed = (
+        hidden * lax.rsqrt(sums[..., None] / D + EPSILON) * norm_gain.astype(jnp.float32)
+    ).astype(jnp.bfloat16)
+    normed = normed.reshape(rows, width)
+
+    own, other = handover(cache_pool, cache_scale, chip)
+
+    bits = [jnp.reshape((device >> b) & 1, (1,)).astype(jnp.int32) for b in range(4)]
+    chunks = []
+    for chunk in range(GQ // 4):
+        held, sent = project(bits[0], normed, qkv_weight, chunk, chunk == 0)
+        for b in (1, 2, 3):
+            held, sent = fold(bits[b], held, swap(sent, MESH_BITS[b - 1]))
+        chunks.append(finish(held, swap(sent, MESH_BITS[3])))
+    pair = chunks[0][:, 2 * HD :]
+    query_columns = jnp.concatenate([chunks[0][:, : 2 * HD]] + chunks[1:], 1)
+    pair_other = swap(pair, 1)
+    raw_keys = jnp.where(core == 0, pair, pair_other)
+    raw_values = jnp.where(core == 0, pair_other, pair)
+
+    step_ids = jnp.arange(STEPS, dtype=jnp.int32)
+    row_ids = jnp.arange(QR, dtype=jnp.int32)
+    position = (
+        request_length[None, :, None] + QR * step_ids[:, None, None] + row_ids[None, None, :]
+    )
+    queries = rotate(
+        query_columns.reshape(STEPS, requests, QR, heads, HD).astype(jnp.float32),
+        position[..., None],
+    ).astype(jnp.bfloat16)
+    queries = jnp.transpose(queries, (1, 0, 2, 3, 4)).reshape(requests, STEPS * QR * heads, HD)
+    keys = rotate(
+        raw_keys.reshape(STEPS, requests, QR, HD).astype(jnp.float32), position
+    ).astype(jnp.bfloat16)
+
+    def by_request(value):
+        value = jnp.transpose(value.reshape(STEPS, requests, QR, HD), (1, 0, 2, 3))
+        value = value.reshape(requests, STEPS * QR, HD)
+        return jnp.pad(value, ((0, 0), (0, TILE - STEPS * QR), (0, 0)))
+
+    slot_request, slot_rank, slot_length = slot_layout(request_length, block_table, slots, stripe)
+    source = chip ^ jnp.arange(KVH, dtype=jnp.int32)
+    sources = jnp.stack([source * 2 + core, source * 2 + 1 - core])
+    offset = sources[:, :, None] * BLK + jnp.arange(BLK, dtype=jnp.int32)[None, None, :]
+    token = slot_rank[:, None] * stripe + offset.reshape(1, stripe)
+    cache_bias = jnp.where(token < slot_length[:, None], 0.0, NEG_FILL).astype(jnp.float32)
+    scales = jnp.stack([own[:, slots * BLK, : 2 * slots], other[:, slots * BLK, : 2 * slots]])
+    scales = scales.astype(jnp.float32).reshape(2 * KVH, 2, slots)
+    scales = jnp.repeat(jnp.transpose(scales, (1, 2, 0)), BLK, axis=2)
+    order = jnp.arange(STEPS * QR * heads, dtype=jnp.int32) // heads
+    key_order = jnp.arange(TILE, dtype=jnp.int32)
+    new_bias = jnp.where(key_order[None, :] <= order[:, None], 0.0, NEG_FILL).astype(jnp.float32)
+    attention = attend(
+        slot_request,
+        queries,
+        by_request(keys),
+        by_request(raw_values),
+        own,
+        other,
+        scales[0] * HD ** (-0.5),
+        scales[1],
+        cache_bias,
+        new_bias,
+    )
+    attention = jnp.transpose(
+        attention.reshape(requests, STEPS, QR, heads, HD), (1, 0, 2, 3, 4)
+    ).reshape(STEPS, requests * QR, heads * HD)
+    outputs = []
+    for step in range(STEPS):
+        gathered = lax.all_gather(attention[step], "tensor", axis=1, tiled=True)
+        mixed = jnp.dot(gathered, out_weight, preferred_element_type=jnp.float32)
+        outputs.append((hidden[step] + mixed).astype(jnp.bfloat16))
+    return jnp.stack(outputs)
+
+
 def solution(mesh):
     return jax.shard_map(
-        local,
+        local_pairs if mesh.shape["tensor"] == 2 * KVH else local_general,
         mesh=mesh,
         in_specs=(
             P(None, "groups", "tensor"),

time: 423 us -> 302 us (0.71)
  waiting for transfers between devices: 190 us -> 122 us
  matrix products: 93.9 us -> 34 us
  Pallas kernels: 0 us -> 55.7 us
  starting transfers between devices: 10 us -> 53.4 us
  other arithmetic: 47.7 us -> 4.95 us
  blocking collectives: 34.9 us -> 0 us
  local copies, waits for them, and re-layouts: 31.5 us -> 16.3 us
    reduce_scatter x2 -> x0, waiting for transfers between devices: 112 us -> none  [local(): mine = lax.psum_scatter(term, 'tensor', scatter_dimension=0, tiled=True)]
    dot_general x12 -> x2, matrix products: 93.9 us -> 34 us  [local_pairs(): mixed = jnp.dot(gathered, out_weight, preferred_element_type=jnp.float32)]
    pallas_call x0 -> x21, Pallas kernels: none -> 55.7 us  [the longest x4 39.1 us: project(): pl.pallas_call(project_kernel, grid_spec=pltpu.PrefetchScalarGridSpec(num...]
    ppermute x0 -> x29, starting transfers between devices: none -> 53.2 us  [swap(): return lax.ppermute(value, 'tensor', [(i, i ^ bit) for i in range(devices)])]
    ppermute x0 -> x29, waiting for transfers between devices: none -> 50.7 us  [swap(): return lax.ppermute(value, 'tensor', [(i, i ^ bit) for i in range(devices)])]
    psum x1 -> x0, blocking collectives: 34.9 us -> none  [local(): sums = lax.psum(jnp.sum(values * values, -1), 'tensor')]
    all_to_all x2 -> x0, waiting for transfers between devices: 25.2 us -> none  [the longest x1 25.2 us: local(): lax.all_to_all(sent, 'tensor', split_axis=1, concat_axis=1, tiled=True)]
    lt x1, other arithmetic: 21.3 us -> 0.08 us  [slot_layout(): held = columns[None, :] < stripes[:, None]]
  transfers between devices with their start and end apart: 6 -> 31, of which waited for: 5 -> 14; matrix products, arithmetic and copies ran while one was open for 25% -> 10% of each run, Pallas kernels for 0% -> 16%
where the time goes in v1:
time: 302 us; the launch traced here: 301 us
  waiting for transfers between devices  122 us (40%)
  Pallas kernels  55.7 us (18%)
  starting transfers between devices  53.4 us (18%)
  matrix products  34 us (11%)
  local copies, waits for them, and re-layouts  16.3 us (5%)
  between operations  13.9 us (5%)
  other arithmetic  4.95 us (2%)
    all_gather x2, waiting for transfers between devices, local_pairs(): gathered = lax.all_gather(attention[step], 'tensor', axis=1, tiled=True)  71.7 us
    ppermute x29, starting transfers between devices, swap(): return lax.ppermute(value, 'tensor', [(i, i ^ bit) for i in range(devices)])  53.2 us
    ppermute x29, waiting for transfers between devices, swap(): return lax.ppermute(value, 'tensor', [(i, i ^ bit) for i in range(devices)])  50.7 us
    pallas_call x4, Pallas kernels, project(): pl.pallas_call(project_kernel, grid_spec=pltpu.PrefetchScalarGridSpec(num...  39.1 us
    dot_general x2, matrix products, local_pairs(): mixed = jnp.dot(gathered, out_weight, preferred_element_type=jnp.float32)  34 us
    unnamed x41, local copies, waits for them, and re-layouts  10.5 us
    pallas_call x1, Pallas kernels, attend(): pl.pallas_call(attend_kernel, in_specs=[pl.BlockSpec(memory_space=pltpu.S...  8.86 us
    pallas_call x12, Pallas kernels, fold(): pl.pallas_call(lambda *refs: fold_kernel(steps, *refs), grid_spec=pltpu.P...  7.62 us
  transfers between devices with their start and end apart: 31, of which 14 were waited for; matrix products, arithmetic and copies ran while one was open for 10% of the time, Pallas kernels for 16%

profile of v1, /device:TPU:0, one launch (start us, length us, event | category | flops | bytes accessed | tf_op | source)
XLA Modules:
  0.0 300.7 jit_solution(16721302036461174604)
XLA Ops:
  6.5 1.2 multiply_reduce_fusion
  8.2 0.8 reshape.277
  9.0 1.6 constant_dynamic-slice_fusion
  10.7 2.6 collective-permute-start.21
  13.3 1.6 collective-permute-start.22
  15.1 3.0 %collective-permute-start.24 = (bf16[400,256]{1,0:T(8,128)(2,1)S(1)}, bf16[400,256]{1,0:T(8,128)(2,1)S(1)}, u32[]{:S(2)}, u32[]{:S(2)}) collective-permute-start(bf16[400,256]{1,0:T(8,128)(2,1)S(1)} %pad_maximum_fusion.5), channel_id=1, source_target_pairs={{0,8},{1,9},{2,10},{3,11},{4,12},{5,13},{6,14},{7,15},{8,0},{9,1},... | collective-permute-start | bytes 614408 | tf_op jit(solution)/shard_map/ppermute | solution.py:216
  18.3 0.7 fusion.4
  19.0 1.5 collective-permute-start.1
  20.5 2.0 collective-permute-done.1
  22.6 1.7 collective-permute-start.2
  24.3 5.0 %collective-permute-done.2 = f32[2,96]{1,0:T(2,128)S(1)} collective-permute-done((f32[2,96]{1,0:T(2,128)S(1)}, f32[2,96]{1,0:T(2,128)S(1)}, u32[]{:S(2)}, u32[]{:S(2)}) %collective-permute-start.2) | collective-permute-done | bytes 800 | tf_op jit(solution)/shard_map/ppermute | solution.py:216
  29.3 2.6 collective-permute-start.3
  32.0 1.8 collective-permute-done.3
  33.8 2.5 collective-permute-start.25
  36.5 9.6 %project.7 = (f32[8,192,256]{2,1,0:T(8,128)S(1)}, s16[1552,256]{1,0:T(8,128)(2,1)}) custom-call(s32[1]{0:T(128)} %bitcast.4.core, bf16[192,1024]{1,0:T(8,128)(2,1)S(1)} %bitcast.100, bf16[1024,18432]{1,0:T(8,128)(2,1)} %refs_1_.7, bf16[1024,18432]{1,0:T(8,128)(2,1)} %refs_1_.7), custom_call_target="tpu_custom_call" | custom-call | flops 1610612736 | bytes 10747904 | tf_op jit(solution)/shard_map/project/pallas_call | solution.py:291
  46.1 1.2 copy-done.2
  47.2 9.5 %project.6 = (f32[8,192,256]{2,1,0:T(8,128)S(1)}, s16[1552,256]{1,0:T(8,128)(2,1)}) custom-call(s32[1]{0:T(128)} %bitcast.4.core, bf16[192,1024]{1,0:T(8,128)(2,1)S(1)} %bitcast.101, bf16[1024,18432]{1,0:T(8,128)(2,1)} %refs_1_.7, bf16[1024,18432]{1,0:T(8,128)(2,1)} %refs_1_.7), custom_call_target="tpu_custom_call" | custom-call | flops 1610612736 | bytes 10747904 | tf_op jit(solution)/shard_map/project/pallas_call | solution.py:291
  56.8 10.5 %project.4 = (f32[8,192,384]{2,1,0:T(8,128)S(1)}, s16[1552,384]{1,0:T(8,128)(2,1)S(1)}) custom-call(s32[1]{0:T(128)} %bitcast.4.core, bf16[192,1024]{1,0:T(8,128)(2,1)S(1)} %bitcast.102, bf16[1024,18432]{1,0:T(8,128)(2,1)} %refs_1_.7, bf16[1024,18432]{1,0:T(8,128)(2,1)} %refs_1_.7, bf16[1024,18432]{1,0:T(8,128)(2,1)} %refs_1_.7, bf16[1024,18432]{1,0:T(8,128)(2,1)} %refs_1_.7), custom_call_target="tpu_custom_call" | custom-call | flops 2415919104 | bytes 16121856 | tf_op jit(solution)/shard_map/project/pallas_call | solution.py:291
  67.3 1.4 collective-permute-start.26
  68.7 0.7 bitcast_dynamic-update-slice_fusion.6
  69.4 3.4 %collective-permute-start.27 = (bf16[400,256]{1,0:T(8,128)(2,1)S(1)}, bf16[400,256]{1,0:T(8,128)(2,1)S(1)}, u32[]{:S(2)}, u32[]{:S(2)}) collective-permute-start(bf16[400,256]{1,0:T(8,128)(2,1)S(1)} %pad_maximum_fusion.8), channel_id=1, source_target_pairs={{0,14},{1,15},{2,12},{3,13},{4,10},{5,11},{6,8},{7,9},{8,6},{9,7},... | collective-permute-start | bytes 614408 | tf_op jit(solution)/shard_map/ppermute | solution.py:216
  72.8 0.7 bitcast_dynamic-update-slice_fusion.5
  73.5 0.7 bitcast_dynamic-update-slice_fusion.4
  74.2 0.7 bitcast_dynamic-update-slice_fusion.3
  74.9 0.7 bitcast_dynamic-update-slice_fusion.2
  75.6 1.2 collective-permute-done.26
  76.8 0.7 bitcast_dynamic-update-slice_fusion.1
  77.5 2.0 collective-permute-done.27
  80.2 9.5 %project.5 = (f32[8,192,256]{2,1,0:T(8,128)S(1)}, s16[1552,256]{1,0:T(8,128)(2,1)}) custom-call(s32[1]{0:T(128)} %bitcast.4.core, bf16[192,1024]{1,0:T(8,128)(2,1)S(1)} %bitcast.103, bf16[1024,18432]{1,0:T(8,128)(2,1)} %refs_1_.7, bf16[1024,18432]{1,0:T(8,128)(2,1)} %refs_1_.7), custom_call_target="tpu_custom_call" | custom-call | flops 1610612736 | bytes 10747904 | tf_op jit(solution)/shard_map/project/pallas_call | solution.py:291
  91.0 1.6 fold.12
  92.6 1.0 copy-done.6
  93.6 1.0 collective-permute-start.5
  94.6 1.5 copy-done.3
  96.7 1.1 collective-permute-start.17
  98.4 1.1 collective-permute-start.13
  100.0 1.1 collective-permute-start.9
  101.2 17.6 %collective-permute-done.17.refs_2_.refs_3_ = s16[784,256]{1,0:T(8,128)(2,1)S(1)} collective-permute-done((s16[784,256]{1,0:T(8,128)(2,1)S(1)}, s16[784,256]{1,0:T(8,128)(2,1)S(1)}, u32[]{:S(2)}, u32[]{:S(2)}) %collective-permute-start.17) | collective-permute-done | bytes 401440 | tf_op jit(solution)/shard_map/ppermute | solution.py:216
  118.9 0.9 fold.22
  119.8 8.5 %collective-permute-start.18 = (s16[400,256]{1,0:T(8,128)(2,1)}, s16[400,256]{1,0:T(8,128)(2,1)S(1)}, u32[]{:S(2)}, u32[]{:S(2)}) collective-permute-start(s16[400,256]{1,0:T(8,128)(2,1)} %get-tuple-element.66), channel_id=1, source_target_pairs={{0,4},{1,5},{2,6},{3,7},{4,0},{5,1},{6,2},{7,3},{8,12},{9,13},{10,... | collective-permute-start | bytes 614408 | tf_op jit(solution)/shard_map/ppermute | solution.py:216
  128.3 0.9 fold.19
  129.2 7.7 %collective-permute-start.14 = (s16[400,256]{1,0:T(8,128)(2,1)}, s16[400,256]{1,0:T(8,128)(2,1)S(1)}, u32[]{:S(2)}, u32[]{:S(2)}) collective-permute-start(s16[400,256]{1,0:T(8,128)(2,1)} %get-tuple-element.58), channel_id=1, source_target_pairs={{0,4},{1,5},{2,6},{3,7},{4,0},{5,1},{6,2},{7,3},{8,12},{9,13},{10,... | collective-permute-start | bytes 614408 | tf_op jit(solution)/shard_map/ppermute | solution.py:216
  136.8 0.9 fold.16
  137.8 6.7 %collective-permute-start.10 = (s16[400,256]{1,0:T(8,128)(2,1)}, s16[400,256]{1,0:T(8,128)(2,1)S(1)}, u32[]{:S(2)}, u32[]{:S(2)}) collective-permute-start(s16[400,256]{1,0:T(8,128)(2,1)} %get-tuple-element.50), channel_id=1, source_target_pairs={{0,4},{1,5},{2,6},{3,7},{4,0},{5,1},{6,2},{7,3},{8,12},{9,13},{10,... | collective-permute-start | bytes 614408 | tf_op jit(solution)/shard_map/ppermute | solution.py:216
  144.5 1.1 fold.13
  145.8 1.8 collective-permute-start.19
  147.6 1.0 copy-done.9
  148.7 1.3 collective-permute-start.15
  150.0 6.4 %collective-permute-done.10.refs_2_.refs_3_ = s16[400,256]{1,0:T(8,128)(2,1)S(1)} collective-permute-done((s16[400,256]{1,0:T(8,128)(2,1)}, s16[400,256]{1,0:T(8,128)(2,1)S(1)}, u32[]{:S(2)}, u32[]{:S(2)}) %collective-permute-start.10) | collective-permute-done | bytes 204832 | tf_op jit(solution)/shard_map/ppermute | solution.py:216
  156.6 0.7 slice.72
  157.4 1.7 collective-permute-done.19.landed
  159.2 1.6 collective-permute-done.15.landed
  160.8 3.8 %collective-permute-done.11.landed = s16[208,256]{1,0:T(8,128)(2,1)S(1)} collective-permute-done((s16[208,256]{1,0:T(8,128)(2,1)S(1)}, s16[208,256]{1,0:T(8,128)(2,1)S(1)}, u32[]{:S(2)}, u32[]{:S(2)}) %collective-permute-start.11) | collective-permute-done | bytes 106528 | tf_op jit(solution)/shard_map/ppermute | solution.py:216
  164.6 0.7 slice.73
  165.6 0.8 collective-permute-start.7
  167.1 6.5 %collective-permute-done.7.landed = s16[208,384]{1,0:T(8,128)(2,1)S(1)} collective-permute-done((s16[208,384]{1,0:T(8,128)(2,1)S(1)}, s16[208,384]{1,0:T(8,128)(2,1)S(1)}, u32[]{:S(2)}, u32[]{:S(2)}) %collective-permute-start.7) | collective-permute-done | bytes 159776 | tf_op jit(solution)/shard_map/ppermute | solution.py:216
  174.3 0.9 collective-permute-done.20
  176.6 8.9 %attend.1 = bf16[16,96,128]{2,1,0:T(8,128)(2,1)S(1)} custom-call(s32[24]{0:T(128)S(1)} %get-tuple-element.71.slot_request, bf16[16,96,128]{2,1,0:T(8,128)(2,1)S(1)} %bitcast.104, bf16[16,16,128]{2,1,0:T(8,128)(2,1)S(1)} %pad.11.new_keys, bf16[16,16,128]{2,1,0:T(8,128)(2,1)S(1)} %pad.12.new_values, bf16[8,400,256]{2,1,0:T(8,128)(2,1)} %bitcast_dynamic-update-slice_fusion.own, ...), custom_call_target="tpu_custom_call" | custom-call | flops 301989888 | bytes 3145728 | tf_op jit(solution)/shard_map/attend/pallas_call | solution.py:464
  185.5 0.7 copy.71
  186.5 0.7 copy.72
  187.3 42.6 %all-gather.5.cloned.1.call-done = bf16[96,16384]{1,0:T(8,128)(2,1)} async-done(((bf16[96,1024]{1,0:T(8,128)(2,1)}), bf16[96,16384]{1,0:T(8,128)(2,1)}) %all-gather.5.cloned.1.call-update) | async-done | bytes 3145744 | tf_op jit(solution)/shard_map/all_gather | solution.py:612
  229.9 17.1 %fusion.2 = bf16[1,96,1024]{2,1,0:T(8,128)(2,1)S(1)} fusion(bf16[96,16384]{1,0:T(8,128)(2,1)} %all-gather.5.cloned.1.call-done, bf16[16384,1024]{1,0:T(8,128)(2,1)} %param.11, f32[2,96,1024]{2,1,0:T(8,128)S(1)} %convert_element_type.54), kind=kOutput, calls=%fused_computation.4 | convolution fusion | flops 3221422080 | bytes 37289984 | tf_op jit(solution)/shard_map/dot_general | solution.py:613
  247.0 29.1 %all-gather.3.cloned.1.call-done = bf16[96,16384]{1,0:T(8,128)(2,1)} async-done(((bf16[96,1024]{1,0:T(8,128)(2,1)}), bf16[96,16384]{1,0:T(8,128)(2,1)}) %all-gather.3.cloned.1.call-update) | async-done | bytes 3145744 | tf_op jit(solution)/shard_map/all_gather | solution.py:612
  276.2 16.9 %fusion.3 = bf16[1,96,1024]{2,1,0:T(8,128)(2,1)S(1)} fusion(bf16[96,16384]{1,0:T(8,128)(2,1)} %all-gather.3.cloned.1.call-done, bf16[16384,1024]{1,0:T(8,128)(2,1)} %param.11, f32[2,96,1024]{2,1,0:T(8,128)S(1)} %convert_element_type.54), kind=kOutput, calls=%fused_computation.5 | convolution fusion | flops 3221422080 | bytes 37289984 | tf_op jit(solution)/shard_map/dot_general | solution.py:613
  293.0 0.8 pad_maximum_fusion.1
  (129 shorter events, 8.9 us)
Async XLA Ops:
  6.5 223.4 %all-gather.5.cloned.1.call-start = ((), (), s32[]{:S(2)}) async-start(), calls=%async_computation.1 | async-start | bytes 3342336 | tf_op jit(solution)/shard_map/all_gather | solution.py:612
  7.7 11.3 %collective-permute-start = (f32[2,96]{1,0:T(2,128)S(1)}, f32[2,96]{1,0:T(2,128)S(1)}, u32[]{:S(2)}, u32[]{:S(2)}) collective-permute-start(f32[2,96]{1,0:T(2,128)S(1)} %multiply_reduce_fusion), channel_id=1, source_target_pairs={{0,1},{1,0},{2,3},{3,2},{4,5},{5,4},{6,7},{7,6},{8,9},{9,8},{10,11... | collective-permute-start | bytes 2312 | tf_op jit(solution)/shard_map/ppermute | solution.py:216
  9.0 9.1 %copy-start.14 = (s32[16]{0:T(128)S(1)}, s32[16]{0:T(128)}, u32[]{:S(2)}) copy-start(s32[16]{0:T(128)} %param.14) | copy-start | bytes 196
  10.6 21.3 %copy-start.13 = (bf16[1024]{0:T(1024)(128)(2,1)S(1)}, bf16[1024]{0:T(1024)(128)(2,1)}, u32[]{:S(2)}) copy-start(bf16[1024]{0:T(1024)(128)(2,1)} %param.9) | copy-start | bytes 6148
  10.6 25.7 %copy-start.10 = (bf16[2,96,1024]{2,1,0:T(8,128)(2,1)S(1)}, bf16[2,96,1024]{2,1,0:T(8,128)(2,1)}, u32[]{:S(2)}) copy-start(bf16[2,96,1024]{2,1,0:T(8,128)(2,1)} %param.8) | copy-start | bytes 1179652
  10.7 56.6 %collective-permute-start.21 = (bf16[400,256]{1,0:T(8,128)(2,1)S(1)}, bf16[400,256]{1,0:T(8,128)(2,1)S(1)}, u32[]{:S(2)}, u32[]{:S(2)}) collective-permute-start(bf16[400,256]{1,0:T(8,128)(2,1)S(1)} %pad_maximum_fusion.2), channel_id=1, source_target_pairs={{0,2},{1,3},{2,0},{3,1},{4,6},{5,7},{6,4},{7,5},{8,10},{9,11},{10,... | collective-permute-start | bytes 614408 | tf_op jit(solution)/shard_map/ppermute | solution.py:216
  13.3 56.1 %collective-permute-start.22 = (bf16[400,256]{1,0:T(8,128)(2,1)S(1)}, bf16[400,256]{1,0:T(8,128)(2,1)S(1)}, u32[]{:S(2)}, u32[]{:S(2)}) collective-permute-start(bf16[400,256]{1,0:T(8,128)(2,1)S(1)} %pad_maximum_fusion.3), channel_id=1, source_target_pairs={{0,4},{1,5},{2,6},{3,7},{4,0},{5,1},{6,2},{7,3},{8,12},{9,13},{10,... | collective-permute-start | bytes 614408 | tf_op jit(solution)/shard_map/ppermute | solution.py:216
  15.0 58.6 %collective-permute-start.23 = (bf16[400,256]{1,0:T(8,128)(2,1)S(1)}, bf16[400,256]{1,0:T(8,128)(2,1)S(1)}, u32[]{:S(2)}, u32[]{:S(2)}) collective-permute-start(bf16[400,256]{1,0:T(8,128)(2,1)S(1)} %pad_maximum_fusion.4), channel_id=1, source_target_pairs={{0,6},{1,7},{2,4},{3,5},{4,2},{5,3},{6,0},{7,1},{8,14},{9,15},{10,... | collective-permute-start | bytes 614408 | tf_op jit(solution)/shard_map/ppermute | solution.py:216
  15.1 59.2 %collective-permute-start.24 = (bf16[400,256]{1,0:T(8,128)(2,1)S(1)}, bf16[400,256]{1,0:T(8,128)(2,1)S(1)}, u32[]{:S(2)}, u32[]{:S(2)}) collective-permute-start(bf16[400,256]{1,0:T(8,128)(2,1)S(1)} %pad_maximum_fusion.5), channel_id=1, source_target_pairs={{0,8},{1,9},{2,10},{3,11},{4,12},{5,13},{6,14},{7,15},{8,0},{9,1},... | collective-permute-start | bytes 614408 | tf_op jit(solution)/shard_map/ppermute | solution.py:216
  19.0 3.6 %collective-permute-start.1 = (f32[2,96]{1,0:T(2,128)S(1)}, f32[2,96]{1,0:T(2,128)S(1)}, u32[]{:S(2)}, u32[]{:S(2)}) collective-permute-start(f32[2,96]{1,0:T(2,128)S(1)} %add.186), channel_id=1, source_target_pairs={{0,2},{1,3},{2,0},{3,1},{4,6},{5,7},{6,4},{7,5},{8,10},{9,11},{10,... | collective-permute-start | bytes 2312 | tf_op jit(solution)/shard_map/ppermute | solution.py:216
  22.6 6.7 %collective-permute-start.2 = (f32[2,96]{1,0:T(2,128)S(1)}, f32[2,96]{1,0:T(2,128)S(1)}, u32[]{:S(2)}, u32[]{:S(2)}) collective-permute-start(f32[2,96]{1,0:T(2,128)S(1)} %add.187), channel_id=1, source_target_pairs={{0,4},{1,5},{2,6},{3,7},{4,0},{5,1},{6,2},{7,3},{8,12},{9,13},{10,... | collective-permute-start | bytes 2312 | tf_op jit(solution)/shard_map/ppermute | solution.py:216
  29.3 4.5 %collective-permute-start.3 = (f32[2,96]{1,0:T(2,128)S(1)}, f32[2,96]{1,0:T(2,128)S(1)}, u32[]{:S(2)}, u32[]{:S(2)}) collective-permute-start(f32[2,96]{1,0:T(2,128)S(1)} %add.188), channel_id=1, source_target_pairs={{0,8},{1,9},{2,10},{3,11},{4,12},{5,13},{6,14},{7,15},{8,0},{9,1},... | collective-permute-start | bytes 2312 | tf_op jit(solution)/shard_map/ppermute | solution.py:216
  33.8 41.1 %collective-permute-start.25 = (bf16[400,256]{1,0:T(8,128)(2,1)S(1)}, bf16[400,256]{1,0:T(8,128)(2,1)S(1)}, u32[]{:S(2)}, u32[]{:S(2)}) collective-permute-start(bf16[400,256]{1,0:T(8,128)(2,1)S(1)} %pad_maximum_fusion.6), channel_id=1, source_target_pairs={{0,10},{1,11},{2,8},{3,9},{4,14},{5,15},{6,12},{7,13},{8,2},{9,3},... | collective-permute-start | bytes 614408 | tf_op jit(solution)/shard_map/ppermute | solution.py:216
  46.1 1.2 copy-start.2
  56.8 10.5 %copy-start = (f32[8,192,256]{2,1,0:T(8,128)}, f32[8,192,256]{2,1,0:T(8,128)S(1)}, u32[]{:S(2)}) copy-start(f32[8,192,256]{2,1,0:T(8,128)S(1)} %get-tuple-element.53.refs_1_) | copy-start | bytes 4718596
  67.3 9.6 %collective-permute-start.26 = (bf16[400,256]{1,0:T(8,128)(2,1)S(1)}, bf16[400,256]{1,0:T(8,128)(2,1)S(1)}, u32[]{:S(2)}, u32[]{:S(2)}) collective-permute-start(bf16[400,256]{1,0:T(8,128)(2,1)S(1)} %pad_maximum_fusion.7), channel_id=1, source_target_pairs={{0,12},{1,13},{2,14},{3,15},{4,8},{5,9},{6,10},{7,11},{8,4},{9,5},... | collective-permute-start | bytes 614408 | tf_op jit(solution)/shard_map/ppermute | solution.py:216
  69.4 10.1 %collective-permute-start.27 = (bf16[400,256]{1,0:T(8,128)(2,1)S(1)}, bf16[400,256]{1,0:T(8,128)(2,1)S(1)}, u32[]{:S(2)}, u32[]{:S(2)}) collective-permute-start(bf16[400,256]{1,0:T(8,128)(2,1)S(1)} %pad_maximum_fusion.8), channel_id=1, source_target_pairs={{0,14},{1,15},{2,12},{3,13},{4,10},{5,11},{6,8},{7,9},{8,6},{9,7},... | collective-permute-start | bytes 614408 | tf_op jit(solution)/shard_map/ppermute | solution.py:216
  73.5 17.5 %collective-permute-start.4 = (s16[1552,384]{1,0:T(8,128)(2,1)S(1)}, s16[1552,384]{1,0:T(8,128)(2,1)S(1)}, u32[]{:S(2)}, u32[]{:S(2)}) collective-permute-start(s16[1552,384]{1,0:T(8,128)(2,1)S(1)} %get-tuple-element.38), channel_id=1, source_target_pairs={{0,1},{1,0},{2,3},{3,2},{4,5},{5,4},{6,7},{7,6},{8,9},{9,8},{10,11... | collective-permute-start | bytes 3575816 | tf_op jit(solution)/shard_map/ppermute | solution.py:216
  80.2 10.6 %copy-start.12 = (s32[16,16]{1,0:T(8,128)S(1)}, s32[16,16]{1,0:T(8,128)}, u32[]{:S(2)}) copy-start(s32[16,16]{1,0:T(8,128)} %param.15) | copy-start | bytes 3076
  80.2 84.5 %collective-permute-start.28 = (bf16[8,400,256]{2,1,0:T(8,128)(2,1)}, bf16[8,400,256]{2,1,0:T(8,128)(2,1)}, u32[]{:S(2)}, u32[]{:S(2)}) collective-permute-start(bf16[8,400,256]{2,1,0:T(8,128)(2,1)} %bitcast_dynamic-update-slice_fusion.own), channel_id=1, source_target_pairs={{0,1},{1,0},{2,3},{3,2},{4,5},{5,4},{6,7},{7,6},{8,9},{9,8},{10,11... | collective-permute-start | bytes 4915208 | tf_op jit(solution)/shard_map/ppermute | solution.py:216
  89.7 2.8 copy-start.4
  89.7 4.9 %collective-permute-start.16 = (s16[1552,256]{1,0:T(8,128)(2,1)}, s16[1552,256]{1,0:T(8,128)(2,1)S(1)}, u32[]{:S(2)}, u32[]{:S(2)}) collective-permute-start(s16[1552,256]{1,0:T(8,128)(2,1)} %get-tuple-element.62), channel_id=1, source_target_pairs={{0,1},{1,0},{2,3},{3,2},{4,5},{5,4},{6,7},{7,6},{8,9},{9,8},{10,11... | collective-permute-start | bytes 2383880 | tf_op jit(solution)/shard_map/ppermute | solution.py:216
  90.2 7.6 %collective-permute-start.12 = (s16[1552,256]{1,0:T(8,128)(2,1)}, s16[1552,256]{1,0:T(8,128)(2,1)S(1)}, u32[]{:S(2)}, u32[]{:S(2)}) collective-permute-start(s16[1552,256]{1,0:T(8,128)(2,1)} %get-tuple-element.54), channel_id=1, source_target_pairs={{0,1},{1,0},{2,3},{3,2},{4,5},{5,4},{6,7},{7,6},{8,9},{9,8},{10,11... | collective-permute-start | bytes 2383880 | tf_op jit(solution)/shard_map/ppermute | solution.py:216
  90.2 9.2 %collective-permute-start.8 = (s16[1552,256]{1,0:T(8,128)(2,1)}, s16[1552,256]{1,0:T(8,128)(2,1)S(1)}, u32[]{:S(2)}, u32[]{:S(2)}) collective-permute-start(s16[1552,256]{1,0:T(8,128)(2,1)} %get-tuple-element.46), channel_id=1, source_target_pairs={{0,1},{1,0},{2,3},{3,2},{4,5},{5,4},{6,7},{7,6},{8,9},{9,8},{10,11... | collective-permute-start | bytes 2383880 | tf_op jit(solution)/shard_map/ppermute | solution.py:216
  92.6 1.0 copy-start.6
  93.6 50.9 %collective-permute-start.5 = (s16[784,384]{1,0:T(8,128)(2,1)}, s16[784,384]{1,0:T(8,128)(2,1)S(1)}, u32[]{:S(2)}, u32[]{:S(2)}) collective-permute-start(s16[784,384]{1,0:T(8,128)(2,1)} %get-tuple-element.40), channel_id=1, source_target_pairs={{0,2},{1,3},{2,0},{3,1},{4,6},{5,7},{6,4},{7,5},{8,10},{9,11},{10,... | collective-permute-start | bytes 1806344 | tf_op jit(solution)/shard_map/ppermute | solution.py:216
  94.6 3.2 %copy-start.1 = (f32[8,192,256]{2,1,0:T(8,128)S(1)}, f32[8,192,256]{2,1,0:T(8,128)}, u32[]{:S(2)}) copy-start(f32[8,192,256]{2,1,0:T(8,128)} %copy-done) | copy-start | bytes 4718596
  94.6 1.5 copy-start.3
  96.7 2.7 copy-start.5
  96.7 22.2 %collective-permute-start.17 = (s16[784,256]{1,0:T(8,128)(2,1)S(1)}, s16[784,256]{1,0:T(8,128)(2,1)S(1)}, u32[]{:S(2)}, u32[]{:S(2)}) collective-permute-start(s16[784,256]{1,0:T(8,128)(2,1)S(1)} %get-tuple-element.64), channel_id=1, source_target_pairs={{0,2},{1,3},{2,0},{3,1},{4,6},{5,7},{6,4},{7,5},{8,10},{9,11},{10,... | collective-permute-start | bytes 1204232 | tf_op jit(solution)/shard_map/ppermute | solution.py:216
  98.4 29.9 %collective-permute-start.13 = (s16[784,256]{1,0:T(8,128)(2,1)S(1)}, s16[784,256]{1,0:T(8,128)(2,1)S(1)}, u32[]{:S(2)}, u32[]{:S(2)}) collective-permute-start(s16[784,256]{1,0:T(8,128)(2,1)S(1)} %get-tuple-element.56), channel_id=1, source_target_pairs={{0,2},{1,3},{2,0},{3,1},{4,6},{5,7},{6,4},{7,5},{8,10},{9,11},{10,... | collective-permute-start | bytes 1204232 | tf_op jit(solution)/shard_map/ppermute | solution.py:216
  100.0 36.9 %collective-permute-start.9 = (s16[784,256]{1,0:T(8,128)(2,1)S(1)}, s16[784,256]{1,0:T(8,128)(2,1)S(1)}, u32[]{:S(2)}, u32[]{:S(2)}) collective-permute-start(s16[784,256]{1,0:T(8,128)(2,1)S(1)} %get-tuple-element.48), channel_id=1, source_target_pairs={{0,2},{1,3},{2,0},{3,1},{4,6},{5,7},{6,4},{7,5},{8,10},{9,11},{10,... | collective-permute-start | bytes 1204232 | tf_op jit(solution)/shard_map/ppermute | solution.py:216
  119.8 24.7 %copy-start.7 = (f32[4,192,384]{2,1,0:T(8,128)S(1)}, f32[4,192,384]{2,1,0:T(8,128)}, u32[]{:S(2)}) copy-start(f32[4,192,384]{2,1,0:T(8,128)} %copy-done.6) | copy-start | bytes 3538948
  119.8 25.9 %collective-permute-start.18 = (s16[400,256]{1,0:T(8,128)(2,1)}, s16[400,256]{1,0:T(8,128)(2,1)S(1)}, u32[]{:S(2)}, u32[]{:S(2)}) collective-permute-start(s16[400,256]{1,0:T(8,128)(2,1)} %get-tuple-element.66), channel_id=1, source_target_pairs={{0,4},{1,5},{2,6},{3,7},{4,0},{5,1},{6,2},{7,3},{8,12},{9,13},{10,... | collective-permute-start | bytes 614408 | tf_op jit(solution)/shard_map/ppermute | solution.py:216
  129.2 16.4 %copy-start.8 = (f32[2,192,256]{2,1,0:T(8,128)}, f32[2,192,256]{2,1,0:T(8,128)S(1)}, u32[]{:S(2)}) copy-start(f32[2,192,256]{2,1,0:T(8,128)S(1)} %get-tuple-element.57.refs_1_) | copy-start | bytes 1179652
  129.2 18.4 %collective-permute-start.14 = (s16[400,256]{1,0:T(8,128)(2,1)}, s16[400,256]{1,0:T(8,128)(2,1)S(1)}, u32[]{:S(2)}, u32[]{:S(2)}) collective-permute-start(s16[400,256]{1,0:T(8,128)(2,1)} %get-tuple-element.58), channel_id=1, source_target_pairs={{0,4},{1,5},{2,6},{3,7},{4,0},{5,1},{6,2},{7,3},{8,12},{9,13},{10,... | collective-permute-start | bytes 614408 | tf_op jit(solution)/shard_map/ppermute | solution.py:216
  137.8 18.6 %collective-permute-start.10 = (s16[400,256]{1,0:T(8,128)(2,1)}, s16[400,256]{1,0:T(8,128)(2,1)S(1)}, u32[]{:S(2)}, u32[]{:S(2)}) collective-permute-start(s16[400,256]{1,0:T(8,128)(2,1)} %get-tuple-element.50), channel_id=1, source_target_pairs={{0,4},{1,5},{2,6},{3,7},{4,0},{5,1},{6,2},{7,3},{8,12},{9,13},{10,... | collective-permute-start | bytes 614408 | tf_op jit(solution)/shard_map/ppermute | solution.py:216
  145.6 19.9 %collective-permute-start.6 = (s16[400,384]{1,0:T(8,128)(2,1)}, s16[400,384]{1,0:T(8,128)(2,1)S(1)}, u32[]{:S(2)}, u32[]{:S(2)}) collective-permute-start(s16[400,384]{1,0:T(8,128)(2,1)} %get-tuple-element.42), channel_id=1, source_target_pairs={{0,4},{1,5},{2,6},{3,7},{4,0},{5,1},{6,2},{7,3},{8,12},{9,13},{10,... | collective-permute-start | bytes 921608 | tf_op jit(solution)/shard_map/ppermute | solution.py:216
  145.8 13.3 %collective-permute-start.19 = (s16[208,256]{1,0:T(8,128)(2,1)S(1)}, s16[208,256]{1,0:T(8,128)(2,1)S(1)}, u32[]{:S(2)}, u32[]{:S(2)}) collective-permute-start(s16[208,256]{1,0:T(8,128)(2,1)S(1)} %get-tuple-element.68), channel_id=1, source_target_pairs={{0,8},{1,9},{2,10},{3,11},{4,12},{5,13},{6,14},{7,15},{8,0},{9,1},... | collective-permute-start | bytes 319496 | tf_op jit(solution)/shard_map/ppermute | solution.py:216
  147.6 1.0 copy-start.9
  148.7 12.0 %collective-permute-start.15 = (s16[208,256]{1,0:T(8,128)(2,1)S(1)}, s16[208,256]{1,0:T(8,128)(2,1)S(1)}, u32[]{:S(2)}, u32[]{:S(2)}) collective-permute-start(s16[208,256]{1,0:T(8,128)(2,1)S(1)} %get-tuple-element.60), channel_id=1, source_target_pairs={{0,8},{1,9},{2,10},{3,11},{4,12},{5,13},{6,14},{7,15},{8,0},{9,1},... | collective-permute-start | bytes 319496 | tf_op jit(solution)/shard_map/ppermute | solution.py:216
  156.5 8.0 %collective-permute-start.11 = (s16[208,256]{1,0:T(8,128)(2,1)S(1)}, s16[208,256]{1,0:T(8,128)(2,1)S(1)}, u32[]{:S(2)}, u32[]{:S(2)}) collective-permute-start(s16[208,256]{1,0:T(8,128)(2,1)S(1)} %get-tuple-element.52), channel_id=1, source_target_pairs={{0,8},{1,9},{2,10},{3,11},{4,12},{5,13},{6,14},{7,15},{8,0},{9,1},... | collective-permute-start | bytes 319496 | tf_op jit(solution)/shard_map/ppermute | solution.py:216
  165.6 8.0 %collective-permute-start.7 = (s16[208,384]{1,0:T(8,128)(2,1)S(1)}, s16[208,384]{1,0:T(8,128)(2,1)S(1)}, u32[]{:S(2)}, u32[]{:S(2)}) collective-permute-start(s16[208,384]{1,0:T(8,128)(2,1)S(1)} %get-tuple-element.44), channel_id=1, source_target_pairs={{0,8},{1,9},{2,10},{3,11},{4,12},{5,13},{6,14},{7,15},{8,0},{9,1},... | collective-permute-start | bytes 479240 | tf_op jit(solution)/shard_map/ppermute | solution.py:216
  173.9 1.3 collective-permute-start.20
  185.5 1.8 copy-start.11
  186.3 89.9 %all-gather.3.cloned.1.call-start = ((), (), s32[]{:S(2)}) async-start(), calls=%async_computation | async-start | bytes 3342336 | tf_op jit(solution)/shard_map/all_gather | solution.py:612
Sparse Core Ops, SparseCore 0:
  186.4 43.4 all-gather.4
  232.1 44.0 all-gather.2

commit v2 on v1

--- a/solution.py
+++ b/solution.py
@@ -206,7 +206,10 @@
 
 
 VMEM_LIMIT = 48 * 1024 * 1024
-LEVELS = 32000.0
+LOW_BITS = 4
+PACKED = 16 // LOW_BITS
+LEVELS = 32600.0 * 2**LOW_BITS
+POWER_STEPS = 8.0
 TILE = 16
 MESH_BITS = (1, 2, 4, 8)
 
@@ -216,15 +219,32 @@
     return lax.ppermute(value, "tensor", [(i, i ^ bit) for i in range(devices)])
 
 
+def coded_rows(rows):
+    return rows + rows // PACKED
+
+
 def encode(block):
     top = jnp.max(jnp.abs(block), 0, keepdims=True)
-    power = jnp.ceil(jnp.log2(jnp.maximum(top, 1e-30)))
-    codes = jnp.round(block * (jnp.exp2(-power) * LEVELS))
-    return codes.astype(jnp.int32).astype(jnp.int16), power
+    power = jnp.ceil(jnp.log2(jnp.maximum(top, 1e-30)) * POWER_STEPS)
+    codes = jnp.round(block * (jnp.exp2(power * (-1.0 / POWER_STEPS)) * LEVELS)).astype(jnp.int32)
+    low = codes & (2**LOW_BITS - 1)
+    part = block.shape[0] // PACKED
+    packed = low[:part]
+    for i in range(1, PACKED):
+        packed = packed + (low[i * part : (i + 1) * part] << (LOW_BITS * i))
+    high = (codes >> LOW_BITS).astype(jnp.int16)
+    return jnp.concatenate([high, (packed - 32768).astype(jnp.int16)], 0), power
 
 
 def decode(codes, power):
-    return codes.astype(jnp.int32).astype(jnp.float32) * (jnp.exp2(power) * (1.0 / LEVELS))
+    rows = codes.shape[0] * PACKED // (PACKED + 1)
+    high = codes[:rows].astype(jnp.int32) << LOW_BITS
+    packed = codes[rows:].astype(jnp.int32) + 32768
+    low = jnp.concatenate(
+        [(packed >> (LOW_BITS * i)) & (2**LOW_BITS - 1) for i in range(PACKED)], 0
+    )
+    scale = jnp.exp2(power * (1.0 / POWER_STEPS)) * (1.0 / LEVELS)
+    return (high + low).astype(jnp.float32) * scale
 
 
 def pick_row(rows, index):
@@ -233,7 +253,7 @@
 
 
 def store_codes(sent, powers, block, index, steps):
-    rows = block.shape[0]
+    rows = coded_rows(block.shape[0])
     codes, power = encode(block)
     sent[pl.ds(pl.multiple_of(index * rows, TILE), rows), :] = codes
 
@@ -248,61 +268,77 @@
         sent[pl.ds(steps * rows, TILE), :] = powers[...].astype(jnp.int32).astype(jnp.int16)
 
 
+K_PARTS = 4
+
+
 def project_kernel(core, normed, *refs):
-    weights = refs[:-3]
+    weights = refs[:-4]
     kept, sent, powers = refs[-3:]
     half = len(weights) // 2
+    depth = normed.shape[1] // K_PARTS
     index = pl.program_id(0)
 
     def product(blocks):
-        terms = [
-            jnp.dot(normed[...], w[...], preferred_element_type=jnp.float32) for w in blocks
-        ]
-        return terms[0] if len(terms) == 1 else jnp.concatenate(terms, 1)
+        wide = []
+        for first in range(0, len(blocks), K_PARTS):
+            total = None
+            for part in range(K_PARTS):
+                term = jnp.dot(
+                    normed[:, part * depth : (part + 1) * depth],
+                    blocks[first + part][...],
+                    preferred_element_type=jnp.float32,
+                )
+                total = term if total is None else total + term
+            wide.append(total)
+        return wide[0] if len(wide) == 1 else jnp.concatenate(wide, 1)
 
     store_codes(sent, powers, product(weights[half:]), index, KVH)
     kept[0] = product(weights[:half])
 
 
-def project(core, normed, qkv_weight, chunk, with_pair):
+def project(core, normed, qkv_weight, chunk, with_pair, after):
     rows, width = normed.shape
     columns = 2 * HD + (HD if with_pair else 0)
     per_group = GW // (2 * HD)
-
-    def wide(other):
+    depth = width // K_PARTS
+
+    def wide(other, part):
         def place(t, c):
             mine = c[0] if not other else 1 - c[0]
-            return (0, t * per_group + mine * (GQ // 4) + chunk)
-
-        return pl.BlockSpec((width, 2 * HD), place)
-
-    def narrow(other):
+            return (part, t * per_group + mine * (GQ // 4) + chunk)
+
+        return pl.BlockSpec((depth, 2 * HD), place)
+
+    def narrow(other, part):
         def place(t, c):
             mine = c[0] if not other else 1 - c[0]
-            return (0, t * (GW // HD) + GQ + mine)
-
-        return pl.BlockSpec((width, HD), place)
+            return (part, t * (GW // HD) + GQ + mine)
+
+        return pl.BlockSpec((depth, HD), place)
 
     specs = []
     for other in (False, True):
-        specs.append(wide(other))
+        specs += [wide(other, part) for part in range(K_PARTS)]
         if with_pair:
-            specs.append(narrow(other))
+            specs += [narrow(other, part) for part in range(K_PARTS)]
+    sent_rows = KVH * coded_rows(rows) + TILE
     return pl.pallas_call(
         project_kernel,
         grid_spec=pltpu.PrefetchScalarGridSpec(
             num_scalar_prefetch=1,
             grid=(KVH,),
-            in_specs=[pl.BlockSpec((rows, width), lambda t, c: (0, 0))] + specs,
+            in_specs=[pl.BlockSpec((rows, width), lambda t, c: (0, 0))]
+            + specs
+            + [pl.BlockSpec(memory_space=pl.ANY)],
             out_specs=[
                 pl.BlockSpec((1, rows, columns), lambda t, c: (t, 0, 0)),
-                pl.BlockSpec((KVH * rows + TILE, columns), lambda t, c: (0, 0)),
+                pl.BlockSpec((sent_rows, columns), lambda t, c: (0, 0)),
             ],
             scratch_shapes=[pltpu.VMEM((TILE, columns), jnp.float32)],
         ),
         out_shape=[
             jax.ShapeDtypeStruct((KVH, rows, columns), jnp.float32),
-            jax.ShapeDtypeStruct((KVH * rows + TILE, columns), jnp.int16),
+            jax.ShapeDtypeStruct((sent_rows, columns), jnp.int16),
         ],
         compiler_params=pltpu.CompilerParams(vmem_limit_bytes=VMEM_LIMIT),
         cost_estimate=pl.CostEstimate(
@@ -311,12 +347,12 @@
             transcendentals=0,
         ),
         name="project",
-    )(core, normed, *([qkv_weight] * len(specs)))
+    )(core, normed, *([qkv_weight] * len(specs)), after)
 
 
 def fold_kernel(steps, bit, held, landed, landed_powers, kept, sent, powers):
     index = pl.program_id(0)
-    rows = held.shape[1]
+    rows = coded_rows(held.shape[1])
     rows_of_powers = landed_powers[...].astype(jnp.int32).astype(jnp.float32)
 
     def total(side):
@@ -332,6 +368,7 @@
 def fold(bit, held, landed):
     blocks, rows, columns = held.shape
     steps = blocks // 2
+    coded = coded_rows(rows)
     return pl.pallas_call(
         lambda *refs: fold_kernel(steps, *refs),
         grid_spec=pltpu.PrefetchScalarGridSpec(
@@ -339,18 +376,18 @@
             grid=(steps,),
             in_specs=[
                 pl.BlockSpec((2, rows, columns), lambda i, b: (i, 0, 0)),
-                pl.BlockSpec((2 * rows, columns), lambda i, b: (i, 0)),
-                pl.BlockSpec((TILE, columns), lambda i, b: (blocks * rows // TILE, 0)),
+                pl.BlockSpec((2 * coded, columns), lambda i, b: (i, 0)),
+                pl.BlockSpec((TILE, columns), lambda i, b: (blocks * coded // TILE, 0)),
             ],
             out_specs=[
                 pl.BlockSpec((1, rows, columns), lambda i, b: (i, 0, 0)),
-                pl.BlockSpec((steps * rows + TILE, columns), lambda i, b: (0, 0)),
+                pl.BlockSpec((steps * coded + TILE, columns), lambda i, b: (0, 0)),
             ],
             scratch_shapes=[pltpu.VMEM((TILE, columns), jnp.float32)],
         ),
         out_shape=[
             jax.ShapeDtypeStruct((steps, rows, columns), jnp.float32),
-            jax.ShapeDtypeStruct((steps * rows + TILE, columns), jnp.int16),
+            jax.ShapeDtypeStruct((steps * coded + TILE, columns), jnp.int16),
         ],
         compiler_params=pltpu.CompilerParams(vmem_limit_bytes=VMEM_LIMIT),
         cost_estimate=pl.CostEstimate(
@@ -362,20 +399,134 @@
     )(bit, held, landed, landed)
 
 
-def finish_kernel(held, landed, joined):
+def finish_kernel(core, held, landed, cosine, sine, after, queries, *pair):
     rows = held.shape[1]
-    power = landed[pl.ds(rows, TILE), :].astype(jnp.int32).astype(jnp.float32)[0:1]
-    joined[...] = (held[0] + decode(landed[pl.ds(0, rows), :], power)).astype(jnp.bfloat16)
-
-
-def finish(held, landed):
+    coded = coded_rows(rows)
+    power = landed[pl.ds(coded, TILE), :].astype(jnp.int32).astype(jnp.float32)[0:1]
+    total = held[0] + decode(landed[pl.ds(0, coded), :], power)
+    joined = total.astype(jnp.bfloat16)
+    parts = []
+    for head in range(joined.shape[1] // HD):
+        raw = joined[:, head * HD : (head + 1) * HD]
+        wide = raw.astype(jnp.float32)
+        turned = wide * cosine[...] + pltpu.roll(wide, HD // 2, 1) * sine[...]
+        parts.append((raw, turned.astype(jnp.bfloat16)))
+    queries[...] = jnp.concatenate([parts[0][1], parts[1][1]], 1)
+    if pair:
+        raw, turned = parts[2]
+        pair[0][...] = jnp.where(core[0] == 0, turned.astype(jnp.float32), raw.astype(jnp.float32)).astype(
+            jnp.bfloat16
+        )
+
+
+def finish(core, held, landed, cosine, sine, after):
     _, rows, columns = held.shape
+    whole = pl.BlockSpec(memory_space=pltpu.VMEM)
+    shapes = [jax.ShapeDtypeStruct((rows, 2 * HD), jnp.bfloat16)]
+    if columns > 2 * HD:
+        shapes.append(jax.ShapeDtypeStruct((rows, HD), jnp.bfloat16))
     return pl.pallas_call(
         finish_kernel,
-        out_shape=jax.ShapeDtypeStruct((rows, columns), jnp.bfloat16),
+        in_specs=[pl.BlockSpec(memory_space=pltpu.SMEM)]
+        + [whole] * 4
+        + [pl.BlockSpec(memory_space=pl.ANY)],
+        out_specs=[whole] * len(shapes),
+        out_shape=shapes,
         compiler_params=pltpu.CompilerParams(vmem_limit_bytes=VMEM_LIMIT),
         name="finish",
-    )(held, landed)
+    )(core, held, landed, cosine, sine, after)
+
+
+def mix_kernel(places, *refs):
+    pieces, weights, start, mixed = refs[0:2], refs[2], refs[3], refs[4]
+    total = refs[5]
+    step = pl.program_id(0)
+    depth = weights.shape[0]
+    per_piece = pieces[0].shape[1] // depth
+
+    @pl.when(step == 0)
+    def _():
+        total[...] = start[...].astype(jnp.float32)
+
+    for part in range(2 * per_piece):
+
+        @pl.when(step == part)
+        def _():
+            first = part % per_piece * depth
+            total[...] += jnp.dot(
+                pieces[part // per_piece][:, first : first + depth],
+                weights[...],
+                preferred_element_type=jnp.float32,
+            )
+
+    @pl.when(step == 2 * per_piece - 1)
+    def _():
+        mixed[...] = total[...].astype(mixed.dtype)
+
+
+def mix(places, pieces, out_weight, start, dtype):
+    rows, width = pieces[0].shape
+    columns = out_weight.shape[1]
+    depth = width // 2
+    whole = pl.BlockSpec((rows, width), lambda i, p: (0, 0))
+    return pl.pallas_call(
+        mix_kernel,
+        grid_spec=pltpu.PrefetchScalarGridSpec(
+            num_scalar_prefetch=1,
+            grid=(4,),
+            in_specs=[
+                whole,
+                whole,
+                pl.BlockSpec((depth, columns), lambda i, p: (p[i // 2] * 2 + i % 2, 0)),
+                pl.BlockSpec((rows, columns), lambda i, p: (0, 0)),
+            ],
+            out_specs=pl.BlockSpec((rows, columns), lambda i, p: (0, 0)),
+            scratch_shapes=[pltpu.VMEM((rows, columns), jnp.float32)],
+        ),
+        out_shape=jax.ShapeDtypeStruct((rows, columns), dtype),
+        compiler_params=pltpu.CompilerParams(vmem_limit_bytes=VMEM_LIMIT),
+        cost_estimate=pl.CostEstimate(
+            flops=4 * rows * width * columns,
+            bytes_accessed=4 * width * columns + rows * (4 * width + 8 * columns),
+            transcendentals=0,
+        ),
+        name="mix",
+    )(places, *pieces, out_weight, start)
+
+
+def along(value, pairs):
+    devices = lax.axis_size("tensor")
+    side = devices // 4
+    table = [
+        (source * side + i, target * side + i) for source, target in pairs for i in range(side)
+    ]
+    return lax.ppermute(value, "tensor", table)
+
+
+def gather_and_mix(attention, out_weight, start, device):
+    line = device // 4
+    inner = (line == 1) | (line == 2)
+    near = swap(attention, 4)
+    cross = along(attention, [(1, 2), (2, 1)])
+    pieces = {0: attention, 1: near}
+    across = {0: swap(attention, 2)}
+    passed = along(cross, [(1, 0), (2, 3)])
+    cross_near = along(near, [(1, 2), (2, 1)])
+    across[1] = swap(near, 2)
+    pieces[2] = jnp.where(inner, cross_near, passed)
+    last = along(cross_near, [(1, 0), (2, 3)])
+    across[2] = swap(pieces[2], 2)
+    pieces[3] = jnp.where(inner, cross, last)
+    across[3] = swap(pieces[3], 2)
+    mixed = start
+    order = [(0, 0), (1, 0), (0, 2), (1, 2), (2, 0), (2, 2), (3, 0), (3, 2)]
+    for number, (k, y) in enumerate(order):
+        piece = (across if y else pieces)[k]
+        owner = device ^ (4 * k + y)
+        places = jnp.stack([owner, owner ^ 1])
+        dtype = jnp.bfloat16 if number == len(order) - 1 else jnp.float32
+        mixed = mix(places, [piece, swap(piece, 1)], out_weight, mixed, dtype)
+    return mixed
 
 
 def attend_kernel(
@@ -546,34 +697,49 @@
     ).astype(jnp.bfloat16)
     normed = normed.reshape(rows, width)
 
-    own, other = handover(cache_pool, cache_scale, chip)
-
-    bits = [jnp.reshape((device >> b) & 1, (1,)).astype(jnp.int32) for b in range(4)]
-    chunks = []
-    for chunk in range(GQ // 4):
-        held, sent = project(bits[0], normed, qkv_weight, chunk, chunk == 0)
-        for b in (1, 2, 3):
-            held, sent = fold(bits[b], held, swap(sent, MESH_BITS[b - 1]))
-        chunks.append(finish(held, swap(sent, MESH_BITS[3])))
-    pair = chunks[0][:, 2 * HD :]
-    query_columns = jnp.concatenate([chunks[0][:, : 2 * HD]] + chunks[1:], 1)
-    pair_other = swap(pair, 1)
-    raw_keys = jnp.where(core == 0, pair, pair_other)
-    raw_values = jnp.where(core == 0, pair_other, pair)
+    pool, sums = lax.optimization_barrier((cache_pool, sums))
+    own, other = handover(pool, cache_scale, chip)
 
     step_ids = jnp.arange(STEPS, dtype=jnp.int32)
     row_ids = jnp.arange(QR, dtype=jnp.int32)
     position = (
         request_length[None, :, None] + QR * step_ids[:, None, None] + row_ids[None, None, :]
     )
-    queries = rotate(
-        query_columns.reshape(STEPS, requests, QR, heads, HD).astype(jnp.float32),
-        position[..., None],
-    ).astype(jnp.bfloat16)
+    freqs = ROPE_BASE ** (-(jnp.arange(HD // 2, dtype=jnp.float32) * 2.0 / HD))
+    angles = position.reshape(rows, 1).astype(jnp.float32) * freqs
+    cosine = jnp.concatenate([jnp.cos(angles)] * 2, 1)
+    sine = jnp.concatenate([-jnp.sin(angles), jnp.sin(angles)], 1)
+
+    bits = [jnp.reshape((device >> b) & 1, (1,)).astype(jnp.int32) for b in range(4)]
+    count = GQ // 4
+    held, sent = [None] * count, [None] * count
+
+    def folded(chunk, b):
+        held[chunk], sent[chunk] = fold(bits[b], held[chunk], swap(sent[chunk], MESH_BITS[b - 1]))
+
+    for chunk in range(count):
+        after = held[chunk - 2] if chunk >= 2 else normed
+        held[chunk], sent[chunk] = project(
+            bits[0], normed, qkv_weight, chunk, chunk == 0, after
+        )
+        if chunk >= 1:
+            folded(chunk - 1, 1)
+    folded(count - 1, 1)
+    query_chunks = []
+    after = normed
+    for chunk in range(count):
+        folded(chunk, 2)
+        folded(chunk, 3)
+        done = finish(bits[0], held[chunk], swap(sent[chunk], MESH_BITS[3]), cosine, sine, after)
+        query_chunks.append(done[0])
+        if chunk == 0:
+            pair = done[1]
+            pair_other = swap(pair, 1)
+            after = pair_other
+    keys = jnp.where(core == 0, pair, pair_other)
+    raw_values = jnp.where(core == 0, pair_other, pair)
+    queries = jnp.concatenate(query_chunks, 1).reshape(STEPS, requests, QR, heads, HD)
     queries = jnp.transpose(queries, (1, 0, 2, 3, 4)).reshape(requests, STEPS * QR * heads, HD)
-    keys = rotate(
-        raw_keys.reshape(STEPS, requests, QR, HD).astype(jnp.float32), position
-    ).astype(jnp.bfloat16)
 
     def by_request(value):
         value = jnp.transpose(value.reshape(STEPS, requests, QR, HD), (1, 0, 2, 3))
@@ -606,13 +772,9 @@
     )
     attention = jnp.transpose(
         attention.reshape(requests, STEPS, QR, heads, HD), (1, 0, 2, 3, 4)
-    ).reshape(STEPS, requests * QR, heads * HD)
-    outputs = []
-    for step in range(STEPS):
-        gathered = lax.all_gather(attention[step], "tensor", axis=1, tiled=True)
-        mixed = jnp.dot(gathered, out_weight, preferred_element_type=jnp.float32)
-        outputs.append((hidden[step] + mixed).astype(jnp.bfloat16))
-    return jnp.stack(outputs)
+    ).reshape(rows, heads * HD)
+    mixed = gather_and_mix(attention, out_weight, hidden_in.reshape(rows, width), device)
+    return mixed.reshape(hidden_in.shape)
 
 
 def solution(mesh):

time: 302 us -> 279 us (0.924)
  waiting for transfers between devices: 122 us -> 69.6 us
  Pallas kernels: 55.7 us -> 97.3 us
  matrix products: 34 us -> 0 us
  starting transfers between devices: 53.4 us -> 77.4 us
  between operations: 13.9 us -> 0.85 us
  other arithmetic: 4.95 us -> 15.8 us
    all_gather x2 -> x0, waiting for transfers between devices: 71.7 us -> none  [local_pairs(): gathered = lax.all_gather(attention[step], 'tensor', axis=1, tiled=True)]
    pallas_call x4 -> x12, Pallas kernels: 0.16 us -> 36.7 us  [the longest x8 36.1 us: mix(): pl.pallas_call(mix_kernel, grid_spec=pltpu.PrefetchScalarGridSpec(num_sca...]
    dot_general x2 -> x0, matrix products: 34 us -> none  [local_pairs(): mixed = jnp.dot(gathered, out_weight, preferred_element_type=jnp.float32)]
    ppermute x29 -> x42, starting transfers between devices: 53.2 us -> 73.5 us  [swap(): return lax.ppermute(value, 'tensor', [(i, i ^ bit) for i in range(devices)])]
    ppermute x0 -> x4, waiting for transfers between devices: none -> 9.52 us  [along(): return lax.ppermute(value, 'tensor', table)]
    ppermute x29 -> x42, waiting for transfers between devices: 50.7 us -> 60.1 us  [swap(): return lax.ppermute(value, 'tensor', [(i, i ^ bit) for i in range(devices)])]
    ppermute x0 -> x4, starting transfers between devices: none -> 3.92 us  [along(): return lax.ppermute(value, 'tensor', table)]
    pallas_call x12, Pallas kernels: 7.62 us -> 11.3 us  [fold(): pl.pallas_call(lambda *refs: fold_kernel(steps, *refs), grid_spec=pltpu.P...]
  transfers between devices with their start and end apart: 31 -> 46, of which waited for: 14 -> 16; matrix products, arithmetic and copies ran while one was open for 10% -> 9% of each run, Pallas kernels for 16% -> 23%
where the time goes in v2:
time: 279 us; the launch traced here: 277 us
  Pallas kernels  97.3 us (35%)
  starting transfers between devices  77.4 us (28%)
  waiting for transfers between devices  69.6 us (25%)
  local copies, waits for them, and re-layouts  16 us (6%)
  other arithmetic  15.8 us (6%)
    ppermute x42, starting transfers between devices, swap(): return lax.ppermute(value, 'tensor', [(i, i ^ bit) for i in range(devices)])  73.5 us
    ppermute x42, waiting for transfers between devices, swap(): return lax.ppermute(value, 'tensor', [(i, i ^ bit) for i in range(devices)])  60.1 us
    pallas_call x4, Pallas kernels, project(): pl.pallas_call(project_kernel, grid_spec=pltpu.PrefetchScalarGridSpec(num...  40.5 us
    pallas_call x8, Pallas kernels, mix(): pl.pallas_call(mix_kernel, grid_spec=pltpu.PrefetchScalarGridSpec(num_sca...  36.1 us
    pallas_call x12, Pallas kernels, fold(): pl.pallas_call(lambda *refs: fold_kernel(steps, *refs), grid_spec=pltpu.P...  11.3 us
    ppermute x4, waiting for transfers between devices, along(): return lax.ppermute(value, 'tensor', table)  9.52 us
    pallas_call x1, Pallas kernels, attend(): pl.pallas_call(attend_kernel, in_specs=[pl.BlockSpec(memory_space=pltpu.S...  8.85 us
    unnamed x70, local copies, waits for them, and re-layouts  8.72 us
  transfers between devices with their start and end apart: 46, of which 16 were waited for; matrix products, arithmetic and copies ran while one was open for 9% of the time, Pallas kernels for 23%

profile of v2, /device:TPU:0, one launch (start us, length us, event | category | flops | bytes accessed | tf_op | source)
XLA Modules:
  0.0 277.0 jit_solution(3112175810541854293)
XLA Ops:
  0.0 1.2 fusion
  2.4 1.3 broadcast_add_fusion
  4.5 1.4 select_reduce_fusion.1
  6.6 2.7 collective-permute-start.1
  9.2 1.5 collective-permute-done.1
  10.8 2.1 collective-permute-start.2
  13.4 1.0 collective-permute-done.2
  14.4 3.0 %collective-permute-start.3 = (f32[2,96]{1,0:T(2,128)S(1)}, f32[2,96]{1,0:T(2,128)S(1)}, u32[]{:S(2)}, u32[]{:S(2)}) collective-permute-start(f32[2,96]{1,0:T(2,128)S(1)} %add.174), channel_id=1, source_target_pairs={{0,8},{1,9},{2,10},{3,11},{4,12},{5,13},{6,14},{7,15},{8,0},{9,1},... | collective-permute-start | bytes 2312 | tf_op jit(solution)/shard_map/ppermute | solution.py:219
  19.0 1.2 fusion.2
  20.2 9.4 %project.5 = (f32[8,192,256]{2,1,0:T(8,128)S(1)}, s16[1936,256]{1,0:T(8,128)(2,1)S(1)}) custom-call(s32[1]{0:T(128)} %bitcast.2.core, bf16[192,1024]{1,0:T(8,128)(2,1)S(1)} %bitcast.93, bf16[1024,18432]{1,0:T(8,128)(2,1)} %refs_7_.7, bf16[1024,18432]{1,0:T(8,128)(2,1)} %refs_7_.7, bf16[1024,18432]{1,0:T(8,128)(2,1)} %refs_7_.7, bf16[1024,18432]{1,0:T(8,128)(2,1)} %refs_7_.7, ...), custom_call_target="tpu_custom_call" | custom-call | flops 1610612736 | bytes 10747904 | tf_op jit(solution)/shard_map/project/pallas_call | solution.py:325
  29.5 10.9 %project.4 = (f32[8,192,384]{2,1,0:T(8,128)S(1)}, s16[1936,384]{1,0:T(8,128)(2,1)S(1)}) custom-call(s32[1]{0:T(128)} %bitcast.2.core, bf16[192,1024]{1,0:T(8,128)(2,1)S(1)} %bitcast.95, bf16[1024,18432]{1,0:T(8,128)(2,1)} %refs_7_.7, bf16[1024,18432]{1,0:T(8,128)(2,1)} %refs_7_.7, bf16[1024,18432]{1,0:T(8,128)(2,1)} %refs_7_.7, bf16[1024,18432]{1,0:T(8,128)(2,1)} %refs_7_.7, ...), custom_call_target="tpu_custom_call" | custom-call | flops 2415919104 | bytes 16121856 | tf_op jit(solution)/shard_map/project/pallas_call | solution.py:325
  41.3 1.9 collective-permute-start.21
  43.2 1.6 collective-permute-start.22
  45.8 2.7 collective-permute-done.21
  48.5 2.8 %collective-permute-start.24 = (bf16[400,256]{1,0:T(8,128)(2,1)S(1)}, bf16[400,256]{1,0:T(8,128)(2,1)S(1)}, u32[]{:S(2)}, u32[]{:S(2)}) collective-permute-start(bf16[400,256]{1,0:T(8,128)(2,1)S(1)} %pad_maximum_fusion.3), channel_id=1, source_target_pairs={{0,8},{1,9},{2,10},{3,11},{4,12},{5,13},{6,14},{7,15},{8,0},{9,1},... | collective-permute-start | bytes 614408 | tf_op jit(solution)/shard_map/ppermute | solution.py:219
  52.0 1.8 collective-permute-start.25
  54.5 4.0 %collective-permute-done.23 = bf16[400,256]{1,0:T(8,128)(2,1)S(1)} collective-permute-done((bf16[400,256]{1,0:T(8,128)(2,1)S(1)}, bf16[400,256]{1,0:T(8,128)(2,1)S(1)}, u32[]{:S(2)}, u32[]{:S(2)}) %collective-permute-start.23) | collective-permute-done | bytes 204832 | tf_op jit(solution)/shard_map/ppermute | solution.py:219
  58.5 1.4 collective-permute-start.26
  60.6 16.3 %collective-permute-start.27 = (bf16[400,256]{1,0:T(8,128)(2,1)S(1)}, bf16[400,256]{1,0:T(8,128)(2,1)S(1)}, u32[]{:S(2)}, u32[]{:S(2)}) collective-permute-start(bf16[400,256]{1,0:T(8,128)(2,1)S(1)} %pad_maximum_fusion.6), channel_id=1, source_target_pairs={{0,14},{1,15},{2,12},{3,13},{4,10},{5,11},{6,8},{7,9},{8,6},{9,7},... | collective-permute-start | bytes 614408 | tf_op jit(solution)/shard_map/ppermute | solution.py:219
  79.4 1.4 collective-permute-done.27
  81.5 1.6 fold.15
  83.2 10.2 %project.7 = (f32[8,192,256]{2,1,0:T(8,128)S(1)}, s16[1936,256]{1,0:T(8,128)(2,1)}) custom-call(s32[1]{0:T(128)} %bitcast.2.core, bf16[192,1024]{1,0:T(8,128)(2,1)S(1)} %bitcast.97, bf16[1024,18432]{1,0:T(8,128)(2,1)} %refs_7_.7, bf16[1024,18432]{1,0:T(8,128)(2,1)} %refs_7_.7, bf16[1024,18432]{1,0:T(8,128)(2,1)} %refs_7_.7, bf16[1024,18432]{1,0:T(8,128)(2,1)} %refs_7_.7, ...), custom_call_target="tpu_custom_call" | custom-call | flops 1610612736 | bytes 10747904 | tf_op jit(solution)/shard_map/project/pallas_call | solution.py:325
  94.0 2.0 fold.12
  96.0 10.0 %project.6 = (f32[8,192,256]{2,1,0:T(8,128)S(1)}, s16[1936,256]{1,0:T(8,128)(2,1)}) custom-call(s32[1]{0:T(128)} %bitcast.2.core, bf16[192,1024]{1,0:T(8,128)(2,1)S(1)} %bitcast.98, bf16[1024,18432]{1,0:T(8,128)(2,1)} %refs_7_.7, bf16[1024,18432]{1,0:T(8,128)(2,1)} %refs_7_.7, bf16[1024,18432]{1,0:T(8,128)(2,1)} %refs_7_.7, bf16[1024,18432]{1,0:T(8,128)(2,1)} %refs_7_.7, ...), custom_call_target="tpu_custom_call" | custom-call | flops 1610612736 | bytes 10747904 | tf_op jit(solution)/shard_map/project/pallas_call | solution.py:325
  106.1 1.2 copy-done.3
  109.3 2.0 collective-permute-start.9
  111.9 1.4 convert_element_type.35
  113.3 1.3 add.200
  114.6 1.1 fusion.6
  115.7 1.4 copy-done.6
  118.1 9.7 %collective-permute-done.5.refs_2_.refs_3_ = s16[976,384]{1,0:T(8,128)(2,1)} collective-permute-done((s16[976,384]{1,0:T(8,128)(2,1)}, s16[976,384]{1,0:T(8,128)(2,1)}, u32[]{:S(2)}, u32[]{:S(2)}) %collective-permute-start.5) | collective-permute-done | bytes 749600 | tf_op jit(solution)/shard_map/ppermute | solution.py:219
  127.8 1.6 fold.13
  129.5 7.3 %collective-permute-start.6 = (s16[496,384]{1,0:T(8,128)(2,1)S(1)}, s16[496,384]{1,0:T(8,128)(2,1)S(1)}, u32[]{:S(2)}, u32[]{:S(2)}) collective-permute-start(s16[496,384]{1,0:T(8,128)(2,1)S(1)} %get-tuple-element.45), channel_id=1, source_target_pairs={{0,4},{1,5},{2,6},{3,7},{4,0},{5,1},{6,2},{7,3},{8,12},{9,13},{10,... | collective-permute-start | bytes 1142792 | tf_op jit(solution)/shard_map/ppermute | solution.py:219
  138.6 1.4 fold.16
  140.0 7.3 %collective-permute-start.10 = (s16[496,256]{1,0:T(8,128)(2,1)S(1)}, s16[496,256]{1,0:T(8,128)(2,1)S(1)}, u32[]{:S(2)}, u32[]{:S(2)}) collective-permute-start(s16[496,256]{1,0:T(8,128)(2,1)S(1)} %get-tuple-element.54), channel_id=1, source_target_pairs={{0,4},{1,5},{2,6},{3,7},{4,0},{5,1},{6,2},{7,3},{8,12},{9,13},{10,... | collective-permute-start | bytes 761864 | tf_op jit(solution)/shard_map/ppermute | solution.py:219
  147.4 1.0 fold.14
  148.3 2.1 collective-permute-start.7
  151.3 5.7 %collective-permute-done.10.refs_2_.refs_3_ = s16[496,256]{1,0:T(8,128)(2,1)S(1)} collective-permute-done((s16[496,256]{1,0:T(8,128)(2,1)S(1)}, s16[496,256]{1,0:T(8,128)(2,1)S(1)}, u32[]{:S(2)}, u32[]{:S(2)}) %collective-permute-start.10) | collective-permute-done | bytes 253984 | tf_op jit(solution)/shard_map/ppermute | solution.py:219
  157.3 1.4 collective-permute-start.11
  161.1 6.3 %collective-permute-start.15 = (s16[496,256]{1,0:T(8,128)(2,1)S(1)}, s16[496,256]{1,0:T(8,128)(2,1)S(1)}, u32[]{:S(2)}, u32[]{:S(2)}) collective-permute-start(s16[496,256]{1,0:T(8,128)(2,1)S(1)} %get-tuple-element.63), channel_id=1, source_target_pairs={{0,4},{1,5},{2,6},{3,7},{4,0},{5,1},{6,2},{7,3},{8,12},{9,13},{10,... | collective-permute-start | bytes 761864 | tf_op jit(solution)/shard_map/ppermute | solution.py:219
  168.6 2.4 collective-permute-start.20
  171.1 5.2 %collective-permute-done.15.refs_2_.refs_3_ = s16[496,256]{1,0:T(8,128)(2,1)S(1)} collective-permute-done((s16[496,256]{1,0:T(8,128)(2,1)S(1)}, s16[496,256]{1,0:T(8,128)(2,1)S(1)}, u32[]{:S(2)}, u32[]{:S(2)}) %collective-permute-start.15) | collective-permute-done | bytes 253984 | tf_op jit(solution)/shard_map/ppermute | solution.py:219
  176.4 2.4 collective-permute-start.16
  179.3 5.3 %collective-permute-done.16.landed = s16[256,256]{1,0:T(8,128)(2,1)S(1)} collective-permute-done((s16[256,256]{1,0:T(8,128)(2,1)S(1)}, s16[256,256]{1,0:T(8,128)(2,1)S(1)}, u32[]{:S(2)}, u32[]{:S(2)}) %collective-permute-start.16) | collective-permute-done | bytes 131104 | tf_op jit(solution)/shard_map/ppermute | solution.py:219
  185.0 8.9 %attend.1 = bf16[16,96,128]{2,1,0:T(8,128)(2,1)S(1)} custom-call(s32[24]{0:T(128)S(1)} %copy-done.10, bf16[16,96,128]{2,1,0:T(8,128)(2,1)S(1)} %bitcast.106, bf16[16,16,128]{2,1,0:T(8,128)(2,1)S(1)} %pad.11.new_keys, bf16[16,16,128]{2,1,0:T(8,128)(2,1)S(1)} %pad.12.new_values, bf16[8,400,256]{2,1,0:T(8,128)(2,1)} %bitcast_dynamic-update-slice_fusion.own, ...), custom_call_target="tpu_custom_call" | custom-call | flops 301989888 | bytes 3145728 | tf_op jit(solution)/shard_map/attend/pallas_call | solution.py:615
  194.7 9.8 %collective-permute-done.30.refs_0_ = bf16[192,1024]{1,0:T(8,128)(2,1)S(1)} collective-permute-done((bf16[192,1024]{1,0:T(8,128)(2,1)S(1)}, bf16[192,1024]{1,0:T(8,128)(2,1)S(1)}, u32[]{:S(2)}, u32[]{:S(2)}) %collective-permute-start.30) | collective-permute-done | bytes 393248 | tf_op jit(solution)/shard_map/ppermute | solution.py:219
  205.9 1.3 collective-permute-start.36
  207.3 1.3 collective-permute-start.32
  209.3 1.5 collective-permute-start.40
  210.8 6.6 %collective-permute-done.42.refs_0_ = bf16[192,1024]{1,0:T(8,128)(2,1)S(1)} collective-permute-done((bf16[192,1024]{1,0:T(8,128)(2,1)S(1)}, bf16[192,1024]{1,0:T(8,128)(2,1)S(1)}, u32[]{:S(2)}, u32[]{:S(2)}) %collective-permute-start.42) | collective-permute-done | bytes 393248 | tf_op jit(solution)/shard_map/ppermute | solution.py:219
  217.4 2.6 collective-permute-done.36
  220.0 6.9 %collective-permute-done.32 = bf16[192,1024]{1,0:T(8,128)(2,1)} collective-permute-done((bf16[192,1024]{1,0:T(8,128)(2,1)S(1)}, bf16[192,1024]{1,0:T(8,128)(2,1)}, u32[]{:S(2)}, u32[]{:S(2)}) %collective-permute-start.32) | collective-permute-done | bytes 393248 | tf_op jit(solution)/shard_map/ppermute | solution.py:503
  227.9 1.0 broadcast_select_fusion.1.refs_0_
  229.7 1.1 collective-permute-start.33
  232.6 6.4 %collective-permute-done.37.refs_0_ = bf16[192,1024]{1,0:T(8,128)(2,1)S(1)} collective-permute-done((bf16[192,1024]{1,0:T(8,128)(2,1)S(1)}, bf16[192,1024]{1,0:T(8,128)(2,1)S(1)}, u32[]{:S(2)}, u32[]{:S(2)}) %collective-permute-start.37) | collective-permute-done | bytes 393248 | tf_op jit(solution)/shard_map/ppermute | solution.py:219
  239.6 1.0 copy-done.8
  240.6 4.6 %mix.8.refs_3_ = f32[192,1024]{1,0:T(8,128)S(1)} custom-call(s32[2]{0:T(128)S(1)} %pad_add_fusion.7.places, bf16[192,1024]{1,0:T(8,128)(2,1)S(1)} %bitcast.105, bf16[192,1024]{1,0:T(8,128)(2,1)S(1)} %copy-done.8, bf16[16384,1024]{1,0:T(8,128)(2,1)} %refs_2_.23, bf16[192,1024]{1,0:T(8,128)(2,1)S(1)} %bitcast.100), custom_call_target="tpu_custom_call" | custom-call | flops 805306368 | bytes 6553600 | tf_op jit(solution)/shard_map/mix/pallas_call | solution.py:472
  245.3 4.5 %mix.9.refs_3_ = f32[192,1024]{1,0:T(8,128)S(1)} custom-call(s32[2]{0:T(128)S(1)} %copy-done.13, bf16[192,1024]{1,0:T(8,128)(2,1)S(1)} %collective-permute-done.30.refs_0_, bf16[192,1024]{1,0:T(8,128)(2,1)} %collective-permute-done.44.refs_1_, bf16[16384,1024]{1,0:T(8,128)(2,1)} %refs_2_.23, f32[192,1024]{1,0:T(8,128)S(1)} %mix.8.refs_3_), custom_call_target="tpu_custom_call" | custom-call | flops 805306368 | bytes 6553600 | tf_op jit(solution)/shard_map/mix/pallas_call | solution.py:472
  249.8 4.4 %mix.10.refs_3_ = f32[192,1024]{1,0:T(8,128)S(1)} custom-call(s32[2]{0:T(128)S(1)} %copy-done.12, bf16[192,1024]{1,0:T(8,128)(2,1)S(1)} %collective-permute-done.42.refs_0_, bf16[192,1024]{1,0:T(8,128)(2,1)} %collective-permute-done.43.refs_1_, bf16[16384,1024]{1,0:T(8,128)(2,1)} %refs_2_.23, f32[192,1024]{1,0:T(8,128)S(1)} %mix.9.refs_3_), custom_call_target="tpu_custom_call" | custom-call | flops 805306368 | bytes 6553600 | tf_op jit(solution)/shard_map/mix/pallas_call | solution.py:472
  254.3 4.5 %mix.11.refs_3_ = f32[192,1024]{1,0:T(8,128)S(1)} custom-call(s32[2]{0:T(128)S(1)} %copy-done.11, bf16[192,1024]{1,0:T(8,128)(2,1)S(1)} %collective-permute-done.40.refs_0_, bf16[192,1024]{1,0:T(8,128)(2,1)} %collective-permute-done.41.refs_1_, bf16[16384,1024]{1,0:T(8,128)(2,1)} %refs_2_.23, f32[192,1024]{1,0:T(8,128)S(1)} %mix.10.refs_3_), custom_call_target="tpu_custom_call" | custom-call | flops 805306368 | bytes 6553600 | tf_op jit(solution)/shard_map/mix/pallas_call | solution.py:472
  258.8 4.4 %mix.12.refs_3_ = f32[192,1024]{1,0:T(8,128)S(1)} custom-call(s32[2]{0:T(128)S(1)} %pad_add_fusion.3.places, bf16[192,1024]{1,0:T(8,128)(2,1)S(1)} %broadcast_select_fusion.refs_0_, bf16[192,1024]{1,0:T(8,128)(2,1)S(1)} %collective-permute-done.39.refs_1_, bf16[16384,1024]{1,0:T(8,128)(2,1)} %refs_2_.23, f32[192,1024]{1,0:T(8,128)S(1)} %mix.11.refs_3_), custom_call_target="tpu_custom_call" | custom-call | flops 805306368 | bytes 6553600 | tf_op jit(solution)/shard_map/mix/pallas_call | solution.py:472
  263.1 4.4 %mix.13.refs_3_ = f32[192,1024]{1,0:T(8,128)S(1)} custom-call(s32[2]{0:T(128)S(1)} %pad_add_fusion.2.places, bf16[192,1024]{1,0:T(8,128)(2,1)S(1)} %collective-permute-done.37.refs_0_, bf16[192,1024]{1,0:T(8,128)(2,1)S(1)} %collective-permute-done.38.refs_1_, bf16[16384,1024]{1,0:T(8,128)(2,1)} %refs_2_.23, f32[192,1024]{1,0:T(8,128)S(1)} %mix.12.refs_3_), custom_call_target="tpu_custom_call" | custom-call | flops 805306368 | bytes 6553600 | tf_op jit(solution)/shard_map/mix/pallas_call | solution.py:472
  267.5 4.4 %mix.14.refs_3_ = f32[192,1024]{1,0:T(8,128)S(1)} custom-call(s32[2]{0:T(128)S(1)} %pad_add_fusion.1.places, bf16[192,1024]{1,0:T(8,128)(2,1)S(1)} %broadcast_select_fusion.1.refs_0_, bf16[192,1024]{1,0:T(8,128)(2,1)S(1)} %collective-permute-done.35.refs_1_, bf16[16384,1024]{1,0:T(8,128)(2,1)} %refs_2_.23, f32[192,1024]{1,0:T(8,128)S(1)} %mix.13.refs_3_), custom_call_target="tpu_custom_call" | custom-call | flops 805306368 | bytes 6553600 | tf_op jit(solution)/shard_map/mix/pallas_call | solution.py:472
  271.9 5.1 %mix.15 = bf16[192,1024]{1,0:T(8,128)(2,1)} custom-call(s32[2]{0:T(128)S(1)} %pad_add_fusion.places, bf16[192,1024]{1,0:T(8,128)(2,1)S(1)} %collective-permute-done.33.refs_0_, bf16[192,1024]{1,0:T(8,128)(2,1)S(1)} %collective-permute-done.34.refs_1_, bf16[16384,1024]{1,0:T(8,128)(2,1)} %refs_2_.23, f32[192,1024]{1,0:T(8,128)S(1)} %mix.14.refs_3_), custom_call_target="tpu_custom_call" | custom-call | flops 805306368 | bytes 6553600 | tf_op jit(solution)/shard_map/mix/pallas_call | solution.py:472
  (197 shorter events, 30.6 us)
Async XLA Ops:
  1.2 5.4 %collective-permute-start = (f32[2,96]{1,0:T(2,128)S(1)}, f32[2,96]{1,0:T(2,128)S(1)}, u32[]{:S(2)}, u32[]{:S(2)}) collective-permute-start(f32[2,96]{1,0:T(2,128)S(1)} %fusion), channel_id=1, source_target_pairs={{0,1},{1,0},{2,3},{3,2},{4,5},{5,4},{6,7},{7,6},{8,9},{9,8},{10,11... | collective-permute-start | bytes 2312 | tf_op jit(solution)/shard_map/ppermute | solution.py:219
  6.6 4.2 %collective-permute-start.1 = (f32[2,96]{1,0:T(2,128)S(1)}, f32[2,96]{1,0:T(2,128)S(1)}, u32[]{:S(2)}, u32[]{:S(2)}) collective-permute-start(f32[2,96]{1,0:T(2,128)S(1)} %add.172), channel_id=1, source_target_pairs={{0,2},{1,3},{2,0},{3,1},{4,6},{5,7},{6,4},{7,5},{8,10},{9,11},{10,... | collective-permute-start | bytes 2312 | tf_op jit(solution)/shard_map/ppermute | solution.py:219
  10.8 3.6 %collective-permute-start.2 = (f32[2,96]{1,0:T(2,128)S(1)}, f32[2,96]{1,0:T(2,128)S(1)}, u32[]{:S(2)}, u32[]{:S(2)}) collective-permute-start(f32[2,96]{1,0:T(2,128)S(1)} %add.173), channel_id=1, source_target_pairs={{0,4},{1,5},{2,6},{3,7},{4,0},{5,1},{6,2},{7,3},{8,12},{9,13},{10,... | collective-permute-start | bytes 2312 | tf_op jit(solution)/shard_map/ppermute | solution.py:219
  14.4 4.6 %collective-permute-start.3 = (f32[2,96]{1,0:T(2,128)S(1)}, f32[2,96]{1,0:T(2,128)S(1)}, u32[]{:S(2)}, u32[]{:S(2)}) collective-permute-start(f32[2,96]{1,0:T(2,128)S(1)} %add.174), channel_id=1, source_target_pairs={{0,8},{1,9},{2,10},{3,11},{4,12},{5,13},{6,14},{7,15},{8,0},{9,1},... | collective-permute-start | bytes 2312 | tf_op jit(solution)/shard_map/ppermute | solution.py:219
  29.5 11.5 %copy-start.14 = (bf16[24,8,16,256]{3,2,1,0:T(8,128)(2,1)S(1)}, bf16[24,8,16,256]{3,2,1,0:T(8,128)(2,1)}, u32[]{:S(2)}) copy-start(bf16[24,8,16,256]{3,2,1,0:T(8,128)(2,1)} %param.12) | copy-start | bytes 4718596
  40.4 41.1 %collective-permute-start.8 = (s16[1936,256]{1,0:T(8,128)(2,1)S(1)}, s16[1936,256]{1,0:T(8,128)(2,1)S(1)}, u32[]{:S(2)}, u32[]{:S(2)}) collective-permute-start(s16[1936,256]{1,0:T(8,128)(2,1)S(1)} %get-tuple-element.50), channel_id=1, source_target_pairs={{0,1},{1,0},{2,3},{3,2},{4,5},{5,4},{6,7},{7,6},{8,9},{9,8},{10,11... | collective-permute-start | bytes 2973704 | tf_op jit(solution)/shard_map/ppermute | solution.py:219
  40.5 4.5 %copy-start.20 = (bf16[16,256]{1,0:T(8,128)(2,1)S(1)}, bf16[16,256]{1,0:T(8,128)(2,1)}, u32[]{:S(2)}) copy-start(bf16[16,256]{1,0:T(8,128)(2,1)} %get-tuple-element.99) | copy-start | bytes 24580
  40.5 5.2 %copy-start.19 = (bf16[16,256]{1,0:T(8,128)(2,1)S(1)}, bf16[16,256]{1,0:T(8,128)(2,1)}, u32[]{:S(2)}) copy-start(bf16[16,256]{1,0:T(8,128)(2,1)} %get-tuple-element.96) | copy-start | bytes 24580
  40.5 53.5 %collective-permute-start.4 = (s16[1936,384]{1,0:T(8,128)(2,1)S(1)}, s16[1936,384]{1,0:T(8,128)(2,1)S(1)}, u32[]{:S(2)}, u32[]{:S(2)}) collective-permute-start(s16[1936,384]{1,0:T(8,128)(2,1)S(1)} %get-tuple-element.41), channel_id=1, source_target_pairs={{0,1},{1,0},{2,3},{3,2},{4,5},{5,4},{6,7},{7,6},{8,9},{9,8},{10,11... | collective-permute-start | bytes 4460552 | tf_op jit(solution)/shard_map/ppermute | solution.py:219
  41.2 4.5 %copy-start.17 = (bf16[16,256]{1,0:T(8,128)(2,1)S(1)}, bf16[16,256]{1,0:T(8,128)(2,1)}, u32[]{:S(2)}) copy-start(bf16[16,256]{1,0:T(8,128)(2,1)} %get-tuple-element.98) | copy-start | bytes 24580
  41.2 4.6 %copy-start.16 = (bf16[16,256]{1,0:T(8,128)(2,1)S(1)}, bf16[16,256]{1,0:T(8,128)(2,1)}, u32[]{:S(2)}) copy-start(bf16[16,256]{1,0:T(8,128)(2,1)} %get-tuple-element.92) | copy-start | bytes 24580
  41.3 7.2 %collective-permute-start.21 = (bf16[400,256]{1,0:T(8,128)(2,1)S(1)}, bf16[400,256]{1,0:T(8,128)(2,1)S(1)}, u32[]{:S(2)}, u32[]{:S(2)}) collective-permute-start(bf16[400,256]{1,0:T(8,128)(2,1)S(1)} %pad_maximum_fusion), channel_id=1, source_target_pairs={{0,2},{1,3},{2,0},{3,1},{4,6},{5,7},{6,4},{7,5},{8,10},{9,11},{10,... | collective-permute-start | bytes 614408 | tf_op jit(solution)/shard_map/ppermute | solution.py:219
  43.2 8.8 %collective-permute-start.22 = (bf16[400,256]{1,0:T(8,128)(2,1)S(1)}, bf16[400,256]{1,0:T(8,128)(2,1)S(1)}, u32[]{:S(2)}, u32[]{:S(2)}) collective-permute-start(bf16[400,256]{1,0:T(8,128)(2,1)S(1)} %pad_maximum_fusion.1), channel_id=1, source_target_pairs={{0,4},{1,5},{2,6},{3,7},{4,0},{5,1},{6,2},{7,3},{8,12},{9,13},{10,... | collective-permute-start | bytes 614408 | tf_op jit(solution)/shard_map/ppermute | solution.py:219
  44.9 13.6 %collective-permute-start.23 = (bf16[400,256]{1,0:T(8,128)(2,1)S(1)}, bf16[400,256]{1,0:T(8,128)(2,1)S(1)}, u32[]{:S(2)}, u32[]{:S(2)}) collective-permute-start(bf16[400,256]{1,0:T(8,128)(2,1)S(1)} %pad_maximum_fusion.2), channel_id=1, source_target_pairs={{0,6},{1,7},{2,4},{3,5},{4,2},{5,3},{6,0},{7,1},{8,14},{9,15},{10,... | collective-permute-start | bytes 614408 | tf_op jit(solution)/shard_map/ppermute | solution.py:219
  48.5 12.1 %collective-permute-start.24 = (bf16[400,256]{1,0:T(8,128)(2,1)S(1)}, bf16[400,256]{1,0:T(8,128)(2,1)S(1)}, u32[]{:S(2)}, u32[]{:S(2)}) collective-permute-start(bf16[400,256]{1,0:T(8,128)(2,1)S(1)} %pad_maximum_fusion.3), channel_id=1, source_target_pairs={{0,8},{1,9},{2,10},{3,11},{4,12},{5,13},{6,14},{7,15},{8,0},{9,1},... | collective-permute-start | bytes 614408 | tf_op jit(solution)/shard_map/ppermute | solution.py:219
  52.0 26.0 %collective-permute-start.25 = (bf16[400,256]{1,0:T(8,128)(2,1)S(1)}, bf16[400,256]{1,0:T(8,128)(2,1)S(1)}, u32[]{:S(2)}, u32[]{:S(2)}) collective-permute-start(bf16[400,256]{1,0:T(8,128)(2,1)S(1)} %pad_maximum_fusion.4), channel_id=1, source_target_pairs={{0,10},{1,11},{2,8},{3,9},{4,14},{5,15},{6,12},{7,13},{8,2},{9,3},... | collective-permute-start | bytes 614408 | tf_op jit(solution)/shard_map/ppermute | solution.py:219
  58.5 20.2 %collective-permute-start.26 = (bf16[400,256]{1,0:T(8,128)(2,1)S(1)}, bf16[400,256]{1,0:T(8,128)(2,1)S(1)}, u32[]{:S(2)}, u32[]{:S(2)}) collective-permute-start(bf16[400,256]{1,0:T(8,128)(2,1)S(1)} %pad_maximum_fusion.5), channel_id=1, source_target_pairs={{0,12},{1,13},{2,14},{3,15},{4,8},{5,9},{6,10},{7,11},{8,4},{9,5},... | collective-permute-start | bytes 614408 | tf_op jit(solution)/shard_map/ppermute | solution.py:219
  60.6 20.2 %collective-permute-start.27 = (bf16[400,256]{1,0:T(8,128)(2,1)S(1)}, bf16[400,256]{1,0:T(8,128)(2,1)S(1)}, u32[]{:S(2)}, u32[]{:S(2)}) collective-permute-start(bf16[400,256]{1,0:T(8,128)(2,1)S(1)} %pad_maximum_fusion.6), channel_id=1, source_target_pairs={{0,14},{1,15},{2,12},{3,13},{4,10},{5,11},{6,8},{7,9},{8,6},{9,7},... | collective-permute-start | bytes 614408 | tf_op jit(solution)/shard_map/ppermute | solution.py:219
  81.5 77.2 %collective-permute-start.28 = (bf16[8,400,256]{2,1,0:T(8,128)(2,1)}, bf16[8,400,256]{2,1,0:T(8,128)(2,1)}, u32[]{:S(2)}, u32[]{:S(2)}) collective-permute-start(bf16[8,400,256]{2,1,0:T(8,128)(2,1)} %bitcast_dynamic-update-slice_fusion.own), channel_id=1, source_target_pairs={{0,1},{1,0},{2,3},{3,2},{4,5},{5,4},{6,7},{7,6},{8,9},{9,8},{10,11... | collective-permute-start | bytes 4915208 | tf_op jit(solution)/shard_map/ppermute | solution.py:219
  83.2 10.2 %copy-start.1 = (f32[4,192,256]{2,1,0:T(8,128)}, f32[4,192,256]{2,1,0:T(8,128)S(1)}, u32[]{:S(2)}) copy-start(f32[4,192,256]{2,1,0:T(8,128)S(1)} %get-tuple-element.51.refs_1_.refs_8_) | copy-start | bytes 2359300
  93.4 22.3 %collective-permute-start.17 = (s16[1936,256]{1,0:T(8,128)(2,1)}, s16[1936,256]{1,0:T(8,128)(2,1)S(1)}, u32[]{:S(2)}, u32[]{:S(2)}) collective-permute-start(s16[1936,256]{1,0:T(8,128)(2,1)} %get-tuple-element.67), channel_id=1, source_target_pairs={{0,1},{1,0},{2,3},{3,2},{4,5},{5,4},{6,7},{7,6},{8,9},{9,8},{10,11... | collective-permute-start | bytes 2973704 | tf_op jit(solution)/shard_map/ppermute | solution.py:219
  96.0 11.2 %copy-start.24 = (s32[2,16]{1,0:T(2,128)S(1)}, s32[2,16]{1,0:T(2,128)}, u32[]{:S(2)}) copy-start(s32[2,16]{1,0:T(2,128)} %broadcast_add_fusion) | copy-start | bytes 388
  96.0 11.9 %copy-start.25 = (s32[2,8]{1,0:T(2,128)S(1)}, s32[2,8]{1,0:T(2,128)}, u32[]{:S(2)}) copy-start(s32[2,8]{1,0:T(2,128)} %add_multiply_fusion) | copy-start | bytes 196
  96.0 12.6 %copy-start.28 = (s32[96]{0:T(128)S(1)}, s32[96]{0:T(128)}, u32[]{:S(2)}) copy-start(s32[96]{0:T(128)} %and_select_fusion) | copy-start | bytes 1156
  107.2 29.6 %collective-permute-start.13 = (s16[1936,256]{1,0:T(8,128)(2,1)}, s16[1936,256]{1,0:T(8,128)(2,1)S(1)}, u32[]{:S(2)}, u32[]{:S(2)}) collective-permute-start(s16[1936,256]{1,0:T(8,128)(2,1)} %get-tuple-element.59), channel_id=1, source_target_pairs={{0,1},{1,0},{2,3},{3,2},{4,5},{5,4},{6,7},{7,6},{8,9},{9,8},{10,11... | collective-permute-start | bytes 2973704 | tf_op jit(solution)/shard_map/ppermute | solution.py:219
  107.9 19.9 %collective-permute-start.5 = (s16[976,384]{1,0:T(8,128)(2,1)}, s16[976,384]{1,0:T(8,128)(2,1)}, u32[]{:S(2)}, u32[]{:S(2)}) collective-permute-start(s16[976,384]{1,0:T(8,128)(2,1)} %get-tuple-element.43), channel_id=1, source_target_pairs={{0,2},{1,3},{2,0},{3,1},{4,6},{5,7},{6,4},{7,5},{8,10},{9,11},{10,... | collective-permute-start | bytes 2248712 | tf_op jit(solution)/shard_map/ppermute | solution.py:219
  109.3 29.2 %collective-permute-start.9 = (s16[976,256]{1,0:T(8,128)(2,1)}, s16[976,256]{1,0:T(8,128)(2,1)}, u32[]{:S(2)}, u32[]{:S(2)}) collective-permute-start(s16[976,256]{1,0:T(8,128)(2,1)} %get-tuple-element.52), channel_id=1, source_target_pairs={{0,2},{1,3},{2,0},{3,1},{4,6},{5,7},{6,4},{7,5},{8,10},{9,11},{10,... | collective-permute-start | bytes 1499144 | tf_op jit(solution)/shard_map/ppermute | solution.py:219
  118.0 18.8 %copy-start.4 = (f32[8,192,256]{2,1,0:T(8,128)S(1)}, f32[8,192,256]{2,1,0:T(8,128)}, u32[]{:S(2)}) copy-start(f32[8,192,256]{2,1,0:T(8,128)} %copy-done.3) | copy-start | bytes 4718596
  118.0 41.4 %collective-permute-start.18 = (s16[976,256]{1,0:T(8,128)(2,1)S(1)}, s16[976,256]{1,0:T(8,128)(2,1)S(1)}, u32[]{:S(2)}, u32[]{:S(2)}) collective-permute-start(s16[976,256]{1,0:T(8,128)(2,1)S(1)} %get-tuple-element.69), channel_id=1, source_target_pairs={{0,2},{1,3},{2,0},{3,1},{4,6},{5,7},{6,4},{7,5},{8,10},{9,11},{10,... | collective-permute-start | bytes 1499144 | tf_op jit(solution)/shard_map/ppermute | solution.py:219
  129.5 17.9 %collective-permute-start.6 = (s16[496,384]{1,0:T(8,128)(2,1)S(1)}, s16[496,384]{1,0:T(8,128)(2,1)S(1)}, u32[]{:S(2)}, u32[]{:S(2)}) collective-permute-start(s16[496,384]{1,0:T(8,128)(2,1)S(1)} %get-tuple-element.45), channel_id=1, source_target_pairs={{0,4},{1,5},{2,6},{3,7},{4,0},{5,1},{6,2},{7,3},{8,12},{9,13},{10,... | collective-permute-start | bytes 1142792 | tf_op jit(solution)/shard_map/ppermute | solution.py:219
  137.7 9.6 %copy-start.26 = (s32[256]{0:T(256)S(1)}, s32[256]{0:T(256)}, u32[]{:S(2)}) copy-start(s32[256]{0:T(256)} %add.200) | copy-start | bytes 3076
  137.7 9.5 %copy-start.27 = (s32[24]{0:T(128)S(1)}, s32[24]{0:T(128)}, u32[]{:S(2)}) copy-start(s32[24]{0:T(128)} %get-tuple-element.76) | copy-start | bytes 292
  137.7 22.7 %collective-permute-start.14 = (s16[976,256]{1,0:T(8,128)(2,1)S(1)}, s16[976,256]{1,0:T(8,128)(2,1)S(1)}, u32[]{:S(2)}, u32[]{:S(2)}) collective-permute-start(s16[976,256]{1,0:T(8,128)(2,1)S(1)} %get-tuple-element.61), channel_id=1, source_target_pairs={{0,2},{1,3},{2,0},{3,1},{4,6},{5,7},{6,4},{7,5},{8,10},{9,11},{10,... | collective-permute-start | bytes 1499144 | tf_op jit(solution)/shard_map/ppermute | solution.py:219
  140.0 17.0 %collective-permute-start.10 = (s16[496,256]{1,0:T(8,128)(2,1)S(1)}, s16[496,256]{1,0:T(8,128)(2,1)S(1)}, u32[]{:S(2)}, u32[]{:S(2)}) collective-permute-start(s16[496,256]{1,0:T(8,128)(2,1)S(1)} %get-tuple-element.54), channel_id=1, source_target_pairs={{0,4},{1,5},{2,6},{3,7},{4,0},{5,1},{6,2},{7,3},{8,12},{9,13},{10,... | collective-permute-start | bytes 761864 | tf_op jit(solution)/shard_map/ppermute | solution.py:219
  148.3 19.1 %collective-permute-start.7 = (s16[256,384]{1,0:T(8,128)(2,1)}, s16[256,384]{1,0:T(8,128)(2,1)S(1)}, u32[]{:S(2)}, u32[]{:S(2)}) collective-permute-start(s16[256,384]{1,0:T(8,128)(2,1)} %get-tuple-element.47), channel_id=1, source_target_pairs={{0,8},{1,9},{2,10},{3,11},{4,12},{5,13},{6,14},{7,15},{8,0},{9,1},... | collective-permute-start | bytes 589832 | tf_op jit(solution)/shard_map/ppermute | solution.py:219
  157.3 21.7 %collective-permute-start.11 = (s16[256,256]{1,0:T(8,128)(2,1)S(1)}, s16[256,256]{1,0:T(8,128)(2,1)S(1)}, u32[]{:S(2)}, u32[]{:S(2)}) collective-permute-start(s16[256,256]{1,0:T(8,128)(2,1)S(1)} %get-tuple-element.56), channel_id=1, source_target_pairs={{0,8},{1,9},{2,10},{3,11},{4,12},{5,13},{6,14},{7,15},{8,0},{9,1},... | collective-permute-start | bytes 393224 | tf_op jit(solution)/shard_map/ppermute | solution.py:219
  159.9 8.5 %collective-permute-start.19 = (s16[496,256]{1,0:T(8,128)(2,1)S(1)}, s16[496,256]{1,0:T(8,128)(2,1)S(1)}, u32[]{:S(2)}, u32[]{:S(2)}) collective-permute-start(s16[496,256]{1,0:T(8,128)(2,1)S(1)} %get-tuple-element.71), channel_id=1, source_target_pairs={{0,4},{1,5},{2,6},{3,7},{4,0},{5,1},{6,2},{7,3},{8,12},{9,13},{10,... | collective-permute-start | bytes 761864 | tf_op jit(solution)/shard_map/ppermute | solution.py:219
  161.1 15.1 %collective-permute-start.15 = (s16[496,256]{1,0:T(8,128)(2,1)S(1)}, s16[496,256]{1,0:T(8,128)(2,1)S(1)}, u32[]{:S(2)}, u32[]{:S(2)}) collective-permute-start(s16[496,256]{1,0:T(8,128)(2,1)S(1)} %get-tuple-element.63), channel_id=1, source_target_pairs={{0,4},{1,5},{2,6},{3,7},{4,0},{5,1},{6,2},{7,3},{8,12},{9,13},{10,... | collective-permute-start | bytes 761864 | tf_op jit(solution)/shard_map/ppermute | solution.py:219
  167.7 11.1 %collective-permute-start.12 = (bf16[192,128]{1,0:T(8,128)(2,1)S(1)}, bf16[192,128]{1,0:T(8,128)(2,1)S(1)}, u32[]{:S(2)}, u32[]{:S(2)}) collective-permute-start(bf16[192,128]{1,0:T(8,128)(2,1)S(1)} %get-tuple-element.57), channel_id=1, source_target_pairs={{0,1},{1,0},{2,3},{3,2},{4,5},{5,4},{6,7},{7,6},{8,9},{9,8},{10,11... | collective-permute-start | bytes 147464 | tf_op jit(solution)/shard_map/ppermute | solution.py:219
  168.6 10.5 %collective-permute-start.20 = (s16[256,256]{1,0:T(8,128)(2,1)S(1)}, s16[256,256]{1,0:T(8,128)(2,1)S(1)}, u32[]{:S(2)}, u32[]{:S(2)}) collective-permute-start(s16[256,256]{1,0:T(8,128)(2,1)S(1)} %get-tuple-element.73), channel_id=1, source_target_pairs={{0,8},{1,9},{2,10},{3,11},{4,12},{5,13},{6,14},{7,15},{8,0},{9,1},... | collective-permute-start | bytes 393224 | tf_op jit(solution)/shard_map/ppermute | solution.py:219
  176.4 8.2 %collective-permute-start.16 = (s16[256,256]{1,0:T(8,128)(2,1)S(1)}, s16[256,256]{1,0:T(8,128)(2,1)S(1)}, u32[]{:S(2)}, u32[]{:S(2)}) collective-permute-start(s16[256,256]{1,0:T(8,128)(2,1)S(1)} %get-tuple-element.65), channel_id=1, source_target_pairs={{0,8},{1,9},{2,10},{3,11},{4,12},{5,13},{6,14},{7,15},{8,0},{9,1},... | collective-permute-start | bytes 393224 | tf_op jit(solution)/shard_map/ppermute | solution.py:219
  179.3 5.6 %copy-start.9 = (f32[96,16]{1,0:T(8,128)S(1)}, f32[96,16]{1,0:T(8,128)}, u32[]{:S(2)}) copy-start(f32[96,16]{1,0:T(8,128)} %fusion.5.new_bias) | copy-start | bytes 18436
  179.3 5.6 %copy-start.10 = (s32[24]{0:T(128)S(1)}, s32[24]{0:T(128)}, u32[]{:S(2)}) copy-start(s32[24]{0:T(128)} %get-tuple-element.77.slot_request) | copy-start | bytes 292
  193.9 45.7 %copy-start = (bf16[2,96,1024]{2,1,0:T(8,128)(2,1)S(1)}, bf16[2,96,1024]{2,1,0:T(8,128)(2,1)}, u32[]{:S(2)}) copy-start(bf16[2,96,1024]{2,1,0:T(8,128)(2,1)} %param.8) | copy-start | bytes 1179652
  193.9 10.6 %collective-permute-start.30 = (bf16[192,1024]{1,0:T(8,128)(2,1)S(1)}, bf16[192,1024]{1,0:T(8,128)(2,1)S(1)}, u32[]{:S(2)}, u32[]{:S(2)}) collective-permute-start(bf16[192,1024]{1,0:T(8,128)(2,1)S(1)} %bitcast.101), channel_id=1, source_target_pairs={{0,4},{1,5},{2,6},{3,7},{4,0},{5,1},{6,2},{7,3},{8,12},{9,13},{10,... | collective-permute-start | bytes 1179656 | tf_op jit(solution)/shard_map/ppermute | solution.py:219
  194.0 11.9 %collective-permute-start.29 = (bf16[192,1024]{1,0:T(8,128)(2,1)S(1)}, bf16[192,1024]{1,0:T(8,128)(2,1)S(1)}, u32[]{:S(2)}, u32[]{:S(2)}) collective-permute-start(bf16[192,1024]{1,0:T(8,128)(2,1)S(1)} %bitcast.102), channel_id=1, source_target_pairs={{4,8},{5,9},{6,10},{7,11},{8,4},{9,5},{10,6},{11,7},{20,24},{21,25... | collective-permute-start | bytes 1179656 | tf_op jit(solution)/shard_map/ppermute | solution.py:503
  204.6 2.8 %collective-permute-start.31 = (bf16[192,1024]{1,0:T(8,128)(2,1)S(1)}, bf16[192,1024]{1,0:T(8,128)(2,1)S(1)}, u32[]{:S(2)}, u32[]{:S(2)}) collective-permute-start(bf16[192,1024]{1,0:T(8,128)(2,1)S(1)} %collective-permute-done.30.refs_0_), channel_id=1, source_target_pairs={{4,8},{5,9},{6,10},{7,11},{8,4},{9,5},{10,6},{11,7},{20,24},{21,25... | collective-permute-start | bytes 1179656 | tf_op jit(solution)/shard_map/ppermute | solution.py:503
  205.3 12.1 %collective-permute-start.42 = (bf16[192,1024]{1,0:T(8,128)(2,1)S(1)}, bf16[192,1024]{1,0:T(8,128)(2,1)S(1)}, u32[]{:S(2)}, u32[]{:S(2)}) collective-permute-start(bf16[192,1024]{1,0:T(8,128)(2,1)S(1)} %bitcast.103), channel_id=1, source_target_pairs={{0,2},{1,3},{2,0},{3,1},{4,6},{5,7},{6,4},{7,5},{8,10},{9,11},{10,... | collective-permute-start | bytes 1179656 | tf_op jit(solution)/shard_map/ppermute | solution.py:219
  205.9 21.1 %copy-start.15 = (bf16[192,1024]{1,0:T(8,128)(2,1)}, bf16[192,1024]{1,0:T(8,128)(2,1)S(1)}, u32[]{:S(2)}) copy-start(bf16[192,1024]{1,0:T(8,128)(2,1)S(1)} %collective-permute-done.29) | copy-start | bytes 1179652
  205.9 14.1 %collective-permute-start.36 = (bf16[192,1024]{1,0:T(8,128)(2,1)S(1)}, bf16[192,1024]{1,0:T(8,128)(2,1)S(1)}, u32[]{:S(2)}, u32[]{:S(2)}) collective-permute-start(bf16[192,1024]{1,0:T(8,128)(2,1)S(1)} %collective-permute-done.29), channel_id=1, source_target_pairs={{4,0},{5,1},{6,2},{7,3},{8,12},{9,13},{10,14},{11,15},{20,16},{21,... | collective-permute-start | bytes 1179656 | tf_op jit(solution)/shard_map/ppermute | solution.py:503
  207.3 19.6 %collective-permute-start.32 = (bf16[192,1024]{1,0:T(8,128)(2,1)S(1)}, bf16[192,1024]{1,0:T(8,128)(2,1)}, u32[]{:S(2)}, u32[]{:S(2)}) collective-permute-start(bf16[192,1024]{1,0:T(8,128)(2,1)S(1)} %collective-permute-done.31), channel_id=1, source_target_pairs={{4,0},{5,1},{6,2},{7,3},{8,12},{9,13},{10,14},{11,15},{20,16},{21,... | collective-permute-start | bytes 1179656 | tf_op jit(solution)/shard_map/ppermute | solution.py:503
  209.3 19.7 %collective-permute-start.45 = (bf16[192,1024]{1,0:T(8,128)(2,1)S(1)}, bf16[192,1024]{1,0:T(8,128)(2,1)S(1)}, u32[]{:S(2)}, u32[]{:S(2)}) collective-permute-start(bf16[192,1024]{1,0:T(8,128)(2,1)S(1)} %bitcast.104), channel_id=1, source_target_pairs={{0,1},{1,0},{2,3},{3,2},{4,5},{5,4},{6,7},{7,6},{8,9},{9,8},{10,11... | collective-permute-start | bytes 1179656 | tf_op jit(solution)/shard_map/ppermute | solution.py:219
  209.3 22.2 %collective-permute-start.40 = (bf16[192,1024]{1,0:T(8,128)(2,1)S(1)}, bf16[192,1024]{1,0:T(8,128)(2,1)S(1)}, u32[]{:S(2)}, u32[]{:S(2)}) collective-permute-start(bf16[192,1024]{1,0:T(8,128)(2,1)S(1)} %collective-permute-done.30.refs_0_), channel_id=1, source_target_pairs={{0,2},{1,3},{2,0},{3,1},{4,6},{5,7},{6,4},{7,5},{8,10},{9,11},{10,... | collective-permute-start | bytes 1179656 | tf_op jit(solution)/shard_map/ppermute | solution.py:219
  217.4 21.7 %collective-permute-start.44 = (bf16[192,1024]{1,0:T(8,128)(2,1)S(1)}, bf16[192,1024]{1,0:T(8,128)(2,1)}, u32[]{:S(2)}, u32[]{:S(2)}) collective-permute-start(bf16[192,1024]{1,0:T(8,128)(2,1)S(1)} %collective-permute-done.30.refs_0_), channel_id=1, source_target_pairs={{0,1},{1,0},{2,3},{3,2},{4,5},{5,4},{6,7},{7,6},{8,9},{9,8},{10,11... | collective-permute-start | bytes 1179656 | tf_op jit(solution)/shard_map/ppermute | solution.py:219
  220.0 12.2 %collective-permute-start.43 = (bf16[192,1024]{1,0:T(8,128)(2,1)S(1)}, bf16[192,1024]{1,0:T(8,128)(2,1)}, u32[]{:S(2)}, u32[]{:S(2)}) collective-permute-start(bf16[192,1024]{1,0:T(8,128)(2,1)S(1)} %collective-permute-done.42.refs_0_), channel_id=1, source_target_pairs={{0,1},{1,0},{2,3},{3,2},{4,5},{5,4},{6,7},{7,6},{8,9},{9,8},{10,11... | collective-permute-start | bytes 1179656 | tf_op jit(solution)/shard_map/ppermute | solution.py:219
  227.0 12.1 %collective-permute-start.37 = (bf16[192,1024]{1,0:T(8,128)(2,1)S(1)}, bf16[192,1024]{1,0:T(8,128)(2,1)S(1)}, u32[]{:S(2)}, u32[]{:S(2)}) collective-permute-start(bf16[192,1024]{1,0:T(8,128)(2,1)S(1)} %broadcast_select_fusion.refs_0_), channel_id=1, source_target_pairs={{0,2},{1,3},{2,0},{3,1},{4,6},{5,7},{6,4},{7,5},{8,10},{9,11},{10,... | collective-permute-start | bytes 1179656 | tf_op jit(solution)/shard_map/ppermute | solution.py:219
  229.7 15.5 %collective-permute-start.33 = (bf16[192,1024]{1,0:T(8,128)(2,1)S(1)}, bf16[192,1024]{1,0:T(8,128)(2,1)S(1)}, u32[]{:S(2)}, u32[]{:S(2)}) collective-permute-start(bf16[192,1024]{1,0:T(8,128)(2,1)S(1)} %broadcast_select_fusion.1.refs_0_), channel_id=1, source_target_pairs={{0,2},{1,3},{2,0},{3,1},{4,6},{5,7},{6,4},{7,5},{8,10},{9,11},{10,... | collective-permute-start | bytes 1179656 | tf_op jit(solution)/shard_map/ppermute | solution.py:219
  231.4 22.8 %collective-permute-start.41 = (bf16[192,1024]{1,0:T(8,128)(2,1)S(1)}, bf16[192,1024]{1,0:T(8,128)(2,1)}, u32[]{:S(2)}, u32[]{:S(2)}) collective-permute-start(bf16[192,1024]{1,0:T(8,128)(2,1)S(1)} %collective-permute-done.40.refs_0_), channel_id=1, source_target_pairs={{0,1},{1,0},{2,3},{3,2},{4,5},{5,4},{6,7},{7,6},{8,9},{9,8},{10,11... | collective-permute-start | bytes 1179656 | tf_op jit(solution)/shard_map/ppermute | solution.py:219
  232.1 26.6 %collective-permute-start.39 = (bf16[192,1024]{1,0:T(8,128)(2,1)S(1)}, bf16[192,1024]{1,0:T(8,128)(2,1)S(1)}, u32[]{:S(2)}, u32[]{:S(2)}) collective-permute-start(bf16[192,1024]{1,0:T(8,128)(2,1)S(1)} %broadcast_select_fusion.refs_0_), channel_id=1, source_target_pairs={{0,1},{1,0},{2,3},{3,2},{4,5},{5,4},{6,7},{7,6},{8,9},{9,8},{10,11... | collective-permute-start | bytes 1179656 | tf_op jit(solution)/shard_map/ppermute | solution.py:219
  239.0 24.1 %collective-permute-start.38 = (bf16[192,1024]{1,0:T(8,128)(2,1)S(1)}, bf16[192,1024]{1,0:T(8,128)(2,1)S(1)}, u32[]{:S(2)}, u32[]{:S(2)}) collective-permute-start(bf16[192,1024]{1,0:T(8,128)(2,1)S(1)} %collective-permute-done.37.refs_0_), channel_id=1, source_target_pairs={{0,1},{1,0},{2,3},{3,2},{4,5},{5,4},{6,7},{7,6},{8,9},{9,8},{10,11... | collective-permute-start | bytes 1179656 | tf_op jit(solution)/shard_map/ppermute | solution.py:219
  239.1 28.4 %collective-permute-start.35 = (bf16[192,1024]{1,0:T(8,128)(2,1)S(1)}, bf16[192,1024]{1,0:T(8,128)(2,1)S(1)}, u32[]{:S(2)}, u32[]{:S(2)}) collective-permute-start(bf16[192,1024]{1,0:T(8,128)(2,1)S(1)} %broadcast_select_fusion.1.refs_0_), channel_id=1, source_target_pairs={{0,1},{1,0},{2,3},{3,2},{4,5},{5,4},{6,7},{7,6},{8,9},{9,8},{10,11... | collective-permute-start | bytes 1179656 | tf_op jit(solution)/shard_map/ppermute | solution.py:219
  240.6 4.7 %copy-start.13 = (s32[2]{0:T(128)S(1)}, s32[2]{0:T(128)}, u32[]{:S(2)}) copy-start(s32[2]{0:T(128)} %pad_add_fusion.6.places) | copy-start | bytes 28
  245.2 4.6 %copy-start.12 = (s32[2]{0:T(128)S(1)}, s32[2]{0:T(128)}, u32[]{:S(2)}) copy-start(s32[2]{0:T(128)} %pad_add_fusion.5.places) | copy-start | bytes 28
  245.2 26.7 %collective-permute-start.34 = (bf16[192,1024]{1,0:T(8,128)(2,1)S(1)}, bf16[192,1024]{1,0:T(8,128)(2,1)S(1)}, u32[]{:S(2)}, u32[]{:S(2)}) collective-permute-start(bf16[192,1024]{1,0:T(8,128)(2,1)S(1)} %collective-permute-done.33.refs_0_), channel_id=1, source_target_pairs={{0,1},{1,0},{2,3},{3,2},{4,5},{5,4},{6,7},{7,6},{8,9},{9,8},{10,11... | collective-permute-start | bytes 1179656 | tf_op jit(solution)/shard_map/ppermute | solution.py:219
  (12 other events, 27.4 us)

commit v3 on v2

--- a/solution.py
+++ b/solution.py
@@ -1,3 +1,5 @@
+import functools
+
 import jax
 import jax.numpy as jnp
 from jax import lax
@@ -206,6 +208,7 @@
 
 
 VMEM_LIMIT = 48 * 1024 * 1024
+SHORT = pl.CostEstimate(flops=1, bytes_accessed=1, transcendentals=0)
 LOW_BITS = 4
 PACKED = 16 // LOW_BITS
 LEVELS = 32600.0 * 2**LOW_BITS
@@ -268,89 +271,77 @@
         sent[pl.ds(steps * rows, TILE), :] = powers[...].astype(jnp.int32).astype(jnp.int16)
 
 
-K_PARTS = 4
-
-
-def project_kernel(core, normed, *refs):
-    weights = refs[:-4]
-    kept, sent, powers = refs[-3:]
-    half = len(weights) // 2
-    depth = normed.shape[1] // K_PARTS
+def project_kernel(chunk, with_pair, core, normed, weights, *refs):
+    kept, sent, powers, wide, arrived = refs[-5:]
     index = pl.program_id(0)
 
-    def product(blocks):
-        wide = []
-        for first in range(0, len(blocks), K_PARTS):
-            total = None
-            for part in range(K_PARTS):
-                term = jnp.dot(
-                    normed[:, part * depth : (part + 1) * depth],
-                    blocks[first + part][...],
-                    preferred_element_type=jnp.float32,
+    def copies(group):
+        found = []
+        for side in range(2):
+            owner = core[0] if side == 0 else 1 - core[0]
+            first = group * GW + owner * (GQ // 2 * HD) + chunk * (2 * HD)
+            spans = [(first, 0, 2 * HD)]
+            if with_pair:
+                spans.append((group * GW + (GQ + owner) * HD, 2 * HD, HD))
+            for number, (start, offset, size) in enumerate(spans):
+                found.append(
+                    pltpu.make_async_copy(
+                        weights.at[:, pl.ds(pl.multiple_of(start, HD), size)],
+                        wide.at[group, side, :, pl.ds(offset, size)],
+                        arrived.at[group, side, number],
+                    )
                 )
-                total = term if total is None else total + term
-            wide.append(total)
-        return wide[0] if len(wide) == 1 else jnp.concatenate(wide, 1)
-
-    store_codes(sent, powers, product(weights[half:]), index, KVH)
-    kept[0] = product(weights[:half])
+        return found
+
+    @pl.when(index == 0)
+    def _():
+        for group in range(KVH):
+            for copy in copies(group):
+                copy.start()
+
+    for copy in copies(index):
+        copy.wait()
+
+    def product(side):
+        return jnp.dot(normed[...], wide[index, side], preferred_element_type=jnp.float32)
+
+    store_codes(sent, powers, product(1), index, KVH)
+    kept[0] = product(0)
 
 
 def project(core, normed, qkv_weight, chunk, with_pair, after):
     rows, width = normed.shape
     columns = 2 * HD + (HD if with_pair else 0)
-    per_group = GW // (2 * HD)
-    depth = width // K_PARTS
-
-    def wide(other, part):
-        def place(t, c):
-            mine = c[0] if not other else 1 - c[0]
-            return (part, t * per_group + mine * (GQ // 4) + chunk)
-
-        return pl.BlockSpec((depth, 2 * HD), place)
-
-    def narrow(other, part):
-        def place(t, c):
-            mine = c[0] if not other else 1 - c[0]
-            return (part, t * (GW // HD) + GQ + mine)
-
-        return pl.BlockSpec((depth, HD), place)
-
-    specs = []
-    for other in (False, True):
-        specs += [wide(other, part) for part in range(K_PARTS)]
-        if with_pair:
-            specs += [narrow(other, part) for part in range(K_PARTS)]
     sent_rows = KVH * coded_rows(rows) + TILE
     return pl.pallas_call(
-        project_kernel,
+        functools.partial(project_kernel, chunk, with_pair),
         grid_spec=pltpu.PrefetchScalarGridSpec(
             num_scalar_prefetch=1,
             grid=(KVH,),
             in_specs=[pl.BlockSpec((rows, width), lambda t, c: (0, 0))]
-            + specs
-            + [pl.BlockSpec(memory_space=pl.ANY)],
+            + [pl.BlockSpec(memory_space=pl.ANY)] * (1 + len(after)),
             out_specs=[
                 pl.BlockSpec((1, rows, columns), lambda t, c: (t, 0, 0)),
                 pl.BlockSpec((sent_rows, columns), lambda t, c: (0, 0)),
             ],
-            scratch_shapes=[pltpu.VMEM((TILE, columns), jnp.float32)],
+            scratch_shapes=[
+                pltpu.VMEM((TILE, columns), jnp.float32),
+                pltpu.VMEM((KVH, 2, width, columns), jnp.bfloat16),
+                pltpu.SemaphoreType.DMA((KVH, 2, 2)),
+            ],
         ),
         out_shape=[
             jax.ShapeDtypeStruct((KVH, rows, columns), jnp.float32),
             jax.ShapeDtypeStruct((sent_rows, columns), jnp.int16),
         ],
         compiler_params=pltpu.CompilerParams(vmem_limit_bytes=VMEM_LIMIT),
-        cost_estimate=pl.CostEstimate(
-            flops=2 * rows * width * columns * 2 * KVH,
-            bytes_accessed=width * columns * 4 * KVH + rows * columns * 6 * KVH,
-            transcendentals=0,
-        ),
+        cost_estimate=SHORT,
         name="project",
-    )(core, normed, *([qkv_weight] * len(specs)), after)
-
-
-def fold_kernel(steps, bit, held, landed, landed_powers, kept, sent, powers):
+    )(core, normed, qkv_weight, *after)
+
+
+def fold_kernel(steps, bit, held, landed, landed_powers, *refs):
+    kept, sent, powers = refs[-3:]
     index = pl.program_id(0)
     rows = coded_rows(held.shape[1])
     rows_of_powers = landed_powers[...].astype(jnp.int32).astype(jnp.float32)
@@ -365,12 +356,12 @@
     kept[0] = total(mine)
 
 
-def fold(bit, held, landed):
+def fold(bit, held, landed, after):
     blocks, rows, columns = held.shape
     steps = blocks // 2
     coded = coded_rows(rows)
     return pl.pallas_call(
-        lambda *refs: fold_kernel(steps, *refs),
+        functools.partial(fold_kernel, steps),
         grid_spec=pltpu.PrefetchScalarGridSpec(
             num_scalar_prefetch=1,
             grid=(steps,),
@@ -378,7 +369,8 @@
                 pl.BlockSpec((2, rows, columns), lambda i, b: (i, 0, 0)),
                 pl.BlockSpec((2 * coded, columns), lambda i, b: (i, 0)),
                 pl.BlockSpec((TILE, columns), lambda i, b: (blocks * coded // TILE, 0)),
-            ],
+            ]
+            + [pl.BlockSpec(memory_space=pl.ANY)] * len(after),
             out_specs=[
                 pl.BlockSpec((1, rows, columns), lambda i, b: (i, 0, 0)),
                 pl.BlockSpec((steps * coded + TILE, columns), lambda i, b: (0, 0)),
@@ -390,16 +382,13 @@
             jax.ShapeDtypeStruct((steps * coded + TILE, columns), jnp.int16),
         ],
         compiler_params=pltpu.CompilerParams(vmem_limit_bytes=VMEM_LIMIT),
-        cost_estimate=pl.CostEstimate(
-            flops=20 * blocks * rows * columns,
-            bytes_accessed=blocks * rows * columns * 9,
-            transcendentals=0,
-        ),
+        cost_estimate=SHORT,
         name="fold",
-    )(bit, held, landed, landed)
-
-
-def finish_kernel(core, held, landed, cosine, sine, after, queries, *pair):
+    )(bit, held, landed, landed, *after)
+
+
+def finish_kernel(after_count, core, held, landed, cosine, sine, *refs):
+    queries, *pair = refs[after_count:]
     rows = held.shape[1]
     coded = coded_rows(rows)
     power = landed[pl.ds(coded, TILE), :].astype(jnp.int32).astype(jnp.float32)[0:1]
@@ -426,46 +415,59 @@
     if columns > 2 * HD:
         shapes.append(jax.ShapeDtypeStruct((rows, HD), jnp.bfloat16))
     return pl.pallas_call(
-        finish_kernel,
+        functools.partial(finish_kernel, len(after)),
         in_specs=[pl.BlockSpec(memory_space=pltpu.SMEM)]
         + [whole] * 4
-        + [pl.BlockSpec(memory_space=pl.ANY)],
+        + [pl.BlockSpec(memory_space=pl.ANY)] * len(after),
         out_specs=[whole] * len(shapes),
         out_shape=shapes,
         compiler_params=pltpu.CompilerParams(vmem_limit_bytes=VMEM_LIMIT),
+        cost_estimate=SHORT,
         name="finish",
-    )(core, held, landed, cosine, sine, after)
-
-
-def mix_kernel(places, *refs):
-    pieces, weights, start, mixed = refs[0:2], refs[2], refs[3], refs[4]
-    total = refs[5]
+    )(core, held, landed, cosine, sine, *after)
+
+
+MIX_STEPS = 8
+
+
+def mix_kernel(places, first, second, others, weights, start, mixed, total, wide, arrived):
     step = pl.program_id(0)
-    depth = weights.shape[0]
-    per_piece = pieces[0].shape[1] // depth
+    depth = wide.shape[1]
+
+    def copy(part):
+        row = places[part // 2] * (2 * depth) + part % 2 * depth
+        return pltpu.make_async_copy(
+            weights.at[pl.ds(pl.multiple_of(row, depth), depth), :],
+            wide.at[part],
+            arrived.at[part],
+        )
 
     @pl.when(step == 0)
     def _():
+        for part in range(MIX_STEPS):
+            copy(part).start()
         total[...] = start[...].astype(jnp.float32)
 
-    for part in range(2 * per_piece):
+    for part in range(MIX_STEPS):
 
         @pl.when(step == part)
         def _():
-            first = part % per_piece * depth
+            copy(part).wait()
+            piece = (first, second, others.at[0], others.at[1])[part // 2]
+            offset = part % 2 * depth
             total[...] += jnp.dot(
-                pieces[part // per_piece][:, first : first + depth],
-                weights[...],
+                piece[:, offset : offset + depth],
+                wide[part],
                 preferred_element_type=jnp.float32,
             )
 
-    @pl.when(step == 2 * per_piece - 1)
+    @pl.when(step == MIX_STEPS - 1)
     def _():
         mixed[...] = total[...].astype(mixed.dtype)
 
 
-def mix(places, pieces, out_weight, start, dtype):
-    rows, width = pieces[0].shape
+def mix(places, first, second, others, out_weight, start, dtype):
+    rows, width = first.shape
     columns = out_weight.shape[1]
     depth = width // 2
     whole = pl.BlockSpec((rows, width), lambda i, p: (0, 0))
@@ -473,25 +475,26 @@
         mix_kernel,
         grid_spec=pltpu.PrefetchScalarGridSpec(
             num_scalar_prefetch=1,
-            grid=(4,),
+            grid=(MIX_STEPS,),
             in_specs=[
                 whole,
                 whole,
-                pl.BlockSpec((depth, columns), lambda i, p: (p[i // 2] * 2 + i % 2, 0)),
+                pl.BlockSpec((2, rows, width), lambda i, p: (0, 0, 0)),
+                pl.BlockSpec(memory_space=pl.ANY),
                 pl.BlockSpec((rows, columns), lambda i, p: (0, 0)),
             ],
             out_specs=pl.BlockSpec((rows, columns), lambda i, p: (0, 0)),
-            scratch_shapes=[pltpu.VMEM((rows, columns), jnp.float32)],
+            scratch_shapes=[
+                pltpu.VMEM((rows, columns), jnp.float32),
+                pltpu.VMEM((MIX_STEPS, depth, columns), jnp.bfloat16),
+                pltpu.SemaphoreType.DMA((MIX_STEPS,)),
+            ],
         ),
         out_shape=jax.ShapeDtypeStruct((rows, columns), dtype),
         compiler_params=pltpu.CompilerParams(vmem_limit_bytes=VMEM_LIMIT),
-        cost_estimate=pl.CostEstimate(
-            flops=4 * rows * width * columns,
-            bytes_accessed=4 * width * columns + rows * (4 * width + 8 * columns),
-            transcendentals=0,
-        ),
+        cost_estimate=SHORT,
         name="mix",
-    )(places, *pieces, out_weight, start)
+    )(places, first, second, others, out_weight, start)
 
 
 def along(value, pairs):
@@ -508,24 +511,27 @@
     inner = (line == 1) | (line == 2)
     near = swap(attention, 4)
     cross = along(attention, [(1, 2), (2, 1)])
-    pieces = {0: attention, 1: near}
-    across = {0: swap(attention, 2)}
+    across = swap(attention, 2)
     passed = along(cross, [(1, 0), (2, 3)])
     cross_near = along(near, [(1, 2), (2, 1)])
-    across[1] = swap(near, 2)
-    pieces[2] = jnp.where(inner, cross_near, passed)
+    across_near = swap(near, 2)
+    third = jnp.where(inner, cross_near, passed)
     last = along(cross_near, [(1, 0), (2, 3)])
-    across[2] = swap(pieces[2], 2)
-    pieces[3] = jnp.where(inner, cross, last)
-    across[3] = swap(pieces[3], 2)
+    across_third = swap(third, 2)
+    fourth = jnp.where(inner, cross, last)
+    across_fourth = swap(fourth, 2)
+    groups = [
+        (attention, near, 0, 4),
+        (across, across_near, 2, 6),
+        (third, across_third, 8, 10),
+        (fourth, across_fourth, 12, 14),
+    ]
     mixed = start
-    order = [(0, 0), (1, 0), (0, 2), (1, 2), (2, 0), (2, 2), (3, 0), (3, 2)]
-    for number, (k, y) in enumerate(order):
-        piece = (across if y else pieces)[k]
-        owner = device ^ (4 * k + y)
-        places = jnp.stack([owner, owner ^ 1])
-        dtype = jnp.bfloat16 if number == len(order) - 1 else jnp.float32
-        mixed = mix(places, [piece, swap(piece, 1)], out_weight, mixed, dtype)
+    for number, (one, two, x, y) in enumerate(groups):
+        others = swap(jnp.stack([one, two]), 1)
+        places = jnp.stack([device ^ x, device ^ y, device ^ x ^ 1, device ^ y ^ 1])
+        dtype = jnp.bfloat16 if number == len(groups) - 1 else jnp.float32
+        mixed = mix(places, one, two, others, out_weight, mixed, dtype)
     return mixed
 
 
@@ -534,8 +540,10 @@
     queries,
     new_keys,
     new_values,
-    own,
-    other,
+    own_near,
+    own_far,
+    other_near,
+    other_far,
     key_scale,
     value_scale,
     cache_bias,
@@ -573,8 +581,8 @@
         request = slot_request[slot]
         query = queries[request]
         raw = [
-            part[:, slot * BLK : (slot + 1) * BLK, :].reshape(KVH * BLK, 2 * HD)
-            for part in (own, other)
+            part[:, slot * BLK : (slot + 1) * BLK, :].reshape(KVH // 2 * BLK, 2 * HD)
+            for part in (own_near, own_far, other_near, other_far)
         ]
         scores = jnp.concatenate(
             [
@@ -609,7 +617,7 @@
 
 def attend(slot_request, *arrays):
     queries = arrays[0]
-    slots = arrays[5].shape[0]
+    slots = arrays[7].shape[0]
     requests, count, _ = queries.shape
     whole = pl.BlockSpec(memory_space=pltpu.VMEM)
     return pl.pallas_call(
@@ -620,11 +628,7 @@
         scratch_shapes=[pltpu.VMEM((slots, count, HD), jnp.float32)] * 3
         + [pltpu.VMEM((requests, count, HD), jnp.float32)] * 3,
         compiler_params=pltpu.CompilerParams(vmem_limit_bytes=VMEM_LIMIT),
-        cost_estimate=pl.CostEstimate(
-            flops=4 * slots * count * 2 * KVH * BLK * HD,
-            bytes_accessed=2 * slots * 2 * KVH * BLK * 2 * HD,
-            transcendentals=slots * count * 2 * KVH * BLK,
-        ),
+        cost_estimate=SHORT,
         name="attend",
     )(slot_request, *arrays)
 
@@ -645,26 +649,66 @@
     return request, rank, length
 
 
-def handover(cache_pool, cache_scale, chip):
+def arrange_kernel(chip, even, odd, even_scale, odd_scale, after, kept, sent):
+    slots = even.shape[0]
+    for blocks, scale, target in ((even, even_scale, kept), (odd, odd_scale, sent)):
+        target[0, : slots * BLK, :] = blocks[:, 0].reshape(slots * BLK, 2 * HD)
+        target[0, slots * BLK :, :] = scale[0]
+
+
+def arrange(chip, cache_pool, scales, after):
     slots = cache_pool.shape[0]
-    scales = jnp.pad(
-        jnp.transpose(cache_scale, (1, 2, 0)).reshape(KVH, 1, 2 * slots),
-        ((0, 0), (0, TILE - 1), (0, 2 * HD - 2 * slots)),
-    )
-    landed = []
-    for k in range(KVH):
-        head = chip ^ k
-        blocks = lax.dynamic_index_in_dim(cache_pool, head, 1, keepdims=False)
-        rows = jnp.concatenate(
-            [
-                blocks.reshape(slots * BLK, 2 * HD),
-                lax.dynamic_index_in_dim(scales, head, 0, keepdims=False),
-            ],
-            0,
-        )
-        landed.append(swap(rows, 2 * k) if k else rows)
-    own = jnp.stack(landed)
-    return own, swap(own, 1)
+    pool = [
+        pl.BlockSpec(
+            (slots, 1, BLK, 2 * HD), lambda i, c, side=side: (0, c[0] ^ (2 * i + side), 0, 0)
+        )
+        for side in (0, 1)
+    ]
+    scale = [
+        pl.BlockSpec((1, TILE, 2 * HD), lambda i, c, side=side: (c[0] ^ (2 * i + side), 0, 0))
+        for side in (0, 1)
+    ]
+    rows = slots * BLK + TILE
+    out = pl.BlockSpec((1, rows, 2 * HD), lambda i, c: (i, 0, 0))
+    shape = jax.ShapeDtypeStruct((KVH // 2, rows, 2 * HD), jnp.bfloat16)
+    return pl.pallas_call(
+        arrange_kernel,
+        grid_spec=pltpu.PrefetchScalarGridSpec(
+            num_scalar_prefetch=1,
+            grid=(KVH // 2,),
+            in_specs=pool + scale + [pl.BlockSpec(memory_space=pl.ANY)],
+            out_specs=[out, out],
+        ),
+        out_shape=[shape, shape],
+        compiler_params=pltpu.CompilerParams(vmem_limit_bytes=VMEM_LIMIT),
+        cost_estimate=SHORT,
+        name="arrange",
+    )(chip, cache_pool, cache_pool, scales, scales, after)
+
+
+SPLIT = (((0, 0), (0, 2), (1, 0), (1, 2)), ((0, 1), (0, 3), (1, 1), (1, 3)))
+
+
+def regroup_kernel(index_of, kept, landed, *refs):
+    out_kept, out_sent = refs[-2:]
+    for target, (source, index) in enumerate(index_of[0]):
+        out_kept[target] = (kept, landed)[source][index]
+    for target, (source, index) in enumerate(index_of[1]):
+        out_sent[target] = (kept, landed)[source][index]
+
+
+def regroup(index_of, kept, landed, after):
+    whole = pl.BlockSpec(memory_space=pltpu.VMEM)
+    shape = jax.ShapeDtypeStruct(kept.shape, kept.dtype)
+    return pl.pallas_call(
+        functools.partial(regroup_kernel, index_of),
+        in_specs=[whole, whole] + [pl.BlockSpec(memory_space=pl.ANY)] * len(after),
+        out_specs=[whole, whole],
+        out_shape=[shape, shape],
+        compiler_params=pltpu.CompilerParams(vmem_limit_bytes=VMEM_LIMIT),
+        cost_estimate=SHORT,
+        name="regroup",
+    )(kept, landed, *after)
 
 
 def local_pairs(
@@ -692,13 +736,20 @@
     sums = jnp.sum(hidden * hidden, -1)
     for bit in MESH_BITS:
         sums = sums + swap(sums, bit)
+        if bit == 2:
+            early = sums
     normed = (
         hidden * lax.rsqrt(sums[..., None] / D + EPSILON) * norm_gain.astype(jnp.float32)
     ).astype(jnp.bfloat16)
     normed = normed.reshape(rows, width)
-
-    pool, sums = lax.optimization_barrier((cache_pool, sums))
-    own, other = handover(pool, cache_scale, chip)
+    bits = [jnp.reshape((device >> b) & 1, (1,)).astype(jnp.int32) for b in range(4)]
+    scale_rows = jnp.pad(
+        jnp.transpose(cache_scale, (1, 2, 0)).reshape(KVH, 1, 2 * slots),
+        ((0, 0), (0, TILE - 1), (0, 2 * HD - 2 * slots)),
+    )
+    chip_scalar = jnp.reshape(chip, (1,)).astype(jnp.int32)
+    cache_kept, cache_sent = arrange(chip_scalar, cache_pool, scale_rows, early)
+    cache_landed = swap(cache_sent, 2)
 
     step_ids = jnp.arange(STEPS, dtype=jnp.int32)
     row_ids = jnp.arange(QR, dtype=jnp.int32)
@@ -710,32 +761,54 @@
     cosine = jnp.concatenate([jnp.cos(angles)] * 2, 1)
     sine = jnp.concatenate([-jnp.sin(angles), jnp.sin(angles)], 1)
 
-    bits = [jnp.reshape((device >> b) & 1, (1,)).astype(jnp.int32) for b in range(4)]
     count = GQ // 4
     held, sent = [None] * count, [None] * count
 
-    def folded(chunk, b):
-        held[chunk], sent[chunk] = fold(bits[b], held[chunk], swap(sent[chunk], MESH_BITS[b - 1]))
-
-    for chunk in range(count):
-        after = held[chunk - 2] if chunk >= 2 else normed
+    def folded(chunk, b, *after):
+        held[chunk], sent[chunk] = fold(
+            bits[b], held[chunk], swap(sent[chunk], MESH_BITS[b - 1]), after
+        )
+
+    def projected(chunk, *after):
         held[chunk], sent[chunk] = project(
             bits[0], normed, qkv_weight, chunk, chunk == 0, after
         )
-        if chunk >= 1:
-            folded(chunk - 1, 1)
-    folded(count - 1, 1)
-    query_chunks = []
-    after = normed
-    for chunk in range(count):
-        folded(chunk, 2)
-        folded(chunk, 3)
-        done = finish(bits[0], held[chunk], swap(sent[chunk], MESH_BITS[3]), cosine, sine, after)
-        query_chunks.append(done[0])
-        if chunk == 0:
-            pair = done[1]
-            pair_other = swap(pair, 1)
-            after = pair_other
+
+    projected(0, cache_kept)
+    projected(1, held[0])
+    cache_kept, cache_sent = regroup(SPLIT, cache_kept, cache_landed, (held[1],))
+    cache_landed = swap(cache_sent, 4)
+    projected(2, cache_kept)
+    projected(3, held[2])
+    folded(0, 1, held[3])
+    folded(1, 1, held[0])
+    folded(2, 1, held[1])
+    cache_kept, cache_sent = regroup(SPLIT, cache_kept, cache_landed, (held[2],))
+    cache_landed = swap(cache_sent, 8)
+    kept_other = swap(cache_kept, 1)
+    folded(3, 1, cache_kept)
+    folded(0, 2, held[3])
+    folded(1, 2, held[0])
+    folded(0, 3, held[1])
+    folded(2, 2, held[0])
+    folded(1, 3, held[2])
+
+    def finished(chunk, *after):
+        return finish(
+            bits[0], held[chunk], swap(sent[chunk], MESH_BITS[3]), cosine, sine, after
+        )
+
+    query_chunks = [None] * count
+    query_chunks[0], pair = finished(0, held[1])
+    pair_other = swap(pair, 1)
+    folded(3, 2, query_chunks[0])
+    folded(2, 3, held[3])
+    (query_chunks[1],) = finished(1, held[2])
+    folded(3, 3, query_chunks[1], pair_other)
+    (query_chunks[2],) = finished(2, held[3])
+    landed_other = swap(cache_landed, 1)
+    (query_chunks[3],) = finished(3, query_chunks[2])
+    cache_parts = (cache_kept, cache_landed, kept_other, landed_other)
     keys = jnp.where(core == 0, pair, pair_other)
     raw_values = jnp.where(core == 0, pair_other, pair)
     queries = jnp.concatenate(query_chunks, 1).reshape(STEPS, requests, QR, heads, HD)
@@ -752,7 +825,7 @@
     offset = sources[:, :, None] * BLK + jnp.arange(BLK, dtype=jnp.int32)[None, None, :]
     token = slot_rank[:, None] * stripe + offset.reshape(1, stripe)
     cache_bias = jnp.where(token < slot_length[:, None], 0.0, NEG_FILL).astype(jnp.float32)
-    scales = jnp.stack([own[:, slots * BLK, : 2 * slots], other[:, slots * BLK, : 2 * slots]])
+    scales = jnp.concatenate([part[:, slots * BLK, : 2 * slots] for part in cache_parts])
     scales = scales.astype(jnp.float32).reshape(2 * KVH, 2, slots)
     scales = jnp.repeat(jnp.transpose(scales, (1, 2, 0)), BLK, axis=2)
     order = jnp.arange(STEPS * QR * heads, dtype=jnp.int32) // heads
@@ -763,8 +836,7 @@
         queries,
         by_request(keys),
         by_request(raw_values),
-        own,
-        other,
+        *cache_parts,
         scales[0] * HD ** (-0.5),
         scales[1],
         cache_bias,

time: 279 us -> 247 us (0.89)
  the two profiles are of different devices: /device:TPU:0 before, /device:TPU:13 now
where the time goes in v3:
time: 247 us; the launch traced here: 246 us
  Pallas kernels  101 us (41%)
  waiting for transfers between devices  62.4 us (25%)
  starting transfers between devices  62.3 us (25%)
  other arithmetic  9.95 us (4%)
  local copies, waits for them, and re-layouts  9.43 us (4%)
    ppermute x35, starting transfers between devices, swap(): return lax.ppermute(value, 'tensor', [(i, i ^ bit) for i in range(devices)])  54.4 us
    ppermute x35, waiting for transfers between devices, swap(): return lax.ppermute(value, 'tensor', [(i, i ^ bit) for i in range(devices)])  51.3 us
    pallas_call x4, Pallas kernels, project(): pl.pallas_call(functools.partial(project_kernel, chunk, with_pair), grid_...  35.5 us
    pallas_call x4, Pallas kernels, mix(): pl.pallas_call(mix_kernel, grid_spec=pltpu.PrefetchScalarGridSpec(num_sca...  26.6 us
    pallas_call x12, Pallas kernels, fold(): pl.pallas_call(functools.partial(fold_kernel, steps), grid_spec=pltpu.Pre...  22.8 us
    ppermute x4, waiting for transfers between devices, along(): return lax.ppermute(value, 'tensor', table)  11.1 us
    pallas_call x1, Pallas kernels, attend(): pl.pallas_call(attend_kernel, in_specs=[pl.BlockSpec(memory_space=pltpu.S...  10.5 us
    ppermute x4, starting transfers between devices, along(): return lax.ppermute(value, 'tensor', table)  7.85 us
  transfers between devices with their start and end apart: 39, of which 19 were waited for; matrix products, arithmetic and copies ran while one was open for 5% of the time, Pallas kernels for 34%

profile of v3, /device:TPU:13, one launch (start us, length us, event | category | flops | bytes accessed | tf_op | source)
XLA Modules:
  0.0 245.7 jit_solution(14657517443773826971)
XLA Ops:
  0.0 1.2 fusion
  3.0 2.2 collective-permute-done.1
  5.3 2.2 collective-permute-done.2
  7.6 2.3 collective-permute-start.3
  11.4 1.4 copy-done.1
  13.9 9.6 %project.4 = (f32[8,192,384]{2,1,0:T(8,128)S(1)}, s16[1936,384]{1,0:T(8,128)(2,1)}) custom-call(s32[1]{0:T(128)} %bitcast.4.core, bf16[192,1024]{1,0:T(8,128)(2,1)S(1)} %bitcast.58, bf16[1024,18432]{1,0:T(8,128)(2,1)} %weights.11, bf16[4,400,256]{2,1,0:T(8,128)(2,1)S(1)} %get-tuple-element.45.refs_0_.kept), custom_call_target="tpu_custom_call" | custom-call | flops 1 | bytes 1 | tf_op jit(solution)/shard_map/project/pallas_call | solution.py:316
  23.6 2.9 %collective-permute-start.4 = (s16[1936,384]{1,0:T(8,128)(2,1)}, s16[1936,384]{1,0:T(8,128)(2,1)}, u32[]{:S(2)}, u32[]{:S(2)}) collective-permute-start(s16[1936,384]{1,0:T(8,128)(2,1)} %get-tuple-element.47), channel_id=1, source_target_pairs={{0,1},{1,0},{2,3},{3,2},{4,5},{5,4},{6,7},{7,6},{8,9},{9,8},{10,11... | collective-permute-start | bytes 4460552 | tf_op jit(solution)/shard_map/ppermute | solution.py:222
  26.6 8.5 %project.5 = (f32[8,192,256]{2,1,0:T(8,128)S(1)}, s16[1936,256]{1,0:T(8,128)(2,1)}) custom-call(s32[1]{0:T(128)} %bitcast.4.core, bf16[192,1024]{1,0:T(8,128)(2,1)S(1)} %bitcast.59, bf16[1024,18432]{1,0:T(8,128)(2,1)} %weights.11, f32[8,192,384]{2,1,0:T(8,128)S(1)} %get-tuple-element.46.refs_0_.held), custom_call_target="tpu_custom_call" | custom-call | flops 1 | bytes 1 | tf_op jit(solution)/shard_map/project/pallas_call | solution.py:316
  35.9 1.0 regroup.2
  36.9 8.8 %project.6 = (f32[8,192,256]{2,1,0:T(8,128)S(1)}, s16[1936,256]{1,0:T(8,128)(2,1)}) custom-call(s32[1]{0:T(128)} %bitcast.4.core, bf16[192,1024]{1,0:T(8,128)(2,1)S(1)} %bitcast.60, bf16[1024,18432]{1,0:T(8,128)(2,1)} %weights.11, bf16[4,400,256]{2,1,0:T(8,128)(2,1)S(1)} %get-tuple-element.50.refs_0_.kept), custom_call_target="tpu_custom_call" | custom-call | flops 1 | bytes 1 | tf_op jit(solution)/shard_map/project/pallas_call | solution.py:316
  46.5 8.6 %project.7 = (f32[8,192,256]{2,1,0:T(8,128)S(1)}, s16[1936,256]{1,0:T(8,128)(2,1)}) custom-call(s32[1]{0:T(128)} %bitcast.4.core, bf16[192,1024]{1,0:T(8,128)(2,1)S(1)} %bitcast.61, bf16[1024,18432]{1,0:T(8,128)(2,1)} %weights.11, f32[8,192,256]{2,1,0:T(8,128)S(1)} %get-tuple-element.51.refs_0_.held), custom_call_target="tpu_custom_call" | custom-call | flops 1 | bytes 1 | tf_op jit(solution)/shard_map/project/pallas_call | solution.py:316
  56.3 4.3 %fold.12 = (f32[4,192,384]{2,1,0:T(8,128)S(1)}, s16[976,384]{1,0:T(8,128)(2,1)}) custom-call(s32[1]{0:T(128)} %bitcast.7.bit, f32[8,192,384]{2,1,0:T(8,128)} %copy-done, s16[1936,384]{1,0:T(8,128)(2,1)} %collective-permute-done.4.landed.landed_powers, s16[1936,384]{1,0:T(8,128)(2,1)} %collective-permute-done.4.landed.landed_powers, ...), custom_call_target="tpu_custom_call" | custom-call | flops 1 | bytes 1 | tf_op jit(solution)/shard_map/fold/pallas_call | solution.py:363
  60.6 1.2 collective-permute-start.6
  61.8 1.1 fusion.5
  63.0 3.4 %fold.13 = (f32[4,192,256]{2,1,0:T(8,128)S(1)}, s16[976,256]{1,0:T(8,128)(2,1)}) custom-call(s32[1]{0:T(128)} %bitcast.7.bit, f32[8,192,256]{2,1,0:T(8,128)S(1)} %copy-done.3, s16[1936,256]{1,0:T(8,128)(2,1)} %collective-permute-done.10.landed.landed_powers, s16[1936,256]{1,0:T(8,128)(2,1)} %collective-permute-done.10.landed.landed_powers, ...), custom_call_target="tpu_custom_call" | custom-call | flops 1 | bytes 1 | tf_op jit(solution)/shard_map/fold/pallas_call | solution.py:363
  66.4 3.0 %fold.14 = (f32[4,192,256]{2,1,0:T(8,128)S(1)}, s16[976,256]{1,0:T(8,128)(2,1)S(1)}) custom-call(s32[1]{0:T(128)} %bitcast.7.bit, f32[8,192,256]{2,1,0:T(8,128)S(1)} %get-tuple-element.51.refs_0_.held, s16[1936,256]{1,0:T(8,128)(2,1)} %collective-permute-done.9.landed.landed_powers, s16[1936,256]{1,0:T(8,128)(2,1)} %collective-permute-done.9.landed.landed_powers, ...), custom_call_target="tpu_custom_call" | custom-call | flops 1 | bytes 1 | tf_op jit(solution)/shard_map/fold/pallas_call | solution.py:363
  69.4 2.6 %regroup.3 = (bf16[4,400,256]{2,1,0:T(8,128)(2,1)S(1)}, bf16[4,400,256]{2,1,0:T(8,128)(2,1)}) custom-call(bf16[4,400,256]{2,1,0:T(8,128)(2,1)S(1)} %copy-done.9, bf16[4,400,256]{2,1,0:T(8,128)(2,1)} %collective-permute-done.8.landed, f32[4,192,256]{2,1,0:T(8,128)S(1)} %get-tuple-element.60.refs_0_.held), custom_call_target="tpu_custom_call" | custom-call | flops 1 | bytes 1 | tf_op jit(solution)/shard_map/regroup/pallas_call | solution.py:703
  72.6 1.0 collective-permute-start.15
  73.6 2.7 %fold.15 = (f32[4,192,256]{2,1,0:T(8,128)S(1)}, s16[976,256]{1,0:T(8,128)(2,1)S(1)}) custom-call(s32[1]{0:T(128)} %bitcast.7.bit, f32[8,192,256]{2,1,0:T(8,128)S(1)} %get-tuple-element.52.refs_0_.held, s16[1936,256]{1,0:T(8,128)(2,1)} %collective-permute-done.7.landed.landed_powers, s16[1936,256]{1,0:T(8,128)(2,1)} %collective-permute-done.7.landed.landed_powers, ...), custom_call_target="tpu_custom_call" | custom-call | flops 1 | bytes 1 | tf_op jit(solution)/shard_map/fold/pallas_call | solution.py:363
  76.4 2.9 %collective-permute-done.6.landed.landed_powers = s16[976,384]{1,0:T(8,128)(2,1)} collective-permute-done((s16[976,384]{1,0:T(8,128)(2,1)}, s16[976,384]{1,0:T(8,128)(2,1)}, u32[]{:S(2)}, u32[]{:S(2)}) %collective-permute-start.6) | collective-permute-done | bytes 749600 | tf_op jit(solution)/shard_map/ppermute | solution.py:222
  79.3 2.4 fold.16
  81.7 1.3 collective-permute-start.11
  83.0 1.6 collective-permute-start.24
  84.8 5.1 %collective-permute-done.12.landed.landed_powers = s16[976,256]{1,0:T(8,128)(2,1)} collective-permute-done((s16[976,256]{1,0:T(8,128)(2,1)}, s16[976,256]{1,0:T(8,128)(2,1)}, u32[]{:S(2)}, u32[]{:S(2)}) %collective-permute-start.12) | collective-permute-done | bytes 499744 | tf_op jit(solution)/shard_map/ppermute | solution.py:222
  90.0 1.2 collective-permute-start.18
  91.2 2.0 fold.17
  93.2 6.6 %collective-permute-done.11.landed.landed_powers = s16[496,384]{1,0:T(8,128)(2,1)} collective-permute-done((s16[496,384]{1,0:T(8,128)(2,1)}, s16[496,384]{1,0:T(8,128)(2,1)}, u32[]{:S(2)}, u32[]{:S(2)}) %collective-permute-start.11) | collective-permute-done | bytes 380960 | tf_op jit(solution)/shard_map/ppermute | solution.py:222
  99.9 2.0 fold.18
  102.6 2.5 %collective-permute-start.13 = (s16[256,384]{1,0:T(8,128)(2,1)}, s16[256,384]{1,0:T(8,128)(2,1)}, u32[]{:S(2)}, u32[]{:S(2)}) collective-permute-start(s16[256,384]{1,0:T(8,128)(2,1)} %get-tuple-element.68), channel_id=1, source_target_pairs={{0,8},{1,9},{2,10},{3,11},{4,12},{5,13},{6,14},{7,15},{8,0},{9,1},... | collective-permute-start | bytes 589832 | tf_op jit(solution)/shard_map/ppermute | solution.py:222
  105.0 3.3 %collective-permute-done.23.own_far = bf16[4,400,256]{2,1,0:T(8,128)(2,1)} collective-permute-done((bf16[4,400,256]{2,1,0:T(8,128)(2,1)}, bf16[4,400,256]{2,1,0:T(8,128)(2,1)}, u32[]{:S(2)}, u32[]{:S(2)}) %collective-permute-start.23) | collective-permute-done | bytes 819232 | tf_op jit(solution)/shard_map/ppermute | solution.py:222
  108.3 5.1 %collective-permute-start.25 = (bf16[4,400,256]{2,1,0:T(8,128)(2,1)}, bf16[4,400,256]{2,1,0:T(8,128)(2,1)}, u32[]{:S(2)}, u32[]{:S(2)}) collective-permute-start(bf16[4,400,256]{2,1,0:T(8,128)(2,1)} %collective-permute-done.23.own_far), channel_id=1, source_target_pairs={{0,1},{1,0},{2,3},{3,2},{4,5},{5,4},{6,7},{7,6},{8,9},{9,8},{10,11... | collective-permute-start | bytes 2457608 | tf_op jit(solution)/shard_map/ppermute | solution.py:222
  113.5 1.2 pad_maximum_fusion.4
  115.6 1.1 fold.19
  116.7 2.8 %collective-permute-done.14.landed.landed_powers = s16[496,256]{1,0:T(8,128)(2,1)S(1)} collective-permute-done((s16[496,256]{1,0:T(8,128)(2,1)}, s16[496,256]{1,0:T(8,128)(2,1)S(1)}, u32[]{:S(2)}, u32[]{:S(2)}) %collective-permute-start.14) | collective-permute-done | bytes 253984 | tf_op jit(solution)/shard_map/ppermute | solution.py:222
  119.5 2.1 collective-permute-start.17
  122.5 1.1 finish.4
  125.5 1.4 collective-permute-start.21
  128.7 1.7 collective-permute-start.19
  130.4 4.6 %collective-permute-done.16.landed = s16[256,256]{1,0:T(8,128)(2,1)S(1)} collective-permute-done((s16[256,256]{1,0:T(8,128)(2,1)}, s16[256,256]{1,0:T(8,128)(2,1)S(1)}, u32[]{:S(2)}, u32[]{:S(2)}) %collective-permute-start.16) | collective-permute-done | bytes 131104 | tf_op jit(solution)/shard_map/ppermute | solution.py:222
  135.8 2.0 collective-permute-start.22
  138.2 6.0 %collective-permute-done.22.landed = s16[256,256]{1,0:T(8,128)(2,1)S(1)} collective-permute-done((s16[256,256]{1,0:T(8,128)(2,1)S(1)}, s16[256,256]{1,0:T(8,128)(2,1)S(1)}, u32[]{:S(2)}, u32[]{:S(2)}) %collective-permute-start.22) | collective-permute-done | bytes 131104 | tf_op jit(solution)/shard_map/ppermute | solution.py:222
  146.1 10.5 %attend.1 = bf16[16,96,128]{2,1,0:T(8,128)(2,1)S(1)} custom-call(s32[24]{0:T(128)S(1)} %get-tuple-element.87.slot_request, bf16[16,96,128]{2,1,0:T(8,128)(2,1)S(1)} %bitcast.74, bf16[16,16,128]{2,1,0:T(8,128)(2,1)S(1)} %pad.12.new_keys, bf16[16,16,128]{2,1,0:T(8,128)(2,1)S(1)} %pad.13.new_values, ...), custom_call_target="tpu_custom_call" | custom-call | flops 1 | bytes 1 | tf_op jit(solution)/shard_map/attend/pallas_call | solution.py:623
  156.7 2.8 %collective-permute-start.27 = (bf16[192,1024]{1,0:T(8,128)(2,1)S(1)}, bf16[192,1024]{1,0:T(8,128)(2,1)S(1)}, u32[]{:S(2)}, u32[]{:S(2)}) collective-permute-start(bf16[192,1024]{1,0:T(8,128)(2,1)S(1)} %bitcast.65), channel_id=1, source_target_pairs={{0,4},{1,5},{2,6},{3,7},{4,0},{5,1},{6,2},{7,3},{8,12},{9,13},{10,... | collective-permute-start | bytes 1179656 | tf_op jit(solution)/shard_map/ppermute | solution.py:222
  159.4 2.6 %collective-permute-start.26 = (bf16[192,1024]{1,0:T(8,128)(2,1)S(1)}, bf16[192,1024]{1,0:T(8,128)(2,1)S(1)}, u32[]{:S(2)}, u32[]{:S(2)}) collective-permute-start(bf16[192,1024]{1,0:T(8,128)(2,1)S(1)} %bitcast.66), channel_id=1, source_target_pairs={{4,8},{5,9},{6,10},{7,11},{8,4},{9,5},{10,6},{11,7},{20,24},{21,25... | collective-permute-start | bytes 1179656 | tf_op jit(solution)/shard_map/ppermute | solution.py:506
  162.0 5.8 %collective-permute-done.27.second = bf16[192,1024]{1,0:T(8,128)(2,1)S(1)} collective-permute-done((bf16[192,1024]{1,0:T(8,128)(2,1)S(1)}, bf16[192,1024]{1,0:T(8,128)(2,1)S(1)}, u32[]{:S(2)}, u32[]{:S(2)}) %collective-permute-start.27) | collective-permute-done | bytes 393248 | tf_op jit(solution)/shard_map/ppermute | solution.py:222
  167.9 1.9 collective-permute-start.28
  170.6 1.3 collective-permute-start.32
  171.9 6.8 %collective-permute-done.28 = bf16[192,1024]{1,0:T(8,128)(2,1)S(1)} collective-permute-done((bf16[192,1024]{1,0:T(8,128)(2,1)S(1)}, bf16[192,1024]{1,0:T(8,128)(2,1)S(1)}, u32[]{:S(2)}, u32[]{:S(2)}) %collective-permute-start.28) | collective-permute-done | bytes 393248 | tf_op jit(solution)/shard_map/ppermute | solution.py:506
  178.7 2.1 collective-permute-start.29
  181.7 1.5 collective-permute-start.36
  183.3 3.5 %collective-permute-done.29 = bf16[192,1024]{1,0:T(8,128)(2,1)} collective-permute-done((bf16[192,1024]{1,0:T(8,128)(2,1)S(1)}, bf16[192,1024]{1,0:T(8,128)(2,1)}, u32[]{:S(2)}, u32[]{:S(2)}) %collective-permute-start.29) | collective-permute-done | bytes 393248 | tf_op jit(solution)/shard_map/ppermute | solution.py:506
  186.9 1.0 pad_maximum_fusion.3
  187.8 2.9 %collective-permute-start.38 = (bf16[2,192,1024]{2,1,0:T(8,128)(2,1)}, bf16[2,192,1024]{2,1,0:T(8,128)(2,1)}, u32[]{:S(2)}, u32[]{:S(2)}) collective-permute-start(bf16[2,192,1024]{2,1,0:T(8,128)(2,1)} %pad_maximum_fusion.3), channel_id=1, source_target_pairs={{0,1},{1,0},{2,3},{3,2},{4,5},{5,4},{6,7},{7,6},{8,9},{9,8},{10,11... | collective-permute-start | bytes 2359304 | tf_op jit(solution)/shard_map/ppermute | solution.py:222
  190.7 6.5 %collective-permute-done.36.second = bf16[192,1024]{1,0:T(8,128)(2,1)S(1)} collective-permute-done((bf16[192,1024]{1,0:T(8,128)(2,1)S(1)}, bf16[192,1024]{1,0:T(8,128)(2,1)S(1)}, u32[]{:S(2)}, u32[]{:S(2)}) %collective-permute-start.36) | collective-permute-done | bytes 393248 | tf_op jit(solution)/shard_map/ppermute | solution.py:222
  197.2 1.0 pad_maximum_fusion.2
  198.2 6.6 %collective-permute-start.37 = (bf16[2,192,1024]{2,1,0:T(8,128)(2,1)}, bf16[2,192,1024]{2,1,0:T(8,128)(2,1)}, u32[]{:S(2)}, u32[]{:S(2)}) collective-permute-start(bf16[2,192,1024]{2,1,0:T(8,128)(2,1)} %pad_maximum_fusion.2), channel_id=1, source_target_pairs={{0,1},{1,0},{2,3},{3,2},{4,5},{5,4},{6,7},{7,6},{8,9},{9,8},{10,11... | collective-permute-start | bytes 2359304 | tf_op jit(solution)/shard_map/ppermute | solution.py:222
  205.7 1.0 pad_maximum_fusion.1
  206.6 6.6 %collective-permute-start.34 = (bf16[2,192,1024]{2,1,0:T(8,128)(2,1)}, bf16[2,192,1024]{2,1,0:T(8,128)(2,1)}, u32[]{:S(2)}, u32[]{:S(2)}) collective-permute-start(bf16[2,192,1024]{2,1,0:T(8,128)(2,1)} %pad_maximum_fusion.1), channel_id=1, source_target_pairs={{0,1},{1,0},{2,3},{3,2},{4,5},{5,4},{6,7},{7,6},{8,9},{9,8},{10,11... | collective-permute-start | bytes 2359304 | tf_op jit(solution)/shard_map/ppermute | solution.py:222
  214.1 1.0 pad_maximum_fusion
  215.1 3.5 %collective-permute-start.31 = (bf16[2,192,1024]{2,1,0:T(8,128)(2,1)}, bf16[2,192,1024]{2,1,0:T(8,128)(2,1)}, u32[]{:S(2)}, u32[]{:S(2)}) collective-permute-start(bf16[2,192,1024]{2,1,0:T(8,128)(2,1)} %pad_maximum_fusion), channel_id=1, source_target_pairs={{0,1},{1,0},{2,3},{3,2},{4,5},{5,4},{6,7},{7,6},{8,9},{9,8},{10,11... | collective-permute-start | bytes 2359304 | tf_op jit(solution)/shard_map/ppermute | solution.py:222
  218.9 6.6 %mix.4.start = f32[192,1024]{1,0:T(8,128)S(1)} custom-call(s32[4]{0:T(128)S(1)} %pad_add_fusion.3.places, bf16[192,1024]{1,0:T(8,128)(2,1)S(1)} %bitcast.68, bf16[192,1024]{1,0:T(8,128)(2,1)S(1)} %collective-permute-done.27.second, bf16[2,192,1024]{2,1,0:T(8,128)(2,1)} %collective-permute-done.38.others, bf16[16384,1024]{1,0:T(8,128)(2,1)} %weights.15, ...), custom_call_target="tpu_custom_call" | custom-call | flops 1 | bytes 1 | tf_op jit(solution)/shard_map/mix/pallas_call | solution.py:474
  225.5 6.4 %mix.5.start = f32[192,1024]{1,0:T(8,128)S(1)} custom-call(s32[4]{0:T(128)S(1)} %pad_add_fusion.2.places, bf16[192,1024]{1,0:T(8,128)(2,1)S(1)} %collective-permute-done.35.first, bf16[192,1024]{1,0:T(8,128)(2,1)S(1)} %collective-permute-done.36.second, bf16[2,192,1024]{2,1,0:T(8,128)(2,1)} %collective-permute-done.37.others, bf16[16384,1024]{1,0:T(8,128)(2,1)} %weights.15, ...), custom_call_target="tpu_custom_call" | custom-call | flops 1 | bytes 1 | tf_op jit(solution)/shard_map/mix/pallas_call | solution.py:474
  231.9 6.4 %mix.6.start = f32[192,1024]{1,0:T(8,128)S(1)} custom-call(s32[4]{0:T(128)S(1)} %pad_add_fusion.1.places, bf16[192,1024]{1,0:T(8,128)(2,1)S(1)} %broadcast_select_fusion.first, bf16[192,1024]{1,0:T(8,128)(2,1)S(1)} %collective-permute-done.33.second, bf16[2,192,1024]{2,1,0:T(8,128)(2,1)} %collective-permute-done.34.others, bf16[16384,1024]{1,0:T(8,128)(2,1)} %weights.15, ...), custom_call_target="tpu_custom_call" | custom-call | flops 1 | bytes 1 | tf_op jit(solution)/shard_map/mix/pallas_call | solution.py:474
  238.3 7.2 %mix.7 = bf16[192,1024]{1,0:T(8,128)(2,1)} custom-call(s32[4]{0:T(128)S(1)} %pad_add_fusion.places, bf16[192,1024]{1,0:T(8,128)(2,1)S(1)} %broadcast_select_fusion.1.first, bf16[192,1024]{1,0:T(8,128)(2,1)S(1)} %collective-permute-done.30.second, bf16[2,192,1024]{2,1,0:T(8,128)(2,1)} %collective-permute-done.31.others, bf16[16384,1024]{1,0:T(8,128)(2,1)} %weights.15, ...), custom_call_target="tpu_custom_call" | custom-call | flops 1 | bytes 1 | tf_op jit(solution)/shard_map/mix/pallas_call | solution.py:474
  (166 shorter events, 21.8 us)
Async XLA Ops:
  1.2 1.6 collective-permute-start
  2.7 2.4 collective-permute-start.1
  5.1 2.4 collective-permute-start.2
  7.6 5.9 %collective-permute-start.3 = (f32[2,96]{1,0:T(2,128)S(1)}, f32[2,96]{1,0:T(2,128)S(1)}, u32[]{:S(2)}, u32[]{:S(2)}) collective-permute-start(f32[2,96]{1,0:T(2,128)S(1)} %add.140), channel_id=1, source_target_pairs={{0,8},{1,9},{2,10},{3,11},{4,12},{5,13},{6,14},{7,15},{8,0},{9,1},... | collective-permute-start | bytes 2312 | tf_op jit(solution)/shard_map/ppermute | solution.py:222
  11.3 1.4 copy-start.1
  12.8 1.0 copy-start.6
  13.1 22.7 %collective-permute-start.5 = (bf16[4,400,256]{2,1,0:T(8,128)(2,1)S(1)}, bf16[4,400,256]{2,1,0:T(8,128)(2,1)S(1)}, u32[]{:S(2)}, u32[]{:S(2)}) collective-permute-start(bf16[4,400,256]{2,1,0:T(8,128)(2,1)S(1)} %get-tuple-element.48), channel_id=1, source_target_pairs={{0,2},{1,3},{2,0},{3,1},{4,6},{5,7},{6,4},{7,5},{8,10},{9,11},{10,... | collective-permute-start | bytes 2457608 | tf_op jit(solution)/shard_map/ppermute | solution.py:222
  13.9 12.6 %copy-start.27 = (s32[16]{0:T(128)S(1)}, s32[16]{0:T(128)}, u32[]{:S(2)}) copy-start(s32[16]{0:T(128)} %param.14) | copy-start | bytes 196
  23.6 11.5 %copy-start = (f32[8,192,384]{2,1,0:T(8,128)}, f32[8,192,384]{2,1,0:T(8,128)S(1)}, u32[]{:S(2)}) copy-start(f32[8,192,384]{2,1,0:T(8,128)S(1)} %get-tuple-element.46.refs_0_.held) | copy-start | bytes 7077892
  23.6 32.7 %collective-permute-start.4 = (s16[1936,384]{1,0:T(8,128)(2,1)}, s16[1936,384]{1,0:T(8,128)(2,1)}, u32[]{:S(2)}, u32[]{:S(2)}) collective-permute-start(s16[1936,384]{1,0:T(8,128)(2,1)} %get-tuple-element.47), channel_id=1, source_target_pairs={{0,1},{1,0},{2,3},{3,2},{4,5},{5,4},{6,7},{7,6},{8,9},{9,8},{10,11... | collective-permute-start | bytes 4460552 | tf_op jit(solution)/shard_map/ppermute | solution.py:222
  35.1 1.8 copy-start.2
  35.1 27.9 %collective-permute-start.10 = (s16[1936,256]{1,0:T(8,128)(2,1)}, s16[1936,256]{1,0:T(8,128)(2,1)}, u32[]{:S(2)}, u32[]{:S(2)}) collective-permute-start(s16[1936,256]{1,0:T(8,128)(2,1)} %get-tuple-element.58), channel_id=1, source_target_pairs={{0,1},{1,0},{2,3},{3,2},{4,5},{5,4},{6,7},{7,6},{8,9},{9,8},{10,11... | collective-permute-start | bytes 2973704 | tf_op jit(solution)/shard_map/ppermute | solution.py:222
  36.9 8.8 %copy-start.8 = (bf16[4,400,256]{2,1,0:T(8,128)(2,1)}, bf16[4,400,256]{2,1,0:T(8,128)(2,1)S(1)}, u32[]{:S(2)}) copy-start(bf16[4,400,256]{2,1,0:T(8,128)(2,1)S(1)} %get-tuple-element.50.refs_0_.kept) | copy-start | bytes 2457604
  45.7 20.7 %collective-permute-start.9 = (s16[1936,256]{1,0:T(8,128)(2,1)}, s16[1936,256]{1,0:T(8,128)(2,1)}, u32[]{:S(2)}, u32[]{:S(2)}) collective-permute-start(s16[1936,256]{1,0:T(8,128)(2,1)} %get-tuple-element.57), channel_id=1, source_target_pairs={{0,1},{1,0},{2,3},{3,2},{4,5},{5,4},{6,7},{7,6},{8,9},{9,8},{10,11... | collective-permute-start | bytes 2973704 | tf_op jit(solution)/shard_map/ppermute | solution.py:222
  46.1 23.2 %collective-permute-start.8 = (bf16[4,400,256]{2,1,0:T(8,128)(2,1)}, bf16[4,400,256]{2,1,0:T(8,128)(2,1)}, u32[]{:S(2)}, u32[]{:S(2)}) collective-permute-start(bf16[4,400,256]{2,1,0:T(8,128)(2,1)} %get-tuple-element.56), channel_id=1, source_target_pairs={{0,4},{1,5},{2,6},{3,7},{4,0},{5,1},{6,2},{7,3},{8,12},{9,13},{10,... | collective-permute-start | bytes 2457608 | tf_op jit(solution)/shard_map/ppermute | solution.py:222
  55.1 18.5 %collective-permute-start.7 = (s16[1936,256]{1,0:T(8,128)(2,1)}, s16[1936,256]{1,0:T(8,128)(2,1)}, u32[]{:S(2)}, u32[]{:S(2)}) collective-permute-start(s16[1936,256]{1,0:T(8,128)(2,1)} %get-tuple-element.55), channel_id=1, source_target_pairs={{0,1},{1,0},{2,3},{3,2},{4,5},{5,4},{6,7},{7,6},{8,9},{9,8},{10,11... | collective-permute-start | bytes 2973704 | tf_op jit(solution)/shard_map/ppermute | solution.py:222
  56.3 6.7 %copy-start.3 = (f32[8,192,256]{2,1,0:T(8,128)S(1)}, f32[8,192,256]{2,1,0:T(8,128)}, u32[]{:S(2)}) copy-start(f32[8,192,256]{2,1,0:T(8,128)} %copy-done.2) | copy-start | bytes 4718596
  60.6 5.7 %copy-start.4 = (f32[4,192,384]{2,1,0:T(8,128)}, f32[4,192,384]{2,1,0:T(8,128)S(1)}, u32[]{:S(2)}) copy-start(f32[4,192,384]{2,1,0:T(8,128)S(1)} %get-tuple-element.53.refs_0_.held) | copy-start | bytes 3538948
  60.6 18.6 %collective-permute-start.6 = (s16[976,384]{1,0:T(8,128)(2,1)}, s16[976,384]{1,0:T(8,128)(2,1)}, u32[]{:S(2)}, u32[]{:S(2)}) collective-permute-start(s16[976,384]{1,0:T(8,128)(2,1)} %get-tuple-element.54), channel_id=1, source_target_pairs={{0,2},{1,3},{2,0},{3,1},{4,6},{5,7},{6,4},{7,5},{8,10},{9,11},{10,... | collective-permute-start | bytes 2248712 | tf_op jit(solution)/shard_map/ppermute | solution.py:222
  66.3 3.0 %copy-start.10 = (f32[4,192,256]{2,1,0:T(8,128)}, f32[4,192,256]{2,1,0:T(8,128)S(1)}, u32[]{:S(2)}) copy-start(f32[4,192,256]{2,1,0:T(8,128)S(1)} %get-tuple-element.59.refs_0_.held) | copy-start | bytes 2359300
  66.4 3.0 %copy-start.9 = (bf16[4,400,256]{2,1,0:T(8,128)(2,1)S(1)}, bf16[4,400,256]{2,1,0:T(8,128)(2,1)}, u32[]{:S(2)}) copy-start(bf16[4,400,256]{2,1,0:T(8,128)(2,1)} %copy-done.8) | copy-start | bytes 2457604
  69.3 2.6 %copy-start.12 = (f32[4,192,256]{2,1,0:T(8,128)}, f32[4,192,256]{2,1,0:T(8,128)S(1)}, u32[]{:S(2)}) copy-start(f32[4,192,256]{2,1,0:T(8,128)S(1)} %get-tuple-element.60.refs_0_.held) | copy-start | bytes 2359300
  69.3 2.6 %copy-start.23 = (s16[976,256]{1,0:T(8,128)(2,1)}, s16[976,256]{1,0:T(8,128)(2,1)S(1)}, u32[]{:S(2)}) copy-start(s16[976,256]{1,0:T(8,128)(2,1)S(1)} %get-tuple-element.70) | copy-start | bytes 1499140
  71.9 36.4 %collective-permute-start.23 = (bf16[4,400,256]{2,1,0:T(8,128)(2,1)}, bf16[4,400,256]{2,1,0:T(8,128)(2,1)}, u32[]{:S(2)}, u32[]{:S(2)}) collective-permute-start(bf16[4,400,256]{2,1,0:T(8,128)(2,1)} %get-tuple-element.84), channel_id=1, source_target_pairs={{0,8},{1,9},{2,10},{3,11},{4,12},{5,13},{6,14},{7,15},{8,0},{9,1},... | collective-permute-start | bytes 2457608 | tf_op jit(solution)/shard_map/ppermute | solution.py:222
  72.1 17.9 %collective-permute-start.12 = (s16[976,256]{1,0:T(8,128)(2,1)}, s16[976,256]{1,0:T(8,128)(2,1)}, u32[]{:S(2)}, u32[]{:S(2)}) collective-permute-start(s16[976,256]{1,0:T(8,128)(2,1)} %get-tuple-element.65), channel_id=1, source_target_pairs={{0,2},{1,3},{2,0},{3,1},{4,6},{5,7},{6,4},{7,5},{8,10},{9,11},{10,... | collective-permute-start | bytes 1499144 | tf_op jit(solution)/shard_map/ppermute | solution.py:222
  72.6 29.9 %collective-permute-start.15 = (s16[976,256]{1,0:T(8,128)(2,1)}, s16[976,256]{1,0:T(8,128)(2,1)S(1)}, u32[]{:S(2)}, u32[]{:S(2)}) collective-permute-start(s16[976,256]{1,0:T(8,128)(2,1)} %copy-done.23), channel_id=1, source_target_pairs={{0,2},{1,3},{2,0},{3,1},{4,6},{5,7},{6,4},{7,5},{8,10},{9,11},{10,... | collective-permute-start | bytes 1499144 | tf_op jit(solution)/shard_map/ppermute | solution.py:222
  73.6 5.7 %copy-start.5 = (f32[4,192,384]{2,1,0:T(8,128)S(1)}, f32[4,192,384]{2,1,0:T(8,128)}, u32[]{:S(2)}) copy-start(f32[4,192,384]{2,1,0:T(8,128)} %copy-done.4) | copy-start | bytes 3538948
  76.3 2.9 %copy-start.22 = (s16[976,256]{1,0:T(8,128)(2,1)}, s16[976,256]{1,0:T(8,128)(2,1)S(1)}, u32[]{:S(2)}) copy-start(s16[976,256]{1,0:T(8,128)(2,1)S(1)} %get-tuple-element.76) | copy-start | bytes 1499140
  76.4 5.3 %copy-start.14 = (f32[4,192,256]{2,1,0:T(8,128)}, f32[4,192,256]{2,1,0:T(8,128)S(1)}, u32[]{:S(2)}) copy-start(f32[4,192,256]{2,1,0:T(8,128)S(1)} %get-tuple-element.62.refs_0_.held) | copy-start | bytes 2359300
  79.3 5.3 %copy-start.26 = (s32[16,16]{1,0:T(8,128)S(1)}, s32[16,16]{1,0:T(8,128)}, u32[]{:S(2)}) copy-start(s32[16,16]{1,0:T(8,128)} %param.15) | copy-start | bytes 3076
  79.3 11.9 %copy-start.11 = (f32[4,192,256]{2,1,0:T(8,128)S(1)}, f32[4,192,256]{2,1,0:T(8,128)}, u32[]{:S(2)}) copy-start(f32[4,192,256]{2,1,0:T(8,128)} %copy-done.10) | copy-start | bytes 2359300
  81.7 18.2 %collective-permute-start.11 = (s16[496,384]{1,0:T(8,128)(2,1)}, s16[496,384]{1,0:T(8,128)(2,1)}, u32[]{:S(2)}, u32[]{:S(2)}) collective-permute-start(s16[496,384]{1,0:T(8,128)(2,1)} %get-tuple-element.64), channel_id=1, source_target_pairs={{0,4},{1,5},{2,6},{3,7},{4,0},{5,1},{6,2},{7,3},{8,12},{9,13},{10,... | collective-permute-start | bytes 1142792 | tf_op jit(solution)/shard_map/ppermute | solution.py:222
  83.0 42.5 %collective-permute-start.24 = (bf16[4,400,256]{2,1,0:T(8,128)(2,1)S(1)}, bf16[4,400,256]{2,1,0:T(8,128)(2,1)}, u32[]{:S(2)}, u32[]{:S(2)}) collective-permute-start(bf16[4,400,256]{2,1,0:T(8,128)(2,1)S(1)} %get-tuple-element.61.refs_0_.own_near), channel_id=1, source_target_pairs={{0,1},{1,0},{2,3},{3,2},{4,5},{5,4},{6,7},{7,6},{8,9},{9,8},{10,11... | collective-permute-start | bytes 2457608 | tf_op jit(solution)/shard_map/ppermute | solution.py:222
  90.0 33.6 %collective-permute-start.18 = (s16[976,256]{1,0:T(8,128)(2,1)}, s16[976,256]{1,0:T(8,128)(2,1)S(1)}, u32[]{:S(2)}, u32[]{:S(2)}) collective-permute-start(s16[976,256]{1,0:T(8,128)(2,1)} %copy-done.22), channel_id=1, source_target_pairs={{0,2},{1,3},{2,0},{3,1},{4,6},{5,7},{6,4},{7,5},{8,10},{9,11},{10,... | collective-permute-start | bytes 1499144 | tf_op jit(solution)/shard_map/ppermute | solution.py:222
  93.2 9.3 %copy-start.16 = (f32[2,192,256]{2,1,0:T(8,128)}, f32[2,192,256]{2,1,0:T(8,128)S(1)}, u32[]{:S(2)}) copy-start(f32[2,192,256]{2,1,0:T(8,128)S(1)} %get-tuple-element.66.refs_0_.held) | copy-start | bytes 1179652
  93.2 21.4 %copy-start.13 = (f32[4,192,256]{2,1,0:T(8,128)S(1)}, f32[4,192,256]{2,1,0:T(8,128)}, u32[]{:S(2)}) copy-start(f32[4,192,256]{2,1,0:T(8,128)} %copy-done.12) | copy-start | bytes 2359300
  99.8 19.7 %collective-permute-start.14 = (s16[496,256]{1,0:T(8,128)(2,1)}, s16[496,256]{1,0:T(8,128)(2,1)S(1)}, u32[]{:S(2)}, u32[]{:S(2)}) collective-permute-start(s16[496,256]{1,0:T(8,128)(2,1)} %get-tuple-element.69), channel_id=1, source_target_pairs={{0,4},{1,5},{2,6},{3,7},{4,0},{5,1},{6,2},{7,3},{8,12},{9,13},{10,... | collective-permute-start | bytes 761864 | tf_op jit(solution)/shard_map/ppermute | solution.py:222
  102.6 19.3 %collective-permute-start.13 = (s16[256,384]{1,0:T(8,128)(2,1)}, s16[256,384]{1,0:T(8,128)(2,1)}, u32[]{:S(2)}, u32[]{:S(2)}) collective-permute-start(s16[256,384]{1,0:T(8,128)(2,1)} %get-tuple-element.68), channel_id=1, source_target_pairs={{0,8},{1,9},{2,10},{3,11},{4,12},{5,13},{6,14},{7,15},{8,0},{9,1},... | collective-permute-start | bytes 589832 | tf_op jit(solution)/shard_map/ppermute | solution.py:222
  108.3 36.3 %collective-permute-start.25 = (bf16[4,400,256]{2,1,0:T(8,128)(2,1)}, bf16[4,400,256]{2,1,0:T(8,128)(2,1)}, u32[]{:S(2)}, u32[]{:S(2)}) collective-permute-start(bf16[4,400,256]{2,1,0:T(8,128)(2,1)} %collective-permute-done.23.own_far), channel_id=1, source_target_pairs={{0,1},{1,0},{2,3},{3,2},{4,5},{5,4},{6,7},{7,6},{8,9},{9,8},{10,11... | collective-permute-start | bytes 2457608 | tf_op jit(solution)/shard_map/ppermute | solution.py:222
  113.5 8.1 %copy-start.17 = (f32[2,192,256]{2,1,0:T(8,128)S(1)}, f32[2,192,256]{2,1,0:T(8,128)}, u32[]{:S(2)}) copy-start(f32[2,192,256]{2,1,0:T(8,128)} %copy-done.16) | copy-start | bytes 1179652
  115.6 6.8 %copy-start.20 = (f32[1,192,384]{2,1,0:T(8,128)S(1)}, f32[1,192,384]{2,1,0:T(8,128)}, u32[]{:S(2)}) copy-start(f32[1,192,384]{2,1,0:T(8,128)} %copy-done.18) | copy-start | bytes 884740
  116.7 6.9 %copy-start.15 = (f32[4,192,256]{2,1,0:T(8,128)S(1)}, f32[4,192,256]{2,1,0:T(8,128)}, u32[]{:S(2)}) copy-start(f32[4,192,256]{2,1,0:T(8,128)} %copy-done.14) | copy-start | bytes 2359300
  119.5 8.4 %collective-permute-start.17 = (s16[496,256]{1,0:T(8,128)(2,1)}, s16[496,256]{1,0:T(8,128)(2,1)S(1)}, u32[]{:S(2)}, u32[]{:S(2)}) collective-permute-start(s16[496,256]{1,0:T(8,128)(2,1)} %get-tuple-element.75), channel_id=1, source_target_pairs={{0,4},{1,5},{2,6},{3,7},{4,0},{5,1},{6,2},{7,3},{8,12},{9,13},{10,... | collective-permute-start | bytes 761864 | tf_op jit(solution)/shard_map/ppermute | solution.py:222
  124.3 11.4 %collective-permute-start.20 = (s16[496,256]{1,0:T(8,128)(2,1)S(1)}, s16[496,256]{1,0:T(8,128)(2,1)S(1)}, u32[]{:S(2)}, u32[]{:S(2)}) collective-permute-start(s16[496,256]{1,0:T(8,128)(2,1)S(1)} %get-tuple-element.80), channel_id=1, source_target_pairs={{0,4},{1,5},{2,6},{3,7},{4,0},{5,1},{6,2},{7,3},{8,12},{9,13},{10,... | collective-permute-start | bytes 761864 | tf_op jit(solution)/shard_map/ppermute | solution.py:222
  124.5 10.6 %collective-permute-start.16 = (s16[256,256]{1,0:T(8,128)(2,1)}, s16[256,256]{1,0:T(8,128)(2,1)S(1)}, u32[]{:S(2)}, u32[]{:S(2)}) collective-permute-start(s16[256,256]{1,0:T(8,128)(2,1)} %copy-done.24), channel_id=1, source_target_pairs={{0,8},{1,9},{2,10},{3,11},{4,12},{5,13},{6,14},{7,15},{8,0},{9,1},... | collective-permute-start | bytes 393224 | tf_op jit(solution)/shard_map/ppermute | solution.py:222
  125.5 9.7 %collective-permute-start.21 = (bf16[192,128]{1,0:T(8,128)(2,1)S(1)}, bf16[192,128]{1,0:T(8,128)(2,1)S(1)}, u32[]{:S(2)}, u32[]{:S(2)}) collective-permute-start(bf16[192,128]{1,0:T(8,128)(2,1)S(1)} %get-tuple-element.81), channel_id=1, source_target_pairs={{0,1},{1,0},{2,3},{3,2},{4,5},{5,4},{6,7},{7,6},{8,9},{9,8},{10,11... | collective-permute-start | bytes 147464 | tf_op jit(solution)/shard_map/ppermute | solution.py:222
  128.7 9.3 %collective-permute-start.19 = (s16[256,256]{1,0:T(8,128)(2,1)}, s16[256,256]{1,0:T(8,128)(2,1)S(1)}, u32[]{:S(2)}, u32[]{:S(2)}) collective-permute-start(s16[256,256]{1,0:T(8,128)(2,1)} %get-tuple-element.79), channel_id=1, source_target_pairs={{0,8},{1,9},{2,10},{3,11},{4,12},{5,13},{6,14},{7,15},{8,0},{9,1},... | collective-permute-start | bytes 393224 | tf_op jit(solution)/shard_map/ppermute | solution.py:222
  135.8 8.4 %collective-permute-start.22 = (s16[256,256]{1,0:T(8,128)(2,1)S(1)}, s16[256,256]{1,0:T(8,128)(2,1)S(1)}, u32[]{:S(2)}, u32[]{:S(2)}) collective-permute-start(s16[256,256]{1,0:T(8,128)(2,1)S(1)} %get-tuple-element.83), channel_id=1, source_target_pairs={{0,8},{1,9},{2,10},{3,11},{4,12},{5,13},{6,14},{7,15},{8,0},{9,1},... | collective-permute-start | bytes 393224 | tf_op jit(solution)/shard_map/ppermute | solution.py:222
  144.4 1.7 copy-start.21
  156.7 11.2 %collective-permute-start.27 = (bf16[192,1024]{1,0:T(8,128)(2,1)S(1)}, bf16[192,1024]{1,0:T(8,128)(2,1)S(1)}, u32[]{:S(2)}, u32[]{:S(2)}) collective-permute-start(bf16[192,1024]{1,0:T(8,128)(2,1)S(1)} %bitcast.65), channel_id=1, source_target_pairs={{0,4},{1,5},{2,6},{3,7},{4,0},{5,1},{6,2},{7,3},{8,12},{9,13},{10,... | collective-permute-start | bytes 1179656 | tf_op jit(solution)/shard_map/ppermute | solution.py:222
  159.4 11.2 %collective-permute-start.26 = (bf16[192,1024]{1,0:T(8,128)(2,1)S(1)}, bf16[192,1024]{1,0:T(8,128)(2,1)S(1)}, u32[]{:S(2)}, u32[]{:S(2)}) collective-permute-start(bf16[192,1024]{1,0:T(8,128)(2,1)S(1)} %bitcast.66), channel_id=1, source_target_pairs={{4,8},{5,9},{6,10},{7,11},{8,4},{9,5},{10,6},{11,7},{20,24},{21,25... | collective-permute-start | bytes 1179656 | tf_op jit(solution)/shard_map/ppermute | solution.py:506
  167.9 10.9 %collective-permute-start.28 = (bf16[192,1024]{1,0:T(8,128)(2,1)S(1)}, bf16[192,1024]{1,0:T(8,128)(2,1)S(1)}, u32[]{:S(2)}, u32[]{:S(2)}) collective-permute-start(bf16[192,1024]{1,0:T(8,128)(2,1)S(1)} %collective-permute-done.27.second), channel_id=1, source_target_pairs={{4,8},{5,9},{6,10},{7,11},{8,4},{9,5},{10,6},{11,7},{20,24},{21,25... | collective-permute-start | bytes 1179656 | tf_op jit(solution)/shard_map/ppermute | solution.py:506
  170.6 12.5 %collective-permute-start.32 = (bf16[192,1024]{1,0:T(8,128)(2,1)S(1)}, bf16[192,1024]{1,0:T(8,128)(2,1)S(1)}, u32[]{:S(2)}, u32[]{:S(2)}) collective-permute-start(bf16[192,1024]{1,0:T(8,128)(2,1)S(1)} %collective-permute-done.26), channel_id=1, source_target_pairs={{4,0},{5,1},{6,2},{7,3},{8,12},{9,13},{10,14},{11,15},{20,16},{21,... | collective-permute-start | bytes 1179656 | tf_op jit(solution)/shard_map/ppermute | solution.py:506
  178.7 8.0 %collective-permute-start.29 = (bf16[192,1024]{1,0:T(8,128)(2,1)S(1)}, bf16[192,1024]{1,0:T(8,128)(2,1)}, u32[]{:S(2)}, u32[]{:S(2)}) collective-permute-start(bf16[192,1024]{1,0:T(8,128)(2,1)S(1)} %collective-permute-done.28), channel_id=1, source_target_pairs={{4,0},{5,1},{6,2},{7,3},{8,12},{9,13},{10,14},{11,15},{20,16},{21,... | collective-permute-start | bytes 1179656 | tf_op jit(solution)/shard_map/ppermute | solution.py:506
  180.8 10.0 %collective-permute-start.35 = (bf16[192,1024]{1,0:T(8,128)(2,1)S(1)}, bf16[192,1024]{1,0:T(8,128)(2,1)S(1)}, u32[]{:S(2)}, u32[]{:S(2)}) collective-permute-start(bf16[192,1024]{1,0:T(8,128)(2,1)S(1)} %bitcast.67), channel_id=1, source_target_pairs={{0,2},{1,3},{2,0},{3,1},{4,6},{5,7},{6,4},{7,5},{8,10},{9,11},{10,... | collective-permute-start | bytes 1179656 | tf_op jit(solution)/shard_map/ppermute | solution.py:222
  181.7 5.2 %copy-start.25 = (bf16[1,192,1024]{2,1,0:T(8,128)(2,1)S(1)}, bf16[1,192,1024]{2,1,0:T(8,128)(2,1)}, u32[]{:S(2)}) copy-start(bf16[1,192,1024]{2,1,0:T(8,128)(2,1)} %stack_reshape.3) | copy-start | bytes 1179652
  181.7 15.6 %collective-permute-start.36 = (bf16[192,1024]{1,0:T(8,128)(2,1)S(1)}, bf16[192,1024]{1,0:T(8,128)(2,1)S(1)}, u32[]{:S(2)}, u32[]{:S(2)}) collective-permute-start(bf16[192,1024]{1,0:T(8,128)(2,1)S(1)} %collective-permute-done.27.second), channel_id=1, source_target_pairs={{0,2},{1,3},{2,0},{3,1},{4,6},{5,7},{6,4},{7,5},{8,10},{9,11},{10,... | collective-permute-start | bytes 1179656 | tf_op jit(solution)/shard_map/ppermute | solution.py:222
  183.2 22.5 %collective-permute-start.33 = (bf16[192,1024]{1,0:T(8,128)(2,1)S(1)}, bf16[192,1024]{1,0:T(8,128)(2,1)S(1)}, u32[]{:S(2)}, u32[]{:S(2)}) collective-permute-start(bf16[192,1024]{1,0:T(8,128)(2,1)S(1)} %broadcast_select_fusion.first), channel_id=1, source_target_pairs={{0,2},{1,3},{2,0},{3,1},{4,6},{5,7},{6,4},{7,5},{8,10},{9,11},{10,... | collective-permute-start | bytes 1179656 | tf_op jit(solution)/shard_map/ppermute | solution.py:222
  186.8 27.3 %collective-permute-start.30 = (bf16[192,1024]{1,0:T(8,128)(2,1)S(1)}, bf16[192,1024]{1,0:T(8,128)(2,1)S(1)}, u32[]{:S(2)}, u32[]{:S(2)}) collective-permute-start(bf16[192,1024]{1,0:T(8,128)(2,1)S(1)} %broadcast_select_fusion.1.first), channel_id=1, source_target_pairs={{0,2},{1,3},{2,0},{3,1},{4,6},{5,7},{6,4},{7,5},{8,10},{9,11},{10,... | collective-permute-start | bytes 1179656 | tf_op jit(solution)/shard_map/ppermute | solution.py:222
  187.8 31.0 %collective-permute-start.38 = (bf16[2,192,1024]{2,1,0:T(8,128)(2,1)}, bf16[2,192,1024]{2,1,0:T(8,128)(2,1)}, u32[]{:S(2)}, u32[]{:S(2)}) collective-permute-start(bf16[2,192,1024]{2,1,0:T(8,128)(2,1)} %pad_maximum_fusion.3), channel_id=1, source_target_pairs={{0,1},{1,0},{2,3},{3,2},{4,5},{5,4},{6,7},{7,6},{8,9},{9,8},{10,11... | collective-permute-start | bytes 2359304 | tf_op jit(solution)/shard_map/ppermute | solution.py:222
  198.2 27.3 %collective-permute-start.37 = (bf16[2,192,1024]{2,1,0:T(8,128)(2,1)}, bf16[2,192,1024]{2,1,0:T(8,128)(2,1)}, u32[]{:S(2)}, u32[]{:S(2)}) collective-permute-start(bf16[2,192,1024]{2,1,0:T(8,128)(2,1)} %pad_maximum_fusion.2), channel_id=1, source_target_pairs={{0,1},{1,0},{2,3},{3,2},{4,5},{5,4},{6,7},{7,6},{8,9},{9,8},{10,11... | collective-permute-start | bytes 2359304 | tf_op jit(solution)/shard_map/ppermute | solution.py:222
  205.7 13.2 %copy-start.7 = (bf16[2,96,1024]{2,1,0:T(8,128)(2,1)S(1)}, bf16[2,96,1024]{2,1,0:T(8,128)(2,1)}, u32[]{:S(2)}) copy-start(bf16[2,96,1024]{2,1,0:T(8,128)(2,1)} %param.8) | copy-start | bytes 1179652
  206.6 25.3 %collective-permute-start.34 = (bf16[2,192,1024]{2,1,0:T(8,128)(2,1)}, bf16[2,192,1024]{2,1,0:T(8,128)(2,1)}, u32[]{:S(2)}, u32[]{:S(2)}) collective-permute-start(bf16[2,192,1024]{2,1,0:T(8,128)(2,1)} %pad_maximum_fusion.1), channel_id=1, source_target_pairs={{0,1},{1,0},{2,3},{3,2},{4,5},{5,4},{6,7},{7,6},{8,9},{9,8},{10,11... | collective-permute-start | bytes 2359304 | tf_op jit(solution)/shard_map/ppermute | solution.py:222
  215.1 23.3 %collective-permute-start.31 = (bf16[2,192,1024]{2,1,0:T(8,128)(2,1)}, bf16[2,192,1024]{2,1,0:T(8,128)(2,1)}, u32[]{:S(2)}, u32[]{:S(2)}) collective-permute-start(bf16[2,192,1024]{2,1,0:T(8,128)(2,1)} %pad_maximum_fusion), channel_id=1, source_target_pairs={{0,1},{1,0},{2,3},{3,2},{4,5},{5,4},{6,7},{7,6},{8,9},{9,8},{10,11... | collective-permute-start | bytes 2359304 | tf_op jit(solution)/shard_map/ppermute | solution.py:222
  (3 other events, 2.3 us)

commit v4 on v3

--- a/solution.py
+++ b/solution.py
@@ -222,6 +222,23 @@
     return lax.ppermute(value, "tensor", [(i, i ^ bit) for i in range(devices)])
 
 
+def no_work(*refs):
+    del refs
+
+
+def together(*arrays):
+    anywhere = pl.BlockSpec(memory_space=pl.ANY)
+    return pl.pallas_call(
+        no_work,
+        in_specs=[anywhere] * len(arrays),
+        out_specs=[anywhere] * len(arrays),
+        out_shape=[jax.ShapeDtypeStruct(a.shape, a.dtype) for a in arrays],
+        input_output_aliases={i: i for i in range(len(arrays))},
+        cost_estimate=SHORT,
+        name="together",
+    )(*arrays)
+
+
 def coded_rows(rows):
     return rows + rows // PACKED
 
@@ -260,10 +277,6 @@
     codes, power = encode(block)
     sent[pl.ds(pl.multiple_of(index * rows, TILE), rows), :] = codes
 
-    @pl.when(index == 0)
-    def _():
-        powers[...] = jnp.zeros_like(powers)
-
     powers[pl.ds(index, 1), :] = power
 
     @pl.when(index == steps - 1)
@@ -274,6 +287,7 @@
 def project_kernel(chunk, with_pair, core, normed, weights, *refs):
     kept, sent, powers, wide, arrived = refs[-5:]
     index = pl.program_id(0)
+    columns = kept.shape[2]
 
     def copies(group):
         found = []
@@ -287,7 +301,7 @@
                 found.append(
                     pltpu.make_async_copy(
                         weights.at[:, pl.ds(pl.multiple_of(start, HD), size)],
-                        wide.at[group, side, :, pl.ds(offset, size)],
+                        wide.at[group, :, pl.ds(side * columns + offset, size)],
                         arrived.at[group, side, number],
                     )
                 )
@@ -298,15 +312,14 @@
         for group in range(KVH):
             for copy in copies(group):
                 copy.start()
+        powers[...] = jnp.zeros_like(powers)
 
     for copy in copies(index):
         copy.wait()
 
-    def product(side):
-        return jnp.dot(normed[...], wide[index, side], preferred_element_type=jnp.float32)
-
-    store_codes(sent, powers, product(1), index, KVH)
-    kept[0] = product(0)
+    product = jnp.dot(normed[...], wide[index], preferred_element_type=jnp.float32)
+    kept[0] = product[:, :columns]
+    store_codes(sent, powers, product[:, columns:], index, KVH)
 
 
 def project(core, normed, qkv_weight, chunk, with_pair, after):
@@ -326,7 +339,7 @@
             ],
             scratch_shapes=[
                 pltpu.VMEM((TILE, columns), jnp.float32),
-                pltpu.VMEM((KVH, 2, width, columns), jnp.bfloat16),
+                pltpu.VMEM((KVH, width, 2 * columns), jnp.bfloat16),
                 pltpu.SemaphoreType.DMA((KVH, 2, 2)),
             ],
         ),
@@ -351,9 +364,13 @@
         codes = landed[pl.ds(place, rows), :]
         return held[side] + decode(codes, pick_row(rows_of_powers, 2 * index + side))
 
+    @pl.when(index == 0)
+    def _():
+        powers[...] = jnp.zeros_like(powers)
+
     mine = bit[0]
+    kept[0] = total(mine)
     store_codes(sent, powers, total(1 - mine), index, steps)
-    kept[0] = total(mine)
 
 
 def fold(bit, held, landed, after):
@@ -427,74 +444,59 @@
     )(core, held, landed, cosine, sine, *after)
 
 
-MIX_STEPS = 8
-
-
-def mix_kernel(places, first, second, others, weights, start, mixed, total, wide, arrived):
-    step = pl.program_id(0)
+def mix_kernel(count, places, *refs):
+    pieces = refs[:count]
+    weights, start, mixed, wide, arrived = refs[count:]
     depth = wide.shape[1]
-
-    def copy(part):
-        row = places[part // 2] * (2 * depth) + part % 2 * depth
-        return pltpu.make_async_copy(
-            weights.at[pl.ds(pl.multiple_of(row, depth), depth), :],
-            wide.at[part],
-            arrived.at[part],
-        )
-
-    @pl.when(step == 0)
-    def _():
-        for part in range(MIX_STEPS):
-            copy(part).start()
-        total[...] = start[...].astype(jnp.float32)
-
-    for part in range(MIX_STEPS):
-
-        @pl.when(step == part)
-        def _():
-            copy(part).wait()
-            piece = (first, second, others.at[0], others.at[1])[part // 2]
-            offset = part % 2 * depth
-            total[...] += jnp.dot(
-                piece[:, offset : offset + depth],
-                wide[part],
-                preferred_element_type=jnp.float32,
-            )
-
-    @pl.when(step == MIX_STEPS - 1)
-    def _():
-        mixed[...] = total[...].astype(mixed.dtype)
-
-
-def mix(places, first, second, others, out_weight, start, dtype):
-    rows, width = first.shape
+    columns = wide.shape[2] // 2
+    flat = []
+    for piece in pieces:
+        flat += [piece] if len(piece.shape) == 2 else [piece.at[i] for i in range(piece.shape[0])]
+    copies = [
+        pltpu.make_async_copy(
+            weights.at[pl.ds(pl.multiple_of(places[i] * depth, depth), depth), :],
+            wide.at[i],
+            arrived.at[i],
+        )
+        for i in range(len(flat))
+    ]
+    for copy in copies:
+        copy.start()
+    half = (len(flat) + 1) // 2
+    for first, last in ((0, half), (half, len(flat))):
+        for copy in copies[first:last]:
+            copy.wait()
+        source = start if first == 0 else mixed
+        for side in range(2):
+            span = pl.ds(side * columns, columns)
+            total = source[:, span].astype(jnp.float32)
+            for i in range(first, last):
+                total = total + jnp.dot(
+                    flat[i][...], wide[i, :, span], preferred_element_type=jnp.float32
+                )
+            mixed[:, span] = total.astype(mixed.dtype)
+
+
+def mix(places, pieces, out_weight, start, dtype):
     columns = out_weight.shape[1]
-    depth = width // 2
-    whole = pl.BlockSpec((rows, width), lambda i, p: (0, 0))
+    rows, width = pieces[0].shape[-2:]
+    count = sum(1 if len(p.shape) == 2 else p.shape[0] for p in pieces)
+    whole = pl.BlockSpec(memory_space=pltpu.VMEM)
     return pl.pallas_call(
-        mix_kernel,
-        grid_spec=pltpu.PrefetchScalarGridSpec(
-            num_scalar_prefetch=1,
-            grid=(MIX_STEPS,),
-            in_specs=[
-                whole,
-                whole,
-                pl.BlockSpec((2, rows, width), lambda i, p: (0, 0, 0)),
-                pl.BlockSpec(memory_space=pl.ANY),
-                pl.BlockSpec((rows, columns), lambda i, p: (0, 0)),
-            ],
-            out_specs=pl.BlockSpec((rows, columns), lambda i, p: (0, 0)),
-            scratch_shapes=[
-                pltpu.VMEM((rows, columns), jnp.float32),
-                pltpu.VMEM((MIX_STEPS, depth, columns), jnp.bfloat16),
-                pltpu.SemaphoreType.DMA((MIX_STEPS,)),
-            ],
-        ),
+        functools.partial(mix_kernel, len(pieces)),
+        in_specs=[pl.BlockSpec(memory_space=pltpu.SMEM)]
+        + [whole] * len(pieces)
+        + [pl.BlockSpec(memory_space=pl.ANY), whole],
+        out_specs=whole,
+        scratch_shapes=[
+            pltpu.VMEM((count, width, columns), jnp.bfloat16),
+            pltpu.SemaphoreType.DMA((count,)),
+        ],
         out_shape=jax.ShapeDtypeStruct((rows, columns), dtype),
         compiler_params=pltpu.CompilerParams(vmem_limit_bytes=VMEM_LIMIT),
         cost_estimate=SHORT,
         name="mix",
-    )(places, first, second, others, out_weight, start)
+    )(places, *pieces, out_weight, start)
 
 
 def along(value, pairs):
@@ -509,30 +511,39 @@
 def gather_and_mix(attention, out_weight, start, device):
     line = device // 4
     inner = (line == 1) | (line == 2)
+
+    def add(mixed, pieces, offsets, dtype=jnp.float32):
+        places = jnp.stack([device ^ offset for offset in offsets])
+        return mix(places, pieces, out_weight, mixed, dtype)
+
     near = swap(attention, 4)
     cross = along(attention, [(1, 2), (2, 1)])
     across = swap(attention, 2)
+    near, cross, across = together(near, cross, across)
+
     passed = along(cross, [(1, 0), (2, 3)])
     cross_near = along(near, [(1, 2), (2, 1)])
     across_near = swap(near, 2)
+    first = swap(jnp.stack([attention, near]), 1)
+    passed, cross_near, across_near, first = together(passed, cross_near, across_near, first)
+
     third = jnp.where(inner, cross_near, passed)
     last = along(cross_near, [(1, 0), (2, 3)])
     across_third = swap(third, 2)
+    second = swap(jnp.stack([across, across_near]), 1)
+    mixed = add(start, [attention, near, first], (0, 4, 1, 5))
+    last, across_third, second, mixed = together(last, across_third, second, mixed)
+
     fourth = jnp.where(inner, cross, last)
     across_fourth = swap(fourth, 2)
-    groups = [
-        (attention, near, 0, 4),
-        (across, across_near, 2, 6),
-        (third, across_third, 8, 10),
-        (fourth, across_fourth, 12, 14),
-    ]
-    mixed = start
-    for number, (one, two, x, y) in enumerate(groups):
-        others = swap(jnp.stack([one, two]), 1)
-        places = jnp.stack([device ^ x, device ^ y, device ^ x ^ 1, device ^ y ^ 1])
-        dtype = jnp.bfloat16 if number == len(groups) - 1 else jnp.float32
-        mixed = mix(places, one, two, others, out_weight, mixed, dtype)
-    return mixed
+    both = jnp.stack([third, across_third, fourth])
+    most = swap(both, 1)
+    mixed = add(mixed, [across, across_near, second], (2, 6, 3, 7))
+    across_fourth, most, mixed = together(across_fourth, most, mixed)
+
+    final = swap(across_fourth, 1)
+    mixed = add(mixed, [both, most], (8, 10, 12, 9, 11, 13))
+    return add(mixed, [across_fourth, final], (14, 15), jnp.bfloat16)
 
 
 def attend_kernel(

time: 247 us -> 236 us (0.955)
  the two profiles are of different devices: /device:TPU:13 before, /device:TPU:0 now
where the time goes in v4:
time: 236 us; the launch traced here: 235 us
  Pallas kernels  88.1 us (37%)
  waiting for transfers between devices  80.6 us (34%)
  starting transfers between devices  32.5 us (14%)
  local copies, waits for them, and re-layouts  19.3 us (8%)
  other arithmetic  13.2 us (6%)
    ppermute x35, waiting for transfers between devices, swap(): return lax.ppermute(value, 'tensor', [(i, i ^ bit) for i in range(devices)])  64 us
    pallas_call x4, Pallas kernels, project(): pl.pallas_call(functools.partial(project_kernel, chunk, with_pair), grid_...  27.7 us
    ppermute x35, starting transfers between devices, swap(): return lax.ppermute(value, 'tensor', [(i, i ^ bit) for i in range(devices)])  27.6 us
    pallas_call x12, Pallas kernels, fold(): pl.pallas_call(functools.partial(fold_kernel, steps), grid_spec=pltpu.Pre...  23.1 us
    pallas_call x4, Pallas kernels, mix(): pl.pallas_call(functools.partial(mix_kernel, len(pieces)), in_specs=[pl.B...  21.3 us
    ppermute x4, waiting for transfers between devices, along(): return lax.ppermute(value, 'tensor', table)  16.7 us
    unnamed x98, local copies, waits for them, and re-layouts  14.7 us
    pallas_call x1, Pallas kernels, attend(): pl.pallas_call(attend_kernel, in_specs=[pl.BlockSpec(memory_space=pltpu.S...  10.5 us
  transfers between devices with their start and end apart: 39, of which 20 were waited for; matrix products, arithmetic and copies ran while one was open for 4% of the time, Pallas kernels for 31%

profile of v4, /device:TPU:0, one launch (start us, length us, event | category | flops | bytes accessed | tf_op | source)
XLA Modules:
  0.0 234.7 jit_solution(1897460847879255370)
XLA Ops:
  0.0 1.2 fusion
  2.5 2.8 %collective-permute-start.1 = (f32[2,96]{1,0:T(2,128)S(1)}, f32[2,96]{1,0:T(2,128)S(1)}, u32[]{:S(2)}, u32[]{:S(2)}) collective-permute-start(f32[2,96]{1,0:T(2,128)S(1)} %add.138), channel_id=1, source_target_pairs={{0,2},{1,3},{2,0},{3,1},{4,6},{5,7},{6,4},{7,5},{8,10},{9,11},{10,... | collective-permute-start | bytes 2312 | tf_op jit(solution)/shard_map/ppermute | solution.py:222
  5.3 1.5 collective-permute-done.1
  6.9 2.1 collective-permute-start.2
  9.0 1.5 collective-permute-done.2
  10.5 3.0 %collective-permute-start.3 = (f32[2,96]{1,0:T(2,128)S(1)}, f32[2,96]{1,0:T(2,128)S(1)}, u32[]{:S(2)}, u32[]{:S(2)}) collective-permute-start(f32[2,96]{1,0:T(2,128)S(1)} %add.140), channel_id=1, source_target_pairs={{0,8},{1,9},{2,10},{3,11},{4,12},{5,13},{6,14},{7,15},{8,0},{9,1},... | collective-permute-start | bytes 2312 | tf_op jit(solution)/shard_map/ppermute | solution.py:222
  15.0 1.4 copy-done.5
  16.8 1.6 collective-permute-start.5
  18.6 7.8 %project.4 = (f32[8,192,384]{2,1,0:T(8,128)S(1)}, s16[1936,384]{1,0:T(8,128)(2,1)}) custom-call(s32[1]{0:T(128)} %bitcast.2.core, bf16[192,1024]{1,0:T(8,128)(2,1)S(1)} %bitcast.57, bf16[1024,18432]{1,0:T(8,128)(2,1)} %weights.7, bf16[4,400,256]{2,1,0:T(8,128)(2,1)S(1)} %get-tuple-element.59.refs_0_.kept), custom_call_target="tpu_custom_call" | custom-call | flops 1 | bytes 1 | tf_op jit(solution)/shard_map/project/pallas_call | solution.py:329
  26.6 6.9 %project.5 = (f32[8,192,256]{2,1,0:T(8,128)S(1)}, s16[1936,256]{1,0:T(8,128)(2,1)}) custom-call(s32[1]{0:T(128)} %bitcast.2.core, bf16[192,1024]{1,0:T(8,128)(2,1)S(1)} %bitcast.58, bf16[1024,18432]{1,0:T(8,128)(2,1)} %weights.7, f32[8,192,384]{2,1,0:T(8,128)S(1)} %get-tuple-element.60.refs_0_.held), custom_call_target="tpu_custom_call" | custom-call | flops 1 | bytes 1 | tf_op jit(solution)/shard_map/project/pallas_call | solution.py:329
  33.6 1.0 collective-permute-done.5.landed
  34.6 1.0 regroup.2
  35.7 6.6 %project.6 = (f32[8,192,256]{2,1,0:T(8,128)S(1)}, s16[1936,256]{1,0:T(8,128)(2,1)}) custom-call(s32[1]{0:T(128)} %bitcast.2.core, bf16[192,1024]{1,0:T(8,128)(2,1)S(1)} %bitcast.59, bf16[1024,18432]{1,0:T(8,128)(2,1)} %weights.7, bf16[4,400,256]{2,1,0:T(8,128)(2,1)S(1)} %get-tuple-element.64.refs_0_.kept), custom_call_target="tpu_custom_call" | custom-call | flops 1 | bytes 1 | tf_op jit(solution)/shard_map/project/pallas_call | solution.py:329
  42.4 1.6 collective-permute-start.8
  44.2 6.4 %project.7 = (f32[8,192,256]{2,1,0:T(8,128)S(1)}, s16[1936,256]{1,0:T(8,128)(2,1)}) custom-call(s32[1]{0:T(128)} %bitcast.2.core, bf16[192,1024]{1,0:T(8,128)(2,1)S(1)} %bitcast.60, bf16[1024,18432]{1,0:T(8,128)(2,1)} %weights.7, f32[8,192,256]{2,1,0:T(8,128)S(1)} %get-tuple-element.65.refs_0_.held), custom_call_target="tpu_custom_call" | custom-call | flops 1 | bytes 1 | tf_op jit(solution)/shard_map/project/pallas_call | solution.py:329
  51.5 4.4 %fold.12 = (f32[4,192,384]{2,1,0:T(8,128)S(1)}, s16[976,384]{1,0:T(8,128)(2,1)}) custom-call(s32[1]{0:T(128)} %bitcast.5.bit, f32[8,192,384]{2,1,0:T(8,128)} %copy-done, s16[1936,384]{1,0:T(8,128)(2,1)} %collective-permute-done.4.landed.landed_powers, s16[1936,384]{1,0:T(8,128)(2,1)} %collective-permute-done.4.landed.landed_powers, ...), custom_call_target="tpu_custom_call" | custom-call | flops 1 | bytes 1 | tf_op jit(solution)/shard_map/fold/pallas_call | solution.py:380
  55.9 1.5 collective-permute-start.6
  57.4 1.1 fusion.5
  58.6 3.4 %fold.13 = (f32[4,192,256]{2,1,0:T(8,128)S(1)}, s16[976,256]{1,0:T(8,128)(2,1)}) custom-call(s32[1]{0:T(128)} %bitcast.5.bit, f32[8,192,256]{2,1,0:T(8,128)S(1)} %copy-done.7, s16[1936,256]{1,0:T(8,128)(2,1)} %collective-permute-done.10.landed.landed_powers, s16[1936,256]{1,0:T(8,128)(2,1)} %collective-permute-done.10.landed.landed_powers, ...), custom_call_target="tpu_custom_call" | custom-call | flops 1 | bytes 1 | tf_op jit(solution)/shard_map/fold/pallas_call | solution.py:380
  62.0 2.9 %fold.14 = (f32[4,192,256]{2,1,0:T(8,128)S(1)}, s16[976,256]{1,0:T(8,128)(2,1)S(1)}) custom-call(s32[1]{0:T(128)} %bitcast.5.bit, f32[8,192,256]{2,1,0:T(8,128)S(1)} %get-tuple-element.65.refs_0_.held, s16[1936,256]{1,0:T(8,128)(2,1)} %collective-permute-done.9.landed.landed_powers, s16[1936,256]{1,0:T(8,128)(2,1)} %collective-permute-done.9.landed.landed_powers, ...), custom_call_target="tpu_custom_call" | custom-call | flops 1 | bytes 1 | tf_op jit(solution)/shard_map/fold/pallas_call | solution.py:380
  65.0 2.6 %regroup.3 = (bf16[4,400,256]{2,1,0:T(8,128)(2,1)S(1)}, bf16[4,400,256]{2,1,0:T(8,128)(2,1)}) custom-call(bf16[4,400,256]{2,1,0:T(8,128)(2,1)S(1)} %copy-done.21, bf16[4,400,256]{2,1,0:T(8,128)(2,1)} %collective-permute-done.8.landed, f32[4,192,256]{2,1,0:T(8,128)S(1)} %get-tuple-element.74.refs_0_.held), custom_call_target="tpu_custom_call" | custom-call | flops 1 | bytes 1 | tf_op jit(solution)/shard_map/regroup/pallas_call | solution.py:714
  68.5 1.6 collective-permute-start.15
  70.1 2.7 %fold.15 = (f32[4,192,256]{2,1,0:T(8,128)S(1)}, s16[976,256]{1,0:T(8,128)(2,1)S(1)}) custom-call(s32[1]{0:T(128)} %bitcast.5.bit, f32[8,192,256]{2,1,0:T(8,128)S(1)} %get-tuple-element.66.refs_0_.held, s16[1936,256]{1,0:T(8,128)(2,1)} %collective-permute-done.7.landed.landed_powers, s16[1936,256]{1,0:T(8,128)(2,1)} %collective-permute-done.7.landed.landed_powers, ...), custom_call_target="tpu_custom_call" | custom-call | flops 1 | bytes 1 | tf_op jit(solution)/shard_map/fold/pallas_call | solution.py:380
  72.9 2.9 %collective-permute-done.6.landed.landed_powers = s16[976,384]{1,0:T(8,128)(2,1)} collective-permute-done((s16[976,384]{1,0:T(8,128)(2,1)}, s16[976,384]{1,0:T(8,128)(2,1)}, u32[]{:S(2)}, u32[]{:S(2)}) %collective-permute-start.6) | collective-permute-done | bytes 749600 | tf_op jit(solution)/shard_map/ppermute | solution.py:222
  75.8 2.5 %fold.16 = (f32[2,192,384]{2,1,0:T(8,128)S(1)}, s16[496,384]{1,0:T(8,128)(2,1)}) custom-call(s32[1]{0:T(128)} %bitcast.4.bit, f32[4,192,384]{2,1,0:T(8,128)S(1)} %copy-done.11, s16[976,384]{1,0:T(8,128)(2,1)} %collective-permute-done.6.landed.landed_powers, s16[976,384]{1,0:T(8,128)(2,1)} %collective-permute-done.6.landed.landed_powers, ...), custom_call_target="tpu_custom_call" | custom-call | flops 1 | bytes 1 | tf_op jit(solution)/shard_map/fold/pallas_call | solution.py:380
  79.1 7.4 %collective-permute-done.12.landed.landed_powers = s16[976,256]{1,0:T(8,128)(2,1)} collective-permute-done((s16[976,256]{1,0:T(8,128)(2,1)}, s16[976,256]{1,0:T(8,128)(2,1)}, u32[]{:S(2)}, u32[]{:S(2)}) %collective-permute-start.12) | collective-permute-done | bytes 499744 | tf_op jit(solution)/shard_map/ppermute | solution.py:222
  86.5 1.5 collective-permute-start.18
  88.0 2.1 fold.17
  90.1 4.0 %collective-permute-done.11.landed.landed_powers = s16[496,384]{1,0:T(8,128)(2,1)} collective-permute-done((s16[496,384]{1,0:T(8,128)(2,1)}, s16[496,384]{1,0:T(8,128)(2,1)}, u32[]{:S(2)}, u32[]{:S(2)}) %collective-permute-start.11) | collective-permute-done | bytes 380960 | tf_op jit(solution)/shard_map/ppermute | solution.py:222
  94.2 2.5 %collective-permute-start.14 = (s16[496,256]{1,0:T(8,128)(2,1)}, s16[496,256]{1,0:T(8,128)(2,1)S(1)}, u32[]{:S(2)}, u32[]{:S(2)}) collective-permute-start(s16[496,256]{1,0:T(8,128)(2,1)} %get-tuple-element.83), channel_id=1, source_target_pairs={{0,4},{1,5},{2,6},{3,7},{4,0},{5,1},{6,2},{7,3},{8,12},{9,13},{10,... | collective-permute-start | bytes 761864 | tf_op jit(solution)/shard_map/ppermute | solution.py:222
  96.6 2.0 fold.18
  100.3 10.5 %collective-permute-done.23.own_far = bf16[4,400,256]{2,1,0:T(8,128)(2,1)} collective-permute-done((bf16[4,400,256]{2,1,0:T(8,128)(2,1)}, bf16[4,400,256]{2,1,0:T(8,128)(2,1)}, u32[]{:S(2)}, u32[]{:S(2)}) %collective-permute-start.23) | collective-permute-done | bytes 819232 | tf_op jit(solution)/shard_map/ppermute | solution.py:222
  110.9 1.2 pad_maximum_fusion.3
  113.1 1.1 fold.19
  114.3 1.7 collective-permute-done.14.landed.landed_powers
  116.9 1.1 finish.4
  118.6 2.1 collective-permute-start.20
  122.5 5.5 %collective-permute-done.17.landed.landed_powers = s16[496,256]{1,0:T(8,128)(2,1)S(1)} collective-permute-done((s16[496,256]{1,0:T(8,128)(2,1)}, s16[496,256]{1,0:T(8,128)(2,1)S(1)}, u32[]{:S(2)}, u32[]{:S(2)}) %collective-permute-start.17) | collective-permute-done | bytes 253984 | tf_op jit(solution)/shard_map/ppermute | solution.py:222
  128.9 2.2 collective-permute-done.16.landed
  131.2 2.1 collective-permute-done.20.landed.landed_powers
  133.5 1.4 collective-permute-start.22
  135.0 4.8 %collective-permute-done.19.landed = s16[256,256]{1,0:T(8,128)(2,1)S(1)} collective-permute-done((s16[256,256]{1,0:T(8,128)(2,1)}, s16[256,256]{1,0:T(8,128)(2,1)S(1)}, u32[]{:S(2)}, u32[]{:S(2)}) %collective-permute-start.19) | collective-permute-done | bytes 131104 | tf_op jit(solution)/shard_map/ppermute | solution.py:222
  140.0 1.8 collective-permute-done.22.landed
  143.7 10.5 %attend.1 = bf16[16,96,128]{2,1,0:T(8,128)(2,1)S(1)} custom-call(s32[24]{0:T(128)S(1)} %get-tuple-element.115.slot_request, bf16[16,96,128]{2,1,0:T(8,128)(2,1)S(1)} %bitcast.69, bf16[16,16,128]{2,1,0:T(8,128)(2,1)S(1)} %pad.12.new_keys, bf16[16,16,128]{2,1,0:T(8,128)(2,1)S(1)} %pad.13.new_values, ...), custom_call_target="tpu_custom_call" | custom-call | flops 1 | bytes 1 | tf_op jit(solution)/shard_map/attend/pallas_call | solution.py:634
  155.3 9.4 %collective-permute-done.26.refs_0_ = bf16[192,1024]{1,0:T(8,128)(2,1)S(1)} collective-permute-done((bf16[192,1024]{1,0:T(8,128)(2,1)S(1)}, bf16[192,1024]{1,0:T(8,128)(2,1)S(1)}, u32[]{:S(2)}, u32[]{:S(2)}) %collective-permute-start.26) | collective-permute-done | bytes 393248 | tf_op jit(solution)/shard_map/ppermute | solution.py:222
  166.3 1.2 pad_maximum_fusion.1
  167.6 1.3 collective-permute-start.29
  168.9 1.4 collective-permute-start.30
  170.5 11.8 %collective-permute-done.29.refs_0_ = bf16[192,1024]{1,0:T(8,128)(2,1)S(1)} collective-permute-done((bf16[192,1024]{1,0:T(8,128)(2,1)S(1)}, bf16[192,1024]{1,0:T(8,128)(2,1)S(1)}, u32[]{:S(2)}, u32[]{:S(2)}) %collective-permute-start.29) | collective-permute-done | bytes 393248 | tf_op jit(solution)/shard_map/ppermute | solution.py:508
  184.1 2.1 pad_maximum_fusion.2
  187.2 1.5 collective-permute-start.33
  188.8 5.0 %mix.4.refs_3_ = f32[192,1024]{1,0:T(8,128)S(1)} custom-call(s32[4]{0:T(128)S(1)} %pad_add_fusion.1.places, bf16[192,1024]{1,0:T(8,128)(2,1)S(1)} %bitcast.68, bf16[192,1024]{1,0:T(8,128)(2,1)S(1)} %copy-done.15, bf16[2,192,1024]{2,1,0:T(8,128)(2,1)S(1)} %copy-done.31, bf16[16384,1024]{1,0:T(8,128)(2,1)} %refs_2_.3, bf16[192,1024]{1,0:T(8,128)(2,1)S(1)} %bitcast.61), custom_call_target="tpu_custom_call" | custom-call | flops 1 | bytes 1 | tf_op jit(solution)/shard_map/mix/pallas_call | solution.py:485
  194.8 4.0 %collective-permute-done.34.refs_1_ = bf16[192,1024]{1,0:T(8,128)(2,1)} collective-permute-done((bf16[192,1024]{1,0:T(8,128)(2,1)}, bf16[192,1024]{1,0:T(8,128)(2,1)}, u32[]{:S(2)}, u32[]{:S(2)}) %collective-permute-start.34) | collective-permute-done | bytes 393248 | tf_op jit(solution)/shard_map/ppermute | solution.py:222
  198.8 4.8 %collective-permute-done.33.refs_0_ = bf16[192,1024]{1,0:T(8,128)(2,1)} collective-permute-done((bf16[192,1024]{1,0:T(8,128)(2,1)}, bf16[192,1024]{1,0:T(8,128)(2,1)}, u32[]{:S(2)}, u32[]{:S(2)}) %collective-permute-start.33) | collective-permute-done | bytes 393248 | tf_op jit(solution)/shard_map/ppermute | solution.py:508
  204.5 1.8 broadcast_select_fusion
  206.3 1.4 pad_maximum_fusion.refs_0_
  207.8 1.8 collective-permute-start.36
  210.7 1.1 copy-done.29
  211.8 5.0 %mix.5.refs_2_ = f32[192,1024]{1,0:T(8,128)S(1)} custom-call(s32[4]{0:T(128)S(1)} %pad_add_fusion.2.places, bf16[192,1024]{1,0:T(8,128)(2,1)S(1)} %copy-done.17, bf16[192,1024]{1,0:T(8,128)(2,1)S(1)} %copy-done.19, bf16[2,192,1024]{2,1,0:T(8,128)(2,1)S(1)} %copy-done.29, bf16[16384,1024]{1,0:T(8,128)(2,1)} %refs_2_.3, f32[192,1024]{1,0:T(8,128)S(1)} %copy-done.2), custom_call_target="tpu_custom_call" | custom-call | flops 1 | bytes 1 | tf_op jit(solution)/shard_map/mix/pallas_call | solution.py:485
  217.8 1.9 collective-permute-done.36.refs_0_
  220.9 1.1 copy-done.4
  222.0 1.3 copy-done.9
  223.3 6.7 %mix.6.refs_3_ = f32[192,1024]{1,0:T(8,128)S(1)} custom-call(s32[6]{0:T(128)S(1)} %stack.121.places, bf16[3,192,1024]{2,1,0:T(8,128)(2,1)S(1)} %pad_maximum_fusion.refs_0_, bf16[3,192,1024]{2,1,0:T(8,128)(2,1)S(1)} %copy-done.9, bf16[16384,1024]{1,0:T(8,128)(2,1)} %refs_2_.3, f32[192,1024]{1,0:T(8,128)S(1)} %copy-done.4), custom_call_target="tpu_custom_call" | custom-call | flops 1 | bytes 1 | tf_op jit(solution)/shard_map/mix/pallas_call | solution.py:485
  229.9 4.6 %mix.7 = bf16[192,1024]{1,0:T(8,128)(2,1)} custom-call(s32[2]{0:T(128)S(1)} %pad_add_fusion.places, bf16[192,1024]{1,0:T(8,128)(2,1)} %get-tuple-element.110.refs_0_, bf16[192,1024]{1,0:T(8,128)(2,1)S(1)} %collective-permute-done.38.refs_1_, bf16[16384,1024]{1,0:T(8,128)(2,1)} %refs_2_.3, f32[192,1024]{1,0:T(8,128)S(1)} %mix.6.refs_3_), custom_call_target="tpu_custom_call" | custom-call | flops 1 | bytes 1 | tf_op jit(solution)/shard_map/mix/pallas_call | solution.py:485
  (209 shorter events, 26.7 us)
Async XLA Ops:
  1.2 1.3 collective-permute-start
  2.5 4.4 %collective-permute-start.1 = (f32[2,96]{1,0:T(2,128)S(1)}, f32[2,96]{1,0:T(2,128)S(1)}, u32[]{:S(2)}, u32[]{:S(2)}) collective-permute-start(f32[2,96]{1,0:T(2,128)S(1)} %add.138), channel_id=1, source_target_pairs={{0,2},{1,3},{2,0},{3,1},{4,6},{5,7},{6,4},{7,5},{8,10},{9,11},{10,... | collective-permute-start | bytes 2312 | tf_op jit(solution)/shard_map/ppermute | solution.py:222
  6.9 3.6 %collective-permute-start.2 = (f32[2,96]{1,0:T(2,128)S(1)}, f32[2,96]{1,0:T(2,128)S(1)}, u32[]{:S(2)}, u32[]{:S(2)}) collective-permute-start(f32[2,96]{1,0:T(2,128)S(1)} %add.139.after), channel_id=1, source_target_pairs={{0,4},{1,5},{2,6},{3,7},{4,0},{5,1},{6,2},{7,3},{8,12},{9,13},{10,... | collective-permute-start | bytes 2312 | tf_op jit(solution)/shard_map/ppermute | solution.py:222
  10.5 7.9 %collective-permute-start.3 = (f32[2,96]{1,0:T(2,128)S(1)}, f32[2,96]{1,0:T(2,128)S(1)}, u32[]{:S(2)}, u32[]{:S(2)}) collective-permute-start(f32[2,96]{1,0:T(2,128)S(1)} %add.140), channel_id=1, source_target_pairs={{0,8},{1,9},{2,10},{3,11},{4,12},{5,13},{6,14},{7,15},{8,0},{9,1},... | collective-permute-start | bytes 2312 | tf_op jit(solution)/shard_map/ppermute | solution.py:222
  16.8 17.8 %collective-permute-start.5 = (bf16[4,400,256]{2,1,0:T(8,128)(2,1)S(1)}, bf16[4,400,256]{2,1,0:T(8,128)(2,1)S(1)}, u32[]{:S(2)}, u32[]{:S(2)}) collective-permute-start(bf16[4,400,256]{2,1,0:T(8,128)(2,1)S(1)} %get-tuple-element.62), channel_id=1, source_target_pairs={{0,2},{1,3},{2,0},{3,1},{4,6},{5,7},{6,4},{7,5},{8,10},{9,11},{10,... | collective-permute-start | bytes 2457608 | tf_op jit(solution)/shard_map/ppermute | solution.py:222
  18.6 7.9 %copy-start.47 = (s32[16]{0:T(128)S(1)}, s32[16]{0:T(128)}, u32[]{:S(2)}) copy-start(s32[16]{0:T(128)} %param.14) | copy-start | bytes 196
  26.4 7.1 %copy-start = (f32[8,192,384]{2,1,0:T(8,128)}, f32[8,192,384]{2,1,0:T(8,128)S(1)}, u32[]{:S(2)}) copy-start(f32[8,192,384]{2,1,0:T(8,128)S(1)} %get-tuple-element.60.refs_0_.held) | copy-start | bytes 7077892
  26.4 25.1 %collective-permute-start.4 = (s16[1936,384]{1,0:T(8,128)(2,1)}, s16[1936,384]{1,0:T(8,128)(2,1)}, u32[]{:S(2)}, u32[]{:S(2)}) collective-permute-start(s16[1936,384]{1,0:T(8,128)(2,1)} %get-tuple-element.61), channel_id=1, source_target_pairs={{0,1},{1,0},{2,3},{3,2},{4,5},{5,4},{6,7},{7,6},{8,9},{9,8},{10,11... | collective-permute-start | bytes 4460552 | tf_op jit(solution)/shard_map/ppermute | solution.py:222
  33.5 25.1 %collective-permute-start.10 = (s16[1936,256]{1,0:T(8,128)(2,1)}, s16[1936,256]{1,0:T(8,128)(2,1)}, u32[]{:S(2)}, u32[]{:S(2)}) collective-permute-start(s16[1936,256]{1,0:T(8,128)(2,1)} %get-tuple-element.72), channel_id=1, source_target_pairs={{0,1},{1,0},{2,3},{3,2},{4,5},{5,4},{6,7},{7,6},{8,9},{9,8},{10,11... | collective-permute-start | bytes 2973704 | tf_op jit(solution)/shard_map/ppermute | solution.py:222
  35.6 6.6 %copy-start.20 = (bf16[4,400,256]{2,1,0:T(8,128)(2,1)}, bf16[4,400,256]{2,1,0:T(8,128)(2,1)S(1)}, u32[]{:S(2)}) copy-start(bf16[4,400,256]{2,1,0:T(8,128)(2,1)S(1)} %get-tuple-element.64.refs_0_.kept) | copy-start | bytes 2457604
  42.3 19.7 %collective-permute-start.9 = (s16[1936,256]{1,0:T(8,128)(2,1)}, s16[1936,256]{1,0:T(8,128)(2,1)}, u32[]{:S(2)}, u32[]{:S(2)}) collective-permute-start(s16[1936,256]{1,0:T(8,128)(2,1)} %get-tuple-element.71), channel_id=1, source_target_pairs={{0,1},{1,0},{2,3},{3,2},{4,5},{5,4},{6,7},{7,6},{8,9},{9,8},{10,11... | collective-permute-start | bytes 2973704 | tf_op jit(solution)/shard_map/ppermute | solution.py:222
  42.4 22.6 %collective-permute-start.8 = (bf16[4,400,256]{2,1,0:T(8,128)(2,1)}, bf16[4,400,256]{2,1,0:T(8,128)(2,1)}, u32[]{:S(2)}, u32[]{:S(2)}) collective-permute-start(bf16[4,400,256]{2,1,0:T(8,128)(2,1)} %get-tuple-element.70), channel_id=1, source_target_pairs={{0,4},{1,5},{2,6},{3,7},{4,0},{5,1},{6,2},{7,3},{8,12},{9,13},{10,... | collective-permute-start | bytes 2457608 | tf_op jit(solution)/shard_map/ppermute | solution.py:222
  50.5 19.6 %collective-permute-start.7 = (s16[1936,256]{1,0:T(8,128)(2,1)}, s16[1936,256]{1,0:T(8,128)(2,1)}, u32[]{:S(2)}, u32[]{:S(2)}) collective-permute-start(s16[1936,256]{1,0:T(8,128)(2,1)} %get-tuple-element.69), channel_id=1, source_target_pairs={{0,1},{1,0},{2,3},{3,2},{4,5},{5,4},{6,7},{7,6},{8,9},{9,8},{10,11... | collective-permute-start | bytes 2973704 | tf_op jit(solution)/shard_map/ppermute | solution.py:222
  51.5 7.1 %copy-start.7 = (f32[8,192,256]{2,1,0:T(8,128)S(1)}, f32[8,192,256]{2,1,0:T(8,128)}, u32[]{:S(2)}) copy-start(f32[8,192,256]{2,1,0:T(8,128)} %copy-done.6) | copy-start | bytes 4718596
  55.9 6.1 %copy-start.10 = (f32[4,192,384]{2,1,0:T(8,128)}, f32[4,192,384]{2,1,0:T(8,128)S(1)}, u32[]{:S(2)}) copy-start(f32[4,192,384]{2,1,0:T(8,128)S(1)} %get-tuple-element.67.refs_0_.held) | copy-start | bytes 3538948
  55.9 19.9 %collective-permute-start.6 = (s16[976,384]{1,0:T(8,128)(2,1)}, s16[976,384]{1,0:T(8,128)(2,1)}, u32[]{:S(2)}, u32[]{:S(2)}) collective-permute-start(s16[976,384]{1,0:T(8,128)(2,1)} %get-tuple-element.68), channel_id=1, source_target_pairs={{0,2},{1,3},{2,0},{3,1},{4,6},{5,7},{6,4},{7,5},{8,10},{9,11},{10,... | collective-permute-start | bytes 2248712 | tf_op jit(solution)/shard_map/ppermute | solution.py:222
  62.0 3.0 %copy-start.22 = (f32[4,192,256]{2,1,0:T(8,128)}, f32[4,192,256]{2,1,0:T(8,128)S(1)}, u32[]{:S(2)}) copy-start(f32[4,192,256]{2,1,0:T(8,128)S(1)} %get-tuple-element.73.refs_0_.held) | copy-start | bytes 2359300
  62.0 3.0 %copy-start.21 = (bf16[4,400,256]{2,1,0:T(8,128)(2,1)S(1)}, bf16[4,400,256]{2,1,0:T(8,128)(2,1)}, u32[]{:S(2)}) copy-start(bf16[4,400,256]{2,1,0:T(8,128)(2,1)} %copy-done.20) | copy-start | bytes 2457604
  65.0 2.6 %copy-start.24 = (f32[4,192,256]{2,1,0:T(8,128)}, f32[4,192,256]{2,1,0:T(8,128)S(1)}, u32[]{:S(2)}) copy-start(f32[4,192,256]{2,1,0:T(8,128)S(1)} %get-tuple-element.74.refs_0_.held) | copy-start | bytes 2359300
  65.0 2.6 %copy-start.39 = (s16[976,256]{1,0:T(8,128)(2,1)}, s16[976,256]{1,0:T(8,128)(2,1)S(1)}, u32[]{:S(2)}) copy-start(s16[976,256]{1,0:T(8,128)(2,1)S(1)} %get-tuple-element.84) | copy-start | bytes 1499140
  67.6 43.3 %collective-permute-start.23 = (bf16[4,400,256]{2,1,0:T(8,128)(2,1)}, bf16[4,400,256]{2,1,0:T(8,128)(2,1)}, u32[]{:S(2)}, u32[]{:S(2)}) collective-permute-start(bf16[4,400,256]{2,1,0:T(8,128)(2,1)} %get-tuple-element.98), channel_id=1, source_target_pairs={{0,8},{1,9},{2,10},{3,11},{4,12},{5,13},{6,14},{7,15},{8,0},{9,1},... | collective-permute-start | bytes 2457608 | tf_op jit(solution)/shard_map/ppermute | solution.py:222
  68.0 18.5 %collective-permute-start.12 = (s16[976,256]{1,0:T(8,128)(2,1)}, s16[976,256]{1,0:T(8,128)(2,1)}, u32[]{:S(2)}, u32[]{:S(2)}) collective-permute-start(s16[976,256]{1,0:T(8,128)(2,1)} %get-tuple-element.79), channel_id=1, source_target_pairs={{0,2},{1,3},{2,0},{3,1},{4,6},{5,7},{6,4},{7,5},{8,10},{9,11},{10,... | collective-permute-start | bytes 1499144 | tf_op jit(solution)/shard_map/ppermute | solution.py:222
  68.5 30.8 %collective-permute-start.15 = (s16[976,256]{1,0:T(8,128)(2,1)}, s16[976,256]{1,0:T(8,128)(2,1)S(1)}, u32[]{:S(2)}, u32[]{:S(2)}) collective-permute-start(s16[976,256]{1,0:T(8,128)(2,1)} %copy-done.39), channel_id=1, source_target_pairs={{0,2},{1,3},{2,0},{3,1},{4,6},{5,7},{6,4},{7,5},{8,10},{9,11},{10,... | collective-permute-start | bytes 1499144 | tf_op jit(solution)/shard_map/ppermute | solution.py:222
  70.1 5.7 %copy-start.11 = (f32[4,192,384]{2,1,0:T(8,128)S(1)}, f32[4,192,384]{2,1,0:T(8,128)}, u32[]{:S(2)}) copy-start(f32[4,192,384]{2,1,0:T(8,128)} %copy-done.10) | copy-start | bytes 3538948
  72.8 3.0 %copy-start.38 = (s16[976,256]{1,0:T(8,128)(2,1)}, s16[976,256]{1,0:T(8,128)(2,1)S(1)}, u32[]{:S(2)}) copy-start(s16[976,256]{1,0:T(8,128)(2,1)S(1)} %get-tuple-element.90) | copy-start | bytes 1499140
  72.9 5.5 %copy-start.26 = (f32[4,192,256]{2,1,0:T(8,128)}, f32[4,192,256]{2,1,0:T(8,128)S(1)}, u32[]{:S(2)}) copy-start(f32[4,192,256]{2,1,0:T(8,128)S(1)} %get-tuple-element.76.refs_0_.held) | copy-start | bytes 2359300
  75.8 3.1 %copy-start.46 = (s32[16,16]{1,0:T(8,128)S(1)}, s32[16,16]{1,0:T(8,128)}, u32[]{:S(2)}) copy-start(s32[16,16]{1,0:T(8,128)} %param.15) | copy-start | bytes 3076
  75.8 12.2 %copy-start.23 = (f32[4,192,256]{2,1,0:T(8,128)S(1)}, f32[4,192,256]{2,1,0:T(8,128)}, u32[]{:S(2)}) copy-start(f32[4,192,256]{2,1,0:T(8,128)} %copy-done.22) | copy-start | bytes 2359300
  78.3 15.8 %collective-permute-start.11 = (s16[496,384]{1,0:T(8,128)(2,1)}, s16[496,384]{1,0:T(8,128)(2,1)}, u32[]{:S(2)}, u32[]{:S(2)}) collective-permute-start(s16[496,384]{1,0:T(8,128)(2,1)} %get-tuple-element.78), channel_id=1, source_target_pairs={{0,4},{1,5},{2,6},{3,7},{4,0},{5,1},{6,2},{7,3},{8,12},{9,13},{10,... | collective-permute-start | bytes 1142792 | tf_op jit(solution)/shard_map/ppermute | solution.py:222
  78.9 42.7 %collective-permute-start.24 = (bf16[4,400,256]{2,1,0:T(8,128)(2,1)S(1)}, bf16[4,400,256]{2,1,0:T(8,128)(2,1)}, u32[]{:S(2)}, u32[]{:S(2)}) collective-permute-start(bf16[4,400,256]{2,1,0:T(8,128)(2,1)S(1)} %get-tuple-element.75.refs_0_.own_near), channel_id=1, source_target_pairs={{0,1},{1,0},{2,3},{3,2},{4,5},{5,4},{6,7},{7,6},{8,9},{9,8},{10,11... | collective-permute-start | bytes 2457608 | tf_op jit(solution)/shard_map/ppermute | solution.py:222
  86.5 31.4 %collective-permute-start.18 = (s16[976,256]{1,0:T(8,128)(2,1)}, s16[976,256]{1,0:T(8,128)(2,1)S(1)}, u32[]{:S(2)}, u32[]{:S(2)}) collective-permute-start(s16[976,256]{1,0:T(8,128)(2,1)} %copy-done.38), channel_id=1, source_target_pairs={{0,2},{1,3},{2,0},{3,1},{4,6},{5,7},{6,4},{7,5},{8,10},{9,11},{10,... | collective-permute-start | bytes 1499144 | tf_op jit(solution)/shard_map/ppermute | solution.py:222
  90.1 9.2 %copy-start.32 = (f32[2,192,256]{2,1,0:T(8,128)}, f32[2,192,256]{2,1,0:T(8,128)S(1)}, u32[]{:S(2)}) copy-start(f32[2,192,256]{2,1,0:T(8,128)S(1)} %get-tuple-element.80.refs_0_.held) | copy-start | bytes 1179652
  90.1 22.0 %copy-start.25 = (f32[4,192,256]{2,1,0:T(8,128)S(1)}, f32[4,192,256]{2,1,0:T(8,128)}, u32[]{:S(2)}) copy-start(f32[4,192,256]{2,1,0:T(8,128)} %copy-done.24) | copy-start | bytes 2359300
  94.2 21.8 %collective-permute-start.14 = (s16[496,256]{1,0:T(8,128)(2,1)}, s16[496,256]{1,0:T(8,128)(2,1)S(1)}, u32[]{:S(2)}, u32[]{:S(2)}) collective-permute-start(s16[496,256]{1,0:T(8,128)(2,1)} %get-tuple-element.83), channel_id=1, source_target_pairs={{0,4},{1,5},{2,6},{3,7},{4,0},{5,1},{6,2},{7,3},{8,12},{9,13},{10,... | collective-permute-start | bytes 761864 | tf_op jit(solution)/shard_map/ppermute | solution.py:222
  99.3 16.9 %collective-permute-start.13 = (s16[256,384]{1,0:T(8,128)(2,1)}, s16[256,384]{1,0:T(8,128)(2,1)}, u32[]{:S(2)}, u32[]{:S(2)}) collective-permute-start(s16[256,384]{1,0:T(8,128)(2,1)} %get-tuple-element.82), channel_id=1, source_target_pairs={{0,8},{1,9},{2,10},{3,11},{4,12},{5,13},{6,14},{7,15},{8,0},{9,1},... | collective-permute-start | bytes 589832 | tf_op jit(solution)/shard_map/ppermute | solution.py:222
  110.9 31.3 %collective-permute-start.25 = (bf16[4,400,256]{2,1,0:T(8,128)(2,1)}, bf16[4,400,256]{2,1,0:T(8,128)(2,1)}, u32[]{:S(2)}, u32[]{:S(2)}) collective-permute-start(bf16[4,400,256]{2,1,0:T(8,128)(2,1)} %collective-permute-done.23.own_far), channel_id=1, source_target_pairs={{0,1},{1,0},{2,3},{3,2},{4,5},{5,4},{6,7},{7,6},{8,9},{9,8},{10,11... | collective-permute-start | bytes 2457608 | tf_op jit(solution)/shard_map/ppermute | solution.py:222
  110.9 5.0 %copy-start.33 = (f32[2,192,256]{2,1,0:T(8,128)S(1)}, f32[2,192,256]{2,1,0:T(8,128)}, u32[]{:S(2)}) copy-start(f32[2,192,256]{2,1,0:T(8,128)} %copy-done.32) | copy-start | bytes 1179652
  113.1 3.7 %copy-start.36 = (f32[1,192,384]{2,1,0:T(8,128)S(1)}, f32[1,192,384]{2,1,0:T(8,128)}, u32[]{:S(2)}) copy-start(f32[1,192,384]{2,1,0:T(8,128)} %copy-done.34) | copy-start | bytes 884740
  114.3 3.7 %copy-start.27 = (f32[4,192,256]{2,1,0:T(8,128)S(1)}, f32[4,192,256]{2,1,0:T(8,128)}, u32[]{:S(2)}) copy-start(f32[4,192,256]{2,1,0:T(8,128)} %copy-done.26) | copy-start | bytes 2359300
  116.0 12.0 %collective-permute-start.17 = (s16[496,256]{1,0:T(8,128)(2,1)}, s16[496,256]{1,0:T(8,128)(2,1)S(1)}, u32[]{:S(2)}, u32[]{:S(2)}) collective-permute-start(s16[496,256]{1,0:T(8,128)(2,1)} %get-tuple-element.89), channel_id=1, source_target_pairs={{0,4},{1,5},{2,6},{3,7},{4,0},{5,1},{6,2},{7,3},{8,12},{9,13},{10,... | collective-permute-start | bytes 761864 | tf_op jit(solution)/shard_map/ppermute | solution.py:222
  118.6 14.6 %collective-permute-start.20 = (s16[496,256]{1,0:T(8,128)(2,1)S(1)}, s16[496,256]{1,0:T(8,128)(2,1)S(1)}, u32[]{:S(2)}, u32[]{:S(2)}) collective-permute-start(s16[496,256]{1,0:T(8,128)(2,1)S(1)} %get-tuple-element.94), channel_id=1, source_target_pairs={{0,4},{1,5},{2,6},{3,7},{4,0},{5,1},{6,2},{7,3},{8,12},{9,13},{10,... | collective-permute-start | bytes 761864 | tf_op jit(solution)/shard_map/ppermute | solution.py:222
  120.8 10.2 %collective-permute-start.16 = (s16[256,256]{1,0:T(8,128)(2,1)}, s16[256,256]{1,0:T(8,128)(2,1)S(1)}, u32[]{:S(2)}, u32[]{:S(2)}) collective-permute-start(s16[256,256]{1,0:T(8,128)(2,1)} %copy-done.40), channel_id=1, source_target_pairs={{0,8},{1,9},{2,10},{3,11},{4,12},{5,13},{6,14},{7,15},{8,0},{9,1},... | collective-permute-start | bytes 393224 | tf_op jit(solution)/shard_map/ppermute | solution.py:222
  121.6 9.6 %collective-permute-start.21 = (bf16[192,128]{1,0:T(8,128)(2,1)S(1)}, bf16[192,128]{1,0:T(8,128)(2,1)S(1)}, u32[]{:S(2)}, u32[]{:S(2)}) collective-permute-start(bf16[192,128]{1,0:T(8,128)(2,1)S(1)} %get-tuple-element.95), channel_id=1, source_target_pairs={{0,1},{1,0},{2,3},{3,2},{4,5},{5,4},{6,7},{7,6},{8,9},{9,8},{10,11... | collective-permute-start | bytes 147464 | tf_op jit(solution)/shard_map/ppermute | solution.py:222
  128.9 11.0 %collective-permute-start.19 = (s16[256,256]{1,0:T(8,128)(2,1)}, s16[256,256]{1,0:T(8,128)(2,1)S(1)}, u32[]{:S(2)}, u32[]{:S(2)}) collective-permute-start(s16[256,256]{1,0:T(8,128)(2,1)} %get-tuple-element.93), channel_id=1, source_target_pairs={{0,8},{1,9},{2,10},{3,11},{4,12},{5,13},{6,14},{7,15},{8,0},{9,1},... | collective-permute-start | bytes 393224 | tf_op jit(solution)/shard_map/ppermute | solution.py:222
  133.5 8.4 %collective-permute-start.22 = (s16[256,256]{1,0:T(8,128)(2,1)S(1)}, s16[256,256]{1,0:T(8,128)(2,1)S(1)}, u32[]{:S(2)}, u32[]{:S(2)}) collective-permute-start(s16[256,256]{1,0:T(8,128)(2,1)S(1)} %get-tuple-element.97), channel_id=1, source_target_pairs={{0,8},{1,9},{2,10},{3,11},{4,12},{5,13},{6,14},{7,15},{8,0},{9,1},... | collective-permute-start | bytes 393224 | tf_op jit(solution)/shard_map/ppermute | solution.py:222
  154.3 10.4 %collective-permute-start.26 = (bf16[192,1024]{1,0:T(8,128)(2,1)S(1)}, bf16[192,1024]{1,0:T(8,128)(2,1)S(1)}, u32[]{:S(2)}, u32[]{:S(2)}) collective-permute-start(bf16[192,1024]{1,0:T(8,128)(2,1)S(1)} %bitcast.65), channel_id=1, source_target_pairs={{0,4},{1,5},{2,6},{3,7},{4,0},{5,1},{6,2},{7,3},{8,12},{9,13},{10,... | collective-permute-start | bytes 1179656 | tf_op jit(solution)/shard_map/ppermute | solution.py:222
  154.4 10.3 %collective-permute-start.27 = (bf16[192,1024]{1,0:T(8,128)(2,1)S(1)}, bf16[192,1024]{1,0:T(8,128)(2,1)S(1)}, u32[]{:S(2)}, u32[]{:S(2)}) collective-permute-start(bf16[192,1024]{1,0:T(8,128)(2,1)S(1)} %bitcast.66), channel_id=1, source_target_pairs={{4,8},{5,9},{6,10},{7,11},{8,4},{9,5},{10,6},{11,7},{20,24},{21,25... | collective-permute-start | bytes 1179656 | tf_op jit(solution)/shard_map/ppermute | solution.py:508
  155.1 10.4 %collective-permute-start.28 = (bf16[192,1024]{1,0:T(8,128)(2,1)S(1)}, bf16[192,1024]{1,0:T(8,128)(2,1)S(1)}, u32[]{:S(2)}, u32[]{:S(2)}) collective-permute-start(bf16[192,1024]{1,0:T(8,128)(2,1)S(1)} %bitcast.67), channel_id=1, source_target_pairs={{0,2},{1,3},{2,0},{3,1},{4,6},{5,7},{6,4},{7,5},{8,10},{9,11},{10,... | collective-permute-start | bytes 1179656 | tf_op jit(solution)/shard_map/ppermute | solution.py:222
  166.3 2.6 %copy-start.15 = (bf16[192,1024]{1,0:T(8,128)(2,1)S(1)}, bf16[192,1024]{1,0:T(8,128)(2,1)}, u32[]{:S(2)}) copy-start(bf16[192,1024]{1,0:T(8,128)(2,1)} %get-tuple-element.100.refs_1_) | copy-start | bytes 1179652
  166.3 17.8 %copy-start.17 = (bf16[192,1024]{1,0:T(8,128)(2,1)S(1)}, bf16[192,1024]{1,0:T(8,128)(2,1)}, u32[]{:S(2)}) copy-start(bf16[192,1024]{1,0:T(8,128)(2,1)} %get-tuple-element.103.refs_0_) | copy-start | bytes 1179652
  167.5 14.9 %collective-permute-start.32 = (bf16[2,192,1024]{2,1,0:T(8,128)(2,1)S(1)}, bf16[2,192,1024]{2,1,0:T(8,128)(2,1)S(1)}, u32[]{:S(2)}, u32[]{:S(2)}) collective-permute-start(bf16[2,192,1024]{2,1,0:T(8,128)(2,1)S(1)} %pad_maximum_fusion.1), channel_id=1, source_target_pairs={{0,1},{1,0},{2,3},{3,2},{4,5},{5,4},{6,7},{7,6},{8,9},{9,8},{10,11... | collective-permute-start | bytes 2359304 | tf_op jit(solution)/shard_map/ppermute | solution.py:222
  167.6 14.7 %collective-permute-start.29 = (bf16[192,1024]{1,0:T(8,128)(2,1)S(1)}, bf16[192,1024]{1,0:T(8,128)(2,1)S(1)}, u32[]{:S(2)}, u32[]{:S(2)}) collective-permute-start(bf16[192,1024]{1,0:T(8,128)(2,1)S(1)} %copy-done.42), channel_id=1, source_target_pairs={{4,0},{5,1},{6,2},{7,3},{8,12},{9,13},{10,14},{11,15},{20,16},{21,... | collective-permute-start | bytes 1179656 | tf_op jit(solution)/shard_map/ppermute | solution.py:508
  168.9 13.4 %collective-permute-start.30 = (bf16[192,1024]{1,0:T(8,128)(2,1)S(1)}, bf16[192,1024]{1,0:T(8,128)(2,1)}, u32[]{:S(2)}, u32[]{:S(2)}) collective-permute-start(bf16[192,1024]{1,0:T(8,128)(2,1)S(1)} %copy-done.15), channel_id=1, source_target_pairs={{4,8},{5,9},{6,10},{7,11},{8,4},{9,5},{10,6},{11,7},{20,24},{21,25... | collective-permute-start | bytes 1179656 | tf_op jit(solution)/shard_map/ppermute | solution.py:508
  170.3 12.0 %collective-permute-start.31 = (bf16[192,1024]{1,0:T(8,128)(2,1)S(1)}, bf16[192,1024]{1,0:T(8,128)(2,1)S(1)}, u32[]{:S(2)}, u32[]{:S(2)}) collective-permute-start(bf16[192,1024]{1,0:T(8,128)(2,1)S(1)} %copy-done.15), channel_id=1, source_target_pairs={{0,2},{1,3},{2,0},{3,1},{4,6},{5,7},{6,4},{7,5},{8,10},{9,11},{10,... | collective-permute-start | bytes 1179656 | tf_op jit(solution)/shard_map/ppermute | solution.py:222
  184.1 4.8 %copy-start.13 = (bf16[2,96,1024]{2,1,0:T(8,128)(2,1)S(1)}, bf16[2,96,1024]{2,1,0:T(8,128)(2,1)}, u32[]{:S(2)}) copy-start(bf16[2,96,1024]{2,1,0:T(8,128)(2,1)} %param.8) | copy-start | bytes 1179652
  184.1 4.8 %copy-start.31 = (bf16[2,192,1024]{2,1,0:T(8,128)(2,1)S(1)}, bf16[2,192,1024]{2,1,0:T(8,128)(2,1)}, u32[]{:S(2)}) copy-start(bf16[2,192,1024]{2,1,0:T(8,128)(2,1)} %get-tuple-element.105.refs_2_) | copy-start | bytes 2359300
  186.1 17.5 %collective-permute-start.35 = (bf16[2,192,1024]{2,1,0:T(8,128)(2,1)}, bf16[2,192,1024]{2,1,0:T(8,128)(2,1)S(1)}, u32[]{:S(2)}, u32[]{:S(2)}) collective-permute-start(bf16[2,192,1024]{2,1,0:T(8,128)(2,1)} %pad_maximum_fusion.2), channel_id=1, source_target_pairs={{0,1},{1,0},{2,3},{3,2},{4,5},{5,4},{6,7},{7,6},{8,9},{9,8},{10,11... | collective-permute-start | bytes 2359304 | tf_op jit(solution)/shard_map/ppermute | solution.py:222
  186.9 11.8 %collective-permute-start.34 = (bf16[192,1024]{1,0:T(8,128)(2,1)}, bf16[192,1024]{1,0:T(8,128)(2,1)}, u32[]{:S(2)}, u32[]{:S(2)}) collective-permute-start(bf16[192,1024]{1,0:T(8,128)(2,1)} %broadcast_select_fusion.1), channel_id=1, source_target_pairs={{0,2},{1,3},{2,0},{3,1},{4,6},{5,7},{6,4},{7,5},{8,10},{9,11},{10,... | collective-permute-start | bytes 1179656 | tf_op jit(solution)/shard_map/ppermute | solution.py:222
  187.2 16.4 %collective-permute-start.33 = (bf16[192,1024]{1,0:T(8,128)(2,1)}, bf16[192,1024]{1,0:T(8,128)(2,1)}, u32[]{:S(2)}, u32[]{:S(2)}) collective-permute-start(bf16[192,1024]{1,0:T(8,128)(2,1)} %get-tuple-element.101), channel_id=1, source_target_pairs={{4,0},{5,1},{6,2},{7,3},{8,12},{9,13},{10,14},{11,15},{20,16},{21,... | collective-permute-start | bytes 1179656 | tf_op jit(solution)/shard_map/ppermute | solution.py:508
  194.8 9.7 %copy-start.43 = (bf16[192,1024]{1,0:T(8,128)(2,1)S(1)}, bf16[192,1024]{1,0:T(8,128)(2,1)}, u32[]{:S(2)}) copy-start(bf16[192,1024]{1,0:T(8,128)(2,1)} %get-tuple-element.99) | copy-start | bytes 1179652
  206.3 3.4 %copy-start.2 = (f32[192,1024]{1,0:T(8,128)S(1)}, f32[192,1024]{1,0:T(8,128)}, u32[]{:S(2)}) copy-start(f32[192,1024]{1,0:T(8,128)} %get-tuple-element.109.refs_4_) | copy-start | bytes 2359300
  207.7 11.9 %collective-permute-start.37 = (bf16[3,192,1024]{2,1,0:T(8,128)(2,1)S(1)}, bf16[3,192,1024]{2,1,0:T(8,128)(2,1)S(1)}, u32[]{:S(2)}, u32[]{:S(2)}) collective-permute-start(bf16[3,192,1024]{2,1,0:T(8,128)(2,1)S(1)} %pad_maximum_fusion.refs_0_), channel_id=1, source_target_pairs={{0,1},{1,0},{2,3},{3,2},{4,5},{5,4},{6,7},{7,6},{8,9},{9,8},{10,11... | collective-permute-start | bytes 3538952 | tf_op jit(solution)/shard_map/ppermute | solution.py:222
  207.8 11.8 %collective-permute-start.36 = (bf16[192,1024]{1,0:T(8,128)(2,1)}, bf16[192,1024]{1,0:T(8,128)(2,1)}, u32[]{:S(2)}, u32[]{:S(2)}) collective-permute-start(bf16[192,1024]{1,0:T(8,128)(2,1)} %broadcast_select_fusion), channel_id=1, source_target_pairs={{0,2},{1,3},{2,0},{3,1},{4,6},{5,7},{6,4},{7,5},{8,10},{9,11},{10,... | collective-permute-start | bytes 1179656 | tf_op jit(solution)/shard_map/ppermute | solution.py:222
  220.7 9.2 %collective-permute-start.38 = (bf16[192,1024]{1,0:T(8,128)(2,1)}, bf16[192,1024]{1,0:T(8,128)(2,1)S(1)}, u32[]{:S(2)}, u32[]{:S(2)}) collective-permute-start(bf16[192,1024]{1,0:T(8,128)(2,1)} %get-tuple-element.110.refs_0_), channel_id=1, source_target_pairs={{0,1},{1,0},{2,3},{3,2},{4,5},{5,4},{6,7},{7,6},{8,9},{9,8},{10,11... | collective-permute-start | bytes 1179656 | tf_op jit(solution)/shard_map/ppermute | solution.py:222
  (23 other events, 26.0 us)

commit v5 on v4

--- a/solution.py
+++ b/solution.py
@@ -207,7 +207,7 @@
     return jnp.concatenate(outputs, 0)
 
 
-VMEM_LIMIT = 48 * 1024 * 1024
+MIB = 1024 * 1024
 SHORT = pl.CostEstimate(flops=1, bytes_accessed=1, transcendentals=0)
 LOW_BITS = 4
 PACKED = 16 // LOW_BITS
@@ -347,7 +347,7 @@
             jax.ShapeDtypeStruct((KVH, rows, columns), jnp.float32),
             jax.ShapeDtypeStruct((sent_rows, columns), jnp.int16),
         ],
-        compiler_params=pltpu.CompilerParams(vmem_limit_bytes=VMEM_LIMIT),
+        compiler_params=pltpu.CompilerParams(vmem_limit_bytes=24 * MIB),
         cost_estimate=SHORT,
         name="project",
     )(core, normed, qkv_weight, *after)
@@ -398,7 +398,7 @@
             jax.ShapeDtypeStruct((steps, rows, columns), jnp.float32),
             jax.ShapeDtypeStruct((steps * coded + TILE, columns), jnp.int16),
         ],
-        compiler_params=pltpu.CompilerParams(vmem_limit_bytes=VMEM_LIMIT),
+        compiler_params=pltpu.CompilerParams(vmem_limit_bytes=12 * MIB),
         cost_estimate=SHORT,
         name="fold",
     )(bit, held, landed, landed, *after)
@@ -438,7 +438,7 @@
         + [pl.BlockSpec(memory_space=pl.ANY)] * len(after),
         out_specs=[whole] * len(shapes),
         out_shape=shapes,
-        compiler_params=pltpu.CompilerParams(vmem_limit_bytes=VMEM_LIMIT),
+        compiler_params=pltpu.CompilerParams(vmem_limit_bytes=6 * MIB),
         cost_estimate=SHORT,
         name="finish",
     )(core, held, landed, cosine, sine, *after)
@@ -446,7 +446,7 @@
 
 def mix_kernel(count, places, *refs):
     pieces = refs[:count]
-    weights, start, mixed, wide, arrived = refs[count:]
+    weights, start, mixed, total, wide, arrived = refs[count:]
     depth = wide.shape[1]
     columns = wide.shape[2] // 2
     flat = []
@@ -462,19 +462,21 @@
     ]
     for copy in copies:
         copy.start()
-    half = (len(flat) + 1) // 2
-    for first, last in ((0, half), (half, len(flat))):
+    cuts = [0, 1, 2, 4, len(flat)]
+    cuts = sorted(set(min(cut, len(flat)) for cut in cuts))
+    for first, last in zip(cuts, cuts[1:]):
         for copy in copies[first:last]:
             copy.wait()
-        source = start if first == 0 else mixed
         for side in range(2):
             span = pl.ds(side * columns, columns)
-            total = source[:, span].astype(jnp.float32)
+            source = start if first == 0 else total
+            value = source[:, span].astype(jnp.float32)
             for i in range(first, last):
-                total = total + jnp.dot(
+                value = value + jnp.dot(
                     flat[i][...], wide[i, :, span], preferred_element_type=jnp.float32
                 )
-            mixed[:, span] = total.astype(mixed.dtype)
+            target = mixed if last == len(flat) else total
+            target[:, span] = value.astype(target.dtype)
 
 
 def mix(places, pieces, out_weight, start, dtype):
@@ -489,61 +491,47 @@
         + [pl.BlockSpec(memory_space=pl.ANY), whole],
         out_specs=whole,
         scratch_shapes=[
+            pltpu.VMEM((rows, columns), jnp.float32),
             pltpu.VMEM((count, width, columns), jnp.bfloat16),
             pltpu.SemaphoreType.DMA((count,)),
         ],
         out_shape=jax.ShapeDtypeStruct((rows, columns), dtype),
-        compiler_params=pltpu.CompilerParams(vmem_limit_bytes=VMEM_LIMIT),
+        compiler_params=pltpu.CompilerParams(vmem_limit_bytes=32 * MIB),
         cost_estimate=SHORT,
         name="mix",
     )(places, *pieces, out_weight, start)
 
 
-def along(value, pairs):
-    devices = lax.axis_size("tensor")
-    side = devices // 4
-    table = [
-        (source * side + i, target * side + i) for source, target in pairs for i in range(side)
-    ]
-    return lax.ppermute(value, "tensor", table)
-
-
 def gather_and_mix(attention, out_weight, start, device):
-    line = device // 4
-    inner = (line == 1) | (line == 2)
-
     def add(mixed, pieces, offsets, dtype=jnp.float32):
         places = jnp.stack([device ^ offset for offset in offsets])
         return mix(places, pieces, out_weight, mixed, dtype)
 
     near = swap(attention, 4)
-    cross = along(attention, [(1, 2), (2, 1)])
     across = swap(attention, 2)
-    near, cross, across = together(near, cross, across)
-
-    passed = along(cross, [(1, 0), (2, 3)])
-    cross_near = along(near, [(1, 2), (2, 1)])
+    far = swap(attention, 8)
+    partner = swap(attention, 1)
+    near, across, far, partner = together(near, across, far, partner)
+
     across_near = swap(near, 2)
-    first = swap(jnp.stack([attention, near]), 1)
-    passed, cross_near, across_near, first = together(passed, cross_near, across_near, first)
-
-    third = jnp.where(inner, cross_near, passed)
-    last = along(cross_near, [(1, 0), (2, 3)])
-    across_third = swap(third, 2)
-    second = swap(jnp.stack([across, across_near]), 1)
-    mixed = add(start, [attention, near, first], (0, 4, 1, 5))
-    last, across_third, second, mixed = together(last, across_third, second, mixed)
-
-    fourth = jnp.where(inner, cross, last)
-    across_fourth = swap(fourth, 2)
-    both = jnp.stack([third, across_third, fourth])
-    most = swap(both, 1)
-    mixed = add(mixed, [across, across_near, second], (2, 6, 3, 7))
-    across_fourth, most, mixed = together(across_fourth, most, mixed)
-
-    final = swap(across_fourth, 1)
-    mixed = add(mixed, [both, most], (8, 10, 12, 9, 11, 13))
-    return add(mixed, [across_fourth, final], (14, 15), jnp.bfloat16)
+    across_far = swap(far, 2)
+    farthest = swap(attention, 12)
+    first = jnp.stack([near, across, far])
+    first_partner = swap(first, 1)
+    mixed = add(start, [attention, partner], (0, 1))
+    across_near, across_far, farthest, first_partner, mixed = together(
+        across_near, across_far, farthest, first_partner, mixed
+    )
+
+    last = swap(farthest, 2)
+    second = jnp.stack([across_near, across_far, farthest])
+    second_partner = swap(second, 1)
+    mixed = add(mixed, [first, first_partner], (4, 2, 8, 5, 3, 9))
+    last, second_partner, mixed = together(last, second_partner, mixed)
+
+    last_partner = swap(last, 1)
+    mixed = add(mixed, [second, second_partner], (6, 10, 12, 7, 11, 13))
+    return add(mixed, [last, last_partner], (14, 15), jnp.bfloat16)
 
 
 def attend_kernel(
@@ -638,7 +626,7 @@
         out_shape=jax.ShapeDtypeStruct((requests, count, HD), jnp.bfloat16),
         scratch_shapes=[pltpu.VMEM((slots, count, HD), jnp.float32)] * 3
         + [pltpu.VMEM((requests, count, HD), jnp.float32)] * 3,
-        compiler_params=pltpu.CompilerParams(vmem_limit_bytes=VMEM_LIMIT),
+        compiler_params=pltpu.CompilerParams(vmem_limit_bytes=24 * MIB),
         cost_estimate=SHORT,
         name="attend",
     )(slot_request, *arrays)
@@ -691,13 +679,29 @@
             out_specs=[out, out],
         ),
         out_shape=[shape, shape],
-        compiler_params=pltpu.CompilerParams(vmem_limit_bytes=VMEM_LIMIT),
+        compiler_params=pltpu.CompilerParams(vmem_limit_bytes=6 * MIB),
         cost_estimate=SHORT,
         name="arrange",
     )(chip, cache_pool, cache_pool, scales, scales, after)
 
 
-SPLIT = (((0, 0), (0, 2), (1, 0), (1, 2)), ((0, 1), (0, 3), (1, 1), (1, 3)))
+HANDOVER_BITS = (1, 2, 4)
+
+
+def handover_plan():
+    kept = [(0, dest) for dest in range(0, KVH, 2)]
+    landed = [(1, dest) for dest in range(0, KVH, 2)]
+    splits = []
+    for bit in HANDOVER_BITS[1:]:
+        entries = [(0, i, e) for i, e in enumerate(kept)] + [
+            (1, i, e) for i, e in enumerate(landed)
+        ]
+        stay = [e for e in entries if not e[2][1] & bit]
+        leave = [e for e in entries if e[2][1] & bit]
+        splits.append(tuple(tuple((side, i) for side, i, _ in part) for part in (stay, leave)))
+        kept = [e for _, _, e in stay]
+        landed = [(source ^ bit, dest ^ bit) for _, _, (source, dest) in leave]
+    return splits, [source for source, _ in kept + landed]
 
 
 def regroup_kernel(index_of, kept, landed, *refs):
@@ -716,7 +720,7 @@
         in_specs=[whole, whole] + [pl.BlockSpec(memory_space=pl.ANY)] * len(after),
         out_specs=[whole, whole],
         out_shape=[shape, shape],
-        compiler_params=pltpu.CompilerParams(vmem_limit_bytes=VMEM_LIMIT),
+        compiler_params=pltpu.CompilerParams(vmem_limit_bytes=8 * MIB),
         cost_estimate=SHORT,
         name="regroup",
     )(kept, landed, *after)
@@ -745,22 +749,22 @@
 
     hidden = hidden_in.astype(jnp.float32)
     sums = jnp.sum(hidden * hidden, -1)
-    for bit in MESH_BITS:
+    bits = [jnp.reshape((device >> b) & 1, (1,)).astype(jnp.int32) for b in range(4)]
+    scale_rows = jnp.pad(
+        jnp.transpose(cache_scale, (1, 2, 0)).reshape(KVH, 1, 2 * slots),
+        ((0, 0), (0, TILE - 1), (0, 2 * HD - 2 * slots)),
+    )
+    chip_scalar = jnp.reshape(chip, (1,)).astype(jnp.int32)
+    sums = sums + swap(sums, 2)
+    cache_kept, cache_sent = arrange(chip_scalar, cache_pool, scale_rows, sums)
+    cache_landed = swap(cache_sent, 2)
+    for bit in (1, 4, 8):
         sums = sums + swap(sums, bit)
-        if bit == 2:
-            early = sums
+    sums, cache_landed = together(sums, cache_landed)
     normed = (
         hidden * lax.rsqrt(sums[..., None] / D + EPSILON) * norm_gain.astype(jnp.float32)
     ).astype(jnp.bfloat16)
     normed = normed.reshape(rows, width)
-    bits = [jnp.reshape((device >> b) & 1, (1,)).astype(jnp.int32) for b in range(4)]
-    scale_rows = jnp.pad(
-        jnp.transpose(cache_scale, (1, 2, 0)).reshape(KVH, 1, 2 * slots),
-        ((0, 0), (0, TILE - 1), (0, 2 * HD - 2 * slots)),
-    )
-    chip_scalar = jnp.reshape(chip, (1,)).astype(jnp.int32)
-    cache_kept, cache_sent = arrange(chip_scalar, cache_pool, scale_rows, early)
-    cache_landed = swap(cache_sent, 2)
 
     step_ids = jnp.arange(STEPS, dtype=jnp.int32)
     row_ids = jnp.arange(QR, dtype=jnp.int32)
@@ -774,51 +778,80 @@
 
     count = GQ // 4
     held, sent = [None] * count, [None] * count
-
-    def folded(chunk, b, *after):
-        held[chunk], sent[chunk] = fold(
-            bits[b], held[chunk], swap(sent[chunk], MESH_BITS[b - 1]), after
-        )
+    splits, sources_of_cache = handover_plan()
 
     def projected(chunk, *after):
         held[chunk], sent[chunk] = project(
             bits[0], normed, qkv_weight, chunk, chunk == 0, after
         )
 
+    def hop(chunk, b):
+        return swap(sent[chunk], MESH_BITS[b])
+
+    def folded(chunk, b, landed, *after):
+        held[chunk], sent[chunk] = fold(bits[b], held[chunk], landed, after)
+
+    def finished(chunk, landed, *after):
+        return finish(bits[0], held[chunk], landed, cosine, sine, after)
+
     projected(0, cache_kept)
+    core_0 = hop(0, 0)
     projected(1, held[0])
-    cache_kept, cache_sent = regroup(SPLIT, cache_kept, cache_landed, (held[1],))
+    core_0, sent[1] = together(core_0, sent[1])
+
+    folded(0, 1, core_0)
+    core_1, y_0 = hop(1, 0), hop(0, 1)
+    cache_kept, cache_sent = regroup(splits[0], cache_kept, cache_landed, (held[0],))
     cache_landed = swap(cache_sent, 4)
-    projected(2, cache_kept)
+    projected(2, held[0], cache_kept)
     projected(3, held[2])
-    folded(0, 1, held[3])
-    folded(1, 1, held[0])
-    folded(2, 1, held[1])
-    cache_kept, cache_sent = regroup(SPLIT, cache_kept, cache_landed, (held[2],))
+    core_1, y_0, sent[2], sent[3], cache_landed = together(
+        core_1, y_0, sent[2], sent[3], cache_landed
+    )
+
+    core_2, core_3 = hop(2, 0), hop(3, 0)
+    folded(1, 1, core_1)
+    y_1 = hop(1, 1)
+    folded(0, 2, y_0, held[1])
+    near_0 = hop(0, 2)
+    cache_kept, cache_sent = regroup(splits[1], cache_kept, cache_landed, (held[0],))
     cache_landed = swap(cache_sent, 8)
+    folded(2, 1, core_2, cache_kept)
+    folded(3, 1, core_3, held[2])
+    y_1, near_0, sent[2], sent[3] = together(y_1, near_0, sent[2], sent[3])
+
+    y_2 = hop(2, 1)
+    folded(0, 3, near_0)
+    far_0 = hop(0, 3)
+    folded(1, 2, y_1)
+    near_1 = hop(1, 2)
+    y_2, far_0, near_1 = together(y_2, far_0, near_1)
+
+    y_3 = hop(3, 1)
+    folded(1, 3, near_1)
+    far_1 = hop(1, 3)
+    folded(2, 2, y_2)
+    near_2 = hop(2, 2)
+    query_chunks = [None] * count
+    query_chunks[0], pair = finished(0, far_0, cache_kept)
+    pair_other = swap(pair, 1)
     kept_other = swap(cache_kept, 1)
-    folded(3, 1, cache_kept)
-    folded(0, 2, held[3])
-    folded(1, 2, held[0])
-    folded(0, 3, held[1])
-    folded(2, 2, held[0])
-    folded(1, 3, held[2])
-
-    def finished(chunk, *after):
-        return finish(
-            bits[0], held[chunk], swap(sent[chunk], MESH_BITS[3]), cosine, sine, after
-        )
-
-    query_chunks = [None] * count
-    query_chunks[0], pair = finished(0, held[1])
-    pair_other = swap(pair, 1)
-    folded(3, 2, query_chunks[0])
-    folded(2, 3, held[3])
-    (query_chunks[1],) = finished(1, held[2])
-    folded(3, 3, query_chunks[1], pair_other)
-    (query_chunks[2],) = finished(2, held[3])
+    y_3, far_1, near_2, pair_other, kept_other = together(
+        y_3, far_1, near_2, pair_other, kept_other
+    )
+
+    folded(3, 2, y_3)
+    near_3 = hop(3, 2)
+    folded(2, 3, near_2)
+    far_2 = hop(2, 3)
+    (query_chunks[1],) = finished(1, far_1, held[2])
+    near_3, far_2, cache_landed = together(near_3, far_2, cache_landed)
     landed_other = swap(cache_landed, 1)
-    (query_chunks[3],) = finished(3, query_chunks[2])
+
+    folded(3, 3, near_3)
+    far_3 = hop(3, 3)
+    (query_chunks[2],) = finished(2, far_2, held[3])
+    (query_chunks[3],) = finished(3, far_3, query_chunks[2])
     cache_parts = (cache_kept, cache_landed, kept_other, landed_other)
     keys = jnp.where(core == 0, pair, pair_other)
     raw_values = jnp.where(core == 0, pair_other, pair)
@@ -831,7 +864,7 @@
         return jnp.pad(value, ((0, 0), (0, TILE - STEPS * QR), (0, 0)))
 
     slot_request, slot_rank, slot_length = slot_layout(request_length, block_table, slots, stripe)
-    source = chip ^ jnp.arange(KVH, dtype=jnp.int32)
+    source = chip ^ jnp.array(sources_of_cache, dtype=jnp.int32)
     sources = jnp.stack([source * 2 + core, source * 2 + 1 - core])
     offset = sources[:, :, None] * BLK + jnp.arange(BLK, dtype=jnp.int32)[None, None, :]
     token = slot_rank[:, None] * stripe + offset.reshape(1, stripe)

time: 236 us -> 270 us (1.14)
  local copies, waits for them, and re-layouts: 19.3 us -> 47.4 us
  waiting for transfers between devices: 80.6 us -> 98.9 us
  Pallas kernels: 88.1 us -> 72.1 us
  starting transfers between devices: 32.5 us -> 38.1 us
    ppermute x35 -> x37, waiting for transfers between devices: 64 us -> 98.9 us  [swap(): return lax.ppermute(value, 'tensor', [(i, i ^ bit) for i in range(devices)])]
    unnamed x98 -> x180, local copies, waits for them, and re-layouts: 14.7 us -> 42.8 us
    ppermute x4 -> x0, waiting for transfers between devices: 16.7 us -> none  [along(): return lax.ppermute(value, 'tensor', table)]
    ppermute x35 -> x37, starting transfers between devices: 27.6 us -> 38.1 us  [swap(): return lax.ppermute(value, 'tensor', [(i, i ^ bit) for i in range(devices)])]
    pallas_call x12, Pallas kernels: 23.1 us -> 14.5 us  [fold(): pl.pallas_call(functools.partial(fold_kernel, steps), grid_spec=pltpu.Pre...]
    ppermute x4 -> x0, starting transfers between devices: 4.9 us -> none  [along(): return lax.ppermute(value, 'tensor', table)]
    pallas_call x4, Pallas kernels: 27.7 us -> 24.1 us  [project(): pl.pallas_call(functools.partial(project_kernel, chunk, with_pair), grid_...]
  transfers between devices with their start and end apart: 39 -> 37, of which waited for: 20 -> 19; matrix products, arithmetic and copies ran while one was open for 4% -> 3% of each run, Pallas kernels for 31% -> 19%
where the time goes in v5:
time: 270 us; the launch traced here: 269 us
  waiting for transfers between devices  98.9 us (37%)
  Pallas kernels  72.1 us (27%)
  local copies, waits for them, and re-layouts  47.4 us (18%)
  starting transfers between devices  38.1 us (14%)
  other arithmetic  11.1 us (4%)
    ppermute x37, waiting for transfers between devices, swap(): return lax.ppermute(value, 'tensor', [(i, i ^ bit) for i in range(devices)])  98.9 us
    unnamed x180, local copies, waits for them, and re-layouts  42.8 us
    ppermute x37, starting transfers between devices, swap(): return lax.ppermute(value, 'tensor', [(i, i ^ bit) for i in range(devices)])  38.1 us
    pallas_call x4, Pallas kernels, project(): pl.pallas_call(functools.partial(project_kernel, chunk, with_pair), grid_...  24.1 us
    pallas_call x4, Pallas kernels, mix(): pl.pallas_call(functools.partial(mix_kernel, len(pieces)), in_specs=[pl.B...  21.1 us
    pallas_call x12, Pallas kernels, fold(): pl.pallas_call(functools.partial(fold_kernel, steps), grid_spec=pltpu.Pre...  14.5 us
    pallas_call x1, Pallas kernels, attend(): pl.pallas_call(attend_kernel, in_specs=[pl.BlockSpec(memory_space=pltpu.S...  10.2 us
  transfers between devices with their start and end apart: 37, of which 19 were waited for; matrix products, arithmetic and copies ran while one was open for 3% of the time, Pallas kernels for 19%

profile of v5, /device:TPU:0, one launch (start us, length us, event | category | flops | bytes accessed | tf_op | source)
XLA Modules:
  0.0 268.5 jit_solution(1675546256849469853)
XLA Ops:
  0.0 1.2 fusion
  1.2 3.0 %collective-permute-start = (f32[2,96]{1,0:T(2,128)S(1)}, f32[2,96]{1,0:T(2,128)S(1)}, u32[]{:S(2)}, u32[]{:S(2)}) collective-permute-start(f32[2,96]{1,0:T(2,128)S(1)} %fusion), channel_id=1, source_target_pairs={{0,2},{1,3},{2,0},{3,1},{4,6},{5,7},{6,4},{7,5},{8,10},{9,11},{10,... | collective-permute-start | bytes 2312 | tf_op jit(solution)/shard_map/ppermute | solution.py:222
  5.7 1.4 copy-done.12
  7.5 2.1 collective-permute-start.4
  9.6 1.1 collective-permute-done.1
  10.8 1.6 collective-permute-start.2
  12.3 2.0 collective-permute-done.2
  14.3 2.6 collective-permute-start.3
  16.9 1.9 collective-permute-done.3
  19.4 7.3 %collective-permute-done.4.refs_1_ = bf16[4,400,256]{2,1,0:T(8,128)(2,1)S(1)} collective-permute-done((bf16[4,400,256]{2,1,0:T(8,128)(2,1)S(1)}, bf16[4,400,256]{2,1,0:T(8,128)(2,1)S(1)}, u32[]{:S(2)}, u32[]{:S(2)}) %collective-permute-start.4) | collective-permute-done | bytes 819232 | tf_op jit(solution)/shard_map/ppermute | solution.py:222
  28.5 6.6 %project.4 = (f32[8,192,384]{2,1,0:T(8,128)S(1)}, s16[1936,384]{1,0:T(8,128)(2,1)S(1)}) custom-call(s32[1]{0:T(128)} %bitcast.2.core, bf16[192,1024]{1,0:T(8,128)(2,1)S(1)} %bitcast.57, bf16[1024,18432]{1,0:T(8,128)(2,1)} %weights.7, bf16[4,400,256]{2,1,0:T(8,128)(2,1)S(1)} %get-tuple-element.83.refs_0_.kept), custom_call_target="tpu_custom_call" | custom-call | flops 1 | bytes 1 | tf_op jit(solution)/shard_map/project/pallas_call | solution.py:329
  36.1 6.2 %project.5 = (f32[8,192,256]{2,1,0:T(8,128)S(1)}, s16[1936,256]{1,0:T(8,128)(2,1)S(1)}) custom-call(s32[1]{0:T(128)} %bitcast.2.core, bf16[192,1024]{1,0:T(8,128)(2,1)S(1)} %bitcast.58, bf16[1024,18432]{1,0:T(8,128)(2,1)} %weights.7, f32[8,192,384]{2,1,0:T(8,128)S(1)} %get-tuple-element.84.refs_0_.held), custom_call_target="tpu_custom_call" | custom-call | flops 1 | bytes 1 | tf_op jit(solution)/shard_map/project/pallas_call | solution.py:329
  42.3 1.2 copy-done.53
  44.9 1.4 copy-done.1
  46.3 1.7 copy-done.3
  48.0 1.3 fold.12
  49.5 1.9 collective-permute-start.8
  51.4 1.5 collective-permute-start.7
  52.9 5.3 %project.6 = (f32[8,192,256]{2,1,0:T(8,128)S(1)}, s16[1936,256]{1,0:T(8,128)(2,1)S(1)}) custom-call(s32[1]{0:T(128)} %bitcast.2.core, bf16[192,1024]{1,0:T(8,128)(2,1)S(1)} %bitcast.59, bf16[1024,18432]{1,0:T(8,128)(2,1)} %weights.7, f32[4,192,384]{2,1,0:T(8,128)S(1)} %get-tuple-element.88.refs_0_.held, bf16[4,400,256]{2,1,0:T(8,128)(2,1)S(1)} %get-tuple-element.92.refs_1_.kept), custom_call_target="tpu_custom_call" | custom-call | flops 1 | bytes 1 | tf_op jit(solution)/shard_map/project/pallas_call | solution.py:329
  59.3 5.9 %project.7 = (f32[8,192,256]{2,1,0:T(8,128)S(1)}, s16[1936,256]{1,0:T(8,128)(2,1)S(1)}) custom-call(s32[1]{0:T(128)} %bitcast.2.core, bf16[192,1024]{1,0:T(8,128)(2,1)S(1)} %bitcast.60, bf16[1024,18432]{1,0:T(8,128)(2,1)} %weights.7, f32[8,192,256]{2,1,0:T(8,128)S(1)} %get-tuple-element.94.refs_0_.held), custom_call_target="tpu_custom_call" | custom-call | flops 1 | bytes 1 | tf_op jit(solution)/shard_map/project/pallas_call | solution.py:329
  65.2 1.2 copy-done.51
  66.4 3.9 %collective-permute-done.7.refs_1_ = s16[976,384]{1,0:T(8,128)(2,1)S(1)} collective-permute-done((s16[976,384]{1,0:T(8,128)(2,1)S(1)}, s16[976,384]{1,0:T(8,128)(2,1)S(1)}, u32[]{:S(2)}, u32[]{:S(2)}) %collective-permute-start.7) | collective-permute-done | bytes 749600 | tf_op jit(solution)/shard_map/ppermute | solution.py:222
  72.8 1.2 copy-done.5
  74.0 1.4 copy-done.54
  75.4 1.7 fold.13
  78.0 1.5 collective-permute-start.9
  80.6 1.1 copy-done.37
  81.7 1.4 fold.14
  83.1 1.2 collective-permute-start.10
  86.1 2.8 %fold.15 = (f32[4,192,256]{2,1,0:T(8,128)S(1)}, s16[976,256]{1,0:T(8,128)(2,1)S(1)}) custom-call(s32[1]{0:T(128)} %bitcast.5.bit, f32[8,192,256]{2,1,0:T(8,128)S(1)} %copy-done.14, s16[1936,256]{1,0:T(8,128)(2,1)} %collective-permute-done.11.landed.landed_powers, s16[1936,256]{1,0:T(8,128)(2,1)} %collective-permute-done.11.landed.landed_powers, ...), custom_call_target="tpu_custom_call" | custom-call | flops 1 | bytes 1 | tf_op jit(solution)/shard_map/fold/pallas_call | solution.py:380
  89.7 3.4 %fold.16 = (f32[4,192,256]{2,1,0:T(8,128)S(1)}, s16[976,256]{1,0:T(8,128)(2,1)}) custom-call(s32[1]{0:T(128)} %bitcast.5.bit, f32[8,192,256]{2,1,0:T(8,128)S(1)} %copy-done.52, s16[1936,256]{1,0:T(8,128)(2,1)} %collective-permute-done.12.landed.landed_powers, s16[1936,256]{1,0:T(8,128)(2,1)} %collective-permute-done.12.landed.landed_powers, ...), custom_call_target="tpu_custom_call" | custom-call | flops 1 | bytes 1 | tf_op jit(solution)/shard_map/fold/pallas_call | solution.py:380
  96.3 1.3 fold.17
  98.4 2.5 collective-permute-start.14
  102.1 1.2 collective-permute-start.15
  103.8 7.3 %collective-permute-done.14.refs_1_ = s16[256,384]{1,0:T(8,128)(2,1)S(1)} collective-permute-done((s16[256,384]{1,0:T(8,128)(2,1)S(1)}, s16[256,384]{1,0:T(8,128)(2,1)S(1)}, u32[]{:S(2)}, u32[]{:S(2)}) %collective-permute-start.14) | collective-permute-done | bytes 196640 | tf_op jit(solution)/shard_map/ppermute | solution.py:222
  111.0 1.4 collective-permute-start.16
  112.4 3.2 %collective-permute-done.15.refs_2_ = s16[496,256]{1,0:T(8,128)(2,1)S(1)} collective-permute-done((s16[496,256]{1,0:T(8,128)(2,1)S(1)}, s16[496,256]{1,0:T(8,128)(2,1)S(1)}, u32[]{:S(2)}, u32[]{:S(2)}) %collective-permute-start.15) | collective-permute-done | bytes 253984 | tf_op jit(solution)/shard_map/ppermute | solution.py:222
  119.8 1.3 pad_maximum_fusion.2
  122.4 1.3 collective-permute-start.17
  124.0 27.4 %collective-permute-done.17.refs_1_ = s16[256,256]{1,0:T(8,128)(2,1)S(1)} collective-permute-done((s16[256,256]{1,0:T(8,128)(2,1)S(1)}, s16[256,256]{1,0:T(8,128)(2,1)S(1)}, u32[]{:S(2)}, u32[]{:S(2)}) %collective-permute-start.17) | collective-permute-done | bytes 131104 | tf_op jit(solution)/shard_map/ppermute | solution.py:222
  154.9 1.1 fold.22
  158.0 3.3 %collective-permute-start.22 = (s16[256,256]{1,0:T(8,128)(2,1)S(1)}, s16[256,256]{1,0:T(8,128)(2,1)S(1)}, u32[]{:S(2)}, u32[]{:S(2)}) collective-permute-start(s16[256,256]{1,0:T(8,128)(2,1)S(1)} %get-tuple-element.135), channel_id=1, source_target_pairs={{0,8},{1,9},{2,10},{3,11},{4,12},{5,13},{6,14},{7,15},{8,0},{9,1},... | collective-permute-start | bytes 393224 | tf_op jit(solution)/shard_map/ppermute | solution.py:222
  161.3 4.2 %collective-permute-done.22.refs_1_ = s16[256,256]{1,0:T(8,128)(2,1)S(1)} collective-permute-done((s16[256,256]{1,0:T(8,128)(2,1)S(1)}, s16[256,256]{1,0:T(8,128)(2,1)S(1)}, u32[]{:S(2)}, u32[]{:S(2)}) %collective-permute-start.22) | collective-permute-done | bytes 131104 | tf_op jit(solution)/shard_map/ppermute | solution.py:222
  165.5 2.2 collective-permute-done.21.refs_0_
  171.4 1.9 collective-permute-start.24
  178.3 2.8 %collective-permute-done.24.landed = s16[256,256]{1,0:T(8,128)(2,1)S(1)} collective-permute-done((s16[256,256]{1,0:T(8,128)(2,1)S(1)}, s16[256,256]{1,0:T(8,128)(2,1)S(1)}, u32[]{:S(2)}, u32[]{:S(2)}) %collective-permute-start.24) | collective-permute-done | bytes 131104 | tf_op jit(solution)/shard_map/ppermute | solution.py:222
  182.9 10.2 %attend.1 = bf16[16,96,128]{2,1,0:T(8,128)(2,1)S(1)} custom-call(s32[24]{0:T(128)S(1)} %get-tuple-element.159.slot_request, bf16[16,96,128]{2,1,0:T(8,128)(2,1)S(1)} %bitcast.68, bf16[16,16,128]{2,1,0:T(8,128)(2,1)S(1)} %pad.12.new_keys, bf16[16,16,128]{2,1,0:T(8,128)(2,1)S(1)} %pad.13.new_values, ...), custom_call_target="tpu_custom_call" | custom-call | flops 1 | bytes 1 | tf_op jit(solution)/shard_map/attend/pallas_call | solution.py:622
  193.3 1.4 collective-permute-start.27
  194.8 2.9 %collective-permute-start.28 = (bf16[192,1024]{1,0:T(8,128)(2,1)S(1)}, bf16[192,1024]{1,0:T(8,128)(2,1)}, u32[]{:S(2)}, u32[]{:S(2)}) collective-permute-start(bf16[192,1024]{1,0:T(8,128)(2,1)S(1)} %bitcast.64), channel_id=1, source_target_pairs={{0,8},{1,9},{2,10},{3,11},{4,12},{5,13},{6,14},{7,15},{8,0},{9,1},... | collective-permute-start | bytes 1179656 | tf_op jit(solution)/shard_map/ppermute | solution.py:222
  197.7 13.4 %collective-permute-done.26.refs_0_ = bf16[192,1024]{1,0:T(8,128)(2,1)} collective-permute-done((bf16[192,1024]{1,0:T(8,128)(2,1)S(1)}, bf16[192,1024]{1,0:T(8,128)(2,1)}, u32[]{:S(2)}, u32[]{:S(2)}) %collective-permute-start.26) | collective-permute-done | bytes 393248 | tf_op jit(solution)/shard_map/ppermute | solution.py:222
  211.1 3.6 %collective-permute-done.28.refs_2_ = bf16[192,1024]{1,0:T(8,128)(2,1)} collective-permute-done((bf16[192,1024]{1,0:T(8,128)(2,1)S(1)}, bf16[192,1024]{1,0:T(8,128)(2,1)}, u32[]{:S(2)}, u32[]{:S(2)}) %collective-permute-start.28) | collective-permute-done | bytes 393248 | tf_op jit(solution)/shard_map/ppermute | solution.py:222
  215.5 1.4 pad_maximum_fusion.refs_0_
  217.0 2.5 collective-permute-start.32
  220.0 1.6 collective-permute-start.31
  221.6 3.4 %mix.4.refs_4_ = f32[192,1024]{1,0:T(8,128)S(1)} custom-call(s32[2]{0:T(128)S(1)} %pad_add_fusion.1.places, bf16[192,1024]{1,0:T(8,128)(2,1)S(1)} %bitcast.67, bf16[192,1024]{1,0:T(8,128)(2,1)S(1)} %copy-done.50, bf16[16384,1024]{1,0:T(8,128)(2,1)} %refs_2_.7, bf16[192,1024]{1,0:T(8,128)(2,1)S(1)} %bitcast.61), custom_call_target="tpu_custom_call" | custom-call | flops 1 | bytes 1 | tf_op jit(solution)/shard_map/mix/pallas_call | solution.py:487
  225.9 4.6 %collective-permute-done.32.refs_2_ = bf16[192,1024]{1,0:T(8,128)(2,1)} collective-permute-done((bf16[192,1024]{1,0:T(8,128)(2,1)S(1)}, bf16[192,1024]{1,0:T(8,128)(2,1)}, u32[]{:S(2)}, u32[]{:S(2)}) %collective-permute-start.32) | collective-permute-done | bytes 393248 | tf_op jit(solution)/shard_map/ppermute | solution.py:222
  230.5 1.3 collective-permute-done.30.refs_0_
  231.8 7.6 %collective-permute-done.31.refs_1_ = bf16[192,1024]{1,0:T(8,128)(2,1)} collective-permute-done((bf16[192,1024]{1,0:T(8,128)(2,1)}, bf16[192,1024]{1,0:T(8,128)(2,1)}, u32[]{:S(2)}, u32[]{:S(2)}) %collective-permute-start.31) | collective-permute-done | bytes 393248 | tf_op jit(solution)/shard_map/ppermute | solution.py:222
  240.5 2.5 pad_maximum_fusion.1.refs_0_
  243.6 6.3 %mix.5.refs_2_ = f32[192,1024]{1,0:T(8,128)S(1)} custom-call(s32[6]{0:T(128)S(1)} %stack.116.places, bf16[3,192,1024]{2,1,0:T(8,128)(2,1)S(1)} %pad_maximum_fusion.refs_0_, bf16[3,192,1024]{2,1,0:T(8,128)(2,1)S(1)} %copy-done.16, bf16[16384,1024]{1,0:T(8,128)(2,1)} %refs_2_.7, f32[192,1024]{1,0:T(8,128)S(1)} %copy-done.7), custom_call_target="tpu_custom_call" | custom-call | flops 1 | bytes 1 | tf_op jit(solution)/shard_map/mix/pallas_call | solution.py:487
  250.8 4.0 %collective-permute-done.34.refs_0_ = bf16[192,1024]{1,0:T(8,128)(2,1)S(1)} collective-permute-done((bf16[192,1024]{1,0:T(8,128)(2,1)}, bf16[192,1024]{1,0:T(8,128)(2,1)S(1)}, u32[]{:S(2)}, u32[]{:S(2)}) %collective-permute-start.34) | collective-permute-done | bytes 393248 | tf_op jit(solution)/shard_map/ppermute | solution.py:222
  255.7 1.1 copy-done.9
  256.8 7.4 %mix.6.refs_3_ = f32[192,1024]{1,0:T(8,128)S(1)} custom-call(s32[6]{0:T(128)S(1)} %stack.123.places, bf16[3,192,1024]{2,1,0:T(8,128)(2,1)} %pad_maximum_fusion.1.refs_0_, bf16[3,192,1024]{2,1,0:T(8,128)(2,1)} %get-tuple-element.155.refs_1_, bf16[16384,1024]{1,0:T(8,128)(2,1)} %refs_2_.7, f32[192,1024]{1,0:T(8,128)S(1)} %copy-done.9), custom_call_target="tpu_custom_call" | custom-call | flops 1 | bytes 1 | tf_op jit(solution)/shard_map/mix/pallas_call | solution.py:487
  264.3 4.1 %mix.7 = bf16[192,1024]{1,0:T(8,128)(2,1)} custom-call(s32[2]{0:T(128)S(1)} %pad_add_fusion.places, bf16[192,1024]{1,0:T(8,128)(2,1)S(1)} %copy-done.48, bf16[192,1024]{1,0:T(8,128)(2,1)S(1)} %collective-permute-done.36.refs_1_, bf16[16384,1024]{1,0:T(8,128)(2,1)} %refs_2_.7, f32[192,1024]{1,0:T(8,128)S(1)} %mix.6.refs_3_), custom_call_target="tpu_custom_call" | custom-call | flops 1 | bytes 1 | tf_op jit(solution)/shard_map/mix/pallas_call | solution.py:487
  (290 shorter events, 47.9 us)
Async XLA Ops:
  1.2 4.6 %collective-permute-start = (f32[2,96]{1,0:T(2,128)S(1)}, f32[2,96]{1,0:T(2,128)S(1)}, u32[]{:S(2)}, u32[]{:S(2)}) collective-permute-start(f32[2,96]{1,0:T(2,128)S(1)} %fusion), channel_id=1, source_target_pairs={{0,2},{1,3},{2,0},{3,1},{4,6},{5,7},{6,4},{7,5},{8,10},{9,11},{10,... | collective-permute-start | bytes 2312 | tf_op jit(solution)/shard_map/ppermute | solution.py:222
  7.2 9.8 %copy-start.87 = (bf16[1024]{0:T(1024)(128)(2,1)S(1)}, bf16[1024]{0:T(1024)(128)(2,1)}, u32[]{:S(2)}) copy-start(bf16[1024]{0:T(1024)(128)(2,1)} %param.10) | copy-start | bytes 6148
  7.2 21.1 %copy-start.23 = (bf16[2,96,1024]{2,1,0:T(8,128)(2,1)S(1)}, bf16[2,96,1024]{2,1,0:T(8,128)(2,1)}, u32[]{:S(2)}) copy-start(bf16[2,96,1024]{2,1,0:T(8,128)(2,1)} %param.9) | copy-start | bytes 1179652
  7.5 19.2 %collective-permute-start.4 = (bf16[4,400,256]{2,1,0:T(8,128)(2,1)S(1)}, bf16[4,400,256]{2,1,0:T(8,128)(2,1)S(1)}, u32[]{:S(2)}, u32[]{:S(2)}) collective-permute-start(bf16[4,400,256]{2,1,0:T(8,128)(2,1)S(1)} %get-tuple-element.81), channel_id=1, source_target_pairs={{0,2},{1,3},{2,0},{3,1},{4,6},{5,7},{6,4},{7,5},{8,10},{9,11},{10,... | collective-permute-start | bytes 2457608 | tf_op jit(solution)/shard_map/ppermute | solution.py:222
  9.6 1.1 collective-permute-start.1
  10.8 3.6 %collective-permute-start.2 = (f32[2,96]{1,0:T(2,128)S(1)}, f32[2,96]{1,0:T(2,128)S(1)}, u32[]{:S(2)}, u32[]{:S(2)}) collective-permute-start(f32[2,96]{1,0:T(2,128)S(1)} %add.120), channel_id=1, source_target_pairs={{0,4},{1,5},{2,6},{3,7},{4,0},{5,1},{6,2},{7,3},{8,12},{9,13},{10,... | collective-permute-start | bytes 2312 | tf_op jit(solution)/shard_map/ppermute | solution.py:222
  14.3 4.5 %collective-permute-start.3 = (f32[2,96]{1,0:T(2,128)S(1)}, f32[2,96]{1,0:T(2,128)S(1)}, u32[]{:S(2)}, u32[]{:S(2)}) collective-permute-start(f32[2,96]{1,0:T(2,128)S(1)} %add.121), channel_id=1, source_target_pairs={{0,8},{1,9},{2,10},{3,11},{4,12},{5,13},{6,14},{7,15},{8,0},{9,1},... | collective-permute-start | bytes 2312 | tf_op jit(solution)/shard_map/ppermute | solution.py:222
  36.1 6.2 %copy-start.2 = (f32[8,192,384]{2,1,0:T(8,128)}, f32[8,192,384]{2,1,0:T(8,128)S(1)}, u32[]{:S(2)}) copy-start(f32[8,192,384]{2,1,0:T(8,128)S(1)} %get-tuple-element.84.refs_0_.held) | copy-start | bytes 7077892
  36.1 7.4 %collective-permute-start.5 = (s16[1936,384]{1,0:T(8,128)(2,1)S(1)}, s16[1936,384]{1,0:T(8,128)(2,1)S(1)}, u32[]{:S(2)}, u32[]{:S(2)}) collective-permute-start(s16[1936,384]{1,0:T(8,128)(2,1)S(1)} %get-tuple-element.85), channel_id=1, source_target_pairs={{0,1},{1,0},{2,3},{3,2},{4,5},{5,4},{6,7},{7,6},{8,9},{9,8},{10,11... | collective-permute-start | bytes 4460552 | tf_op jit(solution)/shard_map/ppermute | solution.py:222
  44.9 25.4 %collective-permute-start.6 = (s16[1936,256]{1,0:T(8,128)(2,1)}, s16[1936,256]{1,0:T(8,128)(2,1)S(1)}, u32[]{:S(2)}, u32[]{:S(2)}) collective-permute-start(s16[1936,256]{1,0:T(8,128)(2,1)} %get-tuple-element.89), channel_id=1, source_target_pairs={{0,1},{1,0},{2,3},{3,2},{4,5},{5,4},{6,7},{7,6},{8,9},{9,8},{10,11... | collective-permute-start | bytes 2973704 | tf_op jit(solution)/shard_map/ppermute | solution.py:222
  49.4 3.5 %copy-start.88 = (s32[16]{0:T(128)S(1)}, s32[16]{0:T(128)}, u32[]{:S(2)}) copy-start(s32[16]{0:T(128)} %param.15) | copy-start | bytes 196
  49.5 8.8 %copy-start.26 = (bf16[4,400,256]{2,1,0:T(8,128)(2,1)}, bf16[4,400,256]{2,1,0:T(8,128)(2,1)S(1)}, u32[]{:S(2)}) copy-start(bf16[4,400,256]{2,1,0:T(8,128)(2,1)S(1)} %get-tuple-element.92.refs_1_.kept) | copy-start | bytes 2457604
  49.5 20.8 %collective-permute-start.8 = (bf16[4,400,256]{2,1,0:T(8,128)(2,1)S(1)}, bf16[4,400,256]{2,1,0:T(8,128)(2,1)S(1)}, u32[]{:S(2)}, u32[]{:S(2)}) collective-permute-start(bf16[4,400,256]{2,1,0:T(8,128)(2,1)S(1)} %get-tuple-element.96), channel_id=1, source_target_pairs={{0,4},{1,5},{2,6},{3,7},{4,0},{5,1},{6,2},{7,3},{8,12},{9,13},{10,... | collective-permute-start | bytes 2457608 | tf_op jit(solution)/shard_map/ppermute | solution.py:222
  51.4 18.9 %collective-permute-start.7 = (s16[976,384]{1,0:T(8,128)(2,1)S(1)}, s16[976,384]{1,0:T(8,128)(2,1)S(1)}, u32[]{:S(2)}, u32[]{:S(2)}) collective-permute-start(s16[976,384]{1,0:T(8,128)(2,1)S(1)} %get-tuple-element.90), channel_id=1, source_target_pairs={{0,2},{1,3},{2,0},{3,1},{4,6},{5,7},{6,4},{7,5},{8,10},{9,11},{10,... | collective-permute-start | bytes 2248712 | tf_op jit(solution)/shard_map/ppermute | solution.py:222
  59.3 5.9 %copy-start.13 = (f32[8,192,256]{2,1,0:T(8,128)}, f32[8,192,256]{2,1,0:T(8,128)S(1)}, u32[]{:S(2)}) copy-start(f32[8,192,256]{2,1,0:T(8,128)S(1)} %get-tuple-element.94.refs_0_.held) | copy-start | bytes 4718596
  66.4 4.8 %copy-start.56 = (s16[1936,256]{1,0:T(8,128)(2,1)}, s16[1936,256]{1,0:T(8,128)(2,1)S(1)}, u32[]{:S(2)}) copy-start(s16[1936,256]{1,0:T(8,128)(2,1)S(1)} %get-tuple-element.95.refs_3_) | copy-start | bytes 2973700
  72.1 14.0 %collective-permute-start.11 = (s16[1936,256]{1,0:T(8,128)(2,1)}, s16[1936,256]{1,0:T(8,128)(2,1)}, u32[]{:S(2)}, u32[]{:S(2)}) collective-permute-start(s16[1936,256]{1,0:T(8,128)(2,1)} %get-tuple-element.104), channel_id=1, source_target_pairs={{0,1},{1,0},{2,3},{3,2},{4,5},{5,4},{6,7},{7,6},{8,9},{9,8},{10,11... | collective-permute-start | bytes 2973704 | tf_op jit(solution)/shard_map/ppermute | solution.py:222
  72.1 16.8 %collective-permute-start.12 = (s16[1936,256]{1,0:T(8,128)(2,1)}, s16[1936,256]{1,0:T(8,128)(2,1)}, u32[]{:S(2)}, u32[]{:S(2)}) collective-permute-start(s16[1936,256]{1,0:T(8,128)(2,1)} %get-tuple-element.109), channel_id=1, source_target_pairs={{0,1},{1,0},{2,3},{3,2},{4,5},{5,4},{6,7},{7,6},{8,9},{9,8},{10,11... | collective-permute-start | bytes 2973704 | tf_op jit(solution)/shard_map/ppermute | solution.py:222
  75.4 5.2 %copy-start.11 = (s16[976,384]{1,0:T(8,128)(2,1)S(1)}, s16[976,384]{1,0:T(8,128)(2,1)}, u32[]{:S(2)}) copy-start(s16[976,384]{1,0:T(8,128)(2,1)} %get-tuple-element.97.landed.landed_powers) | copy-start | bytes 2248708
  78.0 16.0 %collective-permute-start.9 = (s16[976,256]{1,0:T(8,128)(2,1)}, s16[976,256]{1,0:T(8,128)(2,1)S(1)}, u32[]{:S(2)}, u32[]{:S(2)}) collective-permute-start(s16[976,256]{1,0:T(8,128)(2,1)} %get-tuple-element.102), channel_id=1, source_target_pairs={{0,2},{1,3},{2,0},{3,1},{4,6},{5,7},{6,4},{7,5},{8,10},{9,11},{10,... | collective-permute-start | bytes 1499144 | tf_op jit(solution)/shard_map/ppermute | solution.py:222
  83.1 10.8 %collective-permute-start.10 = (s16[496,384]{1,0:T(8,128)(2,1)}, s16[496,384]{1,0:T(8,128)(2,1)}, u32[]{:S(2)}, u32[]{:S(2)}) collective-permute-start(s16[496,384]{1,0:T(8,128)(2,1)} %get-tuple-element.103), channel_id=1, source_target_pairs={{0,4},{1,5},{2,6},{3,7},{4,0},{5,1},{6,2},{7,3},{8,12},{9,13},{10,... | collective-permute-start | bytes 1142792 | tf_op jit(solution)/shard_map/ppermute | solution.py:222
  85.4 37.0 %collective-permute-start.20 = (bf16[4,400,256]{2,1,0:T(8,128)(2,1)S(1)}, bf16[4,400,256]{2,1,0:T(8,128)(2,1)}, u32[]{:S(2)}, u32[]{:S(2)}) collective-permute-start(bf16[4,400,256]{2,1,0:T(8,128)(2,1)S(1)} %get-tuple-element.106.refs_0_.own_near), channel_id=1, source_target_pairs={{0,1},{1,0},{2,3},{3,2},{4,5},{5,4},{6,7},{7,6},{8,9},{9,8},{10,11... | collective-permute-start | bytes 2457608 | tf_op jit(solution)/shard_map/ppermute | solution.py:222
  86.1 3.6 %copy-start.52 = (f32[8,192,256]{2,1,0:T(8,128)S(1)}, f32[8,192,256]{2,1,0:T(8,128)}, u32[]{:S(2)}) copy-start(f32[8,192,256]{2,1,0:T(8,128)} %copy-done.51) | copy-start | bytes 4718596
  88.9 4.2 %copy-start.34 = (f32[4,192,256]{2,1,0:T(8,128)}, f32[4,192,256]{2,1,0:T(8,128)S(1)}, u32[]{:S(2)}) copy-start(f32[4,192,256]{2,1,0:T(8,128)S(1)} %get-tuple-element.110.refs_0_.held) | copy-start | bytes 2359300
  94.8 6.1 %copy-start.18 = (s16[976,256]{1,0:T(8,128)(2,1)S(1)}, s16[976,256]{1,0:T(8,128)(2,1)}, u32[]{:S(2)}) copy-start(s16[976,256]{1,0:T(8,128)(2,1)} %get-tuple-element.116.landed.landed_powers) | copy-start | bytes 1499140
  94.8 6.1 %copy-start.38 = (f32[4,192,256]{2,1,0:T(8,128)S(1)}, f32[4,192,256]{2,1,0:T(8,128)}, u32[]{:S(2)}) copy-start(f32[4,192,256]{2,1,0:T(8,128)} %copy-done.36) | copy-start | bytes 2359300
  94.8 20.9 %collective-permute-start.13 = (s16[976,256]{1,0:T(8,128)(2,1)}, s16[976,256]{1,0:T(8,128)(2,1)S(1)}, u32[]{:S(2)}, u32[]{:S(2)}) collective-permute-start(s16[976,256]{1,0:T(8,128)(2,1)} %get-tuple-element.114), channel_id=1, source_target_pairs={{0,2},{1,3},{2,0},{3,1},{4,6},{5,7},{6,4},{7,5},{8,10},{9,11},{10,... | collective-permute-start | bytes 1499144 | tf_op jit(solution)/shard_map/ppermute | solution.py:222
  98.4 12.7 %collective-permute-start.14 = (s16[256,384]{1,0:T(8,128)(2,1)S(1)}, s16[256,384]{1,0:T(8,128)(2,1)S(1)}, u32[]{:S(2)}, u32[]{:S(2)}) collective-permute-start(s16[256,384]{1,0:T(8,128)(2,1)S(1)} %get-tuple-element.115), channel_id=1, source_target_pairs={{0,8},{1,9},{2,10},{3,11},{4,12},{5,13},{6,14},{7,15},{8,0},{9,1},... | collective-permute-start | bytes 589832 | tf_op jit(solution)/shard_map/ppermute | solution.py:222
  102.1 13.5 %collective-permute-start.15 = (s16[496,256]{1,0:T(8,128)(2,1)S(1)}, s16[496,256]{1,0:T(8,128)(2,1)S(1)}, u32[]{:S(2)}, u32[]{:S(2)}) collective-permute-start(s16[496,256]{1,0:T(8,128)(2,1)S(1)} %get-tuple-element.117), channel_id=1, source_target_pairs={{0,4},{1,5},{2,6},{3,7},{4,0},{5,1},{6,2},{7,3},{8,12},{9,13},{10,... | collective-permute-start | bytes 761864 | tf_op jit(solution)/shard_map/ppermute | solution.py:222
  103.4 57.9 %collective-permute-start.23 = (bf16[4,400,256]{2,1,0:T(8,128)(2,1)}, bf16[4,400,256]{2,1,0:T(8,128)(2,1)S(1)}, u32[]{:S(2)}, u32[]{:S(2)}) collective-permute-start(bf16[4,400,256]{2,1,0:T(8,128)(2,1)} %get-tuple-element.136), channel_id=1, source_target_pairs={{0,8},{1,9},{2,10},{3,11},{4,12},{5,13},{6,14},{7,15},{8,0},{9,1},... | collective-permute-start | bytes 2457608 | tf_op jit(solution)/shard_map/ppermute | solution.py:222
  111.0 4.6 %copy-start.63 = (s16[256,384]{1,0:T(8,128)(2,1)}, s16[256,384]{1,0:T(8,128)(2,1)S(1)}, u32[]{:S(2)}) copy-start(s16[256,384]{1,0:T(8,128)(2,1)S(1)} %collective-permute-done.14.refs_1_) | copy-start | bytes 589828
  111.0 13.0 %collective-permute-start.16 = (s16[976,256]{1,0:T(8,128)(2,1)}, s16[976,256]{1,0:T(8,128)(2,1)S(1)}, u32[]{:S(2)}, u32[]{:S(2)}) collective-permute-start(s16[976,256]{1,0:T(8,128)(2,1)} %get-tuple-element.123), channel_id=1, source_target_pairs={{0,2},{1,3},{2,0},{3,1},{4,6},{5,7},{6,4},{7,5},{8,10},{9,11},{10,... | collective-permute-start | bytes 1499144 | tf_op jit(solution)/shard_map/ppermute | solution.py:222
  119.8 31.6 %collective-permute-start.18 = (s16[496,256]{1,0:T(8,128)(2,1)S(1)}, s16[496,256]{1,0:T(8,128)(2,1)S(1)}, u32[]{:S(2)}, u32[]{:S(2)}) collective-permute-start(s16[496,256]{1,0:T(8,128)(2,1)S(1)} %get-tuple-element.126), channel_id=1, source_target_pairs={{0,4},{1,5},{2,6},{3,7},{4,0},{5,1},{6,2},{7,3},{8,12},{9,13},{10,... | collective-permute-start | bytes 761864 | tf_op jit(solution)/shard_map/ppermute | solution.py:222
  121.4 31.4 %copy-start.81 = (bf16[192,256]{1,0:T(8,128)(2,1)}, bf16[192,256]{1,0:T(8,128)(2,1)S(1)}, u32[]{:S(2)}) copy-start(bf16[192,256]{1,0:T(8,128)(2,1)S(1)} %get-tuple-element.119) | copy-start | bytes 294916
  121.4 2.6 collective-permute-start.19
  122.4 29.0 %collective-permute-start.17 = (s16[256,256]{1,0:T(8,128)(2,1)S(1)}, s16[256,256]{1,0:T(8,128)(2,1)S(1)}, u32[]{:S(2)}, u32[]{:S(2)}) collective-permute-start(s16[256,256]{1,0:T(8,128)(2,1)S(1)} %get-tuple-element.124), channel_id=1, source_target_pairs={{0,8},{1,9},{2,10},{3,11},{4,12},{5,13},{6,14},{7,15},{8,0},{9,1},... | collective-permute-start | bytes 393224 | tf_op jit(solution)/shard_map/ppermute | solution.py:222
  124.0 27.4 %copy-start.19 = (s16[976,256]{1,0:T(8,128)(2,1)}, s16[976,256]{1,0:T(8,128)(2,1)S(1)}, u32[]{:S(2)}) copy-start(s16[976,256]{1,0:T(8,128)(2,1)S(1)} %collective-permute-done.16.refs_0_) | copy-start | bytes 1499140
  124.0 27.4 %copy-start.84 = (bf16[192,128]{1,0:T(8,128)(2,1)}, bf16[192,128]{1,0:T(8,128)(2,1)S(1)}, u32[]{:S(2)}) copy-start(bf16[192,128]{1,0:T(8,128)(2,1)S(1)} %collective-permute-done.19.refs_3_) | copy-start | bytes 147460
  152.8 4.1 %copy-start.86 = (s32[16,16]{1,0:T(8,128)S(1)}, s32[16,16]{1,0:T(8,128)}, u32[]{:S(2)}) copy-start(s32[16,16]{1,0:T(8,128)} %param.16) | copy-start | bytes 3076
  156.8 11.8 %copy-start.85 = (bf16[192,128]{1,0:T(8,128)(2,1)S(1)}, bf16[192,128]{1,0:T(8,128)(2,1)}, u32[]{:S(2)}) copy-start(bf16[192,128]{1,0:T(8,128)(2,1)} %get-tuple-element.142) | copy-start | bytes 147460
  156.8 10.9 %collective-permute-start.21 = (s16[496,256]{1,0:T(8,128)(2,1)}, s16[496,256]{1,0:T(8,128)(2,1)S(1)}, u32[]{:S(2)}, u32[]{:S(2)}) collective-permute-start(s16[496,256]{1,0:T(8,128)(2,1)} %get-tuple-element.134), channel_id=1, source_target_pairs={{0,4},{1,5},{2,6},{3,7},{4,0},{5,1},{6,2},{7,3},{8,12},{9,13},{10,... | collective-permute-start | bytes 761864 | tf_op jit(solution)/shard_map/ppermute | solution.py:222
  158.0 7.5 %collective-permute-start.22 = (s16[256,256]{1,0:T(8,128)(2,1)S(1)}, s16[256,256]{1,0:T(8,128)(2,1)S(1)}, u32[]{:S(2)}, u32[]{:S(2)}) collective-permute-start(s16[256,256]{1,0:T(8,128)(2,1)S(1)} %get-tuple-element.135), channel_id=1, source_target_pairs={{0,8},{1,9},{2,10},{3,11},{4,12},{5,13},{6,14},{7,15},{8,0},{9,1},... | collective-permute-start | bytes 393224 | tf_op jit(solution)/shard_map/ppermute | solution.py:222
  161.3 6.4 %copy-start.24 = (bf16[4,400,256]{2,1,0:T(8,128)(2,1)}, bf16[4,400,256]{2,1,0:T(8,128)(2,1)S(1)}, u32[]{:S(2)}) copy-start(bf16[4,400,256]{2,1,0:T(8,128)(2,1)S(1)} %collective-permute-done.23.refs_2_) | copy-start | bytes 2457604
  168.4 13.0 %collective-permute-start.25 = (bf16[4,400,256]{2,1,0:T(8,128)(2,1)}, bf16[4,400,256]{2,1,0:T(8,128)(2,1)}, u32[]{:S(2)}, u32[]{:S(2)}) collective-permute-start(bf16[4,400,256]{2,1,0:T(8,128)(2,1)} %get-tuple-element.143.own_far), channel_id=1, source_target_pairs={{0,1},{1,0},{2,3},{3,2},{4,5},{5,4},{6,7},{7,6},{8,9},{9,8},{10,11... | collective-permute-start | bytes 2457608 | tf_op jit(solution)/shard_map/ppermute | solution.py:222
  171.2 6.8 %copy-start.62 = (f32[1,192,256]{2,1,0:T(8,128)S(1)}, f32[1,192,256]{2,1,0:T(8,128)}, u32[]{:S(2)}) copy-start(f32[1,192,256]{2,1,0:T(8,128)} %copy-done.60) | copy-start | bytes 589828
  171.2 6.8 %copy-start.66 = (s16[256,256]{1,0:T(8,128)(2,1)S(1)}, s16[256,256]{1,0:T(8,128)(2,1)}, u32[]{:S(2)}) copy-start(s16[256,256]{1,0:T(8,128)(2,1)} %get-tuple-element.137.landed) | copy-start | bytes 393220
  171.4 9.7 %collective-permute-start.24 = (s16[256,256]{1,0:T(8,128)(2,1)S(1)}, s16[256,256]{1,0:T(8,128)(2,1)S(1)}, u32[]{:S(2)}, u32[]{:S(2)}) collective-permute-start(s16[256,256]{1,0:T(8,128)(2,1)S(1)} %get-tuple-element.141), channel_id=1, source_target_pairs={{0,8},{1,9},{2,10},{3,11},{4,12},{5,13},{6,14},{7,15},{8,0},{9,1},... | collective-permute-start | bytes 393224 | tf_op jit(solution)/shard_map/ppermute | solution.py:222
  177.0 4.2 %copy-start.82 = (bf16[192,256]{1,0:T(8,128)(2,1)S(1)}, bf16[192,256]{1,0:T(8,128)(2,1)}, u32[]{:S(2)}) copy-start(bf16[192,256]{1,0:T(8,128)(2,1)} %copy-done.81) | copy-start | bytes 294916
  193.2 17.9 %collective-permute-start.26 = (bf16[192,1024]{1,0:T(8,128)(2,1)S(1)}, bf16[192,1024]{1,0:T(8,128)(2,1)}, u32[]{:S(2)}, u32[]{:S(2)}) collective-permute-start(bf16[192,1024]{1,0:T(8,128)(2,1)S(1)} %bitcast.62), channel_id=1, source_target_pairs={{0,4},{1,5},{2,6},{3,7},{4,0},{5,1},{6,2},{7,3},{8,12},{9,13},{10,... | collective-permute-start | bytes 1179656 | tf_op jit(solution)/shard_map/ppermute | solution.py:222
  193.3 17.8 %collective-permute-start.27 = (bf16[192,1024]{1,0:T(8,128)(2,1)S(1)}, bf16[192,1024]{1,0:T(8,128)(2,1)S(1)}, u32[]{:S(2)}, u32[]{:S(2)}) collective-permute-start(bf16[192,1024]{1,0:T(8,128)(2,1)S(1)} %bitcast.63), channel_id=1, source_target_pairs={{0,2},{1,3},{2,0},{3,1},{4,6},{5,7},{6,4},{7,5},{8,10},{9,11},{10,... | collective-permute-start | bytes 1179656 | tf_op jit(solution)/shard_map/ppermute | solution.py:222
  194.8 20.0 %collective-permute-start.28 = (bf16[192,1024]{1,0:T(8,128)(2,1)S(1)}, bf16[192,1024]{1,0:T(8,128)(2,1)}, u32[]{:S(2)}, u32[]{:S(2)}) collective-permute-start(bf16[192,1024]{1,0:T(8,128)(2,1)S(1)} %bitcast.64), channel_id=1, source_target_pairs={{0,8},{1,9},{2,10},{3,11},{4,12},{5,13},{6,14},{7,15},{8,0},{9,1},... | collective-permute-start | bytes 1179656 | tf_op jit(solution)/shard_map/ppermute | solution.py:222
  197.7 17.1 %collective-permute-start.29 = (bf16[192,1024]{1,0:T(8,128)(2,1)S(1)}, bf16[192,1024]{1,0:T(8,128)(2,1)S(1)}, u32[]{:S(2)}, u32[]{:S(2)}) collective-permute-start(bf16[192,1024]{1,0:T(8,128)(2,1)S(1)} %bitcast.65), channel_id=1, source_target_pairs={{0,1},{1,0},{2,3},{3,2},{4,5},{5,4},{6,7},{7,6},{8,9},{9,8},{10,11... | collective-permute-start | bytes 1179656 | tf_op jit(solution)/shard_map/ppermute | solution.py:222
  211.1 3.6 %copy-start.83 = (bf16[192,1024]{1,0:T(8,128)(2,1)}, bf16[192,1024]{1,0:T(8,128)(2,1)S(1)}, u32[]{:S(2)}) copy-start(bf16[192,1024]{1,0:T(8,128)(2,1)S(1)} %collective-permute-done.27.refs_1_) | copy-start | bytes 1179652
  215.5 6.1 %copy-start.50 = (bf16[192,1024]{1,0:T(8,128)(2,1)S(1)}, bf16[192,1024]{1,0:T(8,128)(2,1)}, u32[]{:S(2)}) copy-start(bf16[192,1024]{1,0:T(8,128)(2,1)} %get-tuple-element.148.refs_1_) | copy-start | bytes 1179652
  216.9 22.5 %collective-permute-start.33 = (bf16[3,192,1024]{2,1,0:T(8,128)(2,1)S(1)}, bf16[3,192,1024]{2,1,0:T(8,128)(2,1)S(1)}, u32[]{:S(2)}, u32[]{:S(2)}) collective-permute-start(bf16[3,192,1024]{2,1,0:T(8,128)(2,1)S(1)} %pad_maximum_fusion.refs_0_), channel_id=1, source_target_pairs={{0,1},{1,0},{2,3},{3,2},{4,5},{5,4},{6,7},{7,6},{8,9},{9,8},{10,11... | collective-permute-start | bytes 3538952 | tf_op jit(solution)/shard_map/ppermute | solution.py:222
  217.0 13.5 %collective-permute-start.32 = (bf16[192,1024]{1,0:T(8,128)(2,1)S(1)}, bf16[192,1024]{1,0:T(8,128)(2,1)}, u32[]{:S(2)}, u32[]{:S(2)}) collective-permute-start(bf16[192,1024]{1,0:T(8,128)(2,1)S(1)} %bitcast.66), channel_id=1, source_target_pairs={{0,12},{1,13},{2,14},{3,15},{4,8},{5,9},{6,10},{7,11},{8,4},{9,5},... | collective-permute-start | bytes 1179656 | tf_op jit(solution)/shard_map/ppermute | solution.py:222
  219.5 12.3 %collective-permute-start.30 = (bf16[192,1024]{1,0:T(8,128)(2,1)}, bf16[192,1024]{1,0:T(8,128)(2,1)}, u32[]{:S(2)}, u32[]{:S(2)}) collective-permute-start(bf16[192,1024]{1,0:T(8,128)(2,1)} %get-tuple-element.145), channel_id=1, source_target_pairs={{0,2},{1,3},{2,0},{3,1},{4,6},{5,7},{6,4},{7,5},{8,10},{9,11},{10,... | collective-permute-start | bytes 1179656 | tf_op jit(solution)/shard_map/ppermute | solution.py:222
  220.0 19.4 %collective-permute-start.31 = (bf16[192,1024]{1,0:T(8,128)(2,1)}, bf16[192,1024]{1,0:T(8,128)(2,1)}, u32[]{:S(2)}, u32[]{:S(2)}) collective-permute-start(bf16[192,1024]{1,0:T(8,128)(2,1)} %get-tuple-element.146), channel_id=1, source_target_pairs={{0,2},{1,3},{2,0},{3,1},{4,6},{5,7},{6,4},{7,5},{8,10},{9,11},{10,... | collective-permute-start | bytes 1179656 | tf_op jit(solution)/shard_map/ppermute | solution.py:222
  240.5 3.1 %copy-start.7 = (f32[192,1024]{1,0:T(8,128)S(1)}, f32[192,1024]{1,0:T(8,128)}, u32[]{:S(2)}) copy-start(f32[192,1024]{1,0:T(8,128)} %get-tuple-element.153.refs_3_) | copy-start | bytes 2359300
  240.5 3.1 %copy-start.16 = (bf16[3,192,1024]{2,1,0:T(8,128)(2,1)S(1)}, bf16[3,192,1024]{2,1,0:T(8,128)(2,1)}, u32[]{:S(2)}) copy-start(bf16[3,192,1024]{2,1,0:T(8,128)(2,1)} %get-tuple-element.152.refs_1_) | copy-start | bytes 3538948
  243.0 11.7 %collective-permute-start.35 = (bf16[3,192,1024]{2,1,0:T(8,128)(2,1)}, bf16[3,192,1024]{2,1,0:T(8,128)(2,1)}, u32[]{:S(2)}, u32[]{:S(2)}) collective-permute-start(bf16[3,192,1024]{2,1,0:T(8,128)(2,1)} %pad_maximum_fusion.1.refs_0_), channel_id=1, source_target_pairs={{0,1},{1,0},{2,3},{3,2},{4,5},{5,4},{6,7},{7,6},{8,9},{9,8},{10,11... | collective-permute-start | bytes 3538952 | tf_op jit(solution)/shard_map/ppermute | solution.py:222
  243.0 11.7 %collective-permute-start.34 = (bf16[192,1024]{1,0:T(8,128)(2,1)}, bf16[192,1024]{1,0:T(8,128)(2,1)S(1)}, u32[]{:S(2)}, u32[]{:S(2)}) collective-permute-start(bf16[192,1024]{1,0:T(8,128)(2,1)} %get-tuple-element.149), channel_id=1, source_target_pairs={{0,2},{1,3},{2,0},{3,1},{4,6},{5,7},{6,4},{7,5},{8,10},{9,11},{10,... | collective-permute-start | bytes 1179656 | tf_op jit(solution)/shard_map/ppermute | solution.py:222
  255.5 8.7 %collective-permute-start.36 = (bf16[192,1024]{1,0:T(8,128)(2,1)}, bf16[192,1024]{1,0:T(8,128)(2,1)S(1)}, u32[]{:S(2)}, u32[]{:S(2)}) collective-permute-start(bf16[192,1024]{1,0:T(8,128)(2,1)} %get-tuple-element.154.refs_0_), channel_id=1, source_target_pairs={{0,1},{1,0},{2,3},{3,2},{4,5},{5,4},{6,7},{7,6},{8,9},{9,8},{10,11... | collective-permute-start | bytes 1179656 | tf_op jit(solution)/shard_map/ppermute | solution.py:222
  256.8 7.4 %copy-start.48 = (bf16[192,1024]{1,0:T(8,128)(2,1)S(1)}, bf16[192,1024]{1,0:T(8,128)(2,1)}, u32[]{:S(2)}) copy-start(bf16[192,1024]{1,0:T(8,128)(2,1)} %get-tuple-element.154.refs_0_) | copy-start | bytes 1179652
  (62 other events, 77.0 us)

commit v6 on v5

--- a/solution.py
+++ b/solution.py
@@ -207,7 +207,7 @@
     return jnp.concatenate(outputs, 0)
 
 
-MIB = 1024 * 1024
+VMEM_LIMIT = 66977792
 SHORT = pl.CostEstimate(flops=1, bytes_accessed=1, transcendentals=0)
 LOW_BITS = 4
 PACKED = 16 // LOW_BITS
@@ -222,21 +222,26 @@
     return lax.ppermute(value, "tensor", [(i, i ^ bit) for i in range(devices)])
 
 
+def in_hbm(*arrays):
+    return [pltpu.with_memory_space_constraint(a, pltpu.HBM) for a in arrays]
+
+
 def no_work(*refs):
     del refs
 
 
-def together(*arrays):
+def together(arrays, after):
     anywhere = pl.BlockSpec(memory_space=pl.ANY)
     return pl.pallas_call(
         no_work,
-        in_specs=[anywhere] * len(arrays),
+        in_specs=[anywhere] * (len(arrays) + len(after)),
         out_specs=[anywhere] * len(arrays),
-        out_shape=[jax.ShapeDtypeStruct(a.shape, a.dtype) for a in arrays],
+        out_shape=[pltpu.HBM(a.shape, a.dtype) for a in arrays],
         input_output_aliases={i: i for i in range(len(arrays))},
+        compiler_params=pltpu.CompilerParams(vmem_limit_bytes=VMEM_LIMIT),
         cost_estimate=SHORT,
         name="together",
-    )(*arrays)
+    )(*in_hbm(*arrays), *after)
 
 
 def coded_rows(rows):
@@ -344,13 +349,13 @@
             ],
         ),
         out_shape=[
-            jax.ShapeDtypeStruct((KVH, rows, columns), jnp.float32),
-            jax.ShapeDtypeStruct((sent_rows, columns), jnp.int16),
+            pltpu.HBM((KVH, rows, columns), jnp.float32),
+            pltpu.HBM((sent_rows, columns), jnp.int16),
         ],
-        compiler_params=pltpu.CompilerParams(vmem_limit_bytes=24 * MIB),
+        compiler_params=pltpu.CompilerParams(vmem_limit_bytes=VMEM_LIMIT),
         cost_estimate=SHORT,
         name="project",
-    )(core, normed, qkv_weight, *after)
+    )(core, normed, *in_hbm(qkv_weight), *after)
 
 
 def fold_kernel(steps, bit, held, landed, landed_powers, *refs):
@@ -395,13 +400,13 @@
             scratch_shapes=[pltpu.VMEM((TILE, columns), jnp.float32)],
         ),
         out_shape=[
-            jax.ShapeDtypeStruct((steps, rows, columns), jnp.float32),
-            jax.ShapeDtypeStruct((steps * coded + TILE, columns), jnp.int16),
+            pltpu.HBM((steps, rows, columns), jnp.float32),
+            pltpu.HBM((steps * coded + TILE, columns), jnp.int16),
         ],
-        compiler_params=pltpu.CompilerParams(vmem_limit_bytes=12 * MIB),
+        compiler_params=pltpu.CompilerParams(vmem_limit_bytes=VMEM_LIMIT),
         cost_estimate=SHORT,
         name="fold",
-    )(bit, held, landed, landed, *after)
+    )(bit, *in_hbm(held), landed, landed, *after)
 
 
 def finish_kernel(after_count, core, held, landed, cosine, sine, *refs):
@@ -428,9 +433,9 @@
 def finish(core, held, landed, cosine, sine, after):
     _, rows, columns = held.shape
     whole = pl.BlockSpec(memory_space=pltpu.VMEM)
-    shapes = [jax.ShapeDtypeStruct((rows, 2 * HD), jnp.bfloat16)]
+    shapes = [pltpu.HBM((rows, 2 * HD), jnp.bfloat16)]
     if columns > 2 * HD:
-        shapes.append(jax.ShapeDtypeStruct((rows, HD), jnp.bfloat16))
+        shapes.append(pltpu.HBM((rows, HD), jnp.bfloat16))
     return pl.pallas_call(
         functools.partial(finish_kernel, len(after)),
         in_specs=[pl.BlockSpec(memory_space=pltpu.SMEM)]
@@ -438,10 +443,10 @@
         + [pl.BlockSpec(memory_space=pl.ANY)] * len(after),
         out_specs=[whole] * len(shapes),
         out_shape=shapes,
-        compiler_params=pltpu.CompilerParams(vmem_limit_bytes=6 * MIB),
+        compiler_params=pltpu.CompilerParams(vmem_limit_bytes=VMEM_LIMIT),
         cost_estimate=SHORT,
         name="finish",
-    )(core, held, landed, cosine, sine, *after)
+    )(core, *in_hbm(held), landed, *in_hbm(cosine, sine), *after)
 
 
 def mix_kernel(count, places, *refs):
@@ -495,11 +500,34 @@
             pltpu.VMEM((count, width, columns), jnp.bfloat16),
             pltpu.SemaphoreType.DMA((count,)),
         ],
-        out_shape=jax.ShapeDtypeStruct((rows, columns), dtype),
-        compiler_params=pltpu.CompilerParams(vmem_limit_bytes=32 * MIB),
+        out_shape=pltpu.HBM((rows, columns), dtype),
+        compiler_params=pltpu.CompilerParams(vmem_limit_bytes=VMEM_LIMIT),
         cost_estimate=SHORT,
         name="mix",
-    )(places, *pieces, out_weight, start)
+    )(places, *pieces, *in_hbm(out_weight, start))
+
+
+def pack_kernel(groups, count, *refs):
+    flat = []
+    for ref in refs[:count]:
+        flat += [ref] if len(ref.shape) == 2 else [ref.at[i] for i in range(ref.shape[0])]
+    for group, target in zip(groups, refs[-len(groups) :]):
+        for place, index in enumerate(group):
+            target[place] = flat[index][...]
+
+
+def pack(pieces, groups, after):
+    whole = pl.BlockSpec(memory_space=pltpu.VMEM)
+    shape = pieces[0].shape[-2:]
+    return pl.pallas_call(
+        functools.partial(pack_kernel, groups, len(pieces)),
+        in_specs=[whole] * len(pieces) + [pl.BlockSpec(memory_space=pl.ANY)] * len(after),
+        out_specs=[whole] * len(groups),
+        out_shape=[pltpu.HBM((len(g),) + shape, pieces[0].dtype) for g in groups],
+        compiler_params=pltpu.CompilerParams(vmem_limit_bytes=VMEM_LIMIT),
+        cost_estimate=SHORT,
+        name="pack",
+    )(*pieces, *after)
 
 
 def gather_and_mix(attention, out_weight, start, device):
@@ -511,26 +539,22 @@
     across = swap(attention, 2)
     far = swap(attention, 8)
     partner = swap(attention, 1)
-    near, across, far, partner = together(near, across, far, partner)
-
-    across_near = swap(near, 2)
-    across_far = swap(far, 2)
+    first, onward = pack([near, across, far], [(0, 1, 2), (0, 2)], [partner])
+    (attention,) = together([attention], [onward])
+
+    across_onward = swap(onward, 2)
     farthest = swap(attention, 12)
-    first = jnp.stack([near, across, far])
     first_partner = swap(first, 1)
     mixed = add(start, [attention, partner], (0, 1))
-    across_near, across_far, farthest, first_partner, mixed = together(
-        across_near, across_far, farthest, first_partner, mixed
-    )
+    mixed = add(mixed, [first, first_partner], (4, 2, 8, 5, 3, 9))
+    (second,) = pack([across_onward, farthest], [(0, 1, 2)], [mixed])
 
     last = swap(farthest, 2)
-    second = jnp.stack([across_near, across_far, farthest])
     second_partner = swap(second, 1)
-    mixed = add(mixed, [first, first_partner], (4, 2, 8, 5, 3, 9))
-    last, second_partner, mixed = together(last, second_partner, mixed)
+    mixed = add(mixed, [second, second_partner], (6, 10, 12, 7, 11, 13))
+    (last,) = together([last], [mixed])
 
     last_partner = swap(last, 1)
-    mixed = add(mixed, [second, second_partner], (6, 10, 12, 7, 11, 13))
     return add(mixed, [last, last_partner], (14, 15), jnp.bfloat16)
 
 
@@ -623,10 +647,10 @@
         attend_kernel,
         in_specs=[pl.BlockSpec(memory_space=pltpu.SMEM)] + [whole] * len(arrays),
         out_specs=whole,
-        out_shape=jax.ShapeDtypeStruct((requests, count, HD), jnp.bfloat16),
+        out_shape=pltpu.HBM((requests, count, HD), jnp.bfloat16),
         scratch_shapes=[pltpu.VMEM((slots, count, HD), jnp.float32)] * 3
         + [pltpu.VMEM((requests, count, HD), jnp.float32)] * 3,
-        compiler_params=pltpu.CompilerParams(vmem_limit_bytes=24 * MIB),
+        compiler_params=pltpu.CompilerParams(vmem_limit_bytes=VMEM_LIMIT),
         cost_estimate=SHORT,
         name="attend",
     )(slot_request, *arrays)
@@ -655,75 +679,70 @@
         target[0, slots * BLK :, :] = scale[0]
 
 
-def arrange(chip, cache_pool, scales, after):
+def arrange(chip, cache_pool, scales, first, after):
     slots = cache_pool.shape[0]
     pool = [
         pl.BlockSpec(
-            (slots, 1, BLK, 2 * HD), lambda i, c, side=side: (0, c[0] ^ (2 * i + side), 0, 0)
+            (slots, 1, BLK, 2 * HD), lambda i, c, side=side: (0, c[0] ^ (first + 2 * i + side), 0, 0)
         )
         for side in (0, 1)
     ]
     scale = [
-        pl.BlockSpec((1, TILE, 2 * HD), lambda i, c, side=side: (c[0] ^ (2 * i + side), 0, 0))
+        pl.BlockSpec((1, TILE, 2 * HD), lambda i, c, side=side: (c[0] ^ (first + 2 * i + side), 0, 0))
         for side in (0, 1)
     ]
     rows = slots * BLK + TILE
     out = pl.BlockSpec((1, rows, 2 * HD), lambda i, c: (i, 0, 0))
-    shape = jax.ShapeDtypeStruct((KVH // 2, rows, 2 * HD), jnp.bfloat16)
+    shape = pltpu.HBM((KVH // 4, rows, 2 * HD), jnp.bfloat16)
     return pl.pallas_call(
         arrange_kernel,
         grid_spec=pltpu.PrefetchScalarGridSpec(
             num_scalar_prefetch=1,
-            grid=(KVH // 2,),
+            grid=(KVH // 4,),
             in_specs=pool + scale + [pl.BlockSpec(memory_space=pl.ANY)],
             out_specs=[out, out],
         ),
         out_shape=[shape, shape],
-        compiler_params=pltpu.CompilerParams(vmem_limit_bytes=6 * MIB),
+        compiler_params=pltpu.CompilerParams(vmem_limit_bytes=VMEM_LIMIT),
         cost_estimate=SHORT,
         name="arrange",
-    )(chip, cache_pool, cache_pool, scales, scales, after)
-
-
-HANDOVER_BITS = (1, 2, 4)
+    )(chip, *in_hbm(cache_pool, cache_pool, scales, scales), after)
 
 
 def handover_plan():
-    kept = [(0, dest) for dest in range(0, KVH, 2)]
-    landed = [(1, dest) for dest in range(0, KVH, 2)]
+    arrays = [[(0, 0), (0, 2)], [(0, 4), (0, 6)], [(1, 0), (1, 2)], [(1, 4), (1, 6)]]
     splits = []
-    for bit in HANDOVER_BITS[1:]:
-        entries = [(0, i, e) for i, e in enumerate(kept)] + [
-            (1, i, e) for i, e in enumerate(landed)
-        ]
+    for bit, parts in ((4, 2), (2, 1)):
+        entries = [(a, i, e) for a, part in enumerate(arrays) for i, e in enumerate(part)]
         stay = [e for e in entries if not e[2][1] & bit]
         leave = [e for e in entries if e[2][1] & bit]
-        splits.append(tuple(tuple((side, i) for side, i, _ in part) for part in (stay, leave)))
-        kept = [e for _, _, e in stay]
-        landed = [(source ^ bit, dest ^ bit) for _, _, (source, dest) in leave]
-    return splits, [source for source, _ in kept + landed]
-
-
-def regroup_kernel(index_of, kept, landed, *refs):
-    out_kept, out_sent = refs[-2:]
-    for target, (source, index) in enumerate(index_of[0]):
-        out_kept[target] = (kept, landed)[source][index]
-    for target, (source, index) in enumerate(index_of[1]):
-        out_sent[target] = (kept, landed)[source][index]
-
-
-def regroup(index_of, kept, landed, after):
+        size = len(leave) // parts
+        groups = [stay] + [leave[i : i + size] for i in range(0, len(leave), size)]
+        splits.append([[(a, i) for a, i, _ in group] for group in groups])
+        arrays = [[e for _, _, e in stay]]
+        arrays += [[(x ^ bit, y ^ bit) for _, _, (x, y) in group] for group in groups[1:]]
+    return splits, [source for part in arrays for source, _ in part]
+
+
+def regroup_kernel(groups, count, *refs):
+    sources, targets = refs[:count], refs[-len(groups) :]
+    for group, target in zip(groups, targets):
+        for place, (array, index) in enumerate(group):
+            target[place] = sources[array][index]
+
+
+def regroup(groups, sources, after):
     whole = pl.BlockSpec(memory_space=pltpu.VMEM)
-    shape = jax.ShapeDtypeStruct(kept.shape, kept.dtype)
+    rows = sources[0].shape[1:]
     return pl.pallas_call(
-        functools.partial(regroup_kernel, index_of),
-        in_specs=[whole, whole] + [pl.BlockSpec(memory_space=pl.ANY)] * len(after),
-        out_specs=[whole, whole],
-        out_shape=[shape, shape],
-        compiler_params=pltpu.CompilerParams(vmem_limit_bytes=8 * MIB),
+        functools.partial(regroup_kernel, groups, len(sources)),
+        in_specs=[whole] * len(sources) + [pl.BlockSpec(memory_space=pl.ANY)] * len(after),
+        out_specs=[whole] * len(groups),
+        out_shape=[pltpu.HBM((len(g),) + rows, sources[0].dtype) for g in groups],
+        compiler_params=pltpu.CompilerParams(vmem_limit_bytes=VMEM_LIMIT),
         cost_estimate=SHORT,
         name="regroup",
-    )(kept, landed, *after)
+    )(*sources, *after)
 
 
 def local_pairs(
@@ -756,11 +775,13 @@
     )
     chip_scalar = jnp.reshape(chip, (1,)).astype(jnp.int32)
     sums = sums + swap(sums, 2)
-    cache_kept, cache_sent = arrange(chip_scalar, cache_pool, scale_rows, sums)
-    cache_landed = swap(cache_sent, 2)
+    kept_a, sent_a = arrange(chip_scalar, cache_pool, scale_rows, 0, sums)
+    landed_a = swap(sent_a, 2)
+    kept_b, sent_b = arrange(chip_scalar, cache_pool, scale_rows, KVH // 2, sent_a)
     for bit in (1, 4, 8):
         sums = sums + swap(sums, bit)
-    sums, cache_landed = together(sums, cache_landed)
+    (sent_b,) = together([sent_b], [sums, landed_a])
+    landed_b = swap(sent_b, 2)
     normed = (
         hidden * lax.rsqrt(sums[..., None] / D + EPSILON) * norm_gain.astype(jnp.float32)
     ).astype(jnp.bfloat16)
@@ -794,59 +815,60 @@
     def finished(chunk, landed, *after):
         return finish(bits[0], held[chunk], landed, cosine, sine, after)
 
-    projected(0, cache_kept)
+    projected(0, sent_b)
     core_0 = hop(0, 0)
     projected(1, held[0])
-    core_0, sent[1] = together(core_0, sent[1])
-
-    folded(0, 1, core_0)
+    (sent[1],) = together([sent[1]], [core_0, landed_b])
+
+    folded(0, 1, core_0, sent[1])
     core_1, y_0 = hop(1, 0), hop(0, 1)
-    cache_kept, cache_sent = regroup(splits[0], cache_kept, cache_landed, (held[0],))
-    cache_landed = swap(cache_sent, 4)
+    cache_kept, sent_a, sent_b = regroup(
+        splits[0], (kept_a, kept_b, landed_a, landed_b), (held[0],)
+    )
+    landed_a = swap(sent_a, 8)
     projected(2, held[0], cache_kept)
     projected(3, held[2])
-    core_1, y_0, sent[2], sent[3], cache_landed = together(
-        core_1, y_0, sent[2], sent[3], cache_landed
+    sent[2], sent[3], sent_b = together(
+        [sent[2], sent[3], sent_b], [core_1, y_0, landed_a]
     )
 
     core_2, core_3 = hop(2, 0), hop(3, 0)
-    folded(1, 1, core_1)
+    landed_b = swap(sent_b, 8)
+    folded(1, 1, core_1, sent[2])
     y_1 = hop(1, 1)
     folded(0, 2, y_0, held[1])
     near_0 = hop(0, 2)
-    cache_kept, cache_sent = regroup(splits[1], cache_kept, cache_landed, (held[0],))
-    cache_landed = swap(cache_sent, 8)
-    folded(2, 1, core_2, cache_kept)
+    folded(2, 1, core_2, held[0])
     folded(3, 1, core_3, held[2])
-    y_1, near_0, sent[2], sent[3] = together(y_1, near_0, sent[2], sent[3])
+    sent[2], sent[3] = together([sent[2], sent[3]], [y_1, near_0, landed_b])
 
     y_2 = hop(2, 1)
-    folded(0, 3, near_0)
+    folded(0, 3, near_0, sent[2])
     far_0 = hop(0, 3)
-    folded(1, 2, y_1)
+    folded(1, 2, y_1, sent[2])
     near_1 = hop(1, 2)
-    y_2, far_0, near_1 = together(y_2, far_0, near_1)
+    cache_kept, cache_sent = regroup(splits[1], (cache_kept, landed_a, landed_b), (held[1],))
+    cache_landed = swap(cache_sent, 4)
+    sent[3], cache_kept = together([sent[3], cache_kept], [y_2, far_0, near_1, cache_landed])
 
     y_3 = hop(3, 1)
-    folded(1, 3, near_1)
+    folded(1, 3, near_1, sent[3])
     far_1 = hop(1, 3)
-    folded(2, 2, y_2)
+    folded(2, 2, y_2, sent[3])
     near_2 = hop(2, 2)
     query_chunks = [None] * count
-    query_chunks[0], pair = finished(0, far_0, cache_kept)
+    query_chunks[0], pair = finished(0, far_0, held[2])
     pair_other = swap(pair, 1)
     kept_other = swap(cache_kept, 1)
-    y_3, far_1, near_2, pair_other, kept_other = together(
-        y_3, far_1, near_2, pair_other, kept_other
-    )
+    landed_other = swap(cache_landed, 1)
+    (held[3],) = together([held[3]], [y_3, far_1, near_2, pair_other, kept_other, landed_other])
 
     folded(3, 2, y_3)
     near_3 = hop(3, 2)
-    folded(2, 3, near_2)
+    folded(2, 3, near_2, held[3])
     far_2 = hop(2, 3)
     (query_chunks[1],) = finished(1, far_1, held[2])
-    near_3, far_2, cache_landed = together(near_3, far_2, cache_landed)
-    landed_other = swap(cache_landed, 1)
+    (held[3],) = together([held[3]], [near_3, far_2])
 
     folded(3, 3, near_3)
     far_3 = hop(3, 3)

time: 270 us -> 280 us (1.037)
  Pallas kernels: 72.1 us -> 129 us
  local copies, waits for them, and re-layouts: 47.4 us -> 13.2 us
  waiting for transfers between devices: 98.9 us -> 91.4 us
  starting transfers between devices: 38.1 us -> 34.1 us
    unnamed x180 -> x24, local copies, waits for them, and re-layouts: 42.8 us -> 0.92 us
    pallas_call x12, Pallas kernels: 14.5 us -> 35.1 us  [fold(): pl.pallas_call(functools.partial(fold_kernel, steps), grid_spec=pltpu.Pre...]
    pallas_call x12 -> x13, Pallas kernels: 1.16 us -> 10.2 us  [the longest x2 5.19 us: regroup(): pl.pallas_call(functools.partial(regroup_kernel, groups, len(sources)), i...]
    pallas_call x4, Pallas kernels: 24.1 us -> 33 us  [project(): pl.pallas_call(functools.partial(project_kernel, chunk, with_pair), grid_...]
    ppermute x37 -> x38, waiting for transfers between devices: 98.9 us -> 91.4 us  [swap(): return lax.ppermute(value, 'tensor', [(i, i ^ bit) for i in range(devices)])]
    pallas_call x4, Pallas kernels: 0.62 us -> 7.6 us  [finish(): pl.pallas_call(functools.partial(finish_kernel, len(after)), in_specs=[pl...]
    pallas_call x4, Pallas kernels: 21.1 us -> 26.8 us  [mix(): pl.pallas_call(functools.partial(mix_kernel, len(pieces)), in_specs=[pl.B...]
    ppermute x37 -> x38, starting transfers between devices: 38.1 us -> 34.1 us  [swap(): return lax.ppermute(value, 'tensor', [(i, i ^ bit) for i in range(devices)])]
  transfers between devices with their start and end apart: 37 -> 38, of which waited for: 19 -> 20; matrix products, arithmetic and copies ran while one was open for 3% -> 7% of each run, Pallas kernels for 19% -> 30%
where the time goes in v6:
time: 280 us; the launch traced here: 279 us
  Pallas kernels  129 us (46%)
  waiting for transfers between devices  91.4 us (33%)
  starting transfers between devices  34.1 us (12%)
  local copies, waits for them, and re-layouts  13.2 us (5%)
  other arithmetic  11.1 us (4%)
    ppermute x38, waiting for transfers between devices, swap(): return lax.ppermute(value, 'tensor', [(i, i ^ bit) for i in range(devices)])  91.4 us
    pallas_call x12, Pallas kernels, fold(): pl.pallas_call(functools.partial(fold_kernel, steps), grid_spec=pltpu.Pre...  35.1 us
    ppermute x38, starting transfers between devices, swap(): return lax.ppermute(value, 'tensor', [(i, i ^ bit) for i in range(devices)])  34.1 us
    pallas_call x4, Pallas kernels, project(): pl.pallas_call(functools.partial(project_kernel, chunk, with_pair), grid_...  33 us
    pallas_call x4, Pallas kernels, mix(): pl.pallas_call(functools.partial(mix_kernel, len(pieces)), in_specs=[pl.B...  26.8 us
    pallas_call x1, Pallas kernels, attend(): pl.pallas_call(attend_kernel, in_specs=[pl.BlockSpec(memory_space=pltpu.S...  11.7 us
    pallas_call x4, Pallas kernels, finish(): pl.pallas_call(functools.partial(finish_kernel, len(after)), in_specs=[pl...  7.6 us
  transfers between devices with their start and end apart: 38, of which 20 were waited for; matrix products, arithmetic and copies ran while one was open for 7% of the time, Pallas kernels for 30%

profile of v6, /device:TPU:0, one launch (start us, length us, event | category | flops | bytes accessed | tf_op | source)
XLA Modules:
  0.0 278.9 jit_solution(9639795047288231722)
XLA Ops:
  1.2 3.0 %collective-permute-start = (f32[2,96]{1,0:T(2,128)S(1)}, f32[2,96]{1,0:T(2,128)S(1)}, u32[]{:S(2)}, u32[]{:S(2)}) collective-permute-start(f32[2,96]{1,0:T(2,128)S(1)} %fusion), channel_id=1, source_target_pairs={{0,2},{1,3},{2,0},{3,1},{4,6},{5,7},{6,4},{7,5},{8,10},{9,11},{10,... | collective-permute-start | bytes 2312 | tf_op jit(solution)/shard_map/ppermute | solution.py:222
  4.2 1.5 collective-permute-done
  6.9 2.1 collective-permute-start.2
  10.5 3.0 %collective-permute-start.3 = (f32[2,96]{1,0:T(2,128)S(1)}, f32[2,96]{1,0:T(2,128)S(1)}, u32[]{:S(2)}, u32[]{:S(2)}) collective-permute-start(f32[2,96]{1,0:T(2,128)S(1)} %add.121), channel_id=1, source_target_pairs={{0,8},{1,9},{2,10},{3,11},{4,12},{5,13},{6,14},{7,15},{8,0},{9,1},... | collective-permute-start | bytes 2312 | tf_op jit(solution)/shard_map/ppermute | solution.py:222
  14.9 2.1 arrange.2
  17.0 2.1 arrange.3
  19.1 1.5 collective-permute-start.4
  21.2 1.9 fusion.2
  23.1 6.4 %collective-permute-done.4.refs_2_ = bf16[2,400,256]{2,1,0:T(8,128)(2,1)} collective-permute-done((bf16[2,400,256]{2,1,0:T(8,128)(2,1)}, bf16[2,400,256]{2,1,0:T(8,128)(2,1)}, u32[]{:S(2)}, u32[]{:S(2)}) %collective-permute-start.4) | collective-permute-done | bytes 409632 | tf_op jit(solution)/shard_map/ppermute | solution.py:222
  29.6 9.1 %project.4 = (f32[8,192,384]{2,1,0:T(8,128)}, s16[1936,384]{1,0:T(8,128)(2,1)}) custom-call(s32[1]{0:T(128)} %bitcast.2.core, bf16[192,1024]{1,0:T(8,128)(2,1)} %bitcast.51, bf16[1024,18432]{1,0:T(8,128)(2,1)} %weights.7, bf16[2,400,256]{2,1,0:T(8,128)(2,1)} %together.9.refs_0_), custom_call_target="tpu_custom_call" | custom-call | flops 1 | bytes 1 | tf_op jit(solution)/shard_map/project/pallas_call | solution.py:334
  38.8 1.6 collective-permute-start.6
  40.3 8.0 %project.5 = (f32[8,192,256]{2,1,0:T(8,128)}, s16[1936,256]{1,0:T(8,128)(2,1)}) custom-call(s32[1]{0:T(128)} %bitcast.2.core, bf16[192,1024]{1,0:T(8,128)(2,1)} %bitcast.52, bf16[1024,18432]{1,0:T(8,128)(2,1)} %weights.7, f32[8,192,384]{2,1,0:T(8,128)} %get-tuple-element.59.refs_0_.held), custom_call_target="tpu_custom_call" | custom-call | flops 1 | bytes 1 | tf_op jit(solution)/shard_map/project/pallas_call | solution.py:334
  48.3 2.6 collective-permute-done.6.refs_2_.refs_3_
  51.0 4.8 %fold.12 = (f32[4,192,384]{2,1,0:T(8,128)}, s16[976,384]{1,0:T(8,128)(2,1)}) custom-call(s32[1]{0:T(128)} %bitcast.5.bit, f32[8,192,384]{2,1,0:T(8,128)} %get-tuple-element.59.refs_0_.held, s16[1936,384]{1,0:T(8,128)(2,1)} %collective-permute-done.5.refs_1_.landed.landed_powers, s16[1936,384]{1,0:T(8,128)(2,1)} %collective-permute-done.5.refs_1_.landed.landed_powers, ...), custom_call_target="tpu_custom_call" | custom-call | flops 1 | bytes 1 | tf_op jit(solution)/shard_map/fold/pallas_call | solution.py:385
  55.7 1.6 collective-permute-start.7
  57.3 2.6 regroup.2
  60.3 8.0 %project.6 = (f32[8,192,256]{2,1,0:T(8,128)}, s16[1936,256]{1,0:T(8,128)(2,1)}) custom-call(s32[1]{0:T(128)} %bitcast.2.core, bf16[192,1024]{1,0:T(8,128)(2,1)} %bitcast.53, bf16[1024,18432]{1,0:T(8,128)(2,1)} %weights.7, f32[4,192,384]{2,1,0:T(8,128)} %get-tuple-element.62.refs_4_.refs_0_.held, bf16[4,400,256]{2,1,0:T(8,128)(2,1)} %get-tuple-element.67.refs_1_.refs_0_), custom_call_target="tpu_custom_call" | custom-call | flops 1 | bytes 1 | tf_op jit(solution)/shard_map/project/pallas_call | solution.py:334
  68.3 7.9 %project.7 = (f32[8,192,256]{2,1,0:T(8,128)}, s16[1936,256]{1,0:T(8,128)(2,1)}) custom-call(s32[1]{0:T(128)} %bitcast.2.core, bf16[192,1024]{1,0:T(8,128)(2,1)} %bitcast.54, bf16[1024,18432]{1,0:T(8,128)(2,1)} %weights.7, f32[8,192,256]{2,1,0:T(8,128)} %get-tuple-element.69.refs_0_.held), custom_call_target="tpu_custom_call" | custom-call | flops 1 | bytes 1 | tf_op jit(solution)/shard_map/project/pallas_call | solution.py:334
  76.2 5.3 %collective-permute-done.9.refs_5_.refs_1_ = bf16[2,400,256]{2,1,0:T(8,128)(2,1)} collective-permute-done((bf16[2,400,256]{2,1,0:T(8,128)(2,1)}, bf16[2,400,256]{2,1,0:T(8,128)(2,1)}, u32[]{:S(2)}, u32[]{:S(2)}) %collective-permute-start.9) | collective-permute-done | bytes 409632 | tf_op jit(solution)/shard_map/ppermute | solution.py:222
  82.2 4.2 %fold.13 = (f32[4,192,256]{2,1,0:T(8,128)}, s16[976,256]{1,0:T(8,128)(2,1)}) custom-call(s32[1]{0:T(128)} %bitcast.5.bit, f32[8,192,256]{2,1,0:T(8,128)} %get-tuple-element.64.held, s16[1936,256]{1,0:T(8,128)(2,1)} %collective-permute-done.8.refs_3_.landed.landed_powers, s16[1936,256]{1,0:T(8,128)(2,1)} %collective-permute-done.8.refs_3_.landed.landed_powers, ...), custom_call_target="tpu_custom_call" | custom-call | flops 1 | bytes 1 | tf_op jit(solution)/shard_map/fold/pallas_call | solution.py:385
  87.7 2.7 fold.14
  90.4 1.7 collective-permute-start.14
  92.8 4.2 %fold.15 = (f32[4,192,256]{2,1,0:T(8,128)}, s16[976,256]{1,0:T(8,128)(2,1)}) custom-call(s32[1]{0:T(128)} %bitcast.5.bit, f32[8,192,256]{2,1,0:T(8,128)} %get-tuple-element.69.refs_0_.held, s16[1936,256]{1,0:T(8,128)(2,1)} %collective-permute-done.11.landed.landed_powers, s16[1936,256]{1,0:T(8,128)(2,1)} %collective-permute-done.11.landed.landed_powers, ...), custom_call_target="tpu_custom_call" | custom-call | flops 1 | bytes 1 | tf_op jit(solution)/shard_map/fold/pallas_call | solution.py:385
  97.0 4.2 %fold.16 = (f32[4,192,256]{2,1,0:T(8,128)}, s16[976,256]{1,0:T(8,128)(2,1)}) custom-call(s32[1]{0:T(128)} %bitcast.5.bit, f32[8,192,256]{2,1,0:T(8,128)} %get-tuple-element.78.held, s16[1936,256]{1,0:T(8,128)(2,1)} %collective-permute-done.12.landed.landed_powers, s16[1936,256]{1,0:T(8,128)(2,1)} %collective-permute-done.12.landed.landed_powers, ...), custom_call_target="tpu_custom_call" | custom-call | flops 1 | bytes 1 | tf_op jit(solution)/shard_map/fold/pallas_call | solution.py:385
  101.2 6.8 %collective-permute-done.10.refs_3_.landed.landed_powers = s16[496,384]{1,0:T(8,128)(2,1)} collective-permute-done((s16[496,384]{1,0:T(8,128)(2,1)}, s16[496,384]{1,0:T(8,128)(2,1)}, u32[]{:S(2)}, u32[]{:S(2)}) %collective-permute-start.10) | collective-permute-done | bytes 380960 | tf_op jit(solution)/shard_map/ppermute | solution.py:222
  108.0 3.7 %collective-permute-done.14.refs_4_.refs_2_ = bf16[2,400,256]{2,1,0:T(8,128)(2,1)} collective-permute-done((bf16[2,400,256]{2,1,0:T(8,128)(2,1)}, bf16[2,400,256]{2,1,0:T(8,128)(2,1)}, u32[]{:S(2)}, u32[]{:S(2)}) %collective-permute-start.14) | collective-permute-done | bytes 409632 | tf_op jit(solution)/shard_map/ppermute | solution.py:222
  111.7 2.3 fold.18
  114.0 2.6 regroup.3
  117.3 1.5 collective-permute-start.16
  118.8 2.0 collective-permute-start.17
  120.9 2.1 fold.17
  123.1 20.3 %collective-permute-done.15.refs_3_.landed = s16[256,384]{1,0:T(8,128)(2,1)} collective-permute-done((s16[256,384]{1,0:T(8,128)(2,1)}, s16[256,384]{1,0:T(8,128)(2,1)}, u32[]{:S(2)}, u32[]{:S(2)}) %collective-permute-start.15) | collective-permute-done | bytes 196640 | tf_op jit(solution)/shard_map/ppermute | solution.py:222
  143.5 2.2 collective-permute-done.17.refs_4_.landed.landed_powers
  146.8 1.6 collective-permute-start.21
  149.2 2.3 fold.19
  151.5 2.0 finish.4
  154.9 2.0 fold.20
  158.3 1.2 collective-permute-start.19
  161.1 7.1 %collective-permute-done.19.refs_2_.landed = s16[256,256]{1,0:T(8,128)(2,1)} collective-permute-done((s16[256,256]{1,0:T(8,128)(2,1)}, s16[256,256]{1,0:T(8,128)(2,1)}, u32[]{:S(2)}, u32[]{:S(2)}) %collective-permute-start.19) | collective-permute-done | bytes 131104 | tf_op jit(solution)/shard_map/ppermute | solution.py:222
  168.9 2.3 fold.21
  171.2 2.0 fold.22
  173.2 2.7 collective-permute-start.26
  177.5 4.7 %collective-permute-done.25.refs_2_.landed = s16[256,256]{1,0:T(8,128)(2,1)} collective-permute-done((s16[256,256]{1,0:T(8,128)(2,1)}, s16[256,256]{1,0:T(8,128)(2,1)}, u32[]{:S(2)}, u32[]{:S(2)}) %collective-permute-start.25) | collective-permute-done | bytes 131104 | tf_op jit(solution)/shard_map/ppermute | solution.py:222
  182.2 2.8 %collective-permute-done.26.refs_1_.landed.landed_powers = s16[496,256]{1,0:T(8,128)(2,1)} collective-permute-done((s16[496,256]{1,0:T(8,128)(2,1)}, s16[496,256]{1,0:T(8,128)(2,1)}, u32[]{:S(2)}, u32[]{:S(2)}) %collective-permute-start.26) | collective-permute-done | bytes 253984 | tf_op jit(solution)/shard_map/ppermute | solution.py:222
  185.1 1.9 finish.5
  186.9 2.0 fold.23
  191.1 1.9 finish.6.refs_0_
  193.0 3.6 %collective-permute-done.27.landed = s16[256,256]{1,0:T(8,128)(2,1)} collective-permute-done((s16[256,256]{1,0:T(8,128)(2,1)}, s16[256,256]{1,0:T(8,128)(2,1)}, u32[]{:S(2)}, u32[]{:S(2)}) %collective-permute-start.27) | collective-permute-done | bytes 131104 | tf_op jit(solution)/shard_map/ppermute | solution.py:222
  196.6 1.9 finish.7
  200.4 11.7 %attend.1 = bf16[16,96,128]{2,1,0:T(8,128)(2,1)} custom-call(s32[24]{0:T(128)} %get-tuple-element.111.slot_request, bf16[16,96,128]{2,1,0:T(8,128)(2,1)} %bitcast.61, bf16[16,16,128]{2,1,0:T(8,128)(2,1)} %pad.12.new_keys, bf16[16,16,128]{2,1,0:T(8,128)(2,1)} %pad.13.new_values, bf16[4,400,256]{2,1,0:T(8,128)(2,1)} %get-tuple-element.100.own_near, ...), custom_call_target="tpu_custom_call" | custom-call | flops 1 | bytes 1 | tf_op jit(solution)/shard_map/attend/pallas_call | solution.py:646
  213.9 2.6 collective-permute-start.30
  216.5 15.1 %collective-permute-done.28.refs_0_ = bf16[192,1024]{1,0:T(8,128)(2,1)S(1)} collective-permute-done((bf16[192,1024]{1,0:T(8,128)(2,1)S(1)}, bf16[192,1024]{1,0:T(8,128)(2,1)S(1)}, u32[]{:S(2)}, u32[]{:S(2)}) %collective-permute-start.28) | collective-permute-done | bytes 393248 | tf_op jit(solution)/shard_map/ppermute | solution.py:222
  231.6 2.3 collective-permute-done.30.refs_2_
  234.6 2.6 pack.2
  237.2 1.5 collective-permute-start.34
  238.7 1.9 collective-permute-start.32
  241.8 5.0 %mix.4.refs_3_ = f32[192,1024]{1,0:T(8,128)} custom-call(s32[2]{0:T(128)} %pad_add_fusion.1.places, bf16[192,1024]{1,0:T(8,128)(2,1)} %together.16.refs_0_, bf16[192,1024]{1,0:T(8,128)(2,1)} %collective-permute-done.31.refs_3_.refs_1_, bf16[16384,1024]{1,0:T(8,128)(2,1)} %refs_2_.7, bf16[192,1024]{1,0:T(8,128)(2,1)} %bitcast.55), custom_call_target="tpu_custom_call" | custom-call | flops 1 | bytes 1 | tf_op jit(solution)/shard_map/mix/pallas_call | solution.py:492
  246.8 8.5 %mix.5.refs_2_.refs_3_ = f32[192,1024]{1,0:T(8,128)} custom-call(s32[6]{0:T(128)} %stack.88.places, bf16[3,192,1024]{2,1,0:T(8,128)(2,1)} %get-tuple-element.108.refs_0_, bf16[3,192,1024]{2,1,0:T(8,128)(2,1)} %collective-permute-done.35.refs_1_, bf16[16384,1024]{1,0:T(8,128)(2,1)} %refs_2_.7, f32[192,1024]{1,0:T(8,128)} %mix.4.refs_3_), custom_call_target="tpu_custom_call" | custom-call | flops 1 | bytes 1 | tf_op jit(solution)/shard_map/mix/pallas_call | solution.py:492
  255.3 2.2 collective-permute-done.34.refs_0_
  257.5 2.4 pack.3.refs_0_
  259.8 1.5 collective-permute-start.33
  263.0 8.4 %mix.6.refs_1_.refs_3_ = f32[192,1024]{1,0:T(8,128)} custom-call(s32[6]{0:T(128)} %stack.81.places, bf16[3,192,1024]{2,1,0:T(8,128)(2,1)} %pack.3.refs_0_, bf16[3,192,1024]{2,1,0:T(8,128)(2,1)} %collective-permute-done.36.refs_1_, bf16[16384,1024]{1,0:T(8,128)(2,1)} %refs_2_.7, f32[192,1024]{1,0:T(8,128)} %mix.5.refs_2_.refs_3_), custom_call_target="tpu_custom_call" | custom-call | flops 1 | bytes 1 | tf_op jit(solution)/shard_map/mix/pallas_call | solution.py:492
  272.4 1.4 collective-permute-done.37.refs_1_
  273.8 5.0 %mix.7 = bf16[192,1024]{1,0:T(8,128)(2,1)} custom-call(s32[2]{0:T(128)} %pad_add_fusion.places, bf16[192,1024]{1,0:T(8,128)(2,1)} %together.17.refs_0_, bf16[192,1024]{1,0:T(8,128)(2,1)} %collective-permute-done.37.refs_1_, bf16[16384,1024]{1,0:T(8,128)(2,1)} %refs_2_.7, f32[192,1024]{1,0:T(8,128)} %mix.6.refs_1_.refs_3_), custom_call_target="tpu_custom_call" | custom-call | flops 1 | bytes 1 | tf_op jit(solution)/shard_map/mix/pallas_call | solution.py:492
  (135 shorter events, 28.7 us)
Async XLA Ops:
  1.2 4.6 %collective-permute-start = (f32[2,96]{1,0:T(2,128)S(1)}, f32[2,96]{1,0:T(2,128)S(1)}, u32[]{:S(2)}, u32[]{:S(2)}) collective-permute-start(f32[2,96]{1,0:T(2,128)S(1)} %fusion), channel_id=1, source_target_pairs={{0,2},{1,3},{2,0},{3,1},{4,6},{5,7},{6,4},{7,5},{8,10},{9,11},{10,... | collective-permute-start | bytes 2312 | tf_op jit(solution)/shard_map/ppermute | solution.py:222
  5.7 9.1 %copy-start.5 = (f32[2,96]{1,0:T(2,128)}, f32[2,96]{1,0:T(2,128)S(1)}, u32[]{:S(2)}) copy-start(f32[2,96]{1,0:T(2,128)S(1)} %add.119.after) | copy-start | bytes 2308
  5.7 1.1 collective-permute-start.1
  6.9 3.6 %collective-permute-start.2 = (f32[2,96]{1,0:T(2,128)S(1)}, f32[2,96]{1,0:T(2,128)S(1)}, u32[]{:S(2)}, u32[]{:S(2)}) collective-permute-start(f32[2,96]{1,0:T(2,128)S(1)} %add.120), channel_id=1, source_target_pairs={{0,4},{1,5},{2,6},{3,7},{4,0},{5,1},{6,2},{7,3},{8,12},{9,13},{10,... | collective-permute-start | bytes 2312 | tf_op jit(solution)/shard_map/ppermute | solution.py:222
  10.5 10.1 %collective-permute-start.3 = (f32[2,96]{1,0:T(2,128)S(1)}, f32[2,96]{1,0:T(2,128)S(1)}, u32[]{:S(2)}, u32[]{:S(2)}) collective-permute-start(f32[2,96]{1,0:T(2,128)S(1)} %add.121), channel_id=1, source_target_pairs={{0,8},{1,9},{2,10},{3,11},{4,12},{5,13},{6,14},{7,15},{8,0},{9,1},... | collective-permute-start | bytes 2312 | tf_op jit(solution)/shard_map/ppermute | solution.py:222
  19.1 10.4 %collective-permute-start.4 = (bf16[2,400,256]{2,1,0:T(8,128)(2,1)}, bf16[2,400,256]{2,1,0:T(8,128)(2,1)}, u32[]{:S(2)}, u32[]{:S(2)}) collective-permute-start(bf16[2,400,256]{2,1,0:T(8,128)(2,1)} %get-tuple-element.57.after), channel_id=1, source_target_pairs={{0,2},{1,3},{2,0},{3,1},{4,6},{5,7},{6,4},{7,5},{8,10},{9,11},{10,... | collective-permute-start | bytes 1228808 | tf_op jit(solution)/shard_map/ppermute | solution.py:222
  38.7 12.3 %collective-permute-start.5 = (s16[1936,384]{1,0:T(8,128)(2,1)}, s16[1936,384]{1,0:T(8,128)(2,1)}, u32[]{:S(2)}, u32[]{:S(2)}) collective-permute-start(s16[1936,384]{1,0:T(8,128)(2,1)} %get-tuple-element.60), channel_id=1, source_target_pairs={{0,1},{1,0},{2,3},{3,2},{4,5},{5,4},{6,7},{7,6},{8,9},{9,8},{10,11... | collective-permute-start | bytes 4460552 | tf_op jit(solution)/shard_map/ppermute | solution.py:222
  38.8 12.2 %collective-permute-start.6 = (bf16[2,400,256]{2,1,0:T(8,128)(2,1)}, bf16[2,400,256]{2,1,0:T(8,128)(2,1)}, u32[]{:S(2)}, u32[]{:S(2)}) collective-permute-start(bf16[2,400,256]{2,1,0:T(8,128)(2,1)} %together.9.refs_0_), channel_id=1, source_target_pairs={{0,2},{1,3},{2,0},{3,1},{4,6},{5,7},{6,4},{7,5},{8,10},{9,11},{10,... | collective-permute-start | bytes 1228808 | tf_op jit(solution)/shard_map/ppermute | solution.py:222
  51.0 30.5 %collective-permute-start.8 = (s16[1936,256]{1,0:T(8,128)(2,1)}, s16[1936,256]{1,0:T(8,128)(2,1)}, u32[]{:S(2)}, u32[]{:S(2)}) collective-permute-start(s16[1936,256]{1,0:T(8,128)(2,1)} %together.10.refs_0_), channel_id=1, source_target_pairs={{0,1},{1,0},{2,3},{3,2},{4,5},{5,4},{6,7},{7,6},{8,9},{9,8},{10,11... | collective-permute-start | bytes 2973704 | tf_op jit(solution)/shard_map/ppermute | solution.py:222
  55.7 4.5 %copy-start.10 = (s32[8]{0:T(128)S(1)}, s32[8]{0:T(128)}, u32[]{:S(2)}) copy-start(s32[8]{0:T(128)} %constant.116.clone) | copy-start | bytes 100
  55.7 4.5 %copy-start.9 = (s32[16]{0:T(128)S(1)}, s32[16]{0:T(128)}, u32[]{:S(2)}) copy-start(s32[16]{0:T(128)} %param.15) | copy-start | bytes 196
  55.7 25.8 %collective-permute-start.7 = (s16[976,384]{1,0:T(8,128)(2,1)}, s16[976,384]{1,0:T(8,128)(2,1)}, u32[]{:S(2)}, u32[]{:S(2)}) collective-permute-start(s16[976,384]{1,0:T(8,128)(2,1)} %get-tuple-element.63), channel_id=1, source_target_pairs={{0,2},{1,3},{2,0},{3,1},{4,6},{5,7},{6,4},{7,5},{8,10},{9,11},{10,... | collective-permute-start | bytes 2248712 | tf_op jit(solution)/shard_map/ppermute | solution.py:222
  59.9 21.6 %collective-permute-start.9 = (bf16[2,400,256]{2,1,0:T(8,128)(2,1)}, bf16[2,400,256]{2,1,0:T(8,128)(2,1)}, u32[]{:S(2)}, u32[]{:S(2)}) collective-permute-start(bf16[2,400,256]{2,1,0:T(8,128)(2,1)} %get-tuple-element.72), channel_id=1, source_target_pairs={{0,8},{1,9},{2,10},{3,11},{4,12},{5,13},{6,14},{7,15},{8,0},{9,1},... | collective-permute-start | bytes 1228808 | tf_op jit(solution)/shard_map/ppermute | solution.py:222
  81.5 11.3 %collective-permute-start.11 = (s16[1936,256]{1,0:T(8,128)(2,1)}, s16[1936,256]{1,0:T(8,128)(2,1)}, u32[]{:S(2)}, u32[]{:S(2)}) collective-permute-start(s16[1936,256]{1,0:T(8,128)(2,1)} %get-tuple-element.73.refs_0_), channel_id=1, source_target_pairs={{0,1},{1,0},{2,3},{3,2},{4,5},{5,4},{6,7},{7,6},{8,9},{9,8},{10,11... | collective-permute-start | bytes 2973704 | tf_op jit(solution)/shard_map/ppermute | solution.py:222
  81.6 15.4 %collective-permute-start.12 = (s16[1936,256]{1,0:T(8,128)(2,1)}, s16[1936,256]{1,0:T(8,128)(2,1)}, u32[]{:S(2)}, u32[]{:S(2)}) collective-permute-start(s16[1936,256]{1,0:T(8,128)(2,1)} %get-tuple-element.79), channel_id=1, source_target_pairs={{0,1},{1,0},{2,3},{3,2},{4,5},{5,4},{6,7},{7,6},{8,9},{9,8},{10,11... | collective-permute-start | bytes 2973704 | tf_op jit(solution)/shard_map/ppermute | solution.py:222
  82.2 4.7 %copy-start.8 = (s32[16,16]{1,0:T(8,128)S(1)}, s32[16,16]{1,0:T(8,128)}, u32[]{:S(2)}) copy-start(s32[16,16]{1,0:T(8,128)} %param.16) | copy-start | bytes 3076
  86.4 25.3 %collective-permute-start.13 = (s16[976,256]{1,0:T(8,128)(2,1)}, s16[976,256]{1,0:T(8,128)(2,1)}, u32[]{:S(2)}, u32[]{:S(2)}) collective-permute-start(s16[976,256]{1,0:T(8,128)(2,1)} %get-tuple-element.82), channel_id=1, source_target_pairs={{0,2},{1,3},{2,0},{3,1},{4,6},{5,7},{6,4},{7,5},{8,10},{9,11},{10,... | collective-permute-start | bytes 1499144 | tf_op jit(solution)/shard_map/ppermute | solution.py:222
  90.4 17.6 %collective-permute-start.10 = (s16[496,384]{1,0:T(8,128)(2,1)}, s16[496,384]{1,0:T(8,128)(2,1)}, u32[]{:S(2)}, u32[]{:S(2)}) collective-permute-start(s16[496,384]{1,0:T(8,128)(2,1)} %get-tuple-element.76), channel_id=1, source_target_pairs={{0,4},{1,5},{2,6},{3,7},{4,0},{5,1},{6,2},{7,3},{8,12},{9,13},{10,... | collective-permute-start | bytes 1142792 | tf_op jit(solution)/shard_map/ppermute | solution.py:222
  90.4 21.3 %collective-permute-start.14 = (bf16[2,400,256]{2,1,0:T(8,128)(2,1)}, bf16[2,400,256]{2,1,0:T(8,128)(2,1)}, u32[]{:S(2)}, u32[]{:S(2)}) collective-permute-start(bf16[2,400,256]{2,1,0:T(8,128)(2,1)} %get-tuple-element.83), channel_id=1, source_target_pairs={{0,8},{1,9},{2,10},{3,11},{4,12},{5,13},{6,14},{7,15},{8,0},{9,1},... | collective-permute-start | bytes 1228808 | tf_op jit(solution)/shard_map/ppermute | solution.py:222
  116.6 29.1 %collective-permute-start.18 = (bf16[4,400,256]{2,1,0:T(8,128)(2,1)}, bf16[4,400,256]{2,1,0:T(8,128)(2,1)}, u32[]{:S(2)}, u32[]{:S(2)}) collective-permute-start(bf16[4,400,256]{2,1,0:T(8,128)(2,1)} %get-tuple-element.91), channel_id=1, source_target_pairs={{0,4},{1,5},{2,6},{3,7},{4,0},{5,1},{6,2},{7,3},{8,12},{9,13},{10,... | collective-permute-start | bytes 2457608 | tf_op jit(solution)/shard_map/ppermute | solution.py:222
  117.3 28.4 %collective-permute-start.16 = (s16[976,256]{1,0:T(8,128)(2,1)}, s16[976,256]{1,0:T(8,128)(2,1)}, u32[]{:S(2)}, u32[]{:S(2)}) collective-permute-start(s16[976,256]{1,0:T(8,128)(2,1)} %get-tuple-element.84.refs_0_), channel_id=1, source_target_pairs={{0,2},{1,3},{2,0},{3,1},{4,6},{5,7},{6,4},{7,5},{8,10},{9,11},{10,... | collective-permute-start | bytes 1499144 | tf_op jit(solution)/shard_map/ppermute | solution.py:222
  118.8 26.9 %collective-permute-start.17 = (s16[496,256]{1,0:T(8,128)(2,1)}, s16[496,256]{1,0:T(8,128)(2,1)}, u32[]{:S(2)}, u32[]{:S(2)}) collective-permute-start(s16[496,256]{1,0:T(8,128)(2,1)} %get-tuple-element.90), channel_id=1, source_target_pairs={{0,4},{1,5},{2,6},{3,7},{4,0},{5,1},{6,2},{7,3},{8,12},{9,13},{10,... | collective-permute-start | bytes 761864 | tf_op jit(solution)/shard_map/ppermute | solution.py:222
  123.1 20.4 %collective-permute-start.15 = (s16[256,384]{1,0:T(8,128)(2,1)}, s16[256,384]{1,0:T(8,128)(2,1)}, u32[]{:S(2)}, u32[]{:S(2)}) collective-permute-start(s16[256,384]{1,0:T(8,128)(2,1)} %get-tuple-element.86), channel_id=1, source_target_pairs={{0,8},{1,9},{2,10},{3,11},{4,12},{5,13},{6,14},{7,15},{8,0},{9,1},... | collective-permute-start | bytes 589832 | tf_op jit(solution)/shard_map/ppermute | solution.py:222
  145.7 22.5 %collective-permute-start.23 = (bf16[4,400,256]{2,1,0:T(8,128)(2,1)}, bf16[4,400,256]{2,1,0:T(8,128)(2,1)}, u32[]{:S(2)}, u32[]{:S(2)}) collective-permute-start(bf16[4,400,256]{2,1,0:T(8,128)(2,1)} %get-tuple-element.100.own_near), channel_id=1, source_target_pairs={{0,1},{1,0},{2,3},{3,2},{4,5},{5,4},{6,7},{7,6},{8,9},{9,8},{10,11... | collective-permute-start | bytes 2457608 | tf_op jit(solution)/shard_map/ppermute | solution.py:222
  145.8 22.5 %collective-permute-start.24 = (bf16[4,400,256]{2,1,0:T(8,128)(2,1)}, bf16[4,400,256]{2,1,0:T(8,128)(2,1)}, u32[]{:S(2)}, u32[]{:S(2)}) collective-permute-start(bf16[4,400,256]{2,1,0:T(8,128)(2,1)} %collective-permute-done.18.refs_5_.own_far), channel_id=1, source_target_pairs={{0,1},{1,0},{2,3},{3,2},{4,5},{5,4},{6,7},{7,6},{8,9},{9,8},{10,11... | collective-permute-start | bytes 2457608 | tf_op jit(solution)/shard_map/ppermute | solution.py:222
  146.8 21.4 %collective-permute-start.21 = (s16[976,256]{1,0:T(8,128)(2,1)}, s16[976,256]{1,0:T(8,128)(2,1)}, u32[]{:S(2)}, u32[]{:S(2)}) collective-permute-start(s16[976,256]{1,0:T(8,128)(2,1)} %get-tuple-element.92.refs_0_), channel_id=1, source_target_pairs={{0,2},{1,3},{2,0},{3,1},{4,6},{5,7},{6,4},{7,5},{8,10},{9,11},{10,... | collective-permute-start | bytes 1499144 | tf_op jit(solution)/shard_map/ppermute | solution.py:222
  153.5 4.8 %collective-permute-start.22 = (bf16[192,128]{1,0:T(8,128)(2,1)}, bf16[192,128]{1,0:T(8,128)(2,1)S(1)}, u32[]{:S(2)}, u32[]{:S(2)}) collective-permute-start(bf16[192,128]{1,0:T(8,128)(2,1)} %get-tuple-element.99), channel_id=1, source_target_pairs={{0,1},{1,0},{2,3},{3,2},{4,5},{5,4},{6,7},{7,6},{8,9},{9,8},{10,11... | collective-permute-start | bytes 147464 | tf_op jit(solution)/shard_map/ppermute | solution.py:222
  153.5 14.7 %collective-permute-start.20 = (s16[496,256]{1,0:T(8,128)(2,1)}, s16[496,256]{1,0:T(8,128)(2,1)}, u32[]{:S(2)}, u32[]{:S(2)}) collective-permute-start(s16[496,256]{1,0:T(8,128)(2,1)} %get-tuple-element.97), channel_id=1, source_target_pairs={{0,4},{1,5},{2,6},{3,7},{4,0},{5,1},{6,2},{7,3},{8,12},{9,13},{10,... | collective-permute-start | bytes 761864 | tf_op jit(solution)/shard_map/ppermute | solution.py:222
  158.3 2.8 copy-start.4
  158.3 9.9 %collective-permute-start.19 = (s16[256,256]{1,0:T(8,128)(2,1)}, s16[256,256]{1,0:T(8,128)(2,1)}, u32[]{:S(2)}, u32[]{:S(2)}) collective-permute-start(s16[256,256]{1,0:T(8,128)(2,1)} %get-tuple-element.96), channel_id=1, source_target_pairs={{0,8},{1,9},{2,10},{3,11},{4,12},{5,13},{6,14},{7,15},{8,0},{9,1},... | collective-permute-start | bytes 393224 | tf_op jit(solution)/shard_map/ppermute | solution.py:222
  168.9 8.6 %copy-start.6 = (bf16[4,2,24]{2,1,0:T(2,128)(2,1)S(1)}, bf16[4,2,24]{2,1,0:T(2,128)(2,1)}, u32[]{:S(2)}) copy-start(bf16[4,2,24]{2,1,0:T(2,128)(2,1)} %concatenate.28) | copy-start | bytes 1156
  168.9 8.6 %copy-start.7 = (bf16[4,2,24]{2,1,0:T(2,128)(2,1)S(1)}, bf16[4,2,24]{2,1,0:T(2,128)(2,1)}, u32[]{:S(2)}) copy-start(bf16[4,2,24]{2,1,0:T(2,128)(2,1)} %concatenate.29) | copy-start | bytes 1156
  173.2 9.0 %collective-permute-start.25 = (s16[256,256]{1,0:T(8,128)(2,1)}, s16[256,256]{1,0:T(8,128)(2,1)}, u32[]{:S(2)}, u32[]{:S(2)}) collective-permute-start(s16[256,256]{1,0:T(8,128)(2,1)} %get-tuple-element.103), channel_id=1, source_target_pairs={{0,8},{1,9},{2,10},{3,11},{4,12},{5,13},{6,14},{7,15},{8,0},{9,1},... | collective-permute-start | bytes 393224 | tf_op jit(solution)/shard_map/ppermute | solution.py:222
  173.2 11.8 %collective-permute-start.26 = (s16[496,256]{1,0:T(8,128)(2,1)}, s16[496,256]{1,0:T(8,128)(2,1)}, u32[]{:S(2)}, u32[]{:S(2)}) collective-permute-start(s16[496,256]{1,0:T(8,128)(2,1)} %get-tuple-element.104), channel_id=1, source_target_pairs={{0,4},{1,5},{2,6},{3,7},{4,0},{5,1},{6,2},{7,3},{8,12},{9,13},{10,... | collective-permute-start | bytes 761864 | tf_op jit(solution)/shard_map/ppermute | solution.py:222
  188.9 7.7 %collective-permute-start.27 = (s16[256,256]{1,0:T(8,128)(2,1)}, s16[256,256]{1,0:T(8,128)(2,1)}, u32[]{:S(2)}, u32[]{:S(2)}) collective-permute-start(s16[256,256]{1,0:T(8,128)(2,1)} %get-tuple-element.106), channel_id=1, source_target_pairs={{0,8},{1,9},{2,10},{3,11},{4,12},{5,13},{6,14},{7,15},{8,0},{9,1},... | collective-permute-start | bytes 393224 | tf_op jit(solution)/shard_map/ppermute | solution.py:222
  213.2 3.3 %copy-start = (bf16[24,8,8,128]{3,1,2,0:T(8,128)(2,1)}, bf16[24,8,8,128]{3,1,2,0:T(8,128)(2,1)S(1)}, u32[]{:S(2)}) copy-start(bf16[24,8,8,128]{3,1,2,0:T(8,128)(2,1)S(1)} %copy.50) | copy-start | bytes 1179652
  213.2 18.3 %collective-permute-start.28 = (bf16[192,1024]{1,0:T(8,128)(2,1)S(1)}, bf16[192,1024]{1,0:T(8,128)(2,1)S(1)}, u32[]{:S(2)}, u32[]{:S(2)}) collective-permute-start(bf16[192,1024]{1,0:T(8,128)(2,1)S(1)} %bitcast.56), channel_id=1, source_target_pairs={{0,4},{1,5},{2,6},{3,7},{4,0},{5,1},{6,2},{7,3},{8,12},{9,13},{10,... | collective-permute-start | bytes 1179656 | tf_op jit(solution)/shard_map/ppermute | solution.py:222
  213.3 18.3 %collective-permute-start.29 = (bf16[192,1024]{1,0:T(8,128)(2,1)S(1)}, bf16[192,1024]{1,0:T(8,128)(2,1)S(1)}, u32[]{:S(2)}, u32[]{:S(2)}) collective-permute-start(bf16[192,1024]{1,0:T(8,128)(2,1)S(1)} %bitcast.57), channel_id=1, source_target_pairs={{0,2},{1,3},{2,0},{3,1},{4,6},{5,7},{6,4},{7,5},{8,10},{9,11},{10,... | collective-permute-start | bytes 1179656 | tf_op jit(solution)/shard_map/ppermute | solution.py:222
  213.9 19.9 %collective-permute-start.30 = (bf16[192,1024]{1,0:T(8,128)(2,1)S(1)}, bf16[192,1024]{1,0:T(8,128)(2,1)S(1)}, u32[]{:S(2)}, u32[]{:S(2)}) collective-permute-start(bf16[192,1024]{1,0:T(8,128)(2,1)S(1)} %bitcast.58), channel_id=1, source_target_pairs={{0,8},{1,9},{2,10},{3,11},{4,12},{5,13},{6,14},{7,15},{8,0},{9,1},... | collective-permute-start | bytes 1179656 | tf_op jit(solution)/shard_map/ppermute | solution.py:222
  216.5 18.1 %collective-permute-start.31 = (bf16[192,1024]{1,0:T(8,128)(2,1)S(1)}, bf16[192,1024]{1,0:T(8,128)(2,1)}, u32[]{:S(2)}, u32[]{:S(2)}) collective-permute-start(bf16[192,1024]{1,0:T(8,128)(2,1)S(1)} %bitcast.59), channel_id=1, source_target_pairs={{0,1},{1,0},{2,3},{3,2},{4,5},{5,4},{6,7},{7,6},{8,9},{9,8},{10,11... | collective-permute-start | bytes 1179656 | tf_op jit(solution)/shard_map/ppermute | solution.py:222
  231.6 2.3 copy-start.1
  231.6 2.3 copy-start.2
  233.8 0.8 copy-start.3
  237.2 9.6 %collective-permute-start.35 = (bf16[3,192,1024]{2,1,0:T(8,128)(2,1)}, bf16[3,192,1024]{2,1,0:T(8,128)(2,1)}, u32[]{:S(2)}, u32[]{:S(2)}) collective-permute-start(bf16[3,192,1024]{2,1,0:T(8,128)(2,1)} %get-tuple-element.108.refs_0_), channel_id=1, source_target_pairs={{0,1},{1,0},{2,3},{3,2},{4,5},{5,4},{6,7},{7,6},{8,9},{9,8},{10,11... | collective-permute-start | bytes 3538952 | tf_op jit(solution)/shard_map/ppermute | solution.py:222
  237.2 20.3 %collective-permute-start.34 = (bf16[2,192,1024]{2,1,0:T(8,128)(2,1)}, bf16[2,192,1024]{2,1,0:T(8,128)(2,1)}, u32[]{:S(2)}, u32[]{:S(2)}) collective-permute-start(bf16[2,192,1024]{2,1,0:T(8,128)(2,1)} %get-tuple-element.107.refs_1_), channel_id=1, source_target_pairs={{0,2},{1,3},{2,0},{3,1},{4,6},{5,7},{6,4},{7,5},{8,10},{9,11},{10,... | collective-permute-start | bytes 2359304 | tf_op jit(solution)/shard_map/ppermute | solution.py:222
  238.7 16.6 %collective-permute-start.32 = (bf16[192,1024]{1,0:T(8,128)(2,1)}, bf16[192,1024]{1,0:T(8,128)(2,1)}, u32[]{:S(2)}, u32[]{:S(2)}) collective-permute-start(bf16[192,1024]{1,0:T(8,128)(2,1)} %together.16.refs_0_), channel_id=1, source_target_pairs={{0,12},{1,13},{2,14},{3,15},{4,8},{5,9},{6,10},{7,11},{8,4},{9,5},... | collective-permute-start | bytes 1179656 | tf_op jit(solution)/shard_map/ppermute | solution.py:222
  259.8 3.2 %collective-permute-start.36 = (bf16[3,192,1024]{2,1,0:T(8,128)(2,1)}, bf16[3,192,1024]{2,1,0:T(8,128)(2,1)}, u32[]{:S(2)}, u32[]{:S(2)}) collective-permute-start(bf16[3,192,1024]{2,1,0:T(8,128)(2,1)} %pack.3.refs_0_), channel_id=1, source_target_pairs={{0,1},{1,0},{2,3},{3,2},{4,5},{5,4},{6,7},{7,6},{8,9},{9,8},{10,11... | collective-permute-start | bytes 3538952 | tf_op jit(solution)/shard_map/ppermute | solution.py:222
  259.8 11.8 %collective-permute-start.33 = (bf16[192,1024]{1,0:T(8,128)(2,1)}, bf16[192,1024]{1,0:T(8,128)(2,1)}, u32[]{:S(2)}, u32[]{:S(2)}) collective-permute-start(bf16[192,1024]{1,0:T(8,128)(2,1)} %collective-permute-done.32.refs_1_), channel_id=1, source_target_pairs={{0,2},{1,3},{2,0},{3,1},{4,6},{5,7},{6,4},{7,5},{8,10},{9,11},{10,... | collective-permute-start | bytes 1179656 | tf_op jit(solution)/shard_map/ppermute | solution.py:222
  271.7 2.1 collective-permute-start.37

commit v7 on v6

--- a/solution.py
+++ b/solution.py
@@ -207,7 +207,7 @@
     return jnp.concatenate(outputs, 0)
 
 
-VMEM_LIMIT = 66977792
+VMEM_LIMIT = 48 * 1024 * 1024
 SHORT = pl.CostEstimate(flops=1, bytes_accessed=1, transcendentals=0)
 LOW_BITS = 4
 PACKED = 16 // LOW_BITS
@@ -222,10 +222,6 @@
     return lax.ppermute(value, "tensor", [(i, i ^ bit) for i in range(devices)])
 
 
-def in_hbm(*arrays):
-    return [pltpu.with_memory_space_constraint(a, pltpu.HBM) for a in arrays]
-
-
 def no_work(*refs):
     del refs
 
@@ -236,12 +232,12 @@
         no_work,
         in_specs=[anywhere] * (len(arrays) + len(after)),
         out_specs=[anywhere] * len(arrays),
-        out_shape=[pltpu.HBM(a.shape, a.dtype) for a in arrays],
+        out_shape=[jax.ShapeDtypeStruct(a.shape, a.dtype) for a in arrays],
         input_output_aliases={i: i for i in range(len(arrays))},
         compiler_params=pltpu.CompilerParams(vmem_limit_bytes=VMEM_LIMIT),
         cost_estimate=SHORT,
         name="together",
-    )(*in_hbm(*arrays), *after)
+    )(*arrays, *after)
 
 
 def coded_rows(rows):
@@ -349,13 +345,13 @@
             ],
         ),
         out_shape=[
-            pltpu.HBM((KVH, rows, columns), jnp.float32),
-            pltpu.HBM((sent_rows, columns), jnp.int16),
+            jax.ShapeDtypeStruct((KVH, rows, columns), jnp.float32),
+            jax.ShapeDtypeStruct((sent_rows, columns), jnp.int16),
         ],
         compiler_params=pltpu.CompilerParams(vmem_limit_bytes=VMEM_LIMIT),
         cost_estimate=SHORT,
         name="project",
-    )(core, normed, *in_hbm(qkv_weight), *after)
+    )(core, normed, qkv_weight, *after)
 
 
 def fold_kernel(steps, bit, held, landed, landed_powers, *refs):
@@ -400,13 +396,13 @@
             scratch_shapes=[pltpu.VMEM((TILE, columns), jnp.float32)],
         ),
         out_shape=[
-            pltpu.HBM((steps, rows, columns), jnp.float32),
-            pltpu.HBM((steps * coded + TILE, columns), jnp.int16),
+            jax.ShapeDtypeStruct((steps, rows, columns), jnp.float32),
+            jax.ShapeDtypeStruct((steps * coded + TILE, columns), jnp.int16),
         ],
         compiler_params=pltpu.CompilerParams(vmem_limit_bytes=VMEM_LIMIT),
         cost_estimate=SHORT,
         name="fold",
-    )(bit, *in_hbm(held), landed, landed, *after)
+    )(bit, held, landed, landed, *after)
 
 
 def finish_kernel(after_count, core, held, landed, cosine, sine, *refs):
@@ -433,9 +429,9 @@
 def finish(core, held, landed, cosine, sine, after):
     _, rows, columns = held.shape
     whole = pl.BlockSpec(memory_space=pltpu.VMEM)
-    shapes = [pltpu.HBM((rows, 2 * HD), jnp.bfloat16)]
+    shapes = [jax.ShapeDtypeStruct((rows, 2 * HD), jnp.bfloat16)]
     if columns > 2 * HD:
-        shapes.append(pltpu.HBM((rows, HD), jnp.bfloat16))
+        shapes.append(jax.ShapeDtypeStruct((rows, HD), jnp.bfloat16))
     return pl.pallas_call(
         functools.partial(finish_kernel, len(after)),
         in_specs=[pl.BlockSpec(memory_space=pltpu.SMEM)]
@@ -446,7 +442,7 @@
         compiler_params=pltpu.CompilerParams(vmem_limit_bytes=VMEM_LIMIT),
         cost_estimate=SHORT,
         name="finish",
-    )(core, *in_hbm(held), landed, *in_hbm(cosine, sine), *after)
+    )(core, held, landed, cosine, sine, *after)
 
 
 def mix_kernel(count, places, *refs):
@@ -500,11 +496,11 @@
             pltpu.VMEM((count, width, columns), jnp.bfloat16),
             pltpu.SemaphoreType.DMA((count,)),
         ],
-        out_shape=pltpu.HBM((rows, columns), dtype),
+        out_shape=jax.ShapeDtypeStruct((rows, columns), dtype),
         compiler_params=pltpu.CompilerParams(vmem_limit_bytes=VMEM_LIMIT),
         cost_estimate=SHORT,
         name="mix",
-    )(places, *pieces, *in_hbm(out_weight, start))
+    )(places, *pieces, out_weight, start)
 
 
 def pack_kernel(groups, count, *refs):
@@ -523,7 +519,7 @@
         functools.partial(pack_kernel, groups, len(pieces)),
         in_specs=[whole] * len(pieces) + [pl.BlockSpec(memory_space=pl.ANY)] * len(after),
         out_specs=[whole] * len(groups),
-        out_shape=[pltpu.HBM((len(g),) + shape, pieces[0].dtype) for g in groups],
+        out_shape=[jax.ShapeDtypeStruct((len(g),) + shape, pieces[0].dtype) for g in groups],
         compiler_params=pltpu.CompilerParams(vmem_limit_bytes=VMEM_LIMIT),
         cost_estimate=SHORT,
         name="pack",
@@ -563,10 +559,8 @@
     queries,
     new_keys,
     new_values,
-    own_near,
-    own_far,
-    other_near,
-    other_far,
+    own,
+    other,
     key_scale,
     value_scale,
     cache_bias,
@@ -604,8 +598,8 @@
         request = slot_request[slot]
         query = queries[request]
         raw = [
-            part[:, slot * BLK : (slot + 1) * BLK, :].reshape(KVH // 2 * BLK, 2 * HD)
-            for part in (own_near, own_far, other_near, other_far)
+            part[:, slot * BLK : (slot + 1) * BLK, :].reshape(KVH * BLK, 2 * HD)
+            for part in (own, other)
         ]
         scores = jnp.concatenate(
             [
@@ -640,14 +634,14 @@
 
 def attend(slot_request, *arrays):
     queries = arrays[0]
-    slots = arrays[7].shape[0]
+    slots = arrays[5].shape[0]
     requests, count, _ = queries.shape
     whole = pl.BlockSpec(memory_space=pltpu.VMEM)
     return pl.pallas_call(
         attend_kernel,
         in_specs=[pl.BlockSpec(memory_space=pltpu.SMEM)] + [whole] * len(arrays),
         out_specs=whole,
-        out_shape=pltpu.HBM((requests, count, HD), jnp.bfloat16),
+        out_shape=jax.ShapeDtypeStruct((requests, count, HD), jnp.bfloat16),
         scratch_shapes=[pltpu.VMEM((slots, count, HD), jnp.float32)] * 3
         + [pltpu.VMEM((requests, count, HD), jnp.float32)] * 3,
         compiler_params=pltpu.CompilerParams(vmem_limit_bytes=VMEM_LIMIT),
@@ -672,77 +666,31 @@
     return request, rank, length
 
 
-def arrange_kernel(chip, even, odd, even_scale, odd_scale, after, kept, sent):
-    slots = even.shape[0]
-    for blocks, scale, target in ((even, even_scale, kept), (odd, odd_scale, sent)):
-        target[0, : slots * BLK, :] = blocks[:, 0].reshape(slots * BLK, 2 * HD)
-        target[0, slots * BLK :, :] = scale[0]
-
-
-def arrange(chip, cache_pool, scales, first, after):
-    slots = cache_pool.shape[0]
-    pool = [
-        pl.BlockSpec(
-            (slots, 1, BLK, 2 * HD), lambda i, c, side=side: (0, c[0] ^ (first + 2 * i + side), 0, 0)
-        )
-        for side in (0, 1)
-    ]
-    scale = [
-        pl.BlockSpec((1, TILE, 2 * HD), lambda i, c, side=side: (c[0] ^ (first + 2 * i + side), 0, 0))
-        for side in (0, 1)
-    ]
-    rows = slots * BLK + TILE
-    out = pl.BlockSpec((1, rows, 2 * HD), lambda i, c: (i, 0, 0))
-    shape = pltpu.HBM((KVH // 4, rows, 2 * HD), jnp.bfloat16)
+def arrange_kernel(chip, pool, scales, after, *sent):
+    slots = pool.shape[0]
+    for k, target in enumerate(sent):
+        head = chip[0] ^ k
+        target[: slots * BLK, :] = pool[:, head].reshape(slots * BLK, 2 * HD)
+        target[slots * BLK :, :] = scales[head]
+
+
+def arrange(chip, cache_pool, scales, after):
+    rows = cache_pool.shape[0] * BLK + TILE
+    whole = pl.BlockSpec(memory_space=pltpu.VMEM)
     return pl.pallas_call(
         arrange_kernel,
-        grid_spec=pltpu.PrefetchScalarGridSpec(
-            num_scalar_prefetch=1,
-            grid=(KVH // 4,),
-            in_specs=pool + scale + [pl.BlockSpec(memory_space=pl.ANY)],
-            out_specs=[out, out],
-        ),
-        out_shape=[shape, shape],
+        in_specs=[
+            pl.BlockSpec(memory_space=pltpu.SMEM),
+            whole,
+            whole,
+            pl.BlockSpec(memory_space=pl.ANY),
+        ],
+        out_specs=[whole] * KVH,
+        out_shape=[jax.ShapeDtypeStruct((rows, 2 * HD), jnp.bfloat16)] * KVH,
         compiler_params=pltpu.CompilerParams(vmem_limit_bytes=VMEM_LIMIT),
         cost_estimate=SHORT,
         name="arrange",
-    )(chip, *in_hbm(cache_pool, cache_pool, scales, scales), after)
-
-
-def handover_plan():
-    arrays = [[(0, 0), (0, 2)], [(0, 4), (0, 6)], [(1, 0), (1, 2)], [(1, 4), (1, 6)]]
-    splits = []
-    for bit, parts in ((4, 2), (2, 1)):
-        entries = [(a, i, e) for a, part in enumerate(arrays) for i, e in enumerate(part)]
-        stay = [e for e in entries if not e[2][1] & bit]
-        leave = [e for e in entries if e[2][1] & bit]
-        size = len(leave) // parts
-        groups = [stay] + [leave[i : i + size] for i in range(0, len(leave), size)]
-        splits.append([[(a, i) for a, i, _ in group] for group in groups])
-        arrays = [[e for _, _, e in stay]]
-        arrays += [[(x ^ bit, y ^ bit) for _, _, (x, y) in group] for group in groups[1:]]
-    return splits, [source for part in arrays for source, _ in part]
-
-
-def regroup_kernel(groups, count, *refs):
-    sources, targets = refs[:count], refs[-len(groups) :]
-    for group, target in zip(groups, targets):
-        for place, (array, index) in enumerate(group):
-            target[place] = sources[array][index]
-
-
-def regroup(groups, sources, after):
-    whole = pl.BlockSpec(memory_space=pltpu.VMEM)
-    rows = sources[0].shape[1:]
-    return pl.pallas_call(
-        functools.partial(regroup_kernel, groups, len(sources)),
-        in_specs=[whole] * len(sources) + [pl.BlockSpec(memory_space=pl.ANY)] * len(after),
-        out_specs=[whole] * len(groups),
-        out_shape=[pltpu.HBM((len(g),) + rows, sources[0].dtype) for g in groups],
-        compiler_params=pltpu.CompilerParams(vmem_limit_bytes=VMEM_LIMIT),
-        cost_estimate=SHORT,
-        name="regroup",
-    )(*sources, *after)
+    )(chip, cache_pool, scales, after)
 
 
 def local_pairs(
@@ -773,15 +721,15 @@
         jnp.transpose(cache_scale, (1, 2, 0)).reshape(KVH, 1, 2 * slots),
         ((0, 0), (0, TILE - 1), (0, 2 * HD - 2 * slots)),
     )
+    sums = sums + swap(sums, 2)
     chip_scalar = jnp.reshape(chip, (1,)).astype(jnp.int32)
-    sums = sums + swap(sums, 2)
-    kept_a, sent_a = arrange(chip_scalar, cache_pool, scale_rows, 0, sums)
-    landed_a = swap(sent_a, 2)
-    kept_b, sent_b = arrange(chip_scalar, cache_pool, scale_rows, KVH // 2, sent_a)
+    cache_pieces = list(arrange(chip_scalar, cache_pool, scale_rows, sums))
+
+    def handed(k):
+        cache_pieces[k] = swap(cache_pieces[k], 2 * k)
+
     for bit in (1, 4, 8):
         sums = sums + swap(sums, bit)
-    (sent_b,) = together([sent_b], [sums, landed_a])
-    landed_b = swap(sent_b, 2)
     normed = (
         hidden * lax.rsqrt(sums[..., None] / D + EPSILON) * norm_gain.astype(jnp.float32)
     ).astype(jnp.bfloat16)
@@ -799,7 +747,6 @@
 
     count = GQ // 4
     held, sent = [None] * count, [None] * count
-    splits, sources_of_cache = handover_plan()
 
     def projected(chunk, *after):
         held[chunk], sent[chunk] = project(
@@ -815,41 +762,41 @@
     def finished(chunk, landed, *after):
         return finish(bits[0], held[chunk], landed, cosine, sine, after)
 
-    projected(0, sent_b)
+    projected(0, cache_pieces[0])
     core_0 = hop(0, 0)
+    for k in (1, 2, 3, 4):
+        handed(k)
     projected(1, held[0])
-    (sent[1],) = together([sent[1]], [core_0, landed_b])
+    (sent[1],) = together([sent[1]], [core_0] + cache_pieces[1:5])
 
     folded(0, 1, core_0, sent[1])
     core_1, y_0 = hop(1, 0), hop(0, 1)
-    cache_kept, sent_a, sent_b = regroup(
-        splits[0], (kept_a, kept_b, landed_a, landed_b), (held[0],)
-    )
-    landed_a = swap(sent_a, 8)
-    projected(2, held[0], cache_kept)
+    handed(5)
+    handed(6)
+    projected(2, held[0])
     projected(3, held[2])
-    sent[2], sent[3], sent_b = together(
-        [sent[2], sent[3], sent_b], [core_1, y_0, landed_a]
+    sent[2], sent[3] = together(
+        [sent[2], sent[3]], [core_1, y_0, cache_pieces[5], cache_pieces[6]]
     )
 
     core_2, core_3 = hop(2, 0), hop(3, 0)
-    landed_b = swap(sent_b, 8)
+    handed(7)
     folded(1, 1, core_1, sent[2])
     y_1 = hop(1, 1)
     folded(0, 2, y_0, held[1])
     near_0 = hop(0, 2)
     folded(2, 1, core_2, held[0])
     folded(3, 1, core_3, held[2])
-    sent[2], sent[3] = together([sent[2], sent[3]], [y_1, near_0, landed_b])
+    sent[2], sent[3] = together([sent[2], sent[3]], [y_1, near_0, cache_pieces[7]])
 
     y_2 = hop(2, 1)
     folded(0, 3, near_0, sent[2])
     far_0 = hop(0, 3)
     folded(1, 2, y_1, sent[2])
     near_1 = hop(1, 2)
-    cache_kept, cache_sent = regroup(splits[1], (cache_kept, landed_a, landed_b), (held[1],))
-    cache_landed = swap(cache_sent, 4)
-    sent[3], cache_kept = together([sent[3], cache_kept], [y_2, far_0, near_1, cache_landed])
+    (cache_own,) = pack(cache_pieces, [tuple(range(KVH))], [held[1]])
+    cache_other = swap(cache_own, 1)
+    (sent[3],) = together([sent[3]], [y_2, far_0, near_1])
 
     y_3 = hop(3, 1)
     folded(1, 3, near_1, sent[3])
@@ -859,9 +806,7 @@
     query_chunks = [None] * count
     query_chunks[0], pair = finished(0, far_0, held[2])
     pair_other = swap(pair, 1)
-    kept_other = swap(cache_kept, 1)
-    landed_other = swap(cache_landed, 1)
-    (held[3],) = together([held[3]], [y_3, far_1, near_2, pair_other, kept_other, landed_other])
+    (held[3],) = together([held[3]], [y_3, far_1, near_2, pair_other, cache_other])
 
     folded(3, 2, y_3)
     near_3 = hop(3, 2)
@@ -874,7 +819,7 @@
     far_3 = hop(3, 3)
     (query_chunks[2],) = finished(2, far_2, held[3])
     (query_chunks[3],) = finished(3, far_3, query_chunks[2])
-    cache_parts = (cache_kept, cache_landed, kept_other, landed_other)
+    cache_parts = (cache_own, cache_other)
     keys = jnp.where(core == 0, pair, pair_other)
     raw_values = jnp.where(core == 0, pair_other, pair)
     queries = jnp.concatenate(query_chunks, 1).reshape(STEPS, requests, QR, heads, HD)
@@ -886,7 +831,7 @@
         return jnp.pad(value, ((0, 0), (0, TILE - STEPS * QR), (0, 0)))
 
     slot_request, slot_rank, slot_length = slot_layout(request_length, block_table, slots, stripe)
-    source = chip ^ jnp.array(sources_of_cache, dtype=jnp.int32)
+    source = chip ^ jnp.arange(KVH, dtype=jnp.int32)
     sources = jnp.stack([source * 2 + core, source * 2 + 1 - core])
     offset = sources[:, :, None] * BLK + jnp.arange(BLK, dtype=jnp.int32)[None, None, :]
     token = slot_rank[:, None] * stripe + offset.reshape(1, stripe)

time: 280 us -> 230 us (0.82)
  Pallas kernels: 129 us -> 78.2 us
  waiting for transfers between devices: 91.4 us -> 70.8 us
  local copies, waits for them, and re-layouts: 13.2 us -> 31.5 us
  starting transfers between devices: 34.1 us -> 41.2 us
  other arithmetic: 11.1 us -> 6.52 us
    unnamed x24 -> x152, local copies, waits for them, and re-layouts: 0.92 us -> 26.8 us
    ppermute x38 -> x39, waiting for transfers between devices: 91.4 us -> 70.8 us  [swap(): return lax.ppermute(value, 'tensor', [(i, i ^ bit) for i in range(devices)])]
    pallas_call x12, Pallas kernels: 35.1 us -> 17.9 us  [fold(): pl.pallas_call(functools.partial(fold_kernel, steps), grid_spec=pltpu.Pre...]
    pallas_call x4 -> x1, Pallas kernels: 9.42 us -> 0.11 us  [arrange(): pl.pallas_call(arrange_kernel, in_specs=[pl.BlockSpec(memory_space=pltpu....]
    ppermute x38 -> x39, starting transfers between devices: 34.1 us -> 41.2 us  [swap(): return lax.ppermute(value, 'tensor', [(i, i ^ bit) for i in range(devices)])]
    pallas_call x4, Pallas kernels: 33 us -> 26.4 us  [project(): pl.pallas_call(functools.partial(project_kernel, chunk, with_pair), grid_...]
    pallas_call x4, Pallas kernels: 7.6 us -> 1.52 us  [finish(): pl.pallas_call(functools.partial(finish_kernel, len(after)), in_specs=[pl...]
    pallas_call x4, Pallas kernels: 26.8 us -> 21.5 us  [mix(): pl.pallas_call(functools.partial(mix_kernel, len(pieces)), in_specs=[pl.B...]
  transfers between devices with their start and end apart: 38 -> 39, of which waited for: 20 -> 19; matrix products, arithmetic and copies ran while one was open for 7% -> 4% of each run, Pallas kernels for 30% -> 23%
where the time goes in v7:
time: 230 us; the launch traced here: 229 us
  Pallas kernels  78.2 us (34%)
  waiting for transfers between devices  70.8 us (31%)
  starting transfers between devices  41.2 us (18%)
  local copies, waits for them, and re-layouts  31.5 us (14%)
  other arithmetic  6.52 us (3%)
    ppermute x39, waiting for transfers between devices, swap(): return lax.ppermute(value, 'tensor', [(i, i ^ bit) for i in range(devices)])  70.8 us
    ppermute x39, starting transfers between devices, swap(): return lax.ppermute(value, 'tensor', [(i, i ^ bit) for i in range(devices)])  41.2 us
    unnamed x152, local copies, waits for them, and re-layouts  26.8 us
    pallas_call x4, Pallas kernels, project(): pl.pallas_call(functools.partial(project_kernel, chunk, with_pair), grid_...  26.4 us
    pallas_call x4, Pallas kernels, mix(): pl.pallas_call(functools.partial(mix_kernel, len(pieces)), in_specs=[pl.B...  21.5 us
    pallas_call x12, Pallas kernels, fold(): pl.pallas_call(functools.partial(fold_kernel, steps), grid_spec=pltpu.Pre...  17.9 us
    pallas_call x1, Pallas kernels, attend(): pl.pallas_call(attend_kernel, in_specs=[pl.BlockSpec(memory_space=pltpu.S...  8.39 us
  transfers between devices with their start and end apart: 39, of which 19 were waited for; matrix products, arithmetic and copies ran while one was open for 4% of the time, Pallas kernels for 23%

profile of v7, /device:TPU:0, one launch (start us, length us, event | category | flops | bytes accessed | tf_op | source)
XLA Modules:
  0.0 229.3 jit_solution(11779778363464000860)
XLA Ops:
  0.0 1.2 fusion
  1.2 3.0 %collective-permute-start = (f32[2,96]{1,0:T(2,128)S(1)}, f32[2,96]{1,0:T(2,128)S(1)}, u32[]{:S(2)}, u32[]{:S(2)}) collective-permute-start(f32[2,96]{1,0:T(2,128)S(1)} %fusion), channel_id=1, source_target_pairs={{0,2},{1,3},{2,0},{3,1},{4,6},{5,7},{6,4},{7,5},{8,10},{9,11},{10,... | collective-permute-start | bytes 2312 | tf_op jit(solution)/shard_map/ppermute | solution.py:222
  4.3 1.5 collective-permute-done
  5.8 1.1 collective-permute-done.1
  7.0 2.1 collective-permute-start.2
  9.0 1.5 collective-permute-done.2
  10.6 3.0 %collective-permute-start.3 = (f32[2,96]{1,0:T(2,128)S(1)}, f32[2,96]{1,0:T(2,128)S(1)}, u32[]{:S(2)}, u32[]{:S(2)}) collective-permute-start(f32[2,96]{1,0:T(2,128)S(1)} %add.139), channel_id=1, source_target_pairs={{0,8},{1,9},{2,10},{3,11},{4,12},{5,13},{6,14},{7,15},{8,0},{9,1},... | collective-permute-start | bytes 2312 | tf_op jit(solution)/shard_map/ppermute | solution.py:222
  15.1 1.4 copy-done.25
  17.3 6.6 %project.4 = (f32[8,192,384]{2,1,0:T(8,128)S(1)}, s16[1936,384]{1,0:T(8,128)(2,1)S(1)}) custom-call(s32[1]{0:T(128)} %bitcast.2.core, bf16[192,1024]{1,0:T(8,128)(2,1)S(1)} %bitcast.47, bf16[1024,18432]{1,0:T(8,128)(2,1)} %weights.7, bf16[400,256]{1,0:T(8,128)(2,1)S(1)} %get-tuple-element.53.refs_0_), custom_call_target="tpu_custom_call" | custom-call | flops 1 | bytes 1 | tf_op jit(solution)/shard_map/project/pallas_call | solution.py:330
  24.1 1.6 collective-permute-start.5
  25.6 1.6 collective-permute-start.6
  28.6 6.5 %project.5 = (f32[8,192,256]{2,1,0:T(8,128)S(1)}, s16[1936,256]{1,0:T(8,128)(2,1)}) custom-call(s32[1]{0:T(128)} %bitcast.2.core, bf16[192,1024]{1,0:T(8,128)(2,1)S(1)} %bitcast.48, bf16[1024,18432]{1,0:T(8,128)(2,1)} %weights.7, f32[8,192,384]{2,1,0:T(8,128)S(1)} %get-tuple-element.54.refs_0_.held), custom_call_target="tpu_custom_call" | custom-call | flops 1 | bytes 1 | tf_op jit(solution)/shard_map/project/pallas_call | solution.py:330
  35.1 1.2 copy-done.19
  36.3 1.7 collective-permute-done.6.refs_3_.refs_2_
  38.0 3.5 %collective-permute-done.7.refs_4_.refs_3_ = bf16[400,256]{1,0:T(8,128)(2,1)S(1)} collective-permute-done((bf16[400,256]{1,0:T(8,128)(2,1)S(1)}, bf16[400,256]{1,0:T(8,128)(2,1)S(1)}, u32[]{:S(2)}, u32[]{:S(2)}) %collective-permute-start.7) | collective-permute-done | bytes 204832 | tf_op jit(solution)/shard_map/ppermute | solution.py:222
  44.3 3.3 %fold.12 = (f32[4,192,384]{2,1,0:T(8,128)S(1)}, s16[976,384]{1,0:T(8,128)(2,1)S(1)}) custom-call(s32[1]{0:T(128)} %bitcast.5.bit, f32[8,192,384]{2,1,0:T(8,128)} %copy-done, s16[1936,384]{1,0:T(8,128)(2,1)S(1)} %collective-permute-done.4.refs_1_.landed.landed_powers, s16[1936,384]{1,0:T(8,128)(2,1)S(1)} %collective-permute-done.4.refs_1_.landed.landed_powers, ...), custom_call_target="tpu_custom_call" | custom-call | flops 1 | bytes 1 | tf_op jit(solution)/shard_map/fold/pallas_call | solution.py:381
  47.5 1.6 collective-permute-start.9
  49.1 2.5 %collective-permute-start.11 = (bf16[400,256]{1,0:T(8,128)(2,1)S(1)}, bf16[400,256]{1,0:T(8,128)(2,1)S(1)}, u32[]{:S(2)}, u32[]{:S(2)}) collective-permute-start(bf16[400,256]{1,0:T(8,128)(2,1)S(1)} %copy-done.66), channel_id=1, source_target_pairs={{0,10},{1,11},{2,8},{3,9},{4,14},{5,15},{6,12},{7,13},{8,2},{9,3},... | collective-permute-start | bytes 614408 | tf_op jit(solution)/shard_map/ppermute | solution.py:222
  52.5 6.4 %project.6 = (f32[8,192,256]{2,1,0:T(8,128)S(1)}, s16[1936,256]{1,0:T(8,128)(2,1)}) custom-call(s32[1]{0:T(128)} %bitcast.2.core, bf16[192,1024]{1,0:T(8,128)(2,1)S(1)} %bitcast.49, bf16[1024,18432]{1,0:T(8,128)(2,1)} %weights.7, f32[4,192,384]{2,1,0:T(8,128)S(1)} %get-tuple-element.61.refs_0_.held), custom_call_target="tpu_custom_call" | custom-call | flops 1 | bytes 1 | tf_op jit(solution)/shard_map/project/pallas_call | solution.py:330
  58.9 7.0 %project.7 = (f32[8,192,256]{2,1,0:T(8,128)S(1)}, s16[1936,256]{1,0:T(8,128)(2,1)}) custom-call(s32[1]{0:T(128)} %bitcast.2.core, bf16[192,1024]{1,0:T(8,128)(2,1)S(1)} %bitcast.50, bf16[1024,18432]{1,0:T(8,128)(2,1)} %weights.7, f32[8,192,256]{2,1,0:T(8,128)S(1)} %get-tuple-element.65.refs_0_.held), custom_call_target="tpu_custom_call" | custom-call | flops 1 | bytes 1 | tf_op jit(solution)/shard_map/project/pallas_call | solution.py:330
  65.9 1.1 copy-done.21
  67.0 4.1 %collective-permute-done.9.refs_3_.landed.landed_powers = s16[976,384]{1,0:T(8,128)(2,1)S(1)} collective-permute-done((s16[976,384]{1,0:T(8,128)(2,1)S(1)}, s16[976,384]{1,0:T(8,128)(2,1)S(1)}, u32[]{:S(2)}, u32[]{:S(2)}) %collective-permute-start.9) | collective-permute-done | bytes 749600 | tf_op jit(solution)/shard_map/ppermute | solution.py:222
  72.6 1.7 fold.13
  75.2 1.5 collective-permute-start.16
  76.8 1.3 copy-done.4
  78.0 1.1 copy-done.11
  80.1 3.8 %collective-permute-start.17 = (bf16[400,256]{1,0:T(8,128)(2,1)S(1)}, bf16[400,256]{1,0:T(8,128)(2,1)S(1)}, u32[]{:S(2)}, u32[]{:S(2)}) collective-permute-start(bf16[400,256]{1,0:T(8,128)(2,1)S(1)} %copy-done.62), channel_id=1, source_target_pairs={{0,14},{1,15},{2,12},{3,13},{4,10},{5,11},{6,8},{7,9},{8,6},{9,7},... | collective-permute-start | bytes 614408 | tf_op jit(solution)/shard_map/ppermute | solution.py:222
  84.0 2.8 %fold.15 = (f32[4,192,256]{2,1,0:T(8,128)S(1)}, s16[976,256]{1,0:T(8,128)(2,1)S(1)}) custom-call(s32[1]{0:T(128)} %bitcast.5.bit, f32[8,192,256]{2,1,0:T(8,128)S(1)} %copy-done.2, s16[1936,256]{1,0:T(8,128)(2,1)} %collective-permute-done.14.landed.landed_powers, s16[1936,256]{1,0:T(8,128)(2,1)} %collective-permute-done.14.landed.landed_powers, ...), custom_call_target="tpu_custom_call" | custom-call | flops 1 | bytes 1 | tf_op jit(solution)/shard_map/fold/pallas_call | solution.py:381
  86.8 2.9 %fold.16 = (f32[4,192,256]{2,1,0:T(8,128)S(1)}, s16[976,256]{1,0:T(8,128)(2,1)S(1)}) custom-call(s32[1]{0:T(128)} %bitcast.5.bit, f32[8,192,256]{2,1,0:T(8,128)S(1)} %copy-done.22, s16[1936,256]{1,0:T(8,128)(2,1)} %collective-permute-done.15.landed.landed_powers, s16[1936,256]{1,0:T(8,128)(2,1)} %collective-permute-done.15.landed.landed_powers, ...), custom_call_target="tpu_custom_call" | custom-call | flops 1 | bytes 1 | tf_op jit(solution)/shard_map/fold/pallas_call | solution.py:381
  90.6 6.1 %collective-permute-done.17.refs_4_.refs_7_ = bf16[400,256]{1,0:T(8,128)(2,1)S(1)} collective-permute-done((bf16[400,256]{1,0:T(8,128)(2,1)S(1)}, bf16[400,256]{1,0:T(8,128)(2,1)S(1)}, u32[]{:S(2)}, u32[]{:S(2)}) %collective-permute-start.17) | collective-permute-done | bytes 204832 | tf_op jit(solution)/shard_map/ppermute | solution.py:222
  98.7 1.1 fusion.5
  102.1 1.1 copy-done.18
  103.4 1.7 collective-permute-start.18
  105.3 10.4 %collective-permute-done.18.refs_2_.landed = s16[256,384]{1,0:T(8,128)(2,1)S(1)} collective-permute-done((s16[256,384]{1,0:T(8,128)(2,1)S(1)}, s16[256,384]{1,0:T(8,128)(2,1)S(1)}, u32[]{:S(2)}, u32[]{:S(2)}) %collective-permute-start.18) | collective-permute-done | bytes 196640 | tf_op jit(solution)/shard_map/ppermute | solution.py:222
  116.4 1.5 collective-permute-start.23
  119.0 1.1 copy-done.9
  120.2 1.2 fold.19
  122.8 1.8 fold.20
  125.3 2.0 collective-permute-start.21
  127.5 1.1 copy-done.27
  132.5 1.4 collective-permute-done.21.refs_2_.landed
  134.9 1.1 copy-done.16
  136.0 1.1 fold.21
  139.8 2.1 collective-permute-start.26
  142.8 5.9 %collective-permute-done.26.refs_2_.landed = s16[256,256]{1,0:T(8,128)(2,1)S(1)} collective-permute-done((s16[256,256]{1,0:T(8,128)(2,1)}, s16[256,256]{1,0:T(8,128)(2,1)S(1)}, u32[]{:S(2)}, u32[]{:S(2)}) %collective-permute-start.26) | collective-permute-done | bytes 131104 | tf_op jit(solution)/shard_map/ppermute | solution.py:222
  150.3 1.1 finish.5
  154.1 5.2 %collective-permute-done.28.landed = s16[256,256]{1,0:T(8,128)(2,1)S(1)} collective-permute-done((s16[256,256]{1,0:T(8,128)(2,1)}, s16[256,256]{1,0:T(8,128)(2,1)S(1)}, u32[]{:S(2)}, u32[]{:S(2)}) %collective-permute-start.28) | collective-permute-done | bytes 131104 | tf_op jit(solution)/shard_map/ppermute | solution.py:222
  159.6 8.4 %attend.1 = bf16[16,96,128]{2,1,0:T(8,128)(2,1)S(1)} custom-call(s32[24]{0:T(128)S(1)} %copy-done.59, bf16[16,96,128]{2,1,0:T(8,128)(2,1)S(1)} %bitcast.57, bf16[16,16,128]{2,1,0:T(8,128)(2,1)S(1)} %pad.12.new_keys, bf16[16,16,128]{2,1,0:T(8,128)(2,1)S(1)} %copy-done.49, bf16[8,400,256]{2,1,0:T(8,128)(2,1)S(1)} %pack.3.own, ...), custom_call_target="tpu_custom_call" | custom-call | flops 1 | bytes 1 | tf_op jit(solution)/shard_map/attend/pallas_call | solution.py:640
  168.7 3.1 %collective-permute-start.31 = (bf16[192,1024]{1,0:T(8,128)(2,1)S(1)}, bf16[192,1024]{1,0:T(8,128)(2,1)S(1)}, u32[]{:S(2)}, u32[]{:S(2)}) collective-permute-start(bf16[192,1024]{1,0:T(8,128)(2,1)S(1)} %bitcast.54), channel_id=1, source_target_pairs={{0,8},{1,9},{2,10},{3,11},{4,12},{5,13},{6,14},{7,15},{8,0},{9,1},... | collective-permute-start | bytes 1179656 | tf_op jit(solution)/shard_map/ppermute | solution.py:222
  171.8 13.3 %collective-permute-done.29.refs_0_ = bf16[192,1024]{1,0:T(8,128)(2,1)S(1)} collective-permute-done((bf16[192,1024]{1,0:T(8,128)(2,1)S(1)}, bf16[192,1024]{1,0:T(8,128)(2,1)S(1)}, u32[]{:S(2)}, u32[]{:S(2)}) %collective-permute-start.29) | collective-permute-done | bytes 393248 | tf_op jit(solution)/shard_map/ppermute | solution.py:222
  185.2 3.7 %collective-permute-done.31.refs_2_ = bf16[192,1024]{1,0:T(8,128)(2,1)S(1)} collective-permute-done((bf16[192,1024]{1,0:T(8,128)(2,1)S(1)}, bf16[192,1024]{1,0:T(8,128)(2,1)S(1)}, u32[]{:S(2)}, u32[]{:S(2)}) %collective-permute-start.31) | collective-permute-done | bytes 393248 | tf_op jit(solution)/shard_map/ppermute | solution.py:222
  188.9 1.0 pack.4
  189.9 1.5 collective-permute-start.35
  191.4 2.4 %collective-permute-start.33 = (bf16[192,1024]{1,0:T(8,128)(2,1)S(1)}, bf16[192,1024]{1,0:T(8,128)(2,1)}, u32[]{:S(2)}, u32[]{:S(2)}) collective-permute-start(bf16[192,1024]{1,0:T(8,128)(2,1)S(1)} %together.14.refs_0_), channel_id=1, source_target_pairs={{0,12},{1,13},{2,14},{3,15},{4,8},{5,9},{6,10},{7,11},{8,4},{9,5},... | collective-permute-start | bytes 1179656 | tf_op jit(solution)/shard_map/ppermute | solution.py:222
  194.0 3.4 %mix.4.refs_3_ = f32[192,1024]{1,0:T(8,128)S(1)} custom-call(s32[2]{0:T(128)S(1)} %pad_add_fusion.1.places, bf16[192,1024]{1,0:T(8,128)(2,1)S(1)} %together.14.refs_0_, bf16[192,1024]{1,0:T(8,128)(2,1)S(1)} %collective-permute-done.32.refs_3_.refs_1_, bf16[16384,1024]{1,0:T(8,128)(2,1)} %refs_2_.7, bf16[192,1024]{1,0:T(8,128)(2,1)S(1)} %bitcast.51), custom_call_target="tpu_custom_call" | custom-call | flops 1 | bytes 1 | tf_op jit(solution)/shard_map/mix/pallas_call | solution.py:488
  197.4 7.0 %mix.5.refs_2_.refs_3_ = f32[192,1024]{1,0:T(8,128)S(1)} custom-call(s32[6]{0:T(128)S(1)} %stack.82.places, bf16[3,192,1024]{2,1,0:T(8,128)(2,1)S(1)} %get-tuple-element.100.refs_0_, bf16[3,192,1024]{2,1,0:T(8,128)(2,1)} %collective-permute-done.36.refs_1_, bf16[16384,1024]{1,0:T(8,128)(2,1)} %refs_2_.7, f32[192,1024]{1,0:T(8,128)S(1)} %mix.4.refs_3_), custom_call_target="tpu_custom_call" | custom-call | flops 1 | bytes 1 | tf_op jit(solution)/shard_map/mix/pallas_call | solution.py:488
  204.7 5.5 %collective-permute-done.35.refs_0_ = bf16[2,192,1024]{2,1,0:T(8,128)(2,1)} collective-permute-done((bf16[2,192,1024]{2,1,0:T(8,128)(2,1)}, bf16[2,192,1024]{2,1,0:T(8,128)(2,1)}, u32[]{:S(2)}, u32[]{:S(2)}) %collective-permute-start.35) | collective-permute-done | bytes 786464 | tf_op jit(solution)/shard_map/ppermute | solution.py:222
  210.2 1.3 pack.5.refs_0_
  211.5 1.6 collective-permute-start.34
  213.2 1.3 collective-permute-done.37.refs_1_
  214.5 7.0 %mix.6.refs_1_.refs_3_ = f32[192,1024]{1,0:T(8,128)S(1)} custom-call(s32[6]{0:T(128)S(1)} %stack.75.places, bf16[3,192,1024]{2,1,0:T(8,128)(2,1)S(1)} %pack.5.refs_0_, bf16[3,192,1024]{2,1,0:T(8,128)(2,1)} %collective-permute-done.37.refs_1_, bf16[16384,1024]{1,0:T(8,128)(2,1)} %refs_2_.7, f32[192,1024]{1,0:T(8,128)S(1)} %mix.5.refs_2_.refs_3_), custom_call_target="tpu_custom_call" | custom-call | flops 1 | bytes 1 | tf_op jit(solution)/shard_map/mix/pallas_call | solution.py:488
  221.5 1.8 collective-permute-done.34.refs_0_
  223.4 1.6 collective-permute-done.38.refs_1_
  225.0 4.1 %mix.7 = bf16[192,1024]{1,0:T(8,128)(2,1)} custom-call(s32[2]{0:T(128)S(1)} %pad_add_fusion.places, bf16[192,1024]{1,0:T(8,128)(2,1)S(1)} %together.15.refs_0_, bf16[192,1024]{1,0:T(8,128)(2,1)S(1)} %collective-permute-done.38.refs_1_, bf16[16384,1024]{1,0:T(8,128)(2,1)} %refs_2_.7, f32[192,1024]{1,0:T(8,128)S(1)} %mix.6.refs_1_.refs_3_), custom_call_target="tpu_custom_call" | custom-call | flops 1 | bytes 1 | tf_op jit(solution)/shard_map/mix/pallas_call | solution.py:488
  (258 shorter events, 34.3 us)
Async XLA Ops:
  0.0 16.7 %copy-start.5 = (bf16[2,96,1024]{2,1,0:T(8,128)(2,1)S(1)}, bf16[2,96,1024]{2,1,0:T(8,128)(2,1)}, u32[]{:S(2)}) copy-start(bf16[2,96,1024]{2,1,0:T(8,128)(2,1)} %param.8) | copy-start | bytes 1179652
  1.2 4.6 %collective-permute-start = (f32[2,96]{1,0:T(2,128)S(1)}, f32[2,96]{1,0:T(2,128)S(1)}, u32[]{:S(2)}, u32[]{:S(2)}) collective-permute-start(f32[2,96]{1,0:T(2,128)S(1)} %fusion), channel_id=1, source_target_pairs={{0,2},{1,3},{2,0},{3,1},{4,6},{5,7},{6,4},{7,5},{8,10},{9,11},{10,... | collective-permute-start | bytes 2312 | tf_op jit(solution)/shard_map/ppermute | solution.py:222
  5.8 1.1 collective-permute-start.1
  7.0 3.6 %collective-permute-start.2 = (f32[2,96]{1,0:T(2,128)S(1)}, f32[2,96]{1,0:T(2,128)S(1)}, u32[]{:S(2)}, u32[]{:S(2)}) collective-permute-start(f32[2,96]{1,0:T(2,128)S(1)} %add.138), channel_id=1, source_target_pairs={{0,4},{1,5},{2,6},{3,7},{4,0},{5,1},{6,2},{7,3},{8,12},{9,13},{10,... | collective-permute-start | bytes 2312 | tf_op jit(solution)/shard_map/ppermute | solution.py:222
  10.6 6.1 %collective-permute-start.3 = (f32[2,96]{1,0:T(2,128)S(1)}, f32[2,96]{1,0:T(2,128)S(1)}, u32[]{:S(2)}, u32[]{:S(2)}) collective-permute-start(f32[2,96]{1,0:T(2,128)S(1)} %add.139), channel_id=1, source_target_pairs={{0,8},{1,9},{2,10},{3,11},{4,12},{5,13},{6,14},{7,15},{8,0},{9,1},... | collective-permute-start | bytes 2312 | tf_op jit(solution)/shard_map/ppermute | solution.py:222
  16.6 7.3 %copy-start.41 = (bf16[400,256]{1,0:T(8,128)(2,1)}, bf16[400,256]{1,0:T(8,128)(2,1)S(1)}, u32[]{:S(2)}) copy-start(bf16[400,256]{1,0:T(8,128)(2,1)S(1)} %get-tuple-element.53.refs_0_) | copy-start | bytes 614404
  16.6 7.3 %copy-start.63 = (bf16[400,256]{1,0:T(8,128)(2,1)}, bf16[400,256]{1,0:T(8,128)(2,1)S(1)}, u32[]{:S(2)}) copy-start(bf16[400,256]{1,0:T(8,128)(2,1)S(1)} %get-tuple-element.68) | copy-start | bytes 614404
  16.7 7.3 %copy-start.65 = (bf16[400,256]{1,0:T(8,128)(2,1)}, bf16[400,256]{1,0:T(8,128)(2,1)S(1)}, u32[]{:S(2)}) copy-start(bf16[400,256]{1,0:T(8,128)(2,1)S(1)} %get-tuple-element.67) | copy-start | bytes 614404
  24.0 11.1 %copy-start = (f32[8,192,384]{2,1,0:T(8,128)}, f32[8,192,384]{2,1,0:T(8,128)S(1)}, u32[]{:S(2)}) copy-start(f32[8,192,384]{2,1,0:T(8,128)S(1)} %get-tuple-element.54.refs_0_.held) | copy-start | bytes 7077892
  24.0 17.5 %collective-permute-start.4 = (s16[1936,384]{1,0:T(8,128)(2,1)S(1)}, s16[1936,384]{1,0:T(8,128)(2,1)S(1)}, u32[]{:S(2)}, u32[]{:S(2)}) collective-permute-start(s16[1936,384]{1,0:T(8,128)(2,1)S(1)} %get-tuple-element.55), channel_id=1, source_target_pairs={{0,1},{1,0},{2,3},{3,2},{4,5},{5,4},{6,7},{7,6},{8,9},{9,8},{10,11... | collective-permute-start | bytes 4460552 | tf_op jit(solution)/shard_map/ppermute | solution.py:222
  24.1 12.2 %collective-permute-start.5 = (bf16[400,256]{1,0:T(8,128)(2,1)S(1)}, bf16[400,256]{1,0:T(8,128)(2,1)S(1)}, u32[]{:S(2)}, u32[]{:S(2)}) collective-permute-start(bf16[400,256]{1,0:T(8,128)(2,1)S(1)} %get-tuple-element.57), channel_id=1, source_target_pairs={{0,2},{1,3},{2,0},{3,1},{4,6},{5,7},{6,4},{7,5},{8,10},{9,11},{10,... | collective-permute-start | bytes 614408 | tf_op jit(solution)/shard_map/ppermute | solution.py:222
  25.6 12.3 %collective-permute-start.6 = (bf16[400,256]{1,0:T(8,128)(2,1)S(1)}, bf16[400,256]{1,0:T(8,128)(2,1)S(1)}, u32[]{:S(2)}, u32[]{:S(2)}) collective-permute-start(bf16[400,256]{1,0:T(8,128)(2,1)S(1)} %get-tuple-element.58), channel_id=1, source_target_pairs={{0,4},{1,5},{2,6},{3,7},{4,0},{5,1},{6,2},{7,3},{8,12},{9,13},{10,... | collective-permute-start | bytes 614408 | tf_op jit(solution)/shard_map/ppermute | solution.py:222
  27.2 14.3 %collective-permute-start.7 = (bf16[400,256]{1,0:T(8,128)(2,1)S(1)}, bf16[400,256]{1,0:T(8,128)(2,1)S(1)}, u32[]{:S(2)}, u32[]{:S(2)}) collective-permute-start(bf16[400,256]{1,0:T(8,128)(2,1)S(1)} %get-tuple-element.59), channel_id=1, source_target_pairs={{0,6},{1,7},{2,4},{3,5},{4,2},{5,3},{6,0},{7,1},{8,14},{9,15},{10,... | collective-permute-start | bytes 614408 | tf_op jit(solution)/shard_map/ppermute | solution.py:222
  27.6 13.9 %collective-permute-start.8 = (bf16[400,256]{1,0:T(8,128)(2,1)S(1)}, bf16[400,256]{1,0:T(8,128)(2,1)S(1)}, u32[]{:S(2)}, u32[]{:S(2)}) collective-permute-start(bf16[400,256]{1,0:T(8,128)(2,1)S(1)} %get-tuple-element.60), channel_id=1, source_target_pairs={{0,8},{1,9},{2,10},{3,11},{4,12},{5,13},{6,14},{7,15},{8,0},{9,1},... | collective-permute-start | bytes 614408 | tf_op jit(solution)/shard_map/ppermute | solution.py:222
  44.3 26.9 %collective-permute-start.10 = (s16[1936,256]{1,0:T(8,128)(2,1)}, s16[1936,256]{1,0:T(8,128)(2,1)S(1)}, u32[]{:S(2)}, u32[]{:S(2)}) collective-permute-start(s16[1936,256]{1,0:T(8,128)(2,1)} %together.8.refs_0_), channel_id=1, source_target_pairs={{0,1},{1,0},{2,3},{3,2},{4,5},{5,4},{6,7},{7,6},{8,9},{9,8},{10,11... | collective-permute-start | bytes 2973704 | tf_op jit(solution)/shard_map/ppermute | solution.py:222
  44.3 4.9 %copy-start.66 = (bf16[400,256]{1,0:T(8,128)(2,1)S(1)}, bf16[400,256]{1,0:T(8,128)(2,1)}, u32[]{:S(2)}) copy-start(bf16[400,256]{1,0:T(8,128)(2,1)} %copy-done.65) | copy-start | bytes 614404
  44.3 7.3 %copy-start.64 = (bf16[400,256]{1,0:T(8,128)(2,1)S(1)}, bf16[400,256]{1,0:T(8,128)(2,1)}, u32[]{:S(2)}) copy-start(bf16[400,256]{1,0:T(8,128)(2,1)} %copy-done.63) | copy-start | bytes 614404
  47.5 11.3 %copy-start.3 = (f32[4,192,384]{2,1,0:T(8,128)}, f32[4,192,384]{2,1,0:T(8,128)S(1)}, u32[]{:S(2)}) copy-start(f32[4,192,384]{2,1,0:T(8,128)S(1)} %get-tuple-element.61.refs_0_.held) | copy-start | bytes 3538948
  47.5 23.6 %collective-permute-start.9 = (s16[976,384]{1,0:T(8,128)(2,1)S(1)}, s16[976,384]{1,0:T(8,128)(2,1)S(1)}, u32[]{:S(2)}, u32[]{:S(2)}) collective-permute-start(s16[976,384]{1,0:T(8,128)(2,1)S(1)} %get-tuple-element.62), channel_id=1, source_target_pairs={{0,2},{1,3},{2,0},{3,1},{4,6},{5,7},{6,4},{7,5},{8,10},{9,11},{10,... | collective-permute-start | bytes 2248712 | tf_op jit(solution)/shard_map/ppermute | solution.py:222
  49.1 17.9 %collective-permute-start.11 = (bf16[400,256]{1,0:T(8,128)(2,1)S(1)}, bf16[400,256]{1,0:T(8,128)(2,1)S(1)}, u32[]{:S(2)}, u32[]{:S(2)}) collective-permute-start(bf16[400,256]{1,0:T(8,128)(2,1)S(1)} %copy-done.66), channel_id=1, source_target_pairs={{0,10},{1,11},{2,8},{3,9},{4,14},{5,15},{6,12},{7,13},{8,2},{9,3},... | collective-permute-start | bytes 614408 | tf_op jit(solution)/shard_map/ppermute | solution.py:222
  51.6 15.4 %collective-permute-start.12 = (bf16[400,256]{1,0:T(8,128)(2,1)S(1)}, bf16[400,256]{1,0:T(8,128)(2,1)S(1)}, u32[]{:S(2)}, u32[]{:S(2)}) collective-permute-start(bf16[400,256]{1,0:T(8,128)(2,1)S(1)} %copy-done.64), channel_id=1, source_target_pairs={{0,12},{1,13},{2,14},{3,15},{4,8},{5,9},{6,10},{7,11},{8,4},{9,5},... | collective-permute-start | bytes 614408 | tf_op jit(solution)/shard_map/ppermute | solution.py:222
  58.9 7.0 %copy-start.1 = (f32[8,192,256]{2,1,0:T(8,128)}, f32[8,192,256]{2,1,0:T(8,128)S(1)}, u32[]{:S(2)}) copy-start(f32[8,192,256]{2,1,0:T(8,128)S(1)} %get-tuple-element.65.refs_0_.held) | copy-start | bytes 4718596
  67.0 4.1 %copy-start.37 = (bf16[400,256]{1,0:T(8,128)(2,1)}, bf16[400,256]{1,0:T(8,128)(2,1)S(1)}, u32[]{:S(2)}) copy-start(bf16[400,256]{1,0:T(8,128)(2,1)S(1)} %collective-permute-done.11.refs_4_.refs_5_) | copy-start | bytes 614404
  67.0 4.1 %copy-start.39 = (bf16[400,256]{1,0:T(8,128)(2,1)}, bf16[400,256]{1,0:T(8,128)(2,1)S(1)}, u32[]{:S(2)}) copy-start(bf16[400,256]{1,0:T(8,128)(2,1)S(1)} %collective-permute-done.12.refs_5_.refs_6_) | copy-start | bytes 614404
  71.2 12.8 %collective-permute-start.14 = (s16[1936,256]{1,0:T(8,128)(2,1)}, s16[1936,256]{1,0:T(8,128)(2,1)}, u32[]{:S(2)}, u32[]{:S(2)}) collective-permute-start(s16[1936,256]{1,0:T(8,128)(2,1)} %get-tuple-element.69.refs_0_), channel_id=1, source_target_pairs={{0,1},{1,0},{2,3},{3,2},{4,5},{5,4},{6,7},{7,6},{8,9},{9,8},{10,11... | collective-permute-start | bytes 2973704 | tf_op jit(solution)/shard_map/ppermute | solution.py:222
  71.3 15.5 %collective-permute-start.15 = (s16[1936,256]{1,0:T(8,128)(2,1)}, s16[1936,256]{1,0:T(8,128)(2,1)}, u32[]{:S(2)}, u32[]{:S(2)}) collective-permute-start(s16[1936,256]{1,0:T(8,128)(2,1)} %get-tuple-element.75), channel_id=1, source_target_pairs={{0,1},{1,0},{2,3},{3,2},{4,5},{5,4},{6,7},{7,6},{8,9},{9,8},{10,11... | collective-permute-start | bytes 2973704 | tf_op jit(solution)/shard_map/ppermute | solution.py:222
  72.6 4.1 %copy-start.73 = (s32[16]{0:T(128)S(1)}, s32[16]{0:T(128)}, u32[]{:S(2)}) copy-start(s32[16]{0:T(128)} %param.14) | copy-start | bytes 196
  75.2 21.5 %collective-permute-start.16 = (s16[976,256]{1,0:T(8,128)(2,1)}, s16[976,256]{1,0:T(8,128)(2,1)S(1)}, u32[]{:S(2)}, u32[]{:S(2)}) collective-permute-start(s16[976,256]{1,0:T(8,128)(2,1)} %get-tuple-element.78), channel_id=1, source_target_pairs={{0,2},{1,3},{2,0},{3,1},{4,6},{5,7},{6,4},{7,5},{8,10},{9,11},{10,... | collective-permute-start | bytes 1499144 | tf_op jit(solution)/shard_map/ppermute | solution.py:222
  79.2 4.8 %copy-start.2 = (f32[8,192,256]{2,1,0:T(8,128)S(1)}, f32[8,192,256]{2,1,0:T(8,128)}, u32[]{:S(2)}) copy-start(f32[8,192,256]{2,1,0:T(8,128)} %copy-done.1) | copy-start | bytes 4718596
  79.8 6.9 %copy-start.17 = (f32[2,192,384]{2,1,0:T(8,128)}, f32[2,192,384]{2,1,0:T(8,128)S(1)}, u32[]{:S(2)}) copy-start(f32[2,192,384]{2,1,0:T(8,128)S(1)} %get-tuple-element.71.refs_0_.held) | copy-start | bytes 1769476
  79.9 16.8 %collective-permute-start.13 = (s16[496,384]{1,0:T(8,128)(2,1)S(1)}, s16[496,384]{1,0:T(8,128)(2,1)S(1)}, u32[]{:S(2)}, u32[]{:S(2)}) collective-permute-start(s16[496,384]{1,0:T(8,128)(2,1)S(1)} %get-tuple-element.72), channel_id=1, source_target_pairs={{0,4},{1,5},{2,6},{3,7},{4,0},{5,1},{6,2},{7,3},{8,12},{9,13},{10,... | collective-permute-start | bytes 1142792 | tf_op jit(solution)/shard_map/ppermute | solution.py:222
  80.1 16.6 %collective-permute-start.17 = (bf16[400,256]{1,0:T(8,128)(2,1)S(1)}, bf16[400,256]{1,0:T(8,128)(2,1)S(1)}, u32[]{:S(2)}, u32[]{:S(2)}) collective-permute-start(bf16[400,256]{1,0:T(8,128)(2,1)S(1)} %copy-done.62), channel_id=1, source_target_pairs={{0,14},{1,15},{2,12},{3,13},{4,10},{5,11},{6,8},{7,9},{8,6},{9,7},... | collective-permute-start | bytes 614408 | tf_op jit(solution)/shard_map/ppermute | solution.py:222
  86.7 2.9 %copy-start.8 = (f32[4,192,256]{2,1,0:T(8,128)}, f32[4,192,256]{2,1,0:T(8,128)S(1)}, u32[]{:S(2)}) copy-start(f32[4,192,256]{2,1,0:T(8,128)S(1)} %get-tuple-element.76.refs_0_.held) | copy-start | bytes 2359300
  90.6 6.2 %copy-start.12 = (f32[4,192,256]{2,1,0:T(8,128)S(1)}, f32[4,192,256]{2,1,0:T(8,128)}, u32[]{:S(2)}) copy-start(f32[4,192,256]{2,1,0:T(8,128)} %copy-done.10) | copy-start | bytes 2359300
  98.4 35.5 %collective-permute-start.25 = (bf16[8,400,256]{2,1,0:T(8,128)(2,1)S(1)}, bf16[8,400,256]{2,1,0:T(8,128)(2,1)}, u32[]{:S(2)}, u32[]{:S(2)}) collective-permute-start(bf16[8,400,256]{2,1,0:T(8,128)(2,1)S(1)} %pack.3.own), channel_id=1, source_target_pairs={{0,1},{1,0},{2,3},{3,2},{4,5},{5,4},{6,7},{7,6},{8,9},{9,8},{10,11... | collective-permute-start | bytes 4915208 | tf_op jit(solution)/shard_map/ppermute | solution.py:222
  99.8 15.9 %collective-permute-start.19 = (s16[976,256]{1,0:T(8,128)(2,1)S(1)}, s16[976,256]{1,0:T(8,128)(2,1)S(1)}, u32[]{:S(2)}, u32[]{:S(2)}) collective-permute-start(s16[976,256]{1,0:T(8,128)(2,1)S(1)} %get-tuple-element.80.refs_0_), channel_id=1, source_target_pairs={{0,2},{1,3},{2,0},{3,1},{4,6},{5,7},{6,4},{7,5},{8,10},{9,11},{10,... | collective-permute-start | bytes 1499144 | tf_op jit(solution)/shard_map/ppermute | solution.py:222
  101.1 14.6 %collective-permute-start.20 = (s16[496,256]{1,0:T(8,128)(2,1)}, s16[496,256]{1,0:T(8,128)(2,1)}, u32[]{:S(2)}, u32[]{:S(2)}) collective-permute-start(s16[496,256]{1,0:T(8,128)(2,1)} %copy-done.60), channel_id=1, source_target_pairs={{0,4},{1,5},{2,6},{3,7},{4,0},{5,1},{6,2},{7,3},{8,12},{9,13},{10,... | collective-permute-start | bytes 761864 | tf_op jit(solution)/shard_map/ppermute | solution.py:222
  103.4 14.5 %copy-start.47 = (f32[1,192,384]{2,1,0:T(8,128)}, f32[1,192,384]{2,1,0:T(8,128)S(1)}, u32[]{:S(2)}) copy-start(f32[1,192,384]{2,1,0:T(8,128)S(1)} %get-tuple-element.81.held) | copy-start | bytes 884740
  103.4 12.2 %collective-permute-start.18 = (s16[256,384]{1,0:T(8,128)(2,1)S(1)}, s16[256,384]{1,0:T(8,128)(2,1)S(1)}, u32[]{:S(2)}, u32[]{:S(2)}) collective-permute-start(s16[256,384]{1,0:T(8,128)(2,1)S(1)} %get-tuple-element.82), channel_id=1, source_target_pairs={{0,8},{1,9},{2,10},{3,11},{4,12},{5,13},{6,14},{7,15},{8,0},{9,1},... | collective-permute-start | bytes 589832 | tf_op jit(solution)/shard_map/ppermute | solution.py:222
  116.4 17.5 %collective-permute-start.23 = (s16[976,256]{1,0:T(8,128)(2,1)S(1)}, s16[976,256]{1,0:T(8,128)(2,1)S(1)}, u32[]{:S(2)}, u32[]{:S(2)}) collective-permute-start(s16[976,256]{1,0:T(8,128)(2,1)S(1)} %together.11.refs_0_), channel_id=1, source_target_pairs={{0,2},{1,3},{2,0},{3,1},{4,6},{5,7},{6,4},{7,5},{8,10},{9,11},{10,... | collective-permute-start | bytes 1499144 | tf_op jit(solution)/shard_map/ppermute | solution.py:222
  120.2 7.1 %copy-start.67 = (f32[192,64]{1,0:T(8,128)S(1)}, f32[192,64]{1,0:T(8,128)}, u32[]{:S(2)}) copy-start(f32[192,64]{1,0:T(8,128)} %get-tuple-element.108) | copy-start | bytes 147460
  120.2 7.1 %copy-start.68 = (f32[192,64]{1,0:T(8,128)S(1)}, f32[192,64]{1,0:T(8,128)}, u32[]{:S(2)}) copy-start(f32[192,64]{1,0:T(8,128)} %get-tuple-element.109) | copy-start | bytes 147460
  120.2 7.1 %copy-start.69 = (f32[192,64]{1,0:T(8,128)S(1)}, f32[192,64]{1,0:T(8,128)}, u32[]{:S(2)}) copy-start(f32[192,64]{1,0:T(8,128)} %get-tuple-element.110) | copy-start | bytes 147460
  122.1 11.7 %collective-permute-start.22 = (s16[496,256]{1,0:T(8,128)(2,1)}, s16[496,256]{1,0:T(8,128)(2,1)S(1)}, u32[]{:S(2)}, u32[]{:S(2)}) collective-permute-start(s16[496,256]{1,0:T(8,128)(2,1)} %get-tuple-element.90), channel_id=1, source_target_pairs={{0,4},{1,5},{2,6},{3,7},{4,0},{5,1},{6,2},{7,3},{8,12},{9,13},{10,... | collective-permute-start | bytes 761864 | tf_op jit(solution)/shard_map/ppermute | solution.py:222
  125.3 8.6 %collective-permute-start.21 = (s16[256,256]{1,0:T(8,128)(2,1)}, s16[256,256]{1,0:T(8,128)(2,1)}, u32[]{:S(2)}, u32[]{:S(2)}) collective-permute-start(s16[256,256]{1,0:T(8,128)(2,1)} %get-tuple-element.89), channel_id=1, source_target_pairs={{0,8},{1,9},{2,10},{3,11},{4,12},{5,13},{6,14},{7,15},{8,0},{9,1},... | collective-permute-start | bytes 393224 | tf_op jit(solution)/shard_map/ppermute | solution.py:222
  127.4 6.4 %copy-start.14 = (f32[4,192,256]{2,1,0:T(8,128)S(1)}, f32[4,192,256]{2,1,0:T(8,128)}, u32[]{:S(2)}) copy-start(f32[4,192,256]{2,1,0:T(8,128)} %copy-done.13) | copy-start | bytes 2359300
  131.2 1.2 collective-permute-start.24
  137.2 11.6 %collective-permute-start.27 = (s16[496,256]{1,0:T(8,128)(2,1)}, s16[496,256]{1,0:T(8,128)(2,1)S(1)}, u32[]{:S(2)}, u32[]{:S(2)}) collective-permute-start(s16[496,256]{1,0:T(8,128)(2,1)} %get-tuple-element.96), channel_id=1, source_target_pairs={{0,4},{1,5},{2,6},{3,7},{4,0},{5,1},{6,2},{7,3},{8,12},{9,13},{10,... | collective-permute-start | bytes 761864 | tf_op jit(solution)/shard_map/ppermute | solution.py:222
  139.8 8.9 %collective-permute-start.26 = (s16[256,256]{1,0:T(8,128)(2,1)}, s16[256,256]{1,0:T(8,128)(2,1)S(1)}, u32[]{:S(2)}, u32[]{:S(2)}) collective-permute-start(s16[256,256]{1,0:T(8,128)(2,1)} %get-tuple-element.95), channel_id=1, source_target_pairs={{0,8},{1,9},{2,10},{3,11},{4,12},{5,13},{6,14},{7,15},{8,0},{9,1},... | collective-permute-start | bytes 393224 | tf_op jit(solution)/shard_map/ppermute | solution.py:222
  152.2 7.1 %copy-start.56 = (bf16[192,256]{1,0:T(8,128)(2,1)S(1)}, bf16[192,256]{1,0:T(8,128)(2,1)}, u32[]{:S(2)}) copy-start(bf16[192,256]{1,0:T(8,128)(2,1)} %copy-done.55) | copy-start | bytes 294916
  152.2 7.0 %collective-permute-start.28 = (s16[256,256]{1,0:T(8,128)(2,1)}, s16[256,256]{1,0:T(8,128)(2,1)S(1)}, u32[]{:S(2)}, u32[]{:S(2)}) collective-permute-start(s16[256,256]{1,0:T(8,128)(2,1)} %get-tuple-element.98), channel_id=1, source_target_pairs={{0,8},{1,9},{2,10},{3,11},{4,12},{5,13},{6,14},{7,15},{8,0},{9,1},... | collective-permute-start | bytes 393224 | tf_op jit(solution)/shard_map/ppermute | solution.py:222
  154.0 5.5 %copy-start.49 = (bf16[16,16,128]{2,1,0:T(8,128)(2,1)S(1)}, bf16[16,16,128]{2,1,0:T(8,128)(2,1)}, u32[]{:S(2)}) copy-start(bf16[16,16,128]{2,1,0:T(8,128)(2,1)} %pad.13.new_values) | copy-start | bytes 196612
  154.0 5.5 %copy-start.50 = (f32[96,16]{1,0:T(8,128)S(1)}, f32[96,16]{1,0:T(8,128)}, u32[]{:S(2)}) copy-start(f32[96,16]{1,0:T(8,128)} %fusion.4.new_bias) | copy-start | bytes 18436
  154.0 5.5 %copy-start.59 = (s32[24]{0:T(128)S(1)}, s32[24]{0:T(128)}, u32[]{:S(2)}) copy-start(s32[24]{0:T(128)} %get-tuple-element.103.slot_request) | copy-start | bytes 292
  168.1 17.1 %collective-permute-start.29 = (bf16[192,1024]{1,0:T(8,128)(2,1)S(1)}, bf16[192,1024]{1,0:T(8,128)(2,1)S(1)}, u32[]{:S(2)}, u32[]{:S(2)}) collective-permute-start(bf16[192,1024]{1,0:T(8,128)(2,1)S(1)} %bitcast.52), channel_id=1, source_target_pairs={{0,4},{1,5},{2,6},{3,7},{4,0},{5,1},{6,2},{7,3},{8,12},{9,13},{10,... | collective-permute-start | bytes 1179656 | tf_op jit(solution)/shard_map/ppermute | solution.py:222
  168.2 17.0 %collective-permute-start.30 = (bf16[192,1024]{1,0:T(8,128)(2,1)S(1)}, bf16[192,1024]{1,0:T(8,128)(2,1)S(1)}, u32[]{:S(2)}, u32[]{:S(2)}) collective-permute-start(bf16[192,1024]{1,0:T(8,128)(2,1)S(1)} %bitcast.53), channel_id=1, source_target_pairs={{0,2},{1,3},{2,0},{3,1},{4,6},{5,7},{6,4},{7,5},{8,10},{9,11},{10,... | collective-permute-start | bytes 1179656 | tf_op jit(solution)/shard_map/ppermute | solution.py:222
  168.7 20.1 %collective-permute-start.31 = (bf16[192,1024]{1,0:T(8,128)(2,1)S(1)}, bf16[192,1024]{1,0:T(8,128)(2,1)S(1)}, u32[]{:S(2)}, u32[]{:S(2)}) collective-permute-start(bf16[192,1024]{1,0:T(8,128)(2,1)S(1)} %bitcast.54), channel_id=1, source_target_pairs={{0,8},{1,9},{2,10},{3,11},{4,12},{5,13},{6,14},{7,15},{8,0},{9,1},... | collective-permute-start | bytes 1179656 | tf_op jit(solution)/shard_map/ppermute | solution.py:222
  171.8 17.0 %collective-permute-start.32 = (bf16[192,1024]{1,0:T(8,128)(2,1)S(1)}, bf16[192,1024]{1,0:T(8,128)(2,1)S(1)}, u32[]{:S(2)}, u32[]{:S(2)}) collective-permute-start(bf16[192,1024]{1,0:T(8,128)(2,1)S(1)} %bitcast.55), channel_id=1, source_target_pairs={{0,1},{1,0},{2,3},{3,2},{4,5},{5,4},{6,7},{7,6},{8,9},{9,8},{10,11... | collective-permute-start | bytes 1179656 | tf_op jit(solution)/shard_map/ppermute | solution.py:222
  189.9 7.5 %collective-permute-start.36 = (bf16[3,192,1024]{2,1,0:T(8,128)(2,1)S(1)}, bf16[3,192,1024]{2,1,0:T(8,128)(2,1)}, u32[]{:S(2)}, u32[]{:S(2)}) collective-permute-start(bf16[3,192,1024]{2,1,0:T(8,128)(2,1)S(1)} %get-tuple-element.100.refs_0_), channel_id=1, source_target_pairs={{0,1},{1,0},{2,3},{3,2},{4,5},{5,4},{6,7},{7,6},{8,9},{9,8},{10,11... | collective-permute-start | bytes 3538952 | tf_op jit(solution)/shard_map/ppermute | solution.py:222
  189.9 20.3 %collective-permute-start.35 = (bf16[2,192,1024]{2,1,0:T(8,128)(2,1)}, bf16[2,192,1024]{2,1,0:T(8,128)(2,1)}, u32[]{:S(2)}, u32[]{:S(2)}) collective-permute-start(bf16[2,192,1024]{2,1,0:T(8,128)(2,1)} %get-tuple-element.99.refs_1_), channel_id=1, source_target_pairs={{0,2},{1,3},{2,0},{3,1},{4,6},{5,7},{6,4},{7,5},{8,10},{9,11},{10,... | collective-permute-start | bytes 2359304 | tf_op jit(solution)/shard_map/ppermute | solution.py:222
  191.4 13.3 %collective-permute-start.33 = (bf16[192,1024]{1,0:T(8,128)(2,1)S(1)}, bf16[192,1024]{1,0:T(8,128)(2,1)}, u32[]{:S(2)}, u32[]{:S(2)}) collective-permute-start(bf16[192,1024]{1,0:T(8,128)(2,1)S(1)} %together.14.refs_0_), channel_id=1, source_target_pairs={{0,12},{1,13},{2,14},{3,15},{4,8},{5,9},{6,10},{7,11},{8,4},{9,5},... | collective-permute-start | bytes 1179656 | tf_op jit(solution)/shard_map/ppermute | solution.py:222
  211.5 3.0 %collective-permute-start.37 = (bf16[3,192,1024]{2,1,0:T(8,128)(2,1)S(1)}, bf16[3,192,1024]{2,1,0:T(8,128)(2,1)}, u32[]{:S(2)}, u32[]{:S(2)}) collective-permute-start(bf16[3,192,1024]{2,1,0:T(8,128)(2,1)S(1)} %pack.5.refs_0_), channel_id=1, source_target_pairs={{0,1},{1,0},{2,3},{3,2},{4,5},{5,4},{6,7},{7,6},{8,9},{9,8},{10,11... | collective-permute-start | bytes 3538952 | tf_op jit(solution)/shard_map/ppermute | solution.py:222
  211.5 11.7 %collective-permute-start.34 = (bf16[192,1024]{1,0:T(8,128)(2,1)}, bf16[192,1024]{1,0:T(8,128)(2,1)S(1)}, u32[]{:S(2)}, u32[]{:S(2)}) collective-permute-start(bf16[192,1024]{1,0:T(8,128)(2,1)} %collective-permute-done.33.refs_1_), channel_id=1, source_target_pairs={{0,2},{1,3},{2,0},{3,1},{4,6},{5,7},{6,4},{7,5},{8,10},{9,11},{10,... | collective-permute-start | bytes 1179656 | tf_op jit(solution)/shard_map/ppermute | solution.py:222
  223.3 1.7 collective-permute-start.38
  (50 other events, 58.6 us)

commit v8 on v7

--- a/solution.py
+++ b/solution.py
@@ -285,107 +285,152 @@
         sent[pl.ds(steps * rows, TILE), :] = powers[...].astype(jnp.int32).astype(jnp.int16)
 
 
-def project_kernel(chunk, with_pair, core, normed, weights, *refs):
-    kept, sent, powers, wide, arrived = refs[-5:]
+SLABS = 4
+PART_HEADS = GQ // 4
+
+
+def project_kernel(core, normed, weights, *refs):
+    outs, scratch = refs[-8:-4], refs[-4:]
+    kept, sent = outs[:2], outs[2:]
+    powers, slabs, arrived = scratch[:2], scratch[2], scratch[3]
     index = pl.program_id(0)
-    columns = kept.shape[2]
+    mine = GQ // 2 * HD
+    half = mine + HD
 
     def copies(group):
+        slot = group % SLABS
         found = []
         for side in range(2):
             owner = core[0] if side == 0 else 1 - core[0]
-            first = group * GW + owner * (GQ // 2 * HD) + chunk * (2 * HD)
-            spans = [(first, 0, 2 * HD)]
-            if with_pair:
-                spans.append((group * GW + (GQ + owner) * HD, 2 * HD, HD))
+            spans = (
+                (group * GW + owner * mine, 0, mine),
+                (group * GW + (GQ + owner) * HD, mine, HD),
+            )
             for number, (start, offset, size) in enumerate(spans):
                 found.append(
                     pltpu.make_async_copy(
                         weights.at[:, pl.ds(pl.multiple_of(start, HD), size)],
-                        wide.at[group, :, pl.ds(side * columns + offset, size)],
-                        arrived.at[group, side, number],
+                        slabs.at[slot, :, pl.ds(side * half + offset, size)],
+                        arrived.at[slot, side, number],
                     )
                 )
         return found
 
     @pl.when(index == 0)
     def _():
-        for group in range(KVH):
+        for group in range(SLABS):
             for copy in copies(group):
                 copy.start()
-        powers[...] = jnp.zeros_like(powers)
+        for ref in powers:
+            ref[...] = jnp.zeros_like(ref)
 
     for copy in copies(index):
         copy.wait()
 
-    product = jnp.dot(normed[...], wide[index], preferred_element_type=jnp.float32)
-    kept[0] = product[:, :columns]
-    store_codes(sent, powers, product[:, columns:], index, KVH)
-
-
-def project(core, normed, qkv_weight, chunk, with_pair, after):
+    slot = index % SLABS
+    part = PART_HEADS * HD
+    spans = (((0, part), (mine, HD)), ((part, part),))
+    for side in range(2):
+        for number in range(2):
+            offset = 0
+            found = []
+            for first, size in spans[number]:
+                for start in range(0, size, 2 * HD):
+                    wide = min(2 * HD, size - start)
+                    product = jnp.dot(
+                        normed[...],
+                        slabs[slot, :, side * half + first + start : side * half + first + start + wide],
+                        preferred_element_type=jnp.float32,
+                    )
+                    at = slice(offset, offset + wide)
+                    if side == 0:
+                        kept[number][0, :, at] = product
+                    else:
+                        rows = coded_rows(product.shape[0])
+                        codes, power = encode(product)
+                        sent[number][pl.ds(pl.multiple_of(index * rows, TILE), rows), at] = codes
+                        found.append(power)
+                    offset += wide
+            if found:
+                powers[number][pl.ds(index, 1), :] = jnp.concatenate(found, 1)
+
+    @pl.when(index + SLABS < KVH)
+    def _():
+        for copy in copies(index + SLABS):
+            copy.start()
+
+    @pl.when(index == KVH - 1)
+    def _():
+        for target, ref in zip(sent, powers):
+            target[pl.ds(target.shape[0] - TILE, TILE), :] = (
+                ref[...].astype(jnp.int32).astype(jnp.int16)
+            )
+
+
+def project(core, normed, qkv_weight, after):
     rows, width = normed.shape
-    columns = 2 * HD + (HD if with_pair else 0)
+    columns = (PART_HEADS * HD + HD, PART_HEADS * HD)
     sent_rows = KVH * coded_rows(rows) + TILE
     return pl.pallas_call(
-        functools.partial(project_kernel, chunk, with_pair),
+        project_kernel,
         grid_spec=pltpu.PrefetchScalarGridSpec(
             num_scalar_prefetch=1,
             grid=(KVH,),
             in_specs=[pl.BlockSpec((rows, width), lambda t, c: (0, 0))]
             + [pl.BlockSpec(memory_space=pl.ANY)] * (1 + len(after)),
-            out_specs=[
-                pl.BlockSpec((1, rows, columns), lambda t, c: (t, 0, 0)),
-                pl.BlockSpec((sent_rows, columns), lambda t, c: (0, 0)),
-            ],
-            scratch_shapes=[
-                pltpu.VMEM((TILE, columns), jnp.float32),
-                pltpu.VMEM((KVH, width, 2 * columns), jnp.bfloat16),
-                pltpu.SemaphoreType.DMA((KVH, 2, 2)),
+            out_specs=[pl.BlockSpec((1, rows, n), lambda t, c: (t, 0, 0)) for n in columns]
+            + [pl.BlockSpec((sent_rows, n), lambda t, c: (0, 0)) for n in columns],
+            scratch_shapes=[pltpu.VMEM((TILE, n), jnp.float32) for n in columns]
+            + [
+                pltpu.VMEM((SLABS, width, GW), jnp.bfloat16),
+                pltpu.SemaphoreType.DMA((SLABS, 2, 2)),
             ],
         ),
-        out_shape=[
-            jax.ShapeDtypeStruct((KVH, rows, columns), jnp.float32),
-            jax.ShapeDtypeStruct((sent_rows, columns), jnp.int16),
-        ],
+        out_shape=[jax.ShapeDtypeStruct((KVH, rows, n), jnp.float32) for n in columns]
+        + [jax.ShapeDtypeStruct((sent_rows, n), jnp.int16) for n in columns],
         compiler_params=pltpu.CompilerParams(vmem_limit_bytes=VMEM_LIMIT),
         cost_estimate=SHORT,
         name="project",
     )(core, normed, qkv_weight, *after)
 
 
-def fold_kernel(steps, bit, held, landed, landed_powers, *refs):
+def fold_kernel(steps, low, bit, held, held_out, landed, landed_out, landed_powers, *refs):
     kept, sent, powers = refs[-3:]
     index = pl.program_id(0)
-    rows = coded_rows(held.shape[1])
     rows_of_powers = landed_powers[...].astype(jnp.int32).astype(jnp.float32)
-
-    def total(side):
-        place = pl.multiple_of(side * rows, TILE)
-        codes = landed[pl.ds(place, rows), :]
-        return held[side] + decode(codes, pick_row(rows_of_powers, 2 * index + side))
+    first = index // low * (2 * low) + index % low
+
+    def total(side, block, codes):
+        power = pick_row(rows_of_powers, first + side * low)
+        return block[0] + decode(codes[...], power)
 
     @pl.when(index == 0)
     def _():
         powers[...] = jnp.zeros_like(powers)
 
-    mine = bit[0]
-    kept[0] = total(mine)
-    store_codes(sent, powers, total(1 - mine), index, steps)
-
-
-def fold(bit, held, landed, after):
+    kept[0] = total(bit[0], held, landed)
+    store_codes(sent, powers, total(1 - bit[0], held_out, landed_out), index, steps)
+
+
+def fold(bit, held, landed, low, after):
     blocks, rows, columns = held.shape
     steps = blocks // 2
     coded = coded_rows(rows)
+
+    def block(i, b, out):
+        side = 1 - b[0] if out else b[0]
+        return i // low * (2 * low) + side * low + i % low
+
     return pl.pallas_call(
-        functools.partial(fold_kernel, steps),
+        functools.partial(fold_kernel, steps, low),
         grid_spec=pltpu.PrefetchScalarGridSpec(
             num_scalar_prefetch=1,
             grid=(steps,),
             in_specs=[
-                pl.BlockSpec((2, rows, columns), lambda i, b: (i, 0, 0)),
-                pl.BlockSpec((2 * coded, columns), lambda i, b: (i, 0)),
+                pl.BlockSpec((1, rows, columns), lambda i, b: (block(i, b, False), 0, 0)),
+                pl.BlockSpec((1, rows, columns), lambda i, b: (block(i, b, True), 0, 0)),
+                pl.BlockSpec((coded, columns), lambda i, b: (block(i, b, False), 0)),
+                pl.BlockSpec((coded, columns), lambda i, b: (block(i, b, True), 0)),
                 pl.BlockSpec((TILE, columns), lambda i, b: (blocks * coded // TILE, 0)),
             ]
             + [pl.BlockSpec(memory_space=pl.ANY)] * len(after),
@@ -402,35 +447,29 @@
         compiler_params=pltpu.CompilerParams(vmem_limit_bytes=VMEM_LIMIT),
         cost_estimate=SHORT,
         name="fold",
-    )(bit, held, landed, landed, *after)
+    )(bit, held, held, landed, landed, landed, *after)
 
 
 def finish_kernel(after_count, core, held, landed, cosine, sine, *refs):
     queries, *pair = refs[after_count:]
-    rows = held.shape[1]
-    coded = coded_rows(rows)
+    coded = coded_rows(held.shape[1])
     power = landed[pl.ds(coded, TILE), :].astype(jnp.int32).astype(jnp.float32)[0:1]
     total = held[0] + decode(landed[pl.ds(0, coded), :], power)
     joined = total.astype(jnp.bfloat16)
-    parts = []
     for head in range(joined.shape[1] // HD):
-        raw = joined[:, head * HD : (head + 1) * HD]
-        wide = raw.astype(jnp.float32)
-        turned = wide * cosine[...] + pltpu.roll(wide, HD // 2, 1) * sine[...]
-        parts.append((raw, turned.astype(jnp.bfloat16)))
-    queries[...] = jnp.concatenate([parts[0][1], parts[1][1]], 1)
-    if pair:
-        raw, turned = parts[2]
-        pair[0][...] = jnp.where(core[0] == 0, turned.astype(jnp.float32), raw.astype(jnp.float32)).astype(
-            jnp.bfloat16
-        )
+        raw = joined[:, head * HD : (head + 1) * HD].astype(jnp.float32)
+        turned = raw * cosine[...] + pltpu.roll(raw, HD // 2, 1) * sine[...]
+        if head < PART_HEADS:
+            queries[:, head * HD : (head + 1) * HD] = turned.astype(jnp.bfloat16)
+        else:
+            pair[0][...] = jnp.where(core[0] == 0, turned, raw).astype(jnp.bfloat16)
 
 
 def finish(core, held, landed, cosine, sine, after):
     _, rows, columns = held.shape
     whole = pl.BlockSpec(memory_space=pltpu.VMEM)
-    shapes = [jax.ShapeDtypeStruct((rows, 2 * HD), jnp.bfloat16)]
-    if columns > 2 * HD:
+    shapes = [jax.ShapeDtypeStruct((rows, PART_HEADS * HD), jnp.bfloat16)]
+    if columns > PART_HEADS * HD:
         shapes.append(jax.ShapeDtypeStruct((rows, HD), jnp.bfloat16))
     return pl.pallas_call(
         functools.partial(finish_kernel, len(after)),
@@ -745,80 +784,39 @@
     cosine = jnp.concatenate([jnp.cos(angles)] * 2, 1)
     sine = jnp.concatenate([-jnp.sin(angles), jnp.sin(angles)], 1)
 
-    count = GQ // 4
-    held, sent = [None] * count, [None] * count
-
-    def projected(chunk, *after):
-        held[chunk], sent[chunk] = project(
-            bits[0], normed, qkv_weight, chunk, chunk == 0, after
-        )
-
-    def hop(chunk, b):
-        return swap(sent[chunk], MESH_BITS[b])
-
-    def folded(chunk, b, landed, *after):
-        held[chunk], sent[chunk] = fold(bits[b], held[chunk], landed, after)
-
-    def finished(chunk, landed, *after):
-        return finish(bits[0], held[chunk], landed, cosine, sine, after)
-
-    projected(0, cache_pieces[0])
-    core_0 = hop(0, 0)
-    for k in (1, 2, 3, 4):
+    def folded(part, b, landed, low, *after):
+        return fold(bits[b], part, landed, low, after)
+
+    def finished(part, landed, *after):
+        return finish(bits[0], part, landed, cosine, sine, after)
+
+    for k in range(3, KVH):
         handed(k)
-    projected(1, held[0])
-    (sent[1],) = together([sent[1]], [core_0] + cache_pieces[1:5])
-
-    folded(0, 1, core_0, sent[1])
-    core_1, y_0 = hop(1, 0), hop(0, 1)
-    handed(5)
-    handed(6)
-    projected(2, held[0])
-    projected(3, held[2])
-    sent[2], sent[3] = together(
-        [sent[2], sent[3]], [core_1, y_0, cache_pieces[5], cache_pieces[6]]
-    )
-
-    core_2, core_3 = hop(2, 0), hop(3, 0)
-    handed(7)
-    folded(1, 1, core_1, sent[2])
-    y_1 = hop(1, 1)
-    folded(0, 2, y_0, held[1])
-    near_0 = hop(0, 2)
-    folded(2, 1, core_2, held[0])
-    folded(3, 1, core_3, held[2])
-    sent[2], sent[3] = together([sent[2], sent[3]], [y_1, near_0, cache_pieces[7]])
-
-    y_2 = hop(2, 1)
-    folded(0, 3, near_0, sent[2])
-    far_0 = hop(0, 3)
-    folded(1, 2, y_1, sent[2])
-    near_1 = hop(1, 2)
-    (cache_own,) = pack(cache_pieces, [tuple(range(KVH))], [held[1]])
+    held_a, held_b, sent_a, sent_b = project(bits[0], normed, qkv_weight, cache_pieces[:1])
+    sent_a, sent_b, cache_pieces[1], cache_pieces[2] = together(
+        [sent_a, sent_b] + cache_pieces[1:3], cache_pieces[3:]
+    )
+    core_a, core_b = swap(sent_a, 1), swap(sent_b, 1)
+    for k in (1, 2):
+        handed(k)
+    held_a, sent_a = folded(held_a, 1, core_a, 1)
+    line_a = swap(sent_a, 2)
+    held_b, sent_b = folded(held_b, 2, core_b, 2, held_a)
+    line_b = swap(sent_b, 4)
+    (cache_own,) = pack(cache_pieces, [tuple(range(KVH))], [held_b])
     cache_other = swap(cache_own, 1)
-    (sent[3],) = together([sent[3]], [y_2, far_0, near_1])
-
-    y_3 = hop(3, 1)
-    folded(1, 3, near_1, sent[3])
-    far_1 = hop(1, 3)
-    folded(2, 2, y_2, sent[3])
-    near_2 = hop(2, 2)
-    query_chunks = [None] * count
-    query_chunks[0], pair = finished(0, far_0, held[2])
+    held_b, sent_b = folded(held_b, 1, line_b, 1, cache_own)
+    line_b = swap(sent_b, 2)
+    held_a, sent_a = folded(held_a, 2, line_a, 1, held_b)
+    line_a = swap(sent_a, 4)
+    held_b, sent_b = folded(held_b, 3, line_b, 1, held_a)
+    line_b = swap(sent_b, 8)
+    held_a, sent_a = folded(held_a, 3, line_a, 1, held_b)
+    line_a = swap(sent_a, 8)
+    (query_b,) = finished(held_b, line_b, held_a)
+    query_a, pair = finished(held_a, line_a, query_b)
     pair_other = swap(pair, 1)
-    (held[3],) = together([held[3]], [y_3, far_1, near_2, pair_other, cache_other])
-
-    folded(3, 2, y_3)
-    near_3 = hop(3, 2)
-    folded(2, 3, near_2, held[3])
-    far_2 = hop(2, 3)
-    (query_chunks[1],) = finished(1, far_1, held[2])
-    (held[3],) = together([held[3]], [near_3, far_2])
-
-    folded(3, 3, near_3)
-    far_3 = hop(3, 3)
-    (query_chunks[2],) = finished(2, far_2, held[3])
-    (query_chunks[3],) = finished(3, far_3, query_chunks[2])
+    query_chunks = [query_a, query_b]
     cache_parts = (cache_own, cache_other)
     keys = jnp.where(core == 0, pair, pair_other)
     raw_values = jnp.where(core == 0, pair_other, pair)

time: 230 us -> 222 us (0.965)
  local copies, waits for them, and re-layouts: 31.5 us -> 13.8 us
  waiting for transfers between devices: 70.8 us -> 84.2 us
  Pallas kernels: 78.2 us -> 70.7 us
  starting transfers between devices: 41.2 us -> 46.5 us
    unnamed x152 -> x56, local copies, waits for them, and re-layouts: 26.8 us -> 11 us
    ppermute x39 -> x31, waiting for transfers between devices: 70.8 us -> 84.2 us  [swap(): return lax.ppermute(value, 'tensor', [(i, i ^ bit) for i in range(devices)])]
    pallas_call x16 -> x7, Pallas kernels: 44.3 us -> 35.7 us  [the longest x1 18.2 us: project(): pl.pallas_call(project_kernel, grid_spec=pltpu.PrefetchScalarGridSpec(num...]
    ppermute x39 -> x31, starting transfers between devices: 41.2 us -> 46.5 us  [swap(): return lax.ppermute(value, 'tensor', [(i, i ^ bit) for i in range(devices)])]
  transfers between devices with their start and end apart: 39 -> 31, of which waited for: 19 -> 17; matrix products, arithmetic and copies ran while one was open for 4% -> 3% of each run, Pallas kernels for 23% -> 26%
where the time goes in v8:
time: 222 us; the launch traced here: 221 us
  waiting for transfers between devices  84.2 us (38%)
  Pallas kernels  70.7 us (32%)
  starting transfers between devices  46.5 us (21%)
  local copies, waits for them, and re-layouts  13.8 us (6%)
  other arithmetic  5.27 us (2%)
    ppermute x31, waiting for transfers between devices, swap(): return lax.ppermute(value, 'tensor', [(i, i ^ bit) for i in range(devices)])  84.2 us
    ppermute x31, starting transfers between devices, swap(): return lax.ppermute(value, 'tensor', [(i, i ^ bit) for i in range(devices)])  46.5 us
    pallas_call x4, Pallas kernels, mix(): pl.pallas_call(functools.partial(mix_kernel, len(pieces)), in_specs=[pl.B...  21.5 us
    pallas_call x1, Pallas kernels, project(): pl.pallas_call(project_kernel, grid_spec=pltpu.PrefetchScalarGridSpec(num...  18.2 us
    pallas_call x6, Pallas kernels, fold(): pl.pallas_call(functools.partial(fold_kernel, steps, low), grid_spec=pltp...  17.5 us
    unnamed x56, local copies, waits for them, and re-layouts  11 us
    pallas_call x1, Pallas kernels, attend(): pl.pallas_call(attend_kernel, in_specs=[pl.BlockSpec(memory_space=pltpu.S...  8.36 us
  transfers between devices with their start and end apart: 31, of which 17 were waited for; matrix products, arithmetic and copies ran while one was open for 3% of the time, Pallas kernels for 26%

profile of v8, /device:TPU:0, one launch (start us, length us, event | category | flops | bytes accessed | tf_op | source)
XLA Modules:
  0.0 221.2 jit_solution(13944483820147349535)
XLA Ops:
  0.0 1.2 fusion
  1.2 3.0 %collective-permute-start = (f32[2,96]{1,0:T(2,128)S(1)}, f32[2,96]{1,0:T(2,128)S(1)}, u32[]{:S(2)}, u32[]{:S(2)}) collective-permute-start(f32[2,96]{1,0:T(2,128)S(1)} %fusion), channel_id=1, source_target_pairs={{0,2},{1,3},{2,0},{3,1},{4,6},{5,7},{6,4},{7,5},{8,10},{9,11},{10,... | collective-permute-start | bytes 2312 | tf_op jit(solution)/shard_map/ppermute | solution.py:222
  4.3 1.5 collective-permute-done
  5.8 1.1 collective-permute-done.1
  7.0 2.1 collective-permute-start.2
  9.0 0.8 reshape.240
  9.8 0.7 convert_element_type.29
  10.6 3.0 %collective-permute-start.3 = (f32[2,96]{1,0:T(2,128)S(1)}, f32[2,96]{1,0:T(2,128)S(1)}, u32[]{:S(2)}, u32[]{:S(2)}) collective-permute-start(f32[2,96]{1,0:T(2,128)S(1)} %add.139), channel_id=1, source_target_pairs={{0,8},{1,9},{2,10},{3,11},{4,12},{5,13},{6,14},{7,15},{8,0},{9,1},... | collective-permute-start | bytes 2312 | tf_op jit(solution)/shard_map/ppermute | solution.py:222
  13.6 1.4 copy-done.10
  15.0 0.9 arrange.1
  15.9 2.5 %collective-permute-start.4 = (bf16[400,256]{1,0:T(8,128)(2,1)S(1)}, bf16[400,256]{1,0:T(8,128)(2,1)S(1)}, u32[]{:S(2)}, u32[]{:S(2)}) collective-permute-start(bf16[400,256]{1,0:T(8,128)(2,1)S(1)} %get-tuple-element.43), channel_id=1, source_target_pairs={{0,6},{1,7},{2,4},{3,5},{4,2},{5,3},{6,0},{7,1},{8,14},{9,15},{10,... | collective-permute-start | bytes 614408 | tf_op jit(solution)/shard_map/ppermute | solution.py:222
  18.8 2.5 %collective-permute-start.6 = (bf16[400,256]{1,0:T(8,128)(2,1)S(1)}, bf16[400,256]{1,0:T(8,128)(2,1)S(1)}, u32[]{:S(2)}, u32[]{:S(2)}) collective-permute-start(bf16[400,256]{1,0:T(8,128)(2,1)S(1)} %get-tuple-element.45), channel_id=1, source_target_pairs={{0,10},{1,11},{2,8},{3,9},{4,14},{5,15},{6,12},{7,13},{8,2},{9,3},... | collective-permute-start | bytes 614408 | tf_op jit(solution)/shard_map/ppermute | solution.py:222
  21.3 4.8 %collective-permute-start.8 = (bf16[400,256]{1,0:T(8,128)(2,1)S(1)}, bf16[400,256]{1,0:T(8,128)(2,1)S(1)}, u32[]{:S(2)}, u32[]{:S(2)}) collective-permute-start(bf16[400,256]{1,0:T(8,128)(2,1)S(1)} %get-tuple-element.47), channel_id=1, source_target_pairs={{0,14},{1,15},{2,12},{3,13},{4,10},{5,11},{6,8},{7,9},{8,6},{9,7},... | collective-permute-start | bytes 614408 | tf_op jit(solution)/shard_map/ppermute | solution.py:222
  26.3 18.2 %project.1 = (f32[8,192,640]{2,1,0:T(8,128)}, f32[8,192,512]{2,1,0:T(8,128)}, s16[1936,640]{1,0:T(8,128)(2,1)}, s16[1936,512]{1,0:T(8,128)(2,1)}) custom-call(s32[1]{0:T(128)} %bitcast.2.core, bf16[192,1024]{1,0:T(8,128)(2,1)S(1)} %bitcast.53, bf16[1024,18432]{1,0:T(8,128)(2,1)} %weights.1, bf16[400,256]{1,0:T(8,128)(2,1)S(1)} %get-tuple-element.37.refs_0_), custom_call_target="tpu_custom_call" | custom-call | flops 1 | bytes 1 | tf_op jit(solution)/shard_map/project/pallas_call | solution.py:374
  44.5 3.8 %collective-permute-done.6.refs_6_.refs_5_ = bf16[400,256]{1,0:T(8,128)(2,1)S(1)} collective-permute-done((bf16[400,256]{1,0:T(8,128)(2,1)S(1)}, bf16[400,256]{1,0:T(8,128)(2,1)S(1)}, u32[]{:S(2)}, u32[]{:S(2)}) %collective-permute-start.6) | collective-permute-done | bytes 204832 | tf_op jit(solution)/shard_map/ppermute | solution.py:222
  48.4 0.6 copy-done.16
  50.0 1.4 collective-permute-start.13
  51.3 7.7 %collective-permute-start.14 = (bf16[400,256]{1,0:T(8,128)(2,1)}, bf16[400,256]{1,0:T(8,128)(2,1)}, u32[]{:S(2)}, u32[]{:S(2)}) collective-permute-start(bf16[400,256]{1,0:T(8,128)(2,1)} %get-tuple-element.56), channel_id=1, source_target_pairs={{0,4},{1,5},{2,6},{3,7},{4,0},{5,1},{6,2},{7,3},{8,12},{9,13},{10,... | collective-permute-start | bytes 614408 | tf_op jit(solution)/shard_map/ppermute | solution.py:222
  59.0 5.1 %fold.6 = (f32[4,192,640]{2,1,0:T(8,128)S(1)}, s16[976,640]{1,0:T(8,128)(2,1)}) custom-call(s32[1]{0:T(128)} %bitcast.5.bit, f32[8,192,640]{2,1,0:T(8,128)} %get-tuple-element.38.held.held_out, f32[8,192,640]{2,1,0:T(8,128)} %get-tuple-element.38.held.held_out, s16[1936,640]{1,0:T(8,128)(2,1)S(1)} %collective-permute-done.9.landed.landed_out.landed_powers, ...), custom_call_target="tpu_custom_call" | custom-call | flops 1 | bytes 1 | tf_op jit(solution)/shard_map/fold/pallas_call | solution.py:424
  64.2 1.4 copy-done
  66.1 1.5 copy-done.1
  67.6 4.2 %fold.7 = (f32[4,192,512]{2,1,0:T(8,128)S(1)}, s16[976,512]{1,0:T(8,128)(2,1)S(1)}) custom-call(s32[1]{0:T(128)} %bitcast.4.bit, f32[8,192,512]{2,1,0:T(8,128)} %get-tuple-element.51.held.held_out, f32[8,192,512]{2,1,0:T(8,128)} %get-tuple-element.51.held.held_out, s16[1936,512]{1,0:T(8,128)(2,1)} %collective-permute-done.11.landed.landed_out.landed_powers, ...), custom_call_target="tpu_custom_call" | custom-call | flops 1 | bytes 1 | tf_op jit(solution)/shard_map/fold/pallas_call | solution.py:424
  72.0 1.4 pack.3.refs_0_.own
  73.7 6.5 %collective-permute-start.12 = (s16[976,512]{1,0:T(8,128)(2,1)}, s16[976,512]{1,0:T(8,128)(2,1)S(1)}, u32[]{:S(2)}, u32[]{:S(2)}) collective-permute-start(s16[976,512]{1,0:T(8,128)(2,1)} %copy-done.24), channel_id=1, source_target_pairs={{0,4},{1,5},{2,6},{3,7},{4,0},{5,1},{6,2},{7,3},{8,12},{9,13},{10,... | collective-permute-start | bytes 2998280 | tf_op jit(solution)/shard_map/ppermute | solution.py:222
  80.5 1.1 fusion.5
  81.7 21.5 %collective-permute-done.12.landed.landed_out.landed_powers = s16[976,512]{1,0:T(8,128)(2,1)S(1)} collective-permute-done((s16[976,512]{1,0:T(8,128)(2,1)}, s16[976,512]{1,0:T(8,128)(2,1)S(1)}, u32[]{:S(2)}, u32[]{:S(2)}) %collective-permute-start.12) | collective-permute-done | bytes 999456 | tf_op jit(solution)/shard_map/ppermute | solution.py:222
  103.2 1.7 fold.8
  105.4 3.1 %fold.9 = (f32[2,192,640]{2,1,0:T(8,128)S(1)}, s16[496,640]{1,0:T(8,128)(2,1)}) custom-call(s32[1]{0:T(128)} %bitcast.4.bit, f32[4,192,640]{2,1,0:T(8,128)S(1)} %copy-done.2, f32[4,192,640]{2,1,0:T(8,128)S(1)} %copy-done.2, s16[976,640]{1,0:T(8,128)(2,1)} %collective-permute-done.10.landed.landed_out.landed_powers, ...), custom_call_target="tpu_custom_call" | custom-call | flops 1 | bytes 1 | tf_op jit(solution)/shard_map/fold/pallas_call | solution.py:424
  108.4 1.7 collective-permute-start.15
  110.2 1.2 pad_maximum_fusion
  111.5 7.0 %collective-permute-done.16.landed.landed_out.landed_powers = s16[496,512]{1,0:T(8,128)(2,1)} collective-permute-done((s16[496,512]{1,0:T(8,128)(2,1)}, s16[496,512]{1,0:T(8,128)(2,1)}, u32[]{:S(2)}, u32[]{:S(2)}) %collective-permute-start.16) | collective-permute-done | bytes 507936 | tf_op jit(solution)/shard_map/ppermute | solution.py:222
  118.6 1.1 copy-done.4
  119.7 2.2 fold.10
  121.9 0.7 copy-done.11
  122.6 0.7 collective-permute-start.18
  123.3 0.7 slice_reduce_fusion
  124.1 0.6 collective-permute-done.15.landed.landed_out.landed_powers
  124.7 1.0 copy-done.12
  125.7 1.2 fold.11
  126.9 0.8 copy-done.7
  127.7 1.6 collective-permute-start.17
  130.1 14.6 %collective-permute-done.18.landed = s16[256,512]{1,0:T(8,128)(2,1)} collective-permute-done((s16[256,512]{1,0:T(8,128)(2,1)}, s16[256,512]{1,0:T(8,128)(2,1)}, u32[]{:S(2)}, u32[]{:S(2)}) %collective-permute-start.18) | collective-permute-done | bytes 262176 | tf_op jit(solution)/shard_map/ppermute | solution.py:222
  144.6 1.0 copy-done.8
  145.7 1.0 copy-done.13
  146.7 1.2 finish.2.refs_0_
  147.8 2.8 %collective-permute-done.17.landed = s16[256,640]{1,0:T(8,128)(2,1)S(1)} collective-permute-done((s16[256,640]{1,0:T(8,128)(2,1)}, s16[256,640]{1,0:T(8,128)(2,1)S(1)}, u32[]{:S(2)}, u32[]{:S(2)}) %collective-permute-start.17) | collective-permute-done | bytes 327712 | tf_op jit(solution)/shard_map/ppermute | solution.py:222
  151.2 1.1 collective-permute-done.19
  152.4 8.4 %attend.1 = bf16[16,96,128]{2,1,0:T(8,128)(2,1)S(1)} custom-call(s32[24]{0:T(128)S(1)} %get-tuple-element.71.slot_request, bf16[16,96,128]{2,1,0:T(8,128)(2,1)S(1)} %bitcast.54, bf16[16,16,128]{2,1,0:T(8,128)(2,1)S(1)} %pad.12.new_keys, bf16[16,16,128]{2,1,0:T(8,128)(2,1)S(1)} %pad.13.new_values, bf16[8,400,256]{2,1,0:T(8,128)(2,1)S(1)} %pack.3.refs_0_.own, ...), custom_call_target="tpu_custom_call" | custom-call | flops 1 | bytes 1 | tf_op jit(solution)/shard_map/attend/pallas_call | solution.py:679
  161.6 1.5 collective-permute-start.23
  163.1 15.6 %collective-permute-done.21.refs_0_ = bf16[192,1024]{1,0:T(8,128)(2,1)S(1)} collective-permute-done((bf16[192,1024]{1,0:T(8,128)(2,1)S(1)}, bf16[192,1024]{1,0:T(8,128)(2,1)S(1)}, u32[]{:S(2)}, u32[]{:S(2)}) %collective-permute-start.21) | collective-permute-done | bytes 393248 | tf_op jit(solution)/shard_map/ppermute | solution.py:222
  178.7 3.1 %collective-permute-done.23.refs_2_ = bf16[192,1024]{1,0:T(8,128)(2,1)S(1)} collective-permute-done((bf16[192,1024]{1,0:T(8,128)(2,1)S(1)}, bf16[192,1024]{1,0:T(8,128)(2,1)S(1)}, u32[]{:S(2)}, u32[]{:S(2)}) %collective-permute-start.23) | collective-permute-done | bytes 393248 | tf_op jit(solution)/shard_map/ppermute | solution.py:222
  182.0 1.6 collective-permute-start.27
  183.6 1.4 collective-permute-start.25
  185.2 3.4 %mix.4.refs_3_ = f32[192,1024]{1,0:T(8,128)S(1)} custom-call(s32[2]{0:T(128)S(1)} %pad_add_fusion.1.places, bf16[192,1024]{1,0:T(8,128)(2,1)S(1)} %together.4.refs_0_, bf16[192,1024]{1,0:T(8,128)(2,1)S(1)} %collective-permute-done.24.refs_3_.refs_1_, bf16[16384,1024]{1,0:T(8,128)(2,1)} %refs_2_.7, bf16[192,1024]{1,0:T(8,128)(2,1)S(1)} %bitcast.47), custom_call_target="tpu_custom_call" | custom-call | flops 1 | bytes 1 | tf_op jit(solution)/shard_map/mix/pallas_call | solution.py:527
  188.6 7.0 %mix.5.refs_2_.refs_3_ = f32[192,1024]{1,0:T(8,128)S(1)} custom-call(s32[6]{0:T(128)S(1)} %stack.82.places, bf16[3,192,1024]{2,1,0:T(8,128)(2,1)S(1)} %get-tuple-element.68.refs_0_, bf16[3,192,1024]{2,1,0:T(8,128)(2,1)} %collective-permute-done.28.refs_1_, bf16[16384,1024]{1,0:T(8,128)(2,1)} %refs_2_.7, f32[192,1024]{1,0:T(8,128)S(1)} %mix.4.refs_3_), custom_call_target="tpu_custom_call" | custom-call | flops 1 | bytes 1 | tf_op jit(solution)/shard_map/mix/pallas_call | solution.py:527
  195.6 1.3 collective-permute-done.25.refs_1_
  196.8 5.3 %collective-permute-done.27.refs_0_ = bf16[2,192,1024]{2,1,0:T(8,128)(2,1)} collective-permute-done((bf16[2,192,1024]{2,1,0:T(8,128)(2,1)S(1)}, bf16[2,192,1024]{2,1,0:T(8,128)(2,1)}, u32[]{:S(2)}, u32[]{:S(2)}) %collective-permute-start.27) | collective-permute-done | bytes 786464 | tf_op jit(solution)/shard_map/ppermute | solution.py:222
  202.1 1.3 pack.5.refs_0_
  203.5 1.6 collective-permute-start.26
  205.2 1.3 collective-permute-done.29.refs_1_
  206.5 7.0 %mix.6.refs_1_.refs_3_ = f32[192,1024]{1,0:T(8,128)S(1)} custom-call(s32[6]{0:T(128)S(1)} %stack.75.places, bf16[3,192,1024]{2,1,0:T(8,128)(2,1)S(1)} %pack.5.refs_0_, bf16[3,192,1024]{2,1,0:T(8,128)(2,1)} %collective-permute-done.29.refs_1_, bf16[16384,1024]{1,0:T(8,128)(2,1)} %refs_2_.7, f32[192,1024]{1,0:T(8,128)S(1)} %mix.5.refs_2_.refs_3_), custom_call_target="tpu_custom_call" | custom-call | flops 1 | bytes 1 | tf_op jit(solution)/shard_map/mix/pallas_call | solution.py:527
  213.5 1.8 collective-permute-done.26.refs_0_
  215.3 1.6 collective-permute-done.30.refs_1_
  217.0 4.1 %mix.7 = bf16[192,1024]{1,0:T(8,128)(2,1)} custom-call(s32[2]{0:T(128)S(1)} %pad_add_fusion.places, bf16[192,1024]{1,0:T(8,128)(2,1)S(1)} %together.5.refs_0_, bf16[192,1024]{1,0:T(8,128)(2,1)S(1)} %collective-permute-done.30.refs_1_, bf16[16384,1024]{1,0:T(8,128)(2,1)} %refs_2_.7, f32[192,1024]{1,0:T(8,128)S(1)} %mix.6.refs_1_.refs_3_), custom_call_target="tpu_custom_call" | custom-call | flops 1 | bytes 1 | tf_op jit(solution)/shard_map/mix/pallas_call | solution.py:527
  (130 shorter events, 6.1 us)
Async XLA Ops:
  0.0 26.1 %copy-start.5 = (bf16[2,96,1024]{2,1,0:T(8,128)(2,1)S(1)}, bf16[2,96,1024]{2,1,0:T(8,128)(2,1)}, u32[]{:S(2)}) copy-start(bf16[2,96,1024]{2,1,0:T(8,128)(2,1)} %param.8) | copy-start | bytes 1179652
  1.2 4.6 %collective-permute-start = (f32[2,96]{1,0:T(2,128)S(1)}, f32[2,96]{1,0:T(2,128)S(1)}, u32[]{:S(2)}, u32[]{:S(2)}) collective-permute-start(f32[2,96]{1,0:T(2,128)S(1)} %fusion), channel_id=1, source_target_pairs={{0,2},{1,3},{2,0},{3,1},{4,6},{5,7},{6,4},{7,5},{8,10},{9,11},{10,... | collective-permute-start | bytes 2312 | tf_op jit(solution)/shard_map/ppermute | solution.py:222
  5.8 1.1 collective-permute-start.1
  7.0 3.6 %collective-permute-start.2 = (f32[2,96]{1,0:T(2,128)S(1)}, f32[2,96]{1,0:T(2,128)S(1)}, u32[]{:S(2)}, u32[]{:S(2)}) collective-permute-start(f32[2,96]{1,0:T(2,128)S(1)} %add.138), channel_id=1, source_target_pairs={{0,4},{1,5},{2,6},{3,7},{4,0},{5,1},{6,2},{7,3},{8,12},{9,13},{10,... | collective-permute-start | bytes 2312 | tf_op jit(solution)/shard_map/ppermute | solution.py:222
  10.6 10.7 %collective-permute-start.3 = (f32[2,96]{1,0:T(2,128)S(1)}, f32[2,96]{1,0:T(2,128)S(1)}, u32[]{:S(2)}, u32[]{:S(2)}) collective-permute-start(f32[2,96]{1,0:T(2,128)S(1)} %add.139), channel_id=1, source_target_pairs={{0,8},{1,9},{2,10},{3,11},{4,12},{5,13},{6,14},{7,15},{8,0},{9,1},... | collective-permute-start | bytes 2312 | tf_op jit(solution)/shard_map/ppermute | solution.py:222
  13.6 1.4 copy-start.10
  15.9 28.6 %copy-start.22 = (bf16[400,256]{1,0:T(8,128)(2,1)}, bf16[400,256]{1,0:T(8,128)(2,1)S(1)}, u32[]{:S(2)}) copy-start(bf16[400,256]{1,0:T(8,128)(2,1)S(1)} %get-tuple-element.37.refs_0_) | copy-start | bytes 614404
  15.9 28.6 %collective-permute-start.4 = (bf16[400,256]{1,0:T(8,128)(2,1)S(1)}, bf16[400,256]{1,0:T(8,128)(2,1)S(1)}, u32[]{:S(2)}, u32[]{:S(2)}) collective-permute-start(bf16[400,256]{1,0:T(8,128)(2,1)S(1)} %get-tuple-element.43), channel_id=1, source_target_pairs={{0,6},{1,7},{2,4},{3,5},{4,2},{5,3},{6,0},{7,1},{8,14},{9,15},{10,... | collective-permute-start | bytes 614408 | tf_op jit(solution)/shard_map/ppermute | solution.py:222
  18.5 26.1 %collective-permute-start.5 = (bf16[400,256]{1,0:T(8,128)(2,1)S(1)}, bf16[400,256]{1,0:T(8,128)(2,1)S(1)}, u32[]{:S(2)}, u32[]{:S(2)}) collective-permute-start(bf16[400,256]{1,0:T(8,128)(2,1)S(1)} %get-tuple-element.44), channel_id=1, source_target_pairs={{0,8},{1,9},{2,10},{3,11},{4,12},{5,13},{6,14},{7,15},{8,0},{9,1},... | collective-permute-start | bytes 614408 | tf_op jit(solution)/shard_map/ppermute | solution.py:222
  18.8 29.6 %collective-permute-start.6 = (bf16[400,256]{1,0:T(8,128)(2,1)S(1)}, bf16[400,256]{1,0:T(8,128)(2,1)S(1)}, u32[]{:S(2)}, u32[]{:S(2)}) collective-permute-start(bf16[400,256]{1,0:T(8,128)(2,1)S(1)} %get-tuple-element.45), channel_id=1, source_target_pairs={{0,10},{1,11},{2,8},{3,9},{4,14},{5,15},{6,12},{7,13},{8,2},{9,3},... | collective-permute-start | bytes 614408 | tf_op jit(solution)/shard_map/ppermute | solution.py:222
  21.3 27.0 %collective-permute-start.7 = (bf16[400,256]{1,0:T(8,128)(2,1)S(1)}, bf16[400,256]{1,0:T(8,128)(2,1)S(1)}, u32[]{:S(2)}, u32[]{:S(2)}) collective-permute-start(bf16[400,256]{1,0:T(8,128)(2,1)S(1)} %get-tuple-element.46), channel_id=1, source_target_pairs={{0,12},{1,13},{2,14},{3,15},{4,8},{5,9},{6,10},{7,11},{8,4},{9,5},... | collective-permute-start | bytes 614408 | tf_op jit(solution)/shard_map/ppermute | solution.py:222
  21.3 27.0 %collective-permute-start.8 = (bf16[400,256]{1,0:T(8,128)(2,1)S(1)}, bf16[400,256]{1,0:T(8,128)(2,1)S(1)}, u32[]{:S(2)}, u32[]{:S(2)}) collective-permute-start(bf16[400,256]{1,0:T(8,128)(2,1)S(1)} %get-tuple-element.47), channel_id=1, source_target_pairs={{0,14},{1,15},{2,12},{3,13},{4,10},{5,11},{6,8},{7,9},{8,6},{9,7},... | collective-permute-start | bytes 614408 | tf_op jit(solution)/shard_map/ppermute | solution.py:222
  44.5 3.9 %copy-start.14 = (bf16[400,256]{1,0:T(8,128)(2,1)}, bf16[400,256]{1,0:T(8,128)(2,1)S(1)}, u32[]{:S(2)}) copy-start(bf16[400,256]{1,0:T(8,128)(2,1)S(1)} %collective-permute-done.5.refs_5_.refs_4_) | copy-start | bytes 614404
  48.4 0.7 copy-start.16
  48.4 0.8 copy-start.18
  48.4 0.8 copy-start.20
  48.4 1.4 copy-start.26
  49.2 9.8 %collective-permute-start.9 = (s16[1936,640]{1,0:T(8,128)(2,1)}, s16[1936,640]{1,0:T(8,128)(2,1)S(1)}, u32[]{:S(2)}, u32[]{:S(2)}) collective-permute-start(s16[1936,640]{1,0:T(8,128)(2,1)} %get-tuple-element.48), channel_id=1, source_target_pairs={{0,1},{1,0},{2,3},{3,2},{4,5},{5,4},{6,7},{7,6},{8,9},{9,8},{10,11... | collective-permute-start | bytes 7434248 | tf_op jit(solution)/shard_map/ppermute | solution.py:222
  49.2 16.9 %collective-permute-start.11 = (s16[1936,512]{1,0:T(8,128)(2,1)}, s16[1936,512]{1,0:T(8,128)(2,1)}, u32[]{:S(2)}, u32[]{:S(2)}) collective-permute-start(s16[1936,512]{1,0:T(8,128)(2,1)} %get-tuple-element.52), channel_id=1, source_target_pairs={{0,1},{1,0},{2,3},{3,2},{4,5},{5,4},{6,7},{7,6},{8,9},{9,8},{10,11... | collective-permute-start | bytes 5947400 | tf_op jit(solution)/shard_map/ppermute | solution.py:222
  50.0 21.9 %collective-permute-start.13 = (bf16[400,256]{1,0:T(8,128)(2,1)}, bf16[400,256]{1,0:T(8,128)(2,1)}, u32[]{:S(2)}, u32[]{:S(2)}) collective-permute-start(bf16[400,256]{1,0:T(8,128)(2,1)} %get-tuple-element.55), channel_id=1, source_target_pairs={{0,2},{1,3},{2,0},{3,1},{4,6},{5,7},{6,4},{7,5},{8,10},{9,11},{10,... | collective-permute-start | bytes 614408 | tf_op jit(solution)/shard_map/ppermute | solution.py:222
  51.3 20.6 %collective-permute-start.14 = (bf16[400,256]{1,0:T(8,128)(2,1)}, bf16[400,256]{1,0:T(8,128)(2,1)}, u32[]{:S(2)}, u32[]{:S(2)}) collective-permute-start(bf16[400,256]{1,0:T(8,128)(2,1)} %get-tuple-element.56), channel_id=1, source_target_pairs={{0,4},{1,5},{2,6},{3,7},{4,0},{5,1},{6,2},{7,3},{8,12},{9,13},{10,... | collective-permute-start | bytes 614408 | tf_op jit(solution)/shard_map/ppermute | solution.py:222
  64.2 1.4 copy-start
  65.5 39.8 %collective-permute-start.10 = (s16[976,640]{1,0:T(8,128)(2,1)}, s16[976,640]{1,0:T(8,128)(2,1)}, u32[]{:S(2)}, u32[]{:S(2)}) collective-permute-start(s16[976,640]{1,0:T(8,128)(2,1)} %get-tuple-element.50), channel_id=1, source_target_pairs={{0,2},{1,3},{2,0},{3,1},{4,6},{5,7},{6,4},{7,5},{8,10},{9,11},{10,... | collective-permute-start | bytes 3747848 | tf_op jit(solution)/shard_map/ppermute | solution.py:222
  66.1 1.5 copy-start.1
  67.6 4.3 %copy-start.15 = (bf16[400,256]{1,0:T(8,128)(2,1)S(1)}, bf16[400,256]{1,0:T(8,128)(2,1)}, u32[]{:S(2)}) copy-start(bf16[400,256]{1,0:T(8,128)(2,1)} %copy-done.14) | copy-start | bytes 614404
  67.6 4.3 %copy-start.17 = (bf16[400,256]{1,0:T(8,128)(2,1)S(1)}, bf16[400,256]{1,0:T(8,128)(2,1)}, u32[]{:S(2)}) copy-start(bf16[400,256]{1,0:T(8,128)(2,1)} %copy-done.16) | copy-start | bytes 614404
  67.6 4.3 %copy-start.19 = (bf16[400,256]{1,0:T(8,128)(2,1)S(1)}, bf16[400,256]{1,0:T(8,128)(2,1)}, u32[]{:S(2)}) copy-start(bf16[400,256]{1,0:T(8,128)(2,1)} %copy-done.18) | copy-start | bytes 614404
  67.6 4.3 %copy-start.21 = (bf16[400,256]{1,0:T(8,128)(2,1)S(1)}, bf16[400,256]{1,0:T(8,128)(2,1)}, u32[]{:S(2)}) copy-start(bf16[400,256]{1,0:T(8,128)(2,1)} %copy-done.20) | copy-start | bytes 614404
  67.6 4.3 %copy-start.23 = (bf16[400,256]{1,0:T(8,128)(2,1)S(1)}, bf16[400,256]{1,0:T(8,128)(2,1)}, u32[]{:S(2)}) copy-start(bf16[400,256]{1,0:T(8,128)(2,1)} %copy-done.22) | copy-start | bytes 614404
  71.9 1.5 copy-start.24
  72.0 8.3 %copy-start.25 = (s32[16,16]{1,0:T(8,128)S(1)}, s32[16,16]{1,0:T(8,128)}, u32[]{:S(2)}) copy-start(s32[16,16]{1,0:T(8,128)} %param.15) | copy-start | bytes 3076
  73.4 49.9 %collective-permute-start.20 = (bf16[8,400,256]{2,1,0:T(8,128)(2,1)S(1)}, bf16[8,400,256]{2,1,0:T(8,128)(2,1)}, u32[]{:S(2)}, u32[]{:S(2)}) collective-permute-start(bf16[8,400,256]{2,1,0:T(8,128)(2,1)S(1)} %pack.3.refs_0_.own), channel_id=1, source_target_pairs={{0,1},{1,0},{2,3},{3,2},{4,5},{5,4},{6,7},{7,6},{8,9},{9,8},{10,11... | collective-permute-start | bytes 4915208 | tf_op jit(solution)/shard_map/ppermute | solution.py:222
  73.7 29.5 %collective-permute-start.12 = (s16[976,512]{1,0:T(8,128)(2,1)}, s16[976,512]{1,0:T(8,128)(2,1)S(1)}, u32[]{:S(2)}, u32[]{:S(2)}) collective-permute-start(s16[976,512]{1,0:T(8,128)(2,1)} %copy-done.24), channel_id=1, source_target_pairs={{0,4},{1,5},{2,6},{3,7},{4,0},{5,1},{6,2},{7,3},{8,12},{9,13},{10,... | collective-permute-start | bytes 2998280 | tf_op jit(solution)/shard_map/ppermute | solution.py:222
  81.7 23.7 %copy-start.2 = (f32[4,192,640]{2,1,0:T(8,128)S(1)}, f32[4,192,640]{2,1,0:T(8,128)}, u32[]{:S(2)}) copy-start(f32[4,192,640]{2,1,0:T(8,128)} %copy-done) | copy-start | bytes 5898244
  104.8 3.6 %copy-start.3 = (f32[2,192,512]{2,1,0:T(8,128)}, f32[2,192,512]{2,1,0:T(8,128)S(1)}, u32[]{:S(2)}) copy-start(f32[2,192,512]{2,1,0:T(8,128)S(1)} %get-tuple-element.57.refs_0_.held.held_out) | copy-start | bytes 2359300
  104.8 13.7 %collective-permute-start.16 = (s16[496,512]{1,0:T(8,128)(2,1)}, s16[496,512]{1,0:T(8,128)(2,1)}, u32[]{:S(2)}, u32[]{:S(2)}) collective-permute-start(s16[496,512]{1,0:T(8,128)(2,1)} %get-tuple-element.60), channel_id=1, source_target_pairs={{0,2},{1,3},{2,0},{3,1},{4,6},{5,7},{6,4},{7,5},{8,10},{9,11},{10,... | collective-permute-start | bytes 1523720 | tf_op jit(solution)/shard_map/ppermute | solution.py:222
  108.4 16.3 %collective-permute-start.15 = (s16[496,640]{1,0:T(8,128)(2,1)}, s16[496,640]{1,0:T(8,128)(2,1)S(1)}, u32[]{:S(2)}, u32[]{:S(2)}) collective-permute-start(s16[496,640]{1,0:T(8,128)(2,1)} %get-tuple-element.59), channel_id=1, source_target_pairs={{0,4},{1,5},{2,6},{3,7},{4,0},{5,1},{6,2},{7,3},{8,12},{9,13},{10,... | collective-permute-start | bytes 1904648 | tf_op jit(solution)/shard_map/ppermute | solution.py:222
  118.6 1.1 copy-start.4
  121.9 0.7 copy-start.11
  122.6 22.0 %collective-permute-start.18 = (s16[256,512]{1,0:T(8,128)(2,1)}, s16[256,512]{1,0:T(8,128)(2,1)}, u32[]{:S(2)}, u32[]{:S(2)}) collective-permute-start(s16[256,512]{1,0:T(8,128)(2,1)} %get-tuple-element.64), channel_id=1, source_target_pairs={{0,8},{1,9},{2,10},{3,11},{4,12},{5,13},{6,14},{7,15},{8,0},{9,1},... | collective-permute-start | bytes 786440 | tf_op jit(solution)/shard_map/ppermute | solution.py:222
  124.7 1.0 copy-start.12
  126.9 0.8 copy-start.7
  127.7 22.9 %copy-start.9 = (f32[1,192,640]{2,1,0:T(8,128)S(1)}, f32[1,192,640]{2,1,0:T(8,128)}, u32[]{:S(2)}) copy-start(f32[1,192,640]{2,1,0:T(8,128)} %copy-done.7) | copy-start | bytes 1474564
  127.7 22.9 %collective-permute-start.17 = (s16[256,640]{1,0:T(8,128)(2,1)}, s16[256,640]{1,0:T(8,128)(2,1)S(1)}, u32[]{:S(2)}, u32[]{:S(2)}) collective-permute-start(s16[256,640]{1,0:T(8,128)(2,1)} %get-tuple-element.63), channel_id=1, source_target_pairs={{0,8},{1,9},{2,10},{3,11},{4,12},{5,13},{6,14},{7,15},{8,0},{9,1},... | collective-permute-start | bytes 983048 | tf_op jit(solution)/shard_map/ppermute | solution.py:222
  144.6 1.0 copy-start.8
  145.7 1.0 copy-start.13
  150.9 1.3 collective-permute-start.19
  160.9 24.3 %copy-start.6 = (bf16[2,96,1024]{2,1,0:T(8,128)(2,1)S(1)}, bf16[2,96,1024]{2,1,0:T(8,128)(2,1)}, u32[]{:S(2)}) copy-start(bf16[2,96,1024]{2,1,0:T(8,128)(2,1)} %param.8) | copy-start | bytes 1179652
  160.9 17.8 %collective-permute-start.21 = (bf16[192,1024]{1,0:T(8,128)(2,1)S(1)}, bf16[192,1024]{1,0:T(8,128)(2,1)S(1)}, u32[]{:S(2)}, u32[]{:S(2)}) collective-permute-start(bf16[192,1024]{1,0:T(8,128)(2,1)S(1)} %bitcast.48), channel_id=1, source_target_pairs={{0,4},{1,5},{2,6},{3,7},{4,0},{5,1},{6,2},{7,3},{8,12},{9,13},{10,... | collective-permute-start | bytes 1179656 | tf_op jit(solution)/shard_map/ppermute | solution.py:222
  161.0 17.7 %collective-permute-start.22 = (bf16[192,1024]{1,0:T(8,128)(2,1)S(1)}, bf16[192,1024]{1,0:T(8,128)(2,1)S(1)}, u32[]{:S(2)}, u32[]{:S(2)}) collective-permute-start(bf16[192,1024]{1,0:T(8,128)(2,1)S(1)} %bitcast.49), channel_id=1, source_target_pairs={{0,2},{1,3},{2,0},{3,1},{4,6},{5,7},{6,4},{7,5},{8,10},{9,11},{10,... | collective-permute-start | bytes 1179656 | tf_op jit(solution)/shard_map/ppermute | solution.py:222
  161.6 20.3 %collective-permute-start.23 = (bf16[192,1024]{1,0:T(8,128)(2,1)S(1)}, bf16[192,1024]{1,0:T(8,128)(2,1)S(1)}, u32[]{:S(2)}, u32[]{:S(2)}) collective-permute-start(bf16[192,1024]{1,0:T(8,128)(2,1)S(1)} %bitcast.50), channel_id=1, source_target_pairs={{0,8},{1,9},{2,10},{3,11},{4,12},{5,13},{6,14},{7,15},{8,0},{9,1},... | collective-permute-start | bytes 1179656 | tf_op jit(solution)/shard_map/ppermute | solution.py:222
  163.1 18.8 %collective-permute-start.24 = (bf16[192,1024]{1,0:T(8,128)(2,1)S(1)}, bf16[192,1024]{1,0:T(8,128)(2,1)S(1)}, u32[]{:S(2)}, u32[]{:S(2)}) collective-permute-start(bf16[192,1024]{1,0:T(8,128)(2,1)S(1)} %bitcast.51), channel_id=1, source_target_pairs={{0,1},{1,0},{2,3},{3,2},{4,5},{5,4},{6,7},{7,6},{8,9},{9,8},{10,11... | collective-permute-start | bytes 1179656 | tf_op jit(solution)/shard_map/ppermute | solution.py:222
  182.0 6.6 %collective-permute-start.28 = (bf16[3,192,1024]{2,1,0:T(8,128)(2,1)S(1)}, bf16[3,192,1024]{2,1,0:T(8,128)(2,1)}, u32[]{:S(2)}, u32[]{:S(2)}) collective-permute-start(bf16[3,192,1024]{2,1,0:T(8,128)(2,1)S(1)} %get-tuple-element.68.refs_0_), channel_id=1, source_target_pairs={{0,1},{1,0},{2,3},{3,2},{4,5},{5,4},{6,7},{7,6},{8,9},{9,8},{10,11... | collective-permute-start | bytes 3538952 | tf_op jit(solution)/shard_map/ppermute | solution.py:222
  182.0 20.1 %collective-permute-start.27 = (bf16[2,192,1024]{2,1,0:T(8,128)(2,1)S(1)}, bf16[2,192,1024]{2,1,0:T(8,128)(2,1)}, u32[]{:S(2)}, u32[]{:S(2)}) collective-permute-start(bf16[2,192,1024]{2,1,0:T(8,128)(2,1)S(1)} %get-tuple-element.67.refs_1_), channel_id=1, source_target_pairs={{0,2},{1,3},{2,0},{3,1},{4,6},{5,7},{6,4},{7,5},{8,10},{9,11},{10,... | collective-permute-start | bytes 2359304 | tf_op jit(solution)/shard_map/ppermute | solution.py:222
  183.6 13.2 %collective-permute-start.25 = (bf16[192,1024]{1,0:T(8,128)(2,1)S(1)}, bf16[192,1024]{1,0:T(8,128)(2,1)}, u32[]{:S(2)}, u32[]{:S(2)}) collective-permute-start(bf16[192,1024]{1,0:T(8,128)(2,1)S(1)} %together.4.refs_0_), channel_id=1, source_target_pairs={{0,12},{1,13},{2,14},{3,15},{4,8},{5,9},{6,10},{7,11},{8,4},{9,5},... | collective-permute-start | bytes 1179656 | tf_op jit(solution)/shard_map/ppermute | solution.py:222
  203.4 3.0 %collective-permute-start.29 = (bf16[3,192,1024]{2,1,0:T(8,128)(2,1)S(1)}, bf16[3,192,1024]{2,1,0:T(8,128)(2,1)}, u32[]{:S(2)}, u32[]{:S(2)}) collective-permute-start(bf16[3,192,1024]{2,1,0:T(8,128)(2,1)S(1)} %pack.5.refs_0_), channel_id=1, source_target_pairs={{0,1},{1,0},{2,3},{3,2},{4,5},{5,4},{6,7},{7,6},{8,9},{9,8},{10,11... | collective-permute-start | bytes 3538952 | tf_op jit(solution)/shard_map/ppermute | solution.py:222
  203.5 11.7 %collective-permute-start.26 = (bf16[192,1024]{1,0:T(8,128)(2,1)}, bf16[192,1024]{1,0:T(8,128)(2,1)S(1)}, u32[]{:S(2)}, u32[]{:S(2)}) collective-permute-start(bf16[192,1024]{1,0:T(8,128)(2,1)} %collective-permute-done.25.refs_1_), channel_id=1, source_target_pairs={{0,2},{1,3},{2,0},{3,1},{4,6},{5,7},{6,4},{7,5},{8,10},{9,11},{10,... | collective-permute-start | bytes 1179656 | tf_op jit(solution)/shard_map/ppermute | solution.py:222
  215.2 1.7 collective-permute-start.30

commit v9 on v8

--- a/solution.py
+++ b/solution.py
@@ -209,6 +209,7 @@
 
 VMEM_LIMIT = 48 * 1024 * 1024
 SHORT = pl.CostEstimate(flops=1, bytes_accessed=1, transcendentals=0)
+LONG = pl.CostEstimate(flops=2 * 10**10, bytes_accessed=1, transcendentals=0)
 LOW_BITS = 4
 PACKED = 16 // LOW_BITS
 LEVELS = 32600.0 * 2**LOW_BITS
@@ -285,109 +286,91 @@
         sent[pl.ds(steps * rows, TILE), :] = powers[...].astype(jnp.int32).astype(jnp.int16)
 
 
-SLABS = 4
-PART_HEADS = GQ // 4
-
-
-def project_kernel(core, normed, weights, *refs):
-    outs, scratch = refs[-8:-4], refs[-4:]
-    kept, sent = outs[:2], outs[2:]
-    powers, slabs, arrived = scratch[:2], scratch[2], scratch[3]
+PART_HEADS = (3, 5)
+
+
+def project_kernel(part, core, normed, weights, *refs):
+    kept, sent, powers, slabs, arrived = refs[-5:]
     index = pl.program_id(0)
-    mine = GQ // 2 * HD
-    half = mine + HD
+    half = kept.shape[2]
+    heads = PART_HEADS[part] * HD
+    first = sum(PART_HEADS[:part]) * HD
 
     def copies(group):
-        slot = group % SLABS
         found = []
         for side in range(2):
             owner = core[0] if side == 0 else 1 - core[0]
-            spans = (
-                (group * GW + owner * mine, 0, mine),
-                (group * GW + (GQ + owner) * HD, mine, HD),
-            )
+            spans = [(group * GW + owner * (GQ // 2 * HD) + first, 0, heads)]
+            if half > heads:
+                spans.append((group * GW + (GQ + owner) * HD, heads, HD))
             for number, (start, offset, size) in enumerate(spans):
                 found.append(
                     pltpu.make_async_copy(
                         weights.at[:, pl.ds(pl.multiple_of(start, HD), size)],
-                        slabs.at[slot, :, pl.ds(side * half + offset, size)],
-                        arrived.at[slot, side, number],
+                        slabs.at[group, :, pl.ds(side * half + offset, size)],
+                        arrived.at[group, side, number],
                     )
                 )
         return found
 
     @pl.when(index == 0)
     def _():
-        for group in range(SLABS):
+        for group in range(KVH):
             for copy in copies(group):
                 copy.start()
-        for ref in powers:
-            ref[...] = jnp.zeros_like(ref)
+        powers[...] = jnp.zeros_like(powers)
 
     for copy in copies(index):
         copy.wait()
 
-    slot = index % SLABS
-    part = PART_HEADS * HD
-    spans = (((0, part), (mine, HD)), ((part, part),))
+    found = []
+    rows = coded_rows(normed.shape[0])
     for side in range(2):
-        for number in range(2):
-            offset = 0
-            found = []
-            for first, size in spans[number]:
-                for start in range(0, size, 2 * HD):
-                    wide = min(2 * HD, size - start)
-                    product = jnp.dot(
-                        normed[...],
-                        slabs[slot, :, side * half + first + start : side * half + first + start + wide],
-                        preferred_element_type=jnp.float32,
-                    )
-                    at = slice(offset, offset + wide)
-                    if side == 0:
-                        kept[number][0, :, at] = product
-                    else:
-                        rows = coded_rows(product.shape[0])
-                        codes, power = encode(product)
-                        sent[number][pl.ds(pl.multiple_of(index * rows, TILE), rows), at] = codes
-                        found.append(power)
-                    offset += wide
-            if found:
-                powers[number][pl.ds(index, 1), :] = jnp.concatenate(found, 1)
-
-    @pl.when(index + SLABS < KVH)
-    def _():
-        for copy in copies(index + SLABS):
-            copy.start()
+        for start in range(0, half, 2 * HD):
+            at = slice(start, min(start + 2 * HD, half))
+            product = jnp.dot(
+                normed[...],
+                slabs[index, :, side * half + at.start : side * half + at.stop],
+                preferred_element_type=jnp.float32,
+            )
+            if side == 0:
+                kept[0, :, at] = product
+            else:
+                codes, power = encode(product)
+                sent[pl.ds(pl.multiple_of(index * rows, TILE), rows), at] = codes
+                found.append(power)
+    powers[pl.ds(index, 1), :] = jnp.concatenate(found, 1)
 
     @pl.when(index == KVH - 1)
     def _():
-        for target, ref in zip(sent, powers):
-            target[pl.ds(target.shape[0] - TILE, TILE), :] = (
-                ref[...].astype(jnp.int32).astype(jnp.int16)
-            )
-
-
-def project(core, normed, qkv_weight, after):
+        sent[pl.ds(KVH * rows, TILE), :] = powers[...].astype(jnp.int32).astype(jnp.int16)
+
+
+def project(core, normed, qkv_weight, part, after):
     rows, width = normed.shape
-    columns = (PART_HEADS * HD + HD, PART_HEADS * HD)
+    columns = PART_HEADS[part] * HD + (HD if part == 0 else 0)
     sent_rows = KVH * coded_rows(rows) + TILE
     return pl.pallas_call(
-        project_kernel,
+        functools.partial(project_kernel, part),
         grid_spec=pltpu.PrefetchScalarGridSpec(
             num_scalar_prefetch=1,
             grid=(KVH,),
             in_specs=[pl.BlockSpec((rows, width), lambda t, c: (0, 0))]
             + [pl.BlockSpec(memory_space=pl.ANY)] * (1 + len(after)),
-            out_specs=[pl.BlockSpec((1, rows, n), lambda t, c: (t, 0, 0)) for n in columns]
-            + [pl.BlockSpec((sent_rows, n), lambda t, c: (0, 0)) for n in columns],
-            scratch_shapes=[pltpu.VMEM((TILE, n), jnp.float32) for n in columns]
-            + [
-                pltpu.VMEM((SLABS, width, GW), jnp.bfloat16),
-                pltpu.SemaphoreType.DMA((SLABS, 2, 2)),
+            out_specs=[
+                pl.BlockSpec((1, rows, columns), lambda t, c: (t, 0, 0)),
+                pl.BlockSpec((sent_rows, columns), lambda t, c: (0, 0)),
+            ],
+            scratch_shapes=[
+                pltpu.VMEM((TILE, columns), jnp.float32),
+                pltpu.VMEM((KVH, width, 2 * columns), jnp.bfloat16),
+                pltpu.SemaphoreType.DMA((KVH, 2, 2)),
             ],
         ),
-        out_shape=[jax.ShapeDtypeStruct((KVH, rows, n), jnp.float32) for n in columns]
-        + [jax.ShapeDtypeStruct((sent_rows, n), jnp.int16) for n in columns],
+        out_shape=[
+            jax.ShapeDtypeStruct((KVH, rows, columns), jnp.float32),
+            jax.ShapeDtypeStruct((sent_rows, columns), jnp.int16),
+        ],
         compiler_params=pltpu.CompilerParams(vmem_limit_bytes=VMEM_LIMIT),
         cost_estimate=SHORT,
         name="project",
@@ -450,7 +433,7 @@
     )(bit, held, held, landed, landed, landed, *after)
 
 
-def finish_kernel(after_count, core, held, landed, cosine, sine, *refs):
+def finish_kernel(heads, after_count, core, held, landed, cosine, sine, *refs):
     queries, *pair = refs[after_count:]
     coded = coded_rows(held.shape[1])
     power = landed[pl.ds(coded, TILE), :].astype(jnp.int32).astype(jnp.float32)[0:1]
@@ -459,27 +442,27 @@
     for head in range(joined.shape[1] // HD):
         raw = joined[:, head * HD : (head + 1) * HD].astype(jnp.float32)
         turned = raw * cosine[...] + pltpu.roll(raw, HD // 2, 1) * sine[...]
-        if head < PART_HEADS:
+        if head < heads:
             queries[:, head * HD : (head + 1) * HD] = turned.astype(jnp.bfloat16)
         else:
             pair[0][...] = jnp.where(core[0] == 0, turned, raw).astype(jnp.bfloat16)
 
 
-def finish(core, held, landed, cosine, sine, after):
+def finish(core, held, landed, cosine, sine, heads, after):
     _, rows, columns = held.shape
     whole = pl.BlockSpec(memory_space=pltpu.VMEM)
-    shapes = [jax.ShapeDtypeStruct((rows, PART_HEADS * HD), jnp.bfloat16)]
-    if columns > PART_HEADS * HD:
+    shapes = [jax.ShapeDtypeStruct((rows, heads * HD), jnp.bfloat16)]
+    if columns > heads * HD:
         shapes.append(jax.ShapeDtypeStruct((rows, HD), jnp.bfloat16))
     return pl.pallas_call(
-        functools.partial(finish_kernel, len(after)),
+        functools.partial(finish_kernel, heads, len(after)),
         in_specs=[pl.BlockSpec(memory_space=pltpu.SMEM)]
         + [whole] * 4
         + [pl.BlockSpec(memory_space=pl.ANY)] * len(after),
         out_specs=[whole] * len(shapes),
         out_shape=shapes,
         compiler_params=pltpu.CompilerParams(vmem_limit_bytes=VMEM_LIMIT),
-        cost_estimate=SHORT,
+        cost_estimate=LONG,
         name="finish",
     )(core, held, landed, cosine, sine, *after)
 
@@ -574,19 +557,22 @@
     across = swap(attention, 2)
     far = swap(attention, 8)
     partner = swap(attention, 1)
-    first, onward = pack([near, across, far], [(0, 1, 2), (0, 2)], [partner])
-    (attention,) = together([attention], [onward])
-
-    across_onward = swap(onward, 2)
+    near, attention = together([near, attention], [across, partner])
+
+    across_near = swap(near, 2)
     farthest = swap(attention, 12)
+    (first,) = pack([near, across], [(0, 1)], [])
     first_partner = swap(first, 1)
     mixed = add(start, [attention, partner], (0, 1))
-    mixed = add(mixed, [first, first_partner], (4, 2, 8, 5, 3, 9))
-    (second,) = pack([across_onward, farthest], [(0, 1, 2)], [mixed])
+    (far,) = together([far], [across_near, first_partner, mixed])
+
+    across_far = swap(far, 2)
+    mixed = add(mixed, [first, first_partner], (4, 2, 5, 3))
+    (second,) = pack([far, across_near, across_far, farthest], [(0, 1, 2, 3)], [mixed])
 
     last = swap(farthest, 2)
     second_partner = swap(second, 1)
-    mixed = add(mixed, [second, second_partner], (6, 10, 12, 7, 11, 13))
+    mixed = add(mixed, [second, second_partner], (8, 6, 10, 12, 9, 7, 11, 13))
     (last,) = together([last], [mixed])
 
     last_partner = swap(last, 1)
@@ -787,35 +773,40 @@
     def folded(part, b, landed, low, *after):
         return fold(bits[b], part, landed, low, after)
 
-    def finished(part, landed, *after):
-        return finish(bits[0], part, landed, cosine, sine, after)
-
-    for k in range(3, KVH):
+    def finished(part, number, landed, *after):
+        return finish(bits[0], part, landed, cosine, sine, PART_HEADS[number], after)
+
+    for k in (1, 3, 4, 5):
         handed(k)
-    held_a, held_b, sent_a, sent_b = project(bits[0], normed, qkv_weight, cache_pieces[:1])
-    sent_a, sent_b, cache_pieces[1], cache_pieces[2] = together(
-        [sent_a, sent_b] + cache_pieces[1:3], cache_pieces[3:]
-    )
-    core_a, core_b = swap(sent_a, 1), swap(sent_b, 1)
-    for k in (1, 2):
+    held_a, sent_a = project(bits[0], normed, qkv_weight, 0, cache_pieces[:1])
+    core_a = swap(sent_a, 1)
+    held_b, sent_b = project(
+        bits[0], normed, qkv_weight, 1, [held_a, cache_pieces[1], cache_pieces[3]]
+    )
+    sent_b, cache_pieces[2], cache_pieces[6], cache_pieces[7] = together(
+        [sent_b, cache_pieces[2], cache_pieces[6], cache_pieces[7]], cache_pieces[4:6]
+    )
+    core_b = swap(sent_b, 1)
+    held_a, sent_a = folded(held_a, 1, core_a, 1, sent_b)
+    line_a = swap(sent_a, 2)
+    for k in (2, 6, 7):
         handed(k)
-    held_a, sent_a = folded(held_a, 1, core_a, 1)
-    line_a = swap(sent_a, 2)
     held_b, sent_b = folded(held_b, 2, core_b, 2, held_a)
     line_b = swap(sent_b, 4)
+    late = [cache_pieces[k] for k in (2, 6, 7)]
+    held_a, sent_a = folded(held_a, 2, line_a, 1, held_b, *late)
+    line_a = swap(sent_a, 4)
+    held_b, sent_b = folded(held_b, 1, line_b, 1, held_a)
+    line_b = swap(sent_b, 2)
     (cache_own,) = pack(cache_pieces, [tuple(range(KVH))], [held_b])
     cache_other = swap(cache_own, 1)
-    held_b, sent_b = folded(held_b, 1, line_b, 1, cache_own)
-    line_b = swap(sent_b, 2)
-    held_a, sent_a = folded(held_a, 2, line_a, 1, held_b)
-    line_a = swap(sent_a, 4)
+    held_a, sent_a = folded(held_a, 3, line_a, 1, cache_own)
+    line_a = swap(sent_a, 8)
     held_b, sent_b = folded(held_b, 3, line_b, 1, held_a)
     line_b = swap(sent_b, 8)
-    held_a, sent_a = folded(held_a, 3, line_a, 1, held_b)
-    line_a = swap(sent_a, 8)
-    (query_b,) = finished(held_b, line_b, held_a)
-    query_a, pair = finished(held_a, line_a, query_b)
+    query_a, pair = finished(held_a, 0, line_a, held_b)
     pair_other = swap(pair, 1)
+    (query_b,) = finished(held_b, 1, line_b, query_a)
     query_chunks = [query_a, query_b]
     cache_parts = (cache_own, cache_other)
     keys = jnp.where(core == 0, pair, pair_other)

time: 222 us -> 237 us (1.068)
  waiting for transfers between devices: 84.2 us -> 112 us
  starting transfers between devices: 46.5 us -> 34.5 us
    ppermute x31 -> x32, waiting for transfers between devices: 84.2 us -> 112 us  [swap(): return lax.ppermute(value, 'tensor', [(i, i ^ bit) for i in range(devices)])]
    ppermute x31 -> x32, starting transfers between devices: 46.5 us -> 34.5 us  [swap(): return lax.ppermute(value, 'tensor', [(i, i ^ bit) for i in range(devices)])]
    pallas_call x3 -> x4, Pallas kernels: 19.6 us -> 22 us  [the longest x2 20.6 us: project(): pl.pallas_call(functools.partial(project_kernel, part), grid_spec=pltpu.P...]
    unnamed x56 -> x68, local copies, waits for them, and re-layouts: 11 us -> 9.41 us
  transfers between devices with their start and end apart: 31 -> 32, of which waited for: 17 -> 17; matrix products, arithmetic and copies ran while one was open for 3% -> 2% of each run, Pallas kernels for 26% -> 24%
where the time goes in v9:
time: 237 us; the launch traced here: 236 us
  waiting for transfers between devices  112 us (47%)
  Pallas kernels  71.6 us (30%)
  starting transfers between devices  34.5 us (15%)
  local copies, waits for them, and re-layouts  12.7 us (5%)
  other arithmetic  4.8 us (2%)
    ppermute x32, waiting for transfers between devices, swap(): return lax.ppermute(value, 'tensor', [(i, i ^ bit) for i in range(devices)])  112 us
    ppermute x32, starting transfers between devices, swap(): return lax.ppermute(value, 'tensor', [(i, i ^ bit) for i in range(devices)])  34.5 us
    pallas_call x4, Pallas kernels, mix(): pl.pallas_call(functools.partial(mix_kernel, len(pieces)), in_specs=[pl.B...  21.7 us
    pallas_call x2, Pallas kernels, project(): pl.pallas_call(functools.partial(project_kernel, part), grid_spec=pltpu.P...  20.6 us
    pallas_call x6, Pallas kernels, fold(): pl.pallas_call(functools.partial(fold_kernel, steps, low), grid_spec=pltp...  16.9 us
    unnamed x68, local copies, waits for them, and re-layouts  9.41 us
    pallas_call x1, Pallas kernels, attend(): pl.pallas_call(attend_kernel, in_specs=[pl.BlockSpec(memory_space=pltpu.S...  8.36 us
  transfers between devices with their start and end apart: 32, of which 17 were waited for; matrix products, arithmetic and copies ran while one was open for 2% of the time, Pallas kernels for 24%

profile of v9, /device:TPU:0, one launch (start us, length us, event | category | flops | bytes accessed | tf_op | source)
XLA Modules:
  0.0 236.4 jit_solution(13663738844250666952)
XLA Ops:
  0.0 1.2 fusion
  1.2 3.0 %collective-permute-start = (f32[2,96]{1,0:T(2,128)S(1)}, f32[2,96]{1,0:T(2,128)S(1)}, u32[]{:S(2)}, u32[]{:S(2)}) collective-permute-start(f32[2,96]{1,0:T(2,128)S(1)} %fusion), channel_id=1, source_target_pairs={{0,2},{1,3},{2,0},{3,1},{4,6},{5,7},{6,4},{7,5},{8,10},{9,11},{10,... | collective-permute-start | bytes 2312 | tf_op jit(solution)/shard_map/ppermute | solution.py:223
  4.3 1.5 collective-permute-done
  5.8 1.1 collective-permute-done.1
  7.0 2.1 collective-permute-start.2
  9.0 0.8 reshape.240
  9.8 0.7 convert_element_type.29
  10.6 3.0 %collective-permute-start.3 = (f32[2,96]{1,0:T(2,128)S(1)}, f32[2,96]{1,0:T(2,128)S(1)}, u32[]{:S(2)}, u32[]{:S(2)}) collective-permute-start(f32[2,96]{1,0:T(2,128)S(1)} %add.139), channel_id=1, source_target_pairs={{0,8},{1,9},{2,10},{3,11},{4,12},{5,13},{6,14},{7,15},{8,0},{9,1},... | collective-permute-start | bytes 2312 | tf_op jit(solution)/shard_map/ppermute | solution.py:223
  13.6 1.4 copy-done.5
  15.2 1.6 collective-permute-start.5
  16.8 1.5 collective-permute-start.6
  18.6 3.5 %collective-permute-start.8 = (bf16[400,256]{1,0:T(8,128)(2,1)S(1)}, bf16[400,256]{1,0:T(8,128)(2,1)S(1)}, u32[]{:S(2)}, u32[]{:S(2)}) collective-permute-start(bf16[400,256]{1,0:T(8,128)(2,1)S(1)} %get-tuple-element.47), channel_id=1, source_target_pairs={{0,10},{1,11},{2,8},{3,9},{4,14},{5,15},{6,12},{7,13},{8,2},{9,3},... | collective-permute-start | bytes 614408 | tf_op jit(solution)/shard_map/ppermute | solution.py:223
  22.4 9.1 %project.2 = (f32[8,192,512]{2,1,0:T(8,128)S(1)}, s16[1936,512]{1,0:T(8,128)(2,1)}) custom-call(s32[1]{0:T(128)} %bitcast.2.core, bf16[192,1024]{1,0:T(8,128)(2,1)S(1)} %bitcast.47, bf16[1024,18432]{1,0:T(8,128)(2,1)} %weights.3, bf16[400,256]{1,0:T(8,128)(2,1)S(1)} %get-tuple-element.37.refs_0_), custom_call_target="tpu_custom_call" | custom-call | flops 1 | bytes 1 | tf_op jit(solution)/shard_map/project/pallas_call | solution.py:353
  31.5 1.6 copy-done
  33.1 11.5 %project.3 = (f32[8,192,640]{2,1,0:T(8,128)}, s16[1936,640]{1,0:T(8,128)(2,1)}) custom-call(s32[1]{0:T(128)} %bitcast.2.core, bf16[192,1024]{1,0:T(8,128)(2,1)S(1)} %bitcast.48, bf16[1024,18432]{1,0:T(8,128)(2,1)} %weights.3, f32[8,192,512]{2,1,0:T(8,128)} %copy-done, bf16[400,256]{1,0:T(8,128)(2,1)S(1)} %collective-permute-done.5.refs_1_, ...), custom_call_target="tpu_custom_call" | custom-call | flops 1 | bytes 1 | tf_op jit(solution)/shard_map/project/pallas_call | solution.py:353
  44.7 0.7 copy-done.19
  45.4 0.7 copy-done.21
  46.1 0.7 copy-done.23
  47.4 0.7 add_convert_fusion
  48.1 6.5 %collective-permute-done.4.landed.landed_out.landed_powers = s16[1936,512]{1,0:T(8,128)(2,1)S(1)} collective-permute-done((s16[1936,512]{1,0:T(8,128)(2,1)}, s16[1936,512]{1,0:T(8,128)(2,1)S(1)}, u32[]{:S(2)}, u32[]{:S(2)}) %collective-permute-start.4) | collective-permute-done | bytes 1982496 | tf_op jit(solution)/shard_map/ppermute | solution.py:223
  54.5 4.6 %fold.6 = (f32[4,192,512]{2,1,0:T(8,128)S(1)}, s16[976,512]{1,0:T(8,128)(2,1)}) custom-call(s32[1]{0:T(128)} %bitcast.5.bit, f32[8,192,512]{2,1,0:T(8,128)} %copy-done, f32[8,192,512]{2,1,0:T(8,128)} %copy-done, s16[1936,512]{1,0:T(8,128)(2,1)S(1)} %collective-permute-done.4.landed.landed_out.landed_powers, ...), custom_call_target="tpu_custom_call" | custom-call | flops 1 | bytes 1 | tf_op jit(solution)/shard_map/fold/pallas_call | solution.py:407
  59.1 0.5 collective-permute-start.9
  59.7 5.9 %fold.7 = (f32[4,192,640]{2,1,0:T(8,128)S(1)}, s16[976,640]{1,0:T(8,128)(2,1)}) custom-call(s32[1]{0:T(128)} %bitcast.4.bit, f32[8,192,640]{2,1,0:T(8,128)} %get-tuple-element.51.held.held_out, f32[8,192,640]{2,1,0:T(8,128)} %get-tuple-element.51.held.held_out, s16[1936,640]{1,0:T(8,128)(2,1)} %collective-permute-done.10.landed.landed_out.landed_powers, ...), custom_call_target="tpu_custom_call" | custom-call | flops 1 | bytes 1 | tf_op jit(solution)/shard_map/fold/pallas_call | solution.py:407
  65.5 1.3 copy-done.1
  67.5 0.6 add.157
  68.2 0.7 select_reduce_fusion.1
  68.9 1.6 collective-permute-start.11
  70.5 4.8 %collective-permute-start.13 = (bf16[400,256]{1,0:T(8,128)(2,1)S(1)}, bf16[400,256]{1,0:T(8,128)(2,1)S(1)}, u32[]{:S(2)}, u32[]{:S(2)}) collective-permute-start(bf16[400,256]{1,0:T(8,128)(2,1)S(1)} %copy-done.24), channel_id=1, source_target_pairs={{0,14},{1,15},{2,12},{3,13},{4,10},{5,11},{6,8},{7,9},{8,6},{9,7},... | collective-permute-start | bytes 614408 | tf_op jit(solution)/shard_map/ppermute | solution.py:223
  75.7 33.7 %collective-permute-done.11.refs_1_.refs_2_ = bf16[400,256]{1,0:T(8,128)(2,1)S(1)} collective-permute-done((bf16[400,256]{1,0:T(8,128)(2,1)S(1)}, bf16[400,256]{1,0:T(8,128)(2,1)S(1)}, u32[]{:S(2)}, u32[]{:S(2)}) %collective-permute-start.11) | collective-permute-done | bytes 204832 | tf_op jit(solution)/shard_map/ppermute | solution.py:223
  109.4 0.8 collective-permute-done.13.refs_3_.refs_7_
  110.3 2.1 fold.8
  112.6 2.0 fold.9
  114.6 0.7 collective-permute-start.17
  115.7 9.2 %collective-permute-done.14.landed.landed_out.landed_powers = s16[496,512]{1,0:T(8,128)(2,1)S(1)} collective-permute-done((s16[496,512]{1,0:T(8,128)(2,1)S(1)}, s16[496,512]{1,0:T(8,128)(2,1)S(1)}, u32[]{:S(2)}, u32[]{:S(2)}) %collective-permute-start.14) | collective-permute-done | bytes 507936 | tf_op jit(solution)/shard_map/ppermute | solution.py:223
  124.8 1.1 fold.10
  125.9 0.7 copy-done.16
  126.7 1.3 collective-permute-start.16
  128.1 1.7 collective-permute-done.17.landed.landed_out.landed_powers
  129.9 1.0 copy-done.17
  130.9 1.2 fold.11
  132.1 7.6 %collective-permute-done.16.landed = s16[256,512]{1,0:T(8,128)(2,1)} collective-permute-done((s16[256,512]{1,0:T(8,128)(2,1)}, s16[256,512]{1,0:T(8,128)(2,1)}, u32[]{:S(2)}, u32[]{:S(2)}) %collective-permute-start.16) | collective-permute-done | bytes 262176 | tf_op jit(solution)/shard_map/ppermute | solution.py:223
  139.7 1.2 finish.2
  141.1 1.0 collective-permute-done.19
  142.4 16.8 %collective-permute-done.18.landed = s16[256,640]{1,0:T(8,128)(2,1)S(1)} collective-permute-done((s16[256,640]{1,0:T(8,128)(2,1)}, s16[256,640]{1,0:T(8,128)(2,1)S(1)}, u32[]{:S(2)}, u32[]{:S(2)}) %collective-permute-start.18) | collective-permute-done | bytes 327712 | tf_op jit(solution)/shard_map/ppermute | solution.py:223
  159.1 1.0 copy-done.27
  160.6 0.7 slice_reduce_fusion
  162.1 8.4 %attend.1 = bf16[16,96,128]{2,1,0:T(8,128)(2,1)S(1)} custom-call(s32[24]{0:T(128)S(1)} %copy-done.25, bf16[16,96,128]{2,1,0:T(8,128)(2,1)S(1)} %bitcast.55, bf16[16,16,128]{2,1,0:T(8,128)(2,1)S(1)} %pad.12.new_keys, bf16[16,16,128]{2,1,0:T(8,128)(2,1)S(1)} %pad.13.new_values, bf16[8,400,256]{2,1,0:T(8,128)(2,1)S(1)} %pack.3.refs_0_.own, ...), custom_call_target="tpu_custom_call" | custom-call | flops 1 | bytes 1 | tf_op jit(solution)/shard_map/attend/pallas_call | solution.py:665
  171.2 1.7 collective-permute-start.26
  172.8 15.2 %collective-permute-done.21.refs_0_ = bf16[192,1024]{1,0:T(8,128)(2,1)} collective-permute-done((bf16[192,1024]{1,0:T(8,128)(2,1)S(1)}, bf16[192,1024]{1,0:T(8,128)(2,1)}, u32[]{:S(2)}, u32[]{:S(2)}) %collective-permute-start.21) | collective-permute-done | bytes 393248 | tf_op jit(solution)/shard_map/ppermute | solution.py:223
  188.1 4.1 %collective-permute-done.26.refs_0_ = bf16[192,1024]{1,0:T(8,128)(2,1)} collective-permute-done((bf16[192,1024]{1,0:T(8,128)(2,1)S(1)}, bf16[192,1024]{1,0:T(8,128)(2,1)}, u32[]{:S(2)}, u32[]{:S(2)}) %collective-permute-start.26) | collective-permute-done | bytes 393248 | tf_op jit(solution)/shard_map/ppermute | solution.py:223
  192.2 1.0 pack.4.refs_0_
  193.3 1.7 collective-permute-start.27
  195.1 1.7 collective-permute-start.24
  196.7 3.4 %mix.4.refs_3_ = f32[192,1024]{1,0:T(8,128)S(1)} custom-call(s32[2]{0:T(128)S(1)} %pad_add_fusion.1.places, bf16[192,1024]{1,0:T(8,128)(2,1)S(1)} %get-tuple-element.67.refs_0_, bf16[192,1024]{1,0:T(8,128)(2,1)S(1)} %collective-permute-done.23.refs_3_.refs_1_, bf16[16384,1024]{1,0:T(8,128)(2,1)} %refs_2_.7, bf16[192,1024]{1,0:T(8,128)(2,1)S(1)} %bitcast.49), custom_call_target="tpu_custom_call" | custom-call | flops 1 | bytes 1 | tf_op jit(solution)/shard_map/mix/pallas_call | solution.py:510
  200.1 5.0 %collective-permute-done.27.refs_1_ = bf16[192,1024]{1,0:T(8,128)(2,1)} collective-permute-done((bf16[192,1024]{1,0:T(8,128)(2,1)}, bf16[192,1024]{1,0:T(8,128)(2,1)}, u32[]{:S(2)}, u32[]{:S(2)}) %collective-permute-start.27) | collective-permute-done | bytes 393248 | tf_op jit(solution)/shard_map/ppermute | solution.py:223
  205.1 1.6 collective-permute-start.29
  206.9 5.0 %mix.5.refs_4_.refs_3_ = f32[192,1024]{1,0:T(8,128)S(1)} custom-call(s32[4]{0:T(128)S(1)} %pad_add_fusion.2.places, bf16[2,192,1024]{2,1,0:T(8,128)(2,1)S(1)} %pack.4.refs_0_, bf16[2,192,1024]{2,1,0:T(8,128)(2,1)S(1)} %collective-permute-done.28.refs_2_.refs_1_, bf16[16384,1024]{1,0:T(8,128)(2,1)} %refs_2_.7, f32[192,1024]{1,0:T(8,128)S(1)} %mix.4.refs_3_), custom_call_target="tpu_custom_call" | custom-call | flops 1 | bytes 1 | tf_op jit(solution)/shard_map/mix/pallas_call | solution.py:510
  211.9 4.2 %collective-permute-done.29.refs_2_ = bf16[192,1024]{1,0:T(8,128)(2,1)} collective-permute-done((bf16[192,1024]{1,0:T(8,128)(2,1)}, bf16[192,1024]{1,0:T(8,128)(2,1)}, u32[]{:S(2)}, u32[]{:S(2)}) %collective-permute-start.29) | collective-permute-done | bytes 393248 | tf_op jit(solution)/shard_map/ppermute | solution.py:223
  216.1 1.5 pack.5.refs_0_
  217.7 1.7 collective-permute-start.25
  219.5 1.7 collective-permute-done.30.refs_1_
  221.2 9.1 %mix.6.refs_1_.refs_3_ = f32[192,1024]{1,0:T(8,128)S(1)} custom-call(s32[8]{0:T(128)S(1)} %stack.77.places, bf16[4,192,1024]{2,1,0:T(8,128)(2,1)S(1)} %pack.5.refs_0_, bf16[4,192,1024]{2,1,0:T(8,128)(2,1)} %collective-permute-done.30.refs_1_, bf16[16384,1024]{1,0:T(8,128)(2,1)} %refs_2_.7, f32[192,1024]{1,0:T(8,128)S(1)} %mix.5.refs_4_.refs_3_), custom_call_target="tpu_custom_call" | custom-call | flops 1 | bytes 1 | tf_op jit(solution)/shard_map/mix/pallas_call | solution.py:510
  230.7 1.5 collective-permute-done.31.refs_1_
  232.2 4.1 %mix.7 = bf16[192,1024]{1,0:T(8,128)(2,1)} custom-call(s32[2]{0:T(128)S(1)} %pad_add_fusion.places, bf16[192,1024]{1,0:T(8,128)(2,1)S(1)} %together.7.refs_0_, bf16[192,1024]{1,0:T(8,128)(2,1)S(1)} %collective-permute-done.31.refs_1_, bf16[16384,1024]{1,0:T(8,128)(2,1)} %refs_2_.7, f32[192,1024]{1,0:T(8,128)S(1)} %mix.6.refs_1_.refs_3_), custom_call_target="tpu_custom_call" | custom-call | flops 1 | bytes 1 | tf_op jit(solution)/shard_map/mix/pallas_call | solution.py:510
  (146 shorter events, 6.0 us)
Async XLA Ops:
  0.0 22.2 %copy-start.3 = (bf16[2,96,1024]{2,1,0:T(8,128)(2,1)S(1)}, bf16[2,96,1024]{2,1,0:T(8,128)(2,1)}, u32[]{:S(2)}) copy-start(bf16[2,96,1024]{2,1,0:T(8,128)(2,1)} %param.8) | copy-start | bytes 1179652
  1.2 4.6 %collective-permute-start = (f32[2,96]{1,0:T(2,128)S(1)}, f32[2,96]{1,0:T(2,128)S(1)}, u32[]{:S(2)}, u32[]{:S(2)}) collective-permute-start(f32[2,96]{1,0:T(2,128)S(1)} %fusion), channel_id=1, source_target_pairs={{0,2},{1,3},{2,0},{3,1},{4,6},{5,7},{6,4},{7,5},{8,10},{9,11},{10,... | collective-permute-start | bytes 2312 | tf_op jit(solution)/shard_map/ppermute | solution.py:223
  5.8 1.1 collective-permute-start.1
  7.0 3.6 %collective-permute-start.2 = (f32[2,96]{1,0:T(2,128)S(1)}, f32[2,96]{1,0:T(2,128)S(1)}, u32[]{:S(2)}, u32[]{:S(2)}) collective-permute-start(f32[2,96]{1,0:T(2,128)S(1)} %add.138), channel_id=1, source_target_pairs={{0,4},{1,5},{2,6},{3,7},{4,0},{5,1},{6,2},{7,3},{8,12},{9,13},{10,... | collective-permute-start | bytes 2312 | tf_op jit(solution)/shard_map/ppermute | solution.py:223
  10.6 11.6 %collective-permute-start.3 = (f32[2,96]{1,0:T(2,128)S(1)}, f32[2,96]{1,0:T(2,128)S(1)}, u32[]{:S(2)}, u32[]{:S(2)}) collective-permute-start(f32[2,96]{1,0:T(2,128)S(1)} %add.139), channel_id=1, source_target_pairs={{0,8},{1,9},{2,10},{3,11},{4,12},{5,13},{6,14},{7,15},{8,0},{9,1},... | collective-permute-start | bytes 2312 | tf_op jit(solution)/shard_map/ppermute | solution.py:223
  13.6 1.4 copy-start.5
  15.2 16.3 %copy-start.14 = (bf16[400,256]{1,0:T(8,128)(2,1)}, bf16[400,256]{1,0:T(8,128)(2,1)S(1)}, u32[]{:S(2)}) copy-start(bf16[400,256]{1,0:T(8,128)(2,1)S(1)} %get-tuple-element.37.refs_0_) | copy-start | bytes 614404
  15.2 17.9 %collective-permute-start.5 = (bf16[400,256]{1,0:T(8,128)(2,1)S(1)}, bf16[400,256]{1,0:T(8,128)(2,1)S(1)}, u32[]{:S(2)}, u32[]{:S(2)}) collective-permute-start(bf16[400,256]{1,0:T(8,128)(2,1)S(1)} %get-tuple-element.40), channel_id=1, source_target_pairs={{0,2},{1,3},{2,0},{3,1},{4,6},{5,7},{6,4},{7,5},{8,10},{9,11},{10,... | collective-permute-start | bytes 614408 | tf_op jit(solution)/shard_map/ppermute | solution.py:223
  16.8 16.3 %collective-permute-start.6 = (bf16[400,256]{1,0:T(8,128)(2,1)S(1)}, bf16[400,256]{1,0:T(8,128)(2,1)S(1)}, u32[]{:S(2)}, u32[]{:S(2)}) collective-permute-start(bf16[400,256]{1,0:T(8,128)(2,1)S(1)} %get-tuple-element.41), channel_id=1, source_target_pairs={{0,6},{1,7},{2,4},{3,5},{4,2},{5,3},{6,0},{7,1},{8,14},{9,15},{10,... | collective-permute-start | bytes 614408 | tf_op jit(solution)/shard_map/ppermute | solution.py:223
  18.3 26.3 %collective-permute-start.7 = (bf16[400,256]{1,0:T(8,128)(2,1)S(1)}, bf16[400,256]{1,0:T(8,128)(2,1)S(1)}, u32[]{:S(2)}, u32[]{:S(2)}) collective-permute-start(bf16[400,256]{1,0:T(8,128)(2,1)S(1)} %get-tuple-element.46), channel_id=1, source_target_pairs={{0,8},{1,9},{2,10},{3,11},{4,12},{5,13},{6,14},{7,15},{8,0},{9,1},... | collective-permute-start | bytes 614408 | tf_op jit(solution)/shard_map/ppermute | solution.py:223
  18.6 26.0 %collective-permute-start.8 = (bf16[400,256]{1,0:T(8,128)(2,1)S(1)}, bf16[400,256]{1,0:T(8,128)(2,1)S(1)}, u32[]{:S(2)}, u32[]{:S(2)}) collective-permute-start(bf16[400,256]{1,0:T(8,128)(2,1)S(1)} %get-tuple-element.47), channel_id=1, source_target_pairs={{0,10},{1,11},{2,8},{3,9},{4,14},{5,15},{6,12},{7,13},{8,2},{9,3},... | collective-permute-start | bytes 614408 | tf_op jit(solution)/shard_map/ppermute | solution.py:223
  31.5 1.6 copy-start
  33.1 11.5 %copy-start.6 = (bf16[400,256]{1,0:T(8,128)(2,1)}, bf16[400,256]{1,0:T(8,128)(2,1)S(1)}, u32[]{:S(2)}) copy-start(bf16[400,256]{1,0:T(8,128)(2,1)S(1)} %collective-permute-done.5.refs_1_) | copy-start | bytes 614404
  33.1 11.5 %copy-start.8 = (bf16[400,256]{1,0:T(8,128)(2,1)}, bf16[400,256]{1,0:T(8,128)(2,1)S(1)}, u32[]{:S(2)}) copy-start(bf16[400,256]{1,0:T(8,128)(2,1)S(1)} %collective-permute-done.6.refs_2_.refs_3_) | copy-start | bytes 614404
  44.6 2.7 %copy-start.31 = (s32[16]{0:T(128)S(1)}, s32[16]{0:T(128)}, u32[]{:S(2)}) copy-start(s32[16]{0:T(128)} %param.14) | copy-start | bytes 196
  44.6 2.1 copy-start.10
  44.6 2.1 copy-start.12
  44.7 0.8 copy-start.19
  46.1 0.7 copy-start.23
  46.8 12.9 %collective-permute-start.10 = (s16[1936,640]{1,0:T(8,128)(2,1)}, s16[1936,640]{1,0:T(8,128)(2,1)}, u32[]{:S(2)}, u32[]{:S(2)}) collective-permute-start(s16[1936,640]{1,0:T(8,128)(2,1)} %get-tuple-element.48.refs_0_), channel_id=1, source_target_pairs={{0,1},{1,0},{2,3},{3,2},{4,5},{5,4},{6,7},{7,6},{8,9},{9,8},{10,11... | collective-permute-start | bytes 7434248 | tf_op jit(solution)/shard_map/ppermute | solution.py:223
  46.8 7.7 %collective-permute-start.4 = (s16[1936,512]{1,0:T(8,128)(2,1)}, s16[1936,512]{1,0:T(8,128)(2,1)S(1)}, u32[]{:S(2)}, u32[]{:S(2)}) collective-permute-start(s16[1936,512]{1,0:T(8,128)(2,1)} %get-tuple-element.39), channel_id=1, source_target_pairs={{0,1},{1,0},{2,3},{3,2},{4,5},{5,4},{6,7},{7,6},{8,9},{9,8},{10,11... | collective-permute-start | bytes 5947400 | tf_op jit(solution)/shard_map/ppermute | solution.py:223
  59.1 51.2 %collective-permute-start.9 = (s16[976,512]{1,0:T(8,128)(2,1)}, s16[976,512]{1,0:T(8,128)(2,1)}, u32[]{:S(2)}, u32[]{:S(2)}) collective-permute-start(s16[976,512]{1,0:T(8,128)(2,1)} %get-tuple-element.50), channel_id=1, source_target_pairs={{0,2},{1,3},{2,0},{3,1},{4,6},{5,7},{6,4},{7,5},{8,10},{9,11},{10,... | collective-permute-start | bytes 2998280 | tf_op jit(solution)/shard_map/ppermute | solution.py:223
  59.6 7.7 %copy-start.28 = (f32[2,16,6]{2,1,0:T(8,128)S(1)}, f32[2,16,6]{2,1,0:T(8,128)}, u32[]{:S(2)}) copy-start(f32[2,16,6]{2,1,0:T(8,128)} %add_convert_fusion) | copy-start | bytes 2308
  59.6 8.4 %copy-start.32 = (s32[16]{0:T(128)S(1)}, s32[16]{0:T(128)}, u32[]{:S(2)}) copy-start(s32[16]{0:T(128)} %param.14) | copy-start | bytes 196
  59.6 8.5 %copy-start.29 = (s32[16,16]{1,0:T(8,128)S(1)}, s32[16,16]{1,0:T(8,128)}, u32[]{:S(2)}) copy-start(s32[16,16]{1,0:T(8,128)} %param.15) | copy-start | bytes 3076
  59.6 9.3 %copy-start.20 = (bf16[400,256]{1,0:T(8,128)(2,1)S(1)}, bf16[400,256]{1,0:T(8,128)(2,1)}, u32[]{:S(2)}) copy-start(bf16[400,256]{1,0:T(8,128)(2,1)} %copy-done.19) | copy-start | bytes 614404
  59.6 10.8 %copy-start.22 = (bf16[400,256]{1,0:T(8,128)(2,1)S(1)}, bf16[400,256]{1,0:T(8,128)(2,1)}, u32[]{:S(2)}) copy-start(bf16[400,256]{1,0:T(8,128)(2,1)} %copy-done.21) | copy-start | bytes 614404
  59.7 10.8 %copy-start.24 = (bf16[400,256]{1,0:T(8,128)(2,1)S(1)}, bf16[400,256]{1,0:T(8,128)(2,1)}, u32[]{:S(2)}) copy-start(bf16[400,256]{1,0:T(8,128)(2,1)} %copy-done.23) | copy-start | bytes 614404
  65.5 1.3 copy-start.1
  66.8 45.7 %collective-permute-start.15 = (s16[976,640]{1,0:T(8,128)(2,1)}, s16[976,640]{1,0:T(8,128)(2,1)S(1)}, u32[]{:S(2)}, u32[]{:S(2)}) collective-permute-start(s16[976,640]{1,0:T(8,128)(2,1)} %get-tuple-element.58), channel_id=1, source_target_pairs={{0,4},{1,5},{2,6},{3,7},{4,0},{5,1},{6,2},{7,3},{8,12},{9,13},{10,... | collective-permute-start | bytes 3747848 | tf_op jit(solution)/shard_map/ppermute | solution.py:223
  68.9 40.5 %collective-permute-start.11 = (bf16[400,256]{1,0:T(8,128)(2,1)S(1)}, bf16[400,256]{1,0:T(8,128)(2,1)S(1)}, u32[]{:S(2)}, u32[]{:S(2)}) collective-permute-start(bf16[400,256]{1,0:T(8,128)(2,1)S(1)} %copy-done.20), channel_id=1, source_target_pairs={{0,4},{1,5},{2,6},{3,7},{4,0},{5,1},{6,2},{7,3},{8,12},{9,13},{10,... | collective-permute-start | bytes 614408 | tf_op jit(solution)/shard_map/ppermute | solution.py:223
  70.5 38.9 %collective-permute-start.12 = (bf16[400,256]{1,0:T(8,128)(2,1)S(1)}, bf16[400,256]{1,0:T(8,128)(2,1)S(1)}, u32[]{:S(2)}, u32[]{:S(2)}) collective-permute-start(bf16[400,256]{1,0:T(8,128)(2,1)S(1)} %copy-done.22), channel_id=1, source_target_pairs={{0,12},{1,13},{2,14},{3,15},{4,8},{5,9},{6,10},{7,11},{8,4},{9,5},... | collective-permute-start | bytes 614408 | tf_op jit(solution)/shard_map/ppermute | solution.py:223
  70.5 39.8 %collective-permute-start.13 = (bf16[400,256]{1,0:T(8,128)(2,1)S(1)}, bf16[400,256]{1,0:T(8,128)(2,1)S(1)}, u32[]{:S(2)}, u32[]{:S(2)}) collective-permute-start(bf16[400,256]{1,0:T(8,128)(2,1)S(1)} %copy-done.24), channel_id=1, source_target_pairs={{0,14},{1,15},{2,12},{3,13},{4,10},{5,11},{6,8},{7,9},{8,6},{9,7},... | collective-permute-start | bytes 614408 | tf_op jit(solution)/shard_map/ppermute | solution.py:223
  110.3 2.3 copy-start.2
  112.4 12.4 %collective-permute-start.14 = (s16[496,512]{1,0:T(8,128)(2,1)S(1)}, s16[496,512]{1,0:T(8,128)(2,1)S(1)}, u32[]{:S(2)}, u32[]{:S(2)}) collective-permute-start(s16[496,512]{1,0:T(8,128)(2,1)S(1)} %get-tuple-element.57), channel_id=1, source_target_pairs={{0,4},{1,5},{2,6},{3,7},{4,0},{5,1},{6,2},{7,3},{8,12},{9,13},{10,... | collective-permute-start | bytes 1523720 | tf_op jit(solution)/shard_map/ppermute | solution.py:223
  112.5 2.9 %copy-start.30 = (s32[256]{0:T(256)S(1)}, s32[256]{0:T(256)}, u32[]{:S(2)}) copy-start(s32[256]{0:T(256)} %add.157) | copy-start | bytes 3076
  112.5 3.0 %copy-start.7 = (bf16[400,256]{1,0:T(8,128)(2,1)S(1)}, bf16[400,256]{1,0:T(8,128)(2,1)}, u32[]{:S(2)}) copy-start(bf16[400,256]{1,0:T(8,128)(2,1)} %copy-done.6) | copy-start | bytes 614404
  112.6 2.9 %copy-start.9 = (bf16[400,256]{1,0:T(8,128)(2,1)S(1)}, bf16[400,256]{1,0:T(8,128)(2,1)}, u32[]{:S(2)}) copy-start(bf16[400,256]{1,0:T(8,128)(2,1)} %copy-done.8) | copy-start | bytes 614404
  112.6 2.9 %copy-start.11 = (bf16[400,256]{1,0:T(8,128)(2,1)S(1)}, bf16[400,256]{1,0:T(8,128)(2,1)}, u32[]{:S(2)}) copy-start(bf16[400,256]{1,0:T(8,128)(2,1)} %copy-done.10) | copy-start | bytes 614404
  112.6 2.9 %copy-start.13 = (bf16[400,256]{1,0:T(8,128)(2,1)S(1)}, bf16[400,256]{1,0:T(8,128)(2,1)}, u32[]{:S(2)}) copy-start(bf16[400,256]{1,0:T(8,128)(2,1)} %copy-done.12) | copy-start | bytes 614404
  112.6 2.9 %copy-start.15 = (bf16[400,256]{1,0:T(8,128)(2,1)S(1)}, bf16[400,256]{1,0:T(8,128)(2,1)}, u32[]{:S(2)}) copy-start(bf16[400,256]{1,0:T(8,128)(2,1)} %copy-done.14) | copy-start | bytes 614404
  114.6 15.3 %collective-permute-start.17 = (s16[496,640]{1,0:T(8,128)(2,1)}, s16[496,640]{1,0:T(8,128)(2,1)S(1)}, u32[]{:S(2)}, u32[]{:S(2)}) collective-permute-start(s16[496,640]{1,0:T(8,128)(2,1)} %get-tuple-element.62), channel_id=1, source_target_pairs={{0,2},{1,3},{2,0},{3,1},{4,6},{5,7},{6,4},{7,5},{8,10},{9,11},{10,... | collective-permute-start | bytes 1904648 | tf_op jit(solution)/shard_map/ppermute | solution.py:223
  125.9 0.7 copy-start.16
  126.7 13.0 %collective-permute-start.16 = (s16[256,512]{1,0:T(8,128)(2,1)}, s16[256,512]{1,0:T(8,128)(2,1)}, u32[]{:S(2)}, u32[]{:S(2)}) collective-permute-start(s16[256,512]{1,0:T(8,128)(2,1)} %get-tuple-element.61), channel_id=1, source_target_pairs={{0,8},{1,9},{2,10},{3,11},{4,12},{5,13},{6,14},{7,15},{8,0},{9,1},... | collective-permute-start | bytes 786440 | tf_op jit(solution)/shard_map/ppermute | solution.py:223
  128.1 32.5 %collective-permute-start.20 = (bf16[8,400,256]{2,1,0:T(8,128)(2,1)S(1)}, bf16[8,400,256]{2,1,0:T(8,128)(2,1)}, u32[]{:S(2)}, u32[]{:S(2)}) collective-permute-start(bf16[8,400,256]{2,1,0:T(8,128)(2,1)S(1)} %pack.3.refs_0_.own), channel_id=1, source_target_pairs={{0,1},{1,0},{2,3},{3,2},{4,5},{5,4},{6,7},{7,6},{8,9},{9,8},{10,11... | collective-permute-start | bytes 4915208 | tf_op jit(solution)/shard_map/ppermute | solution.py:223
  129.9 1.0 copy-start.17
  130.9 8.8 %copy-start.18 = (f32[1,192,512]{2,1,0:T(8,128)S(1)}, f32[1,192,512]{2,1,0:T(8,128)}, u32[]{:S(2)}) copy-start(f32[1,192,512]{2,1,0:T(8,128)} %copy-done.16) | copy-start | bytes 1179652
  132.1 8.8 %copy-start.26 = (f32[1,192,640]{2,1,0:T(8,128)}, f32[1,192,640]{2,1,0:T(8,128)S(1)}, u32[]{:S(2)}) copy-start(f32[1,192,640]{2,1,0:T(8,128)S(1)} %get-tuple-element.63.refs_0_.held) | copy-start | bytes 1474564
  140.9 1.3 collective-permute-start.19
  140.9 18.2 %collective-permute-start.18 = (s16[256,640]{1,0:T(8,128)(2,1)}, s16[256,640]{1,0:T(8,128)(2,1)S(1)}, u32[]{:S(2)}, u32[]{:S(2)}) collective-permute-start(s16[256,640]{1,0:T(8,128)(2,1)} %get-tuple-element.65), channel_id=1, source_target_pairs={{0,8},{1,9},{2,10},{3,11},{4,12},{5,13},{6,14},{7,15},{8,0},{9,1},... | collective-permute-start | bytes 983048 | tf_op jit(solution)/shard_map/ppermute | solution.py:223
  159.1 1.0 copy-start.27
  160.4 1.7 copy-start.25
  170.5 26.2 %copy-start.4 = (bf16[2,96,1024]{2,1,0:T(8,128)(2,1)S(1)}, bf16[2,96,1024]{2,1,0:T(8,128)(2,1)}, u32[]{:S(2)}) copy-start(bf16[2,96,1024]{2,1,0:T(8,128)(2,1)} %param.8) | copy-start | bytes 1179652
  170.6 17.4 %collective-permute-start.21 = (bf16[192,1024]{1,0:T(8,128)(2,1)S(1)}, bf16[192,1024]{1,0:T(8,128)(2,1)}, u32[]{:S(2)}, u32[]{:S(2)}) collective-permute-start(bf16[192,1024]{1,0:T(8,128)(2,1)S(1)} %bitcast.50), channel_id=1, source_target_pairs={{0,4},{1,5},{2,6},{3,7},{4,0},{5,1},{6,2},{7,3},{8,12},{9,13},{10,... | collective-permute-start | bytes 1179656 | tf_op jit(solution)/shard_map/ppermute | solution.py:223
  170.7 17.4 %collective-permute-start.22 = (bf16[192,1024]{1,0:T(8,128)(2,1)S(1)}, bf16[192,1024]{1,0:T(8,128)(2,1)S(1)}, u32[]{:S(2)}, u32[]{:S(2)}) collective-permute-start(bf16[192,1024]{1,0:T(8,128)(2,1)S(1)} %bitcast.51), channel_id=1, source_target_pairs={{0,2},{1,3},{2,0},{3,1},{4,6},{5,7},{6,4},{7,5},{8,10},{9,11},{10,... | collective-permute-start | bytes 1179656 | tf_op jit(solution)/shard_map/ppermute | solution.py:223
  171.1 16.9 %collective-permute-start.23 = (bf16[192,1024]{1,0:T(8,128)(2,1)S(1)}, bf16[192,1024]{1,0:T(8,128)(2,1)S(1)}, u32[]{:S(2)}, u32[]{:S(2)}) collective-permute-start(bf16[192,1024]{1,0:T(8,128)(2,1)S(1)} %bitcast.52), channel_id=1, source_target_pairs={{0,1},{1,0},{2,3},{3,2},{4,5},{5,4},{6,7},{7,6},{8,9},{9,8},{10,11... | collective-permute-start | bytes 1179656 | tf_op jit(solution)/shard_map/ppermute | solution.py:223
  171.2 21.0 %collective-permute-start.26 = (bf16[192,1024]{1,0:T(8,128)(2,1)S(1)}, bf16[192,1024]{1,0:T(8,128)(2,1)}, u32[]{:S(2)}, u32[]{:S(2)}) collective-permute-start(bf16[192,1024]{1,0:T(8,128)(2,1)S(1)} %bitcast.53), channel_id=1, source_target_pairs={{0,8},{1,9},{2,10},{3,11},{4,12},{5,13},{6,14},{7,15},{8,0},{9,1},... | collective-permute-start | bytes 1179656 | tf_op jit(solution)/shard_map/ppermute | solution.py:223
  193.2 11.9 %collective-permute-start.28 = (bf16[2,192,1024]{2,1,0:T(8,128)(2,1)S(1)}, bf16[2,192,1024]{2,1,0:T(8,128)(2,1)S(1)}, u32[]{:S(2)}, u32[]{:S(2)}) collective-permute-start(bf16[2,192,1024]{2,1,0:T(8,128)(2,1)S(1)} %pack.4.refs_0_), channel_id=1, source_target_pairs={{0,1},{1,0},{2,3},{3,2},{4,5},{5,4},{6,7},{7,6},{8,9},{9,8},{10,11... | collective-permute-start | bytes 2359304 | tf_op jit(solution)/shard_map/ppermute | solution.py:223
  193.3 11.8 %collective-permute-start.27 = (bf16[192,1024]{1,0:T(8,128)(2,1)}, bf16[192,1024]{1,0:T(8,128)(2,1)}, u32[]{:S(2)}, u32[]{:S(2)}) collective-permute-start(bf16[192,1024]{1,0:T(8,128)(2,1)} %get-tuple-element.68.refs_0_), channel_id=1, source_target_pairs={{0,2},{1,3},{2,0},{3,1},{4,6},{5,7},{6,4},{7,5},{8,10},{9,11},{10,... | collective-permute-start | bytes 1179656 | tf_op jit(solution)/shard_map/ppermute | solution.py:223
  195.1 16.8 %collective-permute-start.24 = (bf16[192,1024]{1,0:T(8,128)(2,1)S(1)}, bf16[192,1024]{1,0:T(8,128)(2,1)}, u32[]{:S(2)}, u32[]{:S(2)}) collective-permute-start(bf16[192,1024]{1,0:T(8,128)(2,1)S(1)} %get-tuple-element.67.refs_0_), channel_id=1, source_target_pairs={{0,12},{1,13},{2,14},{3,15},{4,8},{5,9},{6,10},{7,11},{8,4},{9,5},... | collective-permute-start | bytes 1179656 | tf_op jit(solution)/shard_map/ppermute | solution.py:223
  205.1 11.0 %collective-permute-start.29 = (bf16[192,1024]{1,0:T(8,128)(2,1)}, bf16[192,1024]{1,0:T(8,128)(2,1)}, u32[]{:S(2)}, u32[]{:S(2)}) collective-permute-start(bf16[192,1024]{1,0:T(8,128)(2,1)} %together.6.refs_0_), channel_id=1, source_target_pairs={{0,2},{1,3},{2,0},{3,1},{4,6},{5,7},{6,4},{7,5},{8,10},{9,11},{10,... | collective-permute-start | bytes 1179656 | tf_op jit(solution)/shard_map/ppermute | solution.py:223
  217.6 3.6 %collective-permute-start.30 = (bf16[4,192,1024]{2,1,0:T(8,128)(2,1)S(1)}, bf16[4,192,1024]{2,1,0:T(8,128)(2,1)}, u32[]{:S(2)}, u32[]{:S(2)}) collective-permute-start(bf16[4,192,1024]{2,1,0:T(8,128)(2,1)S(1)} %pack.5.refs_0_), channel_id=1, source_target_pairs={{0,1},{1,0},{2,3},{3,2},{4,5},{5,4},{6,7},{7,6},{8,9},{9,8},{10,11... | collective-permute-start | bytes 4718600 | tf_op jit(solution)/shard_map/ppermute | solution.py:223
  217.7 12.7 %collective-permute-start.25 = (bf16[192,1024]{1,0:T(8,128)(2,1)}, bf16[192,1024]{1,0:T(8,128)(2,1)S(1)}, u32[]{:S(2)}, u32[]{:S(2)}) collective-permute-start(bf16[192,1024]{1,0:T(8,128)(2,1)} %collective-permute-done.24.refs_3_), channel_id=1, source_target_pairs={{0,2},{1,3},{2,0},{3,1},{4,6},{5,7},{6,4},{7,5},{8,10},{9,11},{10,... | collective-permute-start | bytes 1179656 | tf_op jit(solution)/shard_map/ppermute | solution.py:223
  230.4 1.8 collective-permute-start.31
  (1 other events, 0.7 us)

commit v10 on v9

--- a/solution.py
+++ b/solution.py
@@ -557,22 +557,19 @@
     across = swap(attention, 2)
     far = swap(attention, 8)
     partner = swap(attention, 1)
-    near, attention = together([near, attention], [across, partner])
-
-    across_near = swap(near, 2)
+    first, onward = pack([near, across, far], [(0, 1, 2), (0, 2)], [partner])
+    (attention,) = together([attention], [onward])
+
+    across_onward = swap(onward, 2)
     farthest = swap(attention, 12)
-    (first,) = pack([near, across], [(0, 1)], [])
     first_partner = swap(first, 1)
     mixed = add(start, [attention, partner], (0, 1))
-    (far,) = together([far], [across_near, first_partner, mixed])
-
-    across_far = swap(far, 2)
-    mixed = add(mixed, [first, first_partner], (4, 2, 5, 3))
-    (second,) = pack([far, across_near, across_far, farthest], [(0, 1, 2, 3)], [mixed])
+    mixed = add(mixed, [first, first_partner], (4, 2, 8, 5, 3, 9))
+    (second,) = pack([across_onward, farthest], [(0, 1, 2)], [mixed])
 
     last = swap(farthest, 2)
     second_partner = swap(second, 1)
-    mixed = add(mixed, [second, second_partner], (8, 6, 10, 12, 9, 7, 11, 13))
+    mixed = add(mixed, [second, second_partner], (6, 10, 12, 7, 11, 13))
     (last,) = together([last], [mixed])
 
     last_partner = swap(last, 1)
@@ -791,10 +788,10 @@
     line_a = swap(sent_a, 2)
     for k in (2, 6, 7):
         handed(k)
-    held_b, sent_b = folded(held_b, 2, core_b, 2, held_a)
+    late = [cache_pieces[k] for k in (2, 6, 7)]
+    held_b, sent_b = folded(held_b, 2, core_b, 2, held_a, *late)
     line_b = swap(sent_b, 4)
-    late = [cache_pieces[k] for k in (2, 6, 7)]
-    held_a, sent_a = folded(held_a, 2, line_a, 1, held_b, *late)
+    held_a, sent_a = folded(held_a, 2, line_a, 1, held_b)
     line_a = swap(sent_a, 4)
     held_b, sent_b = folded(held_b, 1, line_b, 1, held_a)
     line_b = swap(sent_b, 2)

time: 237 us -> 220 us (0.928)
  waiting for transfers between devices: 112 us -> 86.1 us
  starting transfers between devices: 34.5 us -> 40.8 us
  other arithmetic: 4.8 us -> 7.3 us
    ppermute x32 -> x31, waiting for transfers between devices: 112 us -> 86.1 us  [swap(): return lax.ppermute(value, 'tensor', [(i, i ^ bit) for i in range(devices)])]
    ppermute x32 -> x31, starting transfers between devices: 34.5 us -> 40.8 us  [swap(): return lax.ppermute(value, 'tensor', [(i, i ^ bit) for i in range(devices)])]
    unnamed x68 -> x58, local copies, waits for them, and re-layouts: 9.41 us -> 5.89 us
  transfers between devices with their start and end apart: 32 -> 31, of which waited for: 17 -> 19; matrix products, arithmetic and copies ran while one was open for 2% -> 4% of each run, Pallas kernels for 24% -> 27%
where the time goes in v10:
time: 220 us; the launch traced here: 219 us
  waiting for transfers between devices  86.1 us (39%)
  Pallas kernels  73.3 us (33%)
  starting transfers between devices  40.8 us (19%)
  local copies, waits for them, and re-layouts  10.6 us (5%)
  other arithmetic  7.3 us (3%)
    ppermute x31, waiting for transfers between devices, swap(): return lax.ppermute(value, 'tensor', [(i, i ^ bit) for i in range(devices)])  86.1 us
    ppermute x31, starting transfers between devices, swap(): return lax.ppermute(value, 'tensor', [(i, i ^ bit) for i in range(devices)])  40.8 us
    pallas_call x4, Pallas kernels, mix(): pl.pallas_call(functools.partial(mix_kernel, len(pieces)), in_specs=[pl.B...  21.5 us
    pallas_call x2, Pallas kernels, project(): pl.pallas_call(functools.partial(project_kernel, part), grid_spec=pltpu.P...  20.6 us
    pallas_call x6, Pallas kernels, fold(): pl.pallas_call(functools.partial(fold_kernel, steps, low), grid_spec=pltp...  19 us
    pallas_call x1, Pallas kernels, attend(): pl.pallas_call(attend_kernel, in_specs=[pl.BlockSpec(memory_space=pltpu.S...  8.35 us
    unnamed x58, local copies, waits for them, and re-layouts  5.89 us
  transfers between devices with their start and end apart: 31, of which 19 were waited for; matrix products, arithmetic and copies ran while one was open for 4% of the time, Pallas kernels for 27%

profile of v10, /device:TPU:0, one launch (start us, length us, event | category | flops | bytes accessed | tf_op | source)
XLA Modules:
  0.0 218.9 jit_solution(13891958922937261264)
XLA Ops:
  0.0 1.2 fusion
  1.2 3.0 %collective-permute-start = (f32[2,96]{1,0:T(2,128)S(1)}, f32[2,96]{1,0:T(2,128)S(1)}, u32[]{:S(2)}, u32[]{:S(2)}) collective-permute-start(f32[2,96]{1,0:T(2,128)S(1)} %fusion), channel_id=1, source_target_pairs={{0,2},{1,3},{2,0},{3,1},{4,6},{5,7},{6,4},{7,5},{8,10},{9,11},{10,... | collective-permute-start | bytes 2312 | tf_op jit(solution)/shard_map/ppermute | solution.py:223
  4.3 1.5 collective-permute-done
  5.8 1.1 collective-permute-done.1
  7.0 2.1 collective-permute-start.2
  9.0 0.8 reshape.240
  9.8 0.7 convert_element_type.29
  10.6 3.0 %collective-permute-start.3 = (f32[2,96]{1,0:T(2,128)S(1)}, f32[2,96]{1,0:T(2,128)S(1)}, u32[]{:S(2)}, u32[]{:S(2)}) collective-permute-start(f32[2,96]{1,0:T(2,128)S(1)} %add.139), channel_id=1, source_target_pairs={{0,8},{1,9},{2,10},{3,11},{4,12},{5,13},{6,14},{7,15},{8,0},{9,1},... | collective-permute-start | bytes 2312 | tf_op jit(solution)/shard_map/ppermute | solution.py:223
  13.6 1.4 copy-done.3
  15.0 0.9 arrange.1
  15.9 1.5 collective-permute-start.5
  17.4 1.5 collective-permute-start.6
  19.3 3.5 %collective-permute-start.8 = (bf16[400,256]{1,0:T(8,128)(2,1)S(1)}, bf16[400,256]{1,0:T(8,128)(2,1)S(1)}, u32[]{:S(2)}, u32[]{:S(2)}) collective-permute-start(bf16[400,256]{1,0:T(8,128)(2,1)S(1)} %get-tuple-element.47), channel_id=1, source_target_pairs={{0,10},{1,11},{2,8},{3,9},{4,14},{5,15},{6,12},{7,13},{8,2},{9,3},... | collective-permute-start | bytes 614408 | tf_op jit(solution)/shard_map/ppermute | solution.py:223
  23.0 9.1 %project.2 = (f32[8,192,512]{2,1,0:T(8,128)S(1)}, s16[1936,512]{1,0:T(8,128)(2,1)}) custom-call(s32[1]{0:T(128)} %bitcast.2.core, bf16[192,1024]{1,0:T(8,128)(2,1)S(1)} %bitcast.47, bf16[1024,18432]{1,0:T(8,128)(2,1)} %weights.3, bf16[400,256]{1,0:T(8,128)(2,1)S(1)} %get-tuple-element.37.refs_0_), custom_call_target="tpu_custom_call" | custom-call | flops 1 | bytes 1 | tf_op jit(solution)/shard_map/project/pallas_call | solution.py:353
  32.2 1.6 copy-done
  33.8 11.4 %project.3 = (f32[8,192,640]{2,1,0:T(8,128)}, s16[1936,640]{1,0:T(8,128)(2,1)}) custom-call(s32[1]{0:T(128)} %bitcast.2.core, bf16[192,1024]{1,0:T(8,128)(2,1)S(1)} %bitcast.48, bf16[1024,18432]{1,0:T(8,128)(2,1)} %weights.3, f32[8,192,512]{2,1,0:T(8,128)} %copy-done, bf16[400,256]{1,0:T(8,128)(2,1)S(1)} %collective-permute-done.5.refs_1_, ...), custom_call_target="tpu_custom_call" | custom-call | flops 1 | bytes 1 | tf_op jit(solution)/shard_map/project/pallas_call | solution.py:353
  47.2 1.3 collective-permute-start.12
  48.5 2.4 %collective-permute-start.13 = (bf16[400,256]{1,0:T(8,128)(2,1)}, bf16[400,256]{1,0:T(8,128)(2,1)S(1)}, u32[]{:S(2)}, u32[]{:S(2)}) collective-permute-start(bf16[400,256]{1,0:T(8,128)(2,1)} %get-tuple-element.54), channel_id=1, source_target_pairs={{0,14},{1,15},{2,12},{3,13},{4,10},{5,11},{6,8},{7,9},{8,6},{9,7},... | collective-permute-start | bytes 614408 | tf_op jit(solution)/shard_map/ppermute | solution.py:223
  50.9 0.7 add_convert_fusion
  51.6 1.9 collective-permute-done.4.landed.landed_out.landed_powers
  53.5 4.6 %fold.6 = (f32[4,192,512]{2,1,0:T(8,128)S(1)}, s16[976,512]{1,0:T(8,128)(2,1)}) custom-call(s32[1]{0:T(128)} %bitcast.5.bit, f32[8,192,512]{2,1,0:T(8,128)} %copy-done, f32[8,192,512]{2,1,0:T(8,128)} %copy-done, s16[1936,512]{1,0:T(8,128)(2,1)S(1)} %collective-permute-done.4.landed.landed_out.landed_powers, ...), custom_call_target="tpu_custom_call" | custom-call | flops 1 | bytes 1 | tf_op jit(solution)/shard_map/fold/pallas_call | solution.py:407
  58.7 4.0 %collective-permute-done.11.refs_1_.refs_2_ = bf16[400,256]{1,0:T(8,128)(2,1)S(1)} collective-permute-done((bf16[400,256]{1,0:T(8,128)(2,1)}, bf16[400,256]{1,0:T(8,128)(2,1)S(1)}, u32[]{:S(2)}, u32[]{:S(2)}) %collective-permute-start.11) | collective-permute-done | bytes 204832 | tf_op jit(solution)/shard_map/ppermute | solution.py:223
  62.7 5.9 %fold.7 = (f32[4,192,640]{2,1,0:T(8,128)S(1)}, s16[976,640]{1,0:T(8,128)(2,1)}) custom-call(s32[1]{0:T(128)} %bitcast.4.bit, f32[8,192,640]{2,1,0:T(8,128)} %get-tuple-element.51.held.held_out, f32[8,192,640]{2,1,0:T(8,128)} %get-tuple-element.51.held.held_out, s16[1936,640]{1,0:T(8,128)(2,1)} %collective-permute-done.10.landed.landed_out.landed_powers, ...), custom_call_target="tpu_custom_call" | custom-call | flops 1 | bytes 1 | tf_op jit(solution)/shard_map/fold/pallas_call | solution.py:407
  68.6 6.1 %collective-permute-start.15 = (s16[976,640]{1,0:T(8,128)(2,1)}, s16[976,640]{1,0:T(8,128)(2,1)}, u32[]{:S(2)}, u32[]{:S(2)}) collective-permute-start(s16[976,640]{1,0:T(8,128)(2,1)} %get-tuple-element.58), channel_id=1, source_target_pairs={{0,4},{1,5},{2,6},{3,7},{4,0},{5,1},{6,2},{7,3},{8,12},{9,13},{10,... | collective-permute-start | bytes 3747848 | tf_op jit(solution)/shard_map/ppermute | solution.py:223
  74.7 0.7 iota_add_fusion
  75.4 0.7 convert_element_type.32
  76.1 1.4 add.157
  77.4 0.7 and_select_fusion.1
  78.2 1.4 select_reduce_fusion.1
  79.6 1.1 fusion.5
  80.7 3.4 %collective-permute-done.9.landed.landed_out.landed_powers = s16[976,512]{1,0:T(8,128)(2,1)} collective-permute-done((s16[976,512]{1,0:T(8,128)(2,1)}, s16[976,512]{1,0:T(8,128)(2,1)}, u32[]{:S(2)}, u32[]{:S(2)}) %collective-permute-start.9) | collective-permute-done | bytes 999456 | tf_op jit(solution)/shard_map/ppermute | solution.py:223
  84.1 2.0 fold.8
  86.1 3.7 %collective-permute-start.14 = (s16[496,512]{1,0:T(8,128)(2,1)S(1)}, s16[496,512]{1,0:T(8,128)(2,1)S(1)}, u32[]{:S(2)}, u32[]{:S(2)}) collective-permute-start(s16[496,512]{1,0:T(8,128)(2,1)S(1)} %get-tuple-element.57), channel_id=1, source_target_pairs={{0,4},{1,5},{2,6},{3,7},{4,0},{5,1},{6,2},{7,3},{8,12},{9,13},{10,... | collective-permute-start | bytes 1523720 | tf_op jit(solution)/shard_map/ppermute | solution.py:223
  89.7 13.7 %collective-permute-done.15.landed.landed_out.landed_powers = s16[976,640]{1,0:T(8,128)(2,1)} collective-permute-done((s16[976,640]{1,0:T(8,128)(2,1)}, s16[976,640]{1,0:T(8,128)(2,1)}, u32[]{:S(2)}, u32[]{:S(2)}) %collective-permute-start.15) | collective-permute-done | bytes 1249312 | tf_op jit(solution)/shard_map/ppermute | solution.py:223
  103.5 3.2 %fold.9 = (f32[2,192,640]{2,1,0:T(8,128)S(1)}, s16[496,640]{1,0:T(8,128)(2,1)}) custom-call(s32[1]{0:T(128)} %bitcast.5.bit, f32[4,192,640]{2,1,0:T(8,128)S(1)} %get-tuple-element.55.refs_0_.held.held_out, f32[4,192,640]{2,1,0:T(8,128)S(1)} %get-tuple-element.55.refs_0_.held.held_out, ...), custom_call_target="tpu_custom_call" | custom-call | flops 1 | bytes 1 | tf_op jit(solution)/shard_map/fold/pallas_call | solution.py:407
  106.6 1.5 collective-permute-start.17
  108.6 3.6 %collective-permute-done.14.landed.landed_out.landed_powers = s16[496,512]{1,0:T(8,128)(2,1)S(1)} collective-permute-done((s16[496,512]{1,0:T(8,128)(2,1)S(1)}, s16[496,512]{1,0:T(8,128)(2,1)S(1)}, u32[]{:S(2)}, u32[]{:S(2)}) %collective-permute-start.14) | collective-permute-done | bytes 507936 | tf_op jit(solution)/shard_map/ppermute | solution.py:223
  112.2 1.1 fold.10
  113.3 1.8 collective-permute-start.16
  115.3 4.0 %collective-permute-done.17.landed.landed_out.landed_powers = s16[496,640]{1,0:T(8,128)(2,1)} collective-permute-done((s16[496,640]{1,0:T(8,128)(2,1)}, s16[496,640]{1,0:T(8,128)(2,1)}, u32[]{:S(2)}, u32[]{:S(2)}) %collective-permute-start.17) | collective-permute-done | bytes 634912 | tf_op jit(solution)/shard_map/ppermute | solution.py:223
  119.3 2.2 %fold.11 = (f32[1,192,640]{2,1,0:T(8,128)S(1)}, s16[256,640]{1,0:T(8,128)(2,1)}) custom-call(s32[1]{0:T(128)} %bitcast.3.bit, f32[2,192,640]{2,1,0:T(8,128)S(1)} %get-tuple-element.59.refs_8_.held.held_out, f32[2,192,640]{2,1,0:T(8,128)S(1)} %get-tuple-element.59.refs_8_.held.held_out, ...), custom_call_target="tpu_custom_call" | custom-call | flops 1 | bytes 1 | tf_op jit(solution)/shard_map/fold/pallas_call | solution.py:407
  121.6 4.9 %collective-permute-done.16.landed = s16[256,512]{1,0:T(8,128)(2,1)} collective-permute-done((s16[256,512]{1,0:T(8,128)(2,1)}, s16[256,512]{1,0:T(8,128)(2,1)}, u32[]{:S(2)}, u32[]{:S(2)}) %collective-permute-start.16) | collective-permute-done | bytes 262176 | tf_op jit(solution)/shard_map/ppermute | solution.py:223
  126.5 1.2 finish.2
  128.0 1.0 collective-permute-done.19
  129.2 16.1 %collective-permute-done.18.landed = s16[256,640]{1,0:T(8,128)(2,1)S(1)} collective-permute-done((s16[256,640]{1,0:T(8,128)(2,1)}, s16[256,640]{1,0:T(8,128)(2,1)S(1)}, u32[]{:S(2)}, u32[]{:S(2)}) %collective-permute-start.18) | collective-permute-done | bytes 327712 | tf_op jit(solution)/shard_map/ppermute | solution.py:223
  145.3 0.9 copy-done.21
  146.2 1.0 copy-done.24
  147.7 0.7 slice_reduce_fusion
  149.2 8.4 %attend.1 = bf16[16,96,128]{2,1,0:T(8,128)(2,1)S(1)} custom-call(s32[24]{0:T(128)S(1)} %copy-done.22, bf16[16,96,128]{2,1,0:T(8,128)(2,1)S(1)} %bitcast.55, bf16[16,16,128]{2,1,0:T(8,128)(2,1)S(1)} %pad.12.new_keys, bf16[16,16,128]{2,1,0:T(8,128)(2,1)S(1)} %pad.13.new_values, bf16[8,400,256]{2,1,0:T(8,128)(2,1)S(1)} %pack.3.refs_0_.own, ...), custom_call_target="tpu_custom_call" | custom-call | flops 1 | bytes 1 | tf_op jit(solution)/shard_map/attend/pallas_call | solution.py:662
  157.8 1.6 collective-permute-start.22
  159.3 2.4 %collective-permute-start.23 = (bf16[192,1024]{1,0:T(8,128)(2,1)S(1)}, bf16[192,1024]{1,0:T(8,128)(2,1)S(1)}, u32[]{:S(2)}, u32[]{:S(2)}) collective-permute-start(bf16[192,1024]{1,0:T(8,128)(2,1)S(1)} %bitcast.52), channel_id=1, source_target_pairs={{0,8},{1,9},{2,10},{3,11},{4,12},{5,13},{6,14},{7,15},{8,0},{9,1},... | collective-permute-start | bytes 1179656 | tf_op jit(solution)/shard_map/ppermute | solution.py:223
  161.7 13.5 %collective-permute-done.21.refs_0_ = bf16[192,1024]{1,0:T(8,128)(2,1)S(1)} collective-permute-done((bf16[192,1024]{1,0:T(8,128)(2,1)S(1)}, bf16[192,1024]{1,0:T(8,128)(2,1)S(1)}, u32[]{:S(2)}, u32[]{:S(2)}) %collective-permute-start.21) | collective-permute-done | bytes 393248 | tf_op jit(solution)/shard_map/ppermute | solution.py:223
  175.3 4.3 %collective-permute-done.23.refs_2_ = bf16[192,1024]{1,0:T(8,128)(2,1)S(1)} collective-permute-done((bf16[192,1024]{1,0:T(8,128)(2,1)S(1)}, bf16[192,1024]{1,0:T(8,128)(2,1)S(1)}, u32[]{:S(2)}, u32[]{:S(2)}) %collective-permute-start.23) | collective-permute-done | bytes 393248 | tf_op jit(solution)/shard_map/ppermute | solution.py:223
  180.3 1.9 collective-permute-start.25
  182.4 3.4 %mix.4.refs_3_ = f32[192,1024]{1,0:T(8,128)S(1)} custom-call(s32[2]{0:T(128)S(1)} %pad_add_fusion.1.places, bf16[192,1024]{1,0:T(8,128)(2,1)S(1)} %together.4.refs_0_, bf16[192,1024]{1,0:T(8,128)(2,1)S(1)} %collective-permute-done.24.refs_3_.refs_1_, bf16[16384,1024]{1,0:T(8,128)(2,1)} %refs_2_.7, bf16[192,1024]{1,0:T(8,128)(2,1)S(1)} %bitcast.49), custom_call_target="tpu_custom_call" | custom-call | flops 1 | bytes 1 | tf_op jit(solution)/shard_map/mix/pallas_call | solution.py:510
  185.8 7.0 %mix.5.refs_2_.refs_3_ = f32[192,1024]{1,0:T(8,128)S(1)} custom-call(s32[6]{0:T(128)S(1)} %stack.82.places, bf16[3,192,1024]{2,1,0:T(8,128)(2,1)S(1)} %get-tuple-element.68.refs_0_, bf16[3,192,1024]{2,1,0:T(8,128)(2,1)} %collective-permute-done.28.refs_1_, bf16[16384,1024]{1,0:T(8,128)(2,1)} %refs_2_.7, f32[192,1024]{1,0:T(8,128)S(1)} %mix.4.refs_3_), custom_call_target="tpu_custom_call" | custom-call | flops 1 | bytes 1 | tf_op jit(solution)/shard_map/mix/pallas_call | solution.py:510
  192.8 0.8 collective-permute-done.25.refs_1_
  193.5 6.3 %collective-permute-done.27.refs_0_ = bf16[2,192,1024]{2,1,0:T(8,128)(2,1)} collective-permute-done((bf16[2,192,1024]{2,1,0:T(8,128)(2,1)S(1)}, bf16[2,192,1024]{2,1,0:T(8,128)(2,1)}, u32[]{:S(2)}, u32[]{:S(2)}) %collective-permute-start.27) | collective-permute-done | bytes 786464 | tf_op jit(solution)/shard_map/ppermute | solution.py:223
  199.8 1.3 pack.5.refs_0_
  201.9 2.3 %collective-permute-done.29.refs_1_ = bf16[3,192,1024]{2,1,0:T(8,128)(2,1)} collective-permute-done((bf16[3,192,1024]{2,1,0:T(8,128)(2,1)S(1)}, bf16[3,192,1024]{2,1,0:T(8,128)(2,1)}, u32[]{:S(2)}, u32[]{:S(2)}) %collective-permute-start.29) | collective-permute-done | bytes 1179680 | tf_op jit(solution)/shard_map/ppermute | solution.py:223
  204.2 7.0 %mix.6.refs_1_.refs_3_ = f32[192,1024]{1,0:T(8,128)S(1)} custom-call(s32[6]{0:T(128)S(1)} %stack.75.places, bf16[3,192,1024]{2,1,0:T(8,128)(2,1)S(1)} %pack.5.refs_0_, bf16[3,192,1024]{2,1,0:T(8,128)(2,1)} %collective-permute-done.29.refs_1_, bf16[16384,1024]{1,0:T(8,128)(2,1)} %refs_2_.7, f32[192,1024]{1,0:T(8,128)S(1)} %mix.5.refs_2_.refs_3_), custom_call_target="tpu_custom_call" | custom-call | flops 1 | bytes 1 | tf_op jit(solution)/shard_map/mix/pallas_call | solution.py:510
  211.2 1.8 collective-permute-done.26.refs_0_
  213.0 1.6 collective-permute-done.30.refs_1_
  214.7 4.1 %mix.7 = bf16[192,1024]{1,0:T(8,128)(2,1)} custom-call(s32[2]{0:T(128)S(1)} %pad_add_fusion.places, bf16[192,1024]{1,0:T(8,128)(2,1)S(1)} %together.5.refs_0_, bf16[192,1024]{1,0:T(8,128)(2,1)S(1)} %collective-permute-done.30.refs_1_, bf16[16384,1024]{1,0:T(8,128)(2,1)} %refs_2_.7, f32[192,1024]{1,0:T(8,128)S(1)} %mix.6.refs_1_.refs_3_), custom_call_target="tpu_custom_call" | custom-call | flops 1 | bytes 1 | tf_op jit(solution)/shard_map/mix/pallas_call | solution.py:510
  (133 shorter events, 7.0 us)
Async XLA Ops:
  0.0 22.9 %copy-start.1 = (bf16[2,96,1024]{2,1,0:T(8,128)(2,1)S(1)}, bf16[2,96,1024]{2,1,0:T(8,128)(2,1)}, u32[]{:S(2)}) copy-start(bf16[2,96,1024]{2,1,0:T(8,128)(2,1)} %param.8) | copy-start | bytes 1179652
  1.2 4.6 %collective-permute-start = (f32[2,96]{1,0:T(2,128)S(1)}, f32[2,96]{1,0:T(2,128)S(1)}, u32[]{:S(2)}, u32[]{:S(2)}) collective-permute-start(f32[2,96]{1,0:T(2,128)S(1)} %fusion), channel_id=1, source_target_pairs={{0,2},{1,3},{2,0},{3,1},{4,6},{5,7},{6,4},{7,5},{8,10},{9,11},{10,... | collective-permute-start | bytes 2312 | tf_op jit(solution)/shard_map/ppermute | solution.py:223
  5.8 1.1 collective-permute-start.1
  7.0 3.6 %collective-permute-start.2 = (f32[2,96]{1,0:T(2,128)S(1)}, f32[2,96]{1,0:T(2,128)S(1)}, u32[]{:S(2)}, u32[]{:S(2)}) collective-permute-start(f32[2,96]{1,0:T(2,128)S(1)} %add.138), channel_id=1, source_target_pairs={{0,4},{1,5},{2,6},{3,7},{4,0},{5,1},{6,2},{7,3},{8,12},{9,13},{10,... | collective-permute-start | bytes 2312 | tf_op jit(solution)/shard_map/ppermute | solution.py:223
  10.6 12.3 %collective-permute-start.3 = (f32[2,96]{1,0:T(2,128)S(1)}, f32[2,96]{1,0:T(2,128)S(1)}, u32[]{:S(2)}, u32[]{:S(2)}) collective-permute-start(f32[2,96]{1,0:T(2,128)S(1)} %add.139), channel_id=1, source_target_pairs={{0,8},{1,9},{2,10},{3,11},{4,12},{5,13},{6,14},{7,15},{8,0},{9,1},... | collective-permute-start | bytes 2312 | tf_op jit(solution)/shard_map/ppermute | solution.py:223
  13.6 1.4 copy-start.3
  15.9 16.2 %copy-start.18 = (bf16[400,256]{1,0:T(8,128)(2,1)}, bf16[400,256]{1,0:T(8,128)(2,1)S(1)}, u32[]{:S(2)}) copy-start(bf16[400,256]{1,0:T(8,128)(2,1)S(1)} %get-tuple-element.37.refs_0_) | copy-start | bytes 614404
  15.9 17.9 %collective-permute-start.5 = (bf16[400,256]{1,0:T(8,128)(2,1)S(1)}, bf16[400,256]{1,0:T(8,128)(2,1)S(1)}, u32[]{:S(2)}, u32[]{:S(2)}) collective-permute-start(bf16[400,256]{1,0:T(8,128)(2,1)S(1)} %get-tuple-element.40), channel_id=1, source_target_pairs={{0,2},{1,3},{2,0},{3,1},{4,6},{5,7},{6,4},{7,5},{8,10},{9,11},{10,... | collective-permute-start | bytes 614408 | tf_op jit(solution)/shard_map/ppermute | solution.py:223
  17.4 16.4 %collective-permute-start.6 = (bf16[400,256]{1,0:T(8,128)(2,1)S(1)}, bf16[400,256]{1,0:T(8,128)(2,1)S(1)}, u32[]{:S(2)}, u32[]{:S(2)}) collective-permute-start(bf16[400,256]{1,0:T(8,128)(2,1)S(1)} %get-tuple-element.41), channel_id=1, source_target_pairs={{0,6},{1,7},{2,4},{3,5},{4,2},{5,3},{6,0},{7,1},{8,14},{9,15},{10,... | collective-permute-start | bytes 614408 | tf_op jit(solution)/shard_map/ppermute | solution.py:223
  19.0 26.4 %collective-permute-start.7 = (bf16[400,256]{1,0:T(8,128)(2,1)S(1)}, bf16[400,256]{1,0:T(8,128)(2,1)S(1)}, u32[]{:S(2)}, u32[]{:S(2)}) collective-permute-start(bf16[400,256]{1,0:T(8,128)(2,1)S(1)} %get-tuple-element.46), channel_id=1, source_target_pairs={{0,8},{1,9},{2,10},{3,11},{4,12},{5,13},{6,14},{7,15},{8,0},{9,1},... | collective-permute-start | bytes 614408 | tf_op jit(solution)/shard_map/ppermute | solution.py:223
  19.3 26.0 %collective-permute-start.8 = (bf16[400,256]{1,0:T(8,128)(2,1)S(1)}, bf16[400,256]{1,0:T(8,128)(2,1)S(1)}, u32[]{:S(2)}, u32[]{:S(2)}) collective-permute-start(bf16[400,256]{1,0:T(8,128)(2,1)S(1)} %get-tuple-element.47), channel_id=1, source_target_pairs={{0,10},{1,11},{2,8},{3,9},{4,14},{5,15},{6,12},{7,13},{8,2},{9,3},... | collective-permute-start | bytes 614408 | tf_op jit(solution)/shard_map/ppermute | solution.py:223
  32.2 1.6 copy-start
  33.8 11.5 %copy-start.4 = (bf16[400,256]{1,0:T(8,128)(2,1)}, bf16[400,256]{1,0:T(8,128)(2,1)S(1)}, u32[]{:S(2)}) copy-start(bf16[400,256]{1,0:T(8,128)(2,1)S(1)} %collective-permute-done.5.refs_1_) | copy-start | bytes 614404
  33.8 11.5 %copy-start.6 = (bf16[400,256]{1,0:T(8,128)(2,1)}, bf16[400,256]{1,0:T(8,128)(2,1)S(1)}, u32[]{:S(2)}) copy-start(bf16[400,256]{1,0:T(8,128)(2,1)S(1)} %collective-permute-done.6.refs_2_.refs_3_) | copy-start | bytes 614404
  45.3 0.7 copy-start.14
  45.4 0.7 copy-start.16
  45.4 1.3 copy-start.27
  46.1 16.6 %collective-permute-start.10 = (s16[1936,640]{1,0:T(8,128)(2,1)}, s16[1936,640]{1,0:T(8,128)(2,1)}, u32[]{:S(2)}, u32[]{:S(2)}) collective-permute-start(s16[1936,640]{1,0:T(8,128)(2,1)} %get-tuple-element.48.refs_0_), channel_id=1, source_target_pairs={{0,1},{1,0},{2,3},{3,2},{4,5},{5,4},{6,7},{7,6},{8,9},{9,8},{10,11... | collective-permute-start | bytes 7434248 | tf_op jit(solution)/shard_map/ppermute | solution.py:223
  46.1 7.4 %collective-permute-start.4 = (s16[1936,512]{1,0:T(8,128)(2,1)}, s16[1936,512]{1,0:T(8,128)(2,1)S(1)}, u32[]{:S(2)}, u32[]{:S(2)}) collective-permute-start(s16[1936,512]{1,0:T(8,128)(2,1)} %get-tuple-element.39), channel_id=1, source_target_pairs={{0,1},{1,0},{2,3},{3,2},{4,5},{5,4},{6,7},{7,6},{8,9},{9,8},{10,11... | collective-permute-start | bytes 5947400 | tf_op jit(solution)/shard_map/ppermute | solution.py:223
  46.7 16.0 %collective-permute-start.11 = (bf16[400,256]{1,0:T(8,128)(2,1)}, bf16[400,256]{1,0:T(8,128)(2,1)S(1)}, u32[]{:S(2)}, u32[]{:S(2)}) collective-permute-start(bf16[400,256]{1,0:T(8,128)(2,1)} %get-tuple-element.52), channel_id=1, source_target_pairs={{0,4},{1,5},{2,6},{3,7},{4,0},{5,1},{6,2},{7,3},{8,12},{9,13},{10,... | collective-permute-start | bytes 614408 | tf_op jit(solution)/shard_map/ppermute | solution.py:223
  47.2 15.5 %collective-permute-start.12 = (bf16[400,256]{1,0:T(8,128)(2,1)}, bf16[400,256]{1,0:T(8,128)(2,1)S(1)}, u32[]{:S(2)}, u32[]{:S(2)}) collective-permute-start(bf16[400,256]{1,0:T(8,128)(2,1)} %get-tuple-element.53), channel_id=1, source_target_pairs={{0,12},{1,13},{2,14},{3,15},{4,8},{5,9},{6,10},{7,11},{8,4},{9,5},... | collective-permute-start | bytes 614408 | tf_op jit(solution)/shard_map/ppermute | solution.py:223
  48.5 14.2 %collective-permute-start.13 = (bf16[400,256]{1,0:T(8,128)(2,1)}, bf16[400,256]{1,0:T(8,128)(2,1)S(1)}, u32[]{:S(2)}, u32[]{:S(2)}) collective-permute-start(bf16[400,256]{1,0:T(8,128)(2,1)} %get-tuple-element.54), channel_id=1, source_target_pairs={{0,14},{1,15},{2,12},{3,13},{4,10},{5,11},{6,8},{7,9},{8,6},{9,7},... | collective-permute-start | bytes 614408 | tf_op jit(solution)/shard_map/ppermute | solution.py:223
  58.1 25.9 %collective-permute-start.9 = (s16[976,512]{1,0:T(8,128)(2,1)}, s16[976,512]{1,0:T(8,128)(2,1)}, u32[]{:S(2)}, u32[]{:S(2)}) collective-permute-start(s16[976,512]{1,0:T(8,128)(2,1)} %get-tuple-element.50), channel_id=1, source_target_pairs={{0,2},{1,3},{2,0},{3,1},{4,6},{5,7},{6,4},{7,5},{8,10},{9,11},{10,... | collective-permute-start | bytes 2998280 | tf_op jit(solution)/shard_map/ppermute | solution.py:223
  62.7 5.9 %copy-start.8 = (bf16[400,256]{1,0:T(8,128)(2,1)}, bf16[400,256]{1,0:T(8,128)(2,1)S(1)}, u32[]{:S(2)}) copy-start(bf16[400,256]{1,0:T(8,128)(2,1)S(1)} %collective-permute-done.11.refs_1_.refs_2_) | copy-start | bytes 614404
  62.7 5.9 %copy-start.10 = (bf16[400,256]{1,0:T(8,128)(2,1)}, bf16[400,256]{1,0:T(8,128)(2,1)S(1)}, u32[]{:S(2)}) copy-start(bf16[400,256]{1,0:T(8,128)(2,1)S(1)} %collective-permute-done.12.refs_2_.refs_6_) | copy-start | bytes 614404
  62.7 5.9 %copy-start.12 = (bf16[400,256]{1,0:T(8,128)(2,1)}, bf16[400,256]{1,0:T(8,128)(2,1)S(1)}, u32[]{:S(2)}) copy-start(bf16[400,256]{1,0:T(8,128)(2,1)S(1)} %collective-permute-done.13.refs_3_.refs_7_) | copy-start | bytes 614404
  62.7 12.7 %copy-start.25 = (f32[2,16,6]{2,1,0:T(8,128)S(1)}, f32[2,16,6]{2,1,0:T(8,128)}, u32[]{:S(2)}) copy-start(f32[2,16,6]{2,1,0:T(8,128)} %add_convert_fusion) | copy-start | bytes 2308
  68.6 34.8 %collective-permute-start.15 = (s16[976,640]{1,0:T(8,128)(2,1)}, s16[976,640]{1,0:T(8,128)(2,1)}, u32[]{:S(2)}, u32[]{:S(2)}) collective-permute-start(s16[976,640]{1,0:T(8,128)(2,1)} %get-tuple-element.58), channel_id=1, source_target_pairs={{0,4},{1,5},{2,6},{3,7},{4,0},{5,1},{6,2},{7,3},{8,12},{9,13},{10,... | collective-permute-start | bytes 3747848 | tf_op jit(solution)/shard_map/ppermute | solution.py:223
  86.1 26.1 %collective-permute-start.14 = (s16[496,512]{1,0:T(8,128)(2,1)S(1)}, s16[496,512]{1,0:T(8,128)(2,1)S(1)}, u32[]{:S(2)}, u32[]{:S(2)}) collective-permute-start(s16[496,512]{1,0:T(8,128)(2,1)S(1)} %get-tuple-element.57), channel_id=1, source_target_pairs={{0,4},{1,5},{2,6},{3,7},{4,0},{5,1},{6,2},{7,3},{8,12},{9,13},{10,... | collective-permute-start | bytes 1523720 | tf_op jit(solution)/shard_map/ppermute | solution.py:223
  103.4 4.9 %copy-start.26 = (s32[256]{0:T(256)S(1)}, s32[256]{0:T(256)}, u32[]{:S(2)}) copy-start(s32[256]{0:T(256)} %add.157) | copy-start | bytes 3076
  103.4 5.0 %copy-start.5 = (bf16[400,256]{1,0:T(8,128)(2,1)S(1)}, bf16[400,256]{1,0:T(8,128)(2,1)}, u32[]{:S(2)}) copy-start(bf16[400,256]{1,0:T(8,128)(2,1)} %copy-done.4) | copy-start | bytes 614404
  103.4 5.0 %copy-start.7 = (bf16[400,256]{1,0:T(8,128)(2,1)S(1)}, bf16[400,256]{1,0:T(8,128)(2,1)}, u32[]{:S(2)}) copy-start(bf16[400,256]{1,0:T(8,128)(2,1)} %copy-done.6) | copy-start | bytes 614404
  103.4 5.0 %copy-start.9 = (bf16[400,256]{1,0:T(8,128)(2,1)S(1)}, bf16[400,256]{1,0:T(8,128)(2,1)}, u32[]{:S(2)}) copy-start(bf16[400,256]{1,0:T(8,128)(2,1)} %copy-done.8) | copy-start | bytes 614404
  103.4 5.0 %copy-start.11 = (bf16[400,256]{1,0:T(8,128)(2,1)S(1)}, bf16[400,256]{1,0:T(8,128)(2,1)}, u32[]{:S(2)}) copy-start(bf16[400,256]{1,0:T(8,128)(2,1)} %copy-done.10) | copy-start | bytes 614404
  103.4 5.0 %copy-start.13 = (bf16[400,256]{1,0:T(8,128)(2,1)S(1)}, bf16[400,256]{1,0:T(8,128)(2,1)}, u32[]{:S(2)}) copy-start(bf16[400,256]{1,0:T(8,128)(2,1)} %copy-done.12) | copy-start | bytes 614404
  103.4 5.0 %copy-start.15 = (bf16[400,256]{1,0:T(8,128)(2,1)S(1)}, bf16[400,256]{1,0:T(8,128)(2,1)}, u32[]{:S(2)}) copy-start(bf16[400,256]{1,0:T(8,128)(2,1)} %copy-done.14) | copy-start | bytes 614404
  103.4 5.0 %copy-start.17 = (bf16[400,256]{1,0:T(8,128)(2,1)S(1)}, bf16[400,256]{1,0:T(8,128)(2,1)}, u32[]{:S(2)}) copy-start(bf16[400,256]{1,0:T(8,128)(2,1)} %copy-done.16) | copy-start | bytes 614404
  103.5 5.0 %copy-start.19 = (bf16[400,256]{1,0:T(8,128)(2,1)S(1)}, bf16[400,256]{1,0:T(8,128)(2,1)}, u32[]{:S(2)}) copy-start(bf16[400,256]{1,0:T(8,128)(2,1)} %copy-done.18) | copy-start | bytes 614404
  106.6 12.7 %collective-permute-start.17 = (s16[496,640]{1,0:T(8,128)(2,1)}, s16[496,640]{1,0:T(8,128)(2,1)}, u32[]{:S(2)}, u32[]{:S(2)}) collective-permute-start(s16[496,640]{1,0:T(8,128)(2,1)} %get-tuple-element.62), channel_id=1, source_target_pairs={{0,2},{1,3},{2,0},{3,1},{4,6},{5,7},{6,4},{7,5},{8,10},{9,11},{10,... | collective-permute-start | bytes 1904648 | tf_op jit(solution)/shard_map/ppermute | solution.py:223
  108.3 18.2 %copy-start.20 = (f32[192,128]{1,0:T(8,128)}, f32[192,128]{1,0:T(8,128)S(1)}, u32[]{:S(2)}) copy-start(f32[192,128]{1,0:T(8,128)S(1)} %get-tuple-element.82.sine) | copy-start | bytes 294916
  113.3 13.2 %collective-permute-start.16 = (s16[256,512]{1,0:T(8,128)(2,1)}, s16[256,512]{1,0:T(8,128)(2,1)}, u32[]{:S(2)}, u32[]{:S(2)}) collective-permute-start(s16[256,512]{1,0:T(8,128)(2,1)} %get-tuple-element.61), channel_id=1, source_target_pairs={{0,8},{1,9},{2,10},{3,11},{4,12},{5,13},{6,14},{7,15},{8,0},{9,1},... | collective-permute-start | bytes 786440 | tf_op jit(solution)/shard_map/ppermute | solution.py:223
  115.2 32.5 %collective-permute-start.20 = (bf16[8,400,256]{2,1,0:T(8,128)(2,1)S(1)}, bf16[8,400,256]{2,1,0:T(8,128)(2,1)}, u32[]{:S(2)}, u32[]{:S(2)}) collective-permute-start(bf16[8,400,256]{2,1,0:T(8,128)(2,1)S(1)} %pack.3.refs_0_.own), channel_id=1, source_target_pairs={{0,1},{1,0},{2,3},{3,2},{4,5},{5,4},{6,7},{7,6},{8,9},{9,8},{10,11... | collective-permute-start | bytes 4915208 | tf_op jit(solution)/shard_map/ppermute | solution.py:223
  121.6 6.1 %copy-start.23 = (f32[1,192,640]{2,1,0:T(8,128)}, f32[1,192,640]{2,1,0:T(8,128)S(1)}, u32[]{:S(2)}) copy-start(f32[1,192,640]{2,1,0:T(8,128)S(1)} %get-tuple-element.63.refs_0_.held) | copy-start | bytes 1474564
  127.7 1.3 collective-permute-start.19
  127.8 17.5 %collective-permute-start.18 = (s16[256,640]{1,0:T(8,128)(2,1)}, s16[256,640]{1,0:T(8,128)(2,1)S(1)}, u32[]{:S(2)}, u32[]{:S(2)}) collective-permute-start(s16[256,640]{1,0:T(8,128)(2,1)} %get-tuple-element.65), channel_id=1, source_target_pairs={{0,8},{1,9},{2,10},{3,11},{4,12},{5,13},{6,14},{7,15},{8,0},{9,1},... | collective-permute-start | bytes 983048 | tf_op jit(solution)/shard_map/ppermute | solution.py:223
  145.3 0.9 copy-start.21
  146.2 1.0 copy-start.24
  147.5 1.7 copy-start.22
  157.7 24.7 %copy-start.2 = (bf16[2,96,1024]{2,1,0:T(8,128)(2,1)S(1)}, bf16[2,96,1024]{2,1,0:T(8,128)(2,1)}, u32[]{:S(2)}) copy-start(bf16[2,96,1024]{2,1,0:T(8,128)(2,1)} %param.8) | copy-start | bytes 1179652
  157.7 17.6 %collective-permute-start.21 = (bf16[192,1024]{1,0:T(8,128)(2,1)S(1)}, bf16[192,1024]{1,0:T(8,128)(2,1)S(1)}, u32[]{:S(2)}, u32[]{:S(2)}) collective-permute-start(bf16[192,1024]{1,0:T(8,128)(2,1)S(1)} %bitcast.50), channel_id=1, source_target_pairs={{0,4},{1,5},{2,6},{3,7},{4,0},{5,1},{6,2},{7,3},{8,12},{9,13},{10,... | collective-permute-start | bytes 1179656 | tf_op jit(solution)/shard_map/ppermute | solution.py:223
  157.8 17.5 %collective-permute-start.22 = (bf16[192,1024]{1,0:T(8,128)(2,1)S(1)}, bf16[192,1024]{1,0:T(8,128)(2,1)S(1)}, u32[]{:S(2)}, u32[]{:S(2)}) collective-permute-start(bf16[192,1024]{1,0:T(8,128)(2,1)S(1)} %bitcast.51), channel_id=1, source_target_pairs={{0,2},{1,3},{2,0},{3,1},{4,6},{5,7},{6,4},{7,5},{8,10},{9,11},{10,... | collective-permute-start | bytes 1179656 | tf_op jit(solution)/shard_map/ppermute | solution.py:223
  159.3 20.2 %collective-permute-start.23 = (bf16[192,1024]{1,0:T(8,128)(2,1)S(1)}, bf16[192,1024]{1,0:T(8,128)(2,1)S(1)}, u32[]{:S(2)}, u32[]{:S(2)}) collective-permute-start(bf16[192,1024]{1,0:T(8,128)(2,1)S(1)} %bitcast.52), channel_id=1, source_target_pairs={{0,8},{1,9},{2,10},{3,11},{4,12},{5,13},{6,14},{7,15},{8,0},{9,1},... | collective-permute-start | bytes 1179656 | tf_op jit(solution)/shard_map/ppermute | solution.py:223
  161.7 17.8 %collective-permute-start.24 = (bf16[192,1024]{1,0:T(8,128)(2,1)S(1)}, bf16[192,1024]{1,0:T(8,128)(2,1)S(1)}, u32[]{:S(2)}, u32[]{:S(2)}) collective-permute-start(bf16[192,1024]{1,0:T(8,128)(2,1)S(1)} %bitcast.53), channel_id=1, source_target_pairs={{0,1},{1,0},{2,3},{3,2},{4,5},{5,4},{6,7},{7,6},{8,9},{9,8},{10,11... | collective-permute-start | bytes 1179656 | tf_op jit(solution)/shard_map/ppermute | solution.py:223
  179.7 6.1 %collective-permute-start.28 = (bf16[3,192,1024]{2,1,0:T(8,128)(2,1)S(1)}, bf16[3,192,1024]{2,1,0:T(8,128)(2,1)}, u32[]{:S(2)}, u32[]{:S(2)}) collective-permute-start(bf16[3,192,1024]{2,1,0:T(8,128)(2,1)S(1)} %get-tuple-element.68.refs_0_), channel_id=1, source_target_pairs={{0,1},{1,0},{2,3},{3,2},{4,5},{5,4},{6,7},{7,6},{8,9},{9,8},{10,11... | collective-permute-start | bytes 3538952 | tf_op jit(solution)/shard_map/ppermute | solution.py:223
  179.7 20.1 %collective-permute-start.27 = (bf16[2,192,1024]{2,1,0:T(8,128)(2,1)S(1)}, bf16[2,192,1024]{2,1,0:T(8,128)(2,1)}, u32[]{:S(2)}, u32[]{:S(2)}) collective-permute-start(bf16[2,192,1024]{2,1,0:T(8,128)(2,1)S(1)} %get-tuple-element.67.refs_1_), channel_id=1, source_target_pairs={{0,2},{1,3},{2,0},{3,1},{4,6},{5,7},{6,4},{7,5},{8,10},{9,11},{10,... | collective-permute-start | bytes 2359304 | tf_op jit(solution)/shard_map/ppermute | solution.py:223
  180.3 13.2 %collective-permute-start.25 = (bf16[192,1024]{1,0:T(8,128)(2,1)S(1)}, bf16[192,1024]{1,0:T(8,128)(2,1)}, u32[]{:S(2)}, u32[]{:S(2)}) collective-permute-start(bf16[192,1024]{1,0:T(8,128)(2,1)S(1)} %together.4.refs_0_), channel_id=1, source_target_pairs={{0,12},{1,13},{2,14},{3,15},{4,8},{5,9},{6,10},{7,11},{8,4},{9,5},... | collective-permute-start | bytes 1179656 | tf_op jit(solution)/shard_map/ppermute | solution.py:223
  201.1 3.0 %collective-permute-start.29 = (bf16[3,192,1024]{2,1,0:T(8,128)(2,1)S(1)}, bf16[3,192,1024]{2,1,0:T(8,128)(2,1)}, u32[]{:S(2)}, u32[]{:S(2)}) collective-permute-start(bf16[3,192,1024]{2,1,0:T(8,128)(2,1)S(1)} %pack.5.refs_0_), channel_id=1, source_target_pairs={{0,1},{1,0},{2,3},{3,2},{4,5},{5,4},{6,7},{7,6},{8,9},{9,8},{10,11... | collective-permute-start | bytes 3538952 | tf_op jit(solution)/shard_map/ppermute | solution.py:223
  201.2 11.7 %collective-permute-start.26 = (bf16[192,1024]{1,0:T(8,128)(2,1)}, bf16[192,1024]{1,0:T(8,128)(2,1)S(1)}, u32[]{:S(2)}, u32[]{:S(2)}) collective-permute-start(bf16[192,1024]{1,0:T(8,128)(2,1)} %collective-permute-done.25.refs_1_), channel_id=1, source_target_pairs={{0,2},{1,3},{2,0},{3,1},{4,6},{5,7},{6,4},{7,5},{8,10},{9,11},{10,... | collective-permute-start | bytes 1179656 | tf_op jit(solution)/shard_map/ppermute | solution.py:223
  212.9 1.7 collective-permute-start.30

commit v11 on v10

--- a/solution.py
+++ b/solution.py
@@ -325,20 +325,19 @@
 
     found = []
     rows = coded_rows(normed.shape[0])
-    for side in range(2):
-        for start in range(0, half, 2 * HD):
-            at = slice(start, min(start + 2 * HD, half))
-            product = jnp.dot(
-                normed[...],
-                slabs[index, :, side * half + at.start : side * half + at.stop],
-                preferred_element_type=jnp.float32,
-            )
-            if side == 0:
-                kept[0, :, at] = product
-            else:
-                codes, power = encode(product)
-                sent[pl.ds(pl.multiple_of(index * rows, TILE), rows), at] = codes
-                found.append(power)
+    place = pl.ds(pl.multiple_of(index * rows, TILE), rows)
+    for start in range(0, 2 * half, 2 * HD):
+        stop = start + 2 * HD
+        product = jnp.dot(
+            normed[...], slabs[index, :, start:stop], preferred_element_type=jnp.float32
+        )
+        if start < half:
+            kept[0, :, start : min(stop, half)] = product[:, : half - start]
+        if stop > half:
+            first = max(start, half)
+            codes, power = encode(product[:, first - start :])
+            sent[place, first - half : stop - half] = codes
+            found.append(power)
     powers[pl.ds(index, 1), :] = jnp.concatenate(found, 1)
 
     @pl.when(index == KVH - 1)
@@ -773,28 +772,27 @@
     def finished(part, number, landed, *after):
         return finish(bits[0], part, landed, cosine, sine, PART_HEADS[number], after)
 
-    for k in (1, 3, 4, 5):
+    for k in (1, 3, 4, 5, 6):
         handed(k)
     held_a, sent_a = project(bits[0], normed, qkv_weight, 0, cache_pieces[:1])
     core_a = swap(sent_a, 1)
     held_b, sent_b = project(
         bits[0], normed, qkv_weight, 1, [held_a, cache_pieces[1], cache_pieces[3]]
     )
-    sent_b, cache_pieces[2], cache_pieces[6], cache_pieces[7] = together(
-        [sent_b, cache_pieces[2], cache_pieces[6], cache_pieces[7]], cache_pieces[4:6]
+    sent_b, cache_pieces[2], cache_pieces[7] = together(
+        [sent_b, cache_pieces[2], cache_pieces[7]], cache_pieces[4:7]
     )
     core_b = swap(sent_b, 1)
-    held_a, sent_a = folded(held_a, 1, core_a, 1, sent_b)
+    for k in (2, 7):
+        handed(k)
+    held_a, sent_a = folded(held_a, 2, core_a, 2, sent_b)
+    line_a = swap(sent_a, 4)
+    held_b, sent_b = folded(held_b, 1, core_b, 1, held_a, cache_pieces[2], cache_pieces[7])
+    line_b = swap(sent_b, 2)
+    held_a, sent_a = folded(held_a, 1, line_a, 1, held_b)
     line_a = swap(sent_a, 2)
-    for k in (2, 6, 7):
-        handed(k)
-    late = [cache_pieces[k] for k in (2, 6, 7)]
-    held_b, sent_b = folded(held_b, 2, core_b, 2, held_a, *late)
+    held_b, sent_b = folded(held_b, 2, line_b, 1, held_a)
     line_b = swap(sent_b, 4)
-    held_a, sent_a = folded(held_a, 2, line_a, 1, held_b)
-    line_a = swap(sent_a, 4)
-    held_b, sent_b = folded(held_b, 1, line_b, 1, held_a)
-    line_b = swap(sent_b, 2)
     (cache_own,) = pack(cache_pieces, [tuple(range(KVH))], [held_b])
     cache_other = swap(cache_own, 1)
     held_a, sent_a = folded(held_a, 3, line_a, 1, cache_own)

time: 220 us -> 214 us (0.973)
  starting transfers between devices: 40.8 us -> 37.6 us
    ppermute x31, starting transfers between devices: 40.8 us -> 37.6 us  [swap(): return lax.ppermute(value, 'tensor', [(i, i ^ bit) for i in range(devices)])]
  transfers between devices with their start and end apart: 31 -> 31, of which waited for: 19 -> 18; matrix products, arithmetic and copies ran while one was open for 4% -> 4% of each run, Pallas kernels for 27% -> 28%
where the time goes in v11:
time: 214 us; the launch traced here: 213 us
  waiting for transfers between devices  84.3 us (39%)
  Pallas kernels  72.8 us (34%)
  starting transfers between devices  37.6 us (18%)
  local copies, waits for them, and re-layouts  10.6 us (5%)
  other arithmetic  7.24 us (3%)
    ppermute x31, waiting for transfers between devices, swap(): return lax.ppermute(value, 'tensor', [(i, i ^ bit) for i in range(devices)])  84.3 us
    ppermute x31, starting transfers between devices, swap(): return lax.ppermute(value, 'tensor', [(i, i ^ bit) for i in range(devices)])  37.6 us
    pallas_call x4, Pallas kernels, mix(): pl.pallas_call(functools.partial(mix_kernel, len(pieces)), in_specs=[pl.B...  21.5 us
    pallas_call x2, Pallas kernels, project(): pl.pallas_call(functools.partial(project_kernel, part), grid_spec=pltpu.P...  20.1 us
    pallas_call x6, Pallas kernels, fold(): pl.pallas_call(functools.partial(fold_kernel, steps, low), grid_spec=pltp...  19 us
    pallas_call x1, Pallas kernels, attend(): pl.pallas_call(attend_kernel, in_specs=[pl.BlockSpec(memory_space=pltpu.S...  8.36 us
    unnamed x58, local copies, waits for them, and re-layouts  5.93 us
  transfers between devices with their start and end apart: 31, of which 18 were waited for; matrix products, arithmetic and copies ran while one was open for 4% of the time, Pallas kernels for 28%

profile of v11, /device:TPU:0, one launch (start us, length us, event | category | flops | bytes accessed | tf_op | source)
XLA Modules:
  0.0 213.4 jit_solution(6973725873857437326)
XLA Ops:
  0.0 1.2 fusion
  1.2 3.0 %collective-permute-start = (f32[2,96]{1,0:T(2,128)S(1)}, f32[2,96]{1,0:T(2,128)S(1)}, u32[]{:S(2)}, u32[]{:S(2)}) collective-permute-start(f32[2,96]{1,0:T(2,128)S(1)} %fusion), channel_id=1, source_target_pairs={{0,2},{1,3},{2,0},{3,1},{4,6},{5,7},{6,4},{7,5},{8,10},{9,11},{10,... | collective-permute-start | bytes 2312 | tf_op jit(solution)/shard_map/ppermute | solution.py:223
  4.3 1.5 collective-permute-done
  5.8 1.1 collective-permute-done.1
  7.0 2.1 collective-permute-start.2
  9.0 0.8 reshape.240
  9.8 0.7 convert_element_type.29
  10.6 3.0 %collective-permute-start.3 = (f32[2,96]{1,0:T(2,128)S(1)}, f32[2,96]{1,0:T(2,128)S(1)}, u32[]{:S(2)}, u32[]{:S(2)}) collective-permute-start(f32[2,96]{1,0:T(2,128)S(1)} %add.139), channel_id=1, source_target_pairs={{0,8},{1,9},{2,10},{3,11},{4,12},{5,13},{6,14},{7,15},{8,0},{9,1},... | collective-permute-start | bytes 2312 | tf_op jit(solution)/shard_map/ppermute | solution.py:223
  13.6 1.4 copy-done.3
  15.0 0.9 arrange.1
  15.9 1.5 collective-permute-start.5
  17.4 1.5 collective-permute-start.6
  19.3 3.5 %collective-permute-start.8 = (bf16[400,256]{1,0:T(8,128)(2,1)S(1)}, bf16[400,256]{1,0:T(8,128)(2,1)S(1)}, u32[]{:S(2)}, u32[]{:S(2)}) collective-permute-start(bf16[400,256]{1,0:T(8,128)(2,1)S(1)} %get-tuple-element.45), channel_id=1, source_target_pairs={{0,10},{1,11},{2,8},{3,9},{4,14},{5,15},{6,12},{7,13},{8,2},{9,3},... | collective-permute-start | bytes 614408 | tf_op jit(solution)/shard_map/ppermute | solution.py:223
  23.2 9.1 %project.2 = (f32[8,192,512]{2,1,0:T(8,128)S(1)}, s16[1936,512]{1,0:T(8,128)(2,1)}) custom-call(s32[1]{0:T(128)} %bitcast.2.core, bf16[192,1024]{1,0:T(8,128)(2,1)S(1)} %bitcast.47, bf16[1024,18432]{1,0:T(8,128)(2,1)} %weights.3, bf16[400,256]{1,0:T(8,128)(2,1)S(1)} %get-tuple-element.36.refs_0_), custom_call_target="tpu_custom_call" | custom-call | flops 1 | bytes 1 | tf_op jit(solution)/shard_map/project/pallas_call | solution.py:352
  32.4 1.6 copy-done
  34.1 11.0 %project.3 = (f32[8,192,640]{2,1,0:T(8,128)}, s16[1936,640]{1,0:T(8,128)(2,1)}) custom-call(s32[1]{0:T(128)} %bitcast.2.core, bf16[192,1024]{1,0:T(8,128)(2,1)S(1)} %bitcast.48, bf16[1024,18432]{1,0:T(8,128)(2,1)} %weights.3, f32[8,192,512]{2,1,0:T(8,128)} %copy-done, bf16[400,256]{1,0:T(8,128)(2,1)S(1)} %collective-permute-done.5.refs_1_, ...), custom_call_target="tpu_custom_call" | custom-call | flops 1 | bytes 1 | tf_op jit(solution)/shard_map/project/pallas_call | solution.py:352
  45.2 0.6 copy-done.8
  46.5 2.3 %collective-permute-start.12 = (bf16[400,256]{1,0:T(8,128)(2,1)}, bf16[400,256]{1,0:T(8,128)(2,1)S(1)}, u32[]{:S(2)}, u32[]{:S(2)}) collective-permute-start(bf16[400,256]{1,0:T(8,128)(2,1)} %get-tuple-element.51), channel_id=1, source_target_pairs={{0,4},{1,5},{2,6},{3,7},{4,0},{5,1},{6,2},{7,3},{8,12},{9,13},{10,... | collective-permute-start | bytes 614408 | tf_op jit(solution)/shard_map/ppermute | solution.py:223
  48.8 1.6 collective-permute-start.13
  50.4 0.7 add_convert_fusion
  51.1 2.2 %collective-permute-done.4.landed.landed_out.landed_powers = s16[1936,512]{1,0:T(8,128)(2,1)S(1)} collective-permute-done((s16[1936,512]{1,0:T(8,128)(2,1)}, s16[1936,512]{1,0:T(8,128)(2,1)S(1)}, u32[]{:S(2)}, u32[]{:S(2)}) %collective-permute-start.4) | collective-permute-done | bytes 1982496 | tf_op jit(solution)/shard_map/ppermute | solution.py:223
  53.3 4.7 %fold.6 = (f32[4,192,512]{2,1,0:T(8,128)S(1)}, s16[976,512]{1,0:T(8,128)(2,1)}) custom-call(s32[1]{0:T(128)} %bitcast.5.bit, f32[8,192,512]{2,1,0:T(8,128)} %copy-done, f32[8,192,512]{2,1,0:T(8,128)} %copy-done, s16[1936,512]{1,0:T(8,128)(2,1)S(1)} %collective-permute-done.4.landed.landed_out.landed_powers, ...), custom_call_target="tpu_custom_call" | custom-call | flops 1 | bytes 1 | tf_op jit(solution)/shard_map/fold/pallas_call | solution.py:406
  58.0 2.3 %collective-permute-start.10 = (s16[976,512]{1,0:T(8,128)(2,1)}, s16[976,512]{1,0:T(8,128)(2,1)}, u32[]{:S(2)}, u32[]{:S(2)}) collective-permute-start(s16[976,512]{1,0:T(8,128)(2,1)} %get-tuple-element.49), channel_id=1, source_target_pairs={{0,4},{1,5},{2,6},{3,7},{4,0},{5,1},{6,2},{7,3},{8,12},{9,13},{10,... | collective-permute-start | bytes 2998280 | tf_op jit(solution)/shard_map/ppermute | solution.py:223
  60.4 5.8 %fold.7 = (f32[4,192,640]{2,1,0:T(8,128)S(1)}, s16[976,640]{1,0:T(8,128)(2,1)}) custom-call(s32[1]{0:T(128)} %bitcast.4.bit, f32[8,192,640]{2,1,0:T(8,128)} %get-tuple-element.50.held.held_out, f32[8,192,640]{2,1,0:T(8,128)} %get-tuple-element.50.held.held_out, s16[1936,640]{1,0:T(8,128)(2,1)} %collective-permute-done.11.landed.landed_out.landed_powers, ...), custom_call_target="tpu_custom_call" | custom-call | flops 1 | bytes 1 | tf_op jit(solution)/shard_map/fold/pallas_call | solution.py:406
  66.1 1.6 collective-permute-start.15
  67.7 0.7 iota_add_fusion
  68.4 0.7 convert_element_type.32
  69.1 1.4 add.157
  70.4 0.7 and_select_fusion.1
  71.2 1.4 select_reduce_fusion.1
  72.5 1.1 fusion.5
  73.6 9.6 %collective-permute-done.10.landed.landed_out.landed_powers = s16[976,512]{1,0:T(8,128)(2,1)} collective-permute-done((s16[976,512]{1,0:T(8,128)(2,1)}, s16[976,512]{1,0:T(8,128)(2,1)}, u32[]{:S(2)}, u32[]{:S(2)}) %collective-permute-start.10) | collective-permute-done | bytes 999456 | tf_op jit(solution)/shard_map/ppermute | solution.py:223
  83.2 2.0 fold.8
  85.2 1.6 collective-permute-start.14
  86.8 10.0 %collective-permute-done.15.landed.landed_out.landed_powers = s16[976,640]{1,0:T(8,128)(2,1)} collective-permute-done((s16[976,640]{1,0:T(8,128)(2,1)}, s16[976,640]{1,0:T(8,128)(2,1)}, u32[]{:S(2)}, u32[]{:S(2)}) %collective-permute-start.15) | collective-permute-done | bytes 1249312 | tf_op jit(solution)/shard_map/ppermute | solution.py:223
  96.9 3.2 %fold.9 = (f32[2,192,640]{2,1,0:T(8,128)S(1)}, s16[496,640]{1,0:T(8,128)(2,1)}) custom-call(s32[1]{0:T(128)} %bitcast.5.bit, f32[4,192,640]{2,1,0:T(8,128)S(1)} %get-tuple-element.53.refs_0_.held.held_out, f32[4,192,640]{2,1,0:T(8,128)S(1)} %get-tuple-element.53.refs_0_.held.held_out, ...), custom_call_target="tpu_custom_call" | custom-call | flops 1 | bytes 1 | tf_op jit(solution)/shard_map/fold/pallas_call | solution.py:406
  100.1 1.1 collective-permute-start.17
  101.6 5.1 %collective-permute-done.14.landed.landed_out.landed_powers = s16[496,512]{1,0:T(8,128)(2,1)S(1)} collective-permute-done((s16[496,512]{1,0:T(8,128)(2,1)S(1)}, s16[496,512]{1,0:T(8,128)(2,1)S(1)}, u32[]{:S(2)}, u32[]{:S(2)}) %collective-permute-start.14) | collective-permute-done | bytes 507936 | tf_op jit(solution)/shard_map/ppermute | solution.py:223
  106.7 1.1 fold.10
  107.8 1.9 collective-permute-start.16
  109.9 9.7 %collective-permute-done.17.landed.landed_out.landed_powers = s16[496,640]{1,0:T(8,128)(2,1)} collective-permute-done((s16[496,640]{1,0:T(8,128)(2,1)}, s16[496,640]{1,0:T(8,128)(2,1)}, u32[]{:S(2)}, u32[]{:S(2)}) %collective-permute-start.17) | collective-permute-done | bytes 634912 | tf_op jit(solution)/shard_map/ppermute | solution.py:223
  119.6 2.2 %fold.11 = (f32[1,192,640]{2,1,0:T(8,128)S(1)}, s16[256,640]{1,0:T(8,128)(2,1)}) custom-call(s32[1]{0:T(128)} %bitcast.3.bit, f32[2,192,640]{2,1,0:T(8,128)S(1)} %get-tuple-element.57.refs_8_.held.held_out, f32[2,192,640]{2,1,0:T(8,128)S(1)} %get-tuple-element.57.refs_8_.held.held_out, ...), custom_call_target="tpu_custom_call" | custom-call | flops 1 | bytes 1 | tf_op jit(solution)/shard_map/fold/pallas_call | solution.py:406
  122.2 1.2 finish.2
  123.7 1.0 collective-permute-done.19
  124.9 15.8 %collective-permute-done.18.landed = s16[256,640]{1,0:T(8,128)(2,1)S(1)} collective-permute-done((s16[256,640]{1,0:T(8,128)(2,1)}, s16[256,640]{1,0:T(8,128)(2,1)S(1)}, u32[]{:S(2)}, u32[]{:S(2)}) %collective-permute-start.18) | collective-permute-done | bytes 327712 | tf_op jit(solution)/shard_map/ppermute | solution.py:223
  140.8 0.9 copy-done.21
  141.6 1.0 copy-done.24
  143.1 0.7 slice_reduce_fusion
  144.7 8.4 %attend.1 = bf16[16,96,128]{2,1,0:T(8,128)(2,1)S(1)} custom-call(s32[24]{0:T(128)S(1)} %copy-done.22, bf16[16,96,128]{2,1,0:T(8,128)(2,1)S(1)} %bitcast.55, bf16[16,16,128]{2,1,0:T(8,128)(2,1)S(1)} %pad.12.new_keys, bf16[16,16,128]{2,1,0:T(8,128)(2,1)S(1)} %pad.13.new_values, bf16[8,400,256]{2,1,0:T(8,128)(2,1)S(1)} %pack.3.refs_0_.own, ...), custom_call_target="tpu_custom_call" | custom-call | flops 1 | bytes 1 | tf_op jit(solution)/shard_map/attend/pallas_call | solution.py:661
  153.8 3.1 %collective-permute-start.23 = (bf16[192,1024]{1,0:T(8,128)(2,1)S(1)}, bf16[192,1024]{1,0:T(8,128)(2,1)S(1)}, u32[]{:S(2)}, u32[]{:S(2)}) collective-permute-start(bf16[192,1024]{1,0:T(8,128)(2,1)S(1)} %bitcast.52), channel_id=1, source_target_pairs={{0,8},{1,9},{2,10},{3,11},{4,12},{5,13},{6,14},{7,15},{8,0},{9,1},... | collective-permute-start | bytes 1179656 | tf_op jit(solution)/shard_map/ppermute | solution.py:223
  156.9 15.1 %collective-permute-done.21.refs_0_ = bf16[192,1024]{1,0:T(8,128)(2,1)S(1)} collective-permute-done((bf16[192,1024]{1,0:T(8,128)(2,1)S(1)}, bf16[192,1024]{1,0:T(8,128)(2,1)S(1)}, u32[]{:S(2)}, u32[]{:S(2)}) %collective-permute-start.21) | collective-permute-done | bytes 393248 | tf_op jit(solution)/shard_map/ppermute | solution.py:223
  172.0 2.0 collective-permute-done.23.refs_2_
  174.2 1.6 collective-permute-start.27
  175.8 2.2 %collective-permute-start.25 = (bf16[192,1024]{1,0:T(8,128)(2,1)S(1)}, bf16[192,1024]{1,0:T(8,128)(2,1)}, u32[]{:S(2)}, u32[]{:S(2)}) collective-permute-start(bf16[192,1024]{1,0:T(8,128)(2,1)S(1)} %together.4.refs_0_), channel_id=1, source_target_pairs={{0,12},{1,13},{2,14},{3,15},{4,8},{5,9},{6,10},{7,11},{8,4},{9,5},... | collective-permute-start | bytes 1179656 | tf_op jit(solution)/shard_map/ppermute | solution.py:223
  178.1 3.4 %mix.4.refs_3_ = f32[192,1024]{1,0:T(8,128)S(1)} custom-call(s32[2]{0:T(128)S(1)} %pad_add_fusion.1.places, bf16[192,1024]{1,0:T(8,128)(2,1)S(1)} %together.4.refs_0_, bf16[192,1024]{1,0:T(8,128)(2,1)S(1)} %collective-permute-done.24.refs_3_.refs_1_, bf16[16384,1024]{1,0:T(8,128)(2,1)} %refs_2_.7, bf16[192,1024]{1,0:T(8,128)(2,1)S(1)} %bitcast.49), custom_call_target="tpu_custom_call" | custom-call | flops 1 | bytes 1 | tf_op jit(solution)/shard_map/mix/pallas_call | solution.py:509
  181.5 7.0 %mix.5.refs_2_.refs_3_ = f32[192,1024]{1,0:T(8,128)S(1)} custom-call(s32[6]{0:T(128)S(1)} %stack.82.places, bf16[3,192,1024]{2,1,0:T(8,128)(2,1)S(1)} %get-tuple-element.66.refs_0_, bf16[3,192,1024]{2,1,0:T(8,128)(2,1)} %collective-permute-done.28.refs_1_, bf16[16384,1024]{1,0:T(8,128)(2,1)} %refs_2_.7, f32[192,1024]{1,0:T(8,128)S(1)} %mix.4.refs_3_), custom_call_target="tpu_custom_call" | custom-call | flops 1 | bytes 1 | tf_op jit(solution)/shard_map/mix/pallas_call | solution.py:509
  189.0 5.3 %collective-permute-done.27.refs_0_ = bf16[2,192,1024]{2,1,0:T(8,128)(2,1)} collective-permute-done((bf16[2,192,1024]{2,1,0:T(8,128)(2,1)S(1)}, bf16[2,192,1024]{2,1,0:T(8,128)(2,1)}, u32[]{:S(2)}, u32[]{:S(2)}) %collective-permute-start.27) | collective-permute-done | bytes 786464 | tf_op jit(solution)/shard_map/ppermute | solution.py:223
  194.2 1.3 pack.5.refs_0_
  195.6 1.6 collective-permute-start.26
  197.3 1.3 collective-permute-done.29.refs_1_
  198.6 7.0 %mix.6.refs_1_.refs_3_ = f32[192,1024]{1,0:T(8,128)S(1)} custom-call(s32[6]{0:T(128)S(1)} %stack.75.places, bf16[3,192,1024]{2,1,0:T(8,128)(2,1)S(1)} %pack.5.refs_0_, bf16[3,192,1024]{2,1,0:T(8,128)(2,1)} %collective-permute-done.29.refs_1_, bf16[16384,1024]{1,0:T(8,128)(2,1)} %refs_2_.7, f32[192,1024]{1,0:T(8,128)S(1)} %mix.5.refs_2_.refs_3_), custom_call_target="tpu_custom_call" | custom-call | flops 1 | bytes 1 | tf_op jit(solution)/shard_map/mix/pallas_call | solution.py:509
  205.6 1.8 collective-permute-done.26.refs_0_
  207.5 1.6 collective-permute-done.30.refs_1_
  209.1 4.1 %mix.7 = bf16[192,1024]{1,0:T(8,128)(2,1)} custom-call(s32[2]{0:T(128)S(1)} %pad_add_fusion.places, bf16[192,1024]{1,0:T(8,128)(2,1)S(1)} %together.5.refs_0_, bf16[192,1024]{1,0:T(8,128)(2,1)S(1)} %collective-permute-done.30.refs_1_, bf16[16384,1024]{1,0:T(8,128)(2,1)} %refs_2_.7, f32[192,1024]{1,0:T(8,128)S(1)} %mix.6.refs_1_.refs_3_), custom_call_target="tpu_custom_call" | custom-call | flops 1 | bytes 1 | tf_op jit(solution)/shard_map/mix/pallas_call | solution.py:509
  (133 shorter events, 6.1 us)
Async XLA Ops:
  0.0 23.1 %copy-start.1 = (bf16[2,96,1024]{2,1,0:T(8,128)(2,1)S(1)}, bf16[2,96,1024]{2,1,0:T(8,128)(2,1)}, u32[]{:S(2)}) copy-start(bf16[2,96,1024]{2,1,0:T(8,128)(2,1)} %param.8) | copy-start | bytes 1179652
  1.2 4.6 %collective-permute-start = (f32[2,96]{1,0:T(2,128)S(1)}, f32[2,96]{1,0:T(2,128)S(1)}, u32[]{:S(2)}, u32[]{:S(2)}) collective-permute-start(f32[2,96]{1,0:T(2,128)S(1)} %fusion), channel_id=1, source_target_pairs={{0,2},{1,3},{2,0},{3,1},{4,6},{5,7},{6,4},{7,5},{8,10},{9,11},{10,... | collective-permute-start | bytes 2312 | tf_op jit(solution)/shard_map/ppermute | solution.py:223
  5.8 1.1 collective-permute-start.1
  7.0 3.6 %collective-permute-start.2 = (f32[2,96]{1,0:T(2,128)S(1)}, f32[2,96]{1,0:T(2,128)S(1)}, u32[]{:S(2)}, u32[]{:S(2)}) collective-permute-start(f32[2,96]{1,0:T(2,128)S(1)} %add.138), channel_id=1, source_target_pairs={{0,4},{1,5},{2,6},{3,7},{4,0},{5,1},{6,2},{7,3},{8,12},{9,13},{10,... | collective-permute-start | bytes 2312 | tf_op jit(solution)/shard_map/ppermute | solution.py:223
  10.6 12.3 %collective-permute-start.3 = (f32[2,96]{1,0:T(2,128)S(1)}, f32[2,96]{1,0:T(2,128)S(1)}, u32[]{:S(2)}, u32[]{:S(2)}) collective-permute-start(f32[2,96]{1,0:T(2,128)S(1)} %add.139), channel_id=1, source_target_pairs={{0,8},{1,9},{2,10},{3,11},{4,12},{5,13},{6,14},{7,15},{8,0},{9,1},... | collective-permute-start | bytes 2312 | tf_op jit(solution)/shard_map/ppermute | solution.py:223
  13.6 1.4 copy-start.3
  15.9 16.5 %copy-start.18 = (bf16[400,256]{1,0:T(8,128)(2,1)}, bf16[400,256]{1,0:T(8,128)(2,1)S(1)}, u32[]{:S(2)}) copy-start(bf16[400,256]{1,0:T(8,128)(2,1)S(1)} %get-tuple-element.36.refs_0_) | copy-start | bytes 614404
  15.9 18.1 %collective-permute-start.5 = (bf16[400,256]{1,0:T(8,128)(2,1)S(1)}, bf16[400,256]{1,0:T(8,128)(2,1)S(1)}, u32[]{:S(2)}, u32[]{:S(2)}) collective-permute-start(bf16[400,256]{1,0:T(8,128)(2,1)S(1)} %get-tuple-element.39), channel_id=1, source_target_pairs={{0,2},{1,3},{2,0},{3,1},{4,6},{5,7},{6,4},{7,5},{8,10},{9,11},{10,... | collective-permute-start | bytes 614408 | tf_op jit(solution)/shard_map/ppermute | solution.py:223
  17.4 16.6 %collective-permute-start.6 = (bf16[400,256]{1,0:T(8,128)(2,1)S(1)}, bf16[400,256]{1,0:T(8,128)(2,1)S(1)}, u32[]{:S(2)}, u32[]{:S(2)}) collective-permute-start(bf16[400,256]{1,0:T(8,128)(2,1)S(1)} %get-tuple-element.40), channel_id=1, source_target_pairs={{0,6},{1,7},{2,4},{3,5},{4,2},{5,3},{6,0},{7,1},{8,14},{9,15},{10,... | collective-permute-start | bytes 614408 | tf_op jit(solution)/shard_map/ppermute | solution.py:223
  19.0 26.1 %collective-permute-start.7 = (bf16[400,256]{1,0:T(8,128)(2,1)S(1)}, bf16[400,256]{1,0:T(8,128)(2,1)S(1)}, u32[]{:S(2)}, u32[]{:S(2)}) collective-permute-start(bf16[400,256]{1,0:T(8,128)(2,1)S(1)} %get-tuple-element.44), channel_id=1, source_target_pairs={{0,8},{1,9},{2,10},{3,11},{4,12},{5,13},{6,14},{7,15},{8,0},{9,1},... | collective-permute-start | bytes 614408 | tf_op jit(solution)/shard_map/ppermute | solution.py:223
  19.3 25.8 %collective-permute-start.8 = (bf16[400,256]{1,0:T(8,128)(2,1)S(1)}, bf16[400,256]{1,0:T(8,128)(2,1)S(1)}, u32[]{:S(2)}, u32[]{:S(2)}) collective-permute-start(bf16[400,256]{1,0:T(8,128)(2,1)S(1)} %get-tuple-element.45), channel_id=1, source_target_pairs={{0,10},{1,11},{2,8},{3,9},{4,14},{5,15},{6,12},{7,13},{8,2},{9,3},... | collective-permute-start | bytes 614408 | tf_op jit(solution)/shard_map/ppermute | solution.py:223
  22.8 22.3 %collective-permute-start.9 = (bf16[400,256]{1,0:T(8,128)(2,1)S(1)}, bf16[400,256]{1,0:T(8,128)(2,1)S(1)}, u32[]{:S(2)}, u32[]{:S(2)}) collective-permute-start(bf16[400,256]{1,0:T(8,128)(2,1)S(1)} %get-tuple-element.46), channel_id=1, source_target_pairs={{0,12},{1,13},{2,14},{3,15},{4,8},{5,9},{6,10},{7,11},{8,4},{9,5},... | collective-permute-start | bytes 614408 | tf_op jit(solution)/shard_map/ppermute | solution.py:223
  32.4 1.6 copy-start
  34.0 11.0 %copy-start.4 = (bf16[400,256]{1,0:T(8,128)(2,1)}, bf16[400,256]{1,0:T(8,128)(2,1)S(1)}, u32[]{:S(2)}) copy-start(bf16[400,256]{1,0:T(8,128)(2,1)S(1)} %collective-permute-done.5.refs_1_) | copy-start | bytes 614404
  34.1 11.0 %copy-start.6 = (bf16[400,256]{1,0:T(8,128)(2,1)}, bf16[400,256]{1,0:T(8,128)(2,1)S(1)}, u32[]{:S(2)}) copy-start(bf16[400,256]{1,0:T(8,128)(2,1)S(1)} %collective-permute-done.6.refs_2_.refs_3_) | copy-start | bytes 614404
  45.1 0.7 copy-start.8
  45.1 0.7 copy-start.10
  45.1 0.8 copy-start.12
  45.1 1.3 copy-start.27
  45.9 14.4 %collective-permute-start.11 = (s16[1936,640]{1,0:T(8,128)(2,1)}, s16[1936,640]{1,0:T(8,128)(2,1)}, u32[]{:S(2)}, u32[]{:S(2)}) collective-permute-start(s16[1936,640]{1,0:T(8,128)(2,1)} %get-tuple-element.47.refs_0_), channel_id=1, source_target_pairs={{0,1},{1,0},{2,3},{3,2},{4,5},{5,4},{6,7},{7,6},{8,9},{9,8},{10,11... | collective-permute-start | bytes 7434248 | tf_op jit(solution)/shard_map/ppermute | solution.py:223
  45.9 7.4 %collective-permute-start.4 = (s16[1936,512]{1,0:T(8,128)(2,1)}, s16[1936,512]{1,0:T(8,128)(2,1)S(1)}, u32[]{:S(2)}, u32[]{:S(2)}) collective-permute-start(s16[1936,512]{1,0:T(8,128)(2,1)} %get-tuple-element.38), channel_id=1, source_target_pairs={{0,1},{1,0},{2,3},{3,2},{4,5},{5,4},{6,7},{7,6},{8,9},{9,8},{10,11... | collective-permute-start | bytes 5947400 | tf_op jit(solution)/shard_map/ppermute | solution.py:223
  46.5 13.8 %collective-permute-start.12 = (bf16[400,256]{1,0:T(8,128)(2,1)}, bf16[400,256]{1,0:T(8,128)(2,1)S(1)}, u32[]{:S(2)}, u32[]{:S(2)}) collective-permute-start(bf16[400,256]{1,0:T(8,128)(2,1)} %get-tuple-element.51), channel_id=1, source_target_pairs={{0,4},{1,5},{2,6},{3,7},{4,0},{5,1},{6,2},{7,3},{8,12},{9,13},{10,... | collective-permute-start | bytes 614408 | tf_op jit(solution)/shard_map/ppermute | solution.py:223
  48.8 11.5 %collective-permute-start.13 = (bf16[400,256]{1,0:T(8,128)(2,1)}, bf16[400,256]{1,0:T(8,128)(2,1)S(1)}, u32[]{:S(2)}, u32[]{:S(2)}) collective-permute-start(bf16[400,256]{1,0:T(8,128)(2,1)} %get-tuple-element.52), channel_id=1, source_target_pairs={{0,14},{1,15},{2,12},{3,13},{4,10},{5,11},{6,8},{7,9},{8,6},{9,7},... | collective-permute-start | bytes 614408 | tf_op jit(solution)/shard_map/ppermute | solution.py:223
  58.0 25.2 %collective-permute-start.10 = (s16[976,512]{1,0:T(8,128)(2,1)}, s16[976,512]{1,0:T(8,128)(2,1)}, u32[]{:S(2)}, u32[]{:S(2)}) collective-permute-start(s16[976,512]{1,0:T(8,128)(2,1)} %get-tuple-element.49), channel_id=1, source_target_pairs={{0,4},{1,5},{2,6},{3,7},{4,0},{5,1},{6,2},{7,3},{8,12},{9,13},{10,... | collective-permute-start | bytes 2998280 | tf_op jit(solution)/shard_map/ppermute | solution.py:223
  60.3 5.8 %copy-start.14 = (bf16[400,256]{1,0:T(8,128)(2,1)}, bf16[400,256]{1,0:T(8,128)(2,1)S(1)}, u32[]{:S(2)}) copy-start(bf16[400,256]{1,0:T(8,128)(2,1)S(1)} %collective-permute-done.12.refs_1_.refs_2_) | copy-start | bytes 614404
  60.3 5.8 %copy-start.16 = (bf16[400,256]{1,0:T(8,128)(2,1)}, bf16[400,256]{1,0:T(8,128)(2,1)S(1)}, u32[]{:S(2)}) copy-start(bf16[400,256]{1,0:T(8,128)(2,1)S(1)} %collective-permute-done.13.refs_2_.refs_7_) | copy-start | bytes 614404
  60.3 8.0 %copy-start.25 = (f32[2,16,6]{2,1,0:T(8,128)S(1)}, f32[2,16,6]{2,1,0:T(8,128)}, u32[]{:S(2)}) copy-start(f32[2,16,6]{2,1,0:T(8,128)} %add_convert_fusion) | copy-start | bytes 2308
  66.1 30.7 %collective-permute-start.15 = (s16[976,640]{1,0:T(8,128)(2,1)}, s16[976,640]{1,0:T(8,128)(2,1)}, u32[]{:S(2)}, u32[]{:S(2)}) collective-permute-start(s16[976,640]{1,0:T(8,128)(2,1)} %get-tuple-element.56), channel_id=1, source_target_pairs={{0,2},{1,3},{2,0},{3,1},{4,6},{5,7},{6,4},{7,5},{8,10},{9,11},{10,... | collective-permute-start | bytes 3747848 | tf_op jit(solution)/shard_map/ppermute | solution.py:223
  85.2 21.5 %collective-permute-start.14 = (s16[496,512]{1,0:T(8,128)(2,1)S(1)}, s16[496,512]{1,0:T(8,128)(2,1)S(1)}, u32[]{:S(2)}, u32[]{:S(2)}) collective-permute-start(s16[496,512]{1,0:T(8,128)(2,1)S(1)} %get-tuple-element.55), channel_id=1, source_target_pairs={{0,2},{1,3},{2,0},{3,1},{4,6},{5,7},{6,4},{7,5},{8,10},{9,11},{10,... | collective-permute-start | bytes 1523720 | tf_op jit(solution)/shard_map/ppermute | solution.py:223
  96.8 4.5 %copy-start.26 = (s32[256]{0:T(256)S(1)}, s32[256]{0:T(256)}, u32[]{:S(2)}) copy-start(s32[256]{0:T(256)} %add.157) | copy-start | bytes 3076
  96.8 4.6 %copy-start.5 = (bf16[400,256]{1,0:T(8,128)(2,1)S(1)}, bf16[400,256]{1,0:T(8,128)(2,1)}, u32[]{:S(2)}) copy-start(bf16[400,256]{1,0:T(8,128)(2,1)} %copy-done.4) | copy-start | bytes 614404
  96.8 4.6 %copy-start.7 = (bf16[400,256]{1,0:T(8,128)(2,1)S(1)}, bf16[400,256]{1,0:T(8,128)(2,1)}, u32[]{:S(2)}) copy-start(bf16[400,256]{1,0:T(8,128)(2,1)} %copy-done.6) | copy-start | bytes 614404
  96.8 4.6 %copy-start.9 = (bf16[400,256]{1,0:T(8,128)(2,1)S(1)}, bf16[400,256]{1,0:T(8,128)(2,1)}, u32[]{:S(2)}) copy-start(bf16[400,256]{1,0:T(8,128)(2,1)} %copy-done.8) | copy-start | bytes 614404
  96.8 4.6 %copy-start.11 = (bf16[400,256]{1,0:T(8,128)(2,1)S(1)}, bf16[400,256]{1,0:T(8,128)(2,1)}, u32[]{:S(2)}) copy-start(bf16[400,256]{1,0:T(8,128)(2,1)} %copy-done.10) | copy-start | bytes 614404
  96.9 4.6 %copy-start.13 = (bf16[400,256]{1,0:T(8,128)(2,1)S(1)}, bf16[400,256]{1,0:T(8,128)(2,1)}, u32[]{:S(2)}) copy-start(bf16[400,256]{1,0:T(8,128)(2,1)} %copy-done.12) | copy-start | bytes 614404
  96.9 4.6 %copy-start.15 = (bf16[400,256]{1,0:T(8,128)(2,1)S(1)}, bf16[400,256]{1,0:T(8,128)(2,1)}, u32[]{:S(2)}) copy-start(bf16[400,256]{1,0:T(8,128)(2,1)} %copy-done.14) | copy-start | bytes 614404
  96.9 4.6 %copy-start.17 = (bf16[400,256]{1,0:T(8,128)(2,1)S(1)}, bf16[400,256]{1,0:T(8,128)(2,1)}, u32[]{:S(2)}) copy-start(bf16[400,256]{1,0:T(8,128)(2,1)} %copy-done.16) | copy-start | bytes 614404
  96.9 4.6 %copy-start.19 = (bf16[400,256]{1,0:T(8,128)(2,1)S(1)}, bf16[400,256]{1,0:T(8,128)(2,1)}, u32[]{:S(2)}) copy-start(bf16[400,256]{1,0:T(8,128)(2,1)} %copy-done.18) | copy-start | bytes 614404
  100.1 19.5 %collective-permute-start.17 = (s16[496,640]{1,0:T(8,128)(2,1)}, s16[496,640]{1,0:T(8,128)(2,1)}, u32[]{:S(2)}, u32[]{:S(2)}) collective-permute-start(s16[496,640]{1,0:T(8,128)(2,1)} %get-tuple-element.60), channel_id=1, source_target_pairs={{0,4},{1,5},{2,6},{3,7},{4,0},{5,1},{6,2},{7,3},{8,12},{9,13},{10,... | collective-permute-start | bytes 1904648 | tf_op jit(solution)/shard_map/ppermute | solution.py:223
  101.3 20.9 %copy-start.20 = (f32[192,128]{1,0:T(8,128)}, f32[192,128]{1,0:T(8,128)S(1)}, u32[]{:S(2)}) copy-start(f32[192,128]{1,0:T(8,128)S(1)} %get-tuple-element.80.sine) | copy-start | bytes 294916
  107.8 14.4 %collective-permute-start.16 = (s16[256,512]{1,0:T(8,128)(2,1)}, s16[256,512]{1,0:T(8,128)(2,1)}, u32[]{:S(2)}, u32[]{:S(2)}) collective-permute-start(s16[256,512]{1,0:T(8,128)(2,1)} %get-tuple-element.59), channel_id=1, source_target_pairs={{0,8},{1,9},{2,10},{3,11},{4,12},{5,13},{6,14},{7,15},{8,0},{9,1},... | collective-permute-start | bytes 786440 | tf_op jit(solution)/shard_map/ppermute | solution.py:223
  109.8 33.3 %collective-permute-start.20 = (bf16[8,400,256]{2,1,0:T(8,128)(2,1)S(1)}, bf16[8,400,256]{2,1,0:T(8,128)(2,1)}, u32[]{:S(2)}, u32[]{:S(2)}) collective-permute-start(bf16[8,400,256]{2,1,0:T(8,128)(2,1)S(1)} %pack.3.refs_0_.own), channel_id=1, source_target_pairs={{0,1},{1,0},{2,3},{3,2},{4,5},{5,4},{6,7},{7,6},{8,9},{9,8},{10,11... | collective-permute-start | bytes 4915208 | tf_op jit(solution)/shard_map/ppermute | solution.py:223
  121.8 1.6 copy-start.23
  123.4 1.3 collective-permute-start.19
  123.5 17.3 %collective-permute-start.18 = (s16[256,640]{1,0:T(8,128)(2,1)}, s16[256,640]{1,0:T(8,128)(2,1)S(1)}, u32[]{:S(2)}, u32[]{:S(2)}) collective-permute-start(s16[256,640]{1,0:T(8,128)(2,1)} %get-tuple-element.63), channel_id=1, source_target_pairs={{0,8},{1,9},{2,10},{3,11},{4,12},{5,13},{6,14},{7,15},{8,0},{9,1},... | collective-permute-start | bytes 983048 | tf_op jit(solution)/shard_map/ppermute | solution.py:223
  140.7 0.9 copy-start.21
  141.6 1.0 copy-start.24
  142.9 1.7 copy-start.22
  153.1 25.0 %copy-start.2 = (bf16[2,96,1024]{2,1,0:T(8,128)(2,1)S(1)}, bf16[2,96,1024]{2,1,0:T(8,128)(2,1)}, u32[]{:S(2)}) copy-start(bf16[2,96,1024]{2,1,0:T(8,128)(2,1)} %param.8) | copy-start | bytes 1179652
  153.1 18.8 %collective-permute-start.21 = (bf16[192,1024]{1,0:T(8,128)(2,1)S(1)}, bf16[192,1024]{1,0:T(8,128)(2,1)S(1)}, u32[]{:S(2)}, u32[]{:S(2)}) collective-permute-start(bf16[192,1024]{1,0:T(8,128)(2,1)S(1)} %bitcast.50), channel_id=1, source_target_pairs={{0,4},{1,5},{2,6},{3,7},{4,0},{5,1},{6,2},{7,3},{8,12},{9,13},{10,... | collective-permute-start | bytes 1179656 | tf_op jit(solution)/shard_map/ppermute | solution.py:223
  153.2 18.8 %collective-permute-start.22 = (bf16[192,1024]{1,0:T(8,128)(2,1)S(1)}, bf16[192,1024]{1,0:T(8,128)(2,1)S(1)}, u32[]{:S(2)}, u32[]{:S(2)}) collective-permute-start(bf16[192,1024]{1,0:T(8,128)(2,1)S(1)} %bitcast.51), channel_id=1, source_target_pairs={{0,2},{1,3},{2,0},{3,1},{4,6},{5,7},{6,4},{7,5},{8,10},{9,11},{10,... | collective-permute-start | bytes 1179656 | tf_op jit(solution)/shard_map/ppermute | solution.py:223
  153.8 20.2 %collective-permute-start.23 = (bf16[192,1024]{1,0:T(8,128)(2,1)S(1)}, bf16[192,1024]{1,0:T(8,128)(2,1)S(1)}, u32[]{:S(2)}, u32[]{:S(2)}) collective-permute-start(bf16[192,1024]{1,0:T(8,128)(2,1)S(1)} %bitcast.52), channel_id=1, source_target_pairs={{0,8},{1,9},{2,10},{3,11},{4,12},{5,13},{6,14},{7,15},{8,0},{9,1},... | collective-permute-start | bytes 1179656 | tf_op jit(solution)/shard_map/ppermute | solution.py:223
  156.9 17.1 %collective-permute-start.24 = (bf16[192,1024]{1,0:T(8,128)(2,1)S(1)}, bf16[192,1024]{1,0:T(8,128)(2,1)S(1)}, u32[]{:S(2)}, u32[]{:S(2)}) collective-permute-start(bf16[192,1024]{1,0:T(8,128)(2,1)S(1)} %bitcast.53), channel_id=1, source_target_pairs={{0,1},{1,0},{2,3},{3,2},{4,5},{5,4},{6,7},{7,6},{8,9},{9,8},{10,11... | collective-permute-start | bytes 1179656 | tf_op jit(solution)/shard_map/ppermute | solution.py:223
  174.1 7.4 %collective-permute-start.28 = (bf16[3,192,1024]{2,1,0:T(8,128)(2,1)S(1)}, bf16[3,192,1024]{2,1,0:T(8,128)(2,1)}, u32[]{:S(2)}, u32[]{:S(2)}) collective-permute-start(bf16[3,192,1024]{2,1,0:T(8,128)(2,1)S(1)} %get-tuple-element.66.refs_0_), channel_id=1, source_target_pairs={{0,1},{1,0},{2,3},{3,2},{4,5},{5,4},{6,7},{7,6},{8,9},{9,8},{10,11... | collective-permute-start | bytes 3538952 | tf_op jit(solution)/shard_map/ppermute | solution.py:223
  174.2 20.1 %collective-permute-start.27 = (bf16[2,192,1024]{2,1,0:T(8,128)(2,1)S(1)}, bf16[2,192,1024]{2,1,0:T(8,128)(2,1)}, u32[]{:S(2)}, u32[]{:S(2)}) collective-permute-start(bf16[2,192,1024]{2,1,0:T(8,128)(2,1)S(1)} %get-tuple-element.65.refs_1_), channel_id=1, source_target_pairs={{0,2},{1,3},{2,0},{3,1},{4,6},{5,7},{6,4},{7,5},{8,10},{9,11},{10,... | collective-permute-start | bytes 2359304 | tf_op jit(solution)/shard_map/ppermute | solution.py:223
  175.8 13.2 %collective-permute-start.25 = (bf16[192,1024]{1,0:T(8,128)(2,1)S(1)}, bf16[192,1024]{1,0:T(8,128)(2,1)}, u32[]{:S(2)}, u32[]{:S(2)}) collective-permute-start(bf16[192,1024]{1,0:T(8,128)(2,1)S(1)} %together.4.refs_0_), channel_id=1, source_target_pairs={{0,12},{1,13},{2,14},{3,15},{4,8},{5,9},{6,10},{7,11},{8,4},{9,5},... | collective-permute-start | bytes 1179656 | tf_op jit(solution)/shard_map/ppermute | solution.py:223
  195.6 3.0 %collective-permute-start.29 = (bf16[3,192,1024]{2,1,0:T(8,128)(2,1)S(1)}, bf16[3,192,1024]{2,1,0:T(8,128)(2,1)}, u32[]{:S(2)}, u32[]{:S(2)}) collective-permute-start(bf16[3,192,1024]{2,1,0:T(8,128)(2,1)S(1)} %pack.5.refs_0_), channel_id=1, source_target_pairs={{0,1},{1,0},{2,3},{3,2},{4,5},{5,4},{6,7},{7,6},{8,9},{9,8},{10,11... | collective-permute-start | bytes 3538952 | tf_op jit(solution)/shard_map/ppermute | solution.py:223
  195.6 11.7 %collective-permute-start.26 = (bf16[192,1024]{1,0:T(8,128)(2,1)}, bf16[192,1024]{1,0:T(8,128)(2,1)S(1)}, u32[]{:S(2)}, u32[]{:S(2)}) collective-permute-start(bf16[192,1024]{1,0:T(8,128)(2,1)} %collective-permute-done.25.refs_1_), channel_id=1, source_target_pairs={{0,2},{1,3},{2,0},{3,1},{4,6},{5,7},{6,4},{7,5},{8,10},{9,11},{10,... | collective-permute-start | bytes 1179656 | tf_op jit(solution)/shard_map/ppermute | solution.py:223
  207.4 1.7 collective-permute-start.30

commit v12 on v11

--- a/solution.py
+++ b/solution.py
@@ -367,7 +367,7 @@
             ],
         ),
         out_shape=[
-            jax.ShapeDtypeStruct((KVH, rows, columns), jnp.float32),
+            pltpu.HBM((KVH, rows, columns), jnp.float32),
             jax.ShapeDtypeStruct((sent_rows, columns), jnp.int16),
         ],
         compiler_params=pltpu.CompilerParams(vmem_limit_bytes=VMEM_LIMIT),
@@ -800,6 +800,7 @@
     held_b, sent_b = folded(held_b, 3, line_b, 1, held_a)
     line_b = swap(sent_b, 8)
     query_a, pair = finished(held_a, 0, line_a, held_b)
+    (pair,) = together([pair], [line_b])
     pair_other = swap(pair, 1)
     (query_b,) = finished(held_b, 1, line_b, query_a)
     query_chunks = [query_a, query_b]

time: 214 us -> 210 us (0.981)
  waiting for transfers between devices: 84.3 us -> 89.5 us
  Pallas kernels: 72.8 us -> 69.1 us
  starting transfers between devices: 37.6 us -> 34.8 us
    ppermute x31, waiting for transfers between devices: 84.3 us -> 89.5 us  [swap(): return lax.ppermute(value, 'tensor', [(i, i ^ bit) for i in range(devices)])]
    pallas_call x6, Pallas kernels: 19 us -> 15.8 us  [fold(): pl.pallas_call(functools.partial(fold_kernel, steps, low), grid_spec=pltp...]
    ppermute x31, starting transfers between devices: 37.6 us -> 34.8 us  [swap(): return lax.ppermute(value, 'tensor', [(i, i ^ bit) for i in range(devices)])]
    unnamed x58 -> x56, local copies, waits for them, and re-layouts: 5.93 us -> 6.13 us
  transfers between devices with their start and end apart: 31 -> 31, of which waited for: 18 -> 20; matrix products, arithmetic and copies ran while one was open for 4% -> 3% of each run, Pallas kernels for 28% -> 26%
where the time goes in v12:
time: 210 us; the launch traced here: 209 us
  waiting for transfers between devices  89.5 us (43%)
  Pallas kernels  69.1 us (33%)
  starting transfers between devices  34.8 us (17%)
  local copies, waits for them, and re-layouts  8.98 us (4%)
  other arithmetic  5.91 us (3%)
    ppermute x31, waiting for transfers between devices, swap(): return lax.ppermute(value, 'tensor', [(i, i ^ bit) for i in range(devices)])  89.5 us
    ppermute x31, starting transfers between devices, swap(): return lax.ppermute(value, 'tensor', [(i, i ^ bit) for i in range(devices)])  34.8 us
    pallas_call x4, Pallas kernels, mix(): pl.pallas_call(functools.partial(mix_kernel, len(pieces)), in_specs=[pl.B...  21.5 us
    pallas_call x2, Pallas kernels, project(): pl.pallas_call(functools.partial(project_kernel, part), grid_spec=pltpu.P...  20.3 us
    pallas_call x6, Pallas kernels, fold(): pl.pallas_call(functools.partial(fold_kernel, steps, low), grid_spec=pltp...  15.8 us
    pallas_call x1, Pallas kernels, attend(): pl.pallas_call(attend_kernel, in_specs=[pl.BlockSpec(memory_space=pltpu.S...  8.39 us
    unnamed x56, local copies, waits for them, and re-layouts  6.13 us
  transfers between devices with their start and end apart: 31, of which 20 were waited for; matrix products, arithmetic and copies ran while one was open for 3% of the time, Pallas kernels for 26%

profile of v12, /device:TPU:0, one launch (start us, length us, event | category | flops | bytes accessed | tf_op | source)
XLA Modules:
  0.0 208.9 jit_solution(10070844363211650283)
XLA Ops:
  0.0 1.2 fusion
  1.2 3.0 %collective-permute-start = (f32[2,96]{1,0:T(2,128)S(1)}, f32[2,96]{1,0:T(2,128)S(1)}, u32[]{:S(2)}, u32[]{:S(2)}) collective-permute-start(f32[2,96]{1,0:T(2,128)S(1)} %fusion), channel_id=1, source_target_pairs={{0,2},{1,3},{2,0},{3,1},{4,6},{5,7},{6,4},{7,5},{8,10},{9,11},{10,... | collective-permute-start | bytes 2312 | tf_op jit(solution)/shard_map/ppermute | solution.py:223
  4.3 1.5 collective-permute-done
  5.8 1.1 collective-permute-done.1
  7.0 2.1 collective-permute-start.2
  9.0 0.8 reshape.240
  9.8 0.7 convert_element_type.29
  10.6 3.0 %collective-permute-start.3 = (f32[2,96]{1,0:T(2,128)S(1)}, f32[2,96]{1,0:T(2,128)S(1)}, u32[]{:S(2)}, u32[]{:S(2)}) collective-permute-start(f32[2,96]{1,0:T(2,128)S(1)} %add.139), channel_id=1, source_target_pairs={{0,8},{1,9},{2,10},{3,11},{4,12},{5,13},{6,14},{7,15},{8,0},{9,1},... | collective-permute-start | bytes 2312 | tf_op jit(solution)/shard_map/ppermute | solution.py:223
  13.6 1.4 copy-done.6
  15.2 1.6 collective-permute-start.5
  16.8 1.5 collective-permute-start.6
  18.6 3.5 %collective-permute-start.8 = (bf16[400,256]{1,0:T(8,128)(2,1)S(1)}, bf16[400,256]{1,0:T(8,128)(2,1)S(1)}, u32[]{:S(2)}, u32[]{:S(2)}) collective-permute-start(bf16[400,256]{1,0:T(8,128)(2,1)S(1)} %get-tuple-element.45), channel_id=1, source_target_pairs={{0,10},{1,11},{2,8},{3,9},{4,14},{5,15},{6,12},{7,13},{8,2},{9,3},... | collective-permute-start | bytes 614408 | tf_op jit(solution)/shard_map/ppermute | solution.py:223
  22.6 9.3 %project.2 = (f32[8,192,512]{2,1,0:T(8,128)}, s16[1936,512]{1,0:T(8,128)(2,1)}) custom-call(s32[1]{0:T(128)} %bitcast.2.core, bf16[192,1024]{1,0:T(8,128)(2,1)S(1)} %bitcast.47, bf16[1024,18432]{1,0:T(8,128)(2,1)} %weights.3, bf16[400,256]{1,0:T(8,128)(2,1)S(1)} %get-tuple-element.36.refs_0_), custom_call_target="tpu_custom_call" | custom-call | flops 1 | bytes 1 | tf_op jit(solution)/shard_map/project/pallas_call | solution.py:352
  32.0 11.0 %project.3 = (f32[8,192,640]{2,1,0:T(8,128)}, s16[1936,640]{1,0:T(8,128)(2,1)}) custom-call(s32[1]{0:T(128)} %bitcast.2.core, bf16[192,1024]{1,0:T(8,128)(2,1)S(1)} %bitcast.48, bf16[1024,18432]{1,0:T(8,128)(2,1)} %weights.3, f32[8,192,512]{2,1,0:T(8,128)} %get-tuple-element.37.refs_0_.held.held_out, bf16[400,256]{1,0:T(8,128)(2,1)S(1)} %collective-permute-done.5.refs_1_, ...), custom_call_target="tpu_custom_call" | custom-call | flops 1 | bytes 1 | tf_op jit(solution)/shard_map/project/pallas_call | solution.py:352
  43.0 1.4 collective-permute-done.8.refs_4_.refs_5_
  44.5 0.6 copy-done.11
  45.2 0.5 collective-permute-start.4
  45.8 2.4 %collective-permute-start.12 = (bf16[400,256]{1,0:T(8,128)(2,1)S(1)}, bf16[400,256]{1,0:T(8,128)(2,1)S(1)}, u32[]{:S(2)}, u32[]{:S(2)}) collective-permute-start(bf16[400,256]{1,0:T(8,128)(2,1)S(1)} %get-tuple-element.51), channel_id=1, source_target_pairs={{0,4},{1,5},{2,6},{3,7},{4,0},{5,1},{6,2},{7,3},{8,12},{9,13},{10,... | collective-permute-start | bytes 614408 | tf_op jit(solution)/shard_map/ppermute | solution.py:223
  48.2 1.6 collective-permute-start.13
  49.9 2.7 %collective-permute-done.4.landed.landed_out.landed_powers = s16[1936,512]{1,0:T(8,128)(2,1)S(1)} collective-permute-done((s16[1936,512]{1,0:T(8,128)(2,1)}, s16[1936,512]{1,0:T(8,128)(2,1)S(1)}, u32[]{:S(2)}, u32[]{:S(2)}) %collective-permute-start.4) | collective-permute-done | bytes 1982496 | tf_op jit(solution)/shard_map/ppermute | solution.py:223
  52.6 3.7 %fold.6 = (f32[4,192,512]{2,1,0:T(8,128)S(1)}, s16[976,512]{1,0:T(8,128)(2,1)S(1)}) custom-call(s32[1]{0:T(128)} %bitcast.5.bit, f32[8,192,512]{2,1,0:T(8,128)} %get-tuple-element.37.refs_0_.held.held_out, f32[8,192,512]{2,1,0:T(8,128)} %get-tuple-element.37.refs_0_.held.held_out, ...), custom_call_target="tpu_custom_call" | custom-call | flops 1 | bytes 1 | tf_op jit(solution)/shard_map/fold/pallas_call | solution.py:406
  56.3 2.4 %collective-permute-start.10 = (s16[976,512]{1,0:T(8,128)(2,1)S(1)}, s16[976,512]{1,0:T(8,128)(2,1)S(1)}, u32[]{:S(2)}, u32[]{:S(2)}) collective-permute-start(s16[976,512]{1,0:T(8,128)(2,1)S(1)} %get-tuple-element.49), channel_id=1, source_target_pairs={{0,4},{1,5},{2,6},{3,7},{4,0},{5,1},{6,2},{7,3},{8,12},{9,13},{10,... | collective-permute-start | bytes 2998280 | tf_op jit(solution)/shard_map/ppermute | solution.py:223
  58.7 0.5 collective-permute-done.13.refs_2_.refs_7_
  59.2 5.7 %fold.7 = (f32[4,192,640]{2,1,0:T(8,128)S(1)}, s16[976,640]{1,0:T(8,128)(2,1)}) custom-call(s32[1]{0:T(128)} %bitcast.4.bit, f32[8,192,640]{2,1,0:T(8,128)} %get-tuple-element.50.held.held_out, f32[8,192,640]{2,1,0:T(8,128)} %get-tuple-element.50.held.held_out, s16[1936,640]{1,0:T(8,128)(2,1)} %collective-permute-done.11.landed.landed_out.landed_powers, ...), custom_call_target="tpu_custom_call" | custom-call | flops 1 | bytes 1 | tf_op jit(solution)/shard_map/fold/pallas_call | solution.py:406
  65.0 1.2 collective-permute-start.15
  66.5 14.9 %collective-permute-done.10.landed.landed_out.landed_powers = s16[976,512]{1,0:T(8,128)(2,1)S(1)} collective-permute-done((s16[976,512]{1,0:T(8,128)(2,1)S(1)}, s16[976,512]{1,0:T(8,128)(2,1)S(1)}, u32[]{:S(2)}, u32[]{:S(2)}) %collective-permute-start.10) | collective-permute-done | bytes 999456 | tf_op jit(solution)/shard_map/ppermute | solution.py:223
  81.3 1.7 fold.8
  83.0 0.9 copy-done.2
  83.9 1.5 collective-permute-start.14
  85.6 1.1 fusion.5
  86.8 8.8 %collective-permute-done.15.landed.landed_out.landed_powers = s16[976,640]{1,0:T(8,128)(2,1)S(1)} collective-permute-done((s16[976,640]{1,0:T(8,128)(2,1)}, s16[976,640]{1,0:T(8,128)(2,1)S(1)}, u32[]{:S(2)}, u32[]{:S(2)}) %collective-permute-start.15) | collective-permute-done | bytes 1249312 | tf_op jit(solution)/shard_map/ppermute | solution.py:223
  95.6 1.1 copy-done.3
  96.8 2.0 fold.9
  98.8 1.4 collective-permute-start.17
  100.3 4.9 %collective-permute-done.14.landed.landed_out.landed_powers = s16[496,512]{1,0:T(8,128)(2,1)} collective-permute-done((s16[496,512]{1,0:T(8,128)(2,1)}, s16[496,512]{1,0:T(8,128)(2,1)}, u32[]{:S(2)}, u32[]{:S(2)}) %collective-permute-start.14) | collective-permute-done | bytes 507936 | tf_op jit(solution)/shard_map/ppermute | solution.py:223
  105.3 2.2 %fold.10 = (f32[1,192,512]{2,1,0:T(8,128)S(1)}, s16[256,512]{1,0:T(8,128)(2,1)}) custom-call(s32[1]{0:T(128)} %bitcast.3.bit, f32[2,192,512]{2,1,0:T(8,128)S(1)} %copy-done.3, f32[2,192,512]{2,1,0:T(8,128)S(1)} %copy-done.3, s16[496,512]{1,0:T(8,128)(2,1)} %collective-permute-done.14.landed.landed_out.landed_powers, ...), custom_call_target="tpu_custom_call" | custom-call | flops 1 | bytes 1 | tf_op jit(solution)/shard_map/fold/pallas_call | solution.py:406
  107.5 0.7 copy-done.21
  108.2 0.5 collective-permute-start.16
  108.8 1.8 pad_maximum_fusion
  110.7 3.8 %collective-permute-done.17.landed.landed_out.landed_powers = s16[496,640]{1,0:T(8,128)(2,1)S(1)} collective-permute-done((s16[496,640]{1,0:T(8,128)(2,1)}, s16[496,640]{1,0:T(8,128)(2,1)S(1)}, u32[]{:S(2)}, u32[]{:S(2)}) %collective-permute-start.17) | collective-permute-done | bytes 634912 | tf_op jit(solution)/shard_map/ppermute | solution.py:223
  114.5 1.0 copy-done.22
  115.5 0.5 fold.11
  115.9 1.7 collective-permute-start.18
  117.7 12.3 %collective-permute-done.16.landed = s16[256,512]{1,0:T(8,128)(2,1)} collective-permute-done((s16[256,512]{1,0:T(8,128)(2,1)}, s16[256,512]{1,0:T(8,128)(2,1)}, u32[]{:S(2)}, u32[]{:S(2)}) %collective-permute-start.16) | collective-permute-done | bytes 262176 | tf_op jit(solution)/shard_map/ppermute | solution.py:223
  130.0 1.2 finish.2
  131.1 4.6 %collective-permute-done.18.landed.refs_1_ = s16[256,640]{1,0:T(8,128)(2,1)S(1)} collective-permute-done((s16[256,640]{1,0:T(8,128)(2,1)S(1)}, s16[256,640]{1,0:T(8,128)(2,1)S(1)}, u32[]{:S(2)}, u32[]{:S(2)}) %collective-permute-start.18) | collective-permute-done | bytes 327712 | tf_op jit(solution)/shard_map/ppermute | solution.py:223
  136.1 0.8 collective-permute-done.19
  137.2 0.7 slice_reduce_fusion
  138.7 8.4 %attend.1 = bf16[16,96,128]{2,1,0:T(8,128)(2,1)S(1)} custom-call(s32[24]{0:T(128)S(1)} %get-tuple-element.69.slot_request, bf16[16,96,128]{2,1,0:T(8,128)(2,1)S(1)} %bitcast.55, bf16[16,16,128]{2,1,0:T(8,128)(2,1)S(1)} %pad.12.new_keys, bf16[16,16,128]{2,1,0:T(8,128)(2,1)S(1)} %pad.13.new_values, bf16[8,400,256]{2,1,0:T(8,128)(2,1)S(1)} %pack.3.refs_0_.own, ...), custom_call_target="tpu_custom_call" | custom-call | flops 1 | bytes 1 | tf_op jit(solution)/shard_map/attend/pallas_call | solution.py:661
  147.2 2.0 collective-permute-start.22
  149.3 1.4 collective-permute-start.23
  150.7 13.9 %collective-permute-done.21.refs_0_ = bf16[192,1024]{1,0:T(8,128)(2,1)S(1)} collective-permute-done((bf16[192,1024]{1,0:T(8,128)(2,1)S(1)}, bf16[192,1024]{1,0:T(8,128)(2,1)S(1)}, u32[]{:S(2)}, u32[]{:S(2)}) %collective-permute-start.21) | collective-permute-done | bytes 393248 | tf_op jit(solution)/shard_map/ppermute | solution.py:223
  164.6 4.9 %collective-permute-done.23.refs_2_ = bf16[192,1024]{1,0:T(8,128)(2,1)S(1)} collective-permute-done((bf16[192,1024]{1,0:T(8,128)(2,1)S(1)}, bf16[192,1024]{1,0:T(8,128)(2,1)S(1)}, u32[]{:S(2)}, u32[]{:S(2)}) %collective-permute-start.23) | collective-permute-done | bytes 393248 | tf_op jit(solution)/shard_map/ppermute | solution.py:223
  170.2 1.8 collective-permute-start.25
  172.1 3.4 %mix.4.refs_3_ = f32[192,1024]{1,0:T(8,128)S(1)} custom-call(s32[2]{0:T(128)S(1)} %pad_add_fusion.1.places, bf16[192,1024]{1,0:T(8,128)(2,1)S(1)} %together.6.refs_0_, bf16[192,1024]{1,0:T(8,128)(2,1)S(1)} %collective-permute-done.24.refs_3_.refs_1_, bf16[16384,1024]{1,0:T(8,128)(2,1)} %refs_2_.7, bf16[192,1024]{1,0:T(8,128)(2,1)S(1)} %bitcast.49), custom_call_target="tpu_custom_call" | custom-call | flops 1 | bytes 1 | tf_op jit(solution)/shard_map/mix/pallas_call | solution.py:509
  175.5 7.0 %mix.5.refs_2_.refs_3_ = f32[192,1024]{1,0:T(8,128)S(1)} custom-call(s32[6]{0:T(128)S(1)} %stack.82.places, bf16[3,192,1024]{2,1,0:T(8,128)(2,1)S(1)} %get-tuple-element.66.refs_0_, bf16[3,192,1024]{2,1,0:T(8,128)(2,1)} %collective-permute-done.28.refs_1_, bf16[16384,1024]{1,0:T(8,128)(2,1)} %refs_2_.7, f32[192,1024]{1,0:T(8,128)S(1)} %mix.4.refs_3_), custom_call_target="tpu_custom_call" | custom-call | flops 1 | bytes 1 | tf_op jit(solution)/shard_map/mix/pallas_call | solution.py:509
  182.5 0.9 collective-permute-done.25.refs_1_
  183.4 6.4 %collective-permute-done.27.refs_0_ = bf16[2,192,1024]{2,1,0:T(8,128)(2,1)} collective-permute-done((bf16[2,192,1024]{2,1,0:T(8,128)(2,1)S(1)}, bf16[2,192,1024]{2,1,0:T(8,128)(2,1)}, u32[]{:S(2)}, u32[]{:S(2)}) %collective-permute-start.27) | collective-permute-done | bytes 786464 | tf_op jit(solution)/shard_map/ppermute | solution.py:223
  189.8 1.3 pack.5.refs_0_
  191.7 2.5 %collective-permute-done.29.refs_1_ = bf16[3,192,1024]{2,1,0:T(8,128)(2,1)} collective-permute-done((bf16[3,192,1024]{2,1,0:T(8,128)(2,1)S(1)}, bf16[3,192,1024]{2,1,0:T(8,128)(2,1)}, u32[]{:S(2)}, u32[]{:S(2)}) %collective-permute-start.29) | collective-permute-done | bytes 1179680 | tf_op jit(solution)/shard_map/ppermute | solution.py:223
  194.2 7.0 %mix.6.refs_1_.refs_3_ = f32[192,1024]{1,0:T(8,128)S(1)} custom-call(s32[6]{0:T(128)S(1)} %stack.75.places, bf16[3,192,1024]{2,1,0:T(8,128)(2,1)S(1)} %pack.5.refs_0_, bf16[3,192,1024]{2,1,0:T(8,128)(2,1)} %collective-permute-done.29.refs_1_, bf16[16384,1024]{1,0:T(8,128)(2,1)} %refs_2_.7, f32[192,1024]{1,0:T(8,128)S(1)} %mix.5.refs_2_.refs_3_), custom_call_target="tpu_custom_call" | custom-call | flops 1 | bytes 1 | tf_op jit(solution)/shard_map/mix/pallas_call | solution.py:509
  201.2 1.8 collective-permute-done.26.refs_0_
  203.0 1.6 collective-permute-done.30.refs_1_
  204.7 4.1 %mix.7 = bf16[192,1024]{1,0:T(8,128)(2,1)} custom-call(s32[2]{0:T(128)S(1)} %pad_add_fusion.places, bf16[192,1024]{1,0:T(8,128)(2,1)S(1)} %together.7.refs_0_, bf16[192,1024]{1,0:T(8,128)(2,1)S(1)} %collective-permute-done.30.refs_1_, bf16[16384,1024]{1,0:T(8,128)(2,1)} %refs_2_.7, f32[192,1024]{1,0:T(8,128)S(1)} %mix.6.refs_1_.refs_3_), custom_call_target="tpu_custom_call" | custom-call | flops 1 | bytes 1 | tf_op jit(solution)/shard_map/mix/pallas_call | solution.py:509
  (132 shorter events, 5.1 us)
Async XLA Ops:
  0.0 22.4 %copy-start.4 = (bf16[2,96,1024]{2,1,0:T(8,128)(2,1)S(1)}, bf16[2,96,1024]{2,1,0:T(8,128)(2,1)}, u32[]{:S(2)}) copy-start(bf16[2,96,1024]{2,1,0:T(8,128)(2,1)} %param.8) | copy-start | bytes 1179652
  1.2 4.6 %collective-permute-start = (f32[2,96]{1,0:T(2,128)S(1)}, f32[2,96]{1,0:T(2,128)S(1)}, u32[]{:S(2)}, u32[]{:S(2)}) collective-permute-start(f32[2,96]{1,0:T(2,128)S(1)} %fusion), channel_id=1, source_target_pairs={{0,2},{1,3},{2,0},{3,1},{4,6},{5,7},{6,4},{7,5},{8,10},{9,11},{10,... | collective-permute-start | bytes 2312 | tf_op jit(solution)/shard_map/ppermute | solution.py:223
  5.8 1.1 collective-permute-start.1
  7.0 3.6 %collective-permute-start.2 = (f32[2,96]{1,0:T(2,128)S(1)}, f32[2,96]{1,0:T(2,128)S(1)}, u32[]{:S(2)}, u32[]{:S(2)}) collective-permute-start(f32[2,96]{1,0:T(2,128)S(1)} %add.138), channel_id=1, source_target_pairs={{0,4},{1,5},{2,6},{3,7},{4,0},{5,1},{6,2},{7,3},{8,12},{9,13},{10,... | collective-permute-start | bytes 2312 | tf_op jit(solution)/shard_map/ppermute | solution.py:223
  10.6 11.6 %collective-permute-start.3 = (f32[2,96]{1,0:T(2,128)S(1)}, f32[2,96]{1,0:T(2,128)S(1)}, u32[]{:S(2)}, u32[]{:S(2)}) collective-permute-start(f32[2,96]{1,0:T(2,128)S(1)} %add.139), channel_id=1, source_target_pairs={{0,8},{1,9},{2,10},{3,11},{4,12},{5,13},{6,14},{7,15},{8,0},{9,1},... | collective-permute-start | bytes 2312 | tf_op jit(solution)/shard_map/ppermute | solution.py:223
  13.6 1.4 copy-start.6
  15.2 16.8 %copy-start.19 = (bf16[400,256]{1,0:T(8,128)(2,1)}, bf16[400,256]{1,0:T(8,128)(2,1)S(1)}, u32[]{:S(2)}) copy-start(bf16[400,256]{1,0:T(8,128)(2,1)S(1)} %get-tuple-element.36.refs_0_) | copy-start | bytes 614404
  15.2 16.8 %collective-permute-start.5 = (bf16[400,256]{1,0:T(8,128)(2,1)S(1)}, bf16[400,256]{1,0:T(8,128)(2,1)S(1)}, u32[]{:S(2)}, u32[]{:S(2)}) collective-permute-start(bf16[400,256]{1,0:T(8,128)(2,1)S(1)} %get-tuple-element.39), channel_id=1, source_target_pairs={{0,2},{1,3},{2,0},{3,1},{4,6},{5,7},{6,4},{7,5},{8,10},{9,11},{10,... | collective-permute-start | bytes 614408 | tf_op jit(solution)/shard_map/ppermute | solution.py:223
  16.8 15.2 %collective-permute-start.6 = (bf16[400,256]{1,0:T(8,128)(2,1)S(1)}, bf16[400,256]{1,0:T(8,128)(2,1)S(1)}, u32[]{:S(2)}, u32[]{:S(2)}) collective-permute-start(bf16[400,256]{1,0:T(8,128)(2,1)S(1)} %get-tuple-element.40), channel_id=1, source_target_pairs={{0,6},{1,7},{2,4},{3,5},{4,2},{5,3},{6,0},{7,1},{8,14},{9,15},{10,... | collective-permute-start | bytes 614408 | tf_op jit(solution)/shard_map/ppermute | solution.py:223
  18.3 24.7 %collective-permute-start.7 = (bf16[400,256]{1,0:T(8,128)(2,1)S(1)}, bf16[400,256]{1,0:T(8,128)(2,1)S(1)}, u32[]{:S(2)}, u32[]{:S(2)}) collective-permute-start(bf16[400,256]{1,0:T(8,128)(2,1)S(1)} %get-tuple-element.44), channel_id=1, source_target_pairs={{0,8},{1,9},{2,10},{3,11},{4,12},{5,13},{6,14},{7,15},{8,0},{9,1},... | collective-permute-start | bytes 614408 | tf_op jit(solution)/shard_map/ppermute | solution.py:223
  18.6 25.8 %collective-permute-start.8 = (bf16[400,256]{1,0:T(8,128)(2,1)S(1)}, bf16[400,256]{1,0:T(8,128)(2,1)S(1)}, u32[]{:S(2)}, u32[]{:S(2)}) collective-permute-start(bf16[400,256]{1,0:T(8,128)(2,1)S(1)} %get-tuple-element.45), channel_id=1, source_target_pairs={{0,10},{1,11},{2,8},{3,9},{4,14},{5,15},{6,12},{7,13},{8,2},{9,3},... | collective-permute-start | bytes 614408 | tf_op jit(solution)/shard_map/ppermute | solution.py:223
  22.2 22.3 %collective-permute-start.9 = (bf16[400,256]{1,0:T(8,128)(2,1)S(1)}, bf16[400,256]{1,0:T(8,128)(2,1)S(1)}, u32[]{:S(2)}, u32[]{:S(2)}) collective-permute-start(bf16[400,256]{1,0:T(8,128)(2,1)S(1)} %get-tuple-element.46), channel_id=1, source_target_pairs={{0,12},{1,13},{2,14},{3,15},{4,8},{5,9},{6,10},{7,11},{8,4},{9,5},... | collective-permute-start | bytes 614408 | tf_op jit(solution)/shard_map/ppermute | solution.py:223
  32.0 11.0 %copy-start.7 = (bf16[400,256]{1,0:T(8,128)(2,1)}, bf16[400,256]{1,0:T(8,128)(2,1)S(1)}, u32[]{:S(2)}) copy-start(bf16[400,256]{1,0:T(8,128)(2,1)S(1)} %collective-permute-done.6.refs_2_.refs_3_) | copy-start | bytes 614404
  43.0 1.5 copy-start.9
  44.4 0.7 copy-start.11
  44.4 0.8 copy-start.13
  44.4 1.3 copy-start.26
  44.5 5.3 %copy-start.25 = (s32[16,16]{1,0:T(8,128)S(1)}, s32[16,16]{1,0:T(8,128)}, u32[]{:S(2)}) copy-start(s32[16,16]{1,0:T(8,128)} %param.15) | copy-start | bytes 3076
  45.2 14.0 %collective-permute-start.11 = (s16[1936,640]{1,0:T(8,128)(2,1)}, s16[1936,640]{1,0:T(8,128)(2,1)}, u32[]{:S(2)}, u32[]{:S(2)}) collective-permute-start(s16[1936,640]{1,0:T(8,128)(2,1)} %get-tuple-element.47.refs_0_), channel_id=1, source_target_pairs={{0,1},{1,0},{2,3},{3,2},{4,5},{5,4},{6,7},{7,6},{8,9},{9,8},{10,11... | collective-permute-start | bytes 7434248 | tf_op jit(solution)/shard_map/ppermute | solution.py:223
  45.2 7.4 %collective-permute-start.4 = (s16[1936,512]{1,0:T(8,128)(2,1)}, s16[1936,512]{1,0:T(8,128)(2,1)S(1)}, u32[]{:S(2)}, u32[]{:S(2)}) collective-permute-start(s16[1936,512]{1,0:T(8,128)(2,1)} %get-tuple-element.38), channel_id=1, source_target_pairs={{0,1},{1,0},{2,3},{3,2},{4,5},{5,4},{6,7},{7,6},{8,9},{9,8},{10,11... | collective-permute-start | bytes 5947400 | tf_op jit(solution)/shard_map/ppermute | solution.py:223
  45.8 12.9 %collective-permute-start.12 = (bf16[400,256]{1,0:T(8,128)(2,1)S(1)}, bf16[400,256]{1,0:T(8,128)(2,1)S(1)}, u32[]{:S(2)}, u32[]{:S(2)}) collective-permute-start(bf16[400,256]{1,0:T(8,128)(2,1)S(1)} %get-tuple-element.51), channel_id=1, source_target_pairs={{0,4},{1,5},{2,6},{3,7},{4,0},{5,1},{6,2},{7,3},{8,12},{9,13},{10,... | collective-permute-start | bytes 614408 | tf_op jit(solution)/shard_map/ppermute | solution.py:223
  48.2 11.0 %collective-permute-start.13 = (bf16[400,256]{1,0:T(8,128)(2,1)S(1)}, bf16[400,256]{1,0:T(8,128)(2,1)S(1)}, u32[]{:S(2)}, u32[]{:S(2)}) collective-permute-start(bf16[400,256]{1,0:T(8,128)(2,1)S(1)} %get-tuple-element.52), channel_id=1, source_target_pairs={{0,14},{1,15},{2,12},{3,13},{4,10},{5,11},{6,8},{7,9},{8,6},{9,7},... | collective-permute-start | bytes 614408 | tf_op jit(solution)/shard_map/ppermute | solution.py:223
  56.3 25.0 %collective-permute-start.10 = (s16[976,512]{1,0:T(8,128)(2,1)S(1)}, s16[976,512]{1,0:T(8,128)(2,1)S(1)}, u32[]{:S(2)}, u32[]{:S(2)}) collective-permute-start(s16[976,512]{1,0:T(8,128)(2,1)S(1)} %get-tuple-element.49), channel_id=1, source_target_pairs={{0,4},{1,5},{2,6},{3,7},{4,0},{5,1},{6,2},{7,3},{8,12},{9,13},{10,... | collective-permute-start | bytes 2998280 | tf_op jit(solution)/shard_map/ppermute | solution.py:223
  58.7 6.2 %copy-start.15 = (bf16[400,256]{1,0:T(8,128)(2,1)}, bf16[400,256]{1,0:T(8,128)(2,1)S(1)}, u32[]{:S(2)}) copy-start(bf16[400,256]{1,0:T(8,128)(2,1)S(1)} %collective-permute-done.12.refs_1_.refs_2_) | copy-start | bytes 614404
  59.2 5.7 %copy-start.17 = (bf16[400,256]{1,0:T(8,128)(2,1)}, bf16[400,256]{1,0:T(8,128)(2,1)S(1)}, u32[]{:S(2)}) copy-start(bf16[400,256]{1,0:T(8,128)(2,1)S(1)} %collective-permute-done.13.refs_2_.refs_7_) | copy-start | bytes 614404
  65.0 30.7 %collective-permute-start.15 = (s16[976,640]{1,0:T(8,128)(2,1)}, s16[976,640]{1,0:T(8,128)(2,1)S(1)}, u32[]{:S(2)}, u32[]{:S(2)}) collective-permute-start(s16[976,640]{1,0:T(8,128)(2,1)} %get-tuple-element.56), channel_id=1, source_target_pairs={{0,2},{1,3},{2,0},{3,1},{4,6},{5,7},{6,4},{7,5},{8,10},{9,11},{10,... | collective-permute-start | bytes 3747848 | tf_op jit(solution)/shard_map/ppermute | solution.py:223
  83.0 0.9 copy-start.2
  83.9 21.3 %collective-permute-start.14 = (s16[496,512]{1,0:T(8,128)(2,1)}, s16[496,512]{1,0:T(8,128)(2,1)}, u32[]{:S(2)}, u32[]{:S(2)}) collective-permute-start(s16[496,512]{1,0:T(8,128)(2,1)} %get-tuple-element.55), channel_id=1, source_target_pairs={{0,2},{1,3},{2,0},{3,1},{4,6},{5,7},{6,4},{7,5},{8,10},{9,11},{10,... | collective-permute-start | bytes 1523720 | tf_op jit(solution)/shard_map/ppermute | solution.py:223
  95.6 1.1 copy-start.3
  96.8 3.4 %copy-start.8 = (bf16[400,256]{1,0:T(8,128)(2,1)S(1)}, bf16[400,256]{1,0:T(8,128)(2,1)}, u32[]{:S(2)}) copy-start(bf16[400,256]{1,0:T(8,128)(2,1)} %copy-done.7) | copy-start | bytes 614404
  96.8 3.4 %copy-start.10 = (bf16[400,256]{1,0:T(8,128)(2,1)S(1)}, bf16[400,256]{1,0:T(8,128)(2,1)}, u32[]{:S(2)}) copy-start(bf16[400,256]{1,0:T(8,128)(2,1)} %copy-done.9) | copy-start | bytes 614404
  96.8 3.4 %copy-start.12 = (bf16[400,256]{1,0:T(8,128)(2,1)S(1)}, bf16[400,256]{1,0:T(8,128)(2,1)}, u32[]{:S(2)}) copy-start(bf16[400,256]{1,0:T(8,128)(2,1)} %copy-done.11) | copy-start | bytes 614404
  96.8 3.4 %copy-start.14 = (bf16[400,256]{1,0:T(8,128)(2,1)S(1)}, bf16[400,256]{1,0:T(8,128)(2,1)}, u32[]{:S(2)}) copy-start(bf16[400,256]{1,0:T(8,128)(2,1)} %copy-done.13) | copy-start | bytes 614404
  96.8 3.4 %copy-start.16 = (bf16[400,256]{1,0:T(8,128)(2,1)S(1)}, bf16[400,256]{1,0:T(8,128)(2,1)}, u32[]{:S(2)}) copy-start(bf16[400,256]{1,0:T(8,128)(2,1)} %copy-done.15) | copy-start | bytes 614404
  96.8 3.4 %copy-start.18 = (bf16[400,256]{1,0:T(8,128)(2,1)S(1)}, bf16[400,256]{1,0:T(8,128)(2,1)}, u32[]{:S(2)}) copy-start(bf16[400,256]{1,0:T(8,128)(2,1)} %copy-done.17) | copy-start | bytes 614404
  96.8 3.4 %copy-start.20 = (bf16[400,256]{1,0:T(8,128)(2,1)S(1)}, bf16[400,256]{1,0:T(8,128)(2,1)}, u32[]{:S(2)}) copy-start(bf16[400,256]{1,0:T(8,128)(2,1)} %copy-done.19) | copy-start | bytes 614404
  98.8 1.5 copy-start
  98.8 15.7 %collective-permute-start.17 = (s16[496,640]{1,0:T(8,128)(2,1)}, s16[496,640]{1,0:T(8,128)(2,1)S(1)}, u32[]{:S(2)}, u32[]{:S(2)}) collective-permute-start(s16[496,640]{1,0:T(8,128)(2,1)} %get-tuple-element.60), channel_id=1, source_target_pairs={{0,4},{1,5},{2,6},{3,7},{4,0},{5,1},{6,2},{7,3},{8,12},{9,13},{10,... | collective-permute-start | bytes 1904648 | tf_op jit(solution)/shard_map/ppermute | solution.py:223
  105.3 9.2 %copy-start.1 = (f32[2,192,640]{2,1,0:T(8,128)S(1)}, f32[2,192,640]{2,1,0:T(8,128)}, u32[]{:S(2)}) copy-start(f32[2,192,640]{2,1,0:T(8,128)} %copy-done) | copy-start | bytes 2949124
  107.5 0.7 copy-start.21
  108.2 21.7 %collective-permute-start.16 = (s16[256,512]{1,0:T(8,128)(2,1)}, s16[256,512]{1,0:T(8,128)(2,1)}, u32[]{:S(2)}, u32[]{:S(2)}) collective-permute-start(s16[256,512]{1,0:T(8,128)(2,1)} %get-tuple-element.59), channel_id=1, source_target_pairs={{0,8},{1,9},{2,10},{3,11},{4,12},{5,13},{6,14},{7,15},{8,0},{9,1},... | collective-permute-start | bytes 786440 | tf_op jit(solution)/shard_map/ppermute | solution.py:223
  110.6 26.6 %collective-permute-start.20 = (bf16[8,400,256]{2,1,0:T(8,128)(2,1)S(1)}, bf16[8,400,256]{2,1,0:T(8,128)(2,1)}, u32[]{:S(2)}, u32[]{:S(2)}) collective-permute-start(bf16[8,400,256]{2,1,0:T(8,128)(2,1)S(1)} %pack.3.refs_0_.own), channel_id=1, source_target_pairs={{0,1},{1,0},{2,3},{3,2},{4,5},{5,4},{6,7},{7,6},{8,9},{9,8},{10,11... | collective-permute-start | bytes 4915208 | tf_op jit(solution)/shard_map/ppermute | solution.py:223
  114.5 1.0 copy-start.22
  115.5 14.5 %copy-start.23 = (f32[1,192,512]{2,1,0:T(8,128)S(1)}, f32[1,192,512]{2,1,0:T(8,128)}, u32[]{:S(2)}) copy-start(f32[1,192,512]{2,1,0:T(8,128)} %copy-done.21) | copy-start | bytes 1179652
  115.5 14.5 %copy-start.24 = (f32[192,128]{1,0:T(8,128)S(1)}, f32[192,128]{1,0:T(8,128)}, u32[]{:S(2)}) copy-start(f32[192,128]{1,0:T(8,128)} %get-tuple-element.80.sine) | copy-start | bytes 294916
  115.9 19.8 %collective-permute-start.18 = (s16[256,640]{1,0:T(8,128)(2,1)S(1)}, s16[256,640]{1,0:T(8,128)(2,1)S(1)}, u32[]{:S(2)}, u32[]{:S(2)}) collective-permute-start(s16[256,640]{1,0:T(8,128)(2,1)S(1)} %get-tuple-element.63), channel_id=1, source_target_pairs={{0,8},{1,9},{2,10},{3,11},{4,12},{5,13},{6,14},{7,15},{8,0},{9,1},... | collective-permute-start | bytes 983048 | tf_op jit(solution)/shard_map/ppermute | solution.py:223
  135.7 1.2 collective-permute-start.19
  147.2 25.0 %copy-start.5 = (bf16[2,96,1024]{2,1,0:T(8,128)(2,1)S(1)}, bf16[2,96,1024]{2,1,0:T(8,128)(2,1)}, u32[]{:S(2)}) copy-start(bf16[2,96,1024]{2,1,0:T(8,128)(2,1)} %param.8) | copy-start | bytes 1179652
  147.2 17.4 %collective-permute-start.21 = (bf16[192,1024]{1,0:T(8,128)(2,1)S(1)}, bf16[192,1024]{1,0:T(8,128)(2,1)S(1)}, u32[]{:S(2)}, u32[]{:S(2)}) collective-permute-start(bf16[192,1024]{1,0:T(8,128)(2,1)S(1)} %bitcast.50), channel_id=1, source_target_pairs={{0,4},{1,5},{2,6},{3,7},{4,0},{5,1},{6,2},{7,3},{8,12},{9,13},{10,... | collective-permute-start | bytes 1179656 | tf_op jit(solution)/shard_map/ppermute | solution.py:223
  147.2 17.4 %collective-permute-start.22 = (bf16[192,1024]{1,0:T(8,128)(2,1)S(1)}, bf16[192,1024]{1,0:T(8,128)(2,1)S(1)}, u32[]{:S(2)}, u32[]{:S(2)}) collective-permute-start(bf16[192,1024]{1,0:T(8,128)(2,1)S(1)} %bitcast.51), channel_id=1, source_target_pairs={{0,2},{1,3},{2,0},{3,1},{4,6},{5,7},{6,4},{7,5},{8,10},{9,11},{10,... | collective-permute-start | bytes 1179656 | tf_op jit(solution)/shard_map/ppermute | solution.py:223
  149.3 20.3 %collective-permute-start.23 = (bf16[192,1024]{1,0:T(8,128)(2,1)S(1)}, bf16[192,1024]{1,0:T(8,128)(2,1)S(1)}, u32[]{:S(2)}, u32[]{:S(2)}) collective-permute-start(bf16[192,1024]{1,0:T(8,128)(2,1)S(1)} %bitcast.52), channel_id=1, source_target_pairs={{0,8},{1,9},{2,10},{3,11},{4,12},{5,13},{6,14},{7,15},{8,0},{9,1},... | collective-permute-start | bytes 1179656 | tf_op jit(solution)/shard_map/ppermute | solution.py:223
  150.7 18.9 %collective-permute-start.24 = (bf16[192,1024]{1,0:T(8,128)(2,1)S(1)}, bf16[192,1024]{1,0:T(8,128)(2,1)S(1)}, u32[]{:S(2)}, u32[]{:S(2)}) collective-permute-start(bf16[192,1024]{1,0:T(8,128)(2,1)S(1)} %bitcast.53), channel_id=1, source_target_pairs={{0,1},{1,0},{2,3},{3,2},{4,5},{5,4},{6,7},{7,6},{8,9},{9,8},{10,11... | collective-permute-start | bytes 1179656 | tf_op jit(solution)/shard_map/ppermute | solution.py:223
  169.7 5.8 %collective-permute-start.28 = (bf16[3,192,1024]{2,1,0:T(8,128)(2,1)S(1)}, bf16[3,192,1024]{2,1,0:T(8,128)(2,1)}, u32[]{:S(2)}, u32[]{:S(2)}) collective-permute-start(bf16[3,192,1024]{2,1,0:T(8,128)(2,1)S(1)} %get-tuple-element.66.refs_0_), channel_id=1, source_target_pairs={{0,1},{1,0},{2,3},{3,2},{4,5},{5,4},{6,7},{7,6},{8,9},{9,8},{10,11... | collective-permute-start | bytes 3538952 | tf_op jit(solution)/shard_map/ppermute | solution.py:223
  169.8 20.1 %collective-permute-start.27 = (bf16[2,192,1024]{2,1,0:T(8,128)(2,1)S(1)}, bf16[2,192,1024]{2,1,0:T(8,128)(2,1)}, u32[]{:S(2)}, u32[]{:S(2)}) collective-permute-start(bf16[2,192,1024]{2,1,0:T(8,128)(2,1)S(1)} %get-tuple-element.65.refs_1_), channel_id=1, source_target_pairs={{0,2},{1,3},{2,0},{3,1},{4,6},{5,7},{6,4},{7,5},{8,10},{9,11},{10,... | collective-permute-start | bytes 2359304 | tf_op jit(solution)/shard_map/ppermute | solution.py:223
  170.2 13.2 %collective-permute-start.25 = (bf16[192,1024]{1,0:T(8,128)(2,1)S(1)}, bf16[192,1024]{1,0:T(8,128)(2,1)}, u32[]{:S(2)}, u32[]{:S(2)}) collective-permute-start(bf16[192,1024]{1,0:T(8,128)(2,1)S(1)} %together.6.refs_0_), channel_id=1, source_target_pairs={{0,12},{1,13},{2,14},{3,15},{4,8},{5,9},{6,10},{7,11},{8,4},{9,5},... | collective-permute-start | bytes 1179656 | tf_op jit(solution)/shard_map/ppermute | solution.py:223
  191.1 3.0 %collective-permute-start.29 = (bf16[3,192,1024]{2,1,0:T(8,128)(2,1)S(1)}, bf16[3,192,1024]{2,1,0:T(8,128)(2,1)}, u32[]{:S(2)}, u32[]{:S(2)}) collective-permute-start(bf16[3,192,1024]{2,1,0:T(8,128)(2,1)S(1)} %pack.5.refs_0_), channel_id=1, source_target_pairs={{0,1},{1,0},{2,3},{3,2},{4,5},{5,4},{6,7},{7,6},{8,9},{9,8},{10,11... | collective-permute-start | bytes 3538952 | tf_op jit(solution)/shard_map/ppermute | solution.py:223
  191.2 11.7 %collective-permute-start.26 = (bf16[192,1024]{1,0:T(8,128)(2,1)}, bf16[192,1024]{1,0:T(8,128)(2,1)S(1)}, u32[]{:S(2)}, u32[]{:S(2)}) collective-permute-start(bf16[192,1024]{1,0:T(8,128)(2,1)} %collective-permute-done.25.refs_1_), channel_id=1, source_target_pairs={{0,2},{1,3},{2,0},{3,1},{4,6},{5,7},{6,4},{7,5},{8,10},{9,11},{10,... | collective-permute-start | bytes 1179656 | tf_op jit(solution)/shard_map/ppermute | solution.py:223
  203.0 1.7 collective-permute-start.30

commit v13 on v12

--- a/solution.py
+++ b/solution.py
@@ -214,6 +214,7 @@
 PACKED = 16 // LOW_BITS
 LEVELS = 32600.0 * 2**LOW_BITS
 POWER_STEPS = 8.0
+FIRST = (1, 3, 4)
 TILE = 16
 MESH_BITS = (1, 2, 4, 8)
 
@@ -345,7 +346,7 @@
         sent[pl.ds(KVH * rows, TILE), :] = powers[...].astype(jnp.int32).astype(jnp.int16)
 
 
-def project(core, normed, qkv_weight, part, after):
+def project(core, normed, qkv_weight, part, cost, after):
     rows, width = normed.shape
     columns = PART_HEADS[part] * HD + (HD if part == 0 else 0)
     sent_rows = KVH * coded_rows(rows) + TILE
@@ -371,7 +372,7 @@
             jax.ShapeDtypeStruct((sent_rows, columns), jnp.int16),
         ],
         compiler_params=pltpu.CompilerParams(vmem_limit_bytes=VMEM_LIMIT),
-        cost_estimate=SHORT,
+        cost_estimate=cost,
         name="project",
     )(core, normed, qkv_weight, *after)
 
@@ -774,13 +775,13 @@
 
     for k in (1, 3, 4, 5, 6):
         handed(k)
-    held_a, sent_a = project(bits[0], normed, qkv_weight, 0, cache_pieces[:1])
+    held_a, sent_a = project(bits[0], normed, qkv_weight, 0, SHORT, cache_pieces[:1])
     core_a = swap(sent_a, 1)
-    held_b, sent_b = project(
-        bits[0], normed, qkv_weight, 1, [held_a, cache_pieces[1], cache_pieces[3]]
-    )
+    first = [held_a] + [cache_pieces[k] for k in FIRST]
+    held_b, sent_b = project(bits[0], normed, qkv_weight, 1, LONG, first)
     sent_b, cache_pieces[2], cache_pieces[7] = together(
-        [sent_b, cache_pieces[2], cache_pieces[7]], cache_pieces[4:7]
+        [sent_b, cache_pieces[2], cache_pieces[7]],
+        [core_a] + [cache_pieces[k] for k in (1, 3, 4, 5, 6) if k not in FIRST],
     )
     core_b = swap(sent_b, 1)
     for k in (2, 7):

time: 210 us -> 213 us (1.014)
  transfers between devices with their start and end apart: 31 -> 31, of which waited for: 20 -> 19; matrix products, arithmetic and copies ran while one was open for 3% -> 3% of each run, Pallas kernels for 26% -> 26%
where the time goes in v13:
time: 213 us; the launch traced here: 212 us
  waiting for transfers between devices  90.7 us (43%)
  Pallas kernels  68.4 us (32%)
  starting transfers between devices  36.9 us (17%)
  local copies, waits for them, and re-layouts  9.67 us (5%)
  other arithmetic  5.91 us (3%)
    ppermute x31, waiting for transfers between devices, swap(): return lax.ppermute(value, 'tensor', [(i, i ^ bit) for i in range(devices)])  90.7 us
    ppermute x31, starting transfers between devices, swap(): return lax.ppermute(value, 'tensor', [(i, i ^ bit) for i in range(devices)])  36.9 us
    pallas_call x4, Pallas kernels, mix(): pl.pallas_call(functools.partial(mix_kernel, len(pieces)), in_specs=[pl.B...  21.5 us
    pallas_call x2, Pallas kernels, project(): pl.pallas_call(functools.partial(project_kernel, part), grid_spec=pltpu.P...  19.7 us
    pallas_call x6, Pallas kernels, fold(): pl.pallas_call(functools.partial(fold_kernel, steps, low), grid_spec=pltp...  15.8 us
    pallas_call x1, Pallas kernels, attend(): pl.pallas_call(attend_kernel, in_specs=[pl.BlockSpec(memory_space=pltpu.S...  8.39 us
    unnamed x56, local copies, waits for them, and re-layouts  6.82 us
  transfers between devices with their start and end apart: 31, of which 19 were waited for; matrix products, arithmetic and copies ran while one was open for 3% of the time, Pallas kernels for 26%

profile of v13, /device:TPU:0, one launch (start us, length us, event | category | flops | bytes accessed | tf_op | source)
XLA Modules:
  0.0 212.4 jit_solution(17669528177527647403)
XLA Ops:
  0.0 1.2 fusion
  1.2 3.0 %collective-permute-start = (f32[2,96]{1,0:T(2,128)S(1)}, f32[2,96]{1,0:T(2,128)S(1)}, u32[]{:S(2)}, u32[]{:S(2)}) collective-permute-start(f32[2,96]{1,0:T(2,128)S(1)} %fusion), channel_id=1, source_target_pairs={{0,2},{1,3},{2,0},{3,1},{4,6},{5,7},{6,4},{7,5},{8,10},{9,11},{10,... | collective-permute-start | bytes 2312 | tf_op jit(solution)/shard_map/ppermute | solution.py:224
  4.3 1.5 collective-permute-done
  5.8 1.1 collective-permute-done.1
  7.0 2.1 collective-permute-start.2
  9.0 0.8 reshape.240
  9.8 0.7 convert_element_type.29
  10.6 3.0 %collective-permute-start.3 = (f32[2,96]{1,0:T(2,128)S(1)}, f32[2,96]{1,0:T(2,128)S(1)}, u32[]{:S(2)}, u32[]{:S(2)}) collective-permute-start(f32[2,96]{1,0:T(2,128)S(1)} %add.139), channel_id=1, source_target_pairs={{0,8},{1,9},{2,10},{3,11},{4,12},{5,13},{6,14},{7,15},{8,0},{9,1},... | collective-permute-start | bytes 2312 | tf_op jit(solution)/shard_map/ppermute | solution.py:224
  13.6 1.4 copy-done.6
  15.2 1.6 collective-permute-start.5
  16.8 1.5 collective-permute-start.6
  18.3 0.3 collective-permute-start.7
  18.8 8.6 %project.2 = (f32[8,192,512]{2,1,0:T(8,128)}, s16[1936,512]{1,0:T(8,128)(2,1)S(1)}) custom-call(s32[1]{0:T(128)} %bitcast.2.core, bf16[192,1024]{1,0:T(8,128)(2,1)S(1)} %bitcast.53, bf16[1024,18432]{1,0:T(8,128)(2,1)} %weights.3, bf16[400,256]{1,0:T(8,128)(2,1)S(1)} %get-tuple-element.36.refs_0_), custom_call_target="tpu_custom_call" | custom-call | flops 1 | bytes 1 | tf_op jit(solution)/shard_map/project/pallas_call | solution.py:353
  27.5 3.6 %collective-permute-start.8 = (bf16[400,256]{1,0:T(8,128)(2,1)S(1)}, bf16[400,256]{1,0:T(8,128)(2,1)S(1)}, u32[]{:S(2)}, u32[]{:S(2)}) collective-permute-start(bf16[400,256]{1,0:T(8,128)(2,1)S(1)} %get-tuple-element.45), channel_id=1, source_target_pairs={{0,10},{1,11},{2,8},{3,9},{4,14},{5,15},{6,12},{7,13},{8,2},{9,3},... | collective-permute-start | bytes 614408 | tf_op jit(solution)/shard_map/ppermute | solution.py:224
  31.4 11.1 %project.3 = (f32[8,192,640]{2,1,0:T(8,128)}, s16[1936,640]{1,0:T(8,128)(2,1)}) custom-call(s32[1]{0:T(128)} %bitcast.2.core, bf16[192,1024]{1,0:T(8,128)(2,1)S(1)} %bitcast.54, bf16[1024,18432]{1,0:T(8,128)(2,1)} %weights.3, f32[8,192,512]{2,1,0:T(8,128)} %get-tuple-element.37.refs_0_.held.held_out, bf16[400,256]{1,0:T(8,128)(2,1)S(1)} %collective-permute-done.5.refs_1_, ...), custom_call_target="tpu_custom_call" | custom-call | flops 20000000000 | bytes 1 | tf_op jit(solution)/shard_map/project/pallas_call | solution.py:353
  42.5 3.0 %collective-permute-done.8.refs_4_.refs_5_ = bf16[400,256]{1,0:T(8,128)(2,1)S(1)} collective-permute-done((bf16[400,256]{1,0:T(8,128)(2,1)S(1)}, bf16[400,256]{1,0:T(8,128)(2,1)S(1)}, u32[]{:S(2)}, u32[]{:S(2)}) %collective-permute-start.8) | collective-permute-done | bytes 204832 | tf_op jit(solution)/shard_map/ppermute | solution.py:224
  45.5 0.6 copy-done.7
  46.3 5.0 %collective-permute-start.12 = (bf16[400,256]{1,0:T(8,128)(2,1)S(1)}, bf16[400,256]{1,0:T(8,128)(2,1)S(1)}, u32[]{:S(2)}, u32[]{:S(2)}) collective-permute-start(bf16[400,256]{1,0:T(8,128)(2,1)S(1)} %get-tuple-element.51), channel_id=1, source_target_pairs={{0,4},{1,5},{2,6},{3,7},{4,0},{5,1},{6,2},{7,3},{8,12},{9,13},{10,... | collective-permute-start | bytes 614408 | tf_op jit(solution)/shard_map/ppermute | solution.py:224
  51.4 2.5 %collective-permute-start.13 = (bf16[400,256]{1,0:T(8,128)(2,1)S(1)}, bf16[400,256]{1,0:T(8,128)(2,1)S(1)}, u32[]{:S(2)}, u32[]{:S(2)}) collective-permute-start(bf16[400,256]{1,0:T(8,128)(2,1)S(1)} %get-tuple-element.52), channel_id=1, source_target_pairs={{0,14},{1,15},{2,12},{3,13},{4,10},{5,11},{6,8},{7,9},{8,6},{9,7},... | collective-permute-start | bytes 614408 | tf_op jit(solution)/shard_map/ppermute | solution.py:224
  54.0 3.7 %fold.6 = (f32[4,192,512]{2,1,0:T(8,128)S(1)}, s16[976,512]{1,0:T(8,128)(2,1)S(1)}) custom-call(s32[1]{0:T(128)} %bitcast.5.bit, f32[8,192,512]{2,1,0:T(8,128)} %get-tuple-element.37.refs_0_.held.held_out, f32[8,192,512]{2,1,0:T(8,128)} %get-tuple-element.37.refs_0_.held.held_out, ...), custom_call_target="tpu_custom_call" | custom-call | flops 1 | bytes 1 | tf_op jit(solution)/shard_map/fold/pallas_call | solution.py:407
  57.8 6.2 %collective-permute-done.13.refs_2_.refs_7_ = bf16[400,256]{1,0:T(8,128)(2,1)S(1)} collective-permute-done((bf16[400,256]{1,0:T(8,128)(2,1)S(1)}, bf16[400,256]{1,0:T(8,128)(2,1)S(1)}, u32[]{:S(2)}, u32[]{:S(2)}) %collective-permute-start.13) | collective-permute-done | bytes 204832 | tf_op jit(solution)/shard_map/ppermute | solution.py:224
  64.1 5.7 %fold.7 = (f32[4,192,640]{2,1,0:T(8,128)S(1)}, s16[976,640]{1,0:T(8,128)(2,1)}) custom-call(s32[1]{0:T(128)} %bitcast.4.bit, f32[8,192,640]{2,1,0:T(8,128)} %get-tuple-element.50.held.held_out, f32[8,192,640]{2,1,0:T(8,128)} %get-tuple-element.50.held.held_out, s16[1936,640]{1,0:T(8,128)(2,1)} %collective-permute-done.11.landed.landed_out.landed_powers, ...), custom_call_target="tpu_custom_call" | custom-call | flops 1 | bytes 1 | tf_op jit(solution)/shard_map/fold/pallas_call | solution.py:407
  69.8 1.6 collective-permute-start.15
  71.7 13.4 %collective-permute-done.10.landed.landed_out.landed_powers = s16[976,512]{1,0:T(8,128)(2,1)S(1)} collective-permute-done((s16[976,512]{1,0:T(8,128)(2,1)S(1)}, s16[976,512]{1,0:T(8,128)(2,1)S(1)}, u32[]{:S(2)}, u32[]{:S(2)}) %collective-permute-start.10) | collective-permute-done | bytes 999456 | tf_op jit(solution)/shard_map/ppermute | solution.py:224
  85.1 1.7 fold.8
  86.8 0.9 copy-done.2
  87.7 0.5 collective-permute-start.14
  88.4 1.1 fusion.5
  89.6 10.9 %collective-permute-done.15.landed.landed_out.landed_powers = s16[976,640]{1,0:T(8,128)(2,1)S(1)} collective-permute-done((s16[976,640]{1,0:T(8,128)(2,1)}, s16[976,640]{1,0:T(8,128)(2,1)S(1)}, u32[]{:S(2)}, u32[]{:S(2)}) %collective-permute-start.15) | collective-permute-done | bytes 1249312 | tf_op jit(solution)/shard_map/ppermute | solution.py:224
  100.5 1.1 copy-done.3
  101.7 2.0 fold.9
  103.8 0.8 copy-done
  104.6 5.2 %collective-permute-done.14.landed.landed_out.landed_powers = s16[496,512]{1,0:T(8,128)(2,1)} collective-permute-done((s16[496,512]{1,0:T(8,128)(2,1)}, s16[496,512]{1,0:T(8,128)(2,1)}, u32[]{:S(2)}, u32[]{:S(2)}) %collective-permute-start.14) | collective-permute-done | bytes 507936 | tf_op jit(solution)/shard_map/ppermute | solution.py:224
  109.8 2.2 %fold.10 = (f32[1,192,512]{2,1,0:T(8,128)S(1)}, s16[256,512]{1,0:T(8,128)(2,1)}) custom-call(s32[1]{0:T(128)} %bitcast.3.bit, f32[2,192,512]{2,1,0:T(8,128)S(1)} %copy-done.3, f32[2,192,512]{2,1,0:T(8,128)S(1)} %copy-done.3, s16[496,512]{1,0:T(8,128)(2,1)} %collective-permute-done.14.landed.landed_out.landed_powers, ...), custom_call_target="tpu_custom_call" | custom-call | flops 1 | bytes 1 | tf_op jit(solution)/shard_map/fold/pallas_call | solution.py:407
  112.0 0.7 copy-done.15
  112.8 1.6 collective-permute-start.16
  114.4 1.8 pad_maximum_fusion
  116.3 2.3 %collective-permute-done.17.landed.landed_out.landed_powers = s16[496,640]{1,0:T(8,128)(2,1)S(1)} collective-permute-done((s16[496,640]{1,0:T(8,128)(2,1)}, s16[496,640]{1,0:T(8,128)(2,1)S(1)}, u32[]{:S(2)}, u32[]{:S(2)}) %collective-permute-start.17) | collective-permute-done | bytes 634912 | tf_op jit(solution)/shard_map/ppermute | solution.py:224
  118.6 1.0 copy-done.16
  119.6 0.5 fold.11
  120.1 3.0 %collective-permute-start.18 = (s16[256,640]{1,0:T(8,128)(2,1)S(1)}, s16[256,640]{1,0:T(8,128)(2,1)S(1)}, u32[]{:S(2)}, u32[]{:S(2)}) collective-permute-start(s16[256,640]{1,0:T(8,128)(2,1)S(1)} %get-tuple-element.63), channel_id=1, source_target_pairs={{0,8},{1,9},{2,10},{3,11},{4,12},{5,13},{6,14},{7,15},{8,0},{9,1},... | collective-permute-start | bytes 983048 | tf_op jit(solution)/shard_map/ppermute | solution.py:224
  123.1 11.4 %collective-permute-done.16.landed = s16[256,512]{1,0:T(8,128)(2,1)} collective-permute-done((s16[256,512]{1,0:T(8,128)(2,1)}, s16[256,512]{1,0:T(8,128)(2,1)}, u32[]{:S(2)}, u32[]{:S(2)}) %collective-permute-start.16) | collective-permute-done | bytes 262176 | tf_op jit(solution)/shard_map/ppermute | solution.py:224
  134.5 1.2 finish.2
  135.7 4.4 %collective-permute-done.18.landed.refs_1_ = s16[256,640]{1,0:T(8,128)(2,1)S(1)} collective-permute-done((s16[256,640]{1,0:T(8,128)(2,1)S(1)}, s16[256,640]{1,0:T(8,128)(2,1)S(1)}, u32[]{:S(2)}, u32[]{:S(2)}) %collective-permute-start.18) | collective-permute-done | bytes 327712 | tf_op jit(solution)/shard_map/ppermute | solution.py:224
  140.5 0.8 collective-permute-done.19
  141.5 0.7 slice_reduce_fusion
  143.0 8.4 %attend.1 = bf16[16,96,128]{2,1,0:T(8,128)(2,1)S(1)} custom-call(s32[24]{0:T(128)S(1)} %get-tuple-element.69.slot_request, bf16[16,96,128]{2,1,0:T(8,128)(2,1)S(1)} %bitcast.55, bf16[16,16,128]{2,1,0:T(8,128)(2,1)S(1)} %pad.12.new_keys, bf16[16,16,128]{2,1,0:T(8,128)(2,1)S(1)} %pad.13.new_values, bf16[8,400,256]{2,1,0:T(8,128)(2,1)S(1)} %pack.3.refs_0_.own, ...), custom_call_target="tpu_custom_call" | custom-call | flops 1 | bytes 1 | tf_op jit(solution)/shard_map/attend/pallas_call | solution.py:662
  151.6 1.1 collective-permute-start.22
  152.7 2.2 %collective-permute-start.23 = (bf16[192,1024]{1,0:T(8,128)(2,1)S(1)}, bf16[192,1024]{1,0:T(8,128)(2,1)S(1)}, u32[]{:S(2)}, u32[]{:S(2)}) collective-permute-start(bf16[192,1024]{1,0:T(8,128)(2,1)S(1)} %bitcast.50), channel_id=1, source_target_pairs={{0,8},{1,9},{2,10},{3,11},{4,12},{5,13},{6,14},{7,15},{8,0},{9,1},... | collective-permute-start | bytes 1179656 | tf_op jit(solution)/shard_map/ppermute | solution.py:224
  154.9 14.1 %collective-permute-done.21.refs_0_ = bf16[192,1024]{1,0:T(8,128)(2,1)S(1)} collective-permute-done((bf16[192,1024]{1,0:T(8,128)(2,1)S(1)}, bf16[192,1024]{1,0:T(8,128)(2,1)S(1)}, u32[]{:S(2)}, u32[]{:S(2)}) %collective-permute-start.21) | collective-permute-done | bytes 393248 | tf_op jit(solution)/shard_map/ppermute | solution.py:224
  169.0 3.9 %collective-permute-done.23.refs_2_ = bf16[192,1024]{1,0:T(8,128)(2,1)S(1)} collective-permute-done((bf16[192,1024]{1,0:T(8,128)(2,1)S(1)}, bf16[192,1024]{1,0:T(8,128)(2,1)S(1)}, u32[]{:S(2)}, u32[]{:S(2)}) %collective-permute-start.23) | collective-permute-done | bytes 393248 | tf_op jit(solution)/shard_map/ppermute | solution.py:224
  173.2 1.1 collective-permute-start.27
  174.3 1.4 collective-permute-start.25
  175.8 3.4 %mix.4.refs_3_ = f32[192,1024]{1,0:T(8,128)S(1)} custom-call(s32[2]{0:T(128)S(1)} %pad_add_fusion.1.places, bf16[192,1024]{1,0:T(8,128)(2,1)S(1)} %together.6.refs_0_, bf16[192,1024]{1,0:T(8,128)(2,1)S(1)} %collective-permute-done.24.refs_3_.refs_1_, bf16[16384,1024]{1,0:T(8,128)(2,1)} %refs_2_.7, bf16[192,1024]{1,0:T(8,128)(2,1)S(1)} %bitcast.47), custom_call_target="tpu_custom_call" | custom-call | flops 1 | bytes 1 | tf_op jit(solution)/shard_map/mix/pallas_call | solution.py:510
  179.2 7.0 %mix.5.refs_2_.refs_3_ = f32[192,1024]{1,0:T(8,128)S(1)} custom-call(s32[6]{0:T(128)S(1)} %stack.82.places, bf16[3,192,1024]{2,1,0:T(8,128)(2,1)S(1)} %get-tuple-element.66.refs_0_, bf16[3,192,1024]{2,1,0:T(8,128)(2,1)} %collective-permute-done.28.refs_1_, bf16[16384,1024]{1,0:T(8,128)(2,1)} %refs_2_.7, f32[192,1024]{1,0:T(8,128)S(1)} %mix.4.refs_3_), custom_call_target="tpu_custom_call" | custom-call | flops 1 | bytes 1 | tf_op jit(solution)/shard_map/mix/pallas_call | solution.py:510
  186.2 1.3 collective-permute-done.25.refs_1_
  187.5 5.8 %collective-permute-done.27.refs_0_ = bf16[2,192,1024]{2,1,0:T(8,128)(2,1)} collective-permute-done((bf16[2,192,1024]{2,1,0:T(8,128)(2,1)S(1)}, bf16[2,192,1024]{2,1,0:T(8,128)(2,1)}, u32[]{:S(2)}, u32[]{:S(2)}) %collective-permute-start.27) | collective-permute-done | bytes 786464 | tf_op jit(solution)/shard_map/ppermute | solution.py:224
  193.3 1.3 pack.5.refs_0_
  194.6 1.1 collective-permute-start.26
  195.8 1.8 collective-permute-done.29.refs_1_
  197.6 7.0 %mix.6.refs_1_.refs_3_ = f32[192,1024]{1,0:T(8,128)S(1)} custom-call(s32[6]{0:T(128)S(1)} %stack.75.places, bf16[3,192,1024]{2,1,0:T(8,128)(2,1)S(1)} %pack.5.refs_0_, bf16[3,192,1024]{2,1,0:T(8,128)(2,1)} %collective-permute-done.29.refs_1_, bf16[16384,1024]{1,0:T(8,128)(2,1)} %refs_2_.7, f32[192,1024]{1,0:T(8,128)S(1)} %mix.5.refs_2_.refs_3_), custom_call_target="tpu_custom_call" | custom-call | flops 1 | bytes 1 | tf_op jit(solution)/shard_map/mix/pallas_call | solution.py:510
  204.6 1.8 collective-permute-done.26.refs_0_
  206.5 1.6 collective-permute-done.30.refs_1_
  208.1 4.1 %mix.7 = bf16[192,1024]{1,0:T(8,128)(2,1)} custom-call(s32[2]{0:T(128)S(1)} %pad_add_fusion.places, bf16[192,1024]{1,0:T(8,128)(2,1)S(1)} %together.7.refs_0_, bf16[192,1024]{1,0:T(8,128)(2,1)S(1)} %collective-permute-done.30.refs_1_, bf16[16384,1024]{1,0:T(8,128)(2,1)} %refs_2_.7, f32[192,1024]{1,0:T(8,128)S(1)} %mix.6.refs_1_.refs_3_), custom_call_target="tpu_custom_call" | custom-call | flops 1 | bytes 1 | tf_op jit(solution)/shard_map/mix/pallas_call | solution.py:510
  (132 shorter events, 4.0 us)
Async XLA Ops:
  0.0 18.6 %copy-start.4 = (bf16[2,96,1024]{2,1,0:T(8,128)(2,1)S(1)}, bf16[2,96,1024]{2,1,0:T(8,128)(2,1)}, u32[]{:S(2)}) copy-start(bf16[2,96,1024]{2,1,0:T(8,128)(2,1)} %param.8) | copy-start | bytes 1179652
  1.2 4.6 %collective-permute-start = (f32[2,96]{1,0:T(2,128)S(1)}, f32[2,96]{1,0:T(2,128)S(1)}, u32[]{:S(2)}, u32[]{:S(2)}) collective-permute-start(f32[2,96]{1,0:T(2,128)S(1)} %fusion), channel_id=1, source_target_pairs={{0,2},{1,3},{2,0},{3,1},{4,6},{5,7},{6,4},{7,5},{8,10},{9,11},{10,... | collective-permute-start | bytes 2312 | tf_op jit(solution)/shard_map/ppermute | solution.py:224
  5.8 1.1 collective-permute-start.1
  7.0 3.6 %collective-permute-start.2 = (f32[2,96]{1,0:T(2,128)S(1)}, f32[2,96]{1,0:T(2,128)S(1)}, u32[]{:S(2)}, u32[]{:S(2)}) collective-permute-start(f32[2,96]{1,0:T(2,128)S(1)} %add.138), channel_id=1, source_target_pairs={{0,4},{1,5},{2,6},{3,7},{4,0},{5,1},{6,2},{7,3},{8,12},{9,13},{10,... | collective-permute-start | bytes 2312 | tf_op jit(solution)/shard_map/ppermute | solution.py:224
  10.6 8.0 %collective-permute-start.3 = (f32[2,96]{1,0:T(2,128)S(1)}, f32[2,96]{1,0:T(2,128)S(1)}, u32[]{:S(2)}, u32[]{:S(2)}) collective-permute-start(f32[2,96]{1,0:T(2,128)S(1)} %add.139), channel_id=1, source_target_pairs={{0,8},{1,9},{2,10},{3,11},{4,12},{5,13},{6,14},{7,15},{8,0},{9,1},... | collective-permute-start | bytes 2312 | tf_op jit(solution)/shard_map/ppermute | solution.py:224
  13.6 1.4 copy-start.6
  15.2 12.3 %copy-start.13 = (bf16[400,256]{1,0:T(8,128)(2,1)}, bf16[400,256]{1,0:T(8,128)(2,1)S(1)}, u32[]{:S(2)}) copy-start(bf16[400,256]{1,0:T(8,128)(2,1)S(1)} %get-tuple-element.36.refs_0_) | copy-start | bytes 614404
  15.2 15.9 %collective-permute-start.5 = (bf16[400,256]{1,0:T(8,128)(2,1)S(1)}, bf16[400,256]{1,0:T(8,128)(2,1)S(1)}, u32[]{:S(2)}, u32[]{:S(2)}) collective-permute-start(bf16[400,256]{1,0:T(8,128)(2,1)S(1)} %get-tuple-element.39), channel_id=1, source_target_pairs={{0,2},{1,3},{2,0},{3,1},{4,6},{5,7},{6,4},{7,5},{8,10},{9,11},{10,... | collective-permute-start | bytes 614408 | tf_op jit(solution)/shard_map/ppermute | solution.py:224
  16.8 14.6 %collective-permute-start.6 = (bf16[400,256]{1,0:T(8,128)(2,1)S(1)}, bf16[400,256]{1,0:T(8,128)(2,1)S(1)}, u32[]{:S(2)}, u32[]{:S(2)}) collective-permute-start(bf16[400,256]{1,0:T(8,128)(2,1)S(1)} %get-tuple-element.40), channel_id=1, source_target_pairs={{0,6},{1,7},{2,4},{3,5},{4,2},{5,3},{6,0},{7,1},{8,14},{9,15},{10,... | collective-permute-start | bytes 614408 | tf_op jit(solution)/shard_map/ppermute | solution.py:224
  18.3 13.1 %collective-permute-start.7 = (bf16[400,256]{1,0:T(8,128)(2,1)S(1)}, bf16[400,256]{1,0:T(8,128)(2,1)S(1)}, u32[]{:S(2)}, u32[]{:S(2)}) collective-permute-start(bf16[400,256]{1,0:T(8,128)(2,1)S(1)} %get-tuple-element.41), channel_id=1, source_target_pairs={{0,8},{1,9},{2,10},{3,11},{4,12},{5,13},{6,14},{7,15},{8,0},{9,1},... | collective-permute-start | bytes 614408 | tf_op jit(solution)/shard_map/ppermute | solution.py:224
  27.4 18.1 %collective-permute-start.4 = (s16[1936,512]{1,0:T(8,128)(2,1)S(1)}, s16[1936,512]{1,0:T(8,128)(2,1)S(1)}, u32[]{:S(2)}, u32[]{:S(2)}) collective-permute-start(s16[1936,512]{1,0:T(8,128)(2,1)S(1)} %get-tuple-element.38), channel_id=1, source_target_pairs={{0,1},{1,0},{2,3},{3,2},{4,5},{5,4},{6,7},{7,6},{8,9},{9,8},{10,11... | collective-permute-start | bytes 5947400 | tf_op jit(solution)/shard_map/ppermute | solution.py:224
  27.5 18.0 %collective-permute-start.8 = (bf16[400,256]{1,0:T(8,128)(2,1)S(1)}, bf16[400,256]{1,0:T(8,128)(2,1)S(1)}, u32[]{:S(2)}, u32[]{:S(2)}) collective-permute-start(bf16[400,256]{1,0:T(8,128)(2,1)S(1)} %get-tuple-element.45), channel_id=1, source_target_pairs={{0,10},{1,11},{2,8},{3,9},{4,14},{5,15},{6,12},{7,13},{8,2},{9,3},... | collective-permute-start | bytes 614408 | tf_op jit(solution)/shard_map/ppermute | solution.py:224
  31.1 11.3 %copy-start.18 = (bf16[400,256]{1,0:T(8,128)(2,1)}, bf16[400,256]{1,0:T(8,128)(2,1)S(1)}, u32[]{:S(2)}) copy-start(bf16[400,256]{1,0:T(8,128)(2,1)S(1)} %collective-permute-done.5.refs_1_) | copy-start | bytes 614404
  31.1 14.4 %collective-permute-start.9 = (bf16[400,256]{1,0:T(8,128)(2,1)S(1)}, bf16[400,256]{1,0:T(8,128)(2,1)S(1)}, u32[]{:S(2)}, u32[]{:S(2)}) collective-permute-start(bf16[400,256]{1,0:T(8,128)(2,1)S(1)} %get-tuple-element.46), channel_id=1, source_target_pairs={{0,12},{1,13},{2,14},{3,15},{4,8},{5,9},{6,10},{7,11},{8,4},{9,5},... | collective-permute-start | bytes 614408 | tf_op jit(solution)/shard_map/ppermute | solution.py:224
  31.4 11.1 %copy-start.20 = (bf16[400,256]{1,0:T(8,128)(2,1)}, bf16[400,256]{1,0:T(8,128)(2,1)S(1)}, u32[]{:S(2)}) copy-start(bf16[400,256]{1,0:T(8,128)(2,1)S(1)} %collective-permute-done.6.refs_2_.refs_3_) | copy-start | bytes 614404
  31.4 11.1 %copy-start.22 = (bf16[400,256]{1,0:T(8,128)(2,1)}, bf16[400,256]{1,0:T(8,128)(2,1)S(1)}, u32[]{:S(2)}) copy-start(bf16[400,256]{1,0:T(8,128)(2,1)S(1)} %collective-permute-done.7.refs_3_.refs_4_) | copy-start | bytes 614404
  45.5 0.7 copy-start.7
  45.5 0.7 copy-start.26
  45.5 8.3 %copy-start.25 = (s32[16,16]{1,0:T(8,128)S(1)}, s32[16,16]{1,0:T(8,128)}, u32[]{:S(2)}) copy-start(s32[16,16]{1,0:T(8,128)} %param.15) | copy-start | bytes 3076
  46.2 17.9 %collective-permute-start.11 = (s16[1936,640]{1,0:T(8,128)(2,1)}, s16[1936,640]{1,0:T(8,128)(2,1)}, u32[]{:S(2)}, u32[]{:S(2)}) collective-permute-start(s16[1936,640]{1,0:T(8,128)(2,1)} %get-tuple-element.47.refs_0_), channel_id=1, source_target_pairs={{0,1},{1,0},{2,3},{3,2},{4,5},{5,4},{6,7},{7,6},{8,9},{9,8},{10,11... | collective-permute-start | bytes 7434248 | tf_op jit(solution)/shard_map/ppermute | solution.py:224
  46.3 11.5 %collective-permute-start.12 = (bf16[400,256]{1,0:T(8,128)(2,1)S(1)}, bf16[400,256]{1,0:T(8,128)(2,1)S(1)}, u32[]{:S(2)}, u32[]{:S(2)}) collective-permute-start(bf16[400,256]{1,0:T(8,128)(2,1)S(1)} %get-tuple-element.51), channel_id=1, source_target_pairs={{0,4},{1,5},{2,6},{3,7},{4,0},{5,1},{6,2},{7,3},{8,12},{9,13},{10,... | collective-permute-start | bytes 614408 | tf_op jit(solution)/shard_map/ppermute | solution.py:224
  51.4 12.7 %collective-permute-start.13 = (bf16[400,256]{1,0:T(8,128)(2,1)S(1)}, bf16[400,256]{1,0:T(8,128)(2,1)S(1)}, u32[]{:S(2)}, u32[]{:S(2)}) collective-permute-start(bf16[400,256]{1,0:T(8,128)(2,1)S(1)} %get-tuple-element.52), channel_id=1, source_target_pairs={{0,14},{1,15},{2,12},{3,13},{4,10},{5,11},{6,8},{7,9},{8,6},{9,7},... | collective-permute-start | bytes 614408 | tf_op jit(solution)/shard_map/ppermute | solution.py:224
  57.7 27.4 %collective-permute-start.10 = (s16[976,512]{1,0:T(8,128)(2,1)S(1)}, s16[976,512]{1,0:T(8,128)(2,1)S(1)}, u32[]{:S(2)}, u32[]{:S(2)}) collective-permute-start(s16[976,512]{1,0:T(8,128)(2,1)S(1)} %get-tuple-element.49), channel_id=1, source_target_pairs={{0,4},{1,5},{2,6},{3,7},{4,0},{5,1},{6,2},{7,3},{8,12},{9,13},{10,... | collective-permute-start | bytes 2998280 | tf_op jit(solution)/shard_map/ppermute | solution.py:224
  57.8 12.0 %copy-start.9 = (bf16[400,256]{1,0:T(8,128)(2,1)}, bf16[400,256]{1,0:T(8,128)(2,1)S(1)}, u32[]{:S(2)}) copy-start(bf16[400,256]{1,0:T(8,128)(2,1)S(1)} %collective-permute-done.12.refs_1_.refs_2_) | copy-start | bytes 614404
  64.1 5.7 %copy-start.11 = (bf16[400,256]{1,0:T(8,128)(2,1)}, bf16[400,256]{1,0:T(8,128)(2,1)S(1)}, u32[]{:S(2)}) copy-start(bf16[400,256]{1,0:T(8,128)(2,1)S(1)} %collective-permute-done.13.refs_2_.refs_7_) | copy-start | bytes 614404
  69.8 30.7 %collective-permute-start.15 = (s16[976,640]{1,0:T(8,128)(2,1)}, s16[976,640]{1,0:T(8,128)(2,1)S(1)}, u32[]{:S(2)}, u32[]{:S(2)}) collective-permute-start(s16[976,640]{1,0:T(8,128)(2,1)} %get-tuple-element.56), channel_id=1, source_target_pairs={{0,2},{1,3},{2,0},{3,1},{4,6},{5,7},{6,4},{7,5},{8,10},{9,11},{10,... | collective-permute-start | bytes 3747848 | tf_op jit(solution)/shard_map/ppermute | solution.py:224
  86.8 0.9 copy-start.2
  87.7 22.1 %collective-permute-start.14 = (s16[496,512]{1,0:T(8,128)(2,1)}, s16[496,512]{1,0:T(8,128)(2,1)}, u32[]{:S(2)}, u32[]{:S(2)}) collective-permute-start(s16[496,512]{1,0:T(8,128)(2,1)} %get-tuple-element.55), channel_id=1, source_target_pairs={{0,2},{1,3},{2,0},{3,1},{4,6},{5,7},{6,4},{7,5},{8,10},{9,11},{10,... | collective-permute-start | bytes 1523720 | tf_op jit(solution)/shard_map/ppermute | solution.py:224
  100.5 1.1 copy-start.3
  101.6 2.0 copy-start.8
  101.6 2.0 copy-start.10
  101.6 2.1 copy-start.12
  101.6 2.1 copy-start.14
  101.6 2.1 copy-start.19
  101.6 2.1 copy-start.21
  101.6 2.1 copy-start.23
  103.6 1.0 copy-start
  103.6 15.0 %collective-permute-start.17 = (s16[496,640]{1,0:T(8,128)(2,1)}, s16[496,640]{1,0:T(8,128)(2,1)S(1)}, u32[]{:S(2)}, u32[]{:S(2)}) collective-permute-start(s16[496,640]{1,0:T(8,128)(2,1)} %get-tuple-element.60), channel_id=1, source_target_pairs={{0,4},{1,5},{2,6},{3,7},{4,0},{5,1},{6,2},{7,3},{8,12},{9,13},{10,... | collective-permute-start | bytes 1904648 | tf_op jit(solution)/shard_map/ppermute | solution.py:224
  109.8 8.9 %copy-start.1 = (f32[2,192,640]{2,1,0:T(8,128)S(1)}, f32[2,192,640]{2,1,0:T(8,128)}, u32[]{:S(2)}) copy-start(f32[2,192,640]{2,1,0:T(8,128)} %copy-done) | copy-start | bytes 2949124
  112.0 0.7 copy-start.15
  112.8 21.7 %collective-permute-start.16 = (s16[256,512]{1,0:T(8,128)(2,1)}, s16[256,512]{1,0:T(8,128)(2,1)}, u32[]{:S(2)}, u32[]{:S(2)}) collective-permute-start(s16[256,512]{1,0:T(8,128)(2,1)} %get-tuple-element.59), channel_id=1, source_target_pairs={{0,8},{1,9},{2,10},{3,11},{4,12},{5,13},{6,14},{7,15},{8,0},{9,1},... | collective-permute-start | bytes 786440 | tf_op jit(solution)/shard_map/ppermute | solution.py:224
  116.2 25.3 %collective-permute-start.20 = (bf16[8,400,256]{2,1,0:T(8,128)(2,1)S(1)}, bf16[8,400,256]{2,1,0:T(8,128)(2,1)}, u32[]{:S(2)}, u32[]{:S(2)}) collective-permute-start(bf16[8,400,256]{2,1,0:T(8,128)(2,1)S(1)} %pack.3.refs_0_.own), channel_id=1, source_target_pairs={{0,1},{1,0},{2,3},{3,2},{4,5},{5,4},{6,7},{7,6},{8,9},{9,8},{10,11... | collective-permute-start | bytes 4915208 | tf_op jit(solution)/shard_map/ppermute | solution.py:224
  118.6 1.0 copy-start.16
  119.6 14.9 %copy-start.17 = (f32[1,192,512]{2,1,0:T(8,128)S(1)}, f32[1,192,512]{2,1,0:T(8,128)}, u32[]{:S(2)}) copy-start(f32[1,192,512]{2,1,0:T(8,128)} %copy-done.15) | copy-start | bytes 1179652
  119.6 14.9 %copy-start.24 = (f32[192,128]{1,0:T(8,128)S(1)}, f32[192,128]{1,0:T(8,128)}, u32[]{:S(2)}) copy-start(f32[192,128]{1,0:T(8,128)} %get-tuple-element.80.sine) | copy-start | bytes 294916
  120.1 20.0 %collective-permute-start.18 = (s16[256,640]{1,0:T(8,128)(2,1)S(1)}, s16[256,640]{1,0:T(8,128)(2,1)S(1)}, u32[]{:S(2)}, u32[]{:S(2)}) collective-permute-start(s16[256,640]{1,0:T(8,128)(2,1)S(1)} %get-tuple-element.63), channel_id=1, source_target_pairs={{0,8},{1,9},{2,10},{3,11},{4,12},{5,13},{6,14},{7,15},{8,0},{9,1},... | collective-permute-start | bytes 983048 | tf_op jit(solution)/shard_map/ppermute | solution.py:224
  140.1 1.2 collective-permute-start.19
  151.5 24.3 %copy-start.5 = (bf16[2,96,1024]{2,1,0:T(8,128)(2,1)S(1)}, bf16[2,96,1024]{2,1,0:T(8,128)(2,1)}, u32[]{:S(2)}) copy-start(bf16[2,96,1024]{2,1,0:T(8,128)(2,1)} %param.8) | copy-start | bytes 1179652
  151.6 17.5 %collective-permute-start.21 = (bf16[192,1024]{1,0:T(8,128)(2,1)S(1)}, bf16[192,1024]{1,0:T(8,128)(2,1)S(1)}, u32[]{:S(2)}, u32[]{:S(2)}) collective-permute-start(bf16[192,1024]{1,0:T(8,128)(2,1)S(1)} %bitcast.48), channel_id=1, source_target_pairs={{0,4},{1,5},{2,6},{3,7},{4,0},{5,1},{6,2},{7,3},{8,12},{9,13},{10,... | collective-permute-start | bytes 1179656 | tf_op jit(solution)/shard_map/ppermute | solution.py:224
  151.6 17.4 %collective-permute-start.22 = (bf16[192,1024]{1,0:T(8,128)(2,1)S(1)}, bf16[192,1024]{1,0:T(8,128)(2,1)S(1)}, u32[]{:S(2)}, u32[]{:S(2)}) collective-permute-start(bf16[192,1024]{1,0:T(8,128)(2,1)S(1)} %bitcast.49), channel_id=1, source_target_pairs={{0,2},{1,3},{2,0},{3,1},{4,6},{5,7},{6,4},{7,5},{8,10},{9,11},{10,... | collective-permute-start | bytes 1179656 | tf_op jit(solution)/shard_map/ppermute | solution.py:224
  152.7 20.3 %collective-permute-start.23 = (bf16[192,1024]{1,0:T(8,128)(2,1)S(1)}, bf16[192,1024]{1,0:T(8,128)(2,1)S(1)}, u32[]{:S(2)}, u32[]{:S(2)}) collective-permute-start(bf16[192,1024]{1,0:T(8,128)(2,1)S(1)} %bitcast.50), channel_id=1, source_target_pairs={{0,8},{1,9},{2,10},{3,11},{4,12},{5,13},{6,14},{7,15},{8,0},{9,1},... | collective-permute-start | bytes 1179656 | tf_op jit(solution)/shard_map/ppermute | solution.py:224
  154.9 18.0 %collective-permute-start.24 = (bf16[192,1024]{1,0:T(8,128)(2,1)S(1)}, bf16[192,1024]{1,0:T(8,128)(2,1)S(1)}, u32[]{:S(2)}, u32[]{:S(2)}) collective-permute-start(bf16[192,1024]{1,0:T(8,128)(2,1)S(1)} %bitcast.51), channel_id=1, source_target_pairs={{0,1},{1,0},{2,3},{3,2},{4,5},{5,4},{6,7},{7,6},{8,9},{9,8},{10,11... | collective-permute-start | bytes 1179656 | tf_op jit(solution)/shard_map/ppermute | solution.py:224
  173.1 6.1 %collective-permute-start.28 = (bf16[3,192,1024]{2,1,0:T(8,128)(2,1)S(1)}, bf16[3,192,1024]{2,1,0:T(8,128)(2,1)}, u32[]{:S(2)}, u32[]{:S(2)}) collective-permute-start(bf16[3,192,1024]{2,1,0:T(8,128)(2,1)S(1)} %get-tuple-element.66.refs_0_), channel_id=1, source_target_pairs={{0,1},{1,0},{2,3},{3,2},{4,5},{5,4},{6,7},{7,6},{8,9},{9,8},{10,11... | collective-permute-start | bytes 3538952 | tf_op jit(solution)/shard_map/ppermute | solution.py:224
  173.2 20.1 %collective-permute-start.27 = (bf16[2,192,1024]{2,1,0:T(8,128)(2,1)S(1)}, bf16[2,192,1024]{2,1,0:T(8,128)(2,1)}, u32[]{:S(2)}, u32[]{:S(2)}) collective-permute-start(bf16[2,192,1024]{2,1,0:T(8,128)(2,1)S(1)} %get-tuple-element.65.refs_1_), channel_id=1, source_target_pairs={{0,2},{1,3},{2,0},{3,1},{4,6},{5,7},{6,4},{7,5},{8,10},{9,11},{10,... | collective-permute-start | bytes 2359304 | tf_op jit(solution)/shard_map/ppermute | solution.py:224
  174.3 13.2 %collective-permute-start.25 = (bf16[192,1024]{1,0:T(8,128)(2,1)S(1)}, bf16[192,1024]{1,0:T(8,128)(2,1)}, u32[]{:S(2)}, u32[]{:S(2)}) collective-permute-start(bf16[192,1024]{1,0:T(8,128)(2,1)S(1)} %together.6.refs_0_), channel_id=1, source_target_pairs={{0,12},{1,13},{2,14},{3,15},{4,8},{5,9},{6,10},{7,11},{8,4},{9,5},... | collective-permute-start | bytes 1179656 | tf_op jit(solution)/shard_map/ppermute | solution.py:224
  194.6 3.0 %collective-permute-start.29 = (bf16[3,192,1024]{2,1,0:T(8,128)(2,1)S(1)}, bf16[3,192,1024]{2,1,0:T(8,128)(2,1)}, u32[]{:S(2)}, u32[]{:S(2)}) collective-permute-start(bf16[3,192,1024]{2,1,0:T(8,128)(2,1)S(1)} %pack.5.refs_0_), channel_id=1, source_target_pairs={{0,1},{1,0},{2,3},{3,2},{4,5},{5,4},{6,7},{7,6},{8,9},{9,8},{10,11... | collective-permute-start | bytes 3538952 | tf_op jit(solution)/shard_map/ppermute | solution.py:224
  194.6 11.7 %collective-permute-start.26 = (bf16[192,1024]{1,0:T(8,128)(2,1)}, bf16[192,1024]{1,0:T(8,128)(2,1)S(1)}, u32[]{:S(2)}, u32[]{:S(2)}) collective-permute-start(bf16[192,1024]{1,0:T(8,128)(2,1)} %collective-permute-done.25.refs_1_), channel_id=1, source_target_pairs={{0,2},{1,3},{2,0},{3,1},{4,6},{5,7},{6,4},{7,5},{8,10},{9,11},{10,... | collective-permute-start | bytes 1179656 | tf_op jit(solution)/shard_map/ppermute | solution.py:224
  206.4 1.7 collective-permute-start.30

commit v14 on v12

--- a/solution.py
+++ b/solution.py
@@ -785,14 +785,14 @@
     core_b = swap(sent_b, 1)
     for k in (2, 7):
         handed(k)
-    held_a, sent_a = folded(held_a, 2, core_a, 2, sent_b)
+    held_a, sent_a = folded(held_a, 1, core_a, 1, sent_b)
+    line_a = swap(sent_a, 2)
+    held_b, sent_b = folded(held_b, 2, core_b, 2, held_a, cache_pieces[2], cache_pieces[7])
+    line_b = swap(sent_b, 4)
+    held_a, sent_a = folded(held_a, 2, line_a, 1, held_b)
     line_a = swap(sent_a, 4)
-    held_b, sent_b = folded(held_b, 1, core_b, 1, held_a, cache_pieces[2], cache_pieces[7])
+    held_b, sent_b = folded(held_b, 1, line_b, 1, held_a)
     line_b = swap(sent_b, 2)
-    held_a, sent_a = folded(held_a, 1, line_a, 1, held_b)
-    line_a = swap(sent_a, 2)
-    held_b, sent_b = folded(held_b, 2, line_b, 1, held_a)
-    line_b = swap(sent_b, 4)
     (cache_own,) = pack(cache_pieces, [tuple(range(KVH))], [held_b])
     cache_other = swap(cache_own, 1)
     held_a, sent_a = folded(held_a, 3, line_a, 1, cache_own)

time: 210 us -> 208 us (level)
  waiting for transfers between devices: 89.5 us -> 85.6 us
  starting transfers between devices: 34.8 us -> 37.4 us
    ppermute x31, waiting for transfers between devices: 89.5 us -> 85.6 us  [swap(): return lax.ppermute(value, 'tensor', [(i, i ^ bit) for i in range(devices)])]
    ppermute x31, starting transfers between devices: 34.8 us -> 37.4 us  [swap(): return lax.ppermute(value, 'tensor', [(i, i ^ bit) for i in range(devices)])]
  transfers between devices with their start and end apart: 31 -> 31, of which waited for: 20 -> 20; matrix products, arithmetic and copies ran while one was open for 3% -> 3% of each run, Pallas kernels for 26% -> 27%
where the time goes in v14:
time: 208 us
  waiting for transfers between devices  85.6 us (41%)
  Pallas kernels  69.1 us (33%)
  starting transfers between devices  37.4 us (18%)
  local copies, waits for them, and re-layouts  8.98 us (4%)
  other arithmetic  5.91 us (3%)
    ppermute x31, waiting for transfers between devices, swap(): return lax.ppermute(value, 'tensor', [(i, i ^ bit) for i in range(devices)])  85.6 us
    ppermute x31, starting transfers between devices, swap(): return lax.ppermute(value, 'tensor', [(i, i ^ bit) for i in range(devices)])  37.4 us
    pallas_call x4, Pallas kernels, mix(): pl.pallas_call(functools.partial(mix_kernel, len(pieces)), in_specs=[pl.B...  21.5 us
    pallas_call x2, Pallas kernels, project(): pl.pallas_call(functools.partial(project_kernel, part), grid_spec=pltpu.P...  20.4 us
    pallas_call x6, Pallas kernels, fold(): pl.pallas_call(functools.partial(fold_kernel, steps, low), grid_spec=pltp...  15.8 us
    pallas_call x1, Pallas kernels, attend(): pl.pallas_call(attend_kernel, in_specs=[pl.BlockSpec(memory_space=pltpu.S...  8.39 us
    unnamed x56, local copies, waits for them, and re-layouts  6.13 us
  transfers between devices with their start and end apart: 31, of which 20 were waited for; matrix products, arithmetic and copies ran while one was open for 3% of the time, Pallas kernels for 27%

profile of v14, /device:TPU:0, one launch (start us, length us, event | category | flops | bytes accessed | tf_op | source)
XLA Modules:
  0.0 207.7 jit_solution(7729191030250944420)
XLA Ops:
  0.0 1.2 fusion
  1.2 3.0 %collective-permute-start = (f32[2,96]{1,0:T(2,128)S(1)}, f32[2,96]{1,0:T(2,128)S(1)}, u32[]{:S(2)}, u32[]{:S(2)}) collective-permute-start(f32[2,96]{1,0:T(2,128)S(1)} %fusion), channel_id=1, source_target_pairs={{0,2},{1,3},{2,0},{3,1},{4,6},{5,7},{6,4},{7,5},{8,10},{9,11},{10,... | collective-permute-start | bytes 2312 | tf_op jit(solution)/shard_map/ppermute | solution.py:223
  4.3 1.5 collective-permute-done
  5.8 1.1 collective-permute-done.1
  7.0 2.1 collective-permute-start.2
  9.0 0.8 reshape.240
  9.8 0.7 convert_element_type.29
  10.6 3.0 %collective-permute-start.3 = (f32[2,96]{1,0:T(2,128)S(1)}, f32[2,96]{1,0:T(2,128)S(1)}, u32[]{:S(2)}, u32[]{:S(2)}) collective-permute-start(f32[2,96]{1,0:T(2,128)S(1)} %add.139), channel_id=1, source_target_pairs={{0,8},{1,9},{2,10},{3,11},{4,12},{5,13},{6,14},{7,15},{8,0},{9,1},... | collective-permute-start | bytes 2312 | tf_op jit(solution)/shard_map/ppermute | solution.py:223
  13.6 1.4 copy-done.6
  15.2 1.6 collective-permute-start.5
  16.8 1.5 collective-permute-start.6
  18.6 3.5 %collective-permute-start.8 = (bf16[400,256]{1,0:T(8,128)(2,1)S(1)}, bf16[400,256]{1,0:T(8,128)(2,1)S(1)}, u32[]{:S(2)}, u32[]{:S(2)}) collective-permute-start(bf16[400,256]{1,0:T(8,128)(2,1)S(1)} %get-tuple-element.45), channel_id=1, source_target_pairs={{0,10},{1,11},{2,8},{3,9},{4,14},{5,15},{6,12},{7,13},{8,2},{9,3},... | collective-permute-start | bytes 614408 | tf_op jit(solution)/shard_map/ppermute | solution.py:223
  22.6 9.4 %project.2 = (f32[8,192,512]{2,1,0:T(8,128)}, s16[1936,512]{1,0:T(8,128)(2,1)}) custom-call(s32[1]{0:T(128)} %bitcast.2.core, bf16[192,1024]{1,0:T(8,128)(2,1)S(1)} %bitcast.47, bf16[1024,18432]{1,0:T(8,128)(2,1)} %weights.3, bf16[400,256]{1,0:T(8,128)(2,1)S(1)} %get-tuple-element.36.refs_0_), custom_call_target="tpu_custom_call" | custom-call | flops 1 | bytes 1 | tf_op jit(solution)/shard_map/project/pallas_call | solution.py:352
  32.0 11.0 %project.3 = (f32[8,192,640]{2,1,0:T(8,128)}, s16[1936,640]{1,0:T(8,128)(2,1)}) custom-call(s32[1]{0:T(128)} %bitcast.2.core, bf16[192,1024]{1,0:T(8,128)(2,1)S(1)} %bitcast.48, bf16[1024,18432]{1,0:T(8,128)(2,1)} %weights.3, f32[8,192,512]{2,1,0:T(8,128)} %get-tuple-element.37.refs_0_.held.held_out, bf16[400,256]{1,0:T(8,128)(2,1)S(1)} %collective-permute-done.5.refs_1_, ...), custom_call_target="tpu_custom_call" | custom-call | flops 1 | bytes 1 | tf_op jit(solution)/shard_map/project/pallas_call | solution.py:352
  43.0 1.4 collective-permute-done.8.refs_4_.refs_5_
  44.5 0.6 copy-done.11
  45.2 0.5 collective-permute-start.4
  45.8 2.4 %collective-permute-start.12 = (bf16[400,256]{1,0:T(8,128)(2,1)S(1)}, bf16[400,256]{1,0:T(8,128)(2,1)S(1)}, u32[]{:S(2)}, u32[]{:S(2)}) collective-permute-start(bf16[400,256]{1,0:T(8,128)(2,1)S(1)} %get-tuple-element.51), channel_id=1, source_target_pairs={{0,4},{1,5},{2,6},{3,7},{4,0},{5,1},{6,2},{7,3},{8,12},{9,13},{10,... | collective-permute-start | bytes 614408 | tf_op jit(solution)/shard_map/ppermute | solution.py:223
  48.2 1.6 collective-permute-start.13
  49.9 2.7 %collective-permute-done.4.landed.landed_out.landed_powers = s16[1936,512]{1,0:T(8,128)(2,1)S(1)} collective-permute-done((s16[1936,512]{1,0:T(8,128)(2,1)}, s16[1936,512]{1,0:T(8,128)(2,1)S(1)}, u32[]{:S(2)}, u32[]{:S(2)}) %collective-permute-start.4) | collective-permute-done | bytes 1982496 | tf_op jit(solution)/shard_map/ppermute | solution.py:223
  52.6 3.6 %fold.6 = (f32[4,192,512]{2,1,0:T(8,128)S(1)}, s16[976,512]{1,0:T(8,128)(2,1)S(1)}) custom-call(s32[1]{0:T(128)} %bitcast.5.bit, f32[8,192,512]{2,1,0:T(8,128)} %get-tuple-element.37.refs_0_.held.held_out, f32[8,192,512]{2,1,0:T(8,128)} %get-tuple-element.37.refs_0_.held.held_out, ...), custom_call_target="tpu_custom_call" | custom-call | flops 1 | bytes 1 | tf_op jit(solution)/shard_map/fold/pallas_call | solution.py:406
  56.3 0.7 collective-permute-start.10
  57.0 2.2 %collective-permute-done.13.refs_2_.refs_7_ = bf16[400,256]{1,0:T(8,128)(2,1)S(1)} collective-permute-done((bf16[400,256]{1,0:T(8,128)(2,1)S(1)}, bf16[400,256]{1,0:T(8,128)(2,1)S(1)}, u32[]{:S(2)}, u32[]{:S(2)}) %collective-permute-start.13) | collective-permute-done | bytes 204832 | tf_op jit(solution)/shard_map/ppermute | solution.py:223
  59.2 5.8 %fold.7 = (f32[4,192,640]{2,1,0:T(8,128)S(1)}, s16[976,640]{1,0:T(8,128)(2,1)}) custom-call(s32[1]{0:T(128)} %bitcast.4.bit, f32[8,192,640]{2,1,0:T(8,128)} %get-tuple-element.50.held.held_out, f32[8,192,640]{2,1,0:T(8,128)} %get-tuple-element.50.held.held_out, s16[1936,640]{1,0:T(8,128)(2,1)} %collective-permute-done.11.landed.landed_out.landed_powers, ...), custom_call_target="tpu_custom_call" | custom-call | flops 1 | bytes 1 | tf_op jit(solution)/shard_map/fold/pallas_call | solution.py:406
  65.0 1.4 collective-permute-start.15
  66.7 14.0 %collective-permute-done.10.landed.landed_out.landed_powers = s16[976,512]{1,0:T(8,128)(2,1)S(1)} collective-permute-done((s16[976,512]{1,0:T(8,128)(2,1)S(1)}, s16[976,512]{1,0:T(8,128)(2,1)S(1)}, u32[]{:S(2)}, u32[]{:S(2)}) %collective-permute-start.10) | collective-permute-done | bytes 999456 | tf_op jit(solution)/shard_map/ppermute | solution.py:223
  80.7 1.7 fold.8
  82.3 0.9 copy-done.2
  83.3 2.4 %collective-permute-start.14 = (s16[496,512]{1,0:T(8,128)(2,1)}, s16[496,512]{1,0:T(8,128)(2,1)}, u32[]{:S(2)}, u32[]{:S(2)}) collective-permute-start(s16[496,512]{1,0:T(8,128)(2,1)} %get-tuple-element.55), channel_id=1, source_target_pairs={{0,4},{1,5},{2,6},{3,7},{4,0},{5,1},{6,2},{7,3},{8,12},{9,13},{10,... | collective-permute-start | bytes 1523720 | tf_op jit(solution)/shard_map/ppermute | solution.py:223
  85.8 1.1 fusion.5
  87.0 8.7 %collective-permute-done.15.landed.landed_out.landed_powers = s16[976,640]{1,0:T(8,128)(2,1)S(1)} collective-permute-done((s16[976,640]{1,0:T(8,128)(2,1)}, s16[976,640]{1,0:T(8,128)(2,1)S(1)}, u32[]{:S(2)}, u32[]{:S(2)}) %collective-permute-start.15) | collective-permute-done | bytes 1249312 | tf_op jit(solution)/shard_map/ppermute | solution.py:223
  95.7 1.1 copy-done.3
  96.9 2.0 fold.9
  98.8 0.8 collective-permute-start.17
  99.8 5.2 %collective-permute-done.14.landed.landed_out.landed_powers = s16[496,512]{1,0:T(8,128)(2,1)} collective-permute-done((s16[496,512]{1,0:T(8,128)(2,1)}, s16[496,512]{1,0:T(8,128)(2,1)}, u32[]{:S(2)}, u32[]{:S(2)}) %collective-permute-start.14) | collective-permute-done | bytes 507936 | tf_op jit(solution)/shard_map/ppermute | solution.py:223
  105.0 2.2 %fold.10 = (f32[1,192,512]{2,1,0:T(8,128)S(1)}, s16[256,512]{1,0:T(8,128)(2,1)}) custom-call(s32[1]{0:T(128)} %bitcast.3.bit, f32[2,192,512]{2,1,0:T(8,128)S(1)} %copy-done.3, f32[2,192,512]{2,1,0:T(8,128)S(1)} %copy-done.3, s16[496,512]{1,0:T(8,128)(2,1)} %collective-permute-done.14.landed.landed_out.landed_powers, ...), custom_call_target="tpu_custom_call" | custom-call | flops 1 | bytes 1 | tf_op jit(solution)/shard_map/fold/pallas_call | solution.py:406
  107.3 0.7 copy-done.21
  108.0 1.7 collective-permute-start.16
  109.8 1.8 pad_maximum_fusion
  112.1 1.0 copy-done.22
  113.1 0.5 fold.11
  113.5 1.8 collective-permute-start.18
  115.3 15.0 %collective-permute-done.16.landed = s16[256,512]{1,0:T(8,128)(2,1)} collective-permute-done((s16[256,512]{1,0:T(8,128)(2,1)}, s16[256,512]{1,0:T(8,128)(2,1)}, u32[]{:S(2)}, u32[]{:S(2)}) %collective-permute-start.16) | collective-permute-done | bytes 262176 | tf_op jit(solution)/shard_map/ppermute | solution.py:223
  130.3 1.2 finish.2
  131.5 3.9 %collective-permute-done.18.landed.refs_1_ = s16[256,640]{1,0:T(8,128)(2,1)S(1)} collective-permute-done((s16[256,640]{1,0:T(8,128)(2,1)S(1)}, s16[256,640]{1,0:T(8,128)(2,1)S(1)}, u32[]{:S(2)}, u32[]{:S(2)}) %collective-permute-start.18) | collective-permute-done | bytes 327712 | tf_op jit(solution)/shard_map/ppermute | solution.py:223
  135.9 0.8 collective-permute-done.19
  136.9 0.7 slice_reduce_fusion
  138.4 8.4 %attend.1 = bf16[16,96,128]{2,1,0:T(8,128)(2,1)S(1)} custom-call(s32[24]{0:T(128)S(1)} %get-tuple-element.69.slot_request, bf16[16,96,128]{2,1,0:T(8,128)(2,1)S(1)} %bitcast.55, bf16[16,16,128]{2,1,0:T(8,128)(2,1)S(1)} %pad.12.new_keys, bf16[16,16,128]{2,1,0:T(8,128)(2,1)S(1)} %pad.13.new_values, bf16[8,400,256]{2,1,0:T(8,128)(2,1)S(1)} %pack.3.refs_0_.own, ...), custom_call_target="tpu_custom_call" | custom-call | flops 1 | bytes 1 | tf_op jit(solution)/shard_map/attend/pallas_call | solution.py:661
  147.0 1.0 collective-permute-start.22
  148.0 2.6 %collective-permute-start.23 = (bf16[192,1024]{1,0:T(8,128)(2,1)S(1)}, bf16[192,1024]{1,0:T(8,128)(2,1)S(1)}, u32[]{:S(2)}, u32[]{:S(2)}) collective-permute-start(bf16[192,1024]{1,0:T(8,128)(2,1)S(1)} %bitcast.52), channel_id=1, source_target_pairs={{0,8},{1,9},{2,10},{3,11},{4,12},{5,13},{6,14},{7,15},{8,0},{9,1},... | collective-permute-start | bytes 1179656 | tf_op jit(solution)/shard_map/ppermute | solution.py:223
  150.6 15.2 %collective-permute-done.21.refs_0_ = bf16[192,1024]{1,0:T(8,128)(2,1)S(1)} collective-permute-done((bf16[192,1024]{1,0:T(8,128)(2,1)S(1)}, bf16[192,1024]{1,0:T(8,128)(2,1)S(1)}, u32[]{:S(2)}, u32[]{:S(2)}) %collective-permute-start.21) | collective-permute-done | bytes 393248 | tf_op jit(solution)/shard_map/ppermute | solution.py:223
  165.8 2.4 %collective-permute-done.23.refs_2_ = bf16[192,1024]{1,0:T(8,128)(2,1)S(1)} collective-permute-done((bf16[192,1024]{1,0:T(8,128)(2,1)S(1)}, bf16[192,1024]{1,0:T(8,128)(2,1)S(1)}, u32[]{:S(2)}, u32[]{:S(2)}) %collective-permute-start.23) | collective-permute-done | bytes 393248 | tf_op jit(solution)/shard_map/ppermute | solution.py:223
  168.5 1.3 collective-permute-start.27
  169.8 2.4 %collective-permute-start.25 = (bf16[192,1024]{1,0:T(8,128)(2,1)S(1)}, bf16[192,1024]{1,0:T(8,128)(2,1)}, u32[]{:S(2)}, u32[]{:S(2)}) collective-permute-start(bf16[192,1024]{1,0:T(8,128)(2,1)S(1)} %together.6.refs_0_), channel_id=1, source_target_pairs={{0,12},{1,13},{2,14},{3,15},{4,8},{5,9},{6,10},{7,11},{8,4},{9,5},... | collective-permute-start | bytes 1179656 | tf_op jit(solution)/shard_map/ppermute | solution.py:223
  172.4 3.4 %mix.4.refs_3_ = f32[192,1024]{1,0:T(8,128)S(1)} custom-call(s32[2]{0:T(128)S(1)} %pad_add_fusion.1.places, bf16[192,1024]{1,0:T(8,128)(2,1)S(1)} %together.6.refs_0_, bf16[192,1024]{1,0:T(8,128)(2,1)S(1)} %collective-permute-done.24.refs_3_.refs_1_, bf16[16384,1024]{1,0:T(8,128)(2,1)} %refs_2_.7, bf16[192,1024]{1,0:T(8,128)(2,1)S(1)} %bitcast.49), custom_call_target="tpu_custom_call" | custom-call | flops 1 | bytes 1 | tf_op jit(solution)/shard_map/mix/pallas_call | solution.py:509
  175.8 7.0 %mix.5.refs_2_.refs_3_ = f32[192,1024]{1,0:T(8,128)S(1)} custom-call(s32[6]{0:T(128)S(1)} %stack.82.places, bf16[3,192,1024]{2,1,0:T(8,128)(2,1)S(1)} %get-tuple-element.66.refs_0_, bf16[3,192,1024]{2,1,0:T(8,128)(2,1)} %collective-permute-done.28.refs_1_, bf16[16384,1024]{1,0:T(8,128)(2,1)} %refs_2_.7, f32[192,1024]{1,0:T(8,128)S(1)} %mix.4.refs_3_), custom_call_target="tpu_custom_call" | custom-call | flops 1 | bytes 1 | tf_op jit(solution)/shard_map/mix/pallas_call | solution.py:509
  183.0 5.6 %collective-permute-done.27.refs_0_ = bf16[2,192,1024]{2,1,0:T(8,128)(2,1)} collective-permute-done((bf16[2,192,1024]{2,1,0:T(8,128)(2,1)S(1)}, bf16[2,192,1024]{2,1,0:T(8,128)(2,1)}, u32[]{:S(2)}, u32[]{:S(2)}) %collective-permute-start.27) | collective-permute-done | bytes 786464 | tf_op jit(solution)/shard_map/ppermute | solution.py:223
  188.6 1.3 pack.5.refs_0_
  190.0 1.3 collective-permute-start.26
  191.3 1.6 collective-permute-done.29.refs_1_
  192.9 7.0 %mix.6.refs_1_.refs_3_ = f32[192,1024]{1,0:T(8,128)S(1)} custom-call(s32[6]{0:T(128)S(1)} %stack.75.places, bf16[3,192,1024]{2,1,0:T(8,128)(2,1)S(1)} %pack.5.refs_0_, bf16[3,192,1024]{2,1,0:T(8,128)(2,1)} %collective-permute-done.29.refs_1_, bf16[16384,1024]{1,0:T(8,128)(2,1)} %refs_2_.7, f32[192,1024]{1,0:T(8,128)S(1)} %mix.5.refs_2_.refs_3_), custom_call_target="tpu_custom_call" | custom-call | flops 1 | bytes 1 | tf_op jit(solution)/shard_map/mix/pallas_call | solution.py:509
  199.9 1.8 collective-permute-done.26.refs_0_
  201.8 1.6 collective-permute-done.30.refs_1_
  203.4 4.1 %mix.7 = bf16[192,1024]{1,0:T(8,128)(2,1)} custom-call(s32[2]{0:T(128)S(1)} %pad_add_fusion.places, bf16[192,1024]{1,0:T(8,128)(2,1)S(1)} %together.7.refs_0_, bf16[192,1024]{1,0:T(8,128)(2,1)S(1)} %collective-permute-done.30.refs_1_, bf16[16384,1024]{1,0:T(8,128)(2,1)} %refs_2_.7, f32[192,1024]{1,0:T(8,128)S(1)} %mix.6.refs_1_.refs_3_), custom_call_target="tpu_custom_call" | custom-call | flops 1 | bytes 1 | tf_op jit(solution)/shard_map/mix/pallas_call | solution.py:509
  (132 shorter events, 4.9 us)
Async XLA Ops:
  0.0 22.4 %copy-start.4 = (bf16[2,96,1024]{2,1,0:T(8,128)(2,1)S(1)}, bf16[2,96,1024]{2,1,0:T(8,128)(2,1)}, u32[]{:S(2)}) copy-start(bf16[2,96,1024]{2,1,0:T(8,128)(2,1)} %param.8) | copy-start | bytes 1179652
  1.2 4.6 %collective-permute-start = (f32[2,96]{1,0:T(2,128)S(1)}, f32[2,96]{1,0:T(2,128)S(1)}, u32[]{:S(2)}, u32[]{:S(2)}) collective-permute-start(f32[2,96]{1,0:T(2,128)S(1)} %fusion), channel_id=1, source_target_pairs={{0,2},{1,3},{2,0},{3,1},{4,6},{5,7},{6,4},{7,5},{8,10},{9,11},{10,... | collective-permute-start | bytes 2312 | tf_op jit(solution)/shard_map/ppermute | solution.py:223
  5.8 1.1 collective-permute-start.1
  7.0 3.6 %collective-permute-start.2 = (f32[2,96]{1,0:T(2,128)S(1)}, f32[2,96]{1,0:T(2,128)S(1)}, u32[]{:S(2)}, u32[]{:S(2)}) collective-permute-start(f32[2,96]{1,0:T(2,128)S(1)} %add.138), channel_id=1, source_target_pairs={{0,4},{1,5},{2,6},{3,7},{4,0},{5,1},{6,2},{7,3},{8,12},{9,13},{10,... | collective-permute-start | bytes 2312 | tf_op jit(solution)/shard_map/ppermute | solution.py:223
  10.6 11.6 %collective-permute-start.3 = (f32[2,96]{1,0:T(2,128)S(1)}, f32[2,96]{1,0:T(2,128)S(1)}, u32[]{:S(2)}, u32[]{:S(2)}) collective-permute-start(f32[2,96]{1,0:T(2,128)S(1)} %add.139), channel_id=1, source_target_pairs={{0,8},{1,9},{2,10},{3,11},{4,12},{5,13},{6,14},{7,15},{8,0},{9,1},... | collective-permute-start | bytes 2312 | tf_op jit(solution)/shard_map/ppermute | solution.py:223
  13.6 1.4 copy-start.6
  15.2 16.8 %copy-start.19 = (bf16[400,256]{1,0:T(8,128)(2,1)}, bf16[400,256]{1,0:T(8,128)(2,1)S(1)}, u32[]{:S(2)}) copy-start(bf16[400,256]{1,0:T(8,128)(2,1)S(1)} %get-tuple-element.36.refs_0_) | copy-start | bytes 614404
  15.2 16.8 %collective-permute-start.5 = (bf16[400,256]{1,0:T(8,128)(2,1)S(1)}, bf16[400,256]{1,0:T(8,128)(2,1)S(1)}, u32[]{:S(2)}, u32[]{:S(2)}) collective-permute-start(bf16[400,256]{1,0:T(8,128)(2,1)S(1)} %get-tuple-element.39), channel_id=1, source_target_pairs={{0,2},{1,3},{2,0},{3,1},{4,6},{5,7},{6,4},{7,5},{8,10},{9,11},{10,... | collective-permute-start | bytes 614408 | tf_op jit(solution)/shard_map/ppermute | solution.py:223
  16.8 15.2 %collective-permute-start.6 = (bf16[400,256]{1,0:T(8,128)(2,1)S(1)}, bf16[400,256]{1,0:T(8,128)(2,1)S(1)}, u32[]{:S(2)}, u32[]{:S(2)}) collective-permute-start(bf16[400,256]{1,0:T(8,128)(2,1)S(1)} %get-tuple-element.40), channel_id=1, source_target_pairs={{0,6},{1,7},{2,4},{3,5},{4,2},{5,3},{6,0},{7,1},{8,14},{9,15},{10,... | collective-permute-start | bytes 614408 | tf_op jit(solution)/shard_map/ppermute | solution.py:223
  18.3 24.7 %collective-permute-start.7 = (bf16[400,256]{1,0:T(8,128)(2,1)S(1)}, bf16[400,256]{1,0:T(8,128)(2,1)S(1)}, u32[]{:S(2)}, u32[]{:S(2)}) collective-permute-start(bf16[400,256]{1,0:T(8,128)(2,1)S(1)} %get-tuple-element.44), channel_id=1, source_target_pairs={{0,8},{1,9},{2,10},{3,11},{4,12},{5,13},{6,14},{7,15},{8,0},{9,1},... | collective-permute-start | bytes 614408 | tf_op jit(solution)/shard_map/ppermute | solution.py:223
  18.6 25.8 %collective-permute-start.8 = (bf16[400,256]{1,0:T(8,128)(2,1)S(1)}, bf16[400,256]{1,0:T(8,128)(2,1)S(1)}, u32[]{:S(2)}, u32[]{:S(2)}) collective-permute-start(bf16[400,256]{1,0:T(8,128)(2,1)S(1)} %get-tuple-element.45), channel_id=1, source_target_pairs={{0,10},{1,11},{2,8},{3,9},{4,14},{5,15},{6,12},{7,13},{8,2},{9,3},... | collective-permute-start | bytes 614408 | tf_op jit(solution)/shard_map/ppermute | solution.py:223
  22.2 22.3 %collective-permute-start.9 = (bf16[400,256]{1,0:T(8,128)(2,1)S(1)}, bf16[400,256]{1,0:T(8,128)(2,1)S(1)}, u32[]{:S(2)}, u32[]{:S(2)}) collective-permute-start(bf16[400,256]{1,0:T(8,128)(2,1)S(1)} %get-tuple-element.46), channel_id=1, source_target_pairs={{0,12},{1,13},{2,14},{3,15},{4,8},{5,9},{6,10},{7,11},{8,4},{9,5},... | collective-permute-start | bytes 614408 | tf_op jit(solution)/shard_map/ppermute | solution.py:223
  32.0 11.0 %copy-start.7 = (bf16[400,256]{1,0:T(8,128)(2,1)}, bf16[400,256]{1,0:T(8,128)(2,1)S(1)}, u32[]{:S(2)}) copy-start(bf16[400,256]{1,0:T(8,128)(2,1)S(1)} %collective-permute-done.6.refs_2_.refs_3_) | copy-start | bytes 614404
  43.0 1.5 copy-start.9
  44.4 0.7 copy-start.11
  44.4 0.8 copy-start.13
  44.4 1.3 copy-start.26
  44.5 5.3 %copy-start.25 = (s32[16,16]{1,0:T(8,128)S(1)}, s32[16,16]{1,0:T(8,128)}, u32[]{:S(2)}) copy-start(s32[16,16]{1,0:T(8,128)} %param.15) | copy-start | bytes 3076
  45.2 14.0 %collective-permute-start.11 = (s16[1936,640]{1,0:T(8,128)(2,1)}, s16[1936,640]{1,0:T(8,128)(2,1)}, u32[]{:S(2)}, u32[]{:S(2)}) collective-permute-start(s16[1936,640]{1,0:T(8,128)(2,1)} %get-tuple-element.47.refs_0_), channel_id=1, source_target_pairs={{0,1},{1,0},{2,3},{3,2},{4,5},{5,4},{6,7},{7,6},{8,9},{9,8},{10,11... | collective-permute-start | bytes 7434248 | tf_op jit(solution)/shard_map/ppermute | solution.py:223
  45.2 7.4 %collective-permute-start.4 = (s16[1936,512]{1,0:T(8,128)(2,1)}, s16[1936,512]{1,0:T(8,128)(2,1)S(1)}, u32[]{:S(2)}, u32[]{:S(2)}) collective-permute-start(s16[1936,512]{1,0:T(8,128)(2,1)} %get-tuple-element.38), channel_id=1, source_target_pairs={{0,1},{1,0},{2,3},{3,2},{4,5},{5,4},{6,7},{7,6},{8,9},{9,8},{10,11... | collective-permute-start | bytes 5947400 | tf_op jit(solution)/shard_map/ppermute | solution.py:223
  45.8 11.2 %collective-permute-start.12 = (bf16[400,256]{1,0:T(8,128)(2,1)S(1)}, bf16[400,256]{1,0:T(8,128)(2,1)S(1)}, u32[]{:S(2)}, u32[]{:S(2)}) collective-permute-start(bf16[400,256]{1,0:T(8,128)(2,1)S(1)} %get-tuple-element.51), channel_id=1, source_target_pairs={{0,4},{1,5},{2,6},{3,7},{4,0},{5,1},{6,2},{7,3},{8,12},{9,13},{10,... | collective-permute-start | bytes 614408 | tf_op jit(solution)/shard_map/ppermute | solution.py:223
  48.2 11.0 %collective-permute-start.13 = (bf16[400,256]{1,0:T(8,128)(2,1)S(1)}, bf16[400,256]{1,0:T(8,128)(2,1)S(1)}, u32[]{:S(2)}, u32[]{:S(2)}) collective-permute-start(bf16[400,256]{1,0:T(8,128)(2,1)S(1)} %get-tuple-element.52), channel_id=1, source_target_pairs={{0,14},{1,15},{2,12},{3,13},{4,10},{5,11},{6,8},{7,9},{8,6},{9,7},... | collective-permute-start | bytes 614408 | tf_op jit(solution)/shard_map/ppermute | solution.py:223
  56.3 24.4 %collective-permute-start.10 = (s16[976,512]{1,0:T(8,128)(2,1)S(1)}, s16[976,512]{1,0:T(8,128)(2,1)S(1)}, u32[]{:S(2)}, u32[]{:S(2)}) collective-permute-start(s16[976,512]{1,0:T(8,128)(2,1)S(1)} %get-tuple-element.49), channel_id=1, source_target_pairs={{0,2},{1,3},{2,0},{3,1},{4,6},{5,7},{6,4},{7,5},{8,10},{9,11},{10,... | collective-permute-start | bytes 2998280 | tf_op jit(solution)/shard_map/ppermute | solution.py:223
  57.0 8.0 %copy-start.15 = (bf16[400,256]{1,0:T(8,128)(2,1)}, bf16[400,256]{1,0:T(8,128)(2,1)S(1)}, u32[]{:S(2)}) copy-start(bf16[400,256]{1,0:T(8,128)(2,1)S(1)} %collective-permute-done.12.refs_1_.refs_2_) | copy-start | bytes 614404
  59.2 5.8 %copy-start.17 = (bf16[400,256]{1,0:T(8,128)(2,1)}, bf16[400,256]{1,0:T(8,128)(2,1)S(1)}, u32[]{:S(2)}) copy-start(bf16[400,256]{1,0:T(8,128)(2,1)S(1)} %collective-permute-done.13.refs_2_.refs_7_) | copy-start | bytes 614404
  65.0 30.7 %collective-permute-start.15 = (s16[976,640]{1,0:T(8,128)(2,1)}, s16[976,640]{1,0:T(8,128)(2,1)S(1)}, u32[]{:S(2)}, u32[]{:S(2)}) collective-permute-start(s16[976,640]{1,0:T(8,128)(2,1)} %get-tuple-element.56), channel_id=1, source_target_pairs={{0,4},{1,5},{2,6},{3,7},{4,0},{5,1},{6,2},{7,3},{8,12},{9,13},{10,... | collective-permute-start | bytes 3747848 | tf_op jit(solution)/shard_map/ppermute | solution.py:223
  82.3 0.9 copy-start.2
  83.3 21.8 %collective-permute-start.14 = (s16[496,512]{1,0:T(8,128)(2,1)}, s16[496,512]{1,0:T(8,128)(2,1)}, u32[]{:S(2)}, u32[]{:S(2)}) collective-permute-start(s16[496,512]{1,0:T(8,128)(2,1)} %get-tuple-element.55), channel_id=1, source_target_pairs={{0,4},{1,5},{2,6},{3,7},{4,0},{5,1},{6,2},{7,3},{8,12},{9,13},{10,... | collective-permute-start | bytes 1523720 | tf_op jit(solution)/shard_map/ppermute | solution.py:223
  95.7 1.1 copy-start.3
  96.8 2.9 %copy-start.8 = (bf16[400,256]{1,0:T(8,128)(2,1)S(1)}, bf16[400,256]{1,0:T(8,128)(2,1)}, u32[]{:S(2)}) copy-start(bf16[400,256]{1,0:T(8,128)(2,1)} %copy-done.7) | copy-start | bytes 614404
  96.8 2.9 %copy-start.10 = (bf16[400,256]{1,0:T(8,128)(2,1)S(1)}, bf16[400,256]{1,0:T(8,128)(2,1)}, u32[]{:S(2)}) copy-start(bf16[400,256]{1,0:T(8,128)(2,1)} %copy-done.9) | copy-start | bytes 614404
  96.8 2.9 %copy-start.12 = (bf16[400,256]{1,0:T(8,128)(2,1)S(1)}, bf16[400,256]{1,0:T(8,128)(2,1)}, u32[]{:S(2)}) copy-start(bf16[400,256]{1,0:T(8,128)(2,1)} %copy-done.11) | copy-start | bytes 614404
  96.8 2.9 %copy-start.14 = (bf16[400,256]{1,0:T(8,128)(2,1)S(1)}, bf16[400,256]{1,0:T(8,128)(2,1)}, u32[]{:S(2)}) copy-start(bf16[400,256]{1,0:T(8,128)(2,1)} %copy-done.13) | copy-start | bytes 614404
  96.8 2.9 %copy-start.16 = (bf16[400,256]{1,0:T(8,128)(2,1)S(1)}, bf16[400,256]{1,0:T(8,128)(2,1)}, u32[]{:S(2)}) copy-start(bf16[400,256]{1,0:T(8,128)(2,1)} %copy-done.15) | copy-start | bytes 614404
  96.8 2.9 %copy-start.18 = (bf16[400,256]{1,0:T(8,128)(2,1)S(1)}, bf16[400,256]{1,0:T(8,128)(2,1)}, u32[]{:S(2)}) copy-start(bf16[400,256]{1,0:T(8,128)(2,1)} %copy-done.17) | copy-start | bytes 614404
  96.8 2.9 %copy-start.20 = (bf16[400,256]{1,0:T(8,128)(2,1)S(1)}, bf16[400,256]{1,0:T(8,128)(2,1)}, u32[]{:S(2)}) copy-start(bf16[400,256]{1,0:T(8,128)(2,1)} %copy-done.19) | copy-start | bytes 614404
  98.8 1.0 copy-start
  98.8 13.2 %collective-permute-start.17 = (s16[496,640]{1,0:T(8,128)(2,1)}, s16[496,640]{1,0:T(8,128)(2,1)S(1)}, u32[]{:S(2)}, u32[]{:S(2)}) collective-permute-start(s16[496,640]{1,0:T(8,128)(2,1)} %get-tuple-element.60), channel_id=1, source_target_pairs={{0,2},{1,3},{2,0},{3,1},{4,6},{5,7},{6,4},{7,5},{8,10},{9,11},{10,... | collective-permute-start | bytes 1904648 | tf_op jit(solution)/shard_map/ppermute | solution.py:223
  105.0 7.0 %copy-start.1 = (f32[2,192,640]{2,1,0:T(8,128)S(1)}, f32[2,192,640]{2,1,0:T(8,128)}, u32[]{:S(2)}) copy-start(f32[2,192,640]{2,1,0:T(8,128)} %copy-done) | copy-start | bytes 2949124
  107.3 0.7 copy-start.21
  108.0 22.3 %collective-permute-start.16 = (s16[256,512]{1,0:T(8,128)(2,1)}, s16[256,512]{1,0:T(8,128)(2,1)}, u32[]{:S(2)}, u32[]{:S(2)}) collective-permute-start(s16[256,512]{1,0:T(8,128)(2,1)} %get-tuple-element.59), channel_id=1, source_target_pairs={{0,8},{1,9},{2,10},{3,11},{4,12},{5,13},{6,14},{7,15},{8,0},{9,1},... | collective-permute-start | bytes 786440 | tf_op jit(solution)/shard_map/ppermute | solution.py:223
  111.6 25.3 %collective-permute-start.20 = (bf16[8,400,256]{2,1,0:T(8,128)(2,1)S(1)}, bf16[8,400,256]{2,1,0:T(8,128)(2,1)}, u32[]{:S(2)}, u32[]{:S(2)}) collective-permute-start(bf16[8,400,256]{2,1,0:T(8,128)(2,1)S(1)} %pack.3.refs_0_.own), channel_id=1, source_target_pairs={{0,1},{1,0},{2,3},{3,2},{4,5},{5,4},{6,7},{7,6},{8,9},{9,8},{10,11... | collective-permute-start | bytes 4915208 | tf_op jit(solution)/shard_map/ppermute | solution.py:223
  112.1 1.0 copy-start.22
  113.1 17.3 %copy-start.23 = (f32[1,192,512]{2,1,0:T(8,128)S(1)}, f32[1,192,512]{2,1,0:T(8,128)}, u32[]{:S(2)}) copy-start(f32[1,192,512]{2,1,0:T(8,128)} %copy-done.21) | copy-start | bytes 1179652
  113.1 17.3 %copy-start.24 = (f32[192,128]{1,0:T(8,128)S(1)}, f32[192,128]{1,0:T(8,128)}, u32[]{:S(2)}) copy-start(f32[192,128]{1,0:T(8,128)} %get-tuple-element.80.sine) | copy-start | bytes 294916
  113.5 21.9 %collective-permute-start.18 = (s16[256,640]{1,0:T(8,128)(2,1)S(1)}, s16[256,640]{1,0:T(8,128)(2,1)S(1)}, u32[]{:S(2)}, u32[]{:S(2)}) collective-permute-start(s16[256,640]{1,0:T(8,128)(2,1)S(1)} %get-tuple-element.63), channel_id=1, source_target_pairs={{0,8},{1,9},{2,10},{3,11},{4,12},{5,13},{6,14},{7,15},{8,0},{9,1},... | collective-permute-start | bytes 983048 | tf_op jit(solution)/shard_map/ppermute | solution.py:223
  135.4 1.2 collective-permute-start.19
  146.9 25.5 %copy-start.5 = (bf16[2,96,1024]{2,1,0:T(8,128)(2,1)S(1)}, bf16[2,96,1024]{2,1,0:T(8,128)(2,1)}, u32[]{:S(2)}) copy-start(bf16[2,96,1024]{2,1,0:T(8,128)(2,1)} %param.8) | copy-start | bytes 1179652
  146.9 18.9 %collective-permute-start.21 = (bf16[192,1024]{1,0:T(8,128)(2,1)S(1)}, bf16[192,1024]{1,0:T(8,128)(2,1)S(1)}, u32[]{:S(2)}, u32[]{:S(2)}) collective-permute-start(bf16[192,1024]{1,0:T(8,128)(2,1)S(1)} %bitcast.50), channel_id=1, source_target_pairs={{0,4},{1,5},{2,6},{3,7},{4,0},{5,1},{6,2},{7,3},{8,12},{9,13},{10,... | collective-permute-start | bytes 1179656 | tf_op jit(solution)/shard_map/ppermute | solution.py:223
  147.0 18.8 %collective-permute-start.22 = (bf16[192,1024]{1,0:T(8,128)(2,1)S(1)}, bf16[192,1024]{1,0:T(8,128)(2,1)S(1)}, u32[]{:S(2)}, u32[]{:S(2)}) collective-permute-start(bf16[192,1024]{1,0:T(8,128)(2,1)S(1)} %bitcast.51), channel_id=1, source_target_pairs={{0,2},{1,3},{2,0},{3,1},{4,6},{5,7},{6,4},{7,5},{8,10},{9,11},{10,... | collective-permute-start | bytes 1179656 | tf_op jit(solution)/shard_map/ppermute | solution.py:223
  148.0 20.3 %collective-permute-start.23 = (bf16[192,1024]{1,0:T(8,128)(2,1)S(1)}, bf16[192,1024]{1,0:T(8,128)(2,1)S(1)}, u32[]{:S(2)}, u32[]{:S(2)}) collective-permute-start(bf16[192,1024]{1,0:T(8,128)(2,1)S(1)} %bitcast.52), channel_id=1, source_target_pairs={{0,8},{1,9},{2,10},{3,11},{4,12},{5,13},{6,14},{7,15},{8,0},{9,1},... | collective-permute-start | bytes 1179656 | tf_op jit(solution)/shard_map/ppermute | solution.py:223
  150.6 17.7 %collective-permute-start.24 = (bf16[192,1024]{1,0:T(8,128)(2,1)S(1)}, bf16[192,1024]{1,0:T(8,128)(2,1)S(1)}, u32[]{:S(2)}, u32[]{:S(2)}) collective-permute-start(bf16[192,1024]{1,0:T(8,128)(2,1)S(1)} %bitcast.53), channel_id=1, source_target_pairs={{0,1},{1,0},{2,3},{3,2},{4,5},{5,4},{6,7},{7,6},{8,9},{9,8},{10,11... | collective-permute-start | bytes 1179656 | tf_op jit(solution)/shard_map/ppermute | solution.py:223
  168.4 7.3 %collective-permute-start.28 = (bf16[3,192,1024]{2,1,0:T(8,128)(2,1)S(1)}, bf16[3,192,1024]{2,1,0:T(8,128)(2,1)}, u32[]{:S(2)}, u32[]{:S(2)}) collective-permute-start(bf16[3,192,1024]{2,1,0:T(8,128)(2,1)S(1)} %get-tuple-element.66.refs_0_), channel_id=1, source_target_pairs={{0,1},{1,0},{2,3},{3,2},{4,5},{5,4},{6,7},{7,6},{8,9},{9,8},{10,11... | collective-permute-start | bytes 3538952 | tf_op jit(solution)/shard_map/ppermute | solution.py:223
  168.5 20.1 %collective-permute-start.27 = (bf16[2,192,1024]{2,1,0:T(8,128)(2,1)S(1)}, bf16[2,192,1024]{2,1,0:T(8,128)(2,1)}, u32[]{:S(2)}, u32[]{:S(2)}) collective-permute-start(bf16[2,192,1024]{2,1,0:T(8,128)(2,1)S(1)} %get-tuple-element.65.refs_1_), channel_id=1, source_target_pairs={{0,2},{1,3},{2,0},{3,1},{4,6},{5,7},{6,4},{7,5},{8,10},{9,11},{10,... | collective-permute-start | bytes 2359304 | tf_op jit(solution)/shard_map/ppermute | solution.py:223
  169.8 13.2 %collective-permute-start.25 = (bf16[192,1024]{1,0:T(8,128)(2,1)S(1)}, bf16[192,1024]{1,0:T(8,128)(2,1)}, u32[]{:S(2)}, u32[]{:S(2)}) collective-permute-start(bf16[192,1024]{1,0:T(8,128)(2,1)S(1)} %together.6.refs_0_), channel_id=1, source_target_pairs={{0,12},{1,13},{2,14},{3,15},{4,8},{5,9},{6,10},{7,11},{8,4},{9,5},... | collective-permute-start | bytes 1179656 | tf_op jit(solution)/shard_map/ppermute | solution.py:223
  189.9 3.0 %collective-permute-start.29 = (bf16[3,192,1024]{2,1,0:T(8,128)(2,1)S(1)}, bf16[3,192,1024]{2,1,0:T(8,128)(2,1)}, u32[]{:S(2)}, u32[]{:S(2)}) collective-permute-start(bf16[3,192,1024]{2,1,0:T(8,128)(2,1)S(1)} %pack.5.refs_0_), channel_id=1, source_target_pairs={{0,1},{1,0},{2,3},{3,2},{4,5},{5,4},{6,7},{7,6},{8,9},{9,8},{10,11... | collective-permute-start | bytes 3538952 | tf_op jit(solution)/shard_map/ppermute | solution.py:223
  190.0 11.7 %collective-permute-start.26 = (bf16[192,1024]{1,0:T(8,128)(2,1)}, bf16[192,1024]{1,0:T(8,128)(2,1)S(1)}, u32[]{:S(2)}, u32[]{:S(2)}) collective-permute-start(bf16[192,1024]{1,0:T(8,128)(2,1)} %collective-permute-done.25.refs_1_), channel_id=1, source_target_pairs={{0,2},{1,3},{2,0},{3,1},{4,6},{5,7},{6,4},{7,5},{8,10},{9,11},{10,... | collective-permute-start | bytes 1179656 | tf_op jit(solution)/shard_map/ppermute | solution.py:223
  201.7 1.7 collective-permute-start.30

commit v15 on v14

--- a/solution.py
+++ b/solution.py
@@ -394,7 +394,7 @@
     store_codes(sent, powers, total(1 - bit[0], held_out, landed_out), index, steps)
 
 
-def fold(bit, held, landed, low, after):
+def fold(bit, held, landed, low, cost, after):
     blocks, rows, columns = held.shape
     steps = blocks // 2
     coded = coded_rows(rows)
@@ -427,7 +427,7 @@
             jax.ShapeDtypeStruct((steps * coded + TILE, columns), jnp.int16),
         ],
         compiler_params=pltpu.CompilerParams(vmem_limit_bytes=VMEM_LIMIT),
-        cost_estimate=SHORT,
+        cost_estimate=cost,
         name="fold",
     )(bit, held, held, landed, landed, landed, *after)
 
@@ -766,8 +766,8 @@
     cosine = jnp.concatenate([jnp.cos(angles)] * 2, 1)
     sine = jnp.concatenate([-jnp.sin(angles), jnp.sin(angles)], 1)
 
-    def folded(part, b, landed, low, *after):
-        return fold(bits[b], part, landed, low, after)
+    def folded(part, b, landed, low, *after, cost=SHORT):
+        return fold(bits[b], part, landed, low, cost, after)
 
     def finished(part, number, landed, *after):
         return finish(bits[0], part, landed, cosine, sine, PART_HEADS[number], after)
@@ -785,15 +785,17 @@
     core_b = swap(sent_b, 1)
     for k in (2, 7):
         handed(k)
-    held_a, sent_a = folded(held_a, 1, core_a, 1, sent_b)
+    held_b, sent_b = folded(held_b, 2, core_b, 2, sent_b)
+    line_b = swap(sent_b, 4)
+    held_a, sent_a = folded(
+        held_a, 1, core_a, 1, held_b, cache_pieces[2], cache_pieces[7], cost=LONG
+    )
     line_a = swap(sent_a, 2)
-    held_b, sent_b = folded(held_b, 2, core_b, 2, held_a, cache_pieces[2], cache_pieces[7])
-    line_b = swap(sent_b, 4)
+    held_b, sent_b = folded(held_b, 1, line_b, 1, held_a)
+    line_b = swap(sent_b, 2)
     held_a, sent_a = folded(held_a, 2, line_a, 1, held_b)
     line_a = swap(sent_a, 4)
-    held_b, sent_b = folded(held_b, 1, line_b, 1, held_a)
-    line_b = swap(sent_b, 2)
-    (cache_own,) = pack(cache_pieces, [tuple(range(KVH))], [held_b])
+    (cache_own,) = pack(cache_pieces, [tuple(range(KVH))], [held_a])
     cache_other = swap(cache_own, 1)
     held_a, sent_a = folded(held_a, 3, line_a, 1, cache_own)
     line_a = swap(sent_a, 8)

time: 208 us -> 210 us (level)
  local copies, waits for them, and re-layouts: 8.98 us -> 14.3 us
    unnamed x56 -> x52, local copies, waits for them, and re-layouts: 6.13 us -> 11.5 us
  transfers between devices with their start and end apart: 31 -> 31, of which waited for: 20 -> 18; matrix products, arithmetic and copies ran while one was open for 3% -> 3% of each run, Pallas kernels for 27% -> 26%
where the time goes in v15:
time: 210 us; the launch traced here: 209 us
  waiting for transfers between devices  84 us (40%)
  Pallas kernels  69.2 us (33%)
  starting transfers between devices  35.5 us (17%)
  local copies, waits for them, and re-layouts  14.3 us (7%)
  other arithmetic  5.3 us (3%)
    ppermute x31, waiting for transfers between devices, swap(): return lax.ppermute(value, 'tensor', [(i, i ^ bit) for i in range(devices)])  84 us
    ppermute x31, starting transfers between devices, swap(): return lax.ppermute(value, 'tensor', [(i, i ^ bit) for i in range(devices)])  35.5 us
    pallas_call x4, Pallas kernels, mix(): pl.pallas_call(functools.partial(mix_kernel, len(pieces)), in_specs=[pl.B...  21.4 us
    pallas_call x2, Pallas kernels, project(): pl.pallas_call(functools.partial(project_kernel, part), grid_spec=pltpu.P...  20.3 us
    pallas_call x6, Pallas kernels, fold(): pl.pallas_call(functools.partial(fold_kernel, steps, low), grid_spec=pltp...  16.9 us
    unnamed x52, local copies, waits for them, and re-layouts  11.5 us
    pallas_call x1, Pallas kernels, attend(): pl.pallas_call(attend_kernel, in_specs=[pl.BlockSpec(memory_space=pltpu.S...  8.39 us
  transfers between devices with their start and end apart: 31, of which 18 were waited for; matrix products, arithmetic and copies ran while one was open for 3% of the time, Pallas kernels for 26%

profile of v15, /device:TPU:0, one launch (start us, length us, event | category | flops | bytes accessed | tf_op | source)
XLA Modules:
  0.0 209.0 jit_solution(7514084123810309053)
XLA Ops:
  0.0 1.2 fusion
  1.2 3.0 %collective-permute-start = (f32[2,96]{1,0:T(2,128)S(1)}, f32[2,96]{1,0:T(2,128)S(1)}, u32[]{:S(2)}, u32[]{:S(2)}) collective-permute-start(f32[2,96]{1,0:T(2,128)S(1)} %fusion), channel_id=1, source_target_pairs={{0,2},{1,3},{2,0},{3,1},{4,6},{5,7},{6,4},{7,5},{8,10},{9,11},{10,... | collective-permute-start | bytes 2312 | tf_op jit(solution)/shard_map/ppermute | solution.py:223
  4.3 1.5 collective-permute-done
  5.8 1.1 collective-permute-done.1
  7.0 2.1 collective-permute-start.2
  9.0 0.8 reshape.240
  9.8 0.7 convert_element_type.29
  10.6 3.0 %collective-permute-start.3 = (f32[2,96]{1,0:T(2,128)S(1)}, f32[2,96]{1,0:T(2,128)S(1)}, u32[]{:S(2)}, u32[]{:S(2)}) collective-permute-start(f32[2,96]{1,0:T(2,128)S(1)} %add.139), channel_id=1, source_target_pairs={{0,8},{1,9},{2,10},{3,11},{4,12},{5,13},{6,14},{7,15},{8,0},{9,1},... | collective-permute-start | bytes 2312 | tf_op jit(solution)/shard_map/ppermute | solution.py:223
  13.6 1.4 copy-done.3
  15.2 1.6 collective-permute-start.5
  16.8 1.5 collective-permute-start.6
  18.6 3.5 %collective-permute-start.8 = (bf16[400,256]{1,0:T(8,128)(2,1)S(1)}, bf16[400,256]{1,0:T(8,128)(2,1)S(1)}, u32[]{:S(2)}, u32[]{:S(2)}) collective-permute-start(bf16[400,256]{1,0:T(8,128)(2,1)S(1)} %get-tuple-element.46), channel_id=1, source_target_pairs={{0,10},{1,11},{2,8},{3,9},{4,14},{5,15},{6,12},{7,13},{8,2},{9,3},... | collective-permute-start | bytes 614408 | tf_op jit(solution)/shard_map/ppermute | solution.py:223
  22.6 9.3 %project.2 = (f32[8,192,512]{2,1,0:T(8,128)}, s16[1936,512]{1,0:T(8,128)(2,1)}) custom-call(s32[1]{0:T(128)} %bitcast.2.core, bf16[192,1024]{1,0:T(8,128)(2,1)S(1)} %bitcast.47, bf16[1024,18432]{1,0:T(8,128)(2,1)} %weights.3, bf16[400,256]{1,0:T(8,128)(2,1)S(1)} %get-tuple-element.36.refs_0_), custom_call_target="tpu_custom_call" | custom-call | flops 1 | bytes 1 | tf_op jit(solution)/shard_map/project/pallas_call | solution.py:352
  31.9 11.0 %project.3 = (f32[8,192,640]{2,1,0:T(8,128)}, s16[1936,640]{1,0:T(8,128)(2,1)}) custom-call(s32[1]{0:T(128)} %bitcast.2.core, bf16[192,1024]{1,0:T(8,128)(2,1)S(1)} %bitcast.48, bf16[1024,18432]{1,0:T(8,128)(2,1)} %weights.3, f32[8,192,512]{2,1,0:T(8,128)} %get-tuple-element.37.refs_0_.held.held_out, bf16[400,256]{1,0:T(8,128)(2,1)S(1)} %collective-permute-done.5.refs_1_, ...), custom_call_target="tpu_custom_call" | custom-call | flops 1 | bytes 1 | tf_op jit(solution)/shard_map/project/pallas_call | solution.py:352
  43.0 1.5 collective-permute-done.8.refs_4_.refs_5_
  44.5 0.6 copy-done.10
  45.8 2.4 %collective-permute-start.11 = (bf16[400,256]{1,0:T(8,128)(2,1)S(1)}, bf16[400,256]{1,0:T(8,128)(2,1)S(1)}, u32[]{:S(2)}, u32[]{:S(2)}) collective-permute-start(bf16[400,256]{1,0:T(8,128)(2,1)S(1)} %get-tuple-element.50), channel_id=1, source_target_pairs={{0,4},{1,5},{2,6},{3,7},{4,0},{5,1},{6,2},{7,3},{8,12},{9,13},{10,... | collective-permute-start | bytes 614408 | tf_op jit(solution)/shard_map/ppermute | solution.py:223
  48.2 1.6 collective-permute-start.12
  49.9 3.0 %collective-permute-done.10.landed.landed_out.landed_powers = s16[1936,640]{1,0:T(8,128)(2,1)S(1)} collective-permute-done((s16[1936,640]{1,0:T(8,128)(2,1)}, s16[1936,640]{1,0:T(8,128)(2,1)S(1)}, u32[]{:S(2)}, u32[]{:S(2)}) %collective-permute-start.10) | collective-permute-done | bytes 2478112 | tf_op jit(solution)/shard_map/ppermute | solution.py:223
  52.9 4.2 %fold.6 = (f32[4,192,640]{2,1,0:T(8,128)S(1)}, s16[976,640]{1,0:T(8,128)(2,1)S(1)}) custom-call(s32[1]{0:T(128)} %bitcast.4.bit, f32[8,192,640]{2,1,0:T(8,128)} %get-tuple-element.41.held.held_out, f32[8,192,640]{2,1,0:T(8,128)} %get-tuple-element.41.held.held_out, s16[1936,640]{1,0:T(8,128)(2,1)S(1)} %collective-permute-done.10.landed.landed_out.landed_powers, ...), custom_call_target="tpu_custom_call" | custom-call | flops 1 | bytes 1 | tf_op jit(solution)/shard_map/fold/pallas_call | solution.py:406
  57.1 2.4 %collective-permute-start.14 = (s16[976,640]{1,0:T(8,128)(2,1)S(1)}, s16[976,640]{1,0:T(8,128)(2,1)S(1)}, u32[]{:S(2)}, u32[]{:S(2)}) collective-permute-start(s16[976,640]{1,0:T(8,128)(2,1)S(1)} %get-tuple-element.54), channel_id=1, source_target_pairs={{0,4},{1,5},{2,6},{3,7},{4,0},{5,1},{6,2},{7,3},{8,12},{9,13},{10,... | collective-permute-start | bytes 3747848 | tf_op jit(solution)/shard_map/ppermute | solution.py:223
  59.6 4.2 %fold.7 = (f32[4,192,512]{2,1,0:T(8,128)S(1)}, s16[976,512]{1,0:T(8,128)(2,1)S(1)}) custom-call(s32[1]{0:T(128)} %bitcast.5.bit, f32[8,192,512]{2,1,0:T(8,128)} %get-tuple-element.37.refs_0_.held.held_out, f32[8,192,512]{2,1,0:T(8,128)} %get-tuple-element.37.refs_0_.held.held_out, s16[1936,512]{1,0:T(8,128)(2,1)} %collective-permute-done.4.landed.landed_out.landed_powers, ...), custom_call_target="tpu_custom_call" | custom-call | flops 20000000000 | bytes 1 | tf_op jit(solution)/shard_map/fold/pallas_call | solution.py:406
  63.8 1.6 collective-permute-start.13
  65.7 21.6 %collective-permute-done.14.landed.landed_out.landed_powers = s16[976,640]{1,0:T(8,128)(2,1)S(1)} collective-permute-done((s16[976,640]{1,0:T(8,128)(2,1)S(1)}, s16[976,640]{1,0:T(8,128)(2,1)S(1)}, u32[]{:S(2)}, u32[]{:S(2)}) %collective-permute-start.14) | collective-permute-done | bytes 1249312 | tf_op jit(solution)/shard_map/ppermute | solution.py:223
  87.3 3.1 %fold.8 = (f32[2,192,640]{2,1,0:T(8,128)S(1)}, s16[496,640]{1,0:T(8,128)(2,1)}) custom-call(s32[1]{0:T(128)} %bitcast.5.bit, f32[4,192,640]{2,1,0:T(8,128)} %copy-done, f32[4,192,640]{2,1,0:T(8,128)} %copy-done, s16[976,640]{1,0:T(8,128)(2,1)S(1)} %collective-permute-done.14.landed.landed_out.landed_powers, ...), custom_call_target="tpu_custom_call" | custom-call | flops 1 | bytes 1 | tf_op jit(solution)/shard_map/fold/pallas_call | solution.py:406
  90.4 1.7 fold.9
  92.1 1.7 collective-permute-start.15
  94.1 1.1 fusion.5
  95.2 1.5 collective-permute-start.17
  96.7 0.9 copy-done.5
  97.7 0.9 copy-done.7
  98.6 0.9 copy-done.9
  99.5 0.9 copy-done.11
  100.5 0.9 copy-done.13
  101.4 0.9 copy-done.15
  102.3 0.9 copy-done.20
  103.3 0.9 copy-done.22
  104.3 1.3 collective-permute-done.15.landed.landed_out.landed_powers
  105.6 2.2 %fold.10 = (f32[1,192,512]{2,1,0:T(8,128)S(1)}, s16[256,512]{1,0:T(8,128)(2,1)}) custom-call(s32[1]{0:T(128)} %bitcast.3.bit, f32[2,192,512]{2,1,0:T(8,128)S(1)} %get-tuple-element.56.refs_8_.held.held_out, f32[2,192,512]{2,1,0:T(8,128)S(1)} %get-tuple-element.56.refs_8_.held.held_out, ...), custom_call_target="tpu_custom_call" | custom-call | flops 1 | bytes 1 | tf_op jit(solution)/shard_map/fold/pallas_call | solution.py:406
  107.7 0.7 copy-done.16
  109.1 1.2 pad_maximum_fusion
  110.8 1.0 copy-done.17
  111.8 1.6 fold.11
  113.3 2.1 %collective-permute-start.18 = (s16[256,640]{1,0:T(8,128)(2,1)S(1)}, s16[256,640]{1,0:T(8,128)(2,1)S(1)}, u32[]{:S(2)}, u32[]{:S(2)}) collective-permute-start(s16[256,640]{1,0:T(8,128)(2,1)S(1)} %get-tuple-element.63), channel_id=1, source_target_pairs={{0,8},{1,9},{2,10},{3,11},{4,12},{5,13},{6,14},{7,15},{8,0},{9,1},... | collective-permute-start | bytes 983048 | tf_op jit(solution)/shard_map/ppermute | solution.py:223
  115.5 14.4 %collective-permute-done.16.landed = s16[256,512]{1,0:T(8,128)(2,1)S(1)} collective-permute-done((s16[256,512]{1,0:T(8,128)(2,1)}, s16[256,512]{1,0:T(8,128)(2,1)S(1)}, u32[]{:S(2)}, u32[]{:S(2)}) %collective-permute-start.16) | collective-permute-done | bytes 262176 | tf_op jit(solution)/shard_map/ppermute | solution.py:223
  130.1 6.1 %collective-permute-done.18.landed.refs_1_ = s16[256,640]{1,0:T(8,128)(2,1)S(1)} collective-permute-done((s16[256,640]{1,0:T(8,128)(2,1)S(1)}, s16[256,640]{1,0:T(8,128)(2,1)S(1)}, u32[]{:S(2)}, u32[]{:S(2)}) %collective-permute-start.18) | collective-permute-done | bytes 327712 | tf_op jit(solution)/shard_map/ppermute | solution.py:223
  136.6 0.8 collective-permute-done.19
  137.6 0.7 slice_reduce_fusion
  139.1 8.4 %attend.1 = bf16[16,96,128]{2,1,0:T(8,128)(2,1)S(1)} custom-call(s32[24]{0:T(128)S(1)} %get-tuple-element.69.slot_request, bf16[16,96,128]{2,1,0:T(8,128)(2,1)S(1)} %bitcast.55, bf16[16,16,128]{2,1,0:T(8,128)(2,1)S(1)} %pad.12.new_keys, bf16[16,16,128]{2,1,0:T(8,128)(2,1)S(1)} %pad.13.new_values, bf16[8,400,256]{2,1,0:T(8,128)(2,1)S(1)} %pack.3.refs_0_.own, ...), custom_call_target="tpu_custom_call" | custom-call | flops 1 | bytes 1 | tf_op jit(solution)/shard_map/attend/pallas_call | solution.py:661
  147.7 1.6 collective-permute-start.22
  149.3 1.3 collective-permute-start.23
  150.6 13.8 %collective-permute-done.21.refs_0_ = bf16[192,1024]{1,0:T(8,128)(2,1)S(1)} collective-permute-done((bf16[192,1024]{1,0:T(8,128)(2,1)S(1)}, bf16[192,1024]{1,0:T(8,128)(2,1)S(1)}, u32[]{:S(2)}, u32[]{:S(2)}) %collective-permute-start.21) | collective-permute-done | bytes 393248 | tf_op jit(solution)/shard_map/ppermute | solution.py:223
  164.4 5.2 %collective-permute-done.23.refs_2_ = bf16[192,1024]{1,0:T(8,128)(2,1)S(1)} collective-permute-done((bf16[192,1024]{1,0:T(8,128)(2,1)S(1)}, bf16[192,1024]{1,0:T(8,128)(2,1)S(1)}, u32[]{:S(2)}, u32[]{:S(2)}) %collective-permute-start.23) | collective-permute-done | bytes 393248 | tf_op jit(solution)/shard_map/ppermute | solution.py:223
  170.4 1.4 collective-permute-start.25
  171.9 3.4 %mix.4.refs_3_ = f32[192,1024]{1,0:T(8,128)S(1)} custom-call(s32[2]{0:T(128)S(1)} %pad_add_fusion.1.places, bf16[192,1024]{1,0:T(8,128)(2,1)S(1)} %together.6.refs_0_, bf16[192,1024]{1,0:T(8,128)(2,1)S(1)} %collective-permute-done.24.refs_3_.refs_1_, bf16[16384,1024]{1,0:T(8,128)(2,1)} %refs_2_.7, bf16[192,1024]{1,0:T(8,128)(2,1)S(1)} %bitcast.49), custom_call_target="tpu_custom_call" | custom-call | flops 1 | bytes 1 | tf_op jit(solution)/shard_map/mix/pallas_call | solution.py:509
  175.3 7.0 %mix.5.refs_2_.refs_3_ = f32[192,1024]{1,0:T(8,128)S(1)} custom-call(s32[6]{0:T(128)S(1)} %stack.82.places, bf16[3,192,1024]{2,1,0:T(8,128)(2,1)S(1)} %get-tuple-element.66.refs_0_, bf16[3,192,1024]{2,1,0:T(8,128)(2,1)} %collective-permute-done.28.refs_1_, bf16[16384,1024]{1,0:T(8,128)(2,1)} %refs_2_.7, f32[192,1024]{1,0:T(8,128)S(1)} %mix.4.refs_3_), custom_call_target="tpu_custom_call" | custom-call | flops 1 | bytes 1 | tf_op jit(solution)/shard_map/mix/pallas_call | solution.py:509
  182.3 1.3 collective-permute-done.25.refs_1_
  183.6 6.3 %collective-permute-done.27.refs_0_ = bf16[2,192,1024]{2,1,0:T(8,128)(2,1)} collective-permute-done((bf16[2,192,1024]{2,1,0:T(8,128)(2,1)S(1)}, bf16[2,192,1024]{2,1,0:T(8,128)(2,1)}, u32[]{:S(2)}, u32[]{:S(2)}) %collective-permute-start.27) | collective-permute-done | bytes 786464 | tf_op jit(solution)/shard_map/ppermute | solution.py:223
  189.9 1.3 pack.5.refs_0_
  191.9 2.3 %collective-permute-done.29.refs_1_ = bf16[3,192,1024]{2,1,0:T(8,128)(2,1)} collective-permute-done((bf16[3,192,1024]{2,1,0:T(8,128)(2,1)S(1)}, bf16[3,192,1024]{2,1,0:T(8,128)(2,1)}, u32[]{:S(2)}, u32[]{:S(2)}) %collective-permute-start.29) | collective-permute-done | bytes 1179680 | tf_op jit(solution)/shard_map/ppermute | solution.py:223
  194.2 7.0 %mix.6.refs_1_.refs_3_ = f32[192,1024]{1,0:T(8,128)S(1)} custom-call(s32[6]{0:T(128)S(1)} %stack.75.places, bf16[3,192,1024]{2,1,0:T(8,128)(2,1)S(1)} %pack.5.refs_0_, bf16[3,192,1024]{2,1,0:T(8,128)(2,1)} %collective-permute-done.29.refs_1_, bf16[16384,1024]{1,0:T(8,128)(2,1)} %refs_2_.7, f32[192,1024]{1,0:T(8,128)S(1)} %mix.5.refs_2_.refs_3_), custom_call_target="tpu_custom_call" | custom-call | flops 1 | bytes 1 | tf_op jit(solution)/shard_map/mix/pallas_call | solution.py:509
  201.2 1.8 collective-permute-done.26.refs_0_
  203.1 1.6 collective-permute-done.30.refs_1_
  204.7 4.1 %mix.7 = bf16[192,1024]{1,0:T(8,128)(2,1)} custom-call(s32[2]{0:T(128)S(1)} %pad_add_fusion.places, bf16[192,1024]{1,0:T(8,128)(2,1)S(1)} %together.7.refs_0_, bf16[192,1024]{1,0:T(8,128)(2,1)S(1)} %collective-permute-done.30.refs_1_, bf16[16384,1024]{1,0:T(8,128)(2,1)} %refs_2_.7, f32[192,1024]{1,0:T(8,128)S(1)} %mix.6.refs_1_.refs_3_), custom_call_target="tpu_custom_call" | custom-call | flops 1 | bytes 1 | tf_op jit(solution)/shard_map/mix/pallas_call | solution.py:509
  (128 shorter events, 7.0 us)
Async XLA Ops:
  0.0 22.4 %copy-start.1 = (bf16[2,96,1024]{2,1,0:T(8,128)(2,1)S(1)}, bf16[2,96,1024]{2,1,0:T(8,128)(2,1)}, u32[]{:S(2)}) copy-start(bf16[2,96,1024]{2,1,0:T(8,128)(2,1)} %param.8) | copy-start | bytes 1179652
  1.2 4.6 %collective-permute-start = (f32[2,96]{1,0:T(2,128)S(1)}, f32[2,96]{1,0:T(2,128)S(1)}, u32[]{:S(2)}, u32[]{:S(2)}) collective-permute-start(f32[2,96]{1,0:T(2,128)S(1)} %fusion), channel_id=1, source_target_pairs={{0,2},{1,3},{2,0},{3,1},{4,6},{5,7},{6,4},{7,5},{8,10},{9,11},{10,... | collective-permute-start | bytes 2312 | tf_op jit(solution)/shard_map/ppermute | solution.py:223
  5.8 1.1 collective-permute-start.1
  7.0 3.6 %collective-permute-start.2 = (f32[2,96]{1,0:T(2,128)S(1)}, f32[2,96]{1,0:T(2,128)S(1)}, u32[]{:S(2)}, u32[]{:S(2)}) collective-permute-start(f32[2,96]{1,0:T(2,128)S(1)} %add.138), channel_id=1, source_target_pairs={{0,4},{1,5},{2,6},{3,7},{4,0},{5,1},{6,2},{7,3},{8,12},{9,13},{10,... | collective-permute-start | bytes 2312 | tf_op jit(solution)/shard_map/ppermute | solution.py:223
  10.6 11.6 %collective-permute-start.3 = (f32[2,96]{1,0:T(2,128)S(1)}, f32[2,96]{1,0:T(2,128)S(1)}, u32[]{:S(2)}, u32[]{:S(2)}) collective-permute-start(f32[2,96]{1,0:T(2,128)S(1)} %add.139), channel_id=1, source_target_pairs={{0,8},{1,9},{2,10},{3,11},{4,12},{5,13},{6,14},{7,15},{8,0},{9,1},... | collective-permute-start | bytes 2312 | tf_op jit(solution)/shard_map/ppermute | solution.py:223
  13.6 1.4 copy-start.3
  15.2 16.7 %copy-start.14 = (bf16[400,256]{1,0:T(8,128)(2,1)}, bf16[400,256]{1,0:T(8,128)(2,1)S(1)}, u32[]{:S(2)}) copy-start(bf16[400,256]{1,0:T(8,128)(2,1)S(1)} %get-tuple-element.36.refs_0_) | copy-start | bytes 614404
  15.2 16.7 %collective-permute-start.5 = (bf16[400,256]{1,0:T(8,128)(2,1)S(1)}, bf16[400,256]{1,0:T(8,128)(2,1)S(1)}, u32[]{:S(2)}, u32[]{:S(2)}) collective-permute-start(bf16[400,256]{1,0:T(8,128)(2,1)S(1)} %get-tuple-element.39), channel_id=1, source_target_pairs={{0,2},{1,3},{2,0},{3,1},{4,6},{5,7},{6,4},{7,5},{8,10},{9,11},{10,... | collective-permute-start | bytes 614408 | tf_op jit(solution)/shard_map/ppermute | solution.py:223
  16.8 15.1 %collective-permute-start.6 = (bf16[400,256]{1,0:T(8,128)(2,1)S(1)}, bf16[400,256]{1,0:T(8,128)(2,1)S(1)}, u32[]{:S(2)}, u32[]{:S(2)}) collective-permute-start(bf16[400,256]{1,0:T(8,128)(2,1)S(1)} %get-tuple-element.40), channel_id=1, source_target_pairs={{0,6},{1,7},{2,4},{3,5},{4,2},{5,3},{6,0},{7,1},{8,14},{9,15},{10,... | collective-permute-start | bytes 614408 | tf_op jit(solution)/shard_map/ppermute | solution.py:223
  18.3 24.7 %collective-permute-start.7 = (bf16[400,256]{1,0:T(8,128)(2,1)S(1)}, bf16[400,256]{1,0:T(8,128)(2,1)S(1)}, u32[]{:S(2)}, u32[]{:S(2)}) collective-permute-start(bf16[400,256]{1,0:T(8,128)(2,1)S(1)} %get-tuple-element.45), channel_id=1, source_target_pairs={{0,8},{1,9},{2,10},{3,11},{4,12},{5,13},{6,14},{7,15},{8,0},{9,1},... | collective-permute-start | bytes 614408 | tf_op jit(solution)/shard_map/ppermute | solution.py:223
  18.6 25.8 %collective-permute-start.8 = (bf16[400,256]{1,0:T(8,128)(2,1)S(1)}, bf16[400,256]{1,0:T(8,128)(2,1)S(1)}, u32[]{:S(2)}, u32[]{:S(2)}) collective-permute-start(bf16[400,256]{1,0:T(8,128)(2,1)S(1)} %get-tuple-element.46), channel_id=1, source_target_pairs={{0,10},{1,11},{2,8},{3,9},{4,14},{5,15},{6,12},{7,13},{8,2},{9,3},... | collective-permute-start | bytes 614408 | tf_op jit(solution)/shard_map/ppermute | solution.py:223
  22.2 22.3 %collective-permute-start.9 = (bf16[400,256]{1,0:T(8,128)(2,1)S(1)}, bf16[400,256]{1,0:T(8,128)(2,1)S(1)}, u32[]{:S(2)}, u32[]{:S(2)}) collective-permute-start(bf16[400,256]{1,0:T(8,128)(2,1)S(1)} %get-tuple-element.47), channel_id=1, source_target_pairs={{0,12},{1,13},{2,14},{3,15},{4,8},{5,9},{6,10},{7,11},{8,4},{9,5},... | collective-permute-start | bytes 614408 | tf_op jit(solution)/shard_map/ppermute | solution.py:223
  31.9 11.0 %copy-start.4 = (bf16[400,256]{1,0:T(8,128)(2,1)}, bf16[400,256]{1,0:T(8,128)(2,1)S(1)}, u32[]{:S(2)}) copy-start(bf16[400,256]{1,0:T(8,128)(2,1)S(1)} %collective-permute-done.5.refs_1_) | copy-start | bytes 614404
  31.9 11.0 %copy-start.6 = (bf16[400,256]{1,0:T(8,128)(2,1)}, bf16[400,256]{1,0:T(8,128)(2,1)S(1)}, u32[]{:S(2)}) copy-start(bf16[400,256]{1,0:T(8,128)(2,1)S(1)} %collective-permute-done.6.refs_2_.refs_3_) | copy-start | bytes 614404
  43.0 1.5 copy-start.8
  44.4 0.7 copy-start.10
  44.4 0.7 copy-start.12
  44.4 1.3 copy-start.24
  44.5 5.3 %copy-start.23 = (s32[16,16]{1,0:T(8,128)S(1)}, s32[16,16]{1,0:T(8,128)}, u32[]{:S(2)}) copy-start(s32[16,16]{1,0:T(8,128)} %param.15) | copy-start | bytes 3076
  45.2 7.8 %collective-permute-start.10 = (s16[1936,640]{1,0:T(8,128)(2,1)}, s16[1936,640]{1,0:T(8,128)(2,1)S(1)}, u32[]{:S(2)}, u32[]{:S(2)}) collective-permute-start(s16[1936,640]{1,0:T(8,128)(2,1)} %get-tuple-element.48.refs_0_), channel_id=1, source_target_pairs={{0,1},{1,0},{2,3},{3,2},{4,5},{5,4},{6,7},{7,6},{8,9},{9,8},{10,11... | collective-permute-start | bytes 7434248 | tf_op jit(solution)/shard_map/ppermute | solution.py:223
  45.2 14.4 %collective-permute-start.4 = (s16[1936,512]{1,0:T(8,128)(2,1)}, s16[1936,512]{1,0:T(8,128)(2,1)}, u32[]{:S(2)}, u32[]{:S(2)}) collective-permute-start(s16[1936,512]{1,0:T(8,128)(2,1)} %get-tuple-element.38), channel_id=1, source_target_pairs={{0,1},{1,0},{2,3},{3,2},{4,5},{5,4},{6,7},{7,6},{8,9},{9,8},{10,11... | collective-permute-start | bytes 5947400 | tf_op jit(solution)/shard_map/ppermute | solution.py:223
  45.8 13.7 %collective-permute-start.11 = (bf16[400,256]{1,0:T(8,128)(2,1)S(1)}, bf16[400,256]{1,0:T(8,128)(2,1)S(1)}, u32[]{:S(2)}, u32[]{:S(2)}) collective-permute-start(bf16[400,256]{1,0:T(8,128)(2,1)S(1)} %get-tuple-element.50), channel_id=1, source_target_pairs={{0,4},{1,5},{2,6},{3,7},{4,0},{5,1},{6,2},{7,3},{8,12},{9,13},{10,... | collective-permute-start | bytes 614408 | tf_op jit(solution)/shard_map/ppermute | solution.py:223
  48.2 11.4 %collective-permute-start.12 = (bf16[400,256]{1,0:T(8,128)(2,1)S(1)}, bf16[400,256]{1,0:T(8,128)(2,1)S(1)}, u32[]{:S(2)}, u32[]{:S(2)}) collective-permute-start(bf16[400,256]{1,0:T(8,128)(2,1)S(1)} %get-tuple-element.51), channel_id=1, source_target_pairs={{0,14},{1,15},{2,12},{3,13},{4,10},{5,11},{6,8},{7,9},{8,6},{9,7},... | collective-permute-start | bytes 614408 | tf_op jit(solution)/shard_map/ppermute | solution.py:223
  57.1 6.6 %copy-start = (f32[4,192,640]{2,1,0:T(8,128)}, f32[4,192,640]{2,1,0:T(8,128)S(1)}, u32[]{:S(2)}) copy-start(f32[4,192,640]{2,1,0:T(8,128)S(1)} %get-tuple-element.49.refs_0_.held.held_out) | copy-start | bytes 5898244
  57.1 30.2 %collective-permute-start.14 = (s16[976,640]{1,0:T(8,128)(2,1)S(1)}, s16[976,640]{1,0:T(8,128)(2,1)S(1)}, u32[]{:S(2)}, u32[]{:S(2)}) collective-permute-start(s16[976,640]{1,0:T(8,128)(2,1)S(1)} %get-tuple-element.54), channel_id=1, source_target_pairs={{0,4},{1,5},{2,6},{3,7},{4,0},{5,1},{6,2},{7,3},{8,12},{9,13},{10,... | collective-permute-start | bytes 3747848 | tf_op jit(solution)/shard_map/ppermute | solution.py:223
  59.5 4.2 %copy-start.19 = (bf16[400,256]{1,0:T(8,128)(2,1)}, bf16[400,256]{1,0:T(8,128)(2,1)S(1)}, u32[]{:S(2)}) copy-start(bf16[400,256]{1,0:T(8,128)(2,1)S(1)} %collective-permute-done.11.refs_1_.refs_2_) | copy-start | bytes 614404
  59.5 4.2 %copy-start.21 = (bf16[400,256]{1,0:T(8,128)(2,1)}, bf16[400,256]{1,0:T(8,128)(2,1)S(1)}, u32[]{:S(2)}) copy-start(bf16[400,256]{1,0:T(8,128)(2,1)S(1)} %collective-permute-done.12.refs_2_.refs_7_) | copy-start | bytes 614404
  63.8 26.7 %collective-permute-start.13 = (s16[976,512]{1,0:T(8,128)(2,1)S(1)}, s16[976,512]{1,0:T(8,128)(2,1)S(1)}, u32[]{:S(2)}, u32[]{:S(2)}) collective-permute-start(s16[976,512]{1,0:T(8,128)(2,1)S(1)} %get-tuple-element.53), channel_id=1, source_target_pairs={{0,2},{1,3},{2,0},{3,1},{4,6},{5,7},{6,4},{7,5},{8,10},{9,11},{10,... | collective-permute-start | bytes 2998280 | tf_op jit(solution)/shard_map/ppermute | solution.py:223
  92.1 13.4 %collective-permute-start.15 = (s16[496,512]{1,0:T(8,128)(2,1)}, s16[496,512]{1,0:T(8,128)(2,1)}, u32[]{:S(2)}, u32[]{:S(2)}) collective-permute-start(s16[496,512]{1,0:T(8,128)(2,1)} %get-tuple-element.57), channel_id=1, source_target_pairs={{0,4},{1,5},{2,6},{3,7},{4,0},{5,1},{6,2},{7,3},{8,12},{9,13},{10,... | collective-permute-start | bytes 1523720 | tf_op jit(solution)/shard_map/ppermute | solution.py:223
  95.2 15.5 %collective-permute-start.17 = (s16[496,640]{1,0:T(8,128)(2,1)}, s16[496,640]{1,0:T(8,128)(2,1)}, u32[]{:S(2)}, u32[]{:S(2)}) collective-permute-start(s16[496,640]{1,0:T(8,128)(2,1)} %get-tuple-element.60), channel_id=1, source_target_pairs={{0,2},{1,3},{2,0},{3,1},{4,6},{5,7},{6,4},{7,5},{8,10},{9,11},{10,... | collective-permute-start | bytes 1904648 | tf_op jit(solution)/shard_map/ppermute | solution.py:223
  96.7 0.9 copy-start.5
  97.7 0.9 copy-start.7
  98.6 0.9 copy-start.9
  99.5 0.9 copy-start.11
  100.5 0.9 copy-start.13
  101.4 0.9 copy-start.15
  102.3 0.9 copy-start.20
  103.3 0.9 copy-start.22
  107.7 0.7 copy-start.16
  108.5 21.4 %collective-permute-start.16 = (s16[256,512]{1,0:T(8,128)(2,1)}, s16[256,512]{1,0:T(8,128)(2,1)S(1)}, u32[]{:S(2)}, u32[]{:S(2)}) collective-permute-start(s16[256,512]{1,0:T(8,128)(2,1)} %get-tuple-element.59), channel_id=1, source_target_pairs={{0,8},{1,9},{2,10},{3,11},{4,12},{5,13},{6,14},{7,15},{8,0},{9,1},... | collective-permute-start | bytes 786440 | tf_op jit(solution)/shard_map/ppermute | solution.py:223
  110.3 27.3 %collective-permute-start.20 = (bf16[8,400,256]{2,1,0:T(8,128)(2,1)S(1)}, bf16[8,400,256]{2,1,0:T(8,128)(2,1)}, u32[]{:S(2)}, u32[]{:S(2)}) collective-permute-start(bf16[8,400,256]{2,1,0:T(8,128)(2,1)S(1)} %pack.3.refs_0_.own), channel_id=1, source_target_pairs={{0,1},{1,0},{2,3},{3,2},{4,5},{5,4},{6,7},{7,6},{8,9},{9,8},{10,11... | collective-permute-start | bytes 4915208 | tf_op jit(solution)/shard_map/ppermute | solution.py:223
  110.8 1.0 copy-start.17
  111.8 18.1 %copy-start.18 = (f32[1,192,512]{2,1,0:T(8,128)S(1)}, f32[1,192,512]{2,1,0:T(8,128)}, u32[]{:S(2)}) copy-start(f32[1,192,512]{2,1,0:T(8,128)} %copy-done.16) | copy-start | bytes 1179652
  113.3 22.9 %collective-permute-start.18 = (s16[256,640]{1,0:T(8,128)(2,1)S(1)}, s16[256,640]{1,0:T(8,128)(2,1)S(1)}, u32[]{:S(2)}, u32[]{:S(2)}) collective-permute-start(s16[256,640]{1,0:T(8,128)(2,1)S(1)} %get-tuple-element.63), channel_id=1, source_target_pairs={{0,8},{1,9},{2,10},{3,11},{4,12},{5,13},{6,14},{7,15},{8,0},{9,1},... | collective-permute-start | bytes 983048 | tf_op jit(solution)/shard_map/ppermute | solution.py:223
  136.2 1.2 collective-permute-start.19
  147.6 24.3 %copy-start.2 = (bf16[2,96,1024]{2,1,0:T(8,128)(2,1)S(1)}, bf16[2,96,1024]{2,1,0:T(8,128)(2,1)}, u32[]{:S(2)}) copy-start(bf16[2,96,1024]{2,1,0:T(8,128)(2,1)} %param.8) | copy-start | bytes 1179652
  147.7 16.7 %collective-permute-start.21 = (bf16[192,1024]{1,0:T(8,128)(2,1)S(1)}, bf16[192,1024]{1,0:T(8,128)(2,1)S(1)}, u32[]{:S(2)}, u32[]{:S(2)}) collective-permute-start(bf16[192,1024]{1,0:T(8,128)(2,1)S(1)} %bitcast.50), channel_id=1, source_target_pairs={{0,4},{1,5},{2,6},{3,7},{4,0},{5,1},{6,2},{7,3},{8,12},{9,13},{10,... | collective-permute-start | bytes 1179656 | tf_op jit(solution)/shard_map/ppermute | solution.py:223
  147.7 16.6 %collective-permute-start.22 = (bf16[192,1024]{1,0:T(8,128)(2,1)S(1)}, bf16[192,1024]{1,0:T(8,128)(2,1)S(1)}, u32[]{:S(2)}, u32[]{:S(2)}) collective-permute-start(bf16[192,1024]{1,0:T(8,128)(2,1)S(1)} %bitcast.51), channel_id=1, source_target_pairs={{0,2},{1,3},{2,0},{3,1},{4,6},{5,7},{6,4},{7,5},{8,10},{9,11},{10,... | collective-permute-start | bytes 1179656 | tf_op jit(solution)/shard_map/ppermute | solution.py:223
  149.3 20.3 %collective-permute-start.23 = (bf16[192,1024]{1,0:T(8,128)(2,1)S(1)}, bf16[192,1024]{1,0:T(8,128)(2,1)S(1)}, u32[]{:S(2)}, u32[]{:S(2)}) collective-permute-start(bf16[192,1024]{1,0:T(8,128)(2,1)S(1)} %bitcast.52), channel_id=1, source_target_pairs={{0,8},{1,9},{2,10},{3,11},{4,12},{5,13},{6,14},{7,15},{8,0},{9,1},... | collective-permute-start | bytes 1179656 | tf_op jit(solution)/shard_map/ppermute | solution.py:223
  150.6 19.0 %collective-permute-start.24 = (bf16[192,1024]{1,0:T(8,128)(2,1)S(1)}, bf16[192,1024]{1,0:T(8,128)(2,1)S(1)}, u32[]{:S(2)}, u32[]{:S(2)}) collective-permute-start(bf16[192,1024]{1,0:T(8,128)(2,1)S(1)} %bitcast.53), channel_id=1, source_target_pairs={{0,1},{1,0},{2,3},{3,2},{4,5},{5,4},{6,7},{7,6},{8,9},{9,8},{10,11... | collective-permute-start | bytes 1179656 | tf_op jit(solution)/shard_map/ppermute | solution.py:223
  169.7 5.6 %collective-permute-start.28 = (bf16[3,192,1024]{2,1,0:T(8,128)(2,1)S(1)}, bf16[3,192,1024]{2,1,0:T(8,128)(2,1)}, u32[]{:S(2)}, u32[]{:S(2)}) collective-permute-start(bf16[3,192,1024]{2,1,0:T(8,128)(2,1)S(1)} %get-tuple-element.66.refs_0_), channel_id=1, source_target_pairs={{0,1},{1,0},{2,3},{3,2},{4,5},{5,4},{6,7},{7,6},{8,9},{9,8},{10,11... | collective-permute-start | bytes 3538952 | tf_op jit(solution)/shard_map/ppermute | solution.py:223
  169.8 20.1 %collective-permute-start.27 = (bf16[2,192,1024]{2,1,0:T(8,128)(2,1)S(1)}, bf16[2,192,1024]{2,1,0:T(8,128)(2,1)}, u32[]{:S(2)}, u32[]{:S(2)}) collective-permute-start(bf16[2,192,1024]{2,1,0:T(8,128)(2,1)S(1)} %get-tuple-element.65.refs_1_), channel_id=1, source_target_pairs={{0,2},{1,3},{2,0},{3,1},{4,6},{5,7},{6,4},{7,5},{8,10},{9,11},{10,... | collective-permute-start | bytes 2359304 | tf_op jit(solution)/shard_map/ppermute | solution.py:223
  170.4 13.2 %collective-permute-start.25 = (bf16[192,1024]{1,0:T(8,128)(2,1)S(1)}, bf16[192,1024]{1,0:T(8,128)(2,1)}, u32[]{:S(2)}, u32[]{:S(2)}) collective-permute-start(bf16[192,1024]{1,0:T(8,128)(2,1)S(1)} %together.6.refs_0_), channel_id=1, source_target_pairs={{0,12},{1,13},{2,14},{3,15},{4,8},{5,9},{6,10},{7,11},{8,4},{9,5},... | collective-permute-start | bytes 1179656 | tf_op jit(solution)/shard_map/ppermute | solution.py:223
  191.2 3.0 %collective-permute-start.29 = (bf16[3,192,1024]{2,1,0:T(8,128)(2,1)S(1)}, bf16[3,192,1024]{2,1,0:T(8,128)(2,1)}, u32[]{:S(2)}, u32[]{:S(2)}) collective-permute-start(bf16[3,192,1024]{2,1,0:T(8,128)(2,1)S(1)} %pack.5.refs_0_), channel_id=1, source_target_pairs={{0,1},{1,0},{2,3},{3,2},{4,5},{5,4},{6,7},{7,6},{8,9},{9,8},{10,11... | collective-permute-start | bytes 3538952 | tf_op jit(solution)/shard_map/ppermute | solution.py:223
  191.3 11.7 %collective-permute-start.26 = (bf16[192,1024]{1,0:T(8,128)(2,1)}, bf16[192,1024]{1,0:T(8,128)(2,1)S(1)}, u32[]{:S(2)}, u32[]{:S(2)}) collective-permute-start(bf16[192,1024]{1,0:T(8,128)(2,1)} %collective-permute-done.25.refs_1_), channel_id=1, source_target_pairs={{0,2},{1,3},{2,0},{3,1},{4,6},{5,7},{6,4},{7,5},{8,10},{9,11},{10,... | collective-permute-start | bytes 1179656 | tf_op jit(solution)/shard_map/ppermute | solution.py:223
  203.0 1.7 collective-permute-start.30

commit v16 on v15

--- a/solution.py
+++ b/solution.py
@@ -795,7 +795,8 @@
     line_b = swap(sent_b, 2)
     held_a, sent_a = folded(held_a, 2, line_a, 1, held_b)
     line_a = swap(sent_a, 4)
-    (cache_own,) = pack(cache_pieces, [tuple(range(KVH))], [held_a])
+    far_pieces = [pltpu.with_memory_space_constraint(p, pltpu.HBM) for p in cache_pieces]
+    (cache_own,) = pack(far_pieces, [tuple(range(KVH))], [held_a])
     cache_other = swap(cache_own, 1)
     held_a, sent_a = folded(held_a, 3, line_a, 1, cache_own)
     line_a = swap(sent_a, 8)

time: 210 us -> 210 us (level)
  local copies, waits for them, and re-layouts: 14.3 us -> 6.88 us
  waiting for transfers between devices: 84 us -> 90 us
    unnamed x52 -> x36, local copies, waits for them, and re-layouts: 11.5 us -> 4.02 us
    ppermute x31, waiting for transfers between devices: 84 us -> 90 us  [swap(): return lax.ppermute(value, 'tensor', [(i, i ^ bit) for i in range(devices)])]
where the time goes in v16:
time: 210 us; the launch traced here: 209 us
  waiting for transfers between devices  90 us (43%)
  Pallas kernels  70.7 us (34%)
  starting transfers between devices  35.5 us (17%)
  local copies, waits for them, and re-layouts  6.88 us (3%)
  other arithmetic  5.3 us (3%)
    ppermute x31, waiting for transfers between devices, swap(): return lax.ppermute(value, 'tensor', [(i, i ^ bit) for i in range(devices)])  90 us
    ppermute x31, starting transfers between devices, swap(): return lax.ppermute(value, 'tensor', [(i, i ^ bit) for i in range(devices)])  35.5 us
    pallas_call x4, Pallas kernels, mix(): pl.pallas_call(functools.partial(mix_kernel, len(pieces)), in_specs=[pl.B...  21.5 us
    pallas_call x2, Pallas kernels, project(): pl.pallas_call(functools.partial(project_kernel, part), grid_spec=pltpu.P...  20.3 us
    pallas_call x6, Pallas kernels, fold(): pl.pallas_call(functools.partial(fold_kernel, steps, low), grid_spec=pltp...  16.9 us
    pallas_call x1, Pallas kernels, attend(): pl.pallas_call(attend_kernel, in_specs=[pl.BlockSpec(memory_space=pltpu.S...  8.39 us
  transfers between devices with their start and end apart: 31, of which 18 were waited for; matrix products, arithmetic and copies ran while one was open for 3% of the time, Pallas kernels for 26%

profile of v16, /device:TPU:0, one launch (start us, length us, event | category | flops | bytes accessed | tf_op | source)
XLA Modules:
  0.0 209.0 jit_solution(618928015274085380)
XLA Ops:
  0.0 1.2 fusion
  1.2 3.0 %collective-permute-start = (f32[2,96]{1,0:T(2,128)S(1)}, f32[2,96]{1,0:T(2,128)S(1)}, u32[]{:S(2)}, u32[]{:S(2)}) collective-permute-start(f32[2,96]{1,0:T(2,128)S(1)} %fusion), channel_id=1, source_target_pairs={{0,2},{1,3},{2,0},{3,1},{4,6},{5,7},{6,4},{7,5},{8,10},{9,11},{10,... | collective-permute-start | bytes 2312 | tf_op jit(solution)/shard_map/ppermute | solution.py:223
  4.3 1.5 collective-permute-done
  5.8 1.1 collective-permute-done.1
  7.0 2.1 collective-permute-start.2
  9.0 0.8 reshape.240
  9.8 0.7 convert_element_type.29
  10.6 3.0 %collective-permute-start.3 = (f32[2,96]{1,0:T(2,128)S(1)}, f32[2,96]{1,0:T(2,128)S(1)}, u32[]{:S(2)}, u32[]{:S(2)}) collective-permute-start(f32[2,96]{1,0:T(2,128)S(1)} %add.139), channel_id=1, source_target_pairs={{0,8},{1,9},{2,10},{3,11},{4,12},{5,13},{6,14},{7,15},{8,0},{9,1},... | collective-permute-start | bytes 2312 | tf_op jit(solution)/shard_map/ppermute | solution.py:223
  13.6 1.4 copy-done.3
  15.2 1.6 collective-permute-start.5
  16.8 1.5 collective-permute-start.6
  18.3 0.3 collective-permute-start.7
  18.6 3.5 %collective-permute-start.8 = (bf16[400,256]{1,0:T(8,128)(2,1)S(1)}, bf16[400,256]{1,0:T(8,128)(2,1)S(1)}, u32[]{:S(2)}, u32[]{:S(2)}) collective-permute-start(bf16[400,256]{1,0:T(8,128)(2,1)S(1)} %get-tuple-element.46), channel_id=1, source_target_pairs={{0,10},{1,11},{2,8},{3,9},{4,14},{5,15},{6,12},{7,13},{8,2},{9,3},... | collective-permute-start | bytes 614408 | tf_op jit(solution)/shard_map/ppermute | solution.py:223
  22.6 9.3 %project.2 = (f32[8,192,512]{2,1,0:T(8,128)}, s16[1936,512]{1,0:T(8,128)(2,1)}) custom-call(s32[1]{0:T(128)} %bitcast.2.core, bf16[192,1024]{1,0:T(8,128)(2,1)S(1)} %bitcast.47, bf16[1024,18432]{1,0:T(8,128)(2,1)} %weights.3, bf16[400,256]{1,0:T(8,128)(2,1)S(1)} %get-tuple-element.36.refs_0_), custom_call_target="tpu_custom_call" | custom-call | flops 1 | bytes 1 | tf_op jit(solution)/shard_map/project/pallas_call | solution.py:352
  31.9 11.0 %project.3 = (f32[8,192,640]{2,1,0:T(8,128)}, s16[1936,640]{1,0:T(8,128)(2,1)}) custom-call(s32[1]{0:T(128)} %bitcast.2.core, bf16[192,1024]{1,0:T(8,128)(2,1)S(1)} %bitcast.48, bf16[1024,18432]{1,0:T(8,128)(2,1)} %weights.3, f32[8,192,512]{2,1,0:T(8,128)} %get-tuple-element.37.refs_0_.held.held_out, bf16[400,256]{1,0:T(8,128)(2,1)S(1)} %collective-permute-done.5.refs_1_, ...), custom_call_target="tpu_custom_call" | custom-call | flops 1 | bytes 1 | tf_op jit(solution)/shard_map/project/pallas_call | solution.py:352
  43.0 1.5 collective-permute-done.8.refs_4_.refs_5_
  44.5 0.6 copy-done.7
  45.2 0.5 collective-permute-start.4
  45.8 2.4 %collective-permute-start.11 = (bf16[400,256]{1,0:T(8,128)(2,1)S(1)}, bf16[400,256]{1,0:T(8,128)(2,1)S(1)}, u32[]{:S(2)}, u32[]{:S(2)}) collective-permute-start(bf16[400,256]{1,0:T(8,128)(2,1)S(1)} %get-tuple-element.50), channel_id=1, source_target_pairs={{0,4},{1,5},{2,6},{3,7},{4,0},{5,1},{6,2},{7,3},{8,12},{9,13},{10,... | collective-permute-start | bytes 614408 | tf_op jit(solution)/shard_map/ppermute | solution.py:223
  48.2 1.6 collective-permute-start.12
  49.9 3.0 %collective-permute-done.10.landed.landed_out.landed_powers = s16[1936,640]{1,0:T(8,128)(2,1)S(1)} collective-permute-done((s16[1936,640]{1,0:T(8,128)(2,1)}, s16[1936,640]{1,0:T(8,128)(2,1)S(1)}, u32[]{:S(2)}, u32[]{:S(2)}) %collective-permute-start.10) | collective-permute-done | bytes 2478112 | tf_op jit(solution)/shard_map/ppermute | solution.py:223
  52.9 4.2 %fold.6 = (f32[4,192,640]{2,1,0:T(8,128)S(1)}, s16[976,640]{1,0:T(8,128)(2,1)S(1)}) custom-call(s32[1]{0:T(128)} %bitcast.4.bit, f32[8,192,640]{2,1,0:T(8,128)} %get-tuple-element.41.held.held_out, f32[8,192,640]{2,1,0:T(8,128)} %get-tuple-element.41.held.held_out, s16[1936,640]{1,0:T(8,128)(2,1)S(1)} %collective-permute-done.10.landed.landed_out.landed_powers, ...), custom_call_target="tpu_custom_call" | custom-call | flops 1 | bytes 1 | tf_op jit(solution)/shard_map/fold/pallas_call | solution.py:406
  57.1 2.4 %collective-permute-start.14 = (s16[976,640]{1,0:T(8,128)(2,1)S(1)}, s16[976,640]{1,0:T(8,128)(2,1)S(1)}, u32[]{:S(2)}, u32[]{:S(2)}) collective-permute-start(s16[976,640]{1,0:T(8,128)(2,1)S(1)} %get-tuple-element.54), channel_id=1, source_target_pairs={{0,4},{1,5},{2,6},{3,7},{4,0},{5,1},{6,2},{7,3},{8,12},{9,13},{10,... | collective-permute-start | bytes 3747848 | tf_op jit(solution)/shard_map/ppermute | solution.py:223
  59.6 4.2 %fold.7 = (f32[4,192,512]{2,1,0:T(8,128)S(1)}, s16[976,512]{1,0:T(8,128)(2,1)S(1)}) custom-call(s32[1]{0:T(128)} %bitcast.5.bit, f32[8,192,512]{2,1,0:T(8,128)} %get-tuple-element.37.refs_0_.held.held_out, f32[8,192,512]{2,1,0:T(8,128)} %get-tuple-element.37.refs_0_.held.held_out, s16[1936,512]{1,0:T(8,128)(2,1)} %collective-permute-done.4.landed.landed_out.landed_powers, ...), custom_call_target="tpu_custom_call" | custom-call | flops 20000000000 | bytes 1 | tf_op jit(solution)/shard_map/fold/pallas_call | solution.py:406
  63.8 1.6 collective-permute-start.13
  65.7 21.6 %collective-permute-done.14.landed.landed_out.landed_powers = s16[976,640]{1,0:T(8,128)(2,1)S(1)} collective-permute-done((s16[976,640]{1,0:T(8,128)(2,1)S(1)}, s16[976,640]{1,0:T(8,128)(2,1)S(1)}, u32[]{:S(2)}, u32[]{:S(2)}) %collective-permute-start.14) | collective-permute-done | bytes 1249312 | tf_op jit(solution)/shard_map/ppermute | solution.py:223
  87.3 3.1 %fold.8 = (f32[2,192,640]{2,1,0:T(8,128)S(1)}, s16[496,640]{1,0:T(8,128)(2,1)}) custom-call(s32[1]{0:T(128)} %bitcast.5.bit, f32[4,192,640]{2,1,0:T(8,128)} %copy-done, f32[4,192,640]{2,1,0:T(8,128)} %copy-done, s16[976,640]{1,0:T(8,128)(2,1)S(1)} %collective-permute-done.14.landed.landed_out.landed_powers, ...), custom_call_target="tpu_custom_call" | custom-call | flops 1 | bytes 1 | tf_op jit(solution)/shard_map/fold/pallas_call | solution.py:406
  90.4 1.7 fold.9
  92.1 1.7 collective-permute-start.15
  94.1 1.2 fusion.5
  95.2 1.5 collective-permute-start.17
  96.7 1.6 pack.3.refs_0_.own
  98.3 7.2 %collective-permute-done.15.landed.landed_out.landed_powers = s16[496,512]{1,0:T(8,128)(2,1)} collective-permute-done((s16[496,512]{1,0:T(8,128)(2,1)}, s16[496,512]{1,0:T(8,128)(2,1)}, u32[]{:S(2)}, u32[]{:S(2)}) %collective-permute-start.15) | collective-permute-done | bytes 507936 | tf_op jit(solution)/shard_map/ppermute | solution.py:223
  105.5 2.2 %fold.10 = (f32[1,192,512]{2,1,0:T(8,128)S(1)}, s16[256,512]{1,0:T(8,128)(2,1)}) custom-call(s32[1]{0:T(128)} %bitcast.3.bit, f32[2,192,512]{2,1,0:T(8,128)S(1)} %get-tuple-element.56.refs_8_.held.held_out, f32[2,192,512]{2,1,0:T(8,128)S(1)} %get-tuple-element.56.refs_8_.held.held_out, ...), custom_call_target="tpu_custom_call" | custom-call | flops 1 | bytes 1 | tf_op jit(solution)/shard_map/fold/pallas_call | solution.py:406
  107.7 0.7 copy-done.10
  108.5 0.6 collective-permute-start.16
  109.1 1.2 pad_maximum_fusion
  110.5 0.3 collective-permute-done.17.landed.landed_out.landed_powers
  110.8 1.0 copy-done.11
  111.8 1.6 fold.11
  113.3 2.1 %collective-permute-start.18 = (s16[256,640]{1,0:T(8,128)(2,1)S(1)}, s16[256,640]{1,0:T(8,128)(2,1)S(1)}, u32[]{:S(2)}, u32[]{:S(2)}) collective-permute-start(s16[256,640]{1,0:T(8,128)(2,1)S(1)} %get-tuple-element.63), channel_id=1, source_target_pairs={{0,8},{1,9},{2,10},{3,11},{4,12},{5,13},{6,14},{7,15},{8,0},{9,1},... | collective-permute-start | bytes 983048 | tf_op jit(solution)/shard_map/ppermute | solution.py:223
  115.5 14.4 %collective-permute-done.16.landed = s16[256,512]{1,0:T(8,128)(2,1)S(1)} collective-permute-done((s16[256,512]{1,0:T(8,128)(2,1)}, s16[256,512]{1,0:T(8,128)(2,1)S(1)}, u32[]{:S(2)}, u32[]{:S(2)}) %collective-permute-start.16) | collective-permute-done | bytes 262176 | tf_op jit(solution)/shard_map/ppermute | solution.py:223
  130.1 6.1 %collective-permute-done.18.landed.refs_1_ = s16[256,640]{1,0:T(8,128)(2,1)S(1)} collective-permute-done((s16[256,640]{1,0:T(8,128)(2,1)S(1)}, s16[256,640]{1,0:T(8,128)(2,1)S(1)}, u32[]{:S(2)}, u32[]{:S(2)}) %collective-permute-start.18) | collective-permute-done | bytes 327712 | tf_op jit(solution)/shard_map/ppermute | solution.py:223
  136.2 0.3 finish.3
  136.6 0.8 collective-permute-done.19
  137.6 0.7 slice_reduce_fusion
  139.1 8.4 %attend.1 = bf16[16,96,128]{2,1,0:T(8,128)(2,1)S(1)} custom-call(s32[24]{0:T(128)S(1)} %get-tuple-element.69.slot_request, bf16[16,96,128]{2,1,0:T(8,128)(2,1)S(1)} %bitcast.55, bf16[16,16,128]{2,1,0:T(8,128)(2,1)S(1)} %pad.12.new_keys, bf16[16,16,128]{2,1,0:T(8,128)(2,1)S(1)} %pad.13.new_values, bf16[8,400,256]{2,1,0:T(8,128)(2,1)S(1)} %pack.3.refs_0_.own, ...), custom_call_target="tpu_custom_call" | custom-call | flops 1 | bytes 1 | tf_op jit(solution)/shard_map/attend/pallas_call | solution.py:661
  147.7 1.6 collective-permute-start.22
  149.3 1.3 collective-permute-start.23
  150.6 13.8 %collective-permute-done.21.refs_0_ = bf16[192,1024]{1,0:T(8,128)(2,1)S(1)} collective-permute-done((bf16[192,1024]{1,0:T(8,128)(2,1)S(1)}, bf16[192,1024]{1,0:T(8,128)(2,1)S(1)}, u32[]{:S(2)}, u32[]{:S(2)}) %collective-permute-start.21) | collective-permute-done | bytes 393248 | tf_op jit(solution)/shard_map/ppermute | solution.py:223
  164.4 5.2 %collective-permute-done.23.refs_2_ = bf16[192,1024]{1,0:T(8,128)(2,1)S(1)} collective-permute-done((bf16[192,1024]{1,0:T(8,128)(2,1)S(1)}, bf16[192,1024]{1,0:T(8,128)(2,1)S(1)}, u32[]{:S(2)}, u32[]{:S(2)}) %collective-permute-start.23) | collective-permute-done | bytes 393248 | tf_op jit(solution)/shard_map/ppermute | solution.py:223
  169.8 0.6 collective-permute-start.27
  170.4 1.4 collective-permute-start.25
  171.9 3.4 %mix.4.refs_3_ = f32[192,1024]{1,0:T(8,128)S(1)} custom-call(s32[2]{0:T(128)S(1)} %pad_add_fusion.1.places, bf16[192,1024]{1,0:T(8,128)(2,1)S(1)} %together.6.refs_0_, bf16[192,1024]{1,0:T(8,128)(2,1)S(1)} %collective-permute-done.24.refs_3_.refs_1_, bf16[16384,1024]{1,0:T(8,128)(2,1)} %refs_2_.7, bf16[192,1024]{1,0:T(8,128)(2,1)S(1)} %bitcast.49), custom_call_target="tpu_custom_call" | custom-call | flops 1 | bytes 1 | tf_op jit(solution)/shard_map/mix/pallas_call | solution.py:509
  175.3 7.0 %mix.5.refs_2_.refs_3_ = f32[192,1024]{1,0:T(8,128)S(1)} custom-call(s32[6]{0:T(128)S(1)} %stack.82.places, bf16[3,192,1024]{2,1,0:T(8,128)(2,1)S(1)} %get-tuple-element.66.refs_0_, bf16[3,192,1024]{2,1,0:T(8,128)(2,1)} %collective-permute-done.28.refs_1_, bf16[16384,1024]{1,0:T(8,128)(2,1)} %refs_2_.7, f32[192,1024]{1,0:T(8,128)S(1)} %mix.4.refs_3_), custom_call_target="tpu_custom_call" | custom-call | flops 1 | bytes 1 | tf_op jit(solution)/shard_map/mix/pallas_call | solution.py:509
  182.3 1.3 collective-permute-done.25.refs_1_
  183.6 6.3 %collective-permute-done.27.refs_0_ = bf16[2,192,1024]{2,1,0:T(8,128)(2,1)} collective-permute-done((bf16[2,192,1024]{2,1,0:T(8,128)(2,1)S(1)}, bf16[2,192,1024]{2,1,0:T(8,128)(2,1)}, u32[]{:S(2)}, u32[]{:S(2)}) %collective-permute-start.27) | collective-permute-done | bytes 786464 | tf_op jit(solution)/shard_map/ppermute | solution.py:223
  189.9 1.3 pack.5.refs_0_
  191.3 0.6 collective-permute-start.26
  191.9 2.3 %collective-permute-done.29.refs_1_ = bf16[3,192,1024]{2,1,0:T(8,128)(2,1)} collective-permute-done((bf16[3,192,1024]{2,1,0:T(8,128)(2,1)S(1)}, bf16[3,192,1024]{2,1,0:T(8,128)(2,1)}, u32[]{:S(2)}, u32[]{:S(2)}) %collective-permute-start.29) | collective-permute-done | bytes 1179680 | tf_op jit(solution)/shard_map/ppermute | solution.py:223
  194.2 7.0 %mix.6.refs_1_.refs_3_ = f32[192,1024]{1,0:T(8,128)S(1)} custom-call(s32[6]{0:T(128)S(1)} %stack.75.places, bf16[3,192,1024]{2,1,0:T(8,128)(2,1)S(1)} %pack.5.refs_0_, bf16[3,192,1024]{2,1,0:T(8,128)(2,1)} %collective-permute-done.29.refs_1_, bf16[16384,1024]{1,0:T(8,128)(2,1)} %refs_2_.7, f32[192,1024]{1,0:T(8,128)S(1)} %mix.5.refs_2_.refs_3_), custom_call_target="tpu_custom_call" | custom-call | flops 1 | bytes 1 | tf_op jit(solution)/shard_map/mix/pallas_call | solution.py:509
  201.2 1.8 collective-permute-done.26.refs_0_
  203.1 1.6 collective-permute-done.30.refs_1_
  204.7 4.1 %mix.7 = bf16[192,1024]{1,0:T(8,128)(2,1)} custom-call(s32[2]{0:T(128)S(1)} %pad_add_fusion.places, bf16[192,1024]{1,0:T(8,128)(2,1)S(1)} %together.7.refs_0_, bf16[192,1024]{1,0:T(8,128)(2,1)S(1)} %collective-permute-done.30.refs_1_, bf16[16384,1024]{1,0:T(8,128)(2,1)} %refs_2_.7, f32[192,1024]{1,0:T(8,128)S(1)} %mix.6.refs_1_.refs_3_), custom_call_target="tpu_custom_call" | custom-call | flops 1 | bytes 1 | tf_op jit(solution)/shard_map/mix/pallas_call | solution.py:509
  (112 shorter events, 3.8 us)
Async XLA Ops:
  0.0 22.4 %copy-start.1 = (bf16[2,96,1024]{2,1,0:T(8,128)(2,1)S(1)}, bf16[2,96,1024]{2,1,0:T(8,128)(2,1)}, u32[]{:S(2)}) copy-start(bf16[2,96,1024]{2,1,0:T(8,128)(2,1)} %param.8) | copy-start | bytes 1179652
  1.2 4.6 %collective-permute-start = (f32[2,96]{1,0:T(2,128)S(1)}, f32[2,96]{1,0:T(2,128)S(1)}, u32[]{:S(2)}, u32[]{:S(2)}) collective-permute-start(f32[2,96]{1,0:T(2,128)S(1)} %fusion), channel_id=1, source_target_pairs={{0,2},{1,3},{2,0},{3,1},{4,6},{5,7},{6,4},{7,5},{8,10},{9,11},{10,... | collective-permute-start | bytes 2312 | tf_op jit(solution)/shard_map/ppermute | solution.py:223
  5.8 1.1 collective-permute-start.1
  7.0 3.6 %collective-permute-start.2 = (f32[2,96]{1,0:T(2,128)S(1)}, f32[2,96]{1,0:T(2,128)S(1)}, u32[]{:S(2)}, u32[]{:S(2)}) collective-permute-start(f32[2,96]{1,0:T(2,128)S(1)} %add.138), channel_id=1, source_target_pairs={{0,4},{1,5},{2,6},{3,7},{4,0},{5,1},{6,2},{7,3},{8,12},{9,13},{10,... | collective-permute-start | bytes 2312 | tf_op jit(solution)/shard_map/ppermute | solution.py:223
  10.6 11.6 %collective-permute-start.3 = (f32[2,96]{1,0:T(2,128)S(1)}, f32[2,96]{1,0:T(2,128)S(1)}, u32[]{:S(2)}, u32[]{:S(2)}) collective-permute-start(f32[2,96]{1,0:T(2,128)S(1)} %add.139), channel_id=1, source_target_pairs={{0,8},{1,9},{2,10},{3,11},{4,12},{5,13},{6,14},{7,15},{8,0},{9,1},... | collective-permute-start | bytes 2312 | tf_op jit(solution)/shard_map/ppermute | solution.py:223
  13.6 1.4 copy-start.3
  15.2 16.7 %copy-start.9 = (bf16[400,256]{1,0:T(8,128)(2,1)}, bf16[400,256]{1,0:T(8,128)(2,1)S(1)}, u32[]{:S(2)}) copy-start(bf16[400,256]{1,0:T(8,128)(2,1)S(1)} %get-tuple-element.36.refs_0_) | copy-start | bytes 614404
  15.2 16.7 %collective-permute-start.5 = (bf16[400,256]{1,0:T(8,128)(2,1)S(1)}, bf16[400,256]{1,0:T(8,128)(2,1)S(1)}, u32[]{:S(2)}, u32[]{:S(2)}) collective-permute-start(bf16[400,256]{1,0:T(8,128)(2,1)S(1)} %get-tuple-element.39), channel_id=1, source_target_pairs={{0,2},{1,3},{2,0},{3,1},{4,6},{5,7},{6,4},{7,5},{8,10},{9,11},{10,... | collective-permute-start | bytes 614408 | tf_op jit(solution)/shard_map/ppermute | solution.py:223
  16.8 15.2 %collective-permute-start.6 = (bf16[400,256]{1,0:T(8,128)(2,1)S(1)}, bf16[400,256]{1,0:T(8,128)(2,1)S(1)}, u32[]{:S(2)}, u32[]{:S(2)}) collective-permute-start(bf16[400,256]{1,0:T(8,128)(2,1)S(1)} %get-tuple-element.40), channel_id=1, source_target_pairs={{0,6},{1,7},{2,4},{3,5},{4,2},{5,3},{6,0},{7,1},{8,14},{9,15},{10,... | collective-permute-start | bytes 614408 | tf_op jit(solution)/shard_map/ppermute | solution.py:223
  18.3 24.7 %collective-permute-start.7 = (bf16[400,256]{1,0:T(8,128)(2,1)S(1)}, bf16[400,256]{1,0:T(8,128)(2,1)S(1)}, u32[]{:S(2)}, u32[]{:S(2)}) collective-permute-start(bf16[400,256]{1,0:T(8,128)(2,1)S(1)} %get-tuple-element.45), channel_id=1, source_target_pairs={{0,8},{1,9},{2,10},{3,11},{4,12},{5,13},{6,14},{7,15},{8,0},{9,1},... | collective-permute-start | bytes 614408 | tf_op jit(solution)/shard_map/ppermute | solution.py:223
  18.6 25.8 %collective-permute-start.8 = (bf16[400,256]{1,0:T(8,128)(2,1)S(1)}, bf16[400,256]{1,0:T(8,128)(2,1)S(1)}, u32[]{:S(2)}, u32[]{:S(2)}) collective-permute-start(bf16[400,256]{1,0:T(8,128)(2,1)S(1)} %get-tuple-element.46), channel_id=1, source_target_pairs={{0,10},{1,11},{2,8},{3,9},{4,14},{5,15},{6,12},{7,13},{8,2},{9,3},... | collective-permute-start | bytes 614408 | tf_op jit(solution)/shard_map/ppermute | solution.py:223
  22.2 22.3 %collective-permute-start.9 = (bf16[400,256]{1,0:T(8,128)(2,1)S(1)}, bf16[400,256]{1,0:T(8,128)(2,1)S(1)}, u32[]{:S(2)}, u32[]{:S(2)}) collective-permute-start(bf16[400,256]{1,0:T(8,128)(2,1)S(1)} %get-tuple-element.47), channel_id=1, source_target_pairs={{0,12},{1,13},{2,14},{3,15},{4,8},{5,9},{6,10},{7,11},{8,4},{9,5},... | collective-permute-start | bytes 614408 | tf_op jit(solution)/shard_map/ppermute | solution.py:223
  31.9 11.0 %copy-start.4 = (bf16[400,256]{1,0:T(8,128)(2,1)}, bf16[400,256]{1,0:T(8,128)(2,1)S(1)}, u32[]{:S(2)}) copy-start(bf16[400,256]{1,0:T(8,128)(2,1)S(1)} %collective-permute-done.5.refs_1_) | copy-start | bytes 614404
  31.9 11.0 %copy-start.5 = (bf16[400,256]{1,0:T(8,128)(2,1)}, bf16[400,256]{1,0:T(8,128)(2,1)S(1)}, u32[]{:S(2)}) copy-start(bf16[400,256]{1,0:T(8,128)(2,1)S(1)} %collective-permute-done.6.refs_2_.refs_3_) | copy-start | bytes 614404
  43.0 1.5 copy-start.6
  44.4 0.7 copy-start.7
  44.4 0.7 copy-start.8
  44.4 1.3 copy-start.16
  44.5 5.3 %copy-start.15 = (s32[16,16]{1,0:T(8,128)S(1)}, s32[16,16]{1,0:T(8,128)}, u32[]{:S(2)}) copy-start(s32[16,16]{1,0:T(8,128)} %param.15) | copy-start | bytes 3076
  45.2 7.8 %collective-permute-start.10 = (s16[1936,640]{1,0:T(8,128)(2,1)}, s16[1936,640]{1,0:T(8,128)(2,1)S(1)}, u32[]{:S(2)}, u32[]{:S(2)}) collective-permute-start(s16[1936,640]{1,0:T(8,128)(2,1)} %get-tuple-element.48.refs_0_), channel_id=1, source_target_pairs={{0,1},{1,0},{2,3},{3,2},{4,5},{5,4},{6,7},{7,6},{8,9},{9,8},{10,11... | collective-permute-start | bytes 7434248 | tf_op jit(solution)/shard_map/ppermute | solution.py:223
  45.2 14.4 %collective-permute-start.4 = (s16[1936,512]{1,0:T(8,128)(2,1)}, s16[1936,512]{1,0:T(8,128)(2,1)}, u32[]{:S(2)}, u32[]{:S(2)}) collective-permute-start(s16[1936,512]{1,0:T(8,128)(2,1)} %get-tuple-element.38), channel_id=1, source_target_pairs={{0,1},{1,0},{2,3},{3,2},{4,5},{5,4},{6,7},{7,6},{8,9},{9,8},{10,11... | collective-permute-start | bytes 5947400 | tf_op jit(solution)/shard_map/ppermute | solution.py:223
  45.8 13.7 %collective-permute-start.11 = (bf16[400,256]{1,0:T(8,128)(2,1)S(1)}, bf16[400,256]{1,0:T(8,128)(2,1)S(1)}, u32[]{:S(2)}, u32[]{:S(2)}) collective-permute-start(bf16[400,256]{1,0:T(8,128)(2,1)S(1)} %get-tuple-element.50), channel_id=1, source_target_pairs={{0,4},{1,5},{2,6},{3,7},{4,0},{5,1},{6,2},{7,3},{8,12},{9,13},{10,... | collective-permute-start | bytes 614408 | tf_op jit(solution)/shard_map/ppermute | solution.py:223
  48.2 11.4 %collective-permute-start.12 = (bf16[400,256]{1,0:T(8,128)(2,1)S(1)}, bf16[400,256]{1,0:T(8,128)(2,1)S(1)}, u32[]{:S(2)}, u32[]{:S(2)}) collective-permute-start(bf16[400,256]{1,0:T(8,128)(2,1)S(1)} %get-tuple-element.51), channel_id=1, source_target_pairs={{0,14},{1,15},{2,12},{3,13},{4,10},{5,11},{6,8},{7,9},{8,6},{9,7},... | collective-permute-start | bytes 614408 | tf_op jit(solution)/shard_map/ppermute | solution.py:223
  57.1 6.6 %copy-start = (f32[4,192,640]{2,1,0:T(8,128)}, f32[4,192,640]{2,1,0:T(8,128)S(1)}, u32[]{:S(2)}) copy-start(f32[4,192,640]{2,1,0:T(8,128)S(1)} %get-tuple-element.49.refs_0_.held.held_out) | copy-start | bytes 5898244
  57.1 30.2 %collective-permute-start.14 = (s16[976,640]{1,0:T(8,128)(2,1)S(1)}, s16[976,640]{1,0:T(8,128)(2,1)S(1)}, u32[]{:S(2)}, u32[]{:S(2)}) collective-permute-start(s16[976,640]{1,0:T(8,128)(2,1)S(1)} %get-tuple-element.54), channel_id=1, source_target_pairs={{0,4},{1,5},{2,6},{3,7},{4,0},{5,1},{6,2},{7,3},{8,12},{9,13},{10,... | collective-permute-start | bytes 3747848 | tf_op jit(solution)/shard_map/ppermute | solution.py:223
  59.5 4.2 %copy-start.13 = (bf16[400,256]{1,0:T(8,128)(2,1)}, bf16[400,256]{1,0:T(8,128)(2,1)S(1)}, u32[]{:S(2)}) copy-start(bf16[400,256]{1,0:T(8,128)(2,1)S(1)} %collective-permute-done.11.refs_1_.refs_2_) | copy-start | bytes 614404
  59.5 4.2 %copy-start.14 = (bf16[400,256]{1,0:T(8,128)(2,1)}, bf16[400,256]{1,0:T(8,128)(2,1)S(1)}, u32[]{:S(2)}) copy-start(bf16[400,256]{1,0:T(8,128)(2,1)S(1)} %collective-permute-done.12.refs_2_.refs_7_) | copy-start | bytes 614404
  63.8 26.7 %collective-permute-start.13 = (s16[976,512]{1,0:T(8,128)(2,1)S(1)}, s16[976,512]{1,0:T(8,128)(2,1)S(1)}, u32[]{:S(2)}, u32[]{:S(2)}) collective-permute-start(s16[976,512]{1,0:T(8,128)(2,1)S(1)} %get-tuple-element.53), channel_id=1, source_target_pairs={{0,2},{1,3},{2,0},{3,1},{4,6},{5,7},{6,4},{7,5},{8,10},{9,11},{10,... | collective-permute-start | bytes 2998280 | tf_op jit(solution)/shard_map/ppermute | solution.py:223
  92.1 13.4 %collective-permute-start.15 = (s16[496,512]{1,0:T(8,128)(2,1)}, s16[496,512]{1,0:T(8,128)(2,1)}, u32[]{:S(2)}, u32[]{:S(2)}) collective-permute-start(s16[496,512]{1,0:T(8,128)(2,1)} %get-tuple-element.57), channel_id=1, source_target_pairs={{0,4},{1,5},{2,6},{3,7},{4,0},{5,1},{6,2},{7,3},{8,12},{9,13},{10,... | collective-permute-start | bytes 1523720 | tf_op jit(solution)/shard_map/ppermute | solution.py:223
  95.2 15.5 %collective-permute-start.17 = (s16[496,640]{1,0:T(8,128)(2,1)}, s16[496,640]{1,0:T(8,128)(2,1)}, u32[]{:S(2)}, u32[]{:S(2)}) collective-permute-start(s16[496,640]{1,0:T(8,128)(2,1)} %get-tuple-element.60), channel_id=1, source_target_pairs={{0,2},{1,3},{2,0},{3,1},{4,6},{5,7},{6,4},{7,5},{8,10},{9,11},{10,... | collective-permute-start | bytes 1904648 | tf_op jit(solution)/shard_map/ppermute | solution.py:223
  107.7 0.7 copy-start.10
  108.5 21.4 %collective-permute-start.16 = (s16[256,512]{1,0:T(8,128)(2,1)}, s16[256,512]{1,0:T(8,128)(2,1)S(1)}, u32[]{:S(2)}, u32[]{:S(2)}) collective-permute-start(s16[256,512]{1,0:T(8,128)(2,1)} %get-tuple-element.59), channel_id=1, source_target_pairs={{0,8},{1,9},{2,10},{3,11},{4,12},{5,13},{6,14},{7,15},{8,0},{9,1},... | collective-permute-start | bytes 786440 | tf_op jit(solution)/shard_map/ppermute | solution.py:223
  110.3 27.3 %collective-permute-start.20 = (bf16[8,400,256]{2,1,0:T(8,128)(2,1)S(1)}, bf16[8,400,256]{2,1,0:T(8,128)(2,1)}, u32[]{:S(2)}, u32[]{:S(2)}) collective-permute-start(bf16[8,400,256]{2,1,0:T(8,128)(2,1)S(1)} %pack.3.refs_0_.own), channel_id=1, source_target_pairs={{0,1},{1,0},{2,3},{3,2},{4,5},{5,4},{6,7},{7,6},{8,9},{9,8},{10,11... | collective-permute-start | bytes 4915208 | tf_op jit(solution)/shard_map/ppermute | solution.py:223
  110.8 1.0 copy-start.11
  111.8 18.1 %copy-start.12 = (f32[1,192,512]{2,1,0:T(8,128)S(1)}, f32[1,192,512]{2,1,0:T(8,128)}, u32[]{:S(2)}) copy-start(f32[1,192,512]{2,1,0:T(8,128)} %copy-done.10) | copy-start | bytes 1179652
  113.3 22.8 %collective-permute-start.18 = (s16[256,640]{1,0:T(8,128)(2,1)S(1)}, s16[256,640]{1,0:T(8,128)(2,1)S(1)}, u32[]{:S(2)}, u32[]{:S(2)}) collective-permute-start(s16[256,640]{1,0:T(8,128)(2,1)S(1)} %get-tuple-element.63), channel_id=1, source_target_pairs={{0,8},{1,9},{2,10},{3,11},{4,12},{5,13},{6,14},{7,15},{8,0},{9,1},... | collective-permute-start | bytes 983048 | tf_op jit(solution)/shard_map/ppermute | solution.py:223
  136.2 1.2 collective-permute-start.19
  147.6 24.3 %copy-start.2 = (bf16[2,96,1024]{2,1,0:T(8,128)(2,1)S(1)}, bf16[2,96,1024]{2,1,0:T(8,128)(2,1)}, u32[]{:S(2)}) copy-start(bf16[2,96,1024]{2,1,0:T(8,128)(2,1)} %param.8) | copy-start | bytes 1179652
  147.6 16.7 %collective-permute-start.21 = (bf16[192,1024]{1,0:T(8,128)(2,1)S(1)}, bf16[192,1024]{1,0:T(8,128)(2,1)S(1)}, u32[]{:S(2)}, u32[]{:S(2)}) collective-permute-start(bf16[192,1024]{1,0:T(8,128)(2,1)S(1)} %bitcast.50), channel_id=1, source_target_pairs={{0,4},{1,5},{2,6},{3,7},{4,0},{5,1},{6,2},{7,3},{8,12},{9,13},{10,... | collective-permute-start | bytes 1179656 | tf_op jit(solution)/shard_map/ppermute | solution.py:223
  147.7 16.7 %collective-permute-start.22 = (bf16[192,1024]{1,0:T(8,128)(2,1)S(1)}, bf16[192,1024]{1,0:T(8,128)(2,1)S(1)}, u32[]{:S(2)}, u32[]{:S(2)}) collective-permute-start(bf16[192,1024]{1,0:T(8,128)(2,1)S(1)} %bitcast.51), channel_id=1, source_target_pairs={{0,2},{1,3},{2,0},{3,1},{4,6},{5,7},{6,4},{7,5},{8,10},{9,11},{10,... | collective-permute-start | bytes 1179656 | tf_op jit(solution)/shard_map/ppermute | solution.py:223
  149.3 20.3 %collective-permute-start.23 = (bf16[192,1024]{1,0:T(8,128)(2,1)S(1)}, bf16[192,1024]{1,0:T(8,128)(2,1)S(1)}, u32[]{:S(2)}, u32[]{:S(2)}) collective-permute-start(bf16[192,1024]{1,0:T(8,128)(2,1)S(1)} %bitcast.52), channel_id=1, source_target_pairs={{0,8},{1,9},{2,10},{3,11},{4,12},{5,13},{6,14},{7,15},{8,0},{9,1},... | collective-permute-start | bytes 1179656 | tf_op jit(solution)/shard_map/ppermute | solution.py:223
  150.6 19.0 %collective-permute-start.24 = (bf16[192,1024]{1,0:T(8,128)(2,1)S(1)}, bf16[192,1024]{1,0:T(8,128)(2,1)S(1)}, u32[]{:S(2)}, u32[]{:S(2)}) collective-permute-start(bf16[192,1024]{1,0:T(8,128)(2,1)S(1)} %bitcast.53), channel_id=1, source_target_pairs={{0,1},{1,0},{2,3},{3,2},{4,5},{5,4},{6,7},{7,6},{8,9},{9,8},{10,11... | collective-permute-start | bytes 1179656 | tf_op jit(solution)/shard_map/ppermute | solution.py:223
  169.7 5.6 %collective-permute-start.28 = (bf16[3,192,1024]{2,1,0:T(8,128)(2,1)S(1)}, bf16[3,192,1024]{2,1,0:T(8,128)(2,1)}, u32[]{:S(2)}, u32[]{:S(2)}) collective-permute-start(bf16[3,192,1024]{2,1,0:T(8,128)(2,1)S(1)} %get-tuple-element.66.refs_0_), channel_id=1, source_target_pairs={{0,1},{1,0},{2,3},{3,2},{4,5},{5,4},{6,7},{7,6},{8,9},{9,8},{10,11... | collective-permute-start | bytes 3538952 | tf_op jit(solution)/shard_map/ppermute | solution.py:223
  169.8 20.1 %collective-permute-start.27 = (bf16[2,192,1024]{2,1,0:T(8,128)(2,1)S(1)}, bf16[2,192,1024]{2,1,0:T(8,128)(2,1)}, u32[]{:S(2)}, u32[]{:S(2)}) collective-permute-start(bf16[2,192,1024]{2,1,0:T(8,128)(2,1)S(1)} %get-tuple-element.65.refs_1_), channel_id=1, source_target_pairs={{0,2},{1,3},{2,0},{3,1},{4,6},{5,7},{6,4},{7,5},{8,10},{9,11},{10,... | collective-permute-start | bytes 2359304 | tf_op jit(solution)/shard_map/ppermute | solution.py:223
  170.4 13.2 %collective-permute-start.25 = (bf16[192,1024]{1,0:T(8,128)(2,1)S(1)}, bf16[192,1024]{1,0:T(8,128)(2,1)}, u32[]{:S(2)}, u32[]{:S(2)}) collective-permute-start(bf16[192,1024]{1,0:T(8,128)(2,1)S(1)} %together.6.refs_0_), channel_id=1, source_target_pairs={{0,12},{1,13},{2,14},{3,15},{4,8},{5,9},{6,10},{7,11},{8,4},{9,5},... | collective-permute-start | bytes 1179656 | tf_op jit(solution)/shard_map/ppermute | solution.py:223
  191.2 3.0 %collective-permute-start.29 = (bf16[3,192,1024]{2,1,0:T(8,128)(2,1)S(1)}, bf16[3,192,1024]{2,1,0:T(8,128)(2,1)}, u32[]{:S(2)}, u32[]{:S(2)}) collective-permute-start(bf16[3,192,1024]{2,1,0:T(8,128)(2,1)S(1)} %pack.5.refs_0_), channel_id=1, source_target_pairs={{0,1},{1,0},{2,3},{3,2},{4,5},{5,4},{6,7},{7,6},{8,9},{9,8},{10,11... | collective-permute-start | bytes 3538952 | tf_op jit(solution)/shard_map/ppermute | solution.py:223
  191.3 11.7 %collective-permute-start.26 = (bf16[192,1024]{1,0:T(8,128)(2,1)}, bf16[192,1024]{1,0:T(8,128)(2,1)S(1)}, u32[]{:S(2)}, u32[]{:S(2)}) collective-permute-start(bf16[192,1024]{1,0:T(8,128)(2,1)} %collective-permute-done.25.refs_1_), channel_id=1, source_target_pairs={{0,2},{1,3},{2,0},{3,1},{4,6},{5,7},{6,4},{7,5},{8,10},{9,11},{10,... | collective-permute-start | bytes 1179656 | tf_op jit(solution)/shard_map/ppermute | solution.py:223
  203.0 1.7 collective-permute-start.30

commit v17 on v14

--- a/solution.py
+++ b/solution.py
@@ -572,7 +572,8 @@
     (last,) = together([last], [mixed])
 
     last_partner = swap(last, 1)
-    return add(mixed, [last, last_partner], (14, 15), jnp.bfloat16)
+    mixed = add(mixed, [last], (14,))
+    return add(mixed, [last_partner], (15,), jnp.bfloat16)
 
 
 def attend_kernel(

time: 208 us -> 208 us (level)
    pallas_call x4 -> x5, Pallas kernels: 21.5 us -> 22.5 us  [mix(): pl.pallas_call(functools.partial(mix_kernel, len(pieces)), in_specs=[pl.B...]
  transfers between devices with their start and end apart: 31 -> 31, of which waited for: 20 -> 19; matrix products, arithmetic and copies ran while one was open for 3% -> 3% of each run, Pallas kernels for 27% -> 28%
where the time goes in v17:
time: 208 us; the launch traced here: 207 us
  waiting for transfers between devices  84 us (40%)
  Pallas kernels  70.1 us (34%)
  starting transfers between devices  37.4 us (18%)
  local copies, waits for them, and re-layouts  8.98 us (4%)
  other arithmetic  5.84 us (3%)
    ppermute x31, waiting for transfers between devices, swap(): return lax.ppermute(value, 'tensor', [(i, i ^ bit) for i in range(devices)])  84 us
    ppermute x31, starting transfers between devices, swap(): return lax.ppermute(value, 'tensor', [(i, i ^ bit) for i in range(devices)])  37.4 us
    pallas_call x5, Pallas kernels, mix(): pl.pallas_call(functools.partial(mix_kernel, len(pieces)), in_specs=[pl.B...  22.5 us
    pallas_call x2, Pallas kernels, project(): pl.pallas_call(functools.partial(project_kernel, part), grid_spec=pltpu.P...  20.3 us
    pallas_call x6, Pallas kernels, fold(): pl.pallas_call(functools.partial(fold_kernel, steps, low), grid_spec=pltp...  15.8 us
    pallas_call x1, Pallas kernels, attend(): pl.pallas_call(attend_kernel, in_specs=[pl.BlockSpec(memory_space=pltpu.S...  8.39 us
    unnamed x56, local copies, waits for them, and re-layouts  6.13 us
  transfers between devices with their start and end apart: 31, of which 19 were waited for; matrix products, arithmetic and copies ran while one was open for 3% of the time, Pallas kernels for 28%

profile of v17, /device:TPU:0, one launch (start us, length us, event | category | flops | bytes accessed | tf_op | source)
XLA Modules:
  0.0 207.0 jit_solution(8024876034049571739)
XLA Ops:
  0.0 1.2 fusion
  1.2 3.0 %collective-permute-start = (f32[2,96]{1,0:T(2,128)S(1)}, f32[2,96]{1,0:T(2,128)S(1)}, u32[]{:S(2)}, u32[]{:S(2)}) collective-permute-start(f32[2,96]{1,0:T(2,128)S(1)} %fusion), channel_id=1, source_target_pairs={{0,2},{1,3},{2,0},{3,1},{4,6},{5,7},{6,4},{7,5},{8,10},{9,11},{10,... | collective-permute-start | bytes 2312 | tf_op jit(solution)/shard_map/ppermute | solution.py:223
  4.3 1.5 collective-permute-done
  5.8 1.1 collective-permute-done.1
  7.0 2.1 %collective-permute-start.2 = (f32[2,96]{1,0:T(2,128)S(1)}, f32[2,96]{1,0:T(2,128)S(1)}, u32[]{:S(2)}, u32[]{:S(2)}) collective-permute-start(f32[2,96]{1,0:T(2,128)S(1)} %add.138), channel_id=1, source_target_pairs={{0,4},{1,5},{2,6},{3,7},{4,0},{5,1},{6,2},{7,3},{8,12},{9,13},{10,... | collective-permute-start | bytes 2312 | tf_op jit(solution)/shard_map/ppermute | solution.py:223
  9.0 0.8 reshape.240
  9.8 0.7 convert_element_type.29
  10.6 3.0 %collective-permute-start.3 = (f32[2,96]{1,0:T(2,128)S(1)}, f32[2,96]{1,0:T(2,128)S(1)}, u32[]{:S(2)}, u32[]{:S(2)}) collective-permute-start(f32[2,96]{1,0:T(2,128)S(1)} %add.139), channel_id=1, source_target_pairs={{0,8},{1,9},{2,10},{3,11},{4,12},{5,13},{6,14},{7,15},{8,0},{9,1},... | collective-permute-start | bytes 2312 | tf_op jit(solution)/shard_map/ppermute | solution.py:223
  13.6 1.4 copy-done.6
  15.2 1.6 collective-permute-start.5
  16.8 1.5 collective-permute-start.6
  18.6 3.5 %collective-permute-start.8 = (bf16[400,256]{1,0:T(8,128)(2,1)S(1)}, bf16[400,256]{1,0:T(8,128)(2,1)S(1)}, u32[]{:S(2)}, u32[]{:S(2)}) collective-permute-start(bf16[400,256]{1,0:T(8,128)(2,1)S(1)} %get-tuple-element.45), channel_id=1, source_target_pairs={{0,10},{1,11},{2,8},{3,9},{4,14},{5,15},{6,12},{7,13},{8,2},{9,3},... | collective-permute-start | bytes 614408 | tf_op jit(solution)/shard_map/ppermute | solution.py:223
  22.6 9.3 %project.2 = (f32[8,192,512]{2,1,0:T(8,128)}, s16[1936,512]{1,0:T(8,128)(2,1)}) custom-call(s32[1]{0:T(128)} %bitcast.1.core, bf16[192,1024]{1,0:T(8,128)(2,1)S(1)} %bitcast.47, bf16[1024,18432]{1,0:T(8,128)(2,1)} %weights.3, bf16[400,256]{1,0:T(8,128)(2,1)S(1)} %get-tuple-element.36.refs_0_), custom_call_target="tpu_custom_call" | custom-call | flops 1 | bytes 1 | tf_op jit(solution)/shard_map/project/pallas_call | solution.py:352
  32.0 11.0 %project.3 = (f32[8,192,640]{2,1,0:T(8,128)}, s16[1936,640]{1,0:T(8,128)(2,1)}) custom-call(s32[1]{0:T(128)} %bitcast.1.core, bf16[192,1024]{1,0:T(8,128)(2,1)S(1)} %bitcast.48, bf16[1024,18432]{1,0:T(8,128)(2,1)} %weights.3, f32[8,192,512]{2,1,0:T(8,128)} %get-tuple-element.37.refs_0_.held.held_out, bf16[400,256]{1,0:T(8,128)(2,1)S(1)} %collective-permute-done.5.refs_1_, ...), custom_call_target="tpu_custom_call" | custom-call | flops 1 | bytes 1 | tf_op jit(solution)/shard_map/project/pallas_call | solution.py:352
  43.0 1.4 collective-permute-done.8.refs_4_.refs_5_
  44.5 0.6 copy-done.11
  45.2 0.5 collective-permute-start.4
  45.8 2.4 %collective-permute-start.12 = (bf16[400,256]{1,0:T(8,128)(2,1)S(1)}, bf16[400,256]{1,0:T(8,128)(2,1)S(1)}, u32[]{:S(2)}, u32[]{:S(2)}) collective-permute-start(bf16[400,256]{1,0:T(8,128)(2,1)S(1)} %get-tuple-element.51), channel_id=1, source_target_pairs={{0,4},{1,5},{2,6},{3,7},{4,0},{5,1},{6,2},{7,3},{8,12},{9,13},{10,... | collective-permute-start | bytes 614408 | tf_op jit(solution)/shard_map/ppermute | solution.py:223
  48.2 1.6 collective-permute-start.13
  49.9 2.7 %collective-permute-done.4.landed.landed_out.landed_powers = s16[1936,512]{1,0:T(8,128)(2,1)S(1)} collective-permute-done((s16[1936,512]{1,0:T(8,128)(2,1)}, s16[1936,512]{1,0:T(8,128)(2,1)S(1)}, u32[]{:S(2)}, u32[]{:S(2)}) %collective-permute-start.4) | collective-permute-done | bytes 1982496 | tf_op jit(solution)/shard_map/ppermute | solution.py:223
  52.6 3.6 %fold.6 = (f32[4,192,512]{2,1,0:T(8,128)S(1)}, s16[976,512]{1,0:T(8,128)(2,1)S(1)}) custom-call(s32[1]{0:T(128)} %bitcast.4.bit, f32[8,192,512]{2,1,0:T(8,128)} %get-tuple-element.37.refs_0_.held.held_out, f32[8,192,512]{2,1,0:T(8,128)} %get-tuple-element.37.refs_0_.held.held_out, ...), custom_call_target="tpu_custom_call" | custom-call | flops 1 | bytes 1 | tf_op jit(solution)/shard_map/fold/pallas_call | solution.py:406
  56.3 0.7 collective-permute-start.10
  57.0 2.2 %collective-permute-done.13.refs_2_.refs_7_ = bf16[400,256]{1,0:T(8,128)(2,1)S(1)} collective-permute-done((bf16[400,256]{1,0:T(8,128)(2,1)S(1)}, bf16[400,256]{1,0:T(8,128)(2,1)S(1)}, u32[]{:S(2)}, u32[]{:S(2)}) %collective-permute-start.13) | collective-permute-done | bytes 204832 | tf_op jit(solution)/shard_map/ppermute | solution.py:223
  59.2 5.8 %fold.7 = (f32[4,192,640]{2,1,0:T(8,128)S(1)}, s16[976,640]{1,0:T(8,128)(2,1)}) custom-call(s32[1]{0:T(128)} %bitcast.3.bit, f32[8,192,640]{2,1,0:T(8,128)} %get-tuple-element.50.held.held_out, f32[8,192,640]{2,1,0:T(8,128)} %get-tuple-element.50.held.held_out, s16[1936,640]{1,0:T(8,128)(2,1)} %collective-permute-done.11.landed.landed_out.landed_powers, ...), custom_call_target="tpu_custom_call" | custom-call | flops 1 | bytes 1 | tf_op jit(solution)/shard_map/fold/pallas_call | solution.py:406
  65.0 1.4 collective-permute-start.15
  66.7 14.0 %collective-permute-done.10.landed.landed_out.landed_powers = s16[976,512]{1,0:T(8,128)(2,1)S(1)} collective-permute-done((s16[976,512]{1,0:T(8,128)(2,1)S(1)}, s16[976,512]{1,0:T(8,128)(2,1)S(1)}, u32[]{:S(2)}, u32[]{:S(2)}) %collective-permute-start.10) | collective-permute-done | bytes 999456 | tf_op jit(solution)/shard_map/ppermute | solution.py:223
  80.7 1.7 fold.8
  82.3 0.9 copy-done.2
  83.3 2.4 %collective-permute-start.14 = (s16[496,512]{1,0:T(8,128)(2,1)}, s16[496,512]{1,0:T(8,128)(2,1)}, u32[]{:S(2)}, u32[]{:S(2)}) collective-permute-start(s16[496,512]{1,0:T(8,128)(2,1)} %get-tuple-element.55), channel_id=1, source_target_pairs={{0,4},{1,5},{2,6},{3,7},{4,0},{5,1},{6,2},{7,3},{8,12},{9,13},{10,... | collective-permute-start | bytes 1523720 | tf_op jit(solution)/shard_map/ppermute | solution.py:223
  85.8 1.1 fusion.5
  87.0 8.7 %collective-permute-done.15.landed.landed_out.landed_powers = s16[976,640]{1,0:T(8,128)(2,1)S(1)} collective-permute-done((s16[976,640]{1,0:T(8,128)(2,1)}, s16[976,640]{1,0:T(8,128)(2,1)S(1)}, u32[]{:S(2)}, u32[]{:S(2)}) %collective-permute-start.15) | collective-permute-done | bytes 1249312 | tf_op jit(solution)/shard_map/ppermute | solution.py:223
  95.7 1.1 copy-done.3
  96.9 2.0 fold.9
  98.8 0.8 collective-permute-start.17
  99.8 5.2 %collective-permute-done.14.landed.landed_out.landed_powers = s16[496,512]{1,0:T(8,128)(2,1)} collective-permute-done((s16[496,512]{1,0:T(8,128)(2,1)}, s16[496,512]{1,0:T(8,128)(2,1)}, u32[]{:S(2)}, u32[]{:S(2)}) %collective-permute-start.14) | collective-permute-done | bytes 507936 | tf_op jit(solution)/shard_map/ppermute | solution.py:223
  105.0 2.2 %fold.10 = (f32[1,192,512]{2,1,0:T(8,128)S(1)}, s16[256,512]{1,0:T(8,128)(2,1)}) custom-call(s32[1]{0:T(128)} %bitcast.2.bit, f32[2,192,512]{2,1,0:T(8,128)S(1)} %copy-done.3, f32[2,192,512]{2,1,0:T(8,128)S(1)} %copy-done.3, s16[496,512]{1,0:T(8,128)(2,1)} %collective-permute-done.14.landed.landed_out.landed_powers, ...), custom_call_target="tpu_custom_call" | custom-call | flops 1 | bytes 1 | tf_op jit(solution)/shard_map/fold/pallas_call | solution.py:406
  107.3 0.7 copy-done.21
  108.0 1.7 collective-permute-start.16
  109.8 1.8 pad_maximum_fusion
  112.1 1.0 copy-done.22
  113.1 0.5 fold.11
  113.5 1.8 collective-permute-start.18
  115.3 15.0 %collective-permute-done.16.landed = s16[256,512]{1,0:T(8,128)(2,1)} collective-permute-done((s16[256,512]{1,0:T(8,128)(2,1)}, s16[256,512]{1,0:T(8,128)(2,1)}, u32[]{:S(2)}, u32[]{:S(2)}) %collective-permute-start.16) | collective-permute-done | bytes 262176 | tf_op jit(solution)/shard_map/ppermute | solution.py:223
  130.3 1.2 finish.2
  131.5 3.9 %collective-permute-done.18.landed.refs_1_ = s16[256,640]{1,0:T(8,128)(2,1)S(1)} collective-permute-done((s16[256,640]{1,0:T(8,128)(2,1)S(1)}, s16[256,640]{1,0:T(8,128)(2,1)S(1)}, u32[]{:S(2)}, u32[]{:S(2)}) %collective-permute-start.18) | collective-permute-done | bytes 327712 | tf_op jit(solution)/shard_map/ppermute | solution.py:223
  135.9 0.8 collective-permute-done.19
  136.9 0.7 slice_reduce_fusion
  138.4 8.4 %attend.1 = bf16[16,96,128]{2,1,0:T(8,128)(2,1)S(1)} custom-call(s32[24]{0:T(128)S(1)} %get-tuple-element.69.slot_request, bf16[16,96,128]{2,1,0:T(8,128)(2,1)S(1)} %bitcast.55, bf16[16,16,128]{2,1,0:T(8,128)(2,1)S(1)} %pad.12.new_keys, bf16[16,16,128]{2,1,0:T(8,128)(2,1)S(1)} %pad.13.new_values, bf16[8,400,256]{2,1,0:T(8,128)(2,1)S(1)} %pack.3.refs_0_.own, ...), custom_call_target="tpu_custom_call" | custom-call | flops 1 | bytes 1 | tf_op jit(solution)/shard_map/attend/pallas_call | solution.py:662
  147.0 1.0 collective-permute-start.22
  148.0 2.6 %collective-permute-start.23 = (bf16[192,1024]{1,0:T(8,128)(2,1)S(1)}, bf16[192,1024]{1,0:T(8,128)(2,1)S(1)}, u32[]{:S(2)}, u32[]{:S(2)}) collective-permute-start(bf16[192,1024]{1,0:T(8,128)(2,1)S(1)} %bitcast.52), channel_id=1, source_target_pairs={{0,8},{1,9},{2,10},{3,11},{4,12},{5,13},{6,14},{7,15},{8,0},{9,1},... | collective-permute-start | bytes 1179656 | tf_op jit(solution)/shard_map/ppermute | solution.py:223
  150.6 15.2 %collective-permute-done.21.refs_0_ = bf16[192,1024]{1,0:T(8,128)(2,1)S(1)} collective-permute-done((bf16[192,1024]{1,0:T(8,128)(2,1)S(1)}, bf16[192,1024]{1,0:T(8,128)(2,1)S(1)}, u32[]{:S(2)}, u32[]{:S(2)}) %collective-permute-start.21) | collective-permute-done | bytes 393248 | tf_op jit(solution)/shard_map/ppermute | solution.py:223
  165.8 2.4 %collective-permute-done.23.refs_2_ = bf16[192,1024]{1,0:T(8,128)(2,1)S(1)} collective-permute-done((bf16[192,1024]{1,0:T(8,128)(2,1)S(1)}, bf16[192,1024]{1,0:T(8,128)(2,1)S(1)}, u32[]{:S(2)}, u32[]{:S(2)}) %collective-permute-start.23) | collective-permute-done | bytes 393248 | tf_op jit(solution)/shard_map/ppermute | solution.py:223
  168.5 1.3 collective-permute-start.27
  169.8 2.4 %collective-permute-start.25 = (bf16[192,1024]{1,0:T(8,128)(2,1)S(1)}, bf16[192,1024]{1,0:T(8,128)(2,1)}, u32[]{:S(2)}, u32[]{:S(2)}) collective-permute-start(bf16[192,1024]{1,0:T(8,128)(2,1)S(1)} %together.6.refs_0_), channel_id=1, source_target_pairs={{0,12},{1,13},{2,14},{3,15},{4,8},{5,9},{6,10},{7,11},{8,4},{9,5},... | collective-permute-start | bytes 1179656 | tf_op jit(solution)/shard_map/ppermute | solution.py:223
  172.4 3.4 %mix.5.refs_3_ = f32[192,1024]{1,0:T(8,128)S(1)} custom-call(s32[2]{0:T(128)S(1)} %pad_add_fusion.places, bf16[192,1024]{1,0:T(8,128)(2,1)S(1)} %together.6.refs_0_, bf16[192,1024]{1,0:T(8,128)(2,1)S(1)} %collective-permute-done.24.refs_3_.refs_1_, bf16[16384,1024]{1,0:T(8,128)(2,1)} %refs_1_.3, bf16[192,1024]{1,0:T(8,128)(2,1)S(1)} %bitcast.49), custom_call_target="tpu_custom_call" | custom-call | flops 1 | bytes 1 | tf_op jit(solution)/shard_map/mix/pallas_call | solution.py:509
  175.8 7.0 %mix.6.refs_2_.refs_3_ = f32[192,1024]{1,0:T(8,128)S(1)} custom-call(s32[6]{0:T(128)S(1)} %stack.77.places, bf16[3,192,1024]{2,1,0:T(8,128)(2,1)S(1)} %get-tuple-element.66.refs_0_, bf16[3,192,1024]{2,1,0:T(8,128)(2,1)} %collective-permute-done.28.refs_1_, bf16[16384,1024]{1,0:T(8,128)(2,1)} %refs_1_.3, f32[192,1024]{1,0:T(8,128)S(1)} %mix.5.refs_3_), custom_call_target="tpu_custom_call" | custom-call | flops 1 | bytes 1 | tf_op jit(solution)/shard_map/mix/pallas_call | solution.py:509
  183.0 5.6 %collective-permute-done.27.refs_0_ = bf16[2,192,1024]{2,1,0:T(8,128)(2,1)} collective-permute-done((bf16[2,192,1024]{2,1,0:T(8,128)(2,1)S(1)}, bf16[2,192,1024]{2,1,0:T(8,128)(2,1)}, u32[]{:S(2)}, u32[]{:S(2)}) %collective-permute-start.27) | collective-permute-done | bytes 786464 | tf_op jit(solution)/shard_map/ppermute | solution.py:223
  188.6 1.3 pack.5.refs_0_
  190.0 1.3 collective-permute-start.26
  191.3 1.6 collective-permute-done.29.refs_1_
  192.9 7.0 %mix.7.refs_1_.refs_2_ = f32[192,1024]{1,0:T(8,128)S(1)} custom-call(s32[6]{0:T(128)S(1)} %stack.70.places, bf16[3,192,1024]{2,1,0:T(8,128)(2,1)S(1)} %pack.5.refs_0_, bf16[3,192,1024]{2,1,0:T(8,128)(2,1)} %collective-permute-done.29.refs_1_, bf16[16384,1024]{1,0:T(8,128)(2,1)} %refs_1_.3, f32[192,1024]{1,0:T(8,128)S(1)} %mix.6.refs_2_.refs_3_), custom_call_target="tpu_custom_call" | custom-call | flops 1 | bytes 1 | tf_op jit(solution)/shard_map/mix/pallas_call | solution.py:509
  199.9 1.8 collective-permute-done.26.refs_0_
  201.7 2.2 %mix.8.refs_2_ = f32[192,1024]{1,0:T(8,128)S(1)} custom-call(s32[1]{0:T(128)} %bitcast.34.places, bf16[192,1024]{1,0:T(8,128)(2,1)S(1)} %together.7.refs_0_, bf16[16384,1024]{1,0:T(8,128)(2,1)} %refs_1_.3, f32[192,1024]{1,0:T(8,128)S(1)} %mix.7.refs_1_.refs_2_), custom_call_target="tpu_custom_call" | custom-call | flops 1 | bytes 1 | tf_op jit(solution)/shard_map/mix/pallas_call | solution.py:509
  203.9 2.9 %mix.9 = bf16[192,1024]{1,0:T(8,128)(2,1)} custom-call(s32[1]{0:T(128)} %bitcast.places, bf16[192,1024]{1,0:T(8,128)(2,1)S(1)} %collective-permute-done.30.refs_0_, bf16[16384,1024]{1,0:T(8,128)(2,1)} %refs_1_.3, f32[192,1024]{1,0:T(8,128)S(1)} %mix.8.refs_2_), custom_call_target="tpu_custom_call" | custom-call | flops 1 | bytes 1 | tf_op jit(solution)/shard_map/mix/pallas_call | solution.py:509
  (132 shorter events, 4.8 us)
Async XLA Ops:
  0.0 22.4 %copy-start.4 = (bf16[2,96,1024]{2,1,0:T(8,128)(2,1)S(1)}, bf16[2,96,1024]{2,1,0:T(8,128)(2,1)}, u32[]{:S(2)}) copy-start(bf16[2,96,1024]{2,1,0:T(8,128)(2,1)} %param.8) | copy-start | bytes 1179652
  1.2 4.6 %collective-permute-start = (f32[2,96]{1,0:T(2,128)S(1)}, f32[2,96]{1,0:T(2,128)S(1)}, u32[]{:S(2)}, u32[]{:S(2)}) collective-permute-start(f32[2,96]{1,0:T(2,128)S(1)} %fusion), channel_id=1, source_target_pairs={{0,2},{1,3},{2,0},{3,1},{4,6},{5,7},{6,4},{7,5},{8,10},{9,11},{10,... | collective-permute-start | bytes 2312 | tf_op jit(solution)/shard_map/ppermute | solution.py:223
  5.8 1.1 collective-permute-start.1
  7.0 3.6 %collective-permute-start.2 = (f32[2,96]{1,0:T(2,128)S(1)}, f32[2,96]{1,0:T(2,128)S(1)}, u32[]{:S(2)}, u32[]{:S(2)}) collective-permute-start(f32[2,96]{1,0:T(2,128)S(1)} %add.138), channel_id=1, source_target_pairs={{0,4},{1,5},{2,6},{3,7},{4,0},{5,1},{6,2},{7,3},{8,12},{9,13},{10,... | collective-permute-start | bytes 2312 | tf_op jit(solution)/shard_map/ppermute | solution.py:223
  10.6 11.6 %collective-permute-start.3 = (f32[2,96]{1,0:T(2,128)S(1)}, f32[2,96]{1,0:T(2,128)S(1)}, u32[]{:S(2)}, u32[]{:S(2)}) collective-permute-start(f32[2,96]{1,0:T(2,128)S(1)} %add.139), channel_id=1, source_target_pairs={{0,8},{1,9},{2,10},{3,11},{4,12},{5,13},{6,14},{7,15},{8,0},{9,1},... | collective-permute-start | bytes 2312 | tf_op jit(solution)/shard_map/ppermute | solution.py:223
  13.6 1.4 copy-start.6
  15.2 16.8 %copy-start.19 = (bf16[400,256]{1,0:T(8,128)(2,1)}, bf16[400,256]{1,0:T(8,128)(2,1)S(1)}, u32[]{:S(2)}) copy-start(bf16[400,256]{1,0:T(8,128)(2,1)S(1)} %get-tuple-element.36.refs_0_) | copy-start | bytes 614404
  15.2 16.8 %collective-permute-start.5 = (bf16[400,256]{1,0:T(8,128)(2,1)S(1)}, bf16[400,256]{1,0:T(8,128)(2,1)S(1)}, u32[]{:S(2)}, u32[]{:S(2)}) collective-permute-start(bf16[400,256]{1,0:T(8,128)(2,1)S(1)} %get-tuple-element.39), channel_id=1, source_target_pairs={{0,2},{1,3},{2,0},{3,1},{4,6},{5,7},{6,4},{7,5},{8,10},{9,11},{10,... | collective-permute-start | bytes 614408 | tf_op jit(solution)/shard_map/ppermute | solution.py:223
  16.8 15.2 %collective-permute-start.6 = (bf16[400,256]{1,0:T(8,128)(2,1)S(1)}, bf16[400,256]{1,0:T(8,128)(2,1)S(1)}, u32[]{:S(2)}, u32[]{:S(2)}) collective-permute-start(bf16[400,256]{1,0:T(8,128)(2,1)S(1)} %get-tuple-element.40), channel_id=1, source_target_pairs={{0,6},{1,7},{2,4},{3,5},{4,2},{5,3},{6,0},{7,1},{8,14},{9,15},{10,... | collective-permute-start | bytes 614408 | tf_op jit(solution)/shard_map/ppermute | solution.py:223
  18.3 24.7 %collective-permute-start.7 = (bf16[400,256]{1,0:T(8,128)(2,1)S(1)}, bf16[400,256]{1,0:T(8,128)(2,1)S(1)}, u32[]{:S(2)}, u32[]{:S(2)}) collective-permute-start(bf16[400,256]{1,0:T(8,128)(2,1)S(1)} %get-tuple-element.44), channel_id=1, source_target_pairs={{0,8},{1,9},{2,10},{3,11},{4,12},{5,13},{6,14},{7,15},{8,0},{9,1},... | collective-permute-start | bytes 614408 | tf_op jit(solution)/shard_map/ppermute | solution.py:223
  18.6 25.8 %collective-permute-start.8 = (bf16[400,256]{1,0:T(8,128)(2,1)S(1)}, bf16[400,256]{1,0:T(8,128)(2,1)S(1)}, u32[]{:S(2)}, u32[]{:S(2)}) collective-permute-start(bf16[400,256]{1,0:T(8,128)(2,1)S(1)} %get-tuple-element.45), channel_id=1, source_target_pairs={{0,10},{1,11},{2,8},{3,9},{4,14},{5,15},{6,12},{7,13},{8,2},{9,3},... | collective-permute-start | bytes 614408 | tf_op jit(solution)/shard_map/ppermute | solution.py:223
  22.2 22.3 %collective-permute-start.9 = (bf16[400,256]{1,0:T(8,128)(2,1)S(1)}, bf16[400,256]{1,0:T(8,128)(2,1)S(1)}, u32[]{:S(2)}, u32[]{:S(2)}) collective-permute-start(bf16[400,256]{1,0:T(8,128)(2,1)S(1)} %get-tuple-element.46), channel_id=1, source_target_pairs={{0,12},{1,13},{2,14},{3,15},{4,8},{5,9},{6,10},{7,11},{8,4},{9,5},... | collective-permute-start | bytes 614408 | tf_op jit(solution)/shard_map/ppermute | solution.py:223
  32.0 11.0 %copy-start.7 = (bf16[400,256]{1,0:T(8,128)(2,1)}, bf16[400,256]{1,0:T(8,128)(2,1)S(1)}, u32[]{:S(2)}) copy-start(bf16[400,256]{1,0:T(8,128)(2,1)S(1)} %collective-permute-done.6.refs_2_.refs_3_) | copy-start | bytes 614404
  43.0 1.5 copy-start.9
  44.4 0.7 copy-start.11
  44.4 0.8 copy-start.13
  44.4 1.3 copy-start.26
  44.5 5.3 %copy-start.25 = (s32[16,16]{1,0:T(8,128)S(1)}, s32[16,16]{1,0:T(8,128)}, u32[]{:S(2)}) copy-start(s32[16,16]{1,0:T(8,128)} %param.15) | copy-start | bytes 3076
  45.2 14.0 %collective-permute-start.11 = (s16[1936,640]{1,0:T(8,128)(2,1)}, s16[1936,640]{1,0:T(8,128)(2,1)}, u32[]{:S(2)}, u32[]{:S(2)}) collective-permute-start(s16[1936,640]{1,0:T(8,128)(2,1)} %get-tuple-element.47.refs_0_), channel_id=1, source_target_pairs={{0,1},{1,0},{2,3},{3,2},{4,5},{5,4},{6,7},{7,6},{8,9},{9,8},{10,11... | collective-permute-start | bytes 7434248 | tf_op jit(solution)/shard_map/ppermute | solution.py:223
  45.2 7.4 %collective-permute-start.4 = (s16[1936,512]{1,0:T(8,128)(2,1)}, s16[1936,512]{1,0:T(8,128)(2,1)S(1)}, u32[]{:S(2)}, u32[]{:S(2)}) collective-permute-start(s16[1936,512]{1,0:T(8,128)(2,1)} %get-tuple-element.38), channel_id=1, source_target_pairs={{0,1},{1,0},{2,3},{3,2},{4,5},{5,4},{6,7},{7,6},{8,9},{9,8},{10,11... | collective-permute-start | bytes 5947400 | tf_op jit(solution)/shard_map/ppermute | solution.py:223
  45.8 11.2 %collective-permute-start.12 = (bf16[400,256]{1,0:T(8,128)(2,1)S(1)}, bf16[400,256]{1,0:T(8,128)(2,1)S(1)}, u32[]{:S(2)}, u32[]{:S(2)}) collective-permute-start(bf16[400,256]{1,0:T(8,128)(2,1)S(1)} %get-tuple-element.51), channel_id=1, source_target_pairs={{0,4},{1,5},{2,6},{3,7},{4,0},{5,1},{6,2},{7,3},{8,12},{9,13},{10,... | collective-permute-start | bytes 614408 | tf_op jit(solution)/shard_map/ppermute | solution.py:223
  48.2 11.0 %collective-permute-start.13 = (bf16[400,256]{1,0:T(8,128)(2,1)S(1)}, bf16[400,256]{1,0:T(8,128)(2,1)S(1)}, u32[]{:S(2)}, u32[]{:S(2)}) collective-permute-start(bf16[400,256]{1,0:T(8,128)(2,1)S(1)} %get-tuple-element.52), channel_id=1, source_target_pairs={{0,14},{1,15},{2,12},{3,13},{4,10},{5,11},{6,8},{7,9},{8,6},{9,7},... | collective-permute-start | bytes 614408 | tf_op jit(solution)/shard_map/ppermute | solution.py:223
  56.3 24.4 %collective-permute-start.10 = (s16[976,512]{1,0:T(8,128)(2,1)S(1)}, s16[976,512]{1,0:T(8,128)(2,1)S(1)}, u32[]{:S(2)}, u32[]{:S(2)}) collective-permute-start(s16[976,512]{1,0:T(8,128)(2,1)S(1)} %get-tuple-element.49), channel_id=1, source_target_pairs={{0,2},{1,3},{2,0},{3,1},{4,6},{5,7},{6,4},{7,5},{8,10},{9,11},{10,... | collective-permute-start | bytes 2998280 | tf_op jit(solution)/shard_map/ppermute | solution.py:223
  57.0 8.0 %copy-start.15 = (bf16[400,256]{1,0:T(8,128)(2,1)}, bf16[400,256]{1,0:T(8,128)(2,1)S(1)}, u32[]{:S(2)}) copy-start(bf16[400,256]{1,0:T(8,128)(2,1)S(1)} %collective-permute-done.12.refs_1_.refs_2_) | copy-start | bytes 614404
  59.2 5.8 %copy-start.17 = (bf16[400,256]{1,0:T(8,128)(2,1)}, bf16[400,256]{1,0:T(8,128)(2,1)S(1)}, u32[]{:S(2)}) copy-start(bf16[400,256]{1,0:T(8,128)(2,1)S(1)} %collective-permute-done.13.refs_2_.refs_7_) | copy-start | bytes 614404
  65.0 30.7 %collective-permute-start.15 = (s16[976,640]{1,0:T(8,128)(2,1)}, s16[976,640]{1,0:T(8,128)(2,1)S(1)}, u32[]{:S(2)}, u32[]{:S(2)}) collective-permute-start(s16[976,640]{1,0:T(8,128)(2,1)} %get-tuple-element.56), channel_id=1, source_target_pairs={{0,4},{1,5},{2,6},{3,7},{4,0},{5,1},{6,2},{7,3},{8,12},{9,13},{10,... | collective-permute-start | bytes 3747848 | tf_op jit(solution)/shard_map/ppermute | solution.py:223
  82.3 0.9 copy-start.2
  83.3 21.8 %collective-permute-start.14 = (s16[496,512]{1,0:T(8,128)(2,1)}, s16[496,512]{1,0:T(8,128)(2,1)}, u32[]{:S(2)}, u32[]{:S(2)}) collective-permute-start(s16[496,512]{1,0:T(8,128)(2,1)} %get-tuple-element.55), channel_id=1, source_target_pairs={{0,4},{1,5},{2,6},{3,7},{4,0},{5,1},{6,2},{7,3},{8,12},{9,13},{10,... | collective-permute-start | bytes 1523720 | tf_op jit(solution)/shard_map/ppermute | solution.py:223
  95.7 1.1 copy-start.3
  96.8 2.9 %copy-start.8 = (bf16[400,256]{1,0:T(8,128)(2,1)S(1)}, bf16[400,256]{1,0:T(8,128)(2,1)}, u32[]{:S(2)}) copy-start(bf16[400,256]{1,0:T(8,128)(2,1)} %copy-done.7) | copy-start | bytes 614404
  96.8 2.9 %copy-start.10 = (bf16[400,256]{1,0:T(8,128)(2,1)S(1)}, bf16[400,256]{1,0:T(8,128)(2,1)}, u32[]{:S(2)}) copy-start(bf16[400,256]{1,0:T(8,128)(2,1)} %copy-done.9) | copy-start | bytes 614404
  96.8 2.9 %copy-start.12 = (bf16[400,256]{1,0:T(8,128)(2,1)S(1)}, bf16[400,256]{1,0:T(8,128)(2,1)}, u32[]{:S(2)}) copy-start(bf16[400,256]{1,0:T(8,128)(2,1)} %copy-done.11) | copy-start | bytes 614404
  96.8 2.9 %copy-start.14 = (bf16[400,256]{1,0:T(8,128)(2,1)S(1)}, bf16[400,256]{1,0:T(8,128)(2,1)}, u32[]{:S(2)}) copy-start(bf16[400,256]{1,0:T(8,128)(2,1)} %copy-done.13) | copy-start | bytes 614404
  96.8 2.9 %copy-start.16 = (bf16[400,256]{1,0:T(8,128)(2,1)S(1)}, bf16[400,256]{1,0:T(8,128)(2,1)}, u32[]{:S(2)}) copy-start(bf16[400,256]{1,0:T(8,128)(2,1)} %copy-done.15) | copy-start | bytes 614404
  96.8 2.9 %copy-start.18 = (bf16[400,256]{1,0:T(8,128)(2,1)S(1)}, bf16[400,256]{1,0:T(8,128)(2,1)}, u32[]{:S(2)}) copy-start(bf16[400,256]{1,0:T(8,128)(2,1)} %copy-done.17) | copy-start | bytes 614404
  96.8 2.9 %copy-start.20 = (bf16[400,256]{1,0:T(8,128)(2,1)S(1)}, bf16[400,256]{1,0:T(8,128)(2,1)}, u32[]{:S(2)}) copy-start(bf16[400,256]{1,0:T(8,128)(2,1)} %copy-done.19) | copy-start | bytes 614404
  98.8 1.0 copy-start
  98.8 13.2 %collective-permute-start.17 = (s16[496,640]{1,0:T(8,128)(2,1)}, s16[496,640]{1,0:T(8,128)(2,1)S(1)}, u32[]{:S(2)}, u32[]{:S(2)}) collective-permute-start(s16[496,640]{1,0:T(8,128)(2,1)} %get-tuple-element.60), channel_id=1, source_target_pairs={{0,2},{1,3},{2,0},{3,1},{4,6},{5,7},{6,4},{7,5},{8,10},{9,11},{10,... | collective-permute-start | bytes 1904648 | tf_op jit(solution)/shard_map/ppermute | solution.py:223
  105.0 7.0 %copy-start.1 = (f32[2,192,640]{2,1,0:T(8,128)S(1)}, f32[2,192,640]{2,1,0:T(8,128)}, u32[]{:S(2)}) copy-start(f32[2,192,640]{2,1,0:T(8,128)} %copy-done) | copy-start | bytes 2949124
  107.3 0.7 copy-start.21
  108.0 22.3 %collective-permute-start.16 = (s16[256,512]{1,0:T(8,128)(2,1)}, s16[256,512]{1,0:T(8,128)(2,1)}, u32[]{:S(2)}, u32[]{:S(2)}) collective-permute-start(s16[256,512]{1,0:T(8,128)(2,1)} %get-tuple-element.59), channel_id=1, source_target_pairs={{0,8},{1,9},{2,10},{3,11},{4,12},{5,13},{6,14},{7,15},{8,0},{9,1},... | collective-permute-start | bytes 786440 | tf_op jit(solution)/shard_map/ppermute | solution.py:223
  111.6 25.3 %collective-permute-start.20 = (bf16[8,400,256]{2,1,0:T(8,128)(2,1)S(1)}, bf16[8,400,256]{2,1,0:T(8,128)(2,1)}, u32[]{:S(2)}, u32[]{:S(2)}) collective-permute-start(bf16[8,400,256]{2,1,0:T(8,128)(2,1)S(1)} %pack.3.refs_0_.own), channel_id=1, source_target_pairs={{0,1},{1,0},{2,3},{3,2},{4,5},{5,4},{6,7},{7,6},{8,9},{9,8},{10,11... | collective-permute-start | bytes 4915208 | tf_op jit(solution)/shard_map/ppermute | solution.py:223
  112.1 1.0 copy-start.22
  113.1 17.3 %copy-start.23 = (f32[1,192,512]{2,1,0:T(8,128)S(1)}, f32[1,192,512]{2,1,0:T(8,128)}, u32[]{:S(2)}) copy-start(f32[1,192,512]{2,1,0:T(8,128)} %copy-done.21) | copy-start | bytes 1179652
  113.1 17.3 %copy-start.24 = (f32[192,128]{1,0:T(8,128)S(1)}, f32[192,128]{1,0:T(8,128)}, u32[]{:S(2)}) copy-start(f32[192,128]{1,0:T(8,128)} %get-tuple-element.80.sine) | copy-start | bytes 294916
  113.5 21.9 %collective-permute-start.18 = (s16[256,640]{1,0:T(8,128)(2,1)S(1)}, s16[256,640]{1,0:T(8,128)(2,1)S(1)}, u32[]{:S(2)}, u32[]{:S(2)}) collective-permute-start(s16[256,640]{1,0:T(8,128)(2,1)S(1)} %get-tuple-element.63), channel_id=1, source_target_pairs={{0,8},{1,9},{2,10},{3,11},{4,12},{5,13},{6,14},{7,15},{8,0},{9,1},... | collective-permute-start | bytes 983048 | tf_op jit(solution)/shard_map/ppermute | solution.py:223
  135.4 1.2 collective-permute-start.19
  146.9 25.5 %copy-start.5 = (bf16[2,96,1024]{2,1,0:T(8,128)(2,1)S(1)}, bf16[2,96,1024]{2,1,0:T(8,128)(2,1)}, u32[]{:S(2)}) copy-start(bf16[2,96,1024]{2,1,0:T(8,128)(2,1)} %param.8) | copy-start | bytes 1179652
  146.9 18.9 %collective-permute-start.21 = (bf16[192,1024]{1,0:T(8,128)(2,1)S(1)}, bf16[192,1024]{1,0:T(8,128)(2,1)S(1)}, u32[]{:S(2)}, u32[]{:S(2)}) collective-permute-start(bf16[192,1024]{1,0:T(8,128)(2,1)S(1)} %bitcast.50), channel_id=1, source_target_pairs={{0,4},{1,5},{2,6},{3,7},{4,0},{5,1},{6,2},{7,3},{8,12},{9,13},{10,... | collective-permute-start | bytes 1179656 | tf_op jit(solution)/shard_map/ppermute | solution.py:223
  147.0 18.8 %collective-permute-start.22 = (bf16[192,1024]{1,0:T(8,128)(2,1)S(1)}, bf16[192,1024]{1,0:T(8,128)(2,1)S(1)}, u32[]{:S(2)}, u32[]{:S(2)}) collective-permute-start(bf16[192,1024]{1,0:T(8,128)(2,1)S(1)} %bitcast.51), channel_id=1, source_target_pairs={{0,2},{1,3},{2,0},{3,1},{4,6},{5,7},{6,4},{7,5},{8,10},{9,11},{10,... | collective-permute-start | bytes 1179656 | tf_op jit(solution)/shard_map/ppermute | solution.py:223
  148.0 20.3 %collective-permute-start.23 = (bf16[192,1024]{1,0:T(8,128)(2,1)S(1)}, bf16[192,1024]{1,0:T(8,128)(2,1)S(1)}, u32[]{:S(2)}, u32[]{:S(2)}) collective-permute-start(bf16[192,1024]{1,0:T(8,128)(2,1)S(1)} %bitcast.52), channel_id=1, source_target_pairs={{0,8},{1,9},{2,10},{3,11},{4,12},{5,13},{6,14},{7,15},{8,0},{9,1},... | collective-permute-start | bytes 1179656 | tf_op jit(solution)/shard_map/ppermute | solution.py:223
  150.6 17.7 %collective-permute-start.24 = (bf16[192,1024]{1,0:T(8,128)(2,1)S(1)}, bf16[192,1024]{1,0:T(8,128)(2,1)S(1)}, u32[]{:S(2)}, u32[]{:S(2)}) collective-permute-start(bf16[192,1024]{1,0:T(8,128)(2,1)S(1)} %bitcast.53), channel_id=1, source_target_pairs={{0,1},{1,0},{2,3},{3,2},{4,5},{5,4},{6,7},{7,6},{8,9},{9,8},{10,11... | collective-permute-start | bytes 1179656 | tf_op jit(solution)/shard_map/ppermute | solution.py:223
  168.4 7.3 %collective-permute-start.28 = (bf16[3,192,1024]{2,1,0:T(8,128)(2,1)S(1)}, bf16[3,192,1024]{2,1,0:T(8,128)(2,1)}, u32[]{:S(2)}, u32[]{:S(2)}) collective-permute-start(bf16[3,192,1024]{2,1,0:T(8,128)(2,1)S(1)} %get-tuple-element.66.refs_0_), channel_id=1, source_target_pairs={{0,1},{1,0},{2,3},{3,2},{4,5},{5,4},{6,7},{7,6},{8,9},{9,8},{10,11... | collective-permute-start | bytes 3538952 | tf_op jit(solution)/shard_map/ppermute | solution.py:223
  168.5 20.1 %collective-permute-start.27 = (bf16[2,192,1024]{2,1,0:T(8,128)(2,1)S(1)}, bf16[2,192,1024]{2,1,0:T(8,128)(2,1)}, u32[]{:S(2)}, u32[]{:S(2)}) collective-permute-start(bf16[2,192,1024]{2,1,0:T(8,128)(2,1)S(1)} %get-tuple-element.65.refs_1_), channel_id=1, source_target_pairs={{0,2},{1,3},{2,0},{3,1},{4,6},{5,7},{6,4},{7,5},{8,10},{9,11},{10,... | collective-permute-start | bytes 2359304 | tf_op jit(solution)/shard_map/ppermute | solution.py:223
  169.8 13.2 %collective-permute-start.25 = (bf16[192,1024]{1,0:T(8,128)(2,1)S(1)}, bf16[192,1024]{1,0:T(8,128)(2,1)}, u32[]{:S(2)}, u32[]{:S(2)}) collective-permute-start(bf16[192,1024]{1,0:T(8,128)(2,1)S(1)} %together.6.refs_0_), channel_id=1, source_target_pairs={{0,12},{1,13},{2,14},{3,15},{4,8},{5,9},{6,10},{7,11},{8,4},{9,5},... | collective-permute-start | bytes 1179656 | tf_op jit(solution)/shard_map/ppermute | solution.py:223
  189.9 3.0 %collective-permute-start.29 = (bf16[3,192,1024]{2,1,0:T(8,128)(2,1)S(1)}, bf16[3,192,1024]{2,1,0:T(8,128)(2,1)}, u32[]{:S(2)}, u32[]{:S(2)}) collective-permute-start(bf16[3,192,1024]{2,1,0:T(8,128)(2,1)S(1)} %pack.5.refs_0_), channel_id=1, source_target_pairs={{0,1},{1,0},{2,3},{3,2},{4,5},{5,4},{6,7},{7,6},{8,9},{9,8},{10,11... | collective-permute-start | bytes 3538952 | tf_op jit(solution)/shard_map/ppermute | solution.py:223
  190.0 11.7 %collective-permute-start.26 = (bf16[192,1024]{1,0:T(8,128)(2,1)}, bf16[192,1024]{1,0:T(8,128)(2,1)S(1)}, u32[]{:S(2)}, u32[]{:S(2)}) collective-permute-start(bf16[192,1024]{1,0:T(8,128)(2,1)} %collective-permute-done.25.refs_1_), channel_id=1, source_target_pairs={{0,2},{1,3},{2,0},{3,1},{4,6},{5,7},{6,4},{7,5},{8,10},{9,11},{10,... | collective-permute-start | bytes 1179656 | tf_op jit(solution)/shard_map/ppermute | solution.py:223
  201.7 2.2 %collective-permute-start.30 = (bf16[192,1024]{1,0:T(8,128)(2,1)S(1)}, bf16[192,1024]{1,0:T(8,128)(2,1)S(1)}, u32[]{:S(2)}, u32[]{:S(2)}) collective-permute-start(bf16[192,1024]{1,0:T(8,128)(2,1)S(1)} %together.7.refs_0_), channel_id=1, source_target_pairs={{0,1},{1,0},{2,3},{3,2},{4,5},{5,4},{6,7},{7,6},{8,9},{9,8},{10,11... | collective-permute-start | bytes 1179656 | tf_op jit(solution)/shard_map/ppermute | solution.py:223
